TPU v7x, 32 devices: a whole 2x2x4 slice. The times are simulated.
32 devices in a mesh: groups: 2 (over x), band: 16 (over z, y, core).
Axes of the slice: x: 2, y: 2, z: 4, core: 2. Of those that a mesh axis runs over, the one named last changes fastest.
Arguments:
- grid_features: bfloat16 [131072, 227], P(('groups', 'band')), parts along dimension 0, may hold values from -6 to 6
- mesh_latent: bfloat16 [8192, 512], P(('groups', 'band')), parts along dimension 0, may hold values from -6 to 6
- embed_in: bfloat16 [227, 512], replicated, may hold values from -0.375 to 0.375
- embed_out: bfloat16 [512, 512], replicated, may hold values from -0.25 to 0.25
- embed_gain: float32 [512], replicated, may hold values from 0.1 to 1.9
- interp: bfloat16 [256, 4, 32, 256], P('band'), may hold values from -0.375 to 0.375
- block_mask: int32 [256, 4], replicated, may hold values 0 or 1
- tile_list: int32 [256, 4], replicated, may hold values from 0 to 127, as said below
- mesh_up: bfloat16 [512, 512], replicated, may hold values from -0.25 to 0.25
- mesh_down: bfloat16 [512, 512], replicated, may hold values from -0.25 to 0.25
- mesh_gain: float32 [512], replicated, may hold values from 0.1 to 1.9
Outputs:
- grid_out: bfloat16 [131072, 512], P(('groups', 'band')), parts along dimension 0
- mesh_out: bfloat16 [8192, 512], P(('groups', 'band')), parts along dimension 0
There are 2 independent parts, one for each index of `groups`. A program takes and returns all parts, laid end to end along the dimension named above; an argument that names none is the same for every part. Nothing has to cross between parts.
Inputs may be any that keep to these rules, and one draw needn't show every extreme that they name: `tile_list`: tile t is owned by band index t // 8. Number the 64 entries of one band index's rows in row order as p; no two entries with equal p // 16 name tiles of one owner, so at most 4 entries of one band index name one owner's tiles, and exactly 4 do for some owner.
All inputs are finite; a program needn't handle non-finite values.
Results may differ from a plain program's by a relative error of at most 0.007.
Values may be sent and summed in bfloat16 or wider, within the bound.
No kernel may reach another device: no remote copies, remote signals or barrier semaphores. Data moves between devices by JAX's collectives and lax.ppermute only.
A program may use at most 128 MiB of HBM per device.

v0:
```python
import jax
import jax.numpy as jnp
from jax import lax
from jax.sharding import PartitionSpec as P


def layer_norm(values, gain):
    centred = values - jnp.mean(values, axis=-1, keepdims=True)
    spread = jnp.mean(centred * centred, axis=-1, keepdims=True)
    return centred * lax.rsqrt(spread + 1e-05) * gain


def on_device(
    grid_features,
    mesh_latent,
    embed_in,
    embed_out,
    embed_gain,
    interp,
    block_mask,
    tile_list,
    mesh_up,
    mesh_down,
    mesh_gain,
):
    n_band = lax.axis_size("band")
    own_index = lax.axis_index("band")
    blk_count, list_len, tile_rows, block_rows = interp.shape
    width = embed_out.shape[1]
    tiles_here = mesh_latent.shape[0] // tile_rows
    entries = blk_count * list_len
    slots = (entries + n_band - 1) // n_band
    hidden_grid = jax.nn.silu(
        jnp.dot(grid_features, embed_in, preferred_element_type=jnp.float32)
    ).astype(jnp.bfloat16)
    before = jnp.dot(hidden_grid, embed_out, preferred_element_type=jnp.float32)
    latent = layer_norm(before, embed_gain).astype(jnp.bfloat16)
    blocks = latent.reshape(blk_count, block_rows, width)
    my_mask = lax.dynamic_slice_in_dim(block_mask, own_index * blk_count, blk_count, 0).reshape(
        entries
    )
    my_tiles = lax.dynamic_slice_in_dim(tile_list, own_index * blk_count, blk_count, 0).reshape(
        entries
    )
    partial_value = jnp.einsum("bkmr,brd->bkmd", interp, blocks, preferred_element_type=jnp.float32)
    partial_value = (
        partial_value.reshape(entries, tile_rows, width)
        * my_mask.astype(jnp.float32)[:, None, None]
    ).astype(jnp.bfloat16)
    numbers = jnp.arange(entries, dtype=jnp.int32)
    slot_of = numbers // n_band
    owner_ids = jnp.arange(n_band, dtype=jnp.int32)
    slot_ids = jnp.arange(slots, dtype=jnp.int32)
    my_owner = my_tiles // tiles_here
    placing = (
        (my_owner[:, None, None] == owner_ids[None, :, None])
        & (slot_of[:, None, None] == slot_ids[None, None, :])
        & (my_mask[:, None, None] == 1)
    )
    placing = placing.astype(jnp.bfloat16)
    bucket = jnp.einsum(
        "poc,pmd->ocmd", placing, partial_value, preferred_element_type=jnp.float32
    ).astype(jnp.bfloat16)
    received = lax.all_to_all(bucket, "band", split_axis=0, concat_axis=0, tiled=True)
    all_tiles = tile_list.reshape(n_band, entries)
    all_mask = block_mask.reshape(n_band, entries)
    local_ids = jnp.arange(tiles_here, dtype=jnp.int32)
    mine = (all_tiles // tiles_here == own_index) & (all_mask == 1)
    routing = (
        mine[:, :, None, None]
        & (slot_of[None, :, None, None] == slot_ids[None, None, :, None])
        & ((all_tiles % tiles_here)[:, :, None, None] == local_ids[None, None, None, :])
    )
    routing = jnp.sum(routing.astype(jnp.float32), axis=1).astype(jnp.bfloat16)
    aggregate = jnp.einsum("sct,scmd->tmd", routing, received, preferred_element_type=jnp.float32)
    mesh_in = mesh_latent.astype(jnp.float32) + aggregate.reshape(tiles_here * tile_rows, width)
    normed = layer_norm(mesh_in, mesh_gain).astype(jnp.bfloat16)
    mesh_hidden = jax.nn.silu(jnp.dot(normed, mesh_up, preferred_element_type=jnp.float32)).astype(
        jnp.bfloat16
    )
    mesh_out = (
        mesh_in + jnp.dot(mesh_hidden, mesh_down, preferred_element_type=jnp.float32)
    ).astype(jnp.bfloat16)
    offsets = jnp.arange(tile_rows, dtype=jnp.int32)
    piece = lax.all_gather(mesh_out, "band", axis=0, tiled=True)
    wanted = my_tiles[:, None] * tile_rows + offsets[None, :]
    valid = (wanted >= 0) & (wanted < piece.shape[0])
    picked = piece[jnp.clip(wanted, 0, piece.shape[0] - 1)]
    gathered = jnp.where(valid[:, :, None], picked.astype(jnp.float32), 0.0)
    tile_value = (gathered * my_mask.astype(jnp.float32)[:, None, None]).astype(jnp.bfloat16)
    back = jnp.einsum(
        "bkmr,bkmd->brd",
        interp,
        tile_value.reshape(blk_count, list_len, tile_rows, width),
        preferred_element_type=jnp.float32,
    )
    grid_out = (latent.astype(jnp.float32) + back.reshape(blk_count * block_rows, width)).astype(
        jnp.bfloat16
    )
    return (grid_out, mesh_out)


def solution(mesh):
    placed = (
        P(("groups", "band"), None),
        P(("groups", "band"), None),
        P(),
        P(),
        P(),
        P("band", None, None, None),
        P(),
        P(),
        P(),
        P(),
        P(),
    )
    return jax.shard_map(
        on_device,
        mesh=mesh,
        in_specs=placed,
        out_specs=(P(("groups", "band"), None), P(("groups", "band"), None)),
        check_vma=False,
    )
```

profile of v0, /device:TPU:0, one launch (start us, length us, event | category | flops | bytes accessed | tf_op | source)
XLA Modules:
  0.0 174.5 jit_solution(11797630946355838484)
XLA Ops:
  7.2 0.9 dynamic-slice_compare_fusion
  8.1 0.8 dynamic-slice_convert_fusion
  8.8 0.1 copy.55
  8.9 0.1 eq.121
  9.0 0.8 broadcast_multiply_fusion.1
  10.0 0.1 broadcast_in_dim_reshape.4
  10.2 8.9 %fusion.52 = (f32[4096]{0:T(1024)S(1)}, f32[4096,512]{1,0:T(8,128)}) fusion(bf16[512,512]{1,0:T(8,128)(2,1)} %param.14, bf16[4096,227]{0,1:T(8,128)(2,1)S(1)} %copy-done, bf16[227,512]{1,0:T(8,128)(2,1)} %param.13), kind=kOutput, calls=%fused_computation.86 | convolution fusion | flops 3112169472 | bytes 11021312 | tf_op jit(solution)/shard_map/dot_general | solution.py:36
  19.1 4.4 %multiply_reduce_fusion = f32[4096]{0:T(1024)S(1)} fusion(f32[4096,512]{1,0:T(8,128)} %get-tuple-element.9, f32[4096]{0:T(1024)S(1)} %broadcast_multiply_fusion), kind=kLoop, calls=%fused_computation.4 | loop fusion | flops 6287360 | bytes 8421376 | tf_op jit(solution)/shard_map/reduce_sum | solution.py:9
  23.6 1.4 copy-done.1
  25.0 2.3 %multiply_convert_fusion = bf16[4096,512]{1,0:T(8,128)(2,1)S(1)} fusion(f32[4096,512]{1,0:T(8,128)S(1)} %copy-done.1, f32[512]{0:T(512)S(1)} %copy-done.5, f32[4096]{0:T(1024)S(1)} %add_rsqrt_fusion, f32[4096]{0:T(1024)S(1)} %broadcast_multiply_fusion), kind=kLoop, calls=%fused_computation.3 | loop fusion | flops 8388608 | bytes 12617728 | tf_op jit(solution)/shard_map/convert_element_type | solution.py:37
  27.3 0.7 fusion.53
  28.0 2.8 %fusion.18 = bf16[16,4,32,512]{3,0,1,2:T(8,128)(2,1)S(1)} fusion(f32[64,32,512]{2,1,0:T(8,128)S(1)} %bitcast.48, f32[64]{0:T(128)S(1)} %convert_element_type.67, pred[64]{0:T(512)(128)(4,1)S(1)} %eq.121, pred[64,4]{0,1:T(4,128)(4,1)S(1)} %iota_compare_fusion.2, pred[64,16]{0,1:T(8,128)(4,1)S(1)} %iota_compare_fusion.1), kind=kOutput, calls=%fused_computation.22 | convolution fusion | flops 137371648 | bytes 6293056 | tf_op jit(solution)/shard_map/poc,pmd->ocmd/dot_general | solution.py:61
  30.8 2.9 %copy.58 = bf16[16,4,32,512]{3,1,2,0:T(4,128)(2,1)} copy(bf16[16,4,32,512]{3,0,1,2:T(8,128)(2,1)S(1)} %fusion.18) | data formatting | bytes 4194304 | tf_op jit(solution)/shard_map/convert_element_type | solution.py:63
  33.8 7.6 %all-to-all-start = ((bf16[16,4,32,512]{3,1,2,0:T(4,128)(2,1)}), bf16[16,4,32,512]{3,1,2,0:T(4,128)(2,1)}, u32[]{:S(2)}, u32[]{:S(2)}) async-start(bf16[16,4,32,512]{3,1,2,0:T(4,128)(2,1)} %copy.58), calls=%async_computation | async-start | bytes 4194304 | tf_op jit(solution)/shard_map/all_to_all | solution.py:64
  41.3 0.2 all-gather.2.cloned.1.call-start
  41.6 0.1 copy.51
  41.7 0.2 copy.52
  41.9 0.1 eq.110
  42.0 0.1 reshape.340
  42.2 0.2 convert_reduce_fusion
  42.4 0.1 copy.53
  42.5 40.0 %all-to-all-done = bf16[16,4,32,512]{3,1,2,0:T(4,128)(2,1)} async-done(((bf16[16,4,32,512]{3,1,2,0:T(4,128)(2,1)}), bf16[16,4,32,512]{3,1,2,0:T(4,128)(2,1)}, u32[]{:S(2)}, u32[]{:S(2)}) %all-to-all-start) | async-done | bytes 2097184 | tf_op jit(solution)/shard_map/all_to_all | solution.py:64
  82.5 2.9 %fusion.21 = f32[8,32,512]{2,0,1:T(8,128)S(1)} fusion(bf16[16,4,32,512]{3,1,2,0:T(4,128)(2,1)} %all-to-all-done, bf16[16,4,8]{0,2,1:T(8,128)(2,1)S(1)} %copy.53), kind=kOutput, calls=%fused_computation.23 | convolution fusion | flops 16777216 | bytes 2622464 | tf_op jit(solution)/shard_map/sct,scmd->tmd/dot_general | solution.py:75
  85.4 0.3 copy.60
  85.7 1.1 fusion.51
  86.9 0.2 multiply_reduce_fusion.1
  87.1 2.5 %fusion.24 = bf16[256,512]{1,0:T(8,128)(2,1)} fusion(f32[256,512]{1,0:T(8,128)S(1)} %get-tuple-element.5, bf16[512,512]{1,0:T(8,128)(2,1)} %param.20, bf16[512,512]{1,0:T(8,128)(2,1)} %param.19, f32[512]{0:T(512)S(1)} %copy-done.6, f32[256]{0:T(256)S(1)} %add_rsqrt_fusion.1, f32[256]{0:T(256)S(1)} %broadcast_multiply_fusion.2), kind=kOutput, calls=%fused_computation.25 | convolution fusion | flops 269877248 | bytes 1839104 | tf_op jit(solution)/shard_map/dot_general | solution.py:82
  89.9 0.1 fusion.35
  90.0 56.9 %all-gather.2.cloned.1.call-done = bf16[4096,512]{1,0:T(8,128)(2,1)} async-done(((bf16[256,512]{1,0:T(8,128)(2,1)}), bf16[4096,512]{1,0:T(8,128)(2,1)}) %all-gather.2.cloned.1.call-update) | async-done | bytes 4194320 | tf_op jit(solution)/shard_map/all_gather | solution.py:85
  146.9 12.0 %gather_fusion = bf16[2048,512]{1,0:T(8,128)(2,1)} fusion(bf16[4096,512]{1,0:T(8,128)(2,1)} %all-gather.2.cloned.1.call-done, s32[2048]{0:T(1024)S(1)} %broadcast_clamp_fusion), kind=kCustom, calls=%fused_computation | custom fusion | bytes 4202496 | tf_op jit(solution)/shard_map/gather | solution.py:88
  158.9 2.9 %fusion.10 = f32[16,512,256,1]{1,2,3,0:T(8,128)S(1)} fusion(bf16[16,4,32,256]{3,2,1,0:T(8,128)(2,1)S(1)} %copy-done.2, bf16[16,4,32,512]{3,2,1,0:T(8,128)(2,1)} %bitcast.50, f32[16,4]{1,0:T(8,128)S(1)} %copy.56, pred[16,4,32]{2,1,0:T(4,128)(4,1)S(1)} %fusion.35), kind=kOutput, calls=%fused_computation.15 | convolution fusion | flops 541065216 | bytes 11536640 | tf_op jit(solution)/shard_map/bkmr,bkmd->brd/dot_general | solution.py:91
  161.8 5.9 %fusion = bf16[4096,512]{1,0:T(8,128)(2,1)} fusion(f32[16,512,256,1]{1,2,3,0:T(8,128)S(1)} %fusion.10, f32[512]{0:T(512)S(1)} %copy-done.5, f32[4096]{0:T(1024)S(1)} %add_rsqrt_fusion, f32[4096,512]{1,0:T(8,128)} %get-tuple-element.9, f32[4096]{0:T(1024)S(1)} %broadcast_multiply_fusion), kind=kLoop, calls=%fused_computation.2 | loop fusion | flops 14680064 | bytes 21006336 | tf_op jit(solution)/shard_map/convert_element_type | solution.py:97
  (33 shorter events, 0.6 us)
Async XLA Ops:
  7.2 3.0 %copy-start = (bf16[4096,227]{0,1:T(8,128)(2,1)S(1)}, bf16[4096,227]{0,1:T(8,128)(2,1)}, u32[]{:S(2)}) copy-start(bf16[4096,227]{0,1:T(8,128)(2,1)} %param.11) | copy-start | bytes 5578756
  19.1 5.8 %copy-start.1 = (f32[4096,512]{1,0:T(8,128)S(1)}, f32[4096,512]{1,0:T(8,128)}, u32[]{:S(2)}) copy-start(f32[4096,512]{1,0:T(8,128)} %get-tuple-element.9) | copy-start | bytes 25165828
  19.1 5.8 %copy-start.5 = (f32[512]{0:T(512)S(1)}, f32[512]{0:T(512)}, u32[]{:S(2)}) copy-start(f32[512]{0:T(512)} %param.15) | copy-start | bytes 6148
  25.0 2.3 %copy-start.2 = (bf16[16,4,32,256]{3,2,1,0:T(8,128)(2,1)S(1)}, bf16[16,4,32,256]{3,2,1,0:T(8,128)(2,1)}, u32[]{:S(2)}) copy-start(bf16[16,4,32,256]{3,2,1,0:T(8,128)(2,1)} %param.16) | copy-start | bytes 3145732
  30.8 10.8 %copy-start.4 = (s32[256,4]{0,1:T(4,128)S(1)}, s32[256,4]{0,1:T(4,128)}, u32[]{:S(2)}) copy-start(s32[256,4]{0,1:T(4,128)} %param.18) | copy-start | bytes 12292
  30.8 10.9 %copy-start.3 = (s32[256,4]{0,1:T(4,128)S(1)}, s32[256,4]{0,1:T(4,128)}, u32[]{:S(2)}) copy-start(s32[256,4]{0,1:T(4,128)} %param.17) | copy-start | bytes 12292
  33.8 53.3 %copy-start.6 = (f32[512]{0:T(512)S(1)}, f32[512]{0:T(512)}, u32[]{:S(2)}) copy-start(f32[512]{0:T(512)} %param.21) | copy-start | bytes 6148
  33.8 48.7 %all-to-all-start = ((bf16[16,4,32,512]{3,1,2,0:T(4,128)(2,1)}), bf16[16,4,32,512]{3,1,2,0:T(4,128)(2,1)}, u32[]{:S(2)}, u32[]{:S(2)}) async-start(bf16[16,4,32,512]{3,1,2,0:T(4,128)(2,1)} %copy.58), calls=%async_computation | async-start | bytes 4194304 | tf_op jit(solution)/shard_map/all_to_all | solution.py:64
  41.3 105.6 %all-gather.2.cloned.1.call-start = ((), (), s32[]{:S(2)}) async-start(), calls=%async_computation.1 | async-start | bytes 4456448 | tf_op jit(solution)/shard_map/all_gather | solution.py:85
Sparse Core Ops, SparseCore 0:
  89.8 57.0 all-gather.1
where the time goes:
time: 175 us; the launch traced here: 174 us
  waiting for transfers between devices  96.9 us (55%)
  matrix products  20.8 us (12%)
  local copies, waits for them, and re-layouts  18 us (10%)
  other arithmetic  16.7 us (10%)
  between operations  14.3 us (8%)
  starting transfers between devices  7.79 us (4%)
    all_gather x1, waiting for transfers between devices, on_device(): piece = lax.all_gather(mesh_out, 'band', axis=0, tiled=True)  56.9 us
    all_to_all x1, waiting for transfers between devices, on_device(): lax.all_to_all(bucket, 'band', split_axis=0, concat_axis=0, tiled=True)  40 us
    gather x1, local copies, waits for them, and re-layouts, on_device(): picked = piece[jnp.clip(wanted, 0, piece.shape[0] - 1)]  12 us
    dot_general x1, matrix products, on_device(): before = jnp.dot(hidden_grid, embed_out, preferred_element_type=jnp.float32)  8.93 us
    all_to_all x1, starting transfers between devices, on_device(): lax.all_to_all(bucket, 'band', split_axis=0, concat_axis=0, tiled=True)  7.57 us
    convert_element_type x1, other arithmetic, on_device(): (latent.astype(jnp.float32) + back.reshape(blk_count * block_rows, width)...  5.85 us
    reduce_sum x2, other arithmetic, layer_norm(): spread = jnp.mean(centred * centred, axis=-1, keepdims=True)  4.62 us
  transfers between devices with their start and end apart: 2, of which 2 were waited for; matrix products, arithmetic and copies ran while one was open for 1% of the time, Pallas kernels for 0%

commit v1 on v0

v1 whole, which is shorter than its diff:
```python
import functools

import jax
import jax.numpy as jnp
from jax import lax
from jax.experimental import pallas as pl
from jax.experimental.pallas import tpu as pltpu
from jax.sharding import PartitionSpec as P

F32 = jnp.float32
BF16 = jnp.bfloat16
VMEM_LIMIT = 48 * 1024 * 1024


def silu(values):
    half = 0.5 * values
    return half * (1.0 + jnp.tanh(half))


def layer_norm(values, gain):
    centred = values - jnp.mean(values, axis=-1, keepdims=True)
    spread = jnp.mean(centred * centred, axis=-1, keepdims=True)
    return centred * lax.rsqrt(spread + 1e-05) * gain


def embed_kernel(
    first, per_step, info_ref, x_ref, w1_ref, w2_ref, gain_ref, interp_ref, *rest
):
    latent_ref, *outs, placed = rest[1:] if first else rest
    step = pl.program_id(0)
    list_len, tile_rows, block_rows = interp_ref.shape[1:]
    hidden = silu(jnp.dot(x_ref[...], w1_ref[...], preferred_element_type=F32)).astype(BF16)
    before = jnp.dot(hidden, w2_ref[...], preferred_element_type=F32)
    latent = layer_norm(before, gain_ref[...]).astype(BF16)
    latent_ref[...] = latent
    for b in range(per_step):
        weights = interp_ref[b].reshape(list_len * tile_rows, block_rows)
        part = jnp.dot(
            weights, latent[b * block_rows : (b + 1) * block_rows], preferred_element_type=F32
        )
        for k in range(list_len):
            entry = first + (step * per_step + b) * list_len + k
            masked = part[k * tile_rows : (k + 1) * tile_rows] * info_ref[1, entry].astype(F32)
            placed[info_ref[0, entry]] = masked.astype(BF16)

    @pl.when(step == pl.num_programs(0) - 1)
    def _():
        count = outs[0].shape[0]
        for number, out in enumerate(outs):
            out[...] = placed[number * count : (number + 1) * count]


def combine_kernel(slots, ways, core, tile_ref, *refs):
    parts, (send_ref, own_ref, total) = refs[: slots * ways], refs[slots * ways :]
    away = pl.program_id(0)
    total[...] = jnp.zeros_like(total)
    for way in range(ways):
        for slot in range(slots):
            for other in range(core):
                tile = tile_ref[way, slot, away * core + other]
                total[other, tile] += parts[way * slots + slot][other].astype(F32)
    own_ref[0] = total[0]
    send_ref[0] = total[1].astype(BF16)


def add_kernel(own_ref, other_ref, here_ref, *there):
    here_ref[...] = own_ref[0] + other_ref[0].astype(F32)
    for away, out in enumerate(there, 1):
        out[...] = (own_ref[away] + other_ref[away].astype(F32)).astype(BF16)


def mesh_kernel(latent_ref, up_ref, down_ref, gain_ref, here_ref, *rest):
    others, out_ref = rest[:-1], rest[-1]
    mesh_in = latent_ref[...].astype(F32) + here_ref[...]
    for other in others:
        mesh_in = mesh_in + other[...].astype(F32)
    normed = layer_norm(mesh_in, gain_ref[...]).astype(BF16)
    hidden = silu(jnp.dot(normed, up_ref[...], preferred_element_type=F32)).astype(BF16)
    out_ref[...] = (
        mesh_in + jnp.dot(hidden, down_ref[...], preferred_element_type=F32)
    ).astype(BF16)


def back_kernel(count, per_step, info_ref, latent_ref, interp_ref, *rest):
    pieces, (out_ref, held, picked, sems) = rest[:count], rest[count:]
    step = pl.program_id(0)
    list_len, tile_rows, block_rows = interp_ref.shape[1:]

    @pl.when(step == 0)
    def _():
        copies = [
            pltpu.make_async_copy(pieces[i], held.at[i], sems.at[i]) for i in range(count)
        ]
        for copy in copies:
            copy.start()
        for copy in copies:
            copy.wait()

    for b in range(per_step):
        for k in range(list_len):
            entry = (step * per_step + b) * list_len + k
            rows = pl.ds(pl.multiple_of(info_ref[2, entry] * tile_rows, tile_rows), tile_rows)
            value = held[info_ref[3, entry], rows].astype(F32) * info_ref[1, entry].astype(F32)
            picked[b, k * tile_rows : (k + 1) * tile_rows] = value.astype(BF16)
        weights = interp_ref[b].reshape(list_len * tile_rows, block_rows)
        back = lax.dot_general(
            weights, picked[b], (((0,), (0,)), ((), ())), preferred_element_type=F32
        )
        rows = slice(b * block_rows, (b + 1) * block_rows)
        out_ref[rows] = (latent_ref[rows].astype(F32) + back).astype(BF16)


def whole(array):
    zeros = (0,) * array.ndim
    return pl.BlockSpec(array.shape, lambda *_: zeros)


def params():
    return pltpu.CompilerParams(vmem_limit_bytes=VMEM_LIMIT)


def cost(flops, *arrays):
    size = sum(a.size * a.dtype.itemsize for a in arrays)
    return pl.CostEstimate(flops=int(flops), bytes_accessed=int(size), transcendentals=0)


def shape(dims, kind=BF16):
    return jax.ShapeDtypeStruct(dims, kind)


def on_device(
    n_y,
    grid_features,
    mesh_latent,
    embed_in,
    embed_out,
    embed_gain,
    interp,
    block_mask,
    tile_list,
    mesh_up,
    mesh_down,
    mesh_gain,
):
    n_band = lax.axis_size("band")
    n_core = 2
    n_z = n_band // (n_y * n_core)
    me = lax.axis_index("band")
    blk_count, list_len, tile_rows, block_rows = interp.shape
    channels, width = embed_in.shape
    tiles_here = mesh_latent.shape[0] // tile_rows
    node_rows = mesh_latent.shape[0]
    entries = blk_count * list_len
    slots = entries // n_band
    group_blocks = n_band // list_len
    ahead = n_z * n_core

    def index_of(z, y, c):
        return (z % n_z * n_y + y) * n_core + c

    def place_of(i):
        return i // (n_y * n_core), i // n_core % n_y, i % n_core

    def move(value, where):
        pairs = [(i, index_of(*where(*place_of(i)))) for i in range(n_band)]
        return lax.ppermute(value, "band", pairs)

    def over_core(value):
        return move(value, lambda z, y, c: (z, y, 1 - c))

    def over_y(value):
        return move(value, lambda z, y, c: (z, 1 - y, c))

    def over_z(value, by):
        return move(value, lambda z, y, c: (z + by, y, c))

    all_tiles = tile_list.reshape(n_band, entries)
    all_mask = block_mask.reshape(n_band, entries)

    def relative(index):
        tiles = lax.dynamic_index_in_dim(all_tiles, index, 0, keepdims=False)
        owner = tiles // tiles_here
        z, y, c = place_of(owner)
        my_z, my_y, my_c = place_of(index)
        rel = ((y - my_y) % n_y * n_z + (z - my_z) % n_z) * n_core + (c - my_c) % n_core
        return rel, tiles % tiles_here

    my_mask = lax.dynamic_index_in_dim(all_mask, me, 0, keepdims=False)
    my_rel, my_local = relative(me)
    my_z, my_y, my_c = place_of(me)
    z_of, rest_of = my_rel // n_core % n_z, my_rel % n_core + my_rel // ahead * ahead
    piece_of = rest_of + (n_z - z_of) % n_z * n_core
    info = jnp.stack([my_rel, my_mask, my_local, piece_of])

    def by_place(rel, local):
        rel, local = rel.reshape(slots, n_band, 1), local.reshape(slots, n_band, 1)
        return jnp.sum(jnp.where(rel == jnp.arange(n_band), local, 0), axis=1)

    tables = [by_place(my_rel, my_local)[:, :ahead]]
    if n_y > 1:
        tables.append(by_place(*relative(index_of(my_z, 1 - my_y, my_c)))[:, ahead:])
    tables = jnp.stack(tables)

    gain = embed_gain.reshape(1, width)
    per_step = min(2, group_blocks)
    rows = per_step * block_rows
    latent, kept, sent = [], [], []
    for slot in range(slots):
        begin = slot * group_blocks // per_step
        outs = pl.pallas_call(
            functools.partial(embed_kernel, slot * n_band, per_step),
            out_shape=[shape((blk_count * block_rows, width))]
            + [shape((ahead, tile_rows, width))] * n_y,
            grid_spec=pltpu.PrefetchScalarGridSpec(
                num_scalar_prefetch=1,
                grid=(group_blocks // per_step,),
                in_specs=[
                    pl.BlockSpec((rows, channels), lambda i, _, begin=begin: (begin + i, 0)),
                    whole(embed_in),
                    whole(embed_out),
                    whole(gain),
                    pl.BlockSpec(
                        (per_step,) + interp.shape[1:],
                        lambda i, _, begin=begin: (begin + i, 0, 0, 0),
                    ),
                ]
                + [pl.BlockSpec(memory_space=pl.ANY)] * len(latent),
                out_specs=[pl.BlockSpec((rows, width), lambda i, _, begin=begin: (begin + i, 0))]
                + [pl.BlockSpec((ahead, tile_rows, width), lambda i, _: (0, 0, 0))] * n_y,
                scratch_shapes=[pltpu.VMEM((n_band, tile_rows, width), BF16)],
            ),
            input_output_aliases={6: 0} if latent else {},
            compiler_params=params(),
            cost_estimate=cost(
                2 * group_blocks * block_rows * width * (channels + width + list_len * tile_rows),
                grid_features,
                interp,
            ),
            name=f"embed_{slot}",
        )(info, grid_features, embed_in, embed_out, gain, interp, *latent)
        latent = [outs[0]]
        kept.append(outs[1])
        if n_y > 1:
            sent.append(over_y(outs[2]))

    parts = kept + sent
    dense = (n_z, tiles_here, tile_rows, width)
    one = (1,) + dense[1:]
    to_core, own = pl.pallas_call(
        functools.partial(combine_kernel, slots, n_y, n_core),
        out_shape=[shape(dense), shape(dense, F32)],
        grid_spec=pltpu.PrefetchScalarGridSpec(
            num_scalar_prefetch=1,
            grid=(n_z,),
            in_specs=[pl.BlockSpec((n_core, tile_rows, width), lambda i, _: (i, 0, 0))]
            * len(parts),
            out_specs=[pl.BlockSpec(one, lambda i, _: (i, 0, 0, 0))] * 2,
            scratch_shapes=[pltpu.VMEM((n_core,) + dense[1:], F32)],
        ),
        compiler_params=params(),
        cost_estimate=cost(0, *parts),
        name="combine",
    )(tables, *parts)
    from_core = over_core(to_core)
    flat = (n_z, node_rows, width)
    chunks = pl.pallas_call(
        add_kernel,
        out_shape=[shape(flat[1:], F32)] + [shape(flat[1:])] * (n_z - 1),
        compiler_params=params(),
        cost_estimate=cost(0, own, from_core),
        name="add_cores",
    )(own.reshape(flat), from_core.reshape(flat))
    arrived = [over_z(chunk, by) for by, chunk in enumerate(chunks[1:], 1)]
    mesh_out = pl.pallas_call(
        mesh_kernel,
        out_shape=shape((node_rows, width)),
        compiler_params=params(),
        cost_estimate=cost(4 * node_rows * width * width, mesh_up, mesh_down),
        name="mesh_step",
    )(mesh_latent, mesh_up, mesh_down, mesh_gain.reshape(1, width), chunks[0], *arrived)

    line = [mesh_out] + [over_z(mesh_out, by) for by in range(1, n_z)]
    if n_y > 1:
        line = line + [over_y(piece) for piece in line]
    pieces = []
    for piece in line:
        pieces += [piece, over_core(piece)]

    latent = latent[0]
    per_step = 2
    rows = per_step * block_rows
    steps = blk_count // per_step
    grid_out = pl.pallas_call(
        functools.partial(back_kernel, len(pieces), per_step),
        out_shape=shape((blk_count * block_rows, width)),
        grid_spec=pltpu.PrefetchScalarGridSpec(
            num_scalar_prefetch=1,
            grid=(steps,),
            in_specs=[
                pl.BlockSpec((rows, width), lambda i, _: (i, 0)),
                pl.BlockSpec((per_step,) + interp.shape[1:], lambda i, _: (i, 0, 0, 0)),
            ]
            + [pl.BlockSpec(memory_space=pl.ANY)] * len(pieces),
            out_specs=pl.BlockSpec((rows, width), lambda i, _: (i, 0)),
            scratch_shapes=[
                pltpu.VMEM((len(pieces), node_rows, width), BF16),
                pltpu.VMEM((per_step, list_len * tile_rows, width), BF16),
                pltpu.SemaphoreType.DMA((len(pieces),)),
            ],
        ),
        compiler_params=params(),
        cost_estimate=cost(
            2 * blk_count * block_rows * width * list_len * tile_rows, latent, latent, interp
        ),
        name="back",
    )(info, latent, interp, *pieces)
    return (grid_out, mesh_out)


def solution(mesh):
    placed = (
        P(("groups", "band"), None),
        P(("groups", "band"), None),
        P(),
        P(),
        P(),
        P("band", None, None, None),
        P(),
        P(),
        P(),
        P(),
        P(),
    )
    n_y = max(1, 4 // mesh.shape["groups"])
    return jax.shard_map(
        functools.partial(on_device, n_y),
        mesh=mesh,
        in_specs=placed,
        out_specs=(P(("groups", "band"), None), P(("groups", "band"), None)),
        check_vma=False,
    )
```

time: 175 us -> 135 us (0.77)
  the two profiles are of different devices: /device:TPU:0 before, /device:TPU:25 now
where the time goes in v1:
time: 135 us
  waiting for transfers between devices  70.3 us (52%)
  Pallas kernels  26.1 us (19%)
  starting transfers between devices  22.9 us (17%)
  local copies, waits for them, and re-layouts  14 us (10%)
    ppermute x23, waiting for transfers between devices, move(): return lax.ppermute(value, 'band', pairs)  70.3 us
    ppermute x23, starting transfers between devices, move(): return lax.ppermute(value, 'band', pairs)  22.9 us
    pallas_call x4, Pallas kernels, on_device(): pl.pallas_call(functools.partial(embed_kernel, slot * n_band, per_step),...  14.1 us
    unnamed x37, local copies, waits for them, and re-layouts  13.6 us
    pallas_call x1, Pallas kernels, on_device(): pl.pallas_call(functools.partial(back_kernel, len(pieces), per_step), out...  8.6 us
  transfers between devices with their start and end apart: 23, of which 14 were waited for; matrix products, arithmetic and copies ran while one was open for 0% of the time, Pallas kernels for 0%

profile of v1, /device:TPU:25, one launch (start us, length us, event | category | flops | bytes accessed | tf_op | source)
XLA Modules:
  0.0 134.6 jit_solution(6258856139287749827)
XLA Ops:
  2.7 3.2 %copy.33.x_ref = bf16[4096,227]{1,0:T(8,128)(2,1)S(1)} copy(bf16[4096,227]{0,1:T(8,128)(2,1)} %param.11) | data formatting | bytes 3719168 | tf_op args[0]
  6.1 1.0 copy-done.1
  7.1 3.5 %embed_0.1 = (bf16[4096,512]{1,0:T(8,128)(2,1)}, bf16[8,32,512]{2,1,0:T(8,128)(2,1)S(1)}, bf16[8,32,512]{2,1,0:T(8,128)(2,1)}) custom-call(s32[4,64]{1,0:T(4,128)S(1)} %pad_add_fusion.1.info_ref, bf16[4096,227]{1,0:T(8,128)(2,1)S(1)} %copy.33.x_ref, bf16[227,512]{1,0:T(8,128)(2,1)S(1)} %copy-done.2, bf16[512,512]{1,0:T(8,128)(2,1)S(1)} %copy-done.1, ...), custom_call_target="tpu_custom_call" | custom-call | flops 909115392 | bytes 2908160 | tf_op jit(solution)/shard_map/embed_0/pallas_call | solution.py:210
  11.3 3.5 %embed_1.1 = (bf16[4096,512]{1,0:T(8,128)(2,1)}, bf16[8,32,512]{2,1,0:T(8,128)(2,1)S(1)}, bf16[8,32,512]{2,1,0:T(8,128)(2,1)}) custom-call(s32[4,64]{1,0:T(4,128)S(1)} %pad_add_fusion.1.info_ref, bf16[4096,227]{1,0:T(8,128)(2,1)S(1)} %copy.33.x_ref, bf16[227,512]{1,0:T(8,128)(2,1)S(1)} %copy-done.2, ...), custom_call_target="tpu_custom_call", output_to_operand_aliasing={{0}: (6, {})} | custom-call | flops 909115392 | bytes 2908160 | tf_op jit(solution)/shard_map/embed_1/pallas_call | solution.py:210
  15.6 3.6 %embed_2.1 = (bf16[4096,512]{1,0:T(8,128)(2,1)}, bf16[8,32,512]{2,1,0:T(8,128)(2,1)S(1)}, bf16[8,32,512]{2,1,0:T(8,128)(2,1)}) custom-call(s32[4,64]{1,0:T(4,128)S(1)} %pad_add_fusion.1.info_ref, bf16[4096,227]{1,0:T(8,128)(2,1)S(1)} %copy.33.x_ref, bf16[227,512]{1,0:T(8,128)(2,1)S(1)} %copy-done.2, ...), custom_call_target="tpu_custom_call", output_to_operand_aliasing={{0}: (6, {})} | custom-call | flops 909115392 | bytes 2908160 | tf_op jit(solution)/shard_map/embed_2/pallas_call | solution.py:210
  19.8 3.5 %embed_3.1 = (bf16[4096,512]{1,0:T(8,128)(2,1)}, bf16[8,32,512]{2,1,0:T(8,128)(2,1)S(1)}, bf16[8,32,512]{2,1,0:T(8,128)(2,1)}) custom-call(s32[4,64]{1,0:T(4,128)S(1)} %pad_add_fusion.1.info_ref, bf16[4096,227]{1,0:T(8,128)(2,1)S(1)} %copy.33.x_ref, bf16[227,512]{1,0:T(8,128)(2,1)S(1)} %copy-done.2, ...), custom_call_target="tpu_custom_call", output_to_operand_aliasing={{0}: (6, {})} | custom-call | flops 909115392 | bytes 2908160 | tf_op jit(solution)/shard_map/embed_3/pallas_call | solution.py:210
  24.1 1.2 collective-permute-start.3
  25.5 1.2 collective-permute-start.1
  27.6 3.9 %collective-permute-done.3.refs_7_ = bf16[8,32,512]{2,1,0:T(8,128)(2,1)S(1)} collective-permute-done((bf16[8,32,512]{2,1,0:T(8,128)(2,1)}, bf16[8,32,512]{2,1,0:T(8,128)(2,1)S(1)}, u32[]{:S(2)}, u32[]{:S(2)}) %collective-permute-start.3) | collective-permute-done | bytes 262176 | tf_op jit(solution)/shard_map/ppermute | solution.py:166
  31.5 5.6 %collective-permute-done.2.refs_6_ = bf16[8,32,512]{2,1,0:T(8,128)(2,1)S(1)} collective-permute-done((bf16[8,32,512]{2,1,0:T(8,128)(2,1)}, bf16[8,32,512]{2,1,0:T(8,128)(2,1)S(1)}, u32[]{:S(2)}, u32[]{:S(2)}) %collective-permute-start.2) | collective-permute-done | bytes 262176 | tf_op jit(solution)/shard_map/ppermute | solution.py:166
  37.1 5.6 %collective-permute-done.1.refs_5_ = bf16[8,32,512]{2,1,0:T(8,128)(2,1)S(1)} collective-permute-done((bf16[8,32,512]{2,1,0:T(8,128)(2,1)}, bf16[8,32,512]{2,1,0:T(8,128)(2,1)S(1)}, u32[]{:S(2)}, u32[]{:S(2)}) %collective-permute-start.1) | collective-permute-done | bytes 262176 | tf_op jit(solution)/shard_map/ppermute | solution.py:166
  42.7 5.6 %collective-permute-done.refs_4_ = bf16[8,32,512]{2,1,0:T(8,128)(2,1)S(1)} collective-permute-done((bf16[8,32,512]{2,1,0:T(8,128)(2,1)}, bf16[8,32,512]{2,1,0:T(8,128)(2,1)S(1)}, u32[]{:S(2)}, u32[]{:S(2)}) %collective-permute-start) | collective-permute-done | bytes 262176 | tf_op jit(solution)/shard_map/ppermute | solution.py:166
  52.1 1.7 %combine.1 = (bf16[4,8,32,512]{3,2,1,0:T(8,128)(2,1)S(1)}, f32[4,8,32,512]{3,2,1,0:T(8,128)S(1)}) custom-call(s32[2,4,8]{2,1,0:T(4,128)S(1)} %pad_add_fusion.tile_ref, bf16[8,32,512]{2,1,0:T(8,128)(2,1)S(1)} %copy-done.8, bf16[8,32,512]{2,1,0:T(8,128)(2,1)S(1)} %copy-done.10, bf16[8,32,512]{2,1,0:T(8,128)(2,1)S(1)} %copy-done.12, ...), custom_call_target="tpu_custom_call" | custom-call | bytes 2097152 | tf_op jit(solution)/shard_map/combine/pallas_call | solution.py:249
  53.8 1.6 %collective-permute-start.4 = (bf16[4,8,32,512]{3,2,1,0:T(8,128)(2,1)S(1)}, bf16[4,8,32,512]{3,2,1,0:T(8,128)(2,1)S(1)}, u32[]{:S(2)}, u32[]{:S(2)}) collective-permute-start(bf16[4,8,32,512]{3,2,1,0:T(8,128)(2,1)S(1)} %get-tuple-element.33), channel_id=1, source_target_pairs={{0,1},{1,0},{2,3},{3,2},{4,5},{5,4},{6,7},{7,6},{8,9},{9,8},{10,11... | collective-permute-start | bytes 3145736 | tf_op jit(solution)/shard_map/ppermute | solution.py:166
  55.4 2.3 %collective-permute-done.4 = bf16[4,8,32,512]{3,2,1,0:T(8,128)(2,1)S(1)} collective-permute-done((bf16[4,8,32,512]{3,2,1,0:T(8,128)(2,1)S(1)}, bf16[4,8,32,512]{3,2,1,0:T(8,128)(2,1)S(1)}, u32[]{:S(2)}, u32[]{:S(2)}) %collective-permute-start.4) | collective-permute-done | bytes 1048608 | tf_op jit(solution)/shard_map/ppermute | solution.py:166
  57.9 1.3 collective-permute-start.6
  59.4 6.0 %collective-permute-done.5.rest_0_ = bf16[256,512]{1,0:T(8,128)(2,1)S(1)} collective-permute-done((bf16[256,512]{1,0:T(8,128)(2,1)S(1)}, bf16[256,512]{1,0:T(8,128)(2,1)S(1)}, u32[]{:S(2)}, u32[]{:S(2)}) %collective-permute-start.5) | collective-permute-done | bytes 262176 | tf_op jit(solution)/shard_map/ppermute | solution.py:166
  65.5 16.7 %collective-permute-done.6.rest_1_ = bf16[256,512]{1,0:T(8,128)(2,1)S(1)} collective-permute-done((bf16[256,512]{1,0:T(8,128)(2,1)S(1)}, bf16[256,512]{1,0:T(8,128)(2,1)S(1)}, u32[]{:S(2)}, u32[]{:S(2)}) %collective-permute-start.6) | collective-permute-done | bytes 262176 | tf_op jit(solution)/shard_map/ppermute | solution.py:166
  82.2 1.5 %mesh_step.1.rest_0_ = bf16[256,512]{1,0:T(8,128)(2,1)} custom-call(bf16[256,512]{1,0:T(8,128)(2,1)S(1)} %copy-done.6, bf16[512,512]{1,0:T(8,128)(2,1)S(1)} %copy-done.4, bf16[512,512]{1,0:T(8,128)(2,1)S(1)} %copy-done.5, f32[1,512]{1,0:T(1,128)S(1)} %bitcast.14, f32[256,512]{1,0:T(8,128)S(1)} %get-tuple-element.34.here_ref, ...), custom_call_target="tpu_custom_call" | custom-call | flops 268435456 | bytes 1048576 | tf_op jit(solution)/shard_map/mesh_step/pallas_call | solution.py:274
  83.7 1.8 %collective-permute-start.11 = (bf16[256,512]{1,0:T(8,128)(2,1)}, bf16[256,512]{1,0:T(8,128)(2,1)S(1)}, u32[]{:S(2)}, u32[]{:S(2)}) collective-permute-start(bf16[256,512]{1,0:T(8,128)(2,1)} %mesh_step.1.rest_0_), channel_id=1, source_target_pairs={{0,8},{1,9},{2,10},{3,11},{4,12},{5,13},{6,14},{7,15},{8,0},{9,1},... | collective-permute-start | bytes 786440 | tf_op jit(solution)/shard_map/ppermute | solution.py:166
  85.5 1.5 %collective-permute-start.13 = (bf16[256,512]{1,0:T(8,128)(2,1)}, bf16[256,512]{1,0:T(8,128)(2,1)S(1)}, u32[]{:S(2)}, u32[]{:S(2)}) collective-permute-start(bf16[256,512]{1,0:T(8,128)(2,1)} %mesh_step.1.rest_0_), channel_id=1, source_target_pairs={{0,12},{1,13},{2,14},{3,15},{4,0},{5,1},{6,2},{7,3},{8,4},{9,5},{1... | collective-permute-start | bytes 786440 | tf_op jit(solution)/shard_map/ppermute | solution.py:166
  86.9 1.2 collective-permute-start.15
  88.2 1.6 %collective-permute-start.8 = (bf16[256,512]{1,0:T(8,128)(2,1)}, bf16[256,512]{1,0:T(8,128)(2,1)S(1)}, u32[]{:S(2)}, u32[]{:S(2)}) collective-permute-start(bf16[256,512]{1,0:T(8,128)(2,1)} %mesh_step.1.rest_0_), channel_id=1, source_target_pairs={{0,1},{1,0},{2,3},{3,2},{4,5},{5,4},{6,7},{7,6},{8,9},{9,8},{10,11... | collective-permute-start | bytes 786440 | tf_op jit(solution)/shard_map/ppermute | solution.py:166
  90.5 1.2 collective-permute-start.17
  91.7 17.0 %collective-permute-done.11.rest_4_ = bf16[256,512]{1,0:T(8,128)(2,1)S(1)} collective-permute-done((bf16[256,512]{1,0:T(8,128)(2,1)}, bf16[256,512]{1,0:T(8,128)(2,1)S(1)}, u32[]{:S(2)}, u32[]{:S(2)}) %collective-permute-start.11) | collective-permute-done | bytes 262176 | tf_op jit(solution)/shard_map/ppermute | solution.py:166
  108.8 1.2 collective-permute-start.19
  110.3 1.6 %collective-permute-start.10 = (bf16[256,512]{1,0:T(8,128)(2,1)S(1)}, bf16[256,512]{1,0:T(8,128)(2,1)S(1)}, u32[]{:S(2)}, u32[]{:S(2)}) collective-permute-start(bf16[256,512]{1,0:T(8,128)(2,1)S(1)} %collective-permute-done.9.rest_2_), channel_id=1, source_target_pairs={{0,1},{1,0},{2,3},{3,2},{4,5},{5,4},{6,7},{7,6},{8,9},{9,8},{10,11... | collective-permute-start | bytes 786440 | tf_op jit(solution)/shard_map/ppermute | solution.py:166
  112.4 3.2 %collective-permute-done.19.rest_12_ = bf16[256,512]{1,0:T(8,128)(2,1)S(1)} collective-permute-done((bf16[256,512]{1,0:T(8,128)(2,1)S(1)}, bf16[256,512]{1,0:T(8,128)(2,1)S(1)}, u32[]{:S(2)}, u32[]{:S(2)}) %collective-permute-start.19) | collective-permute-done | bytes 262176 | tf_op jit(solution)/shard_map/ppermute | solution.py:166
  115.6 3.5 %collective-permute-start.16 = (bf16[256,512]{1,0:T(8,128)(2,1)S(1)}, bf16[256,512]{1,0:T(8,128)(2,1)S(1)}, u32[]{:S(2)}, u32[]{:S(2)}) collective-permute-start(bf16[256,512]{1,0:T(8,128)(2,1)S(1)} %collective-permute-done.15.rest_8_), channel_id=1, source_target_pairs={{0,1},{1,0},{2,3},{3,2},{4,5},{5,4},{6,7},{7,6},{8,9},{9,8},{10,11... | collective-permute-start | bytes 786440 | tf_op jit(solution)/shard_map/ppermute | solution.py:166
  119.0 2.1 %collective-permute-done.21.rest_14_ = bf16[256,512]{1,0:T(8,128)(2,1)S(1)} collective-permute-done((bf16[256,512]{1,0:T(8,128)(2,1)S(1)}, bf16[256,512]{1,0:T(8,128)(2,1)S(1)}, u32[]{:S(2)}, u32[]{:S(2)}) %collective-permute-start.21) | collective-permute-done | bytes 262176 | tf_op jit(solution)/shard_map/ppermute | solution.py:166
  121.2 1.9 %collective-permute-start.18 = (bf16[256,512]{1,0:T(8,128)(2,1)S(1)}, bf16[256,512]{1,0:T(8,128)(2,1)S(1)}, u32[]{:S(2)}, u32[]{:S(2)}) collective-permute-start(bf16[256,512]{1,0:T(8,128)(2,1)S(1)} %collective-permute-done.17.rest_10_), channel_id=1, source_target_pairs={{0,1},{1,0},{2,3},{3,2},{4,5},{5,4},{6,7},{7,6},{8,9},{9,8},{10,11... | collective-permute-start | bytes 786440 | tf_op jit(solution)/shard_map/ppermute | solution.py:166
  126.0 8.6 %back.1 = bf16[4096,512]{1,0:T(8,128)(2,1)} custom-call(s32[4,64]{1,0:T(4,128)S(1)} %pad_add_fusion.1.info_ref, bf16[4096,512]{1,0:T(8,128)(2,1)} %get-tuple-element.23.latent_ref, bf16[16,4,32,256]{3,2,1,0:T(8,128)(2,1)S(1)} %copy-done, bf16[256,512]{1,0:T(8,128)(2,1)S(1)} %copy-done.3, bf16[256,512]{1,0:T(8,128)(2,1)S(1)} %collective-permute-done.8.rest_1_, ...), custom_call_target="tpu_custom_call" | custom-call | flops 536870912 | bytes 9437184 | tf_op jit(solution)/shard_map/back/pallas_call | solution.py:293
  (72 shorter events, 14.4 us)
Async XLA Ops:
  0.6 5.4 %copy-start.15 = (f32[512]{0:T(512)S(1)}, f32[512]{0:T(512)}, u32[]{:S(2)}) copy-start(f32[512]{0:T(512)} %param.15) | copy-start | bytes 6148
  0.6 5.4 %copy-start.2 = (bf16[227,512]{1,0:T(8,128)(2,1)S(1)}, bf16[227,512]{1,0:T(8,128)(2,1)}, u32[]{:S(2)}) copy-start(bf16[227,512]{1,0:T(8,128)(2,1)} %w1_ref.7) | copy-start | bytes 697348
  0.7 5.4 %copy-start = (bf16[16,4,32,256]{3,2,1,0:T(8,128)(2,1)S(1)}, bf16[16,4,32,256]{3,2,1,0:T(8,128)(2,1)}, u32[]{:S(2)}) copy-start(bf16[16,4,32,256]{3,2,1,0:T(8,128)(2,1)} %interp_ref.9) | copy-start | bytes 3145732
  6.1 1.0 copy-start.1
  19.8 62.4 %copy-start.16 = (f32[512]{0:T(512)S(1)}, f32[512]{0:T(512)}, u32[]{:S(2)}) copy-start(f32[512]{0:T(512)} %param.21) | copy-start | bytes 6148
  24.1 58.1 %copy-start.4 = (bf16[512,512]{1,0:T(8,128)(2,1)S(1)}, bf16[512,512]{1,0:T(8,128)(2,1)}, u32[]{:S(2)}) copy-start(bf16[512,512]{1,0:T(8,128)(2,1)} %up_ref.1) | copy-start | bytes 1572868
  24.1 58.1 %copy-start.5 = (bf16[512,512]{1,0:T(8,128)(2,1)S(1)}, bf16[512,512]{1,0:T(8,128)(2,1)}, u32[]{:S(2)}) copy-start(bf16[512,512]{1,0:T(8,128)(2,1)} %down_ref.1) | copy-start | bytes 1572868
  24.1 58.1 %copy-start.6 = (bf16[256,512]{1,0:T(8,128)(2,1)S(1)}, bf16[256,512]{1,0:T(8,128)(2,1)}, u32[]{:S(2)}) copy-start(bf16[256,512]{1,0:T(8,128)(2,1)} %latent_ref.1) | copy-start | bytes 786436
  24.1 7.4 %collective-permute-start.3 = (bf16[8,32,512]{2,1,0:T(8,128)(2,1)}, bf16[8,32,512]{2,1,0:T(8,128)(2,1)S(1)}, u32[]{:S(2)}, u32[]{:S(2)}) collective-permute-start(bf16[8,32,512]{2,1,0:T(8,128)(2,1)} %get-tuple-element.31), channel_id=1, source_target_pairs={{0,2},{1,3},{2,0},{3,1},{4,6},{5,7},{6,4},{7,5},{8,10},{9,11},{10,... | collective-permute-start | bytes 786440 | tf_op jit(solution)/shard_map/ppermute | solution.py:166
  25.3 11.8 %collective-permute-start.2 = (bf16[8,32,512]{2,1,0:T(8,128)(2,1)}, bf16[8,32,512]{2,1,0:T(8,128)(2,1)S(1)}, u32[]{:S(2)}, u32[]{:S(2)}) collective-permute-start(bf16[8,32,512]{2,1,0:T(8,128)(2,1)} %get-tuple-element.30), channel_id=1, source_target_pairs={{0,2},{1,3},{2,0},{3,1},{4,6},{5,7},{6,4},{7,5},{8,10},{9,11},{10,... | collective-permute-start | bytes 786440 | tf_op jit(solution)/shard_map/ppermute | solution.py:166
  25.5 17.2 %collective-permute-start.1 = (bf16[8,32,512]{2,1,0:T(8,128)(2,1)}, bf16[8,32,512]{2,1,0:T(8,128)(2,1)S(1)}, u32[]{:S(2)}, u32[]{:S(2)}) collective-permute-start(bf16[8,32,512]{2,1,0:T(8,128)(2,1)} %get-tuple-element.29), channel_id=1, source_target_pairs={{0,2},{1,3},{2,0},{3,1},{4,6},{5,7},{6,4},{7,5},{8,10},{9,11},{10,... | collective-permute-start | bytes 786440 | tf_op jit(solution)/shard_map/ppermute | solution.py:166
  26.8 21.5 %collective-permute-start = (bf16[8,32,512]{2,1,0:T(8,128)(2,1)}, bf16[8,32,512]{2,1,0:T(8,128)(2,1)S(1)}, u32[]{:S(2)}, u32[]{:S(2)}) collective-permute-start(bf16[8,32,512]{2,1,0:T(8,128)(2,1)} %get-tuple-element.28), channel_id=1, source_target_pairs={{0,2},{1,3},{2,0},{3,1},{4,6},{5,7},{6,4},{7,5},{8,10},{9,11},{10,... | collective-permute-start | bytes 786440 | tf_op jit(solution)/shard_map/ppermute | solution.py:166
  48.3 1.0 copy-start.8
  53.8 3.9 %collective-permute-start.4 = (bf16[4,8,32,512]{3,2,1,0:T(8,128)(2,1)S(1)}, bf16[4,8,32,512]{3,2,1,0:T(8,128)(2,1)S(1)}, u32[]{:S(2)}, u32[]{:S(2)}) collective-permute-start(bf16[4,8,32,512]{3,2,1,0:T(8,128)(2,1)S(1)} %get-tuple-element.33), channel_id=1, source_target_pairs={{0,1},{1,0},{2,3},{3,2},{4,5},{5,4},{6,7},{7,6},{8,9},{9,8},{10,11... | collective-permute-start | bytes 3145736 | tf_op jit(solution)/shard_map/ppermute | solution.py:166
  57.9 7.6 %collective-permute-start.5 = (bf16[256,512]{1,0:T(8,128)(2,1)S(1)}, bf16[256,512]{1,0:T(8,128)(2,1)S(1)}, u32[]{:S(2)}, u32[]{:S(2)}) collective-permute-start(bf16[256,512]{1,0:T(8,128)(2,1)S(1)} %get-tuple-element.35), channel_id=1, source_target_pairs={{0,4},{1,5},{2,6},{3,7},{4,8},{5,9},{6,10},{7,11},{8,12},{9,13},{1... | collective-permute-start | bytes 786440 | tf_op jit(solution)/shard_map/ppermute | solution.py:166
  57.9 24.2 %collective-permute-start.6 = (bf16[256,512]{1,0:T(8,128)(2,1)S(1)}, bf16[256,512]{1,0:T(8,128)(2,1)S(1)}, u32[]{:S(2)}, u32[]{:S(2)}) collective-permute-start(bf16[256,512]{1,0:T(8,128)(2,1)S(1)} %get-tuple-element.36), channel_id=1, source_target_pairs={{0,8},{1,9},{2,10},{3,11},{4,12},{5,13},{6,14},{7,15},{8,0},{9,1},... | collective-permute-start | bytes 786440 | tf_op jit(solution)/shard_map/ppermute | solution.py:166
  59.3 22.9 %collective-permute-start.7 = (bf16[256,512]{1,0:T(8,128)(2,1)S(1)}, bf16[256,512]{1,0:T(8,128)(2,1)S(1)}, u32[]{:S(2)}, u32[]{:S(2)}) collective-permute-start(bf16[256,512]{1,0:T(8,128)(2,1)S(1)} %get-tuple-element.37), channel_id=1, source_target_pairs={{0,12},{1,13},{2,14},{3,15},{4,0},{5,1},{6,2},{7,3},{8,4},{9,5},{1... | collective-permute-start | bytes 786440 | tf_op jit(solution)/shard_map/ppermute | solution.py:166
  83.7 6.8 %collective-permute-start.9 = (bf16[256,512]{1,0:T(8,128)(2,1)}, bf16[256,512]{1,0:T(8,128)(2,1)S(1)}, u32[]{:S(2)}, u32[]{:S(2)}) collective-permute-start(bf16[256,512]{1,0:T(8,128)(2,1)} %mesh_step.1.rest_0_), channel_id=1, source_target_pairs={{0,4},{1,5},{2,6},{3,7},{4,8},{5,9},{6,10},{7,11},{8,12},{9,13},{1... | collective-permute-start | bytes 786440 | tf_op jit(solution)/shard_map/ppermute | solution.py:166
  83.7 25.1 %collective-permute-start.11 = (bf16[256,512]{1,0:T(8,128)(2,1)}, bf16[256,512]{1,0:T(8,128)(2,1)S(1)}, u32[]{:S(2)}, u32[]{:S(2)}) collective-permute-start(bf16[256,512]{1,0:T(8,128)(2,1)} %mesh_step.1.rest_0_), channel_id=1, source_target_pairs={{0,8},{1,9},{2,10},{3,11},{4,12},{5,13},{6,14},{7,15},{8,0},{9,1},... | collective-permute-start | bytes 786440 | tf_op jit(solution)/shard_map/ppermute | solution.py:166
  85.5 24.5 %collective-permute-start.13 = (bf16[256,512]{1,0:T(8,128)(2,1)}, bf16[256,512]{1,0:T(8,128)(2,1)S(1)}, u32[]{:S(2)}, u32[]{:S(2)}) collective-permute-start(bf16[256,512]{1,0:T(8,128)(2,1)} %mesh_step.1.rest_0_), channel_id=1, source_target_pairs={{0,12},{1,13},{2,14},{3,15},{4,0},{5,1},{6,2},{7,3},{8,4},{9,5},{1... | collective-permute-start | bytes 786440 | tf_op jit(solution)/shard_map/ppermute | solution.py:166
  86.9 23.3 %collective-permute-start.15 = (bf16[256,512]{1,0:T(8,128)(2,1)}, bf16[256,512]{1,0:T(8,128)(2,1)S(1)}, u32[]{:S(2)}, u32[]{:S(2)}) collective-permute-start(bf16[256,512]{1,0:T(8,128)(2,1)} %mesh_step.1.rest_0_), channel_id=1, source_target_pairs={{0,2},{1,3},{2,0},{3,1},{4,6},{5,7},{6,4},{7,5},{8,10},{9,11},{10,... | collective-permute-start | bytes 786440 | tf_op jit(solution)/shard_map/ppermute | solution.py:166
  88.2 23.7 %collective-permute-start.8 = (bf16[256,512]{1,0:T(8,128)(2,1)}, bf16[256,512]{1,0:T(8,128)(2,1)S(1)}, u32[]{:S(2)}, u32[]{:S(2)}) collective-permute-start(bf16[256,512]{1,0:T(8,128)(2,1)} %mesh_step.1.rest_0_), channel_id=1, source_target_pairs={{0,1},{1,0},{2,3},{3,2},{4,5},{5,4},{6,7},{7,6},{8,9},{9,8},{10,11... | collective-permute-start | bytes 786440 | tf_op jit(solution)/shard_map/ppermute | solution.py:166
  90.5 21.4 %collective-permute-start.17 = (bf16[256,512]{1,0:T(8,128)(2,1)S(1)}, bf16[256,512]{1,0:T(8,128)(2,1)S(1)}, u32[]{:S(2)}, u32[]{:S(2)}) collective-permute-start(bf16[256,512]{1,0:T(8,128)(2,1)S(1)} %collective-permute-done.9.rest_2_), channel_id=1, source_target_pairs={{0,2},{1,3},{2,0},{3,1},{4,6},{5,7},{6,4},{7,5},{8,10},{9,11},{10,... | collective-permute-start | bytes 786440 | tf_op jit(solution)/shard_map/ppermute | solution.py:166
  108.8 6.8 %collective-permute-start.19 = (bf16[256,512]{1,0:T(8,128)(2,1)S(1)}, bf16[256,512]{1,0:T(8,128)(2,1)S(1)}, u32[]{:S(2)}, u32[]{:S(2)}) collective-permute-start(bf16[256,512]{1,0:T(8,128)(2,1)S(1)} %collective-permute-done.11.rest_4_), channel_id=1, source_target_pairs={{0,2},{1,3},{2,0},{3,1},{4,6},{5,7},{6,4},{7,5},{8,10},{9,11},{10,... | collective-permute-start | bytes 786440 | tf_op jit(solution)/shard_map/ppermute | solution.py:166
  110.0 11.2 %collective-permute-start.21 = (bf16[256,512]{1,0:T(8,128)(2,1)S(1)}, bf16[256,512]{1,0:T(8,128)(2,1)S(1)}, u32[]{:S(2)}, u32[]{:S(2)}) collective-permute-start(bf16[256,512]{1,0:T(8,128)(2,1)S(1)} %collective-permute-done.13.rest_6_), channel_id=1, source_target_pairs={{0,2},{1,3},{2,0},{3,1},{4,6},{5,7},{6,4},{7,5},{8,10},{9,11},{10,... | collective-permute-start | bytes 786440 | tf_op jit(solution)/shard_map/ppermute | solution.py:166
  110.3 12.9 %collective-permute-start.10 = (bf16[256,512]{1,0:T(8,128)(2,1)S(1)}, bf16[256,512]{1,0:T(8,128)(2,1)S(1)}, u32[]{:S(2)}, u32[]{:S(2)}) collective-permute-start(bf16[256,512]{1,0:T(8,128)(2,1)S(1)} %collective-permute-done.9.rest_2_), channel_id=1, source_target_pairs={{0,1},{1,0},{2,3},{3,2},{4,5},{5,4},{6,7},{7,6},{8,9},{9,8},{10,11... | collective-permute-start | bytes 786440 | tf_op jit(solution)/shard_map/ppermute | solution.py:166
  111.8 11.3 %collective-permute-start.12 = (bf16[256,512]{1,0:T(8,128)(2,1)S(1)}, bf16[256,512]{1,0:T(8,128)(2,1)S(1)}, u32[]{:S(2)}, u32[]{:S(2)}) collective-permute-start(bf16[256,512]{1,0:T(8,128)(2,1)S(1)} %collective-permute-done.11.rest_4_), channel_id=1, source_target_pairs={{0,1},{1,0},{2,3},{3,2},{4,5},{5,4},{6,7},{7,6},{8,9},{9,8},{10,11... | collective-permute-start | bytes 786440 | tf_op jit(solution)/shard_map/ppermute | solution.py:166
  111.9 11.7 %collective-permute-start.14 = (bf16[256,512]{1,0:T(8,128)(2,1)S(1)}, bf16[256,512]{1,0:T(8,128)(2,1)S(1)}, u32[]{:S(2)}, u32[]{:S(2)}) collective-permute-start(bf16[256,512]{1,0:T(8,128)(2,1)S(1)} %collective-permute-done.13.rest_6_), channel_id=1, source_target_pairs={{0,1},{1,0},{2,3},{3,2},{4,5},{5,4},{6,7},{7,6},{8,9},{9,8},{10,11... | collective-permute-start | bytes 786440 | tf_op jit(solution)/shard_map/ppermute | solution.py:166
  115.6 8.1 %collective-permute-start.16 = (bf16[256,512]{1,0:T(8,128)(2,1)S(1)}, bf16[256,512]{1,0:T(8,128)(2,1)S(1)}, u32[]{:S(2)}, u32[]{:S(2)}) collective-permute-start(bf16[256,512]{1,0:T(8,128)(2,1)S(1)} %collective-permute-done.15.rest_8_), channel_id=1, source_target_pairs={{0,1},{1,0},{2,3},{3,2},{4,5},{5,4},{6,7},{7,6},{8,9},{9,8},{10,11... | collective-permute-start | bytes 786440 | tf_op jit(solution)/shard_map/ppermute | solution.py:166
  121.2 3.1 %collective-permute-start.18 = (bf16[256,512]{1,0:T(8,128)(2,1)S(1)}, bf16[256,512]{1,0:T(8,128)(2,1)S(1)}, u32[]{:S(2)}, u32[]{:S(2)}) collective-permute-start(bf16[256,512]{1,0:T(8,128)(2,1)S(1)} %collective-permute-done.17.rest_10_), channel_id=1, source_target_pairs={{0,1},{1,0},{2,3},{3,2},{4,5},{5,4},{6,7},{7,6},{8,9},{9,8},{10,11... | collective-permute-start | bytes 786440 | tf_op jit(solution)/shard_map/ppermute | solution.py:166
  123.1 1.5 %collective-permute-start.20 = (bf16[256,512]{1,0:T(8,128)(2,1)S(1)}, bf16[256,512]{1,0:T(8,128)(2,1)S(1)}, u32[]{:S(2)}, u32[]{:S(2)}) collective-permute-start(bf16[256,512]{1,0:T(8,128)(2,1)S(1)} %collective-permute-done.19.rest_12_), channel_id=1, source_target_pairs={{0,1},{1,0},{2,3},{3,2},{4,5},{5,4},{6,7},{7,6},{8,9},{9,8},{10,11... | collective-permute-start | bytes 786440 | tf_op jit(solution)/shard_map/ppermute | solution.py:166
  123.1 1.9 %collective-permute-start.22 = (bf16[256,512]{1,0:T(8,128)(2,1)S(1)}, bf16[256,512]{1,0:T(8,128)(2,1)S(1)}, u32[]{:S(2)}, u32[]{:S(2)}) collective-permute-start(bf16[256,512]{1,0:T(8,128)(2,1)S(1)} %collective-permute-done.21.rest_14_), channel_id=1, source_target_pairs={{0,1},{1,0},{2,3},{3,2},{4,5},{5,4},{6,7},{7,6},{8,9},{9,8},{10,11... | collective-permute-start | bytes 786440 | tf_op jit(solution)/shard_map/ppermute | solution.py:166
  (8 other events, 6.6 us)

commit v2 on v1

v2 whole, which is shorter than its diff:
```python
import functools

import jax
import jax.numpy as jnp
from jax import lax
from jax.experimental import pallas as pl
from jax.experimental.pallas import tpu as pltpu
from jax.sharding import PartitionSpec as P

F32 = jnp.float32
BF16 = jnp.bfloat16
VMEM_LIMIT = 56 * 1024 * 1024


def silu(values):
    half = 0.5 * values
    return half * (1.0 + jnp.tanh(half))


def layer_norm(values, gain):
    centred = values - jnp.mean(values, axis=-1, keepdims=True)
    spread = jnp.mean(centred * centred, axis=-1, keepdims=True)
    return centred * lax.rsqrt(spread + 1e-05) * gain


def embed_kernel(
    per_step, info_ref, x_ref, w1_ref, w2_ref, gain_ref, interp_ref, latent_ref, *rest
):
    outs, placed = rest[:-1], rest[-1]
    step = pl.program_id(0)
    list_len, tile_rows, block_rows = interp_ref.shape[1:]
    first = lax.dot_general(
        x_ref[...], w1_ref[...], (((0,), (0,)), ((), ())), preferred_element_type=F32
    )
    before = jnp.dot(silu(first).astype(BF16), w2_ref[...], preferred_element_type=F32)
    latent = layer_norm(before, gain_ref[...]).astype(BF16)
    latent_ref[...] = latent
    for b in range(per_step):
        weights = interp_ref[b].reshape(list_len * tile_rows, block_rows)
        part = jnp.dot(
            weights, latent[b * block_rows : (b + 1) * block_rows], preferred_element_type=F32
        )
        for k in range(list_len):
            entry = (step * per_step + b) * list_len + k
            masked = part[k * tile_rows : (k + 1) * tile_rows] * info_ref[1, entry].astype(F32)
            placed[info_ref[0, entry]] = masked.astype(BF16)

    @pl.when(step == pl.num_programs(0) - 1)
    def _():
        count = outs[0].shape[0]
        for number, out in enumerate(outs):
            out[...] = placed[number * count : (number + 1) * count]


def add_entries(total, table_ref, base, parts):
    for way, part in enumerate(parts):
        for slot in range(part.shape[0]):
            total[table_ref[way, base + slot]] += part[slot].astype(F32)


def chunk_kernel(slots, distance, chips, table_ref, *refs):
    kept, other, came = refs[0:2], refs[2:4], refs[4:-3]
    outs, total = refs[-3:-1], refs[-1]
    tiles = total.shape[0]
    half = tiles // 2
    for side in range(2):
        lower = slice(0, half) if side == 0 else slice(half, tiles)
        if not came:
            total[...] = jnp.zeros_like(total)
        elif came[side].shape[0] == tiles:
            total[...] = came[side][...].astype(F32)
        else:
            total[...] = jnp.zeros_like(total)
            total[lower] = came[side][...].astype(F32)
        owner = distance if side == 0 else chips - distance
        add_entries(total, table_ref, owner * slots, [kept[side], other[side]])
        out = outs[side]
        out[...] = (total[...] if out.shape[0] == tiles else total[lower]).astype(BF16)


def mesh_kernel(table_ref, latent_ref, up_ref, down_ref, gain_ref, kept, other, *rest):
    came, out_ref, total = rest[:-2], rest[-2], rest[-1]
    tiles, tile_rows, width = total.shape
    half = tiles // 2
    total[...] = latent_ref[...].astype(F32).reshape(total.shape)
    for side, value in enumerate(came):
        if value.shape[0] == tiles:
            total[...] += value[...].astype(F32)
        else:
            part = slice(0, half) if side == 0 else slice(half, tiles)
            total[part] += value[...].astype(F32)
    add_entries(total, table_ref, 0, [kept, other])
    mesh_in = total[...].reshape(tiles * tile_rows, width)
    normed = layer_norm(mesh_in, gain_ref[...]).astype(BF16)
    hidden = silu(jnp.dot(normed, up_ref[...], preferred_element_type=F32)).astype(BF16)
    out_ref[...] = (
        mesh_in + jnp.dot(hidden, down_ref[...], preferred_element_type=F32)
    ).astype(BF16)


def back_kernel(places, per_step, info_ref, latent_ref, interp_ref, *rest):
    count = len(places)
    pieces, (out_ref, held, picked, sems) = rest[:count], rest[count:]
    step = pl.program_id(0)
    list_len, tile_rows, block_rows = interp_ref.shape[1:]

    @pl.when(step == 0)
    def _():
        copies = []
        for i, (place, row) in enumerate(places):
            into = held.at[place, pl.ds(row, pieces[i].shape[0])]
            copies.append(pltpu.make_async_copy(pieces[i], into, sems.at[i]))
        for copy in copies:
            copy.start()
        for copy in copies:
            copy.wait()

    for b in range(per_step):
        for k in range(list_len):
            entry = (step * per_step + b) * list_len + k
            rows = pl.ds(pl.multiple_of(info_ref[2, entry] * tile_rows, tile_rows), tile_rows)
            value = held[info_ref[3, entry], rows].astype(F32) * info_ref[1, entry].astype(F32)
            picked[b, k * tile_rows : (k + 1) * tile_rows] = value.astype(BF16)
        weights = interp_ref[b].reshape(list_len * tile_rows, block_rows)
        back = lax.dot_general(
            weights, picked[b], (((0,), (0,)), ((), ())), preferred_element_type=F32
        )
        rows = slice(b * block_rows, (b + 1) * block_rows)
        out_ref[rows] = (latent_ref[rows].astype(F32) + back).astype(BF16)


def whole(array):
    zeros = (0,) * array.ndim
    return pl.BlockSpec(array.shape, lambda *_: zeros)


def params():
    return pltpu.CompilerParams(vmem_limit_bytes=VMEM_LIMIT)


def cost(flops, *arrays):
    size = sum(a.size * a.dtype.itemsize for a in arrays)
    return pl.CostEstimate(flops=int(flops), bytes_accessed=int(size), transcendentals=0)


def shape(dims, kind=BF16):
    return jax.ShapeDtypeStruct(dims, kind)


def on_device(
    n_y,
    grid_features,
    mesh_latent,
    embed_in,
    embed_out,
    embed_gain,
    interp,
    block_mask,
    tile_list,
    mesh_up,
    mesh_down,
    mesh_gain,
):
    n_band = lax.axis_size("band")
    n_core = 2
    chips = n_band // n_core
    n_z = chips // n_y
    me = lax.axis_index("band")
    blk_count, list_len, tile_rows, block_rows = interp.shape
    channels, width = embed_in.shape
    node_rows = mesh_latent.shape[0]
    tiles_here = node_rows // tile_rows
    entries = blk_count * list_len
    slots = entries // n_band
    far = chips // 2

    def ring_of(index):
        z, y = index // (n_y * n_core), index // n_core % n_y
        return z + y * (chips - 1 - 2 * z)

    def index_at(ring, core):
        ring = ring % chips
        z, y = (ring, 0) if ring < n_z else (chips - 1 - ring, 1)
        return (z * n_y + y) * n_core + core

    def over_core(value):
        return lax.ppermute(value, "band", [(i, i ^ 1) for i in range(n_band)])

    def over_ring(value, by):
        pairs = [(i, index_at(ring_of(i) + by, i % n_core)) for i in range(n_band)]
        return lax.ppermute(value, "band", pairs)

    def mine(table, index):
        rows = lax.dynamic_slice_in_dim(table.T, index * blk_count, blk_count, 1)
        return rows.T.reshape(entries)

    def relative(index):
        tiles = mine(tile_list, index)
        owner = tiles // tiles_here
        return (ring_of(owner) - ring_of(index)) % chips, (owner - index) % n_core, tiles % tiles_here

    slot_of = jnp.arange(entries, dtype=jnp.int32) // n_band
    ahead, across, local = relative(me)
    info = jnp.stack(
        [(across * chips + ahead) * slots + slot_of, mine(block_mask, me), local, ahead * n_core + across]
    )

    def by_place(ahead, across, local, which):
        place = jnp.where(across == which, ahead * slots + slot_of, -1)
        spots = jnp.arange(chips * slots, dtype=jnp.int32)
        return jnp.sum(jnp.where(place[:, None] == spots, local[:, None], 0), axis=0)

    tables = jnp.stack(
        [by_place(ahead, across, local, 0), by_place(*relative(me + 1 - me % 2 * 2), 1)]
    )

    gain = embed_gain.reshape(1, width)
    per_step = 2
    rows = per_step * block_rows
    held_shape = (chips * slots, tile_rows, width)
    latent, kept, sent = pl.pallas_call(
        functools.partial(embed_kernel, per_step),
        out_shape=[shape((blk_count * block_rows, width))] + [shape(held_shape)] * n_core,
        grid_spec=pltpu.PrefetchScalarGridSpec(
            num_scalar_prefetch=1,
            grid=(blk_count // per_step,),
            in_specs=[
                pl.BlockSpec((channels, rows), lambda i, _: (0, i)),
                whole(embed_in),
                whole(embed_out),
                whole(gain),
                pl.BlockSpec((per_step,) + interp.shape[1:], lambda i, _: (i, 0, 0, 0)),
            ],
            out_specs=[pl.BlockSpec((rows, width), lambda i, _: (i, 0))]
            + [pl.BlockSpec(held_shape, lambda i, _: (0, 0, 0))] * n_core,
            scratch_shapes=[pltpu.VMEM((entries, tile_rows, width), BF16)],
        ),
        compiler_params=params(),
        cost_estimate=cost(
            2 * blk_count * block_rows * width * (channels + width + list_len * tile_rows),
            grid_features,
            interp,
        ),
        name="embed",
    )(info, grid_features.T, embed_in, embed_out, gain, interp)
    other = over_core(sent)

    def entries_of(owner):
        return pl.BlockSpec((slots, tile_rows, width), lambda i, _: (owner, 0, 0))

    dense = (tiles_here, tile_rows, width)
    came = []
    for distance in range(far, 0, -1):
        out = (tiles_here // 2,) + dense[1:] if distance == far else dense
        sides = [entries_of(distance), entries_of(chips - distance)]
        chunks = pl.pallas_call(
            functools.partial(chunk_kernel, slots, distance, chips),
            out_shape=[shape(out)] * 2,
            grid_spec=pltpu.PrefetchScalarGridSpec(
                num_scalar_prefetch=1,
                grid=(1,),
                in_specs=sides + sides + [whole(c) for c in came],
                out_specs=[pl.BlockSpec(out, lambda i, _: (0, 0, 0))] * 2,
                scratch_shapes=[pltpu.VMEM(dense, F32)],
            ),
            compiler_params=params(),
            cost_estimate=cost(0, *came, *came),
            name=f"chunk_{distance}",
        )(tables, kept, kept, other, other, *came)
        came = [over_ring(chunks[0], 1), over_ring(chunks[1], -1)]

    mesh_gain = mesh_gain.reshape(1, width)
    mesh_out = pl.pallas_call(
        mesh_kernel,
        out_shape=shape((node_rows, width)),
        grid_spec=pltpu.PrefetchScalarGridSpec(
            num_scalar_prefetch=1,
            grid=(1,),
            in_specs=[whole(a) for a in (mesh_latent, mesh_up, mesh_down, mesh_gain)]
            + [entries_of(0)] * 2
            + [whole(c) for c in came],
            out_specs=pl.BlockSpec((node_rows, width), lambda i, _: (0, 0)),
            scratch_shapes=[pltpu.VMEM(dense, F32)],
        ),
        compiler_params=params(),
        cost_estimate=cost(4 * node_rows * width * width, mesh_up, mesh_down),
        name="mesh_step",
    )(tables, mesh_latent, mesh_up, mesh_down, mesh_gain, kept, other, *came)

    pieces, places = [], []

    def keep(piece, owner, row=0):
        for across, value in enumerate((piece, over_core(piece))):
            pieces.append(value)
            places.append((owner % chips * n_core + across, row))

    right = left = mesh_out
    for distance in range(1, far):
        right, left = over_ring(right, 1), over_ring(left, -1)
        if distance == 1:
            keep(mesh_out, 0)
        keep(right, -distance)
        keep(left, distance)
    half = node_rows // 2
    right, left = over_ring(right[:half], 1), over_ring(left[half:], -1)
    keep(right, far)
    keep(left, far, half)

    per_step = 2
    rows = per_step * block_rows
    grid_out = pl.pallas_call(
        functools.partial(back_kernel, places, per_step),
        out_shape=shape((blk_count * block_rows, width)),
        grid_spec=pltpu.PrefetchScalarGridSpec(
            num_scalar_prefetch=1,
            grid=(blk_count // per_step,),
            in_specs=[
                pl.BlockSpec((rows, width), lambda i, _: (i, 0)),
                pl.BlockSpec((per_step,) + interp.shape[1:], lambda i, _: (i, 0, 0, 0)),
            ]
            + [pl.BlockSpec(memory_space=pl.ANY)] * len(pieces),
            out_specs=pl.BlockSpec((rows, width), lambda i, _: (i, 0)),
            scratch_shapes=[
                pltpu.VMEM((n_band, node_rows, width), BF16),
                pltpu.VMEM((per_step, list_len * tile_rows, width), BF16),
                pltpu.SemaphoreType.DMA((len(pieces),)),
            ],
        ),
        compiler_params=params(),
        cost_estimate=cost(
            2 * blk_count * block_rows * width * list_len * tile_rows, latent, latent, interp
        ),
        name="back",
    )(info, latent, interp, *pieces)
    return (grid_out, mesh_out)


def solution(mesh):
    placed = (
        P(("groups", "band"), None),
        P(("groups", "band"), None),
        P(),
        P(),
        P(),
        P("band", None, None, None),
        P(),
        P(),
        P(),
        P(),
        P(),
    )
    n_y = max(1, 4 // mesh.shape["groups"])
    return jax.shard_map(
        functools.partial(on_device, n_y),
        mesh=mesh,
        in_specs=placed,
        out_specs=(P(("groups", "band"), None), P(("groups", "band"), None)),
        check_vma=False,
    )
```

time: 135 us -> 115 us (0.85)
  the two profiles are of different devices: /device:TPU:25 before, /device:TPU:0 now
where the time goes in v2:
time: 115 us
  waiting for transfers between devices  48.4 us (42%)
  Pallas kernels  38.4 us (33%)
  starting transfers between devices  18.8 us (16%)
  local copies, waits for them, and re-layouts  6.47 us (6%)
  other arithmetic  1.48 us (1%)
    ppermute x16, waiting for transfers between devices, over_ring(): return lax.ppermute(value, 'band', pairs)  45.8 us
    ppermute x16, starting transfers between devices, over_ring(): return lax.ppermute(value, 'band', pairs)  17.2 us
    pallas_call x1, Pallas kernels, on_device(): pl.pallas_call(functools.partial(embed_kernel, per_step), out_shape=[shap...  12.6 us
    pallas_call x4, Pallas kernels, on_device(): pl.pallas_call(functools.partial(chunk_kernel, slots, distance, chips), o...  11.3 us
    pallas_call x1, Pallas kernels, on_device(): pl.pallas_call(functools.partial(back_kernel, places, per_step), out_shap...  10.7 us
    unnamed x54, local copies, waits for them, and re-layouts  4.94 us
    pallas_call x1, Pallas kernels, on_device(): pl.pallas_call(mesh_kernel, out_shape=shape((node_rows, width)), grid_spe...  3.85 us
    ppermute x10, waiting for transfers between devices, over_core(): return lax.ppermute(value, 'band', [(i, i ^ 1) for i in range(n_band)])  2.66 us
  transfers between devices with their start and end apart: 26, of which 16 were waited for; matrix products, arithmetic and copies ran while one was open for 1% of the time, Pallas kernels for 0%

profile of v2, /device:TPU:0, one launch (start us, length us, event | category | flops | bytes accessed | tf_op | source)
XLA Modules:
  0.0 114.6 jit_solution(7604580987297440089)
XLA Ops:
  3.3 12.6 %embed.1 = (bf16[4096,512]{1,0:T(8,128)(2,1)}, bf16[32,32,512]{2,1,0:T(8,128)(2,1)}, bf16[32,32,512]{2,1,0:T(8,128)(2,1)}) custom-call(s32[4,64]{1,0:T(4,128)} %pad_add_fusion.info_ref, bf16[227,4096]{1,0:T(8,128)(2,1)} %bitcast.8, bf16[227,512]{1,0:T(8,128)(2,1)} %w1_ref.1, bf16[512,512]{1,0:T(8,128)(2,1)} %w2_ref.1, f32[1,512]{1,0:T(1,128)} %bitcast.9, ...), custom_call_target="tpu_custom_call" | custom-call | flops 3636461568 | bytes 2908160 | tf_op jit(solution)/shard_map/embed/pallas_call | solution.py:221
  17.4 1.4 %collective-permute-done.refs_2_.refs_3_.other = bf16[32,32,512]{2,1,0:T(8,128)(2,1)S(1)} collective-permute-done((bf16[32,32,512]{2,1,0:T(8,128)(2,1)}, bf16[32,32,512]{2,1,0:T(8,128)(2,1)S(1)}, u32[]{:S(2)}, u32[]{:S(2)}) %collective-permute-start) | collective-permute-done | bytes 1048608 | tf_op jit(solution)/shard_map/ppermute | solution.py:187
  18.8 1.0 copy-done.1
  19.8 2.6 %chunk_4.1 = (bf16[4,32,512]{2,1,0:T(8,128)(2,1)}, bf16[4,32,512]{2,1,0:T(8,128)(2,1)}) custom-call(s32[2,32]{1,0:T(2,128)} %pad_add_fusion.1.table_ref, bf16[32,32,512]{2,1,0:T(8,128)(2,1)} %get-tuple-element.14.refs_0_.refs_1_.kept, bf16[32,32,512]{2,1,0:T(8,128)(2,1)} %get-tuple-element.14.refs_0_.refs_1_.kept, bf16[32,32,512]{2,1,0:T(8,128)(2,1)} %copy-done.1, ...), custom_call_target="tpu_custom_call" | custom-call | tf_op jit(solution)/shard_map/chunk_4/pallas_call | solution.py:256
  22.4 2.9 %collective-permute-start.1 = (bf16[4,32,512]{2,1,0:T(8,128)(2,1)}, bf16[4,32,512]{2,1,0:T(8,128)(2,1)S(1)}, u32[]{:S(2)}, u32[]{:S(2)}) collective-permute-start(bf16[4,32,512]{2,1,0:T(8,128)(2,1)} %get-tuple-element.16), channel_id=1, source_target_pairs={{0,4},{1,5},{2,0},{3,1},{4,8},{5,9},{6,2},{7,3},{8,12},{9,13},{10,... | collective-permute-start | bytes 393224 | tf_op jit(solution)/shard_map/ppermute | solution.py:191
  25.3 4.0 %collective-permute-done.1.refs_4_ = bf16[4,32,512]{2,1,0:T(8,128)(2,1)S(1)} collective-permute-done((bf16[4,32,512]{2,1,0:T(8,128)(2,1)}, bf16[4,32,512]{2,1,0:T(8,128)(2,1)S(1)}, u32[]{:S(2)}, u32[]{:S(2)}) %collective-permute-start.1) | collective-permute-done | bytes 131104 | tf_op jit(solution)/shard_map/ppermute | solution.py:191
  29.3 1.5 %collective-permute-done.2.refs_5_ = bf16[4,32,512]{2,1,0:T(8,128)(2,1)S(1)} collective-permute-done((bf16[4,32,512]{2,1,0:T(8,128)(2,1)}, bf16[4,32,512]{2,1,0:T(8,128)(2,1)S(1)}, u32[]{:S(2)}, u32[]{:S(2)}) %collective-permute-start.2) | collective-permute-done | bytes 131104 | tf_op jit(solution)/shard_map/ppermute | solution.py:191
  31.5 2.8 %chunk_3.1 = (bf16[8,32,512]{2,1,0:T(8,128)(2,1)}, bf16[8,32,512]{2,1,0:T(8,128)(2,1)}) custom-call(s32[2,32]{1,0:T(2,128)} %pad_add_fusion.1.table_ref, bf16[32,32,512]{2,1,0:T(8,128)(2,1)} %get-tuple-element.14.refs_0_.refs_1_.kept, bf16[32,32,512]{2,1,0:T(8,128)(2,1)} %get-tuple-element.14.refs_0_.refs_1_.kept, bf16[32,32,512]{2,1,0:T(8,128)(2,1)} %copy-done.1, ...), custom_call_target="tpu_custom_call" | custom-call | bytes 524288 | tf_op jit(solution)/shard_map/chunk_3/pallas_call | solution.py:256
  34.3 1.6 %collective-permute-start.3 = (bf16[8,32,512]{2,1,0:T(8,128)(2,1)}, bf16[8,32,512]{2,1,0:T(8,128)(2,1)S(1)}, u32[]{:S(2)}, u32[]{:S(2)}) collective-permute-start(bf16[8,32,512]{2,1,0:T(8,128)(2,1)} %get-tuple-element.18), channel_id=1, source_target_pairs={{0,4},{1,5},{2,0},{3,1},{4,8},{5,9},{6,2},{7,3},{8,12},{9,13},{10,... | collective-permute-start | bytes 786440 | tf_op jit(solution)/shard_map/ppermute | solution.py:191
  36.3 5.4 %collective-permute-done.3.refs_4_ = bf16[8,32,512]{2,1,0:T(8,128)(2,1)S(1)} collective-permute-done((bf16[8,32,512]{2,1,0:T(8,128)(2,1)}, bf16[8,32,512]{2,1,0:T(8,128)(2,1)S(1)}, u32[]{:S(2)}, u32[]{:S(2)}) %collective-permute-start.3) | collective-permute-done | bytes 262176 | tf_op jit(solution)/shard_map/ppermute | solution.py:191
  41.7 1.3 %collective-permute-done.4.refs_5_ = bf16[8,32,512]{2,1,0:T(8,128)(2,1)S(1)} collective-permute-done((bf16[8,32,512]{2,1,0:T(8,128)(2,1)}, bf16[8,32,512]{2,1,0:T(8,128)(2,1)S(1)}, u32[]{:S(2)}, u32[]{:S(2)}) %collective-permute-start.4) | collective-permute-done | bytes 262176 | tf_op jit(solution)/shard_map/ppermute | solution.py:191
  43.7 2.9 %chunk_2.1 = (bf16[8,32,512]{2,1,0:T(8,128)(2,1)}, bf16[8,32,512]{2,1,0:T(8,128)(2,1)}) custom-call(s32[2,32]{1,0:T(2,128)} %pad_add_fusion.1.table_ref, bf16[32,32,512]{2,1,0:T(8,128)(2,1)} %get-tuple-element.14.refs_0_.refs_1_.kept, bf16[32,32,512]{2,1,0:T(8,128)(2,1)} %get-tuple-element.14.refs_0_.refs_1_.kept, bf16[32,32,512]{2,1,0:T(8,128)(2,1)} %copy-done.1, ...), custom_call_target="tpu_custom_call" | custom-call | bytes 1048576 | tf_op jit(solution)/shard_map/chunk_2/pallas_call | solution.py:256
  46.6 1.6 %collective-permute-start.5 = (bf16[8,32,512]{2,1,0:T(8,128)(2,1)}, bf16[8,32,512]{2,1,0:T(8,128)(2,1)S(1)}, u32[]{:S(2)}, u32[]{:S(2)}) collective-permute-start(bf16[8,32,512]{2,1,0:T(8,128)(2,1)} %get-tuple-element.20), channel_id=1, source_target_pairs={{0,4},{1,5},{2,0},{3,1},{4,8},{5,9},{6,2},{7,3},{8,12},{9,13},{10,... | collective-permute-start | bytes 786440 | tf_op jit(solution)/shard_map/ppermute | solution.py:191
  48.7 4.6 %collective-permute-done.5.refs_4_ = bf16[8,32,512]{2,1,0:T(8,128)(2,1)S(1)} collective-permute-done((bf16[8,32,512]{2,1,0:T(8,128)(2,1)}, bf16[8,32,512]{2,1,0:T(8,128)(2,1)S(1)}, u32[]{:S(2)}, u32[]{:S(2)}) %collective-permute-start.5) | collective-permute-done | bytes 262176 | tf_op jit(solution)/shard_map/ppermute | solution.py:191
  53.2 1.6 %collective-permute-done.6.refs_5_ = bf16[8,32,512]{2,1,0:T(8,128)(2,1)S(1)} collective-permute-done((bf16[8,32,512]{2,1,0:T(8,128)(2,1)}, bf16[8,32,512]{2,1,0:T(8,128)(2,1)S(1)}, u32[]{:S(2)}, u32[]{:S(2)}) %collective-permute-start.6) | collective-permute-done | bytes 262176 | tf_op jit(solution)/shard_map/ppermute | solution.py:191
  55.5 2.9 %chunk_1.1 = (bf16[8,32,512]{2,1,0:T(8,128)(2,1)}, bf16[8,32,512]{2,1,0:T(8,128)(2,1)}) custom-call(s32[2,32]{1,0:T(2,128)} %pad_add_fusion.1.table_ref, bf16[32,32,512]{2,1,0:T(8,128)(2,1)} %get-tuple-element.14.refs_0_.refs_1_.kept, bf16[32,32,512]{2,1,0:T(8,128)(2,1)} %get-tuple-element.14.refs_0_.refs_1_.kept, bf16[32,32,512]{2,1,0:T(8,128)(2,1)} %copy-done.1, ...), custom_call_target="tpu_custom_call" | custom-call | bytes 1048576 | tf_op jit(solution)/shard_map/chunk_1/pallas_call | solution.py:256
  58.4 1.5 %collective-permute-start.7 = (bf16[8,32,512]{2,1,0:T(8,128)(2,1)}, bf16[8,32,512]{2,1,0:T(8,128)(2,1)S(1)}, u32[]{:S(2)}, u32[]{:S(2)}) collective-permute-start(bf16[8,32,512]{2,1,0:T(8,128)(2,1)} %get-tuple-element.22), channel_id=1, source_target_pairs={{0,4},{1,5},{2,0},{3,1},{4,8},{5,9},{6,2},{7,3},{8,12},{9,13},{10,... | collective-permute-start | bytes 786440 | tf_op jit(solution)/shard_map/ppermute | solution.py:191
  60.4 4.6 %collective-permute-done.7.rest_0_ = bf16[8,32,512]{2,1,0:T(8,128)(2,1)S(1)} collective-permute-done((bf16[8,32,512]{2,1,0:T(8,128)(2,1)}, bf16[8,32,512]{2,1,0:T(8,128)(2,1)S(1)}, u32[]{:S(2)}, u32[]{:S(2)}) %collective-permute-start.7) | collective-permute-done | bytes 262176 | tf_op jit(solution)/shard_map/ppermute | solution.py:191
  65.0 1.5 %collective-permute-done.8.rest_1_ = bf16[8,32,512]{2,1,0:T(8,128)(2,1)S(1)} collective-permute-done((bf16[8,32,512]{2,1,0:T(8,128)(2,1)}, bf16[8,32,512]{2,1,0:T(8,128)(2,1)S(1)}, u32[]{:S(2)}, u32[]{:S(2)}) %collective-permute-start.8) | collective-permute-done | bytes 262176 | tf_op jit(solution)/shard_map/ppermute | solution.py:191
  67.2 3.8 %mesh_step.1.rest_0_ = bf16[256,512]{1,0:T(8,128)(2,1)} custom-call(s32[2,32]{1,0:T(2,128)} %pad_add_fusion.1.table_ref, bf16[256,512]{1,0:T(8,128)(2,1)} %latent_ref.1, bf16[512,512]{1,0:T(8,128)(2,1)} %up_ref.1, bf16[512,512]{1,0:T(8,128)(2,1)} %down_ref.1, f32[1,512]{1,0:T(1,128)} %bitcast.5, bf16[32,32,512]{2,1,0:T(8,128)(2,1)} %get-tuple-element.14.refs_0_.refs_1_.kept, ...), custom_call_target="tpu_custom_call" | custom-call | flops 268435456 | bytes 1048576 | tf_op jit(solution)/shard_map/mesh_step/pallas_call | solution.py:273
  71.6 1.5 %collective-permute-start.10 = (bf16[256,512]{1,0:T(8,128)(2,1)}, bf16[256,512]{1,0:T(8,128)(2,1)S(1)}, u32[]{:S(2)}, u32[]{:S(2)}) collective-permute-start(bf16[256,512]{1,0:T(8,128)(2,1)} %mesh_step.1.rest_0_), channel_id=1, source_target_pairs={{0,4},{1,5},{2,0},{3,1},{4,8},{5,9},{6,2},{7,3},{8,12},{9,13},{10,... | collective-permute-start | bytes 786440 | tf_op jit(solution)/shard_map/ppermute | solution.py:191
  73.1 6.8 %collective-permute-done.12.rest_4_ = bf16[256,512]{1,0:T(8,128)(2,1)S(1)} collective-permute-done((bf16[256,512]{1,0:T(8,128)(2,1)}, bf16[256,512]{1,0:T(8,128)(2,1)S(1)}, u32[]{:S(2)}, u32[]{:S(2)}) %collective-permute-start.12) | collective-permute-done | bytes 262176 | tf_op jit(solution)/shard_map/ppermute | solution.py:191
  80.4 1.5 %collective-permute-start.14 = (bf16[256,512]{1,0:T(8,128)(2,1)S(1)}, bf16[256,512]{1,0:T(8,128)(2,1)S(1)}, u32[]{:S(2)}, u32[]{:S(2)}) collective-permute-start(bf16[256,512]{1,0:T(8,128)(2,1)S(1)} %collective-permute-done.10.rest_2_), channel_id=1, source_target_pairs={{0,4},{1,5},{2,0},{3,1},{4,8},{5,9},{6,2},{7,3},{8,12},{9,13},{10,... | collective-permute-start | bytes 786440 | tf_op jit(solution)/shard_map/ppermute | solution.py:191
  81.9 5.9 %collective-permute-done.16.rest_8_ = bf16[256,512]{1,0:T(8,128)(2,1)S(1)} collective-permute-done((bf16[256,512]{1,0:T(8,128)(2,1)S(1)}, bf16[256,512]{1,0:T(8,128)(2,1)S(1)}, u32[]{:S(2)}, u32[]{:S(2)}) %collective-permute-start.16) | collective-permute-done | bytes 262176 | tf_op jit(solution)/shard_map/ppermute | solution.py:191
  88.3 1.6 %collective-permute-start.18 = (bf16[256,512]{1,0:T(8,128)(2,1)S(1)}, bf16[256,512]{1,0:T(8,128)(2,1)S(1)}, u32[]{:S(2)}, u32[]{:S(2)}) collective-permute-start(bf16[256,512]{1,0:T(8,128)(2,1)S(1)} %collective-permute-done.14.rest_6_), channel_id=1, source_target_pairs={{0,4},{1,5},{2,0},{3,1},{4,8},{5,9},{6,2},{7,3},{8,12},{9,13},{10,... | collective-permute-start | bytes 786440 | tf_op jit(solution)/shard_map/ppermute | solution.py:191
  90.4 3.8 %collective-permute-done.20.rest_12_ = bf16[256,512]{1,0:T(8,128)(2,1)S(1)} collective-permute-done((bf16[256,512]{1,0:T(8,128)(2,1)S(1)}, bf16[256,512]{1,0:T(8,128)(2,1)S(1)}, u32[]{:S(2)}, u32[]{:S(2)}) %collective-permute-start.20) | collective-permute-done | bytes 262176 | tf_op jit(solution)/shard_map/ppermute | solution.py:191
  94.8 0.9 collective-permute-start.24
  96.3 1.2 %collective-permute-start.22 = (bf16[128,512]{1,0:T(8,128)(2,1)S(1)}, bf16[128,512]{1,0:T(8,128)(2,1)S(1)}, u32[]{:S(2)}, u32[]{:S(2)}) collective-permute-start(bf16[128,512]{1,0:T(8,128)(2,1)S(1)} %slice.8), channel_id=1, source_target_pairs={{0,4},{1,5},{2,0},{3,1},{4,8},{5,9},{6,2},{7,3},{8,12},{9,13},{10,... | collective-permute-start | bytes 393224 | tf_op jit(solution)/shard_map/ppermute | solution.py:191
  97.5 3.2 %collective-permute-done.24.rest_16_ = bf16[128,512]{1,0:T(8,128)(2,1)S(1)} collective-permute-done((bf16[128,512]{1,0:T(8,128)(2,1)S(1)}, bf16[128,512]{1,0:T(8,128)(2,1)S(1)}, u32[]{:S(2)}, u32[]{:S(2)}) %collective-permute-start.24) | collective-permute-done | bytes 131104 | tf_op jit(solution)/shard_map/ppermute | solution.py:191
  100.7 1.3 %collective-permute-done.22.rest_14_ = bf16[128,512]{1,0:T(8,128)(2,1)S(1)} collective-permute-done((bf16[128,512]{1,0:T(8,128)(2,1)S(1)}, bf16[128,512]{1,0:T(8,128)(2,1)S(1)}, u32[]{:S(2)}, u32[]{:S(2)}) %collective-permute-start.22) | collective-permute-done | bytes 131104 | tf_op jit(solution)/shard_map/ppermute | solution.py:191
  102.0 1.3 %collective-permute-done.23.rest_15_ = bf16[128,512]{1,0:T(8,128)(2,1)S(1)} collective-permute-done((bf16[128,512]{1,0:T(8,128)(2,1)S(1)}, bf16[128,512]{1,0:T(8,128)(2,1)S(1)}, u32[]{:S(2)}, u32[]{:S(2)}) %collective-permute-start.23) | collective-permute-done | bytes 131104 | tf_op jit(solution)/shard_map/ppermute | solution.py:187
  103.9 10.7 %back.1 = bf16[4096,512]{1,0:T(8,128)(2,1)} custom-call(s32[4,64]{1,0:T(4,128)} %pad_add_fusion.info_ref, bf16[4096,512]{1,0:T(8,128)(2,1)} %get-tuple-element.13.latent_ref, bf16[16,4,32,256]{3,2,1,0:T(8,128)(2,1)} %interp_ref.3, bf16[256,512]{1,0:T(8,128)(2,1)} %mesh_step.1.rest_0_, bf16[256,512]{1,0:T(8,128)(2,1)} %copy-done.8, ...), custom_call_target="tpu_custom_call" | custom-call | flops 536870912 | bytes 9437184 | tf_op jit(solution)/shard_map/back/pallas_call | solution.py:311
  (100 shorter events, 12.1 us)
Async XLA Ops:
  15.8 2.9 %collective-permute-start = (bf16[32,32,512]{2,1,0:T(8,128)(2,1)}, bf16[32,32,512]{2,1,0:T(8,128)(2,1)S(1)}, u32[]{:S(2)}, u32[]{:S(2)}) collective-permute-start(bf16[32,32,512]{2,1,0:T(8,128)(2,1)} %get-tuple-element.15), channel_id=1, source_target_pairs={{0,1},{1,0},{2,3},{3,2},{4,5},{5,4},{6,7},{7,6},{8,9},{9,8},{10,11... | collective-permute-start | bytes 3145736 | tf_op jit(solution)/shard_map/ppermute | solution.py:187
  22.4 6.9 %collective-permute-start.1 = (bf16[4,32,512]{2,1,0:T(8,128)(2,1)}, bf16[4,32,512]{2,1,0:T(8,128)(2,1)S(1)}, u32[]{:S(2)}, u32[]{:S(2)}) collective-permute-start(bf16[4,32,512]{2,1,0:T(8,128)(2,1)} %get-tuple-element.16), channel_id=1, source_target_pairs={{0,4},{1,5},{2,0},{3,1},{4,8},{5,9},{6,2},{7,3},{8,12},{9,13},{10,... | collective-permute-start | bytes 393224 | tf_op jit(solution)/shard_map/ppermute | solution.py:191
  25.3 5.5 %collective-permute-start.2 = (bf16[4,32,512]{2,1,0:T(8,128)(2,1)}, bf16[4,32,512]{2,1,0:T(8,128)(2,1)S(1)}, u32[]{:S(2)}, u32[]{:S(2)}) collective-permute-start(bf16[4,32,512]{2,1,0:T(8,128)(2,1)} %get-tuple-element.17), channel_id=1, source_target_pairs={{0,2},{1,3},{2,6},{3,7},{4,0},{5,1},{6,10},{7,11},{8,4},{9,5},{10,... | collective-permute-start | bytes 393224 | tf_op jit(solution)/shard_map/ppermute | solution.py:191
  34.3 7.4 %collective-permute-start.3 = (bf16[8,32,512]{2,1,0:T(8,128)(2,1)}, bf16[8,32,512]{2,1,0:T(8,128)(2,1)S(1)}, u32[]{:S(2)}, u32[]{:S(2)}) collective-permute-start(bf16[8,32,512]{2,1,0:T(8,128)(2,1)} %get-tuple-element.18), channel_id=1, source_target_pairs={{0,4},{1,5},{2,0},{3,1},{4,8},{5,9},{6,2},{7,3},{8,12},{9,13},{10,... | collective-permute-start | bytes 786440 | tf_op jit(solution)/shard_map/ppermute | solution.py:191
  35.9 7.1 %collective-permute-start.4 = (bf16[8,32,512]{2,1,0:T(8,128)(2,1)}, bf16[8,32,512]{2,1,0:T(8,128)(2,1)S(1)}, u32[]{:S(2)}, u32[]{:S(2)}) collective-permute-start(bf16[8,32,512]{2,1,0:T(8,128)(2,1)} %get-tuple-element.19), channel_id=1, source_target_pairs={{0,2},{1,3},{2,6},{3,7},{4,0},{5,1},{6,10},{7,11},{8,4},{9,5},{10,... | collective-permute-start | bytes 786440 | tf_op jit(solution)/shard_map/ppermute | solution.py:191
  46.6 6.6 %collective-permute-start.5 = (bf16[8,32,512]{2,1,0:T(8,128)(2,1)}, bf16[8,32,512]{2,1,0:T(8,128)(2,1)S(1)}, u32[]{:S(2)}, u32[]{:S(2)}) collective-permute-start(bf16[8,32,512]{2,1,0:T(8,128)(2,1)} %get-tuple-element.20), channel_id=1, source_target_pairs={{0,4},{1,5},{2,0},{3,1},{4,8},{5,9},{6,2},{7,3},{8,12},{9,13},{10,... | collective-permute-start | bytes 786440 | tf_op jit(solution)/shard_map/ppermute | solution.py:191
  48.2 6.6 %collective-permute-start.6 = (bf16[8,32,512]{2,1,0:T(8,128)(2,1)}, bf16[8,32,512]{2,1,0:T(8,128)(2,1)S(1)}, u32[]{:S(2)}, u32[]{:S(2)}) collective-permute-start(bf16[8,32,512]{2,1,0:T(8,128)(2,1)} %get-tuple-element.21), channel_id=1, source_target_pairs={{0,2},{1,3},{2,6},{3,7},{4,0},{5,1},{6,10},{7,11},{8,4},{9,5},{10,... | collective-permute-start | bytes 786440 | tf_op jit(solution)/shard_map/ppermute | solution.py:191
  58.4 6.6 %collective-permute-start.7 = (bf16[8,32,512]{2,1,0:T(8,128)(2,1)}, bf16[8,32,512]{2,1,0:T(8,128)(2,1)S(1)}, u32[]{:S(2)}, u32[]{:S(2)}) collective-permute-start(bf16[8,32,512]{2,1,0:T(8,128)(2,1)} %get-tuple-element.22), channel_id=1, source_target_pairs={{0,4},{1,5},{2,0},{3,1},{4,8},{5,9},{6,2},{7,3},{8,12},{9,13},{10,... | collective-permute-start | bytes 786440 | tf_op jit(solution)/shard_map/ppermute | solution.py:191
  59.9 6.6 %collective-permute-start.8 = (bf16[8,32,512]{2,1,0:T(8,128)(2,1)}, bf16[8,32,512]{2,1,0:T(8,128)(2,1)S(1)}, u32[]{:S(2)}, u32[]{:S(2)}) collective-permute-start(bf16[8,32,512]{2,1,0:T(8,128)(2,1)} %get-tuple-element.23), channel_id=1, source_target_pairs={{0,2},{1,3},{2,6},{3,7},{4,0},{5,1},{6,10},{7,11},{8,4},{9,5},{10,... | collective-permute-start | bytes 786440 | tf_op jit(solution)/shard_map/ppermute | solution.py:191
  71.0 8.8 %collective-permute-start.12 = (bf16[256,512]{1,0:T(8,128)(2,1)}, bf16[256,512]{1,0:T(8,128)(2,1)S(1)}, u32[]{:S(2)}, u32[]{:S(2)}) collective-permute-start(bf16[256,512]{1,0:T(8,128)(2,1)} %mesh_step.1.rest_0_), channel_id=1, source_target_pairs={{0,2},{1,3},{2,6},{3,7},{4,0},{5,1},{6,10},{7,11},{8,4},{9,5},{10,... | collective-permute-start | bytes 786440 | tf_op jit(solution)/shard_map/ppermute | solution.py:191
  71.6 8.9 %collective-permute-start.10 = (bf16[256,512]{1,0:T(8,128)(2,1)}, bf16[256,512]{1,0:T(8,128)(2,1)S(1)}, u32[]{:S(2)}, u32[]{:S(2)}) collective-permute-start(bf16[256,512]{1,0:T(8,128)(2,1)} %mesh_step.1.rest_0_), channel_id=1, source_target_pairs={{0,4},{1,5},{2,0},{3,1},{4,8},{5,9},{6,2},{7,3},{8,12},{9,13},{10,... | collective-permute-start | bytes 786440 | tf_op jit(solution)/shard_map/ppermute | solution.py:191
  79.9 23.4 %copy-start.4 = (bf16[256,512]{1,0:T(8,128)(2,1)}, bf16[256,512]{1,0:T(8,128)(2,1)S(1)}, u32[]{:S(2)}) copy-start(bf16[256,512]{1,0:T(8,128)(2,1)S(1)} %collective-permute-done.12.rest_4_) | copy-start | bytes 786436
  79.9 7.9 %collective-permute-start.16 = (bf16[256,512]{1,0:T(8,128)(2,1)S(1)}, bf16[256,512]{1,0:T(8,128)(2,1)S(1)}, u32[]{:S(2)}, u32[]{:S(2)}) collective-permute-start(bf16[256,512]{1,0:T(8,128)(2,1)S(1)} %collective-permute-done.12.rest_4_), channel_id=1, source_target_pairs={{0,2},{1,3},{2,6},{3,7},{4,0},{5,1},{6,10},{7,11},{8,4},{9,5},{10,... | collective-permute-start | bytes 786440 | tf_op jit(solution)/shard_map/ppermute | solution.py:191
  80.4 22.9 %copy-start.5 = (bf16[256,512]{1,0:T(8,128)(2,1)}, bf16[256,512]{1,0:T(8,128)(2,1)S(1)}, u32[]{:S(2)}) copy-start(bf16[256,512]{1,0:T(8,128)(2,1)S(1)} %collective-permute-done.10.rest_2_) | copy-start | bytes 786436
  80.4 7.8 %collective-permute-start.14 = (bf16[256,512]{1,0:T(8,128)(2,1)S(1)}, bf16[256,512]{1,0:T(8,128)(2,1)S(1)}, u32[]{:S(2)}, u32[]{:S(2)}) collective-permute-start(bf16[256,512]{1,0:T(8,128)(2,1)S(1)} %collective-permute-done.10.rest_2_), channel_id=1, source_target_pairs={{0,4},{1,5},{2,0},{3,1},{4,8},{5,9},{6,2},{7,3},{8,12},{9,13},{10,... | collective-permute-start | bytes 786440 | tf_op jit(solution)/shard_map/ppermute | solution.py:191
  87.8 15.5 %copy-start.6 = (bf16[256,512]{1,0:T(8,128)(2,1)}, bf16[256,512]{1,0:T(8,128)(2,1)S(1)}, u32[]{:S(2)}) copy-start(bf16[256,512]{1,0:T(8,128)(2,1)S(1)} %collective-permute-done.16.rest_8_) | copy-start | bytes 786436
  87.8 6.4 %collective-permute-start.20 = (bf16[256,512]{1,0:T(8,128)(2,1)S(1)}, bf16[256,512]{1,0:T(8,128)(2,1)S(1)}, u32[]{:S(2)}, u32[]{:S(2)}) collective-permute-start(bf16[256,512]{1,0:T(8,128)(2,1)S(1)} %collective-permute-done.16.rest_8_), channel_id=1, source_target_pairs={{0,2},{1,3},{2,6},{3,7},{4,0},{5,1},{6,10},{7,11},{8,4},{9,5},{10,... | collective-permute-start | bytes 786440 | tf_op jit(solution)/shard_map/ppermute | solution.py:191
  88.3 15.0 %copy-start.7 = (bf16[256,512]{1,0:T(8,128)(2,1)}, bf16[256,512]{1,0:T(8,128)(2,1)S(1)}, u32[]{:S(2)}) copy-start(bf16[256,512]{1,0:T(8,128)(2,1)S(1)} %collective-permute-done.14.rest_6_) | copy-start | bytes 786436
  88.3 6.4 %collective-permute-start.18 = (bf16[256,512]{1,0:T(8,128)(2,1)S(1)}, bf16[256,512]{1,0:T(8,128)(2,1)S(1)}, u32[]{:S(2)}, u32[]{:S(2)}) collective-permute-start(bf16[256,512]{1,0:T(8,128)(2,1)S(1)} %collective-permute-done.14.rest_6_), channel_id=1, source_target_pairs={{0,4},{1,5},{2,0},{3,1},{4,8},{5,9},{6,2},{7,3},{8,12},{9,13},{10,... | collective-permute-start | bytes 786440 | tf_op jit(solution)/shard_map/ppermute | solution.py:191
  89.8 5.0 %collective-permute-start.9 = (bf16[256,512]{1,0:T(8,128)(2,1)}, bf16[256,512]{1,0:T(8,128)(2,1)S(1)}, u32[]{:S(2)}, u32[]{:S(2)}) collective-permute-start(bf16[256,512]{1,0:T(8,128)(2,1)} %mesh_step.1.rest_0_), channel_id=1, source_target_pairs={{0,1},{1,0},{2,3},{3,2},{4,5},{5,4},{6,7},{7,6},{8,9},{9,8},{10,11... | collective-permute-start | bytes 786440 | tf_op jit(solution)/shard_map/ppermute | solution.py:187
  89.8 5.9 %collective-permute-start.13 = (bf16[256,512]{1,0:T(8,128)(2,1)S(1)}, bf16[256,512]{1,0:T(8,128)(2,1)S(1)}, u32[]{:S(2)}, u32[]{:S(2)}) collective-permute-start(bf16[256,512]{1,0:T(8,128)(2,1)S(1)} %collective-permute-done.12.rest_4_), channel_id=1, source_target_pairs={{0,1},{1,0},{2,3},{3,2},{4,5},{5,4},{6,7},{7,6},{8,9},{9,8},{10,11... | collective-permute-start | bytes 786440 | tf_op jit(solution)/shard_map/ppermute | solution.py:187
  90.4 5.7 %collective-permute-start.11 = (bf16[256,512]{1,0:T(8,128)(2,1)S(1)}, bf16[256,512]{1,0:T(8,128)(2,1)S(1)}, u32[]{:S(2)}, u32[]{:S(2)}) collective-permute-start(bf16[256,512]{1,0:T(8,128)(2,1)S(1)} %collective-permute-done.10.rest_2_), channel_id=1, source_target_pairs={{0,1},{1,0},{2,3},{3,2},{4,5},{5,4},{6,7},{7,6},{8,9},{9,8},{10,11... | collective-permute-start | bytes 786440 | tf_op jit(solution)/shard_map/ppermute | solution.py:187
  94.2 9.1 %copy-start.2 = (bf16[256,512]{1,0:T(8,128)(2,1)}, bf16[256,512]{1,0:T(8,128)(2,1)S(1)}, u32[]{:S(2)}) copy-start(bf16[256,512]{1,0:T(8,128)(2,1)S(1)} %collective-permute-done.20.rest_12_) | copy-start | bytes 786436
  94.2 2.1 %collective-permute-start.17 = (bf16[256,512]{1,0:T(8,128)(2,1)S(1)}, bf16[256,512]{1,0:T(8,128)(2,1)S(1)}, u32[]{:S(2)}, u32[]{:S(2)}) collective-permute-start(bf16[256,512]{1,0:T(8,128)(2,1)S(1)} %collective-permute-done.16.rest_8_), channel_id=1, source_target_pairs={{0,1},{1,0},{2,3},{3,2},{4,5},{5,4},{6,7},{7,6},{8,9},{9,8},{10,11... | collective-permute-start | bytes 786440 | tf_op jit(solution)/shard_map/ppermute | solution.py:187
  94.7 8.7 %copy-start.3 = (bf16[256,512]{1,0:T(8,128)(2,1)}, bf16[256,512]{1,0:T(8,128)(2,1)S(1)}, u32[]{:S(2)}) copy-start(bf16[256,512]{1,0:T(8,128)(2,1)S(1)} %collective-permute-done.18.rest_10_) | copy-start | bytes 786436
  94.7 7.3 %collective-permute-start.15 = (bf16[256,512]{1,0:T(8,128)(2,1)S(1)}, bf16[256,512]{1,0:T(8,128)(2,1)S(1)}, u32[]{:S(2)}, u32[]{:S(2)}) collective-permute-start(bf16[256,512]{1,0:T(8,128)(2,1)S(1)} %collective-permute-done.14.rest_6_), channel_id=1, source_target_pairs={{0,1},{1,0},{2,3},{3,2},{4,5},{5,4},{6,7},{7,6},{8,9},{9,8},{10,11... | collective-permute-start | bytes 786440 | tf_op jit(solution)/shard_map/ppermute | solution.py:187
  94.8 5.8 %collective-permute-start.24 = (bf16[128,512]{1,0:T(8,128)(2,1)S(1)}, bf16[128,512]{1,0:T(8,128)(2,1)S(1)}, u32[]{:S(2)}, u32[]{:S(2)}) collective-permute-start(bf16[128,512]{1,0:T(8,128)(2,1)S(1)} %slice.9), channel_id=1, source_target_pairs={{0,2},{1,3},{2,6},{3,7},{4,0},{5,1},{6,10},{7,11},{8,4},{9,5},{10,... | collective-permute-start | bytes 393224 | tf_op jit(solution)/shard_map/ppermute | solution.py:191
  95.8 6.2 %collective-permute-start.21 = (bf16[256,512]{1,0:T(8,128)(2,1)S(1)}, bf16[256,512]{1,0:T(8,128)(2,1)S(1)}, u32[]{:S(2)}, u32[]{:S(2)}) collective-permute-start(bf16[256,512]{1,0:T(8,128)(2,1)S(1)} %collective-permute-done.20.rest_12_), channel_id=1, source_target_pairs={{0,1},{1,0},{2,3},{3,2},{4,5},{5,4},{6,7},{7,6},{8,9},{9,8},{10,11... | collective-permute-start | bytes 786440 | tf_op jit(solution)/shard_map/ppermute | solution.py:187
  96.0 6.0 %collective-permute-start.19 = (bf16[256,512]{1,0:T(8,128)(2,1)S(1)}, bf16[256,512]{1,0:T(8,128)(2,1)S(1)}, u32[]{:S(2)}, u32[]{:S(2)}) collective-permute-start(bf16[256,512]{1,0:T(8,128)(2,1)S(1)} %collective-permute-done.18.rest_10_), channel_id=1, source_target_pairs={{0,1},{1,0},{2,3},{3,2},{4,5},{5,4},{6,7},{7,6},{8,9},{9,8},{10,11... | collective-permute-start | bytes 786440 | tf_op jit(solution)/shard_map/ppermute | solution.py:187
  96.3 5.6 %collective-permute-start.22 = (bf16[128,512]{1,0:T(8,128)(2,1)S(1)}, bf16[128,512]{1,0:T(8,128)(2,1)S(1)}, u32[]{:S(2)}, u32[]{:S(2)}) collective-permute-start(bf16[128,512]{1,0:T(8,128)(2,1)S(1)} %slice.8), channel_id=1, source_target_pairs={{0,4},{1,5},{2,0},{3,1},{4,8},{5,9},{6,2},{7,3},{8,12},{9,13},{10,... | collective-permute-start | bytes 393224 | tf_op jit(solution)/shard_map/ppermute | solution.py:191
  100.7 1.3 %collective-permute-start.25 = (bf16[128,512]{1,0:T(8,128)(2,1)S(1)}, bf16[128,512]{1,0:T(8,128)(2,1)S(1)}, u32[]{:S(2)}, u32[]{:S(2)}) collective-permute-start(bf16[128,512]{1,0:T(8,128)(2,1)S(1)} %collective-permute-done.24.rest_16_), channel_id=1, source_target_pairs={{0,1},{1,0},{2,3},{3,2},{4,5},{5,4},{6,7},{7,6},{8,9},{9,8},{10,11... | collective-permute-start | bytes 393224 | tf_op jit(solution)/shard_map/ppermute | solution.py:187
  101.9 1.3 %collective-permute-start.23 = (bf16[128,512]{1,0:T(8,128)(2,1)S(1)}, bf16[128,512]{1,0:T(8,128)(2,1)S(1)}, u32[]{:S(2)}, u32[]{:S(2)}) collective-permute-start(bf16[128,512]{1,0:T(8,128)(2,1)S(1)} %collective-permute-done.22.rest_14_), channel_id=1, source_target_pairs={{0,1},{1,0},{2,3},{3,2},{4,5},{5,4},{6,7},{7,6},{8,9},{9,8},{10,11... | collective-permute-start | bytes 393224 | tf_op jit(solution)/shard_map/ppermute | solution.py:187
  (21 other events, 51.3 us)

commit v3 on v2

v3 whole, which is shorter than its diff:
```python
import functools

import jax
import jax.numpy as jnp
from jax import lax
from jax.experimental import pallas as pl
from jax.experimental.pallas import tpu as pltpu
from jax.sharding import PartitionSpec as P

F32 = jnp.float32
BF16 = jnp.bfloat16
N_CORE = 2


def silu(values):
    half = 0.5 * values
    return half * (1.0 + jnp.tanh(half))


def layer_norm(values, gain):
    centred = values - jnp.mean(values, axis=-1, keepdims=True)
    spread = jnp.mean(centred * centred, axis=-1, keepdims=True)
    return centred * lax.rsqrt(spread + 1e-05) * gain


def split(value, size):
    if size & (size - 1) == 0:
        return lax.shift_right_logical(value, size.bit_length() - 1), value & (size - 1)
    return lax.div(value, size), lax.rem(value, size)


class Ring:
    def __init__(self, n_band, n_y, tiles):
        self.n_band, self.n_y, self.tiles = n_band, n_y, tiles
        self.chips = n_band // N_CORE
        self.far = self.chips // 2

    def place(self, index):
        chip, core = split(index, N_CORE)
        z, y = split(chip, self.n_y)
        return z + y * (self.chips - 1 - 2 * z), core

    def index(self, ring, core):
        ring = ring % self.chips
        n_z = self.chips // self.n_y
        z, y = (ring, 0) if ring < n_z else (self.chips - 1 - ring, 1)
        return (z * self.n_y + y) * N_CORE + core

    def over_core(self, value):
        return lax.ppermute(value, "band", [(i, i ^ 1) for i in range(self.n_band)])

    def over(self, value, by):
        pairs = []
        for i in range(self.n_band):
            chip, core = divmod(i, N_CORE)
            z, y = divmod(chip, self.n_y)
            ring = z if y == 0 else self.chips - 1 - z
            pairs.append((i, self.index(ring + by, core)))
        return lax.ppermute(value, "band", pairs)

    def entry(self, lists_ref, me, block, k):
        owner, tile = split(lists_ref[k, block], self.tiles)
        ring, core = self.place(owner)
        my_ring, my_core = self.place(me)
        ahead = split(ring - my_ring + self.chips, self.chips)[1]
        return ahead, core ^ my_core, tile


def embed_kernel(
    ring, per_step, slots, me_ref, lists_ref, mask_ref,
    x_ref, w1_ref, w2_ref, gain_ref, interp_ref,
    latent_ref, kept_ref, sent_ref, table_ref, placed,
):
    step = pl.program_id(0)
    me = me_ref[0]
    list_len, tile_rows, block_rows = interp_ref.shape[1:]
    blk_count = pl.num_programs(0) * per_step

    def spot(index, b, k):
        block = step * per_step + b
        ahead, across, tile = ring.entry(lists_ref, index, index * blk_count + block, k)
        slot = split(block * list_len + k, ring.n_band)[0]
        return (across * ring.chips + ahead) * slots + slot, tile

    first = lax.dot_general(
        x_ref[...], w1_ref[...], (((0,), (0,)), ((), ())), preferred_element_type=F32
    )
    before = jnp.dot(silu(first).astype(BF16), w2_ref[...], preferred_element_type=F32)
    latent = layer_norm(before, gain_ref[...]).astype(BF16)
    latent_ref[...] = latent
    for b in range(per_step):
        weights = interp_ref[b].reshape(list_len * tile_rows, block_rows)
        part = jnp.dot(
            weights, latent[b * block_rows : (b + 1) * block_rows], preferred_element_type=F32
        )
        for k in range(list_len):
            place, tile = spot(me, b, k)
            table_ref[0, place] = tile
            there, its_tile = spot(me ^ 1, b, k)
            table_ref[1, there] = its_tile
            mask = mask_ref[k, me * blk_count + step * per_step + b].astype(F32)
            masked = part[k * tile_rows : (k + 1) * tile_rows] * mask
            placed[place] = masked.astype(BF16)

    @pl.when(step == pl.num_programs(0) - 1)
    def _():
        count = kept_ref.shape[0]
        kept_ref[...] = placed[:count]
        sent_ref[...] = placed[count:]


def add_entries(total, table_ref, owner, kept, other, chips):
    slots = kept.shape[0]
    for slot in range(slots):
        total[table_ref[0, owner * slots + slot]] += kept[slot].astype(F32)
        total[table_ref[1, (chips + owner) * slots + slot]] += other[slot].astype(F32)


def far_kernel(ring, table_ref, *refs):
    kept, other = refs[0:3], refs[3:6]
    far_right, far_left, next_right, next_left, total = refs[6:]
    half = total.shape[0] // 2
    owners = (ring.far, ring.far - 1, ring.chips - ring.far + 1)
    for number, owner in enumerate(owners):
        total[...] = jnp.zeros_like(total)
        add_entries(total, table_ref, owner, kept[number], other[number], ring.chips)
        if number == 0:
            far_right[...] = total[:half].astype(BF16)
            far_left[...] = total[half:].astype(BF16)
        elif number == 1:
            next_right[...] = total[half:].astype(BF16)
        else:
            next_left[...] = total[:half].astype(BF16)


def own_kernel(ring, table_ref, kept, other, own):
    number = pl.program_id(0)
    owner = number + (number >= ring.far).astype(jnp.int32)
    own[...] = jnp.zeros_like(own)
    add_entries(own.at[0], table_ref, owner, kept, other, ring.chips)


def mesh_kernel(
    latent_ref, up_ref, down_ref, gain_ref, own, right_a, left_b, right_b, left_a,
    out_ref, out_a, out_b,
):
    tiles, tile_rows, width = own.shape[1:]
    half = tiles // 2
    lower = own[0, :half] + right_a[...].astype(F32) + left_a[...].astype(F32)
    upper = own[0, half:] + right_b[...].astype(F32) + left_b[...].astype(F32)
    came = jnp.concatenate([lower, upper], axis=0).reshape(tiles * tile_rows, width)
    mesh_in = latent_ref[...].astype(F32) + came
    normed = layer_norm(mesh_in, gain_ref[...]).astype(BF16)
    hidden = silu(jnp.dot(normed, up_ref[...], preferred_element_type=F32)).astype(BF16)
    out = (mesh_in + jnp.dot(hidden, down_ref[...], preferred_element_type=F32)).astype(BF16)
    out_ref[...] = out
    out_a[...] = out[: half * tile_rows]
    out_b[...] = out[half * tile_rows :]


def back_kernel(
    ring, places, per_step, me_ref, lists_ref, mask_ref, latent_ref, interp_ref, *rest
):
    count = len(places)
    pieces, (out_ref, held, picked, sems) = rest[:count], rest[count:]
    step = pl.program_id(0)
    me = me_ref[0]
    list_len, tile_rows, block_rows = interp_ref.shape[1:]

    @pl.when(step == 0)
    def _():
        copies = []
        for i, (place, row) in enumerate(places):
            into = held.at[place, pl.ds(row, pieces[i].shape[0])]
            copies.append(pltpu.make_async_copy(pieces[i], into, sems.at[i]))
        for copy in copies:
            copy.start()
        for copy in copies:
            copy.wait()

    for b in range(per_step):
        block = (me * pl.num_programs(0) + step) * per_step + b
        for k in range(list_len):
            ahead, across, tile = ring.entry(lists_ref, me, block, k)
            rows = pl.ds(pl.multiple_of(tile * tile_rows, tile_rows), tile_rows)
            mask = mask_ref[k, block].astype(F32)
            value = held[ahead * N_CORE + across, rows].astype(F32) * mask
            picked[b, k * tile_rows : (k + 1) * tile_rows] = value.astype(BF16)
        weights = interp_ref[b].reshape(list_len * tile_rows, block_rows)
        back = lax.dot_general(
            weights, picked[b], (((0,), (0,)), ((), ())), preferred_element_type=F32
        )
        rows = slice(b * block_rows, (b + 1) * block_rows)
        out_ref[rows] = (latent_ref[rows].astype(F32) + back).astype(BF16)


def whole(array):
    zeros = (0,) * array.ndim
    return pl.BlockSpec(array.shape, lambda *_: zeros)


def params(mib):
    return pltpu.CompilerParams(vmem_limit_bytes=mib * 1024 * 1024)


def cost(flops, *arrays):
    size = sum(a.size * a.dtype.itemsize for a in arrays)
    return pl.CostEstimate(flops=int(flops), bytes_accessed=int(size), transcendentals=0)


def shape(dims, kind=BF16):
    return jax.ShapeDtypeStruct(dims, kind)


def on_device(
    n_y,
    grid_features,
    mesh_latent,
    embed_in,
    embed_out,
    embed_gain,
    interp,
    block_mask,
    tile_list,
    mesh_up,
    mesh_down,
    mesh_gain,
):
    n_band = lax.axis_size("band")
    blk_count, list_len, tile_rows, block_rows = interp.shape
    channels, width = embed_in.shape
    node_rows = mesh_latent.shape[0]
    tiles = node_rows // tile_rows
    half_tiles, half_rows = tiles // 2, node_rows // 2
    entries = blk_count * list_len
    slots = entries // n_band
    ring = Ring(n_band, n_y, tiles)
    chips, far = ring.chips, ring.far
    lists = (lax.axis_index("band").reshape(1), tile_list.T, block_mask.T)

    gain = embed_gain.reshape(1, width)
    per_step = 2
    rows = per_step * block_rows
    held_shape = (chips * slots, tile_rows, width)
    latent, kept, sent, table = pl.pallas_call(
        functools.partial(embed_kernel, ring, per_step, slots),
        out_shape=[shape((blk_count * block_rows, width))]
        + [shape(held_shape)] * N_CORE
        + [shape((2, entries), jnp.int32)],
        grid_spec=pltpu.PrefetchScalarGridSpec(
            num_scalar_prefetch=3,
            grid=(blk_count // per_step,),
            in_specs=[
                pl.BlockSpec((channels, rows), lambda i, *_: (0, i)),
                whole(embed_in),
                whole(embed_out),
                whole(gain),
                pl.BlockSpec((per_step,) + interp.shape[1:], lambda i, *_: (i, 0, 0, 0)),
            ],
            out_specs=[pl.BlockSpec((rows, width), lambda i, *_: (i, 0))]
            + [pl.BlockSpec(held_shape, lambda i, *_: (0, 0, 0))] * N_CORE
            + [pl.BlockSpec(memory_space=pltpu.SMEM)],
            scratch_shapes=[pltpu.VMEM((entries, tile_rows, width), BF16)],
        ),
        compiler_params=params(24),
        cost_estimate=cost(
            2 * blk_count * block_rows * width * (channels + width + list_len * tile_rows),
            grid_features,
            interp,
        ),
        name="embed",
    )(*lists, grid_features.T, embed_in, embed_out, gain, interp)
    other = ring.over_core(sent)

    dense = (tiles, tile_rows, width)
    half_dense = (half_tiles, tile_rows, width)

    def entries_of(owner):
        return pl.BlockSpec((slots, tile_rows, width), lambda i, _: (owner, 0, 0))

    near = [entries_of(owner) for owner in (far, far - 1, chips - far + 1)]
    far_right, far_left, next_right, next_left = pl.pallas_call(
        functools.partial(far_kernel, ring),
        out_shape=[shape(half_dense)] * 4,
        grid_spec=pltpu.PrefetchScalarGridSpec(
            num_scalar_prefetch=1,
            grid=(1,),
            in_specs=near + near,
            out_specs=[pl.BlockSpec(half_dense, lambda i, _: (0, 0, 0))] * 4,
            scratch_shapes=[pltpu.VMEM(dense, F32)],
        ),
        compiler_params=params(8),
        cost_estimate=cost(0, kept),
        name="far_chunks",
    )(table, *[kept] * 3, *[other] * 3)

    def skip_far(i):
        return i + (i >= far).astype(jnp.int32)

    per_owner = pl.BlockSpec((slots, tile_rows, width), lambda i, _: (skip_far(i), 0, 0))
    own = pl.pallas_call(
        functools.partial(own_kernel, ring),
        out_shape=shape((chips,) + dense, F32),
        grid_spec=pltpu.PrefetchScalarGridSpec(
            num_scalar_prefetch=1,
            grid=(chips - 1,),
            in_specs=[per_owner] * 2,
            out_specs=pl.BlockSpec((1,) + dense, lambda i, _: (skip_far(i), 0, 0, 0)),
        ),
        compiler_params=params(8),
        cost_estimate=cost(0, kept, kept, kept, kept),
        name="own_chunks",
    )(table, kept, other)

    def add_own(distance, part, value):
        mine = own[distance % chips, part]
        return (mine + value.astype(F32)).astype(BF16)

    lower, upper = slice(0, half_tiles), slice(half_tiles, tiles)
    right_a, left_b = ring.over(far_right, 1), ring.over(far_left, -1)
    right_b, left_a = ring.over(next_right, 1), ring.over(next_left, -1)
    for distance in range(far - 1, 0, -1):
        right_a = ring.over(add_own(distance, lower, right_a), 1)
        left_b = ring.over(add_own(-distance, upper, left_b), -1)
        if distance > 1:
            right_b = ring.over(add_own(distance - 1, upper, right_b), 1)
            left_a = ring.over(add_own(1 - distance, lower, left_a), -1)

    mesh_gain = mesh_gain.reshape(1, width)
    came = (right_a, left_b, right_b, left_a)
    mesh_out, out_a, out_b = pl.pallas_call(
        mesh_kernel,
        out_shape=[shape((node_rows, width))] + [shape((half_rows, width))] * 2,
        grid=(1,),
        in_specs=[whole(a) for a in (mesh_latent, mesh_up, mesh_down, mesh_gain)]
        + [pl.BlockSpec((1,) + dense, lambda i: (0, 0, 0, 0))]
        + [whole(c) for c in came],
        out_specs=[pl.BlockSpec((node_rows, width), lambda i: (0, 0))]
        + [pl.BlockSpec((half_rows, width), lambda i: (0, 0))] * 2,
        compiler_params=params(16),
        cost_estimate=cost(4 * node_rows * width * width, mesh_up, mesh_down),
        name="mesh_step",
    )(mesh_latent, mesh_up, mesh_down, mesh_gain, own, *came)

    pieces, places = [], []

    def keep(piece, owner, row):
        for across, value in enumerate((piece, ring.over_core(piece))):
            pieces.append(value)
            places.append((owner % chips * N_CORE + across, row))

    right_a, left_b, right_b, left_a = out_a, out_b, out_b, out_a
    keep(mesh_out, 0, 0)
    for distance in range(1, far + 1):
        right_a, left_b = ring.over(right_a, 1), ring.over(left_b, -1)
        keep(right_a, -distance, 0)
        keep(left_b, distance, half_rows)
        if distance < far:
            right_b, left_a = ring.over(right_b, 1), ring.over(left_a, -1)
            keep(right_b, -distance, half_rows)
            keep(left_a, distance, 0)

    per_step = 2
    rows = per_step * block_rows
    grid_out = pl.pallas_call(
        functools.partial(back_kernel, ring, places, per_step),
        out_shape=shape((blk_count * block_rows, width)),
        grid_spec=pltpu.PrefetchScalarGridSpec(
            num_scalar_prefetch=3,
            grid=(blk_count // per_step,),
            in_specs=[
                pl.BlockSpec((rows, width), lambda i, *_: (i, 0)),
                pl.BlockSpec((per_step,) + interp.shape[1:], lambda i, *_: (i, 0, 0, 0)),
            ]
            + [pl.BlockSpec(memory_space=pl.ANY)] * len(pieces),
            out_specs=pl.BlockSpec((rows, width), lambda i, *_: (i, 0)),
            scratch_shapes=[
                pltpu.VMEM((n_band, node_rows, width), BF16),
                pltpu.VMEM((per_step, list_len * tile_rows, width), BF16),
                pltpu.SemaphoreType.DMA((len(pieces),)),
            ],
        ),
        compiler_params=params(16 if n_band <= 16 else 32),
        cost_estimate=cost(
            2 * blk_count * block_rows * width * list_len * tile_rows, latent, latent, interp
        ),
        name="back",
    )(*lists, latent, interp, *pieces)
    return (grid_out, mesh_out)


def solution(mesh):
    placed = (
        P(("groups", "band"), None),
        P(("groups", "band"), None),
        P(),
        P(),
        P(),
        P("band", None, None, None),
        P(),
        P(),
        P(),
        P(),
        P(),
    )
    n_y = max(1, 4 // mesh.shape["groups"])
    return jax.shard_map(
        functools.partial(on_device, n_y),
        mesh=mesh,
        in_specs=placed,
        out_specs=(P(("groups", "band"), None), P(("groups", "band"), None)),
        check_vma=False,
    )
```

time: 115 us -> 104 us (0.904)
  starting transfers between devices: 18.8 us -> 34.1 us
  Pallas kernels: 38.4 us -> 24.9 us
  waiting for transfers between devices: 48.4 us -> 35.2 us
  local copies, waits for them, and re-layouts: 6.47 us -> 7.76 us
    ppermute x26 -> x44, starting transfers between devices: 18.8 us -> 34.1 us  [the longest x28 32.2 us: over(): return lax.ppermute(value, 'band', pairs)]
    pallas_call x7 -> x5, Pallas kernels: 38.4 us -> 24.9 us  [the longest x1 11.2 us: on_device(): pl.pallas_call(functools.partial(back_kernel, ring, places, per_step), ou...]
    ppermute x26 -> x44, waiting for transfers between devices: 48.4 us -> 35.2 us  [the longest x28 31.6 us: over(): return lax.ppermute(value, 'band', pairs)]
    unnamed x54 -> x28, local copies, waits for them, and re-layouts: 4.94 us -> 7.76 us
    another operation x2 -> x0, other arithmetic: 1.17 us -> none  [the longest x1 0.6 us: on_device(): jnp.stack([(across * chips + ahead) * slots + slot_of, mine(block_mask, m...]
    transpose x5 -> x0, local copies, waits for them, and re-layouts: 1.16 us -> none  [mine(): return rows.T.reshape(entries)]
  transfers between devices with their start and end apart: 26 -> 44, of which waited for: 16 -> 25; matrix products, arithmetic and copies ran while one was open for 1% -> 0% of each run, Pallas kernels for 0% -> 1%
where the time goes in v3:
time: 104 us; the launch traced here: 103 us
  waiting for transfers between devices  35.2 us (34%)
  starting transfers between devices  34.1 us (33%)
  Pallas kernels  24.9 us (24%)
  local copies, waits for them, and re-layouts  7.76 us (7%)
    ppermute x28, starting transfers between devices, over(): return lax.ppermute(value, 'band', pairs)  32.2 us
    ppermute x28, waiting for transfers between devices, over(): return lax.ppermute(value, 'band', pairs)  31.6 us
    pallas_call x1, Pallas kernels, on_device(): pl.pallas_call(functools.partial(back_kernel, ring, places, per_step), ou...  11.2 us
    pallas_call x1, Pallas kernels, on_device(): pl.pallas_call(functools.partial(embed_kernel, ring, per_step, slots), ou...  10.1 us
    unnamed x28, local copies, waits for them, and re-layouts  7.76 us
    ppermute x16, waiting for transfers between devices, over_core(): return lax.ppermute(value, 'band', [(i, i ^ 1) for i in range(self.n_band)])  3.65 us
  transfers between devices with their start and end apart: 44, of which 25 were waited for; matrix products, arithmetic and copies ran while one was open for 0% of the time, Pallas kernels for 1%

profile of v3, /device:TPU:0, one launch (start us, length us, event | category | flops | bytes accessed | tf_op | source)
XLA Modules:
  0.0 103.3 jit_solution(5598314077376831723)
XLA Ops:
  3.2 1.5 %copy-done.10 = bf16[4096,227]{0,1:T(8,128)(2,1)S(1)} copy-done((bf16[4096,227]{0,1:T(8,128)(2,1)S(1)}, bf16[4096,227]{0,1:T(8,128)(2,1)}, u32[]{:S(2)}) %copy-start.10) | copy-done | bytes 1859608
  7.4 10.1 %embed.1 = (bf16[4096,512]{1,0:T(8,128)(2,1)S(1)}, bf16[32,32,512]{2,1,0:T(8,128)(2,1)S(1)}, bf16[32,32,512]{2,1,0:T(8,128)(2,1)S(1)}, s32[2,64]{1,0:T(2,128)S(1)}) custom-call(s32[1]{0:T(128)} %bitcast.me_ref, s32[4,256]{1,0:T(4,128)S(1)} %bitcast.66, s32[4,256]{1,0:T(4,128)S(1)} %bitcast.68, bf16[227,4096]{1,0:T(8,128)(2,1)S(1)} %bitcast.71, ...), custom_call_target="tpu_custom_call" | custom-call | flops 3636461568 | bytes 2908160 | tf_op jit(solution)/shard_map/embed/pallas_call | solution.py:245
  18.1 2.3 %collective-permute-done.other.refs_3_.refs_4_.refs_5_ = bf16[32,32,512]{2,1,0:T(8,128)(2,1)S(1)} collective-permute-done((bf16[32,32,512]{2,1,0:T(8,128)(2,1)S(1)}, bf16[32,32,512]{2,1,0:T(8,128)(2,1)S(1)}, u32[]{:S(2)}, u32[]{:S(2)}) %collective-permute-start) | collective-permute-done | bytes 1048608 | tf_op jit(solution)/shard_map/ppermute | solution.py:50
  21.2 2.9 %collective-permute-start.12 = (bf16[4,32,512]{2,1,0:T(8,128)(2,1)S(1)}, bf16[4,32,512]{2,1,0:T(8,128)(2,1)S(1)}, u32[]{:S(2)}, u32[]{:S(2)}) collective-permute-start(bf16[4,32,512]{2,1,0:T(8,128)(2,1)S(1)} %get-tuple-element.20), channel_id=1, source_target_pairs={{0,2},{1,3},{2,6},{3,7},{4,0},{5,1},{6,10},{7,11},{8,4},{9,5},{10,... | collective-permute-start | bytes 393224 | tf_op jit(solution)/shard_map/ppermute | solution.py:59
  24.3 1.9 %collective-permute-start.5 = (bf16[4,32,512]{2,1,0:T(8,128)(2,1)S(1)}, bf16[4,32,512]{2,1,0:T(8,128)(2,1)S(1)}, u32[]{:S(2)}, u32[]{:S(2)}) collective-permute-start(bf16[4,32,512]{2,1,0:T(8,128)(2,1)S(1)} %get-tuple-element.18), channel_id=1, source_target_pairs={{0,2},{1,3},{2,6},{3,7},{4,0},{5,1},{6,10},{7,11},{8,4},{9,5},{10,... | collective-permute-start | bytes 393224 | tf_op jit(solution)/shard_map/ppermute | solution.py:59
  28.5 2.1 %collective-permute-start.13 = (bf16[4,32,512]{2,1,0:T(8,128)(2,1)S(1)}, bf16[4,32,512]{2,1,0:T(8,128)(2,1)S(1)}, u32[]{:S(2)}, u32[]{:S(2)}) collective-permute-start(bf16[4,32,512]{2,1,0:T(8,128)(2,1)S(1)} %fusion.1), channel_id=1, source_target_pairs={{0,2},{1,3},{2,6},{3,7},{4,0},{5,1},{6,10},{7,11},{8,4},{9,5},{10,... | collective-permute-start | bytes 393224 | tf_op jit(solution)/shard_map/ppermute | solution.py:59
  32.2 1.4 %collective-permute-done.13 = bf16[4,32,512]{2,1,0:T(8,128)(2,1)S(1)} collective-permute-done((bf16[4,32,512]{2,1,0:T(8,128)(2,1)S(1)}, bf16[4,32,512]{2,1,0:T(8,128)(2,1)S(1)}, u32[]{:S(2)}, u32[]{:S(2)}) %collective-permute-start.13) | collective-permute-done | bytes 131104 | tf_op jit(solution)/shard_map/ppermute | solution.py:59
  33.9 2.0 %collective-permute-start.10 = (bf16[4,32,512]{2,1,0:T(8,128)(2,1)S(1)}, bf16[4,32,512]{2,1,0:T(8,128)(2,1)S(1)}, u32[]{:S(2)}, u32[]{:S(2)}) collective-permute-start(bf16[4,32,512]{2,1,0:T(8,128)(2,1)S(1)} %get-tuple-element.25), channel_id=1, source_target_pairs={{0,4},{1,5},{2,0},{3,1},{4,8},{5,9},{6,2},{7,3},{8,12},{9,13},{10,... | collective-permute-start | bytes 393224 | tf_op jit(solution)/shard_map/ppermute | solution.py:59
  35.9 2.0 %collective-permute-start.2 = (bf16[4,32,512]{2,1,0:T(8,128)(2,1)S(1)}, bf16[4,32,512]{2,1,0:T(8,128)(2,1)S(1)}, u32[]{:S(2)}, u32[]{:S(2)}) collective-permute-start(bf16[4,32,512]{2,1,0:T(8,128)(2,1)S(1)} %get-tuple-element.27), channel_id=1, source_target_pairs={{0,4},{1,5},{2,0},{3,1},{4,8},{5,9},{6,2},{7,3},{8,12},{9,13},{10,... | collective-permute-start | bytes 393224 | tf_op jit(solution)/shard_map/ppermute | solution.py:59
  37.9 1.6 %collective-permute-done.10 = bf16[4,32,512]{2,1,0:T(8,128)(2,1)S(1)} collective-permute-done((bf16[4,32,512]{2,1,0:T(8,128)(2,1)S(1)}, bf16[4,32,512]{2,1,0:T(8,128)(2,1)S(1)}, u32[]{:S(2)}, u32[]{:S(2)}) %collective-permute-start.10) | collective-permute-done | bytes 131104 | tf_op jit(solution)/shard_map/ppermute | solution.py:59
  39.5 1.4 %collective-permute-done.6 = bf16[4,32,512]{2,1,0:T(8,128)(2,1)S(1)} collective-permute-done((bf16[4,32,512]{2,1,0:T(8,128)(2,1)S(1)}, bf16[4,32,512]{2,1,0:T(8,128)(2,1)S(1)}, u32[]{:S(2)}, u32[]{:S(2)}) %collective-permute-start.6) | collective-permute-done | bytes 131104 | tf_op jit(solution)/shard_map/ppermute | solution.py:59
  41.1 2.0 %collective-permute-start.7 = (bf16[4,32,512]{2,1,0:T(8,128)(2,1)S(1)}, bf16[4,32,512]{2,1,0:T(8,128)(2,1)S(1)}, u32[]{:S(2)}, u32[]{:S(2)}) collective-permute-start(bf16[4,32,512]{2,1,0:T(8,128)(2,1)S(1)} %get-tuple-element.29), channel_id=1, source_target_pairs={{0,2},{1,3},{2,6},{3,7},{4,0},{5,1},{6,10},{7,11},{8,4},{9,5},{10,... | collective-permute-start | bytes 393224 | tf_op jit(solution)/shard_map/ppermute | solution.py:59
  43.1 1.9 %collective-permute-start.14 = (bf16[4,32,512]{2,1,0:T(8,128)(2,1)S(1)}, bf16[4,32,512]{2,1,0:T(8,128)(2,1)S(1)}, u32[]{:S(2)}, u32[]{:S(2)}) collective-permute-start(bf16[4,32,512]{2,1,0:T(8,128)(2,1)S(1)} %get-tuple-element.24), channel_id=1, source_target_pairs={{0,2},{1,3},{2,6},{3,7},{4,0},{5,1},{6,10},{7,11},{8,4},{9,5},{10,... | collective-permute-start | bytes 393224 | tf_op jit(solution)/shard_map/ppermute | solution.py:59
  46.1 2.1 %collective-permute-done.3 = bf16[4,32,512]{2,1,0:T(8,128)(2,1)S(1)} collective-permute-done((bf16[4,32,512]{2,1,0:T(8,128)(2,1)S(1)}, bf16[4,32,512]{2,1,0:T(8,128)(2,1)S(1)}, u32[]{:S(2)}, u32[]{:S(2)}) %collective-permute-start.3) | collective-permute-done | bytes 131104 | tf_op jit(solution)/shard_map/ppermute | solution.py:59
  48.2 1.6 %collective-permute-start.8 = (bf16[4,32,512]{2,1,0:T(8,128)(2,1)S(1)}, bf16[4,32,512]{2,1,0:T(8,128)(2,1)S(1)}, u32[]{:S(2)}, u32[]{:S(2)}) collective-permute-start(bf16[4,32,512]{2,1,0:T(8,128)(2,1)S(1)} %get-tuple-element.31), channel_id=1, source_target_pairs={{0,2},{1,3},{2,6},{3,7},{4,0},{5,1},{6,10},{7,11},{8,4},{9,5},{10,... | collective-permute-start | bytes 393224 | tf_op jit(solution)/shard_map/ppermute | solution.py:59
  50.8 2.5 %collective-permute-done.8.left_b = bf16[4,32,512]{2,1,0:T(8,128)(2,1)S(1)} collective-permute-done((bf16[4,32,512]{2,1,0:T(8,128)(2,1)S(1)}, bf16[4,32,512]{2,1,0:T(8,128)(2,1)S(1)}, u32[]{:S(2)}, u32[]{:S(2)}) %collective-permute-start.8) | collective-permute-done | bytes 131104 | tf_op jit(solution)/shard_map/ppermute | solution.py:59
  53.3 1.6 %collective-permute-done.4.right_a = bf16[4,32,512]{2,1,0:T(8,128)(2,1)S(1)} collective-permute-done((bf16[4,32,512]{2,1,0:T(8,128)(2,1)S(1)}, bf16[4,32,512]{2,1,0:T(8,128)(2,1)S(1)}, u32[]{:S(2)}, u32[]{:S(2)}) %collective-permute-start.4) | collective-permute-done | bytes 131104 | tf_op jit(solution)/shard_map/ppermute | solution.py:59
  54.9 1.5 %mesh_step.1 = (bf16[256,512]{1,0:T(8,128)(2,1)}, bf16[128,512]{1,0:T(8,128)(2,1)S(1)}, bf16[128,512]{1,0:T(8,128)(2,1)S(1)}) custom-call(bf16[256,512]{1,0:T(8,128)(2,1)S(1)} %copy-done.3, bf16[512,512]{1,0:T(8,128)(2,1)S(1)} %copy-done.1, bf16[512,512]{1,0:T(8,128)(2,1)S(1)} %copy-done.2, f32[1,512]{1,0:T(1,128)S(1)} %bitcast.70, ...), custom_call_target="tpu_custom_call" | custom-call | flops 268435456 | bytes 1048576 | tf_op jit(solution)/shard_map/mesh_step/pallas_call | solution.py:331
  56.4 2.2 %collective-permute-start.22 = (bf16[128,512]{1,0:T(8,128)(2,1)S(1)}, bf16[128,512]{1,0:T(8,128)(2,1)S(1)}, u32[]{:S(2)}, u32[]{:S(2)}) collective-permute-start(bf16[128,512]{1,0:T(8,128)(2,1)S(1)} %get-tuple-element.22), channel_id=1, source_target_pairs={{0,2},{1,3},{2,6},{3,7},{4,0},{5,1},{6,10},{7,11},{8,4},{9,5},{10,... | collective-permute-start | bytes 393224 | tf_op jit(solution)/shard_map/ppermute | solution.py:59
  58.8 1.9 %collective-permute-start.18 = (bf16[128,512]{1,0:T(8,128)(2,1)S(1)}, bf16[128,512]{1,0:T(8,128)(2,1)S(1)}, u32[]{:S(2)}, u32[]{:S(2)}) collective-permute-start(bf16[128,512]{1,0:T(8,128)(2,1)S(1)} %get-tuple-element.23), channel_id=1, source_target_pairs={{0,2},{1,3},{2,6},{3,7},{4,0},{5,1},{6,10},{7,11},{8,4},{9,5},{10,... | collective-permute-start | bytes 393224 | tf_op jit(solution)/shard_map/ppermute | solution.py:59
  60.7 2.0 %collective-permute-done.22.rest_8_ = bf16[128,512]{1,0:T(8,128)(2,1)S(1)} collective-permute-done((bf16[128,512]{1,0:T(8,128)(2,1)S(1)}, bf16[128,512]{1,0:T(8,128)(2,1)S(1)}, u32[]{:S(2)}, u32[]{:S(2)}) %collective-permute-start.22) | collective-permute-done | bytes 131104 | tf_op jit(solution)/shard_map/ppermute | solution.py:59
  62.7 2.2 %collective-permute-start.30 = (bf16[128,512]{1,0:T(8,128)(2,1)S(1)}, bf16[128,512]{1,0:T(8,128)(2,1)S(1)}, u32[]{:S(2)}, u32[]{:S(2)}) collective-permute-start(bf16[128,512]{1,0:T(8,128)(2,1)S(1)} %collective-permute-done.22.rest_8_), channel_id=1, source_target_pairs={{0,2},{1,3},{2,6},{3,7},{4,0},{5,1},{6,10},{7,11},{8,4},{9,5},{10,... | collective-permute-start | bytes 393224 | tf_op jit(solution)/shard_map/ppermute | solution.py:59
  64.9 2.4 %collective-permute-done.20.rest_6_ = bf16[128,512]{1,0:T(8,128)(2,1)S(1)} collective-permute-done((bf16[128,512]{1,0:T(8,128)(2,1)S(1)}, bf16[128,512]{1,0:T(8,128)(2,1)S(1)}, u32[]{:S(2)}, u32[]{:S(2)}) %collective-permute-start.20) | collective-permute-done | bytes 131104 | tf_op jit(solution)/shard_map/ppermute | solution.py:59
  67.9 2.2 %collective-permute-start.26 = (bf16[128,512]{1,0:T(8,128)(2,1)S(1)}, bf16[128,512]{1,0:T(8,128)(2,1)S(1)}, u32[]{:S(2)}, u32[]{:S(2)}) collective-permute-start(bf16[128,512]{1,0:T(8,128)(2,1)S(1)} %collective-permute-done.18.rest_4_), channel_id=1, source_target_pairs={{0,2},{1,3},{2,6},{3,7},{4,0},{5,1},{6,10},{7,11},{8,4},{9,5},{10,... | collective-permute-start | bytes 393224 | tf_op jit(solution)/shard_map/ppermute | solution.py:59
  70.1 3.6 %collective-permute-done.24.rest_10_ = bf16[128,512]{1,0:T(8,128)(2,1)S(1)} collective-permute-done((bf16[128,512]{1,0:T(8,128)(2,1)S(1)}, bf16[128,512]{1,0:T(8,128)(2,1)S(1)}, u32[]{:S(2)}, u32[]{:S(2)}) %collective-permute-start.24) | collective-permute-done | bytes 131104 | tf_op jit(solution)/shard_map/ppermute | solution.py:59
  73.7 1.6 %collective-permute-start.38 = (bf16[128,512]{1,0:T(8,128)(2,1)S(1)}, bf16[128,512]{1,0:T(8,128)(2,1)S(1)}, u32[]{:S(2)}, u32[]{:S(2)}) collective-permute-start(bf16[128,512]{1,0:T(8,128)(2,1)S(1)} %collective-permute-done.30.rest_16_), channel_id=1, source_target_pairs={{0,2},{1,3},{2,6},{3,7},{4,0},{5,1},{6,10},{7,11},{8,4},{9,5},{10,... | collective-permute-start | bytes 393224 | tf_op jit(solution)/shard_map/ppermute | solution.py:59
  76.4 3.3 %collective-permute-done.38.rest_24_ = bf16[128,512]{1,0:T(8,128)(2,1)S(1)} collective-permute-done((bf16[128,512]{1,0:T(8,128)(2,1)S(1)}, bf16[128,512]{1,0:T(8,128)(2,1)S(1)}, u32[]{:S(2)}, u32[]{:S(2)}) %collective-permute-start.38) | collective-permute-done | bytes 131104 | tf_op jit(solution)/shard_map/ppermute | solution.py:59
  79.6 1.6 %collective-permute-start.34 = (bf16[128,512]{1,0:T(8,128)(2,1)S(1)}, bf16[128,512]{1,0:T(8,128)(2,1)S(1)}, u32[]{:S(2)}, u32[]{:S(2)}) collective-permute-start(bf16[128,512]{1,0:T(8,128)(2,1)S(1)} %collective-permute-done.26.rest_12_), channel_id=1, source_target_pairs={{0,2},{1,3},{2,6},{3,7},{4,0},{5,1},{6,10},{7,11},{8,4},{9,5},{10,... | collective-permute-start | bytes 393224 | tf_op jit(solution)/shard_map/ppermute | solution.py:59
  82.4 1.7 %collective-permute-done.36.rest_22_ = bf16[128,512]{1,0:T(8,128)(2,1)S(1)} collective-permute-done((bf16[128,512]{1,0:T(8,128)(2,1)S(1)}, bf16[128,512]{1,0:T(8,128)(2,1)S(1)}, u32[]{:S(2)}, u32[]{:S(2)}) %collective-permute-start.36) | collective-permute-done | bytes 131104 | tf_op jit(solution)/shard_map/ppermute | solution.py:59
  84.8 1.6 %collective-permute-start.42 = (bf16[128,512]{1,0:T(8,128)(2,1)S(1)}, bf16[128,512]{1,0:T(8,128)(2,1)S(1)}, u32[]{:S(2)}, u32[]{:S(2)}) collective-permute-start(bf16[128,512]{1,0:T(8,128)(2,1)S(1)} %collective-permute-done.34.rest_20_), channel_id=1, source_target_pairs={{0,2},{1,3},{2,6},{3,7},{4,0},{5,1},{6,10},{7,11},{8,4},{9,5},{10,... | collective-permute-start | bytes 393224 | tf_op jit(solution)/shard_map/ppermute | solution.py:59
  86.9 2.1 %collective-permute-done.40.rest_26_ = bf16[128,512]{1,0:T(8,128)(2,1)S(1)} collective-permute-done((bf16[128,512]{1,0:T(8,128)(2,1)S(1)}, bf16[128,512]{1,0:T(8,128)(2,1)S(1)}, u32[]{:S(2)}, u32[]{:S(2)}) %collective-permute-start.40) | collective-permute-done | bytes 131104 | tf_op jit(solution)/shard_map/ppermute | solution.py:59
  92.0 11.2 %back.1 = bf16[4096,512]{1,0:T(8,128)(2,1)} custom-call(s32[1]{0:T(128)} %bitcast.me_ref, s32[4,256]{1,0:T(4,128)S(1)} %bitcast.67, s32[4,256]{1,0:T(4,128)S(1)} %bitcast.69, bf16[4096,512]{1,0:T(8,128)(2,1)S(1)} %get-tuple-element.13.latent_ref, bf16[16,4,32,256]{3,2,1,0:T(8,128)(2,1)S(1)} %copy-done, bf16[256,512]{1,0:T(8,128)(2,1)S(1)} %copy-done.4, ...), custom_call_target="tpu_custom_call" | custom-call | flops 536870912 | bytes 9437184 | tf_op jit(solution)/shard_map/back/pallas_call | solution.py:365
  (93 shorter events, 20.7 us)
Async XLA Ops:
  21.2 7.3 %collective-permute-start.12 = (bf16[4,32,512]{2,1,0:T(8,128)(2,1)S(1)}, bf16[4,32,512]{2,1,0:T(8,128)(2,1)S(1)}, u32[]{:S(2)}, u32[]{:S(2)}) collective-permute-start(bf16[4,32,512]{2,1,0:T(8,128)(2,1)S(1)} %get-tuple-element.20), channel_id=1, source_target_pairs={{0,2},{1,3},{2,6},{3,7},{4,0},{5,1},{6,10},{7,11},{8,4},{9,5},{10,... | collective-permute-start | bytes 393224 | tf_op jit(solution)/shard_map/ppermute | solution.py:59
  24.2 6.4 %collective-permute-start.1 = (bf16[4,32,512]{2,1,0:T(8,128)(2,1)S(1)}, bf16[4,32,512]{2,1,0:T(8,128)(2,1)S(1)}, u32[]{:S(2)}, u32[]{:S(2)}) collective-permute-start(bf16[4,32,512]{2,1,0:T(8,128)(2,1)S(1)} %get-tuple-element.17), channel_id=1, source_target_pairs={{0,4},{1,5},{2,0},{3,1},{4,8},{5,9},{6,2},{7,3},{8,12},{9,13},{10,... | collective-permute-start | bytes 393224 | tf_op jit(solution)/shard_map/ppermute | solution.py:59
  24.3 7.0 %collective-permute-start.5 = (bf16[4,32,512]{2,1,0:T(8,128)(2,1)S(1)}, bf16[4,32,512]{2,1,0:T(8,128)(2,1)S(1)}, u32[]{:S(2)}, u32[]{:S(2)}) collective-permute-start(bf16[4,32,512]{2,1,0:T(8,128)(2,1)S(1)} %get-tuple-element.18), channel_id=1, source_target_pairs={{0,2},{1,3},{2,6},{3,7},{4,0},{5,1},{6,10},{7,11},{8,4},{9,5},{10,... | collective-permute-start | bytes 393224 | tf_op jit(solution)/shard_map/ppermute | solution.py:59
  26.2 6.0 %collective-permute-start.9 = (bf16[4,32,512]{2,1,0:T(8,128)(2,1)S(1)}, bf16[4,32,512]{2,1,0:T(8,128)(2,1)S(1)}, u32[]{:S(2)}, u32[]{:S(2)}) collective-permute-start(bf16[4,32,512]{2,1,0:T(8,128)(2,1)S(1)} %get-tuple-element.19), channel_id=1, source_target_pairs={{0,4},{1,5},{2,0},{3,1},{4,8},{5,9},{6,2},{7,3},{8,12},{9,13},{10,... | collective-permute-start | bytes 393224 | tf_op jit(solution)/shard_map/ppermute | solution.py:59
  28.5 5.1 %collective-permute-start.13 = (bf16[4,32,512]{2,1,0:T(8,128)(2,1)S(1)}, bf16[4,32,512]{2,1,0:T(8,128)(2,1)S(1)}, u32[]{:S(2)}, u32[]{:S(2)}) collective-permute-start(bf16[4,32,512]{2,1,0:T(8,128)(2,1)S(1)} %fusion.1), channel_id=1, source_target_pairs={{0,2},{1,3},{2,6},{3,7},{4,0},{5,1},{6,10},{7,11},{8,4},{9,5},{10,... | collective-permute-start | bytes 393224 | tf_op jit(solution)/shard_map/ppermute | solution.py:59
  33.9 5.6 %collective-permute-start.10 = (bf16[4,32,512]{2,1,0:T(8,128)(2,1)S(1)}, bf16[4,32,512]{2,1,0:T(8,128)(2,1)S(1)}, u32[]{:S(2)}, u32[]{:S(2)}) collective-permute-start(bf16[4,32,512]{2,1,0:T(8,128)(2,1)S(1)} %get-tuple-element.25), channel_id=1, source_target_pairs={{0,4},{1,5},{2,0},{3,1},{4,8},{5,9},{6,2},{7,3},{8,12},{9,13},{10,... | collective-permute-start | bytes 393224 | tf_op jit(solution)/shard_map/ppermute | solution.py:59
  35.9 5.0 %collective-permute-start.6 = (bf16[4,32,512]{2,1,0:T(8,128)(2,1)S(1)}, bf16[4,32,512]{2,1,0:T(8,128)(2,1)S(1)}, u32[]{:S(2)}, u32[]{:S(2)}) collective-permute-start(bf16[4,32,512]{2,1,0:T(8,128)(2,1)S(1)} %get-tuple-element.26), channel_id=1, source_target_pairs={{0,2},{1,3},{2,6},{3,7},{4,0},{5,1},{6,10},{7,11},{8,4},{9,5},{10,... | collective-permute-start | bytes 393224 | tf_op jit(solution)/shard_map/ppermute | solution.py:59
  41.1 5.0 %collective-permute-start.7 = (bf16[4,32,512]{2,1,0:T(8,128)(2,1)S(1)}, bf16[4,32,512]{2,1,0:T(8,128)(2,1)S(1)}, u32[]{:S(2)}, u32[]{:S(2)}) collective-permute-start(bf16[4,32,512]{2,1,0:T(8,128)(2,1)S(1)} %get-tuple-element.29), channel_id=1, source_target_pairs={{0,2},{1,3},{2,6},{3,7},{4,0},{5,1},{6,10},{7,11},{8,4},{9,5},{10,... | collective-permute-start | bytes 393224 | tf_op jit(solution)/shard_map/ppermute | solution.py:59
  43.0 5.1 %collective-permute-start.3 = (bf16[4,32,512]{2,1,0:T(8,128)(2,1)S(1)}, bf16[4,32,512]{2,1,0:T(8,128)(2,1)S(1)}, u32[]{:S(2)}, u32[]{:S(2)}) collective-permute-start(bf16[4,32,512]{2,1,0:T(8,128)(2,1)S(1)} %get-tuple-element.30), channel_id=1, source_target_pairs={{0,4},{1,5},{2,0},{3,1},{4,8},{5,9},{6,2},{7,3},{8,12},{9,13},{10,... | collective-permute-start | bytes 393224 | tf_op jit(solution)/shard_map/ppermute | solution.py:59
  43.1 7.2 %collective-permute-start.14 = (bf16[4,32,512]{2,1,0:T(8,128)(2,1)S(1)}, bf16[4,32,512]{2,1,0:T(8,128)(2,1)S(1)}, u32[]{:S(2)}, u32[]{:S(2)}) collective-permute-start(bf16[4,32,512]{2,1,0:T(8,128)(2,1)S(1)} %get-tuple-element.24), channel_id=1, source_target_pairs={{0,2},{1,3},{2,6},{3,7},{4,0},{5,1},{6,10},{7,11},{8,4},{9,5},{10,... | collective-permute-start | bytes 393224 | tf_op jit(solution)/shard_map/ppermute | solution.py:59
  45.1 5.8 %collective-permute-start.11 = (bf16[4,32,512]{2,1,0:T(8,128)(2,1)S(1)}, bf16[4,32,512]{2,1,0:T(8,128)(2,1)S(1)}, u32[]{:S(2)}, u32[]{:S(2)}) collective-permute-start(bf16[4,32,512]{2,1,0:T(8,128)(2,1)S(1)} %get-tuple-element.28), channel_id=1, source_target_pairs={{0,4},{1,5},{2,0},{3,1},{4,8},{5,9},{6,2},{7,3},{8,12},{9,13},{10,... | collective-permute-start | bytes 393224 | tf_op jit(solution)/shard_map/ppermute | solution.py:59
  48.2 5.0 %collective-permute-start.8 = (bf16[4,32,512]{2,1,0:T(8,128)(2,1)S(1)}, bf16[4,32,512]{2,1,0:T(8,128)(2,1)S(1)}, u32[]{:S(2)}, u32[]{:S(2)}) collective-permute-start(bf16[4,32,512]{2,1,0:T(8,128)(2,1)S(1)} %get-tuple-element.31), channel_id=1, source_target_pairs={{0,2},{1,3},{2,6},{3,7},{4,0},{5,1},{6,10},{7,11},{8,4},{9,5},{10,... | collective-permute-start | bytes 393224 | tf_op jit(solution)/shard_map/ppermute | solution.py:59
  49.9 5.0 %collective-permute-start.4 = (bf16[4,32,512]{2,1,0:T(8,128)(2,1)S(1)}, bf16[4,32,512]{2,1,0:T(8,128)(2,1)S(1)}, u32[]{:S(2)}, u32[]{:S(2)}) collective-permute-start(bf16[4,32,512]{2,1,0:T(8,128)(2,1)S(1)} %get-tuple-element.32), channel_id=1, source_target_pairs={{0,4},{1,5},{2,0},{3,1},{4,8},{5,9},{6,2},{7,3},{8,12},{9,13},{10,... | collective-permute-start | bytes 393224 | tf_op jit(solution)/shard_map/ppermute | solution.py:59
  56.4 11.0 %collective-permute-start.15 = (bf16[256,512]{1,0:T(8,128)(2,1)}, bf16[256,512]{1,0:T(8,128)(2,1)S(1)}, u32[]{:S(2)}, u32[]{:S(2)}) collective-permute-start(bf16[256,512]{1,0:T(8,128)(2,1)} %get-tuple-element.12.rest_0_), channel_id=1, source_target_pairs={{0,1},{1,0},{2,3},{3,2},{4,5},{5,4},{6,7},{7,6},{8,9},{9,8},{10,11... | collective-permute-start | bytes 786440 | tf_op jit(solution)/shard_map/ppermute | solution.py:50
  56.4 6.3 %collective-permute-start.22 = (bf16[128,512]{1,0:T(8,128)(2,1)S(1)}, bf16[128,512]{1,0:T(8,128)(2,1)S(1)}, u32[]{:S(2)}, u32[]{:S(2)}) collective-permute-start(bf16[128,512]{1,0:T(8,128)(2,1)S(1)} %get-tuple-element.22), channel_id=1, source_target_pairs={{0,2},{1,3},{2,6},{3,7},{4,0},{5,1},{6,10},{7,11},{8,4},{9,5},{10,... | collective-permute-start | bytes 393224 | tf_op jit(solution)/shard_map/ppermute | solution.py:59
  58.6 6.3 %collective-permute-start.16 = (bf16[128,512]{1,0:T(8,128)(2,1)S(1)}, bf16[128,512]{1,0:T(8,128)(2,1)S(1)}, u32[]{:S(2)}, u32[]{:S(2)}) collective-permute-start(bf16[128,512]{1,0:T(8,128)(2,1)S(1)} %get-tuple-element.22), channel_id=1, source_target_pairs={{0,4},{1,5},{2,0},{3,1},{4,8},{5,9},{6,2},{7,3},{8,12},{9,13},{10,... | collective-permute-start | bytes 393224 | tf_op jit(solution)/shard_map/ppermute | solution.py:59
  58.6 8.7 %collective-permute-start.20 = (bf16[128,512]{1,0:T(8,128)(2,1)S(1)}, bf16[128,512]{1,0:T(8,128)(2,1)S(1)}, u32[]{:S(2)}, u32[]{:S(2)}) collective-permute-start(bf16[128,512]{1,0:T(8,128)(2,1)S(1)} %get-tuple-element.23), channel_id=1, source_target_pairs={{0,4},{1,5},{2,0},{3,1},{4,8},{5,9},{6,2},{7,3},{8,12},{9,13},{10,... | collective-permute-start | bytes 393224 | tf_op jit(solution)/shard_map/ppermute | solution.py:59
  58.8 8.5 %collective-permute-start.18 = (bf16[128,512]{1,0:T(8,128)(2,1)S(1)}, bf16[128,512]{1,0:T(8,128)(2,1)S(1)}, u32[]{:S(2)}, u32[]{:S(2)}) collective-permute-start(bf16[128,512]{1,0:T(8,128)(2,1)S(1)} %get-tuple-element.23), channel_id=1, source_target_pairs={{0,2},{1,3},{2,6},{3,7},{4,0},{5,1},{6,10},{7,11},{8,4},{9,5},{10,... | collective-permute-start | bytes 393224 | tf_op jit(solution)/shard_map/ppermute | solution.py:59
  62.7 5.2 %collective-permute-start.30 = (bf16[128,512]{1,0:T(8,128)(2,1)S(1)}, bf16[128,512]{1,0:T(8,128)(2,1)S(1)}, u32[]{:S(2)}, u32[]{:S(2)}) collective-permute-start(bf16[128,512]{1,0:T(8,128)(2,1)S(1)} %collective-permute-done.22.rest_8_), channel_id=1, source_target_pairs={{0,2},{1,3},{2,6},{3,7},{4,0},{5,1},{6,10},{7,11},{8,4},{9,5},{10,... | collective-permute-start | bytes 393224 | tf_op jit(solution)/shard_map/ppermute | solution.py:59
  67.3 6.4 %collective-permute-start.24 = (bf16[128,512]{1,0:T(8,128)(2,1)S(1)}, bf16[128,512]{1,0:T(8,128)(2,1)S(1)}, u32[]{:S(2)}, u32[]{:S(2)}) collective-permute-start(bf16[128,512]{1,0:T(8,128)(2,1)S(1)} %collective-permute-done.16.rest_2_), channel_id=1, source_target_pairs={{0,4},{1,5},{2,0},{3,1},{4,8},{5,9},{6,2},{7,3},{8,12},{9,13},{10,... | collective-permute-start | bytes 393224 | tf_op jit(solution)/shard_map/ppermute | solution.py:59
  67.3 6.4 %collective-permute-start.17 = (bf16[128,512]{1,0:T(8,128)(2,1)S(1)}, bf16[128,512]{1,0:T(8,128)(2,1)S(1)}, u32[]{:S(2)}, u32[]{:S(2)}) collective-permute-start(bf16[128,512]{1,0:T(8,128)(2,1)S(1)} %collective-permute-done.16.rest_2_), channel_id=1, source_target_pairs={{0,1},{1,0},{2,3},{3,2},{4,5},{5,4},{6,7},{7,6},{8,9},{9,8},{10,11... | collective-permute-start | bytes 393224 | tf_op jit(solution)/shard_map/ppermute | solution.py:50
  67.3 7.9 %collective-permute-start.28 = (bf16[128,512]{1,0:T(8,128)(2,1)S(1)}, bf16[128,512]{1,0:T(8,128)(2,1)S(1)}, u32[]{:S(2)}, u32[]{:S(2)}) collective-permute-start(bf16[128,512]{1,0:T(8,128)(2,1)S(1)} %collective-permute-done.20.rest_6_), channel_id=1, source_target_pairs={{0,4},{1,5},{2,0},{3,1},{4,8},{5,9},{6,2},{7,3},{8,12},{9,13},{10,... | collective-permute-start | bytes 393224 | tf_op jit(solution)/shard_map/ppermute | solution.py:59
  67.9 7.6 %collective-permute-start.21 = (bf16[128,512]{1,0:T(8,128)(2,1)S(1)}, bf16[128,512]{1,0:T(8,128)(2,1)S(1)}, u32[]{:S(2)}, u32[]{:S(2)}) collective-permute-start(bf16[128,512]{1,0:T(8,128)(2,1)S(1)} %collective-permute-done.20.rest_6_), channel_id=1, source_target_pairs={{0,1},{1,0},{2,3},{3,2},{4,5},{5,4},{6,7},{7,6},{8,9},{9,8},{10,11... | collective-permute-start | bytes 393224 | tf_op jit(solution)/shard_map/ppermute | solution.py:50
  67.9 8.1 %collective-permute-start.26 = (bf16[128,512]{1,0:T(8,128)(2,1)S(1)}, bf16[128,512]{1,0:T(8,128)(2,1)S(1)}, u32[]{:S(2)}, u32[]{:S(2)}) collective-permute-start(bf16[128,512]{1,0:T(8,128)(2,1)S(1)} %collective-permute-done.18.rest_4_), channel_id=1, source_target_pairs={{0,2},{1,3},{2,6},{3,7},{4,0},{5,1},{6,10},{7,11},{8,4},{9,5},{10,... | collective-permute-start | bytes 393224 | tf_op jit(solution)/shard_map/ppermute | solution.py:59
  73.7 5.9 %collective-permute-start.38 = (bf16[128,512]{1,0:T(8,128)(2,1)S(1)}, bf16[128,512]{1,0:T(8,128)(2,1)S(1)}, u32[]{:S(2)}, u32[]{:S(2)}) collective-permute-start(bf16[128,512]{1,0:T(8,128)(2,1)S(1)} %collective-permute-done.30.rest_16_), channel_id=1, source_target_pairs={{0,2},{1,3},{2,6},{3,7},{4,0},{5,1},{6,10},{7,11},{8,4},{9,5},{10,... | collective-permute-start | bytes 393224 | tf_op jit(solution)/shard_map/ppermute | solution.py:59
  75.3 5.9 %collective-permute-start.31 = (bf16[128,512]{1,0:T(8,128)(2,1)S(1)}, bf16[128,512]{1,0:T(8,128)(2,1)S(1)}, u32[]{:S(2)}, u32[]{:S(2)}) collective-permute-start(bf16[128,512]{1,0:T(8,128)(2,1)S(1)} %collective-permute-done.30.rest_16_), channel_id=1, source_target_pairs={{0,1},{1,0},{2,3},{3,2},{4,5},{5,4},{6,7},{7,6},{8,9},{9,8},{10,11... | collective-permute-start | bytes 393224 | tf_op jit(solution)/shard_map/ppermute | solution.py:50
  75.5 6.3 %collective-permute-start.32 = (bf16[128,512]{1,0:T(8,128)(2,1)S(1)}, bf16[128,512]{1,0:T(8,128)(2,1)S(1)}, u32[]{:S(2)}, u32[]{:S(2)}) collective-permute-start(bf16[128,512]{1,0:T(8,128)(2,1)S(1)} %collective-permute-done.24.rest_10_), channel_id=1, source_target_pairs={{0,4},{1,5},{2,0},{3,1},{4,8},{5,9},{6,2},{7,3},{8,12},{9,13},{10,... | collective-permute-start | bytes 393224 | tf_op jit(solution)/shard_map/ppermute | solution.py:59
  76.0 5.9 %collective-permute-start.25 = (bf16[128,512]{1,0:T(8,128)(2,1)S(1)}, bf16[128,512]{1,0:T(8,128)(2,1)S(1)}, u32[]{:S(2)}, u32[]{:S(2)}) collective-permute-start(bf16[128,512]{1,0:T(8,128)(2,1)S(1)} %collective-permute-done.24.rest_10_), channel_id=1, source_target_pairs={{0,1},{1,0},{2,3},{3,2},{4,5},{5,4},{6,7},{7,6},{8,9},{9,8},{10,11... | collective-permute-start | bytes 393224 | tf_op jit(solution)/shard_map/ppermute | solution.py:50
  76.0 8.0 %collective-permute-start.36 = (bf16[128,512]{1,0:T(8,128)(2,1)S(1)}, bf16[128,512]{1,0:T(8,128)(2,1)S(1)}, u32[]{:S(2)}, u32[]{:S(2)}) collective-permute-start(bf16[128,512]{1,0:T(8,128)(2,1)S(1)} %collective-permute-done.28.rest_14_), channel_id=1, source_target_pairs={{0,4},{1,5},{2,0},{3,1},{4,8},{5,9},{6,2},{7,3},{8,12},{9,13},{10,... | collective-permute-start | bytes 393224 | tf_op jit(solution)/shard_map/ppermute | solution.py:59
  79.6 5.1 %collective-permute-start.34 = (bf16[128,512]{1,0:T(8,128)(2,1)S(1)}, bf16[128,512]{1,0:T(8,128)(2,1)S(1)}, u32[]{:S(2)}, u32[]{:S(2)}) collective-permute-start(bf16[128,512]{1,0:T(8,128)(2,1)S(1)} %collective-permute-done.26.rest_12_), channel_id=1, source_target_pairs={{0,2},{1,3},{2,6},{3,7},{4,0},{5,1},{6,10},{7,11},{8,4},{9,5},{10,... | collective-permute-start | bytes 393224 | tf_op jit(solution)/shard_map/ppermute | solution.py:59
  81.2 5.1 %collective-permute-start.29 = (bf16[128,512]{1,0:T(8,128)(2,1)S(1)}, bf16[128,512]{1,0:T(8,128)(2,1)S(1)}, u32[]{:S(2)}, u32[]{:S(2)}) collective-permute-start(bf16[128,512]{1,0:T(8,128)(2,1)S(1)} %collective-permute-done.28.rest_14_), channel_id=1, source_target_pairs={{0,1},{1,0},{2,3},{3,2},{4,5},{5,4},{6,7},{7,6},{8,9},{9,8},{10,11... | collective-permute-start | bytes 393224 | tf_op jit(solution)/shard_map/ppermute | solution.py:50
  81.9 5.0 %collective-permute-start.39 = (bf16[128,512]{1,0:T(8,128)(2,1)S(1)}, bf16[128,512]{1,0:T(8,128)(2,1)S(1)}, u32[]{:S(2)}, u32[]{:S(2)}) collective-permute-start(bf16[128,512]{1,0:T(8,128)(2,1)S(1)} %collective-permute-done.38.rest_24_), channel_id=1, source_target_pairs={{0,1},{1,0},{2,3},{3,2},{4,5},{5,4},{6,7},{7,6},{8,9},{9,8},{10,11... | collective-permute-start | bytes 393224 | tf_op jit(solution)/shard_map/ppermute | solution.py:50
  (26 other events, 266.9 us)

commit v4 on v3

--- a/solution.py
+++ b/solution.py
@@ -95,11 +95,14 @@
         )
         for k in range(list_len):
             place, tile = spot(me, b, k)
+            there, its_tile = spot(me ^ 1, b, k)
+            block = step * per_step + b
+            mask = mask_ref[k, me * blk_count + block]
             table_ref[0, place] = tile
-            there, its_tile = spot(me ^ 1, b, k)
             table_ref[1, there] = its_tile
-            mask = mask_ref[k, me * blk_count + step * per_step + b].astype(F32)
-            masked = part[k * tile_rows : (k + 1) * tile_rows] * mask
+            table_ref[2, place] = mask
+            table_ref[3, there] = mask_ref[k, (me ^ 1) * blk_count + block]
+            masked = part[k * tile_rows : (k + 1) * tile_rows] * mask.astype(F32)
             placed[place] = masked.astype(BF16)
 
     @pl.when(step == pl.num_programs(0) - 1)
@@ -158,38 +161,70 @@
     out_b[...] = out[half * tile_rows :]
 
 
-def back_kernel(
-    ring, places, per_step, me_ref, lists_ref, mask_ref, latent_ref, interp_ref, *rest
-):
+def add_kernel(own_right, own_left, right, left, token, out_right, out_left):
+    del token
+    out_right[...] = (own_right[0] + right[...].astype(F32)).astype(BF16)
+    out_left[...] = (own_left[0] + left[...].astype(F32)).astype(BF16)
+
+
+def order_kernel(*refs):
+    del refs
+
+
+def pick_kernel(owners, slots, chips, table_ref, *refs):
+    halves, (mine, theirs) = refs[:-2], refs[-2:]
+    tile_rows = mine.shape[1]
+    count = halves[0].shape[0] // tile_rows
+    for number, owner in enumerate(owners):
+        lower, upper = halves[2 * number : 2 * number + 2]
+        for slot in range(slots):
+            for way, out in enumerate((mine, theirs)):
+                place = (way * chips + owner) * slots + slot
+                tile, mask = table_ref[way, place], table_ref[2 + way, place]
+                above = tile >= count
+                within = jnp.where(above, tile - count, tile)
+                rows = pl.ds(pl.multiple_of(within * tile_rows, tile_rows), tile_rows)
+                value = jnp.where(above, upper[rows], lower[rows]).astype(F32)
+                out[number * slots + slot] = (value * mask.astype(F32)).astype(BF16)
+
+
+def back_kernel(ring, places, slots, per_step, me_ref, lists_ref, latent_ref, weights_ref, *rest):
     count = len(places)
-    pieces, (out_ref, held, picked, sems) = rest[:count], rest[count:]
+    pieces, (out_ref, held, sems) = rest[:count], rest[count:]
     step = pl.program_id(0)
     me = me_ref[0]
-    list_len, tile_rows, block_rows = interp_ref.shape[1:]
+    block_rows, listed = weights_ref.shape[1:]
+    list_len = lists_ref.shape[0]
+    tile_rows, width = held.shape[1:]
 
     @pl.when(step == 0)
     def _():
         copies = []
-        for i, (place, row) in enumerate(places):
-            into = held.at[place, pl.ds(row, pieces[i].shape[0])]
-            copies.append(pltpu.make_async_copy(pieces[i], into, sems.at[i]))
+        for i, (piece, place) in enumerate(zip(pieces, places)):
+            for number, start in enumerate(place):
+                copies.append(
+                    pltpu.make_async_copy(
+                        piece.at[pl.ds(number * slots, slots)],
+                        held.at[pl.ds(start * slots, slots)],
+                        sems.at[len(copies)],
+                    )
+                )
         for copy in copies:
             copy.start()
         for copy in copies:
             copy.wait()
 
     for b in range(per_step):
-        block = (me * pl.num_programs(0) + step) * per_step + b
+        number = step * per_step + b
+        values = []
         for k in range(list_len):
-            ahead, across, tile = ring.entry(lists_ref, me, block, k)
-            rows = pl.ds(pl.multiple_of(tile * tile_rows, tile_rows), tile_rows)
-            mask = mask_ref[k, block].astype(F32)
-            value = held[ahead * N_CORE + across, rows].astype(F32) * mask
-            picked[b, k * tile_rows : (k + 1) * tile_rows] = value.astype(BF16)
-        weights = interp_ref[b].reshape(list_len * tile_rows, block_rows)
-        back = lax.dot_general(
-            weights, picked[b], (((0,), (0,)), ((), ())), preferred_element_type=F32
-        )
+            ahead, across, _ = ring.entry(
+                lists_ref, me, me * pl.num_programs(0) * per_step + number, k
+            )
+            slot = split(number * list_len + k, ring.n_band)[0]
+            values.append(held[(across * ring.chips + ahead) * slots + slot])
+        value = jnp.concatenate(values, axis=0)
+        back = jnp.dot(weights_ref[b], value, preferred_element_type=F32)
         rows = slice(b * block_rows, (b + 1) * block_rows)
         out_ref[rows] = (latent_ref[rows].astype(F32) + back).astype(BF16)
 
@@ -238,6 +273,9 @@
     chips, far = ring.chips, ring.far
     lists = (lax.axis_index("band").reshape(1), tile_list.T, block_mask.T)
 
+    def in_hbm(array):
+        return pltpu.with_memory_space_constraint(array, pltpu.HBM)
+
     gain = embed_gain.reshape(1, width)
     per_step = 2
     rows = per_step * block_rows
@@ -246,7 +284,7 @@
         functools.partial(embed_kernel, ring, per_step, slots),
         out_shape=[shape((blk_count * block_rows, width))]
         + [shape(held_shape)] * N_CORE
-        + [shape((2, entries), jnp.int32)],
+        + [shape((4, entries), jnp.int32)],
         grid_spec=pltpu.PrefetchScalarGridSpec(
             num_scalar_prefetch=3,
             grid=(blk_count // per_step,),
@@ -269,7 +307,7 @@
             interp,
         ),
         name="embed",
-    )(*lists, grid_features.T, embed_in, embed_out, gain, interp)
+    )(*lists, *map(in_hbm, (grid_features.T, embed_in, embed_out, gain, interp)))
     other = ring.over_core(sent)
 
     dense = (tiles, tile_rows, width)
@@ -312,22 +350,40 @@
         name="own_chunks",
     )(table, kept, other)
 
-    def add_own(distance, part, value):
-        mine = own[distance % chips, part]
-        return (mine + value.astype(F32)).astype(BF16)
-
-    lower, upper = slice(0, half_tiles), slice(half_tiles, tiles)
-    right_a, left_b = ring.over(far_right, 1), ring.over(far_left, -1)
-    right_b, left_a = ring.over(next_right, 1), ring.over(next_left, -1)
+    lower, upper = 0, 1
+
+    def half_of(owner, part):
+        return pl.BlockSpec((1,) + half_dense, lambda i: (owner % chips, part, 0, 0))
+
+    def add_own(distance, parts, values, token):
+        sums = pl.pallas_call(
+            add_kernel,
+            out_shape=[shape(half_dense)] * 2,
+            grid=(1,),
+            in_specs=[half_of(distance, parts[0]), half_of(-distance, parts[1])]
+            + [whole(v) for v in values]
+            + [pl.BlockSpec(memory_space=pl.ANY)],
+            out_specs=[pl.BlockSpec(half_dense, lambda i: (0, 0, 0))] * 2,
+            compiler_params=params(8),
+            cost_estimate=cost(0, *values, *values),
+            name=f"add_{distance}{'ab'[parts[0]]}",
+        )(own, own, *values, token)
+        return sums, sums[0]
+
+    def both(values):
+        return [ring.over(values[0], 1), ring.over(values[1], -1)]
+
+    first, second = both((far_right, far_left)), both((next_right, next_left))
+    token = own
     for distance in range(far - 1, 0, -1):
-        right_a = ring.over(add_own(distance, lower, right_a), 1)
-        left_b = ring.over(add_own(-distance, upper, left_b), -1)
+        sums, token = add_own(distance, (lower, upper), first, token)
+        first = both(sums)
         if distance > 1:
-            right_b = ring.over(add_own(distance - 1, upper, right_b), 1)
-            left_a = ring.over(add_own(1 - distance, lower, left_a), -1)
+            sums, token = add_own(distance - 1, (upper, lower), second, token)
+            second = both(sums)
 
     mesh_gain = mesh_gain.reshape(1, width)
-    came = (right_a, left_b, right_b, left_a)
+    came = (*first, *second)
     mesh_out, out_a, out_b = pl.pallas_call(
         mesh_kernel,
         out_shape=[shape((node_rows, width))] + [shape((half_rows, width))] * 2,
@@ -342,50 +398,78 @@
         name="mesh_step",
     )(mesh_latent, mesh_up, mesh_down, mesh_gain, own, *came)
 
+    def in_order(values, token):
+        return pl.pallas_call(
+            order_kernel,
+            out_shape=[shape(v.shape) for v in values],
+            in_specs=[pl.BlockSpec(memory_space=pl.ANY)] * (len(values) + 1),
+            out_specs=[pl.BlockSpec(memory_space=pl.ANY)] * len(values),
+            input_output_aliases={i: i for i in range(len(values))},
+            cost_estimate=cost(0),
+            name="in_order",
+        )(*values, token)
+
     pieces, places = [], []
 
-    def keep(piece, owner, row):
-        for across, value in enumerate((piece, ring.over_core(piece))):
+    def pick(owners, halves):
+        owners = [owner % chips for owner in owners]
+        out = shape((len(owners) * slots, tile_rows, width))
+        mine, theirs = pl.pallas_call(
+            functools.partial(pick_kernel, owners, slots, chips),
+            out_shape=[out] * 2,
+            grid_spec=pltpu.PrefetchScalarGridSpec(
+                num_scalar_prefetch=1,
+                grid=(1,),
+                in_specs=[whole(h) for h in halves],
+                out_specs=[whole(out)] * 2,
+            ),
+            compiler_params=params(8),
+            cost_estimate=cost(0, *halves),
+            name=f"pick_{owners[0]}",
+        )(table, *halves)
+        for across, value in enumerate((mine, ring.over_core(theirs))):
             pieces.append(value)
-            places.append((owner % chips * N_CORE + across, row))
-
-    right_a, left_b, right_b, left_a = out_a, out_b, out_b, out_a
-    keep(mesh_out, 0, 0)
-    for distance in range(1, far + 1):
-        right_a, left_b = ring.over(right_a, 1), ring.over(left_b, -1)
-        keep(right_a, -distance, 0)
-        keep(left_b, distance, half_rows)
-        if distance < far:
-            right_b, left_a = ring.over(right_b, 1), ring.over(left_a, -1)
-            keep(right_b, -distance, half_rows)
-            keep(left_a, distance, 0)
-
-    per_step = 2
+            places.append([across * chips + owner for owner in owners])
+        return mine
+
+    first, second = both((out_a, out_b)), both((out_b, out_a))
+    token = pick([0], (out_a, out_b))
+    for distance in range(1, far):
+        first = in_order(first, token)
+        onward = both(first)
+        second = in_order(second, first[0])
+        if distance < far - 1:
+            after = both(second)
+        token = pick([-distance, distance], (first[0], second[0], second[1], first[1]))
+        first, second = onward, after
+    pick([far], first)
+
+    weights = jnp.swapaxes(interp.reshape(blk_count, list_len * tile_rows, block_rows), 1, 2)
+    per_step = 4
     rows = per_step * block_rows
     grid_out = pl.pallas_call(
-        functools.partial(back_kernel, ring, places, per_step),
+        functools.partial(back_kernel, ring, places, slots, per_step),
         out_shape=shape((blk_count * block_rows, width)),
         grid_spec=pltpu.PrefetchScalarGridSpec(
-            num_scalar_prefetch=3,
+            num_scalar_prefetch=2,
             grid=(blk_count // per_step,),
             in_specs=[
                 pl.BlockSpec((rows, width), lambda i, *_: (i, 0)),
-                pl.BlockSpec((per_step,) + interp.shape[1:], lambda i, *_: (i, 0, 0, 0)),
+                pl.BlockSpec((per_step,) + weights.shape[1:], lambda i, *_: (i, 0, 0)),
             ]
             + [pl.BlockSpec(memory_space=pl.ANY)] * len(pieces),
             out_specs=pl.BlockSpec((rows, width), lambda i, *_: (i, 0)),
             scratch_shapes=[
-                pltpu.VMEM((n_band, node_rows, width), BF16),
-                pltpu.VMEM((per_step, list_len * tile_rows, width), BF16),
-                pltpu.SemaphoreType.DMA((len(pieces),)),
+                pltpu.VMEM((entries, tile_rows, width), BF16),
+                pltpu.SemaphoreType.DMA((n_band,)),
             ],
         ),
-        compiler_params=params(16 if n_band <= 16 else 32),
+        compiler_params=params(20),
         cost_estimate=cost(
             2 * blk_count * block_rows * width * list_len * tile_rows, latent, latent, interp
         ),
         name="back",
-    )(*lists, latent, interp, *pieces)
+    )(*lists[:2], latent, weights, *pieces)
     return (grid_out, mesh_out)
 
 

time: 104 us -> 101 us (0.971)
  waiting for transfers between devices: 35.2 us -> 17 us
  local copies, waits for them, and re-layouts: 7.76 us -> 24.2 us
  starting transfers between devices: 34.1 us -> 31.2 us
  Pallas kernels: 24.9 us -> 27 us
    ppermute x28, waiting for transfers between devices: 31.6 us -> 14.7 us  [over(): return lax.ppermute(value, 'band', pairs)]
    unnamed x28 -> x78, local copies, waits for them, and re-layouts: 7.76 us -> 22.6 us
    ppermute x28, starting transfers between devices: 32.2 us -> 29.7 us  [over(): return lax.ppermute(value, 'band', pairs)]
    reshape x0 -> x1, local copies, waits for them, and re-layouts: none -> 1.61 us  [on_device(): interp.reshape(blk_count, list_len * tile_rows, block_rows)]
    ppermute x16 -> x6, waiting for transfers between devices: 3.65 us -> 2.3 us  [over_core(): return lax.ppermute(value, 'band', [(i, i ^ 1) for i in range(self.n_band)])]
    pallas_call x1, Pallas kernels: 10.1 us -> 11.3 us  [on_device(): pl.pallas_call(functools.partial(embed_kernel, ring, per_step, slots), ou...]
    pallas_call x1 -> x17, Pallas kernels: 11.2 us -> 12.1 us  [the longest x1 7.34 us: on_device(): pl.pallas_call(functools.partial(back_kernel, ring, places, slots, per_st...]
  transfers between devices with their start and end apart: 44 -> 34, of which waited for: 25 -> 15; matrix products, arithmetic and copies ran while one was open for 0% -> 2% of each run, Pallas kernels for 1% -> 6%
where the time goes in v4:
time: 101 us; the launch traced here: 100 us
  starting transfers between devices  31.2 us (31%)
  Pallas kernels  27 us (27%)
  local copies, waits for them, and re-layouts  24.2 us (24%)
  waiting for transfers between devices  17 us (17%)
    ppermute x28, starting transfers between devices, over(): return lax.ppermute(value, 'band', pairs)  29.7 us
    unnamed x78, local copies, waits for them, and re-layouts  22.6 us
    ppermute x28, waiting for transfers between devices, over(): return lax.ppermute(value, 'band', pairs)  14.7 us
    pallas_call x1, Pallas kernels, on_device(): pl.pallas_call(functools.partial(embed_kernel, ring, per_step, slots), ou...  11.3 us
    pallas_call x1, Pallas kernels, on_device(): pl.pallas_call(functools.partial(back_kernel, ring, places, slots, per_st...  7.34 us
    pallas_call x5, Pallas kernels, pick(): pl.pallas_call(functools.partial(pick_kernel, owners, slots, chips), out_...  4.57 us
    ppermute x6, waiting for transfers between devices, over_core(): return lax.ppermute(value, 'band', [(i, i ^ 1) for i in range(self.n_band)])  2.3 us
  transfers between devices with their start and end apart: 34, of which 15 were waited for; matrix products, arithmetic and copies ran while one was open for 2% of the time, Pallas kernels for 6%

profile of v4, /device:TPU:0, one launch (start us, length us, event | category | flops | bytes accessed | tf_op | source)
XLA Modules:
  0.0 100.3 jit_solution(72129484622178648)
XLA Ops:
  2.0 11.3 %embed.1 = (bf16[4096,512]{1,0:T(8,128)(2,1)S(1)}, bf16[32,32,512]{2,1,0:T(8,128)(2,1)S(1)}, bf16[32,32,512]{2,1,0:T(8,128)(2,1)S(1)}, s32[4,64]{1,0:T(4,128)S(1)}) custom-call(s32[1]{0:T(128)} %bitcast.me_ref, s32[4,256]{1,0:T(4,128)S(1)} %bitcast.9, s32[4,256]{1,0:T(4,128)S(1)} %bitcast.12, bf16[227,4096]{1,0:T(8,128)(2,1)} %bitcast.14, ...), custom_call_target="tpu_custom_call" | custom-call | flops 3636461568 | bytes 2908160 | tf_op jit(solution)/shard_map/embed/pallas_call | solution.py:283
  13.8 2.3 %collective-permute-done.other.refs_3_.refs_4_.refs_5_ = bf16[32,32,512]{2,1,0:T(8,128)(2,1)S(1)} collective-permute-done((bf16[32,32,512]{2,1,0:T(8,128)(2,1)S(1)}, bf16[32,32,512]{2,1,0:T(8,128)(2,1)S(1)}, u32[]{:S(2)}, u32[]{:S(2)}) %collective-permute-start) | collective-permute-done | bytes 1048608 | tf_op jit(solution)/shard_map/ppermute | solution.py:50
  17.0 3.0 %collective-permute-start.1 = (bf16[4,32,512]{2,1,0:T(8,128)(2,1)S(1)}, bf16[4,32,512]{2,1,0:T(8,128)(2,1)S(1)}, u32[]{:S(2)}, u32[]{:S(2)}) collective-permute-start(bf16[4,32,512]{2,1,0:T(8,128)(2,1)S(1)} %get-tuple-element.49), channel_id=1, source_target_pairs={{0,4},{1,5},{2,0},{3,1},{4,8},{5,9},{6,2},{7,3},{8,12},{9,13},{10,... | collective-permute-start | bytes 393224 | tf_op jit(solution)/shard_map/ppermute | solution.py:59
  20.0 2.0 %collective-permute-start.5 = (bf16[4,32,512]{2,1,0:T(8,128)(2,1)S(1)}, bf16[4,32,512]{2,1,0:T(8,128)(2,1)S(1)}, u32[]{:S(2)}, u32[]{:S(2)}) collective-permute-start(bf16[4,32,512]{2,1,0:T(8,128)(2,1)S(1)} %get-tuple-element.53), channel_id=1, source_target_pairs={{0,4},{1,5},{2,0},{3,1},{4,8},{5,9},{6,2},{7,3},{8,12},{9,13},{10,... | collective-permute-start | bytes 393224 | tf_op jit(solution)/shard_map/ppermute | solution.py:59
  22.0 1.3 %own_chunks.1.own_right.own_left.token.own = f32[8,8,32,512]{3,2,1,0:T(8,128)S(1)} custom-call(s32[4,64]{1,0:T(4,128)S(1)} %get-tuple-element.46.table_ref, bf16[32,32,512]{2,1,0:T(8,128)(2,1)S(1)} %get-tuple-element.47.kept.refs_0_.refs_1_.refs_2_, bf16[32,32,512]{2,1,0:T(8,128)(2,1)S(1)} %collective-permute-done.other.refs_3_.refs_4_.refs_5_), custom_call_target="tpu_custom_call" | custom-call | bytes 4194304 | tf_op jit(solution)/shard_map/own_chunks/pallas_call | solution.py:339
  24.2 2.1 %collective-permute-done.2.left = bf16[4,32,512]{2,1,0:T(8,128)(2,1)S(1)} collective-permute-done((bf16[4,32,512]{2,1,0:T(8,128)(2,1)S(1)}, bf16[4,32,512]{2,1,0:T(8,128)(2,1)S(1)}, u32[]{:S(2)}, u32[]{:S(2)}) %collective-permute-start.2) | collective-permute-done | bytes 131104 | tf_op jit(solution)/shard_map/ppermute | solution.py:59
  26.4 1.6 %collective-permute-start.3 = (bf16[4,32,512]{2,1,0:T(8,128)(2,1)S(1)}, bf16[4,32,512]{2,1,0:T(8,128)(2,1)S(1)}, u32[]{:S(2)}, u32[]{:S(2)}) collective-permute-start(bf16[4,32,512]{2,1,0:T(8,128)(2,1)S(1)} %get-tuple-element.51.token), channel_id=1, source_target_pairs={{0,4},{1,5},{2,0},{3,1},{4,8},{5,9},{6,2},{7,3},{8,12},{9,13},{10,... | collective-permute-start | bytes 393224 | tf_op jit(solution)/shard_map/ppermute | solution.py:59
  29.1 1.6 %collective-permute-start.9 = (bf16[4,32,512]{2,1,0:T(8,128)(2,1)S(1)}, bf16[4,32,512]{2,1,0:T(8,128)(2,1)S(1)}, u32[]{:S(2)}, u32[]{:S(2)}) collective-permute-start(bf16[4,32,512]{2,1,0:T(8,128)(2,1)S(1)} %get-tuple-element.55.token), channel_id=1, source_target_pairs={{0,4},{1,5},{2,0},{3,1},{4,8},{5,9},{6,2},{7,3},{8,12},{9,13},{10,... | collective-permute-start | bytes 393224 | tf_op jit(solution)/shard_map/ppermute | solution.py:59
  30.6 2.2 %collective-permute-done.3.right = bf16[4,32,512]{2,1,0:T(8,128)(2,1)S(1)} collective-permute-done((bf16[4,32,512]{2,1,0:T(8,128)(2,1)S(1)}, bf16[4,32,512]{2,1,0:T(8,128)(2,1)S(1)}, u32[]{:S(2)}, u32[]{:S(2)}) %collective-permute-start.3) | collective-permute-done | bytes 131104 | tf_op jit(solution)/shard_map/ppermute | solution.py:59
  33.1 1.6 %collective-permute-start.7 = (bf16[4,32,512]{2,1,0:T(8,128)(2,1)S(1)}, bf16[4,32,512]{2,1,0:T(8,128)(2,1)S(1)}, u32[]{:S(2)}, u32[]{:S(2)}) collective-permute-start(bf16[4,32,512]{2,1,0:T(8,128)(2,1)S(1)} %get-tuple-element.56.token), channel_id=1, source_target_pairs={{0,4},{1,5},{2,0},{3,1},{4,8},{5,9},{6,2},{7,3},{8,12},{9,13},{10,... | collective-permute-start | bytes 393224 | tf_op jit(solution)/shard_map/ppermute | solution.py:59
  35.7 1.6 %collective-permute-start.13 = (bf16[4,32,512]{2,1,0:T(8,128)(2,1)S(1)}, bf16[4,32,512]{2,1,0:T(8,128)(2,1)S(1)}, u32[]{:S(2)}, u32[]{:S(2)}) collective-permute-start(bf16[4,32,512]{2,1,0:T(8,128)(2,1)S(1)} %get-tuple-element.59.token), channel_id=1, source_target_pairs={{0,4},{1,5},{2,0},{3,1},{4,8},{5,9},{6,2},{7,3},{8,12},{9,13},{10,... | collective-permute-start | bytes 393224 | tf_op jit(solution)/shard_map/ppermute | solution.py:59
  38.5 1.2 %collective-permute-done.8.left = bf16[4,32,512]{2,1,0:T(8,128)(2,1)S(1)} collective-permute-done((bf16[4,32,512]{2,1,0:T(8,128)(2,1)S(1)}, bf16[4,32,512]{2,1,0:T(8,128)(2,1)S(1)}, u32[]{:S(2)}, u32[]{:S(2)}) %collective-permute-start.8) | collective-permute-done | bytes 131104 | tf_op jit(solution)/shard_map/ppermute | solution.py:59
  39.7 1.6 %collective-permute-start.11 = (bf16[4,32,512]{2,1,0:T(8,128)(2,1)S(1)}, bf16[4,32,512]{2,1,0:T(8,128)(2,1)S(1)}, u32[]{:S(2)}, u32[]{:S(2)}) collective-permute-start(bf16[4,32,512]{2,1,0:T(8,128)(2,1)S(1)} %get-tuple-element.60), channel_id=1, source_target_pairs={{0,4},{1,5},{2,0},{3,1},{4,8},{5,9},{6,2},{7,3},{8,12},{9,13},{10,... | collective-permute-start | bytes 393224 | tf_op jit(solution)/shard_map/ppermute | solution.py:59
  42.5 2.2 %collective-permute-done.11.right_a = bf16[4,32,512]{2,1,0:T(8,128)(2,1)S(1)} collective-permute-done((bf16[4,32,512]{2,1,0:T(8,128)(2,1)S(1)}, bf16[4,32,512]{2,1,0:T(8,128)(2,1)S(1)}, u32[]{:S(2)}, u32[]{:S(2)}) %collective-permute-start.11) | collective-permute-done | bytes 131104 | tf_op jit(solution)/shard_map/ppermute | solution.py:59
  44.8 1.5 %collective-permute-done.12.left_b = bf16[4,32,512]{2,1,0:T(8,128)(2,1)S(1)} collective-permute-done((bf16[4,32,512]{2,1,0:T(8,128)(2,1)S(1)}, bf16[4,32,512]{2,1,0:T(8,128)(2,1)S(1)}, u32[]{:S(2)}, u32[]{:S(2)}) %collective-permute-start.12) | collective-permute-done | bytes 131104 | tf_op jit(solution)/shard_map/ppermute | solution.py:59
  46.3 1.5 %mesh_step.1 = (bf16[256,512]{1,0:T(8,128)(2,1)}, bf16[128,512]{1,0:T(8,128)(2,1)S(1)}, bf16[128,512]{1,0:T(8,128)(2,1)S(1)}) custom-call(bf16[256,512]{1,0:T(8,128)(2,1)S(1)} %copy-done.34, bf16[512,512]{1,0:T(8,128)(2,1)S(1)} %copy-done.32, bf16[512,512]{1,0:T(8,128)(2,1)S(1)} %copy-done.33, f32[1,512]{1,0:T(1,128)S(1)} %bitcast.11, ...), custom_call_target="tpu_custom_call" | custom-call | flops 268435456 | bytes 1048576 | tf_op jit(solution)/shard_map/mesh_step/pallas_call | solution.py:387
  47.7 1.6 %collective-permute-start.16 = (bf16[128,512]{1,0:T(8,128)(2,1)S(1)}, bf16[128,512]{1,0:T(8,128)(2,1)S(1)}, u32[]{:S(2)}, u32[]{:S(2)}) collective-permute-start(bf16[128,512]{1,0:T(8,128)(2,1)S(1)} %get-tuple-element.63.refs_0_), channel_id=1, source_target_pairs={{0,4},{1,5},{2,0},{3,1},{4,8},{5,9},{6,2},{7,3},{8,12},{9,13},{10,... | collective-permute-start | bytes 393224 | tf_op jit(solution)/shard_map/ppermute | solution.py:59
  49.8 1.6 %collective-permute-start.18 = (bf16[128,512]{1,0:T(8,128)(2,1)S(1)}, bf16[128,512]{1,0:T(8,128)(2,1)S(1)}, u32[]{:S(2)}, u32[]{:S(2)}) collective-permute-start(bf16[128,512]{1,0:T(8,128)(2,1)S(1)} %get-tuple-element.64.refs_1_), channel_id=1, source_target_pairs={{0,4},{1,5},{2,0},{3,1},{4,8},{5,9},{6,2},{7,3},{8,12},{9,13},{10,... | collective-permute-start | bytes 393224 | tf_op jit(solution)/shard_map/ppermute | solution.py:59
  54.0 1.5 %collective-permute-done.17.refs_1_ = bf16[128,512]{1,0:T(8,128)(2,1)S(1)} collective-permute-done((bf16[128,512]{1,0:T(8,128)(2,1)S(1)}, bf16[128,512]{1,0:T(8,128)(2,1)S(1)}, u32[]{:S(2)}, u32[]{:S(2)}) %collective-permute-start.17) | collective-permute-done | bytes 131104 | tf_op jit(solution)/shard_map/ppermute | solution.py:59
  56.8 1.3 %collective-permute-start.22 = (bf16[128,512]{1,0:T(8,128)(2,1)}, bf16[128,512]{1,0:T(8,128)(2,1)S(1)}, u32[]{:S(2)}, u32[]{:S(2)}) collective-permute-start(bf16[128,512]{1,0:T(8,128)(2,1)} %get-tuple-element.70.refs_3_), channel_id=1, source_target_pairs={{0,2},{1,3},{2,6},{3,7},{4,0},{5,1},{6,10},{7,11},{8,4},{9,5},{10,... | collective-permute-start | bytes 393224 | tf_op jit(solution)/shard_map/ppermute | solution.py:59
  60.2 1.3 %collective-permute-start.24 = (bf16[128,512]{1,0:T(8,128)(2,1)}, bf16[128,512]{1,0:T(8,128)(2,1)S(1)}, u32[]{:S(2)}, u32[]{:S(2)}) collective-permute-start(bf16[128,512]{1,0:T(8,128)(2,1)} %get-tuple-element.69.refs_2_), channel_id=1, source_target_pairs={{0,2},{1,3},{2,6},{3,7},{4,0},{5,1},{6,10},{7,11},{8,4},{9,5},{10,... | collective-permute-start | bytes 393224 | tf_op jit(solution)/shard_map/ppermute | solution.py:59
  61.5 0.9 copy-done.3
  67.9 1.3 %collective-permute-start.27 = (bf16[128,512]{1,0:T(8,128)(2,1)}, bf16[128,512]{1,0:T(8,128)(2,1)S(1)}, u32[]{:S(2)}, u32[]{:S(2)}) collective-permute-start(bf16[128,512]{1,0:T(8,128)(2,1)} %get-tuple-element.76.refs_3_), channel_id=1, source_target_pairs={{0,2},{1,3},{2,6},{3,7},{4,0},{5,1},{6,10},{7,11},{8,4},{9,5},{10,... | collective-permute-start | bytes 393224 | tf_op jit(solution)/shard_map/ppermute | solution.py:59
  71.3 1.3 %collective-permute-start.29 = (bf16[128,512]{1,0:T(8,128)(2,1)}, bf16[128,512]{1,0:T(8,128)(2,1)S(1)}, u32[]{:S(2)}, u32[]{:S(2)}) collective-permute-start(bf16[128,512]{1,0:T(8,128)(2,1)} %get-tuple-element.75.refs_2_), channel_id=1, source_target_pairs={{0,2},{1,3},{2,6},{3,7},{4,0},{5,1},{6,10},{7,11},{8,4},{9,5},{10,... | collective-permute-start | bytes 393224 | tf_op jit(solution)/shard_map/ppermute | solution.py:59
  72.5 0.9 copy-done.7
  79.5 1.3 %collective-permute-start.32 = (bf16[128,512]{1,0:T(8,128)(2,1)}, bf16[128,512]{1,0:T(8,128)(2,1)S(1)}, u32[]{:S(2)}, u32[]{:S(2)}) collective-permute-start(bf16[128,512]{1,0:T(8,128)(2,1)} %get-tuple-element.82.refs_3_), channel_id=1, source_target_pairs={{0,2},{1,3},{2,6},{3,7},{4,0},{5,1},{6,10},{7,11},{8,4},{9,5},{10,... | collective-permute-start | bytes 393224 | tf_op jit(solution)/shard_map/ppermute | solution.py:59
  85.0 1.3 %pick_5.1 = (bf16[8,32,512]{2,1,0:T(8,128)(2,1)S(1)}, bf16[8,32,512]{2,1,0:T(8,128)(2,1)}) custom-call(s32[4,64]{1,0:T(4,128)S(1)} %get-tuple-element.46.table_ref, bf16[128,512]{1,0:T(8,128)(2,1)S(1)} %copy-done.5, bf16[128,512]{1,0:T(8,128)(2,1)S(1)} %copy-done.15, bf16[128,512]{1,0:T(8,128)(2,1)S(1)} %copy-done.17, bf16[128,512]{1,0:T(8,128)(2,1)S(1)} %copy-done.29), custom_call_target="tpu_custom_call" | custom-call | bytes 524288 | tf_op jit(solution)/shard_map/pick_5/pallas_call | solution.py:417
  86.9 1.3 %pick_4.1 = (bf16[4,32,512]{2,1,0:T(8,128)(2,1)S(1)}, bf16[4,32,512]{2,1,0:T(8,128)(2,1)}) custom-call(s32[4,64]{1,0:T(4,128)S(1)} %get-tuple-element.46.table_ref, bf16[128,512]{1,0:T(8,128)(2,1)S(1)} %collective-permute-done.31.refs_0_, bf16[128,512]{1,0:T(8,128)(2,1)S(1)} %collective-permute-done.32.refs_1_), custom_call_target="tpu_custom_call" | custom-call | bytes 262144 | tf_op jit(solution)/shard_map/pick_4/pallas_call | solution.py:417
  88.1 1.6 %copy.26 = bf16[16,128,256]{1,2,0:T(8,128)(2,1)S(1)} copy(bf16[16,128,256]{2,1,0:T(8,128)(2,1)} %bitcast.13) | data formatting | bytes 2097152 | tf_op jit(solution)/shard_map/reshape | solution.py:447
  89.8 2.2 %copy-done.1 = bf16[4096,512]{1,0:T(8,128)(2,1)S(1)} copy-done((bf16[4096,512]{1,0:T(8,128)(2,1)S(1)}, bf16[4096,512]{1,0:T(8,128)(2,1)}, u32[]{:S(2)}) %copy-start.1) | copy-done | bytes 4194328
  92.0 0.9 copy-done.11
  93.0 7.3 %back.1 = bf16[4096,512]{1,0:T(8,128)(2,1)} custom-call(s32[1]{0:T(128)} %bitcast.me_ref, s32[4,256]{1,0:T(4,128)S(1)} %bitcast.10, bf16[4096,512]{1,0:T(8,128)(2,1)S(1)} %copy-done.1, bf16[16,256,128]{2,1,0:T(8,128)(2,1)S(1)} %bitcast.8, bf16[4,32,512]{2,1,0:T(8,128)(2,1)S(1)} %copy-done.13, bf16[4,32,512]{2,1,0:T(8,128)(2,1)S(1)} %collective-permute-done.15.rest_1_, ...), custom_call_target="tpu_custom_call" | custom-call | flops 536870912 | bytes 9437184 | tf_op jit(solution)/shard_map/back/pallas_call | solution.py:450
  (136 shorter events, 33.3 us)
Async XLA Ops:
  17.0 7.2 %collective-permute-start.1 = (bf16[4,32,512]{2,1,0:T(8,128)(2,1)S(1)}, bf16[4,32,512]{2,1,0:T(8,128)(2,1)S(1)}, u32[]{:S(2)}, u32[]{:S(2)}) collective-permute-start(bf16[4,32,512]{2,1,0:T(8,128)(2,1)S(1)} %get-tuple-element.49), channel_id=1, source_target_pairs={{0,4},{1,5},{2,0},{3,1},{4,8},{5,9},{6,2},{7,3},{8,12},{9,13},{10,... | collective-permute-start | bytes 393224 | tf_op jit(solution)/shard_map/ppermute | solution.py:59
  20.0 6.4 %collective-permute-start.2 = (bf16[4,32,512]{2,1,0:T(8,128)(2,1)S(1)}, bf16[4,32,512]{2,1,0:T(8,128)(2,1)S(1)}, u32[]{:S(2)}, u32[]{:S(2)}) collective-permute-start(bf16[4,32,512]{2,1,0:T(8,128)(2,1)S(1)} %get-tuple-element.50), channel_id=1, source_target_pairs={{0,2},{1,3},{2,6},{3,7},{4,0},{5,1},{6,10},{7,11},{8,4},{9,5},{10,... | collective-permute-start | bytes 393224 | tf_op jit(solution)/shard_map/ppermute | solution.py:59
  20.0 8.5 %collective-permute-start.5 = (bf16[4,32,512]{2,1,0:T(8,128)(2,1)S(1)}, bf16[4,32,512]{2,1,0:T(8,128)(2,1)S(1)}, u32[]{:S(2)}, u32[]{:S(2)}) collective-permute-start(bf16[4,32,512]{2,1,0:T(8,128)(2,1)S(1)} %get-tuple-element.53), channel_id=1, source_target_pairs={{0,4},{1,5},{2,0},{3,1},{4,8},{5,9},{6,2},{7,3},{8,12},{9,13},{10,... | collective-permute-start | bytes 393224 | tf_op jit(solution)/shard_map/ppermute | solution.py:59
  22.0 6.5 %collective-permute-start.6 = (bf16[4,32,512]{2,1,0:T(8,128)(2,1)S(1)}, bf16[4,32,512]{2,1,0:T(8,128)(2,1)S(1)}, u32[]{:S(2)}, u32[]{:S(2)}) collective-permute-start(bf16[4,32,512]{2,1,0:T(8,128)(2,1)S(1)} %get-tuple-element.54), channel_id=1, source_target_pairs={{0,2},{1,3},{2,6},{3,7},{4,0},{5,1},{6,10},{7,11},{8,4},{9,5},{10,... | collective-permute-start | bytes 393224 | tf_op jit(solution)/shard_map/ppermute | solution.py:59
  26.4 6.4 %collective-permute-start.3 = (bf16[4,32,512]{2,1,0:T(8,128)(2,1)S(1)}, bf16[4,32,512]{2,1,0:T(8,128)(2,1)S(1)}, u32[]{:S(2)}, u32[]{:S(2)}) collective-permute-start(bf16[4,32,512]{2,1,0:T(8,128)(2,1)S(1)} %get-tuple-element.51.token), channel_id=1, source_target_pairs={{0,4},{1,5},{2,0},{3,1},{4,8},{5,9},{6,2},{7,3},{8,12},{9,13},{10,... | collective-permute-start | bytes 393224 | tf_op jit(solution)/shard_map/ppermute | solution.py:59
  28.1 5.0 %collective-permute-start.4 = (bf16[4,32,512]{2,1,0:T(8,128)(2,1)S(1)}, bf16[4,32,512]{2,1,0:T(8,128)(2,1)S(1)}, u32[]{:S(2)}, u32[]{:S(2)}) collective-permute-start(bf16[4,32,512]{2,1,0:T(8,128)(2,1)S(1)} %get-tuple-element.52), channel_id=1, source_target_pairs={{0,2},{1,3},{2,6},{3,7},{4,0},{5,1},{6,10},{7,11},{8,4},{9,5},{10,... | collective-permute-start | bytes 393224 | tf_op jit(solution)/shard_map/ppermute | solution.py:59
  28.6 6.8 %collective-permute-start.10 = (bf16[4,32,512]{2,1,0:T(8,128)(2,1)S(1)}, bf16[4,32,512]{2,1,0:T(8,128)(2,1)S(1)}, u32[]{:S(2)}, u32[]{:S(2)}) collective-permute-start(bf16[4,32,512]{2,1,0:T(8,128)(2,1)S(1)} %get-tuple-element.58), channel_id=1, source_target_pairs={{0,2},{1,3},{2,6},{3,7},{4,0},{5,1},{6,10},{7,11},{8,4},{9,5},{10,... | collective-permute-start | bytes 393224 | tf_op jit(solution)/shard_map/ppermute | solution.py:59
  29.1 6.5 %collective-permute-start.9 = (bf16[4,32,512]{2,1,0:T(8,128)(2,1)S(1)}, bf16[4,32,512]{2,1,0:T(8,128)(2,1)S(1)}, u32[]{:S(2)}, u32[]{:S(2)}) collective-permute-start(bf16[4,32,512]{2,1,0:T(8,128)(2,1)S(1)} %get-tuple-element.55.token), channel_id=1, source_target_pairs={{0,4},{1,5},{2,0},{3,1},{4,8},{5,9},{6,2},{7,3},{8,12},{9,13},{10,... | collective-permute-start | bytes 393224 | tf_op jit(solution)/shard_map/ppermute | solution.py:59
  33.1 5.4 %collective-permute-start.7 = (bf16[4,32,512]{2,1,0:T(8,128)(2,1)S(1)}, bf16[4,32,512]{2,1,0:T(8,128)(2,1)S(1)}, u32[]{:S(2)}, u32[]{:S(2)}) collective-permute-start(bf16[4,32,512]{2,1,0:T(8,128)(2,1)S(1)} %get-tuple-element.56.token), channel_id=1, source_target_pairs={{0,4},{1,5},{2,0},{3,1},{4,8},{5,9},{6,2},{7,3},{8,12},{9,13},{10,... | collective-permute-start | bytes 393224 | tf_op jit(solution)/shard_map/ppermute | solution.py:59
  34.7 5.0 %collective-permute-start.8 = (bf16[4,32,512]{2,1,0:T(8,128)(2,1)S(1)}, bf16[4,32,512]{2,1,0:T(8,128)(2,1)S(1)}, u32[]{:S(2)}, u32[]{:S(2)}) collective-permute-start(bf16[4,32,512]{2,1,0:T(8,128)(2,1)S(1)} %get-tuple-element.57), channel_id=1, source_target_pairs={{0,2},{1,3},{2,6},{3,7},{4,0},{5,1},{6,10},{7,11},{8,4},{9,5},{10,... | collective-permute-start | bytes 393224 | tf_op jit(solution)/shard_map/ppermute | solution.py:59
  35.7 6.2 %collective-permute-start.13 = (bf16[4,32,512]{2,1,0:T(8,128)(2,1)S(1)}, bf16[4,32,512]{2,1,0:T(8,128)(2,1)S(1)}, u32[]{:S(2)}, u32[]{:S(2)}) collective-permute-start(bf16[4,32,512]{2,1,0:T(8,128)(2,1)S(1)} %get-tuple-element.59.token), channel_id=1, source_target_pairs={{0,4},{1,5},{2,0},{3,1},{4,8},{5,9},{6,2},{7,3},{8,12},{9,13},{10,... | collective-permute-start | bytes 393224 | tf_op jit(solution)/shard_map/ppermute | solution.py:59
  37.3 5.2 %collective-permute-start.14 = (bf16[4,32,512]{2,1,0:T(8,128)(2,1)S(1)}, bf16[4,32,512]{2,1,0:T(8,128)(2,1)S(1)}, u32[]{:S(2)}, u32[]{:S(2)}) collective-permute-start(bf16[4,32,512]{2,1,0:T(8,128)(2,1)S(1)} %get-tuple-element.62), channel_id=1, source_target_pairs={{0,2},{1,3},{2,6},{3,7},{4,0},{5,1},{6,10},{7,11},{8,4},{9,5},{10,... | collective-permute-start | bytes 393224 | tf_op jit(solution)/shard_map/ppermute | solution.py:59
  39.7 5.0 %collective-permute-start.11 = (bf16[4,32,512]{2,1,0:T(8,128)(2,1)S(1)}, bf16[4,32,512]{2,1,0:T(8,128)(2,1)S(1)}, u32[]{:S(2)}, u32[]{:S(2)}) collective-permute-start(bf16[4,32,512]{2,1,0:T(8,128)(2,1)S(1)} %get-tuple-element.60), channel_id=1, source_target_pairs={{0,4},{1,5},{2,0},{3,1},{4,8},{5,9},{6,2},{7,3},{8,12},{9,13},{10,... | collective-permute-start | bytes 393224 | tf_op jit(solution)/shard_map/ppermute | solution.py:59
  41.3 5.0 %collective-permute-start.12 = (bf16[4,32,512]{2,1,0:T(8,128)(2,1)S(1)}, bf16[4,32,512]{2,1,0:T(8,128)(2,1)S(1)}, u32[]{:S(2)}, u32[]{:S(2)}) collective-permute-start(bf16[4,32,512]{2,1,0:T(8,128)(2,1)S(1)} %get-tuple-element.61), channel_id=1, source_target_pairs={{0,2},{1,3},{2,6},{3,7},{4,0},{5,1},{6,10},{7,11},{8,4},{9,5},{10,... | collective-permute-start | bytes 393224 | tf_op jit(solution)/shard_map/ppermute | solution.py:59
  47.7 6.2 %collective-permute-start.16 = (bf16[128,512]{1,0:T(8,128)(2,1)S(1)}, bf16[128,512]{1,0:T(8,128)(2,1)S(1)}, u32[]{:S(2)}, u32[]{:S(2)}) collective-permute-start(bf16[128,512]{1,0:T(8,128)(2,1)S(1)} %get-tuple-element.63.refs_0_), channel_id=1, source_target_pairs={{0,4},{1,5},{2,0},{3,1},{4,8},{5,9},{6,2},{7,3},{8,12},{9,13},{10,... | collective-permute-start | bytes 393224 | tf_op jit(solution)/shard_map/ppermute | solution.py:59
  49.3 6.1 %collective-permute-start.17 = (bf16[128,512]{1,0:T(8,128)(2,1)S(1)}, bf16[128,512]{1,0:T(8,128)(2,1)S(1)}, u32[]{:S(2)}, u32[]{:S(2)}) collective-permute-start(bf16[128,512]{1,0:T(8,128)(2,1)S(1)} %get-tuple-element.64.refs_1_), channel_id=1, source_target_pairs={{0,2},{1,3},{2,6},{3,7},{4,0},{5,1},{6,10},{7,11},{8,4},{9,5},{10,... | collective-permute-start | bytes 393224 | tf_op jit(solution)/shard_map/ppermute | solution.py:59
  49.8 8.3 %collective-permute-start.18 = (bf16[128,512]{1,0:T(8,128)(2,1)S(1)}, bf16[128,512]{1,0:T(8,128)(2,1)S(1)}, u32[]{:S(2)}, u32[]{:S(2)}) collective-permute-start(bf16[128,512]{1,0:T(8,128)(2,1)S(1)} %get-tuple-element.64.refs_1_), channel_id=1, source_target_pairs={{0,4},{1,5},{2,0},{3,1},{4,8},{5,9},{6,2},{7,3},{8,12},{9,13},{10,... | collective-permute-start | bytes 393224 | tf_op jit(solution)/shard_map/ppermute | solution.py:59
  51.4 6.8 %collective-permute-start.19 = (bf16[128,512]{1,0:T(8,128)(2,1)S(1)}, bf16[128,512]{1,0:T(8,128)(2,1)S(1)}, u32[]{:S(2)}, u32[]{:S(2)}) collective-permute-start(bf16[128,512]{1,0:T(8,128)(2,1)S(1)} %get-tuple-element.63.refs_0_), channel_id=1, source_target_pairs={{0,2},{1,3},{2,6},{3,7},{4,0},{5,1},{6,10},{7,11},{8,4},{9,5},{10,... | collective-permute-start | bytes 393224 | tf_op jit(solution)/shard_map/ppermute | solution.py:59
  56.1 10.4 %collective-permute-start.21 = (bf16[128,512]{1,0:T(8,128)(2,1)}, bf16[128,512]{1,0:T(8,128)(2,1)S(1)}, u32[]{:S(2)}, u32[]{:S(2)}) collective-permute-start(bf16[128,512]{1,0:T(8,128)(2,1)} %get-tuple-element.67.refs_2_.refs_0_), channel_id=1, source_target_pairs={{0,4},{1,5},{2,0},{3,1},{4,8},{5,9},{6,2},{7,3},{8,12},{9,13},{10,... | collective-permute-start | bytes 393224 | tf_op jit(solution)/shard_map/ppermute | solution.py:59
  56.8 9.7 %collective-permute-start.22 = (bf16[128,512]{1,0:T(8,128)(2,1)}, bf16[128,512]{1,0:T(8,128)(2,1)S(1)}, u32[]{:S(2)}, u32[]{:S(2)}) collective-permute-start(bf16[128,512]{1,0:T(8,128)(2,1)} %get-tuple-element.70.refs_3_), channel_id=1, source_target_pairs={{0,2},{1,3},{2,6},{3,7},{4,0},{5,1},{6,10},{7,11},{8,4},{9,5},{10,... | collective-permute-start | bytes 393224 | tf_op jit(solution)/shard_map/ppermute | solution.py:59
  59.4 9.8 %collective-permute-start.23 = (bf16[128,512]{1,0:T(8,128)(2,1)}, bf16[128,512]{1,0:T(8,128)(2,1)S(1)}, u32[]{:S(2)}, u32[]{:S(2)}) collective-permute-start(bf16[128,512]{1,0:T(8,128)(2,1)} %get-tuple-element.68.refs_1_), channel_id=1, source_target_pairs={{0,4},{1,5},{2,0},{3,1},{4,8},{5,9},{6,2},{7,3},{8,12},{9,13},{10,... | collective-permute-start | bytes 393224 | tf_op jit(solution)/shard_map/ppermute | solution.py:59
  60.2 9.0 %collective-permute-start.24 = (bf16[128,512]{1,0:T(8,128)(2,1)}, bf16[128,512]{1,0:T(8,128)(2,1)S(1)}, u32[]{:S(2)}, u32[]{:S(2)}) collective-permute-start(bf16[128,512]{1,0:T(8,128)(2,1)} %get-tuple-element.69.refs_2_), channel_id=1, source_target_pairs={{0,2},{1,3},{2,6},{3,7},{4,0},{5,1},{6,10},{7,11},{8,4},{9,5},{10,... | collective-permute-start | bytes 393224 | tf_op jit(solution)/shard_map/ppermute | solution.py:59
  67.2 10.4 %collective-permute-start.26 = (bf16[128,512]{1,0:T(8,128)(2,1)}, bf16[128,512]{1,0:T(8,128)(2,1)S(1)}, u32[]{:S(2)}, u32[]{:S(2)}) collective-permute-start(bf16[128,512]{1,0:T(8,128)(2,1)} %get-tuple-element.73.refs_2_.refs_0_), channel_id=1, source_target_pairs={{0,4},{1,5},{2,0},{3,1},{4,8},{5,9},{6,2},{7,3},{8,12},{9,13},{10,... | collective-permute-start | bytes 393224 | tf_op jit(solution)/shard_map/ppermute | solution.py:59
  67.9 10.1 %collective-permute-start.27 = (bf16[128,512]{1,0:T(8,128)(2,1)}, bf16[128,512]{1,0:T(8,128)(2,1)S(1)}, u32[]{:S(2)}, u32[]{:S(2)}) collective-permute-start(bf16[128,512]{1,0:T(8,128)(2,1)} %get-tuple-element.76.refs_3_), channel_id=1, source_target_pairs={{0,2},{1,3},{2,6},{3,7},{4,0},{5,1},{6,10},{7,11},{8,4},{9,5},{10,... | collective-permute-start | bytes 393224 | tf_op jit(solution)/shard_map/ppermute | solution.py:59
  70.5 9.0 %collective-permute-start.28 = (bf16[128,512]{1,0:T(8,128)(2,1)}, bf16[128,512]{1,0:T(8,128)(2,1)S(1)}, u32[]{:S(2)}, u32[]{:S(2)}) collective-permute-start(bf16[128,512]{1,0:T(8,128)(2,1)} %get-tuple-element.74.refs_1_), channel_id=1, source_target_pairs={{0,4},{1,5},{2,0},{3,1},{4,8},{5,9},{6,2},{7,3},{8,12},{9,13},{10,... | collective-permute-start | bytes 393224 | tf_op jit(solution)/shard_map/ppermute | solution.py:59
  71.3 9.5 %collective-permute-start.29 = (bf16[128,512]{1,0:T(8,128)(2,1)}, bf16[128,512]{1,0:T(8,128)(2,1)S(1)}, u32[]{:S(2)}, u32[]{:S(2)}) collective-permute-start(bf16[128,512]{1,0:T(8,128)(2,1)} %get-tuple-element.75.refs_2_), channel_id=1, source_target_pairs={{0,2},{1,3},{2,6},{3,7},{4,0},{5,1},{6,10},{7,11},{8,4},{9,5},{10,... | collective-permute-start | bytes 393224 | tf_op jit(solution)/shard_map/ppermute | solution.py:59
  72.5 17.2 %collective-permute-start.20 = (bf16[8,32,512]{2,1,0:T(8,128)(2,1)S(1)}, bf16[8,32,512]{2,1,0:T(8,128)(2,1)S(1)}, u32[]{:S(2)}, u32[]{:S(2)}) collective-permute-start(bf16[8,32,512]{2,1,0:T(8,128)(2,1)S(1)} %get-tuple-element.72), channel_id=1, source_target_pairs={{0,1},{1,0},{2,3},{3,2},{4,5},{5,4},{6,7},{7,6},{8,9},{9,8},{10,11... | collective-permute-start | bytes 786440 | tf_op jit(solution)/shard_map/ppermute | solution.py:50
  77.6 12.2 %collective-permute-start.25 = (bf16[8,32,512]{2,1,0:T(8,128)(2,1)S(1)}, bf16[8,32,512]{2,1,0:T(8,128)(2,1)S(1)}, u32[]{:S(2)}, u32[]{:S(2)}) collective-permute-start(bf16[8,32,512]{2,1,0:T(8,128)(2,1)S(1)} %get-tuple-element.78), channel_id=1, source_target_pairs={{0,1},{1,0},{2,3},{3,2},{4,5},{5,4},{6,7},{7,6},{8,9},{9,8},{10,11... | collective-permute-start | bytes 786440 | tf_op jit(solution)/shard_map/ppermute | solution.py:50
  78.7 7.6 %collective-permute-start.31 = (bf16[128,512]{1,0:T(8,128)(2,1)}, bf16[128,512]{1,0:T(8,128)(2,1)S(1)}, u32[]{:S(2)}, u32[]{:S(2)}) collective-permute-start(bf16[128,512]{1,0:T(8,128)(2,1)} %get-tuple-element.79.refs_2_.refs_0_), channel_id=1, source_target_pairs={{0,4},{1,5},{2,0},{3,1},{4,8},{5,9},{6,2},{7,3},{8,12},{9,13},{10,... | collective-permute-start | bytes 393224 | tf_op jit(solution)/shard_map/ppermute | solution.py:59
  79.5 7.4 %collective-permute-start.32 = (bf16[128,512]{1,0:T(8,128)(2,1)}, bf16[128,512]{1,0:T(8,128)(2,1)S(1)}, u32[]{:S(2)}, u32[]{:S(2)}) collective-permute-start(bf16[128,512]{1,0:T(8,128)(2,1)} %get-tuple-element.82.refs_3_), channel_id=1, source_target_pairs={{0,2},{1,3},{2,6},{3,7},{4,0},{5,1},{6,10},{7,11},{8,4},{9,5},{10,... | collective-permute-start | bytes 393224 | tf_op jit(solution)/shard_map/ppermute | solution.py:59
  86.4 3.4 %collective-permute-start.30 = (bf16[8,32,512]{2,1,0:T(8,128)(2,1)}, bf16[8,32,512]{2,1,0:T(8,128)(2,1)S(1)}, u32[]{:S(2)}, u32[]{:S(2)}) collective-permute-start(bf16[8,32,512]{2,1,0:T(8,128)(2,1)} %get-tuple-element.84), channel_id=1, source_target_pairs={{0,1},{1,0},{2,3},{3,2},{4,5},{5,4},{6,7},{7,6},{8,9},{9,8},{10,11... | collective-permute-start | bytes 786440 | tf_op jit(solution)/shard_map/ppermute | solution.py:50
  86.4 3.4 %collective-permute-start.15 = (bf16[4,32,512]{2,1,0:T(8,128)(2,1)S(1)}, bf16[4,32,512]{2,1,0:T(8,128)(2,1)S(1)}, u32[]{:S(2)}, u32[]{:S(2)}) collective-permute-start(bf16[4,32,512]{2,1,0:T(8,128)(2,1)S(1)} %get-tuple-element.66), channel_id=1, source_target_pairs={{0,1},{1,0},{2,3},{3,2},{4,5},{5,4},{6,7},{7,6},{8,9},{9,8},{10,11... | collective-permute-start | bytes 393224 | tf_op jit(solution)/shard_map/ppermute | solution.py:50
  (41 other events, 177.2 us)

commit v5 on v4

--- a/solution.py
+++ b/solution.py
@@ -69,7 +69,7 @@
 def embed_kernel(
     ring, per_step, slots, me_ref, lists_ref, mask_ref,
     x_ref, w1_ref, w2_ref, gain_ref, interp_ref,
-    latent_ref, kept_ref, sent_ref, table_ref, placed,
+    latent_ref, kept_ref, sent_ref, table_ref,
 ):
     step = pl.program_id(0)
     me = me_ref[0]
@@ -82,34 +82,31 @@
         slot = split(block * list_len + k, ring.n_band)[0]
         return (across * ring.chips + ahead) * slots + slot, tile
 
-    first = lax.dot_general(
-        x_ref[...], w1_ref[...], (((0,), (0,)), ((), ())), preferred_element_type=F32
-    )
-    before = jnp.dot(silu(first).astype(BF16), w2_ref[...], preferred_element_type=F32)
-    latent = layer_norm(before, gain_ref[...]).astype(BF16)
-    latent_ref[...] = latent
+    spare = kept_ref.shape[0] - 1
     for b in range(per_step):
+        block = step * per_step + b
+        rows = slice(b * block_rows, (b + 1) * block_rows)
+        first = lax.dot_general(
+            x_ref[:, rows], w1_ref[...], (((0,), (0,)), ((), ())), preferred_element_type=F32
+        )
+        before = jnp.dot(silu(first).astype(BF16), w2_ref[...], preferred_element_type=F32)
+        latent = layer_norm(before, gain_ref[...]).astype(BF16)
+        start = pl.multiple_of(block * block_rows, block_rows)
+        latent_ref[pl.ds(start, block_rows)] = latent
         weights = interp_ref[b].reshape(list_len * tile_rows, block_rows)
-        part = jnp.dot(
-            weights, latent[b * block_rows : (b + 1) * block_rows], preferred_element_type=F32
-        )
+        part = jnp.dot(weights, latent, preferred_element_type=F32)
         for k in range(list_len):
             place, tile = spot(me, b, k)
             there, its_tile = spot(me ^ 1, b, k)
-            block = step * per_step + b
             mask = mask_ref[k, me * blk_count + block]
             table_ref[0, place] = tile
             table_ref[1, there] = its_tile
             table_ref[2, place] = mask
             table_ref[3, there] = mask_ref[k, (me ^ 1) * blk_count + block]
             masked = part[k * tile_rows : (k + 1) * tile_rows] * mask.astype(F32)
-            placed[place] = masked.astype(BF16)
-
-    @pl.when(step == pl.num_programs(0) - 1)
-    def _():
-        count = kept_ref.shape[0]
-        kept_ref[...] = placed[:count]
-        sent_ref[...] = placed[count:]
+            masked = masked.astype(BF16)
+            kept_ref[jnp.minimum(place, spare)] = masked
+            sent_ref[jnp.where(place >= spare, place - spare, spare)] = masked
 
 
 def add_entries(total, table_ref, owner, kept, other, chips):
@@ -193,7 +190,7 @@
     pieces, (out_ref, held, sems) = rest[:count], rest[count:]
     step = pl.program_id(0)
     me = me_ref[0]
-    block_rows, listed = weights_ref.shape[1:]
+    block_rows = weights_ref.shape[1]
     list_len = lists_ref.shape[0]
     tile_rows, width = held.shape[1:]
 
@@ -224,9 +221,10 @@
             slot = split(number * list_len + k, ring.n_band)[0]
             values.append(held[(across * ring.chips + ahead) * slots + slot])
         value = jnp.concatenate(values, axis=0)
-        back = jnp.dot(weights_ref[b], value, preferred_element_type=F32)
-        rows = slice(b * block_rows, (b + 1) * block_rows)
-        out_ref[rows] = (latent_ref[rows].astype(F32) + back).astype(BF16)
+        back = jnp.dot(weights_ref[number], value, preferred_element_type=F32)
+        start = pl.multiple_of(number * block_rows, block_rows)
+        total = latent_ref[pl.ds(start, block_rows)].astype(F32) + back
+        out_ref[b * block_rows : (b + 1) * block_rows] = total.astype(BF16)
 
 
 def whole(array):
@@ -277,9 +275,9 @@
         return pltpu.with_memory_space_constraint(array, pltpu.HBM)
 
     gain = embed_gain.reshape(1, width)
-    per_step = 2
+    per_step = 4
     rows = per_step * block_rows
-    held_shape = (chips * slots, tile_rows, width)
+    held_shape = (chips * slots + 1, tile_rows, width)
     latent, kept, sent, table = pl.pallas_call(
         functools.partial(embed_kernel, ring, per_step, slots),
         out_shape=[shape((blk_count * block_rows, width))]
@@ -295,10 +293,8 @@
                 whole(gain),
                 pl.BlockSpec((per_step,) + interp.shape[1:], lambda i, *_: (i, 0, 0, 0)),
             ],
-            out_specs=[pl.BlockSpec((rows, width), lambda i, *_: (i, 0))]
-            + [pl.BlockSpec(held_shape, lambda i, *_: (0, 0, 0))] * N_CORE
+            out_specs=[pl.BlockSpec(memory_space=pltpu.VMEM)] * (1 + N_CORE)
             + [pl.BlockSpec(memory_space=pltpu.SMEM)],
-            scratch_shapes=[pltpu.VMEM((entries, tile_rows, width), BF16)],
         ),
         compiler_params=params(24),
         cost_estimate=cost(
@@ -405,6 +401,7 @@
             in_specs=[pl.BlockSpec(memory_space=pl.ANY)] * (len(values) + 1),
             out_specs=[pl.BlockSpec(memory_space=pl.ANY)] * len(values),
             input_output_aliases={i: i for i in range(len(values))},
+            compiler_params=params(1),
             cost_estimate=cost(0),
             name="in_order",
         )(*values, token)
@@ -453,10 +450,7 @@
         grid_spec=pltpu.PrefetchScalarGridSpec(
             num_scalar_prefetch=2,
             grid=(blk_count // per_step,),
-            in_specs=[
-                pl.BlockSpec((rows, width), lambda i, *_: (i, 0)),
-                pl.BlockSpec((per_step,) + weights.shape[1:], lambda i, *_: (i, 0, 0)),
-            ]
+            in_specs=[pl.BlockSpec(memory_space=pltpu.VMEM)] * 2
             + [pl.BlockSpec(memory_space=pl.ANY)] * len(pieces),
             out_specs=pl.BlockSpec((rows, width), lambda i, *_: (i, 0)),
             scratch_shapes=[

time: 101 us -> 90.1 us (0.89)
  local copies, waits for them, and re-layouts: 24.2 us -> 5.22 us
  waiting for transfers between devices: 17 us -> 22.3 us
  Pallas kernels: 27 us -> 30.3 us
    unnamed x78 -> x18, local copies, waits for them, and re-layouts: 22.6 us -> 3.58 us
    ppermute x28, waiting for transfers between devices: 14.7 us -> 19.9 us  [over(): return lax.ppermute(value, 'band', pairs)]
    pallas_call x1, Pallas kernels: 11.3 us -> 13.9 us  [on_device(): pl.pallas_call(functools.partial(embed_kernel, ring, per_step, slots), ou...]
  transfers between devices with their start and end apart: 34 -> 34, of which waited for: 15 -> 19; matrix products, arithmetic and copies ran while one was open for 2% -> 2% of each run, Pallas kernels for 6% -> 8%
where the time goes in v5:
time: 90.1 us; the launch traced here: 89.8 us
  starting transfers between devices  31.1 us (35%)
  Pallas kernels  30.3 us (34%)
  waiting for transfers between devices  22.3 us (25%)
  local copies, waits for them, and re-layouts  5.22 us (6%)
    ppermute x28, starting transfers between devices, over(): return lax.ppermute(value, 'band', pairs)  30.1 us
    ppermute x28, waiting for transfers between devices, over(): return lax.ppermute(value, 'band', pairs)  19.9 us
    pallas_call x1, Pallas kernels, on_device(): pl.pallas_call(functools.partial(embed_kernel, ring, per_step, slots), ou...  13.9 us
    pallas_call x1, Pallas kernels, on_device(): pl.pallas_call(functools.partial(back_kernel, ring, places, slots, per_st...  7.33 us
    pallas_call x5, Pallas kernels, pick(): pl.pallas_call(functools.partial(pick_kernel, owners, slots, chips), out_...  5.23 us
    unnamed x18, local copies, waits for them, and re-layouts  3.58 us
    ppermute x6, waiting for transfers between devices, over_core(): return lax.ppermute(value, 'band', [(i, i ^ 1) for i in range(self.n_band)])  2.35 us
  transfers between devices with their start and end apart: 34, of which 19 were waited for; matrix products, arithmetic and copies ran while one was open for 2% of the time, Pallas kernels for 8%

profile of v5, /device:TPU:0, one launch (start us, length us, event | category | flops | bytes accessed | tf_op | source)
XLA Modules:
  0.0 89.8 jit_solution(16285127313137570050)
XLA Ops:
  2.0 13.9 %embed.1 = (bf16[4096,512]{1,0:T(8,128)(2,1)S(1)}, bf16[33,32,512]{2,1,0:T(8,128)(2,1)S(1)}, bf16[33,32,512]{2,1,0:T(8,128)(2,1)S(1)}, s32[4,64]{1,0:T(4,128)S(1)}) custom-call(s32[1]{0:T(128)} %bitcast.me_ref, s32[4,256]{1,0:T(4,128)S(1)} %bitcast.9, s32[4,256]{1,0:T(4,128)S(1)} %bitcast.12, bf16[227,4096]{1,0:T(8,128)(2,1)} %bitcast.14, ...), custom_call_target="tpu_custom_call" | custom-call | flops 3636461568 | bytes 2908160 | tf_op jit(solution)/shard_map/embed/pallas_call | solution.py:281
  16.5 2.3 %collective-permute-done.other.refs_3_.refs_4_.refs_5_ = bf16[33,32,512]{2,1,0:T(8,128)(2,1)S(1)} collective-permute-done((bf16[33,32,512]{2,1,0:T(8,128)(2,1)S(1)}, bf16[33,32,512]{2,1,0:T(8,128)(2,1)S(1)}, u32[]{:S(2)}, u32[]{:S(2)}) %collective-permute-start) | collective-permute-done | bytes 1081376 | tf_op jit(solution)/shard_map/ppermute | solution.py:50
  19.7 3.0 %collective-permute-start.1 = (bf16[4,32,512]{2,1,0:T(8,128)(2,1)S(1)}, bf16[4,32,512]{2,1,0:T(8,128)(2,1)S(1)}, u32[]{:S(2)}, u32[]{:S(2)}) collective-permute-start(bf16[4,32,512]{2,1,0:T(8,128)(2,1)S(1)} %get-tuple-element.49), channel_id=1, source_target_pairs={{0,4},{1,5},{2,0},{3,1},{4,8},{5,9},{6,2},{7,3},{8,12},{9,13},{10,... | collective-permute-start | bytes 393224 | tf_op jit(solution)/shard_map/ppermute | solution.py:59
  22.7 2.0 %collective-permute-start.5 = (bf16[4,32,512]{2,1,0:T(8,128)(2,1)S(1)}, bf16[4,32,512]{2,1,0:T(8,128)(2,1)S(1)}, u32[]{:S(2)}, u32[]{:S(2)}) collective-permute-start(bf16[4,32,512]{2,1,0:T(8,128)(2,1)S(1)} %get-tuple-element.53), channel_id=1, source_target_pairs={{0,4},{1,5},{2,0},{3,1},{4,8},{5,9},{6,2},{7,3},{8,12},{9,13},{10,... | collective-permute-start | bytes 393224 | tf_op jit(solution)/shard_map/ppermute | solution.py:59
  24.7 1.3 %own_chunks.1.own_right.own_left.token.own = f32[8,8,32,512]{3,2,1,0:T(8,128)S(1)} custom-call(s32[4,64]{1,0:T(4,128)S(1)} %get-tuple-element.46.table_ref, bf16[33,32,512]{2,1,0:T(8,128)(2,1)S(1)} %get-tuple-element.47.kept.refs_0_.refs_1_.refs_2_, bf16[33,32,512]{2,1,0:T(8,128)(2,1)S(1)} %collective-permute-done.other.refs_3_.refs_4_.refs_5_), custom_call_target="tpu_custom_call" | custom-call | bytes 4325376 | tf_op jit(solution)/shard_map/own_chunks/pallas_call | solution.py:335
  26.9 2.2 %collective-permute-done.2.left = bf16[4,32,512]{2,1,0:T(8,128)(2,1)S(1)} collective-permute-done((bf16[4,32,512]{2,1,0:T(8,128)(2,1)S(1)}, bf16[4,32,512]{2,1,0:T(8,128)(2,1)S(1)}, u32[]{:S(2)}, u32[]{:S(2)}) %collective-permute-start.2) | collective-permute-done | bytes 131104 | tf_op jit(solution)/shard_map/ppermute | solution.py:59
  29.1 1.6 %collective-permute-start.3 = (bf16[4,32,512]{2,1,0:T(8,128)(2,1)S(1)}, bf16[4,32,512]{2,1,0:T(8,128)(2,1)S(1)}, u32[]{:S(2)}, u32[]{:S(2)}) collective-permute-start(bf16[4,32,512]{2,1,0:T(8,128)(2,1)S(1)} %get-tuple-element.51.token), channel_id=1, source_target_pairs={{0,4},{1,5},{2,0},{3,1},{4,8},{5,9},{6,2},{7,3},{8,12},{9,13},{10,... | collective-permute-start | bytes 393224 | tf_op jit(solution)/shard_map/ppermute | solution.py:59
  31.8 1.6 %collective-permute-start.9 = (bf16[4,32,512]{2,1,0:T(8,128)(2,1)S(1)}, bf16[4,32,512]{2,1,0:T(8,128)(2,1)S(1)}, u32[]{:S(2)}, u32[]{:S(2)}) collective-permute-start(bf16[4,32,512]{2,1,0:T(8,128)(2,1)S(1)} %get-tuple-element.55.token), channel_id=1, source_target_pairs={{0,4},{1,5},{2,0},{3,1},{4,8},{5,9},{6,2},{7,3},{8,12},{9,13},{10,... | collective-permute-start | bytes 393224 | tf_op jit(solution)/shard_map/ppermute | solution.py:59
  33.3 2.2 %collective-permute-done.3.right = bf16[4,32,512]{2,1,0:T(8,128)(2,1)S(1)} collective-permute-done((bf16[4,32,512]{2,1,0:T(8,128)(2,1)S(1)}, bf16[4,32,512]{2,1,0:T(8,128)(2,1)S(1)}, u32[]{:S(2)}, u32[]{:S(2)}) %collective-permute-start.3) | collective-permute-done | bytes 131104 | tf_op jit(solution)/shard_map/ppermute | solution.py:59
  35.8 1.6 %collective-permute-start.7 = (bf16[4,32,512]{2,1,0:T(8,128)(2,1)S(1)}, bf16[4,32,512]{2,1,0:T(8,128)(2,1)S(1)}, u32[]{:S(2)}, u32[]{:S(2)}) collective-permute-start(bf16[4,32,512]{2,1,0:T(8,128)(2,1)S(1)} %get-tuple-element.56.token), channel_id=1, source_target_pairs={{0,4},{1,5},{2,0},{3,1},{4,8},{5,9},{6,2},{7,3},{8,12},{9,13},{10,... | collective-permute-start | bytes 393224 | tf_op jit(solution)/shard_map/ppermute | solution.py:59
  38.4 1.6 %collective-permute-start.13 = (bf16[4,32,512]{2,1,0:T(8,128)(2,1)S(1)}, bf16[4,32,512]{2,1,0:T(8,128)(2,1)S(1)}, u32[]{:S(2)}, u32[]{:S(2)}) collective-permute-start(bf16[4,32,512]{2,1,0:T(8,128)(2,1)S(1)} %get-tuple-element.59.token), channel_id=1, source_target_pairs={{0,4},{1,5},{2,0},{3,1},{4,8},{5,9},{6,2},{7,3},{8,12},{9,13},{10,... | collective-permute-start | bytes 393224 | tf_op jit(solution)/shard_map/ppermute | solution.py:59
  41.2 1.2 %collective-permute-done.8.left = bf16[4,32,512]{2,1,0:T(8,128)(2,1)S(1)} collective-permute-done((bf16[4,32,512]{2,1,0:T(8,128)(2,1)S(1)}, bf16[4,32,512]{2,1,0:T(8,128)(2,1)S(1)}, u32[]{:S(2)}, u32[]{:S(2)}) %collective-permute-start.8) | collective-permute-done | bytes 131104 | tf_op jit(solution)/shard_map/ppermute | solution.py:59
  42.4 1.6 %collective-permute-start.11 = (bf16[4,32,512]{2,1,0:T(8,128)(2,1)S(1)}, bf16[4,32,512]{2,1,0:T(8,128)(2,1)S(1)}, u32[]{:S(2)}, u32[]{:S(2)}) collective-permute-start(bf16[4,32,512]{2,1,0:T(8,128)(2,1)S(1)} %get-tuple-element.60), channel_id=1, source_target_pairs={{0,4},{1,5},{2,0},{3,1},{4,8},{5,9},{6,2},{7,3},{8,12},{9,13},{10,... | collective-permute-start | bytes 393224 | tf_op jit(solution)/shard_map/ppermute | solution.py:59
  45.2 2.2 %collective-permute-done.11.right_a = bf16[4,32,512]{2,1,0:T(8,128)(2,1)S(1)} collective-permute-done((bf16[4,32,512]{2,1,0:T(8,128)(2,1)S(1)}, bf16[4,32,512]{2,1,0:T(8,128)(2,1)S(1)}, u32[]{:S(2)}, u32[]{:S(2)}) %collective-permute-start.11) | collective-permute-done | bytes 131104 | tf_op jit(solution)/shard_map/ppermute | solution.py:59
  47.4 1.5 %collective-permute-done.12.left_b = bf16[4,32,512]{2,1,0:T(8,128)(2,1)S(1)} collective-permute-done((bf16[4,32,512]{2,1,0:T(8,128)(2,1)S(1)}, bf16[4,32,512]{2,1,0:T(8,128)(2,1)S(1)}, u32[]{:S(2)}, u32[]{:S(2)}) %collective-permute-start.12) | collective-permute-done | bytes 131104 | tf_op jit(solution)/shard_map/ppermute | solution.py:59
  49.0 1.5 %mesh_step.1 = (bf16[256,512]{1,0:T(8,128)(2,1)}, bf16[128,512]{1,0:T(8,128)(2,1)S(1)}, bf16[128,512]{1,0:T(8,128)(2,1)S(1)}) custom-call(bf16[256,512]{1,0:T(8,128)(2,1)S(1)} %copy-done.4, bf16[512,512]{1,0:T(8,128)(2,1)S(1)} %copy-done.2, bf16[512,512]{1,0:T(8,128)(2,1)S(1)} %copy-done.3, f32[1,512]{1,0:T(1,128)S(1)} %bitcast.11, ...), custom_call_target="tpu_custom_call" | custom-call | flops 268435456 | bytes 1048576 | tf_op jit(solution)/shard_map/mesh_step/pallas_call | solution.py:383
  50.5 1.6 %collective-permute-start.16 = (bf16[128,512]{1,0:T(8,128)(2,1)S(1)}, bf16[128,512]{1,0:T(8,128)(2,1)S(1)}, u32[]{:S(2)}, u32[]{:S(2)}) collective-permute-start(bf16[128,512]{1,0:T(8,128)(2,1)S(1)} %get-tuple-element.63.refs_0_), channel_id=1, source_target_pairs={{0,4},{1,5},{2,0},{3,1},{4,8},{5,9},{6,2},{7,3},{8,12},{9,13},{10,... | collective-permute-start | bytes 393224 | tf_op jit(solution)/shard_map/ppermute | solution.py:59
  52.5 1.6 %collective-permute-start.18 = (bf16[128,512]{1,0:T(8,128)(2,1)S(1)}, bf16[128,512]{1,0:T(8,128)(2,1)S(1)}, u32[]{:S(2)}, u32[]{:S(2)}) collective-permute-start(bf16[128,512]{1,0:T(8,128)(2,1)S(1)} %get-tuple-element.64.refs_1_), channel_id=1, source_target_pairs={{0,4},{1,5},{2,0},{3,1},{4,8},{5,9},{6,2},{7,3},{8,12},{9,13},{10,... | collective-permute-start | bytes 393224 | tf_op jit(solution)/shard_map/ppermute | solution.py:59
  55.1 1.6 %collective-permute-done.16.refs_0_ = bf16[128,512]{1,0:T(8,128)(2,1)S(1)} collective-permute-done((bf16[128,512]{1,0:T(8,128)(2,1)S(1)}, bf16[128,512]{1,0:T(8,128)(2,1)S(1)}, u32[]{:S(2)}, u32[]{:S(2)}) %collective-permute-start.16) | collective-permute-done | bytes 131104 | tf_op jit(solution)/shard_map/ppermute | solution.py:59
  56.8 1.6 %collective-permute-done.17.refs_1_ = bf16[128,512]{1,0:T(8,128)(2,1)S(1)} collective-permute-done((bf16[128,512]{1,0:T(8,128)(2,1)S(1)}, bf16[128,512]{1,0:T(8,128)(2,1)S(1)}, u32[]{:S(2)}, u32[]{:S(2)}) %collective-permute-start.17) | collective-permute-done | bytes 131104 | tf_op jit(solution)/shard_map/ppermute | solution.py:59
  61.9 1.1 %collective-permute-start.24 = (bf16[128,512]{1,0:T(8,128)(2,1)S(1)}, bf16[128,512]{1,0:T(8,128)(2,1)S(1)}, u32[]{:S(2)}, u32[]{:S(2)}) collective-permute-start(bf16[128,512]{1,0:T(8,128)(2,1)S(1)} %get-tuple-element.69.refs_2_), channel_id=1, source_target_pairs={{0,2},{1,3},{2,6},{3,7},{4,0},{5,1},{6,10},{7,11},{8,4},{9,5},{10,... | collective-permute-start | bytes 393224 | tf_op jit(solution)/shard_map/ppermute | solution.py:59
  65.4 1.4 %collective-permute-start.27 = (bf16[128,512]{1,0:T(8,128)(2,1)S(1)}, bf16[128,512]{1,0:T(8,128)(2,1)S(1)}, u32[]{:S(2)}, u32[]{:S(2)}) collective-permute-start(bf16[128,512]{1,0:T(8,128)(2,1)S(1)} %get-tuple-element.76.refs_3_), channel_id=1, source_target_pairs={{0,2},{1,3},{2,6},{3,7},{4,0},{5,1},{6,10},{7,11},{8,4},{9,5},{10,... | collective-permute-start | bytes 393224 | tf_op jit(solution)/shard_map/ppermute | solution.py:59
  66.9 1.4 %collective-permute-start.28 = (bf16[128,512]{1,0:T(8,128)(2,1)S(1)}, bf16[128,512]{1,0:T(8,128)(2,1)S(1)}, u32[]{:S(2)}, u32[]{:S(2)}) collective-permute-start(bf16[128,512]{1,0:T(8,128)(2,1)S(1)} %get-tuple-element.74.refs_1_), channel_id=1, source_target_pairs={{0,4},{1,5},{2,0},{3,1},{4,8},{5,9},{6,2},{7,3},{8,12},{9,13},{10,... | collective-permute-start | bytes 393224 | tf_op jit(solution)/shard_map/ppermute | solution.py:59
  68.9 1.3 %pick_6.1 = (bf16[8,32,512]{2,1,0:T(8,128)(2,1)S(1)}, bf16[8,32,512]{2,1,0:T(8,128)(2,1)}) custom-call(s32[4,64]{1,0:T(4,128)S(1)} %get-tuple-element.46.table_ref, bf16[128,512]{1,0:T(8,128)(2,1)S(1)} %get-tuple-element.73.refs_2_.refs_0_, bf16[128,512]{1,0:T(8,128)(2,1)S(1)} %get-tuple-element.74.refs_1_, bf16[128,512]{1,0:T(8,128)(2,1)S(1)} %get-tuple-element.75.refs_2_, ...), custom_call_target="tpu_custom_call" | custom-call | bytes 524288 | tf_op jit(solution)/shard_map/pick_6/pallas_call | solution.py:414
  70.8 1.4 %collective-permute-start.31 = (bf16[128,512]{1,0:T(8,128)(2,1)S(1)}, bf16[128,512]{1,0:T(8,128)(2,1)S(1)}, u32[]{:S(2)}, u32[]{:S(2)}) collective-permute-start(bf16[128,512]{1,0:T(8,128)(2,1)S(1)} %get-tuple-element.79.refs_2_.refs_0_), channel_id=1, source_target_pairs={{0,4},{1,5},{2,0},{3,1},{4,8},{5,9},{6,2},{7,3},{8,12},{9,13},{10,... | collective-permute-start | bytes 393224 | tf_op jit(solution)/shard_map/ppermute | solution.py:59
  73.2 1.3 %pick_5.1 = (bf16[8,32,512]{2,1,0:T(8,128)(2,1)S(1)}, bf16[8,32,512]{2,1,0:T(8,128)(2,1)}) custom-call(s32[4,64]{1,0:T(4,128)S(1)} %get-tuple-element.46.table_ref, bf16[128,512]{1,0:T(8,128)(2,1)S(1)} %get-tuple-element.79.refs_2_.refs_0_, bf16[128,512]{1,0:T(8,128)(2,1)S(1)} %get-tuple-element.80.refs_1_, bf16[128,512]{1,0:T(8,128)(2,1)S(1)} %get-tuple-element.81.refs_2_, ...), custom_call_target="tpu_custom_call" | custom-call | bytes 524288 | tf_op jit(solution)/shard_map/pick_5/pallas_call | solution.py:414
  74.6 1.7 %collective-permute-done.31.refs_0_ = bf16[128,512]{1,0:T(8,128)(2,1)S(1)} collective-permute-done((bf16[128,512]{1,0:T(8,128)(2,1)S(1)}, bf16[128,512]{1,0:T(8,128)(2,1)S(1)}, u32[]{:S(2)}, u32[]{:S(2)}) %collective-permute-start.31) | collective-permute-done | bytes 131104 | tf_op jit(solution)/shard_map/ppermute | solution.py:59
  76.2 1.1 %collective-permute-done.32.refs_1_ = bf16[128,512]{1,0:T(8,128)(2,1)S(1)} collective-permute-done((bf16[128,512]{1,0:T(8,128)(2,1)S(1)}, bf16[128,512]{1,0:T(8,128)(2,1)S(1)}, u32[]{:S(2)}, u32[]{:S(2)}) %collective-permute-start.32) | collective-permute-done | bytes 131104 | tf_op jit(solution)/shard_map/ppermute | solution.py:59
  77.3 1.2 %pick_4.1 = (bf16[4,32,512]{2,1,0:T(8,128)(2,1)S(1)}, bf16[4,32,512]{2,1,0:T(8,128)(2,1)}) custom-call(s32[4,64]{1,0:T(4,128)S(1)} %get-tuple-element.46.table_ref, bf16[128,512]{1,0:T(8,128)(2,1)S(1)} %collective-permute-done.31.refs_0_, bf16[128,512]{1,0:T(8,128)(2,1)S(1)} %collective-permute-done.32.refs_1_), custom_call_target="tpu_custom_call" | custom-call | bytes 262144 | tf_op jit(solution)/shard_map/pick_4/pallas_call | solution.py:414
  78.6 1.6 %copy.26 = bf16[16,128,256]{1,2,0:T(8,128)(2,1)S(1)} copy(bf16[16,128,256]{2,1,0:T(8,128)(2,1)} %bitcast.13) | data formatting | bytes 2097152 | tf_op jit(solution)/shard_map/reshape | solution.py:444
  80.3 2.2 %copy-done.1 = bf16[4096,512]{1,0:T(8,128)(2,1)S(1)} copy-done((bf16[4096,512]{1,0:T(8,128)(2,1)S(1)}, bf16[4096,512]{1,0:T(8,128)(2,1)}, u32[]{:S(2)}) %copy-start.1) | copy-done | bytes 4194328
  82.5 7.3 %back.1 = bf16[4096,512]{1,0:T(8,128)(2,1)} custom-call(s32[1]{0:T(128)} %bitcast.me_ref, s32[4,256]{1,0:T(4,128)S(1)} %bitcast.10, bf16[4096,512]{1,0:T(8,128)(2,1)S(1)} %copy-done.1, bf16[16,256,128]{2,1,0:T(8,128)(2,1)S(1)} %bitcast.8, bf16[4,32,512]{2,1,0:T(8,128)(2,1)S(1)} %get-tuple-element.65.refs_2_.rest_0_, ...), custom_call_target="tpu_custom_call" | custom-call | flops 536870912 | bytes 9437184 | tf_op jit(solution)/shard_map/back/pallas_call | solution.py:447
  (76 shorter events, 18.1 us)
Async XLA Ops:
  19.7 7.2 %collective-permute-start.1 = (bf16[4,32,512]{2,1,0:T(8,128)(2,1)S(1)}, bf16[4,32,512]{2,1,0:T(8,128)(2,1)S(1)}, u32[]{:S(2)}, u32[]{:S(2)}) collective-permute-start(bf16[4,32,512]{2,1,0:T(8,128)(2,1)S(1)} %get-tuple-element.49), channel_id=1, source_target_pairs={{0,4},{1,5},{2,0},{3,1},{4,8},{5,9},{6,2},{7,3},{8,12},{9,13},{10,... | collective-permute-start | bytes 393224 | tf_op jit(solution)/shard_map/ppermute | solution.py:59
  22.7 6.4 %collective-permute-start.2 = (bf16[4,32,512]{2,1,0:T(8,128)(2,1)S(1)}, bf16[4,32,512]{2,1,0:T(8,128)(2,1)S(1)}, u32[]{:S(2)}, u32[]{:S(2)}) collective-permute-start(bf16[4,32,512]{2,1,0:T(8,128)(2,1)S(1)} %get-tuple-element.50), channel_id=1, source_target_pairs={{0,2},{1,3},{2,6},{3,7},{4,0},{5,1},{6,10},{7,11},{8,4},{9,5},{10,... | collective-permute-start | bytes 393224 | tf_op jit(solution)/shard_map/ppermute | solution.py:59
  22.7 8.5 %collective-permute-start.5 = (bf16[4,32,512]{2,1,0:T(8,128)(2,1)S(1)}, bf16[4,32,512]{2,1,0:T(8,128)(2,1)S(1)}, u32[]{:S(2)}, u32[]{:S(2)}) collective-permute-start(bf16[4,32,512]{2,1,0:T(8,128)(2,1)S(1)} %get-tuple-element.53), channel_id=1, source_target_pairs={{0,4},{1,5},{2,0},{3,1},{4,8},{5,9},{6,2},{7,3},{8,12},{9,13},{10,... | collective-permute-start | bytes 393224 | tf_op jit(solution)/shard_map/ppermute | solution.py:59
  24.7 6.5 %collective-permute-start.6 = (bf16[4,32,512]{2,1,0:T(8,128)(2,1)S(1)}, bf16[4,32,512]{2,1,0:T(8,128)(2,1)S(1)}, u32[]{:S(2)}, u32[]{:S(2)}) collective-permute-start(bf16[4,32,512]{2,1,0:T(8,128)(2,1)S(1)} %get-tuple-element.54), channel_id=1, source_target_pairs={{0,2},{1,3},{2,6},{3,7},{4,0},{5,1},{6,10},{7,11},{8,4},{9,5},{10,... | collective-permute-start | bytes 393224 | tf_op jit(solution)/shard_map/ppermute | solution.py:59
  29.1 6.4 %collective-permute-start.3 = (bf16[4,32,512]{2,1,0:T(8,128)(2,1)S(1)}, bf16[4,32,512]{2,1,0:T(8,128)(2,1)S(1)}, u32[]{:S(2)}, u32[]{:S(2)}) collective-permute-start(bf16[4,32,512]{2,1,0:T(8,128)(2,1)S(1)} %get-tuple-element.51.token), channel_id=1, source_target_pairs={{0,4},{1,5},{2,0},{3,1},{4,8},{5,9},{6,2},{7,3},{8,12},{9,13},{10,... | collective-permute-start | bytes 393224 | tf_op jit(solution)/shard_map/ppermute | solution.py:59
  30.8 5.0 %collective-permute-start.4 = (bf16[4,32,512]{2,1,0:T(8,128)(2,1)S(1)}, bf16[4,32,512]{2,1,0:T(8,128)(2,1)S(1)}, u32[]{:S(2)}, u32[]{:S(2)}) collective-permute-start(bf16[4,32,512]{2,1,0:T(8,128)(2,1)S(1)} %get-tuple-element.52), channel_id=1, source_target_pairs={{0,2},{1,3},{2,6},{3,7},{4,0},{5,1},{6,10},{7,11},{8,4},{9,5},{10,... | collective-permute-start | bytes 393224 | tf_op jit(solution)/shard_map/ppermute | solution.py:59
  31.3 6.8 %collective-permute-start.10 = (bf16[4,32,512]{2,1,0:T(8,128)(2,1)S(1)}, bf16[4,32,512]{2,1,0:T(8,128)(2,1)S(1)}, u32[]{:S(2)}, u32[]{:S(2)}) collective-permute-start(bf16[4,32,512]{2,1,0:T(8,128)(2,1)S(1)} %get-tuple-element.58), channel_id=1, source_target_pairs={{0,2},{1,3},{2,6},{3,7},{4,0},{5,1},{6,10},{7,11},{8,4},{9,5},{10,... | collective-permute-start | bytes 393224 | tf_op jit(solution)/shard_map/ppermute | solution.py:59
  31.8 6.6 %collective-permute-start.9 = (bf16[4,32,512]{2,1,0:T(8,128)(2,1)S(1)}, bf16[4,32,512]{2,1,0:T(8,128)(2,1)S(1)}, u32[]{:S(2)}, u32[]{:S(2)}) collective-permute-start(bf16[4,32,512]{2,1,0:T(8,128)(2,1)S(1)} %get-tuple-element.55.token), channel_id=1, source_target_pairs={{0,4},{1,5},{2,0},{3,1},{4,8},{5,9},{6,2},{7,3},{8,12},{9,13},{10,... | collective-permute-start | bytes 393224 | tf_op jit(solution)/shard_map/ppermute | solution.py:59
  35.8 5.4 %collective-permute-start.7 = (bf16[4,32,512]{2,1,0:T(8,128)(2,1)S(1)}, bf16[4,32,512]{2,1,0:T(8,128)(2,1)S(1)}, u32[]{:S(2)}, u32[]{:S(2)}) collective-permute-start(bf16[4,32,512]{2,1,0:T(8,128)(2,1)S(1)} %get-tuple-element.56.token), channel_id=1, source_target_pairs={{0,4},{1,5},{2,0},{3,1},{4,8},{5,9},{6,2},{7,3},{8,12},{9,13},{10,... | collective-permute-start | bytes 393224 | tf_op jit(solution)/shard_map/ppermute | solution.py:59
  37.4 5.0 %collective-permute-start.8 = (bf16[4,32,512]{2,1,0:T(8,128)(2,1)S(1)}, bf16[4,32,512]{2,1,0:T(8,128)(2,1)S(1)}, u32[]{:S(2)}, u32[]{:S(2)}) collective-permute-start(bf16[4,32,512]{2,1,0:T(8,128)(2,1)S(1)} %get-tuple-element.57), channel_id=1, source_target_pairs={{0,2},{1,3},{2,6},{3,7},{4,0},{5,1},{6,10},{7,11},{8,4},{9,5},{10,... | collective-permute-start | bytes 393224 | tf_op jit(solution)/shard_map/ppermute | solution.py:59
  38.4 6.1 %collective-permute-start.13 = (bf16[4,32,512]{2,1,0:T(8,128)(2,1)S(1)}, bf16[4,32,512]{2,1,0:T(8,128)(2,1)S(1)}, u32[]{:S(2)}, u32[]{:S(2)}) collective-permute-start(bf16[4,32,512]{2,1,0:T(8,128)(2,1)S(1)} %get-tuple-element.59.token), channel_id=1, source_target_pairs={{0,4},{1,5},{2,0},{3,1},{4,8},{5,9},{6,2},{7,3},{8,12},{9,13},{10,... | collective-permute-start | bytes 393224 | tf_op jit(solution)/shard_map/ppermute | solution.py:59
  40.0 5.2 %collective-permute-start.14 = (bf16[4,32,512]{2,1,0:T(8,128)(2,1)S(1)}, bf16[4,32,512]{2,1,0:T(8,128)(2,1)S(1)}, u32[]{:S(2)}, u32[]{:S(2)}) collective-permute-start(bf16[4,32,512]{2,1,0:T(8,128)(2,1)S(1)} %get-tuple-element.62), channel_id=1, source_target_pairs={{0,2},{1,3},{2,6},{3,7},{4,0},{5,1},{6,10},{7,11},{8,4},{9,5},{10,... | collective-permute-start | bytes 393224 | tf_op jit(solution)/shard_map/ppermute | solution.py:59
  42.4 5.0 %collective-permute-start.11 = (bf16[4,32,512]{2,1,0:T(8,128)(2,1)S(1)}, bf16[4,32,512]{2,1,0:T(8,128)(2,1)S(1)}, u32[]{:S(2)}, u32[]{:S(2)}) collective-permute-start(bf16[4,32,512]{2,1,0:T(8,128)(2,1)S(1)} %get-tuple-element.60), channel_id=1, source_target_pairs={{0,4},{1,5},{2,0},{3,1},{4,8},{5,9},{6,2},{7,3},{8,12},{9,13},{10,... | collective-permute-start | bytes 393224 | tf_op jit(solution)/shard_map/ppermute | solution.py:59
  44.0 5.0 %collective-permute-start.12 = (bf16[4,32,512]{2,1,0:T(8,128)(2,1)S(1)}, bf16[4,32,512]{2,1,0:T(8,128)(2,1)S(1)}, u32[]{:S(2)}, u32[]{:S(2)}) collective-permute-start(bf16[4,32,512]{2,1,0:T(8,128)(2,1)S(1)} %get-tuple-element.61), channel_id=1, source_target_pairs={{0,2},{1,3},{2,6},{3,7},{4,0},{5,1},{6,10},{7,11},{8,4},{9,5},{10,... | collective-permute-start | bytes 393224 | tf_op jit(solution)/shard_map/ppermute | solution.py:59
  50.5 6.3 %collective-permute-start.16 = (bf16[128,512]{1,0:T(8,128)(2,1)S(1)}, bf16[128,512]{1,0:T(8,128)(2,1)S(1)}, u32[]{:S(2)}, u32[]{:S(2)}) collective-permute-start(bf16[128,512]{1,0:T(8,128)(2,1)S(1)} %get-tuple-element.63.refs_0_), channel_id=1, source_target_pairs={{0,4},{1,5},{2,0},{3,1},{4,8},{5,9},{6,2},{7,3},{8,12},{9,13},{10,... | collective-permute-start | bytes 393224 | tf_op jit(solution)/shard_map/ppermute | solution.py:59
  52.0 6.4 %collective-permute-start.17 = (bf16[128,512]{1,0:T(8,128)(2,1)S(1)}, bf16[128,512]{1,0:T(8,128)(2,1)S(1)}, u32[]{:S(2)}, u32[]{:S(2)}) collective-permute-start(bf16[128,512]{1,0:T(8,128)(2,1)S(1)} %get-tuple-element.64.refs_1_), channel_id=1, source_target_pairs={{0,2},{1,3},{2,6},{3,7},{4,0},{5,1},{6,10},{7,11},{8,4},{9,5},{10,... | collective-permute-start | bytes 393224 | tf_op jit(solution)/shard_map/ppermute | solution.py:59
  52.5 8.0 %collective-permute-start.18 = (bf16[128,512]{1,0:T(8,128)(2,1)S(1)}, bf16[128,512]{1,0:T(8,128)(2,1)S(1)}, u32[]{:S(2)}, u32[]{:S(2)}) collective-permute-start(bf16[128,512]{1,0:T(8,128)(2,1)S(1)} %get-tuple-element.64.refs_1_), channel_id=1, source_target_pairs={{0,4},{1,5},{2,0},{3,1},{4,8},{5,9},{6,2},{7,3},{8,12},{9,13},{10,... | collective-permute-start | bytes 393224 | tf_op jit(solution)/shard_map/ppermute | solution.py:59
  54.1 6.9 %collective-permute-start.19 = (bf16[128,512]{1,0:T(8,128)(2,1)S(1)}, bf16[128,512]{1,0:T(8,128)(2,1)S(1)}, u32[]{:S(2)}, u32[]{:S(2)}) collective-permute-start(bf16[128,512]{1,0:T(8,128)(2,1)S(1)} %get-tuple-element.63.refs_0_), channel_id=1, source_target_pairs={{0,2},{1,3},{2,6},{3,7},{4,0},{5,1},{6,10},{7,11},{8,4},{9,5},{10,... | collective-permute-start | bytes 393224 | tf_op jit(solution)/shard_map/ppermute | solution.py:59
  58.4 6.0 %collective-permute-start.21 = (bf16[128,512]{1,0:T(8,128)(2,1)S(1)}, bf16[128,512]{1,0:T(8,128)(2,1)S(1)}, u32[]{:S(2)}, u32[]{:S(2)}) collective-permute-start(bf16[128,512]{1,0:T(8,128)(2,1)S(1)} %get-tuple-element.67.refs_2_.refs_0_), channel_id=1, source_target_pairs={{0,4},{1,5},{2,0},{3,1},{4,8},{5,9},{6,2},{7,3},{8,12},{9,13},{10,... | collective-permute-start | bytes 393224 | tf_op jit(solution)/shard_map/ppermute | solution.py:59
  59.4 5.4 %collective-permute-start.22 = (bf16[128,512]{1,0:T(8,128)(2,1)S(1)}, bf16[128,512]{1,0:T(8,128)(2,1)S(1)}, u32[]{:S(2)}, u32[]{:S(2)}) collective-permute-start(bf16[128,512]{1,0:T(8,128)(2,1)S(1)} %get-tuple-element.70.refs_3_), channel_id=1, source_target_pairs={{0,2},{1,3},{2,6},{3,7},{4,0},{5,1},{6,10},{7,11},{8,4},{9,5},{10,... | collective-permute-start | bytes 393224 | tf_op jit(solution)/shard_map/ppermute | solution.py:59
  60.9 5.9 %collective-permute-start.23 = (bf16[128,512]{1,0:T(8,128)(2,1)S(1)}, bf16[128,512]{1,0:T(8,128)(2,1)S(1)}, u32[]{:S(2)}, u32[]{:S(2)}) collective-permute-start(bf16[128,512]{1,0:T(8,128)(2,1)S(1)} %get-tuple-element.68.refs_1_), channel_id=1, source_target_pairs={{0,4},{1,5},{2,0},{3,1},{4,8},{5,9},{6,2},{7,3},{8,12},{9,13},{10,... | collective-permute-start | bytes 393224 | tf_op jit(solution)/shard_map/ppermute | solution.py:59
  61.9 5.0 %collective-permute-start.24 = (bf16[128,512]{1,0:T(8,128)(2,1)S(1)}, bf16[128,512]{1,0:T(8,128)(2,1)S(1)}, u32[]{:S(2)}, u32[]{:S(2)}) collective-permute-start(bf16[128,512]{1,0:T(8,128)(2,1)S(1)} %get-tuple-element.69.refs_2_), channel_id=1, source_target_pairs={{0,2},{1,3},{2,6},{3,7},{4,0},{5,1},{6,10},{7,11},{8,4},{9,5},{10,... | collective-permute-start | bytes 393224 | tf_op jit(solution)/shard_map/ppermute | solution.py:59
  64.8 5.4 %collective-permute-start.26 = (bf16[128,512]{1,0:T(8,128)(2,1)S(1)}, bf16[128,512]{1,0:T(8,128)(2,1)S(1)}, u32[]{:S(2)}, u32[]{:S(2)}) collective-permute-start(bf16[128,512]{1,0:T(8,128)(2,1)S(1)} %get-tuple-element.73.refs_2_.refs_0_), channel_id=1, source_target_pairs={{0,4},{1,5},{2,0},{3,1},{4,8},{5,9},{6,2},{7,3},{8,12},{9,13},{10,... | collective-permute-start | bytes 393224 | tf_op jit(solution)/shard_map/ppermute | solution.py:59
  65.4 5.3 %collective-permute-start.27 = (bf16[128,512]{1,0:T(8,128)(2,1)S(1)}, bf16[128,512]{1,0:T(8,128)(2,1)S(1)}, u32[]{:S(2)}, u32[]{:S(2)}) collective-permute-start(bf16[128,512]{1,0:T(8,128)(2,1)S(1)} %get-tuple-element.76.refs_3_), channel_id=1, source_target_pairs={{0,2},{1,3},{2,6},{3,7},{4,0},{5,1},{6,10},{7,11},{8,4},{9,5},{10,... | collective-permute-start | bytes 393224 | tf_op jit(solution)/shard_map/ppermute | solution.py:59
  66.9 5.3 %collective-permute-start.28 = (bf16[128,512]{1,0:T(8,128)(2,1)S(1)}, bf16[128,512]{1,0:T(8,128)(2,1)S(1)}, u32[]{:S(2)}, u32[]{:S(2)}) collective-permute-start(bf16[128,512]{1,0:T(8,128)(2,1)S(1)} %get-tuple-element.74.refs_1_), channel_id=1, source_target_pairs={{0,4},{1,5},{2,0},{3,1},{4,8},{5,9},{6,2},{7,3},{8,12},{9,13},{10,... | collective-permute-start | bytes 393224 | tf_op jit(solution)/shard_map/ppermute | solution.py:59
  68.3 5.0 %collective-permute-start.29 = (bf16[128,512]{1,0:T(8,128)(2,1)S(1)}, bf16[128,512]{1,0:T(8,128)(2,1)S(1)}, u32[]{:S(2)}, u32[]{:S(2)}) collective-permute-start(bf16[128,512]{1,0:T(8,128)(2,1)S(1)} %get-tuple-element.75.refs_2_), channel_id=1, source_target_pairs={{0,2},{1,3},{2,6},{3,7},{4,0},{5,1},{6,10},{7,11},{8,4},{9,5},{10,... | collective-permute-start | bytes 393224 | tf_op jit(solution)/shard_map/ppermute | solution.py:59
  68.9 11.4 %collective-permute-start.20 = (bf16[8,32,512]{2,1,0:T(8,128)(2,1)S(1)}, bf16[8,32,512]{2,1,0:T(8,128)(2,1)S(1)}, u32[]{:S(2)}, u32[]{:S(2)}) collective-permute-start(bf16[8,32,512]{2,1,0:T(8,128)(2,1)S(1)} %get-tuple-element.72), channel_id=1, source_target_pairs={{0,1},{1,0},{2,3},{3,2},{4,5},{5,4},{6,7},{7,6},{8,9},{9,8},{10,11... | collective-permute-start | bytes 786440 | tf_op jit(solution)/shard_map/ppermute | solution.py:50
  70.2 10.0 %collective-permute-start.25 = (bf16[8,32,512]{2,1,0:T(8,128)(2,1)}, bf16[8,32,512]{2,1,0:T(8,128)(2,1)S(1)}, u32[]{:S(2)}, u32[]{:S(2)}) collective-permute-start(bf16[8,32,512]{2,1,0:T(8,128)(2,1)} %get-tuple-element.78), channel_id=1, source_target_pairs={{0,1},{1,0},{2,3},{3,2},{4,5},{5,4},{6,7},{7,6},{8,9},{9,8},{10,11... | collective-permute-start | bytes 786440 | tf_op jit(solution)/shard_map/ppermute | solution.py:50
  70.8 5.5 %collective-permute-start.31 = (bf16[128,512]{1,0:T(8,128)(2,1)S(1)}, bf16[128,512]{1,0:T(8,128)(2,1)S(1)}, u32[]{:S(2)}, u32[]{:S(2)}) collective-permute-start(bf16[128,512]{1,0:T(8,128)(2,1)S(1)} %get-tuple-element.79.refs_2_.refs_0_), channel_id=1, source_target_pairs={{0,4},{1,5},{2,0},{3,1},{4,8},{5,9},{6,2},{7,3},{8,12},{9,13},{10,... | collective-permute-start | bytes 393224 | tf_op jit(solution)/shard_map/ppermute | solution.py:59
  72.1 5.2 %collective-permute-start.32 = (bf16[128,512]{1,0:T(8,128)(2,1)S(1)}, bf16[128,512]{1,0:T(8,128)(2,1)S(1)}, u32[]{:S(2)}, u32[]{:S(2)}) collective-permute-start(bf16[128,512]{1,0:T(8,128)(2,1)S(1)} %get-tuple-element.82.refs_3_), channel_id=1, source_target_pairs={{0,2},{1,3},{2,6},{3,7},{4,0},{5,1},{6,10},{7,11},{8,4},{9,5},{10,... | collective-permute-start | bytes 393224 | tf_op jit(solution)/shard_map/ppermute | solution.py:59
  74.6 5.7 %collective-permute-start.30 = (bf16[8,32,512]{2,1,0:T(8,128)(2,1)}, bf16[8,32,512]{2,1,0:T(8,128)(2,1)S(1)}, u32[]{:S(2)}, u32[]{:S(2)}) collective-permute-start(bf16[8,32,512]{2,1,0:T(8,128)(2,1)} %get-tuple-element.84), channel_id=1, source_target_pairs={{0,1},{1,0},{2,3},{3,2},{4,5},{5,4},{6,7},{7,6},{8,9},{9,8},{10,11... | collective-permute-start | bytes 786440 | tf_op jit(solution)/shard_map/ppermute | solution.py:50
  76.2 4.0 %collective-permute-start.15 = (bf16[4,32,512]{2,1,0:T(8,128)(2,1)S(1)}, bf16[4,32,512]{2,1,0:T(8,128)(2,1)S(1)}, u32[]{:S(2)}, u32[]{:S(2)}) collective-permute-start(bf16[4,32,512]{2,1,0:T(8,128)(2,1)S(1)} %get-tuple-element.66), channel_id=1, source_target_pairs={{0,1},{1,0},{2,3},{3,2},{4,5},{5,4},{6,7},{7,6},{8,9},{9,8},{10,11... | collective-permute-start | bytes 393224 | tf_op jit(solution)/shard_map/ppermute | solution.py:50
  (11 other events, 57.4 us)

commit v6 on v5

--- a/solution.py
+++ b/solution.py
@@ -82,48 +82,56 @@
         slot = split(block * list_len + k, ring.n_band)[0]
         return (across * ring.chips + ahead) * slots + slot, tile
 
-    spare = kept_ref.shape[0] - 1
-    for b in range(per_step):
-        block = step * per_step + b
-        rows = slice(b * block_rows, (b + 1) * block_rows)
+    def embedded(rows):
         first = lax.dot_general(
             x_ref[:, rows], w1_ref[...], (((0,), (0,)), ((), ())), preferred_element_type=F32
         )
-        before = jnp.dot(silu(first).astype(BF16), w2_ref[...], preferred_element_type=F32)
-        latent = layer_norm(before, gain_ref[...]).astype(BF16)
-        start = pl.multiple_of(block * block_rows, block_rows)
-        latent_ref[pl.ds(start, block_rows)] = latent
-        weights = interp_ref[b].reshape(list_len * tile_rows, block_rows)
-        part = jnp.dot(weights, latent, preferred_element_type=F32)
-        for k in range(list_len):
-            place, tile = spot(me, b, k)
-            there, its_tile = spot(me ^ 1, b, k)
-            mask = mask_ref[k, me * blk_count + block]
-            table_ref[0, place] = tile
-            table_ref[1, there] = its_tile
-            table_ref[2, place] = mask
-            table_ref[3, there] = mask_ref[k, (me ^ 1) * blk_count + block]
-            masked = part[k * tile_rows : (k + 1) * tile_rows] * mask.astype(F32)
-            masked = masked.astype(BF16)
-            kept_ref[jnp.minimum(place, spare)] = masked
-            sent_ref[jnp.where(place >= spare, place - spare, spare)] = masked
-
-
-def add_entries(total, table_ref, owner, kept, other, chips):
-    slots = kept.shape[0]
+        return jnp.dot(silu(first).astype(BF16), w2_ref[...], preferred_element_type=F32)
+
+    spare = kept_ref.shape[0] - 1
+    parts = 2
+    part_rows = latent_ref.shape[0] // parts
+    spans = [slice(i * part_rows, (i + 1) * part_rows) for i in range(parts)]
+    befores = [embedded(rows) for rows in spans]
+    for number, rows in enumerate(spans):
+        latent = layer_norm(befores[number], gain_ref[...]).astype(BF16)
+        latent_ref[rows] = latent
+        for i in range(per_step // parts):
+            b = number * (per_step // parts) + i
+            block = step * per_step + b
+            weights = interp_ref[b].reshape(list_len * tile_rows, block_rows)
+            part = jnp.dot(
+                weights, latent[i * block_rows : (i + 1) * block_rows], preferred_element_type=F32
+            )
+            for k in range(list_len):
+                place, tile = spot(me, b, k)
+                there, its_tile = spot(me ^ 1, b, k)
+                mask = mask_ref[k, me * blk_count + block]
+                table_ref[0, place] = tile
+                table_ref[1, there] = its_tile
+                table_ref[2, place] = mask
+                table_ref[3, there] = mask_ref[k, (me ^ 1) * blk_count + block]
+                table_ref[4, block * list_len + k] = place
+                masked = part[k * tile_rows : (k + 1) * tile_rows] * mask.astype(F32)
+                masked = masked.astype(BF16)
+                kept_ref[jnp.minimum(place, spare)] = masked
+                sent_ref[jnp.where(place >= spare, place - spare, spare)] = masked
+
+
+def add_entries(total, table_ref, owner, slots, kept, other, chips):
     for slot in range(slots):
-        total[table_ref[0, owner * slots + slot]] += kept[slot].astype(F32)
-        total[table_ref[1, (chips + owner) * slots + slot]] += other[slot].astype(F32)
-
-
-def far_kernel(ring, table_ref, *refs):
-    kept, other = refs[0:3], refs[3:6]
-    far_right, far_left, next_right, next_left, total = refs[6:]
+        place = owner * slots + slot
+        total[table_ref[0, place]] += kept[place].astype(F32)
+        total[table_ref[1, chips * slots + place]] += other[place].astype(F32)
+
+
+def far_kernel(
+    ring, slots, table_ref, kept, other, far_right, far_left, next_right, next_left, total
+):
     half = total.shape[0] // 2
-    owners = (ring.far, ring.far - 1, ring.chips - ring.far + 1)
-    for number, owner in enumerate(owners):
+    for number, owner in enumerate((ring.far, ring.far - 1, ring.chips - ring.far + 1)):
         total[...] = jnp.zeros_like(total)
-        add_entries(total, table_ref, owner, kept[number], other[number], ring.chips)
+        add_entries(total, table_ref, owner, slots, kept, other, ring.chips)
         if number == 0:
             far_right[...] = total[:half].astype(BF16)
             far_left[...] = total[half:].astype(BF16)
@@ -133,11 +141,12 @@
             next_left[...] = total[:half].astype(BF16)
 
 
-def own_kernel(ring, table_ref, kept, other, own):
+def own_kernel(ring, slots, table_ref, kept, other, own):
     number = pl.program_id(0)
     owner = number + (number >= ring.far).astype(jnp.int32)
-    own[...] = jnp.zeros_like(own)
-    add_entries(own.at[0], table_ref, owner, kept, other, ring.chips)
+    total = own.at[owner]
+    total[...] = jnp.zeros_like(total)
+    add_entries(total, table_ref, owner, slots, kept, other, ring.chips)
 
 
 def mesh_kernel(
@@ -158,10 +167,11 @@
     out_b[...] = out[half * tile_rows :]
 
 
-def add_kernel(own_right, own_left, right, left, token, out_right, out_left):
+def add_kernel(owner, part, own, came, token, out):
     del token
-    out_right[...] = (own_right[0] + right[...].astype(F32)).astype(BF16)
-    out_left[...] = (own_left[0] + left[...].astype(F32)).astype(BF16)
+    count = out.shape[0]
+    mine = own[owner, part * count : (part + 1) * count]
+    out[...] = (mine + came[...].astype(F32)).astype(BF16)
 
 
 def order_kernel(*refs):
@@ -181,18 +191,15 @@
                 above = tile >= count
                 within = jnp.where(above, tile - count, tile)
                 rows = pl.ds(pl.multiple_of(within * tile_rows, tile_rows), tile_rows)
-                value = jnp.where(above, upper[rows], lower[rows]).astype(F32)
-                out[number * slots + slot] = (value * mask.astype(F32)).astype(BF16)
-
-
-def back_kernel(ring, places, slots, per_step, me_ref, lists_ref, latent_ref, weights_ref, *rest):
+                value = jnp.where(above, upper[rows], lower[rows])
+                out[number * slots + slot] = jnp.where(mask == 1, value, jnp.zeros_like(value))
+
+
+def back_kernel(places, slots, list_len, per_step, table_ref, latent_ref, weights_ref, *rest):
     count = len(places)
     pieces, (out_ref, held, sems) = rest[:count], rest[count:]
     step = pl.program_id(0)
-    me = me_ref[0]
     block_rows = weights_ref.shape[1]
-    list_len = lists_ref.shape[0]
-    tile_rows, width = held.shape[1:]
 
     @pl.when(step == 0)
     def _():
@@ -212,19 +219,11 @@
             copy.wait()
 
     for b in range(per_step):
-        number = step * per_step + b
-        values = []
-        for k in range(list_len):
-            ahead, across, _ = ring.entry(
-                lists_ref, me, me * pl.num_programs(0) * per_step + number, k
-            )
-            slot = split(number * list_len + k, ring.n_band)[0]
-            values.append(held[(across * ring.chips + ahead) * slots + slot])
-        value = jnp.concatenate(values, axis=0)
-        back = jnp.dot(weights_ref[number], value, preferred_element_type=F32)
-        start = pl.multiple_of(number * block_rows, block_rows)
-        total = latent_ref[pl.ds(start, block_rows)].astype(F32) + back
-        out_ref[b * block_rows : (b + 1) * block_rows] = total.astype(BF16)
+        first = (step * per_step + b) * list_len
+        value = jnp.concatenate([held[table_ref[4, first + k]] for k in range(list_len)], axis=0)
+        back = jnp.dot(weights_ref[b], value, preferred_element_type=F32)
+        rows = slice(b * block_rows, (b + 1) * block_rows)
+        out_ref[rows] = (latent_ref[rows].astype(F32) + back).astype(BF16)
 
 
 def whole(array):
@@ -282,7 +281,7 @@
         functools.partial(embed_kernel, ring, per_step, slots),
         out_shape=[shape((blk_count * block_rows, width))]
         + [shape(held_shape)] * N_CORE
-        + [shape((4, entries), jnp.int32)],
+        + [shape((5, entries), jnp.int32)],
         grid_spec=pltpu.PrefetchScalarGridSpec(
             num_scalar_prefetch=3,
             grid=(blk_count // per_step,),
@@ -293,7 +292,8 @@
                 whole(gain),
                 pl.BlockSpec((per_step,) + interp.shape[1:], lambda i, *_: (i, 0, 0, 0)),
             ],
-            out_specs=[pl.BlockSpec(memory_space=pltpu.VMEM)] * (1 + N_CORE)
+            out_specs=[pl.BlockSpec((rows, width), lambda i, *_: (i, 0))]
+            + [pl.BlockSpec(memory_space=pltpu.VMEM)] * N_CORE
             + [pl.BlockSpec(memory_space=pltpu.SMEM)],
         ),
         compiler_params=params(24),
@@ -303,92 +303,78 @@
             interp,
         ),
         name="embed",
-    )(*lists, *map(in_hbm, (grid_features.T, embed_in, embed_out, gain, interp)))
+    )(lists[0], *map(in_hbm, lists[1:] + (grid_features.T, embed_in, embed_out, gain, interp)))
     other = ring.over_core(sent)
 
     dense = (tiles, tile_rows, width)
     half_dense = (half_tiles, tile_rows, width)
 
-    def entries_of(owner):
-        return pl.BlockSpec((slots, tile_rows, width), lambda i, _: (owner, 0, 0))
-
-    near = [entries_of(owner) for owner in (far, far - 1, chips - far + 1)]
+    in_vmem = pl.BlockSpec(memory_space=pltpu.VMEM)
     far_right, far_left, next_right, next_left = pl.pallas_call(
-        functools.partial(far_kernel, ring),
+        functools.partial(far_kernel, ring, slots),
         out_shape=[shape(half_dense)] * 4,
         grid_spec=pltpu.PrefetchScalarGridSpec(
             num_scalar_prefetch=1,
             grid=(1,),
-            in_specs=near + near,
-            out_specs=[pl.BlockSpec(half_dense, lambda i, _: (0, 0, 0))] * 4,
+            in_specs=[in_vmem] * 2,
+            out_specs=[in_vmem] * 4,
             scratch_shapes=[pltpu.VMEM(dense, F32)],
         ),
         compiler_params=params(8),
         cost_estimate=cost(0, kept),
         name="far_chunks",
-    )(table, *[kept] * 3, *[other] * 3)
-
-    def skip_far(i):
-        return i + (i >= far).astype(jnp.int32)
-
-    per_owner = pl.BlockSpec((slots, tile_rows, width), lambda i, _: (skip_far(i), 0, 0))
+    )(table, kept, other)
     own = pl.pallas_call(
-        functools.partial(own_kernel, ring),
+        functools.partial(own_kernel, ring, slots),
         out_shape=shape((chips,) + dense, F32),
         grid_spec=pltpu.PrefetchScalarGridSpec(
             num_scalar_prefetch=1,
             grid=(chips - 1,),
-            in_specs=[per_owner] * 2,
-            out_specs=pl.BlockSpec((1,) + dense, lambda i, _: (skip_far(i), 0, 0, 0)),
-        ),
-        compiler_params=params(8),
+            in_specs=[in_vmem] * 2,
+            out_specs=in_vmem,
+        ),
+        compiler_params=params(8 if n_band <= 16 else 24),
         cost_estimate=cost(0, kept, kept, kept, kept),
         name="own_chunks",
     )(table, kept, other)
 
     lower, upper = 0, 1
 
-    def half_of(owner, part):
-        return pl.BlockSpec((1,) + half_dense, lambda i: (owner % chips, part, 0, 0))
-
-    def add_own(distance, parts, values, token):
-        sums = pl.pallas_call(
-            add_kernel,
-            out_shape=[shape(half_dense)] * 2,
-            grid=(1,),
-            in_specs=[half_of(distance, parts[0]), half_of(-distance, parts[1])]
-            + [whole(v) for v in values]
-            + [pl.BlockSpec(memory_space=pl.ANY)],
-            out_specs=[pl.BlockSpec(half_dense, lambda i: (0, 0, 0))] * 2,
+    def add_own(distance, part, value, token):
+        return pl.pallas_call(
+            functools.partial(add_kernel, distance % chips, part),
+            out_shape=shape(half_dense),
+            in_specs=[in_vmem] * 2 + [pl.BlockSpec(memory_space=pl.ANY)],
+            out_specs=in_vmem,
             compiler_params=params(8),
-            cost_estimate=cost(0, *values, *values),
-            name=f"add_{distance}{'ab'[parts[0]]}",
-        )(own, own, *values, token)
-        return sums, sums[0]
+            cost_estimate=cost(0, value, value),
+            name=f"add_{'lr'[distance > 0]}{abs(distance)}{'ab'[part]}",
+        )(own, value, token)
 
     def both(values):
         return [ring.over(values[0], 1), ring.over(values[1], -1)]
+
+    def both_with_own(distance, parts, values, token):
+        sent = []
+        for way, part, value in zip((1, -1), parts, values):
+            token = add_own(way * distance, part, value, token)
+            sent.append(ring.over(token, way))
+        return sent, token
 
     first, second = both((far_right, far_left)), both((next_right, next_left))
     token = own
     for distance in range(far - 1, 0, -1):
-        sums, token = add_own(distance, (lower, upper), first, token)
-        first = both(sums)
+        first, token = both_with_own(distance, (lower, upper), first, token)
         if distance > 1:
-            sums, token = add_own(distance - 1, (upper, lower), second, token)
-            second = both(sums)
+            second, token = both_with_own(distance - 1, (upper, lower), second, token)
 
     mesh_gain = mesh_gain.reshape(1, width)
     came = (*first, *second)
     mesh_out, out_a, out_b = pl.pallas_call(
         mesh_kernel,
         out_shape=[shape((node_rows, width))] + [shape((half_rows, width))] * 2,
-        grid=(1,),
-        in_specs=[whole(a) for a in (mesh_latent, mesh_up, mesh_down, mesh_gain)]
-        + [pl.BlockSpec((1,) + dense, lambda i: (0, 0, 0, 0))]
-        + [whole(c) for c in came],
-        out_specs=[pl.BlockSpec((node_rows, width), lambda i: (0, 0))]
-        + [pl.BlockSpec((half_rows, width), lambda i: (0, 0))] * 2,
+        in_specs=[in_vmem] * 9,
+        out_specs=[in_vmem] * 3,
         compiler_params=params(16),
         cost_estimate=cost(4 * node_rows * width * width, mesh_up, mesh_down),
         name="mesh_step",
@@ -417,8 +403,8 @@
             grid_spec=pltpu.PrefetchScalarGridSpec(
                 num_scalar_prefetch=1,
                 grid=(1,),
-                in_specs=[whole(h) for h in halves],
-                out_specs=[whole(out)] * 2,
+                in_specs=[in_vmem] * len(halves),
+                out_specs=[in_vmem] * 2,
             ),
             compiler_params=params(8),
             cost_estimate=cost(0, *halves),
@@ -445,12 +431,15 @@
     per_step = 4
     rows = per_step * block_rows
     grid_out = pl.pallas_call(
-        functools.partial(back_kernel, ring, places, slots, per_step),
+        functools.partial(back_kernel, places, slots, list_len, per_step),
         out_shape=shape((blk_count * block_rows, width)),
         grid_spec=pltpu.PrefetchScalarGridSpec(
-            num_scalar_prefetch=2,
+            num_scalar_prefetch=1,
             grid=(blk_count // per_step,),
-            in_specs=[pl.BlockSpec(memory_space=pltpu.VMEM)] * 2
+            in_specs=[
+                pl.BlockSpec((rows, width), lambda i, *_: (i, 0)),
+                pl.BlockSpec((per_step,) + weights.shape[1:], lambda i, *_: (i, 0, 0)),
+            ]
             + [pl.BlockSpec(memory_space=pl.ANY)] * len(pieces),
             out_specs=pl.BlockSpec((rows, width), lambda i, *_: (i, 0)),
             scratch_shapes=[
@@ -463,7 +452,7 @@
             2 * blk_count * block_rows * width * list_len * tile_rows, latent, latent, interp
         ),
         name="back",
-    )(*lists[:2], latent, weights, *pieces)
+    )(table, latent, weights, *pieces)
     return (grid_out, mesh_out)
 
 

time: 90.1 us -> 86.5 us (0.960)
  Pallas kernels: 30.3 us -> 26.8 us
  waiting for transfers between devices: 22.3 us -> 21.2 us
    pallas_call x1, Pallas kernels: 13.9 us -> 10.3 us  [on_device(): pl.pallas_call(functools.partial(embed_kernel, ring, per_step, slots), ou...]
    ppermute x28, waiting for transfers between devices: 19.9 us -> 18.8 us  [over(): return lax.ppermute(value, 'band', pairs)]
    unnamed x18 -> x12, local copies, waits for them, and re-layouts: 3.58 us -> 4.22 us
    pallas_call x8 -> x13, Pallas kernels: 9.73 us -> 9.73 us  [the longest x1 7.22 us: on_device(): pl.pallas_call(functools.partial(back_kernel, places, slots, list_len, pe...]
  transfers between devices with their start and end apart: 34 -> 34, of which waited for: 19 -> 20; matrix products, arithmetic and copies ran while one was open for 2% -> 2% of each run, Pallas kernels for 8% -> 8%
where the time goes in v6:
time: 86.5 us; the launch traced here: 86.2 us
  starting transfers between devices  31.5 us (36%)
  Pallas kernels  26.8 us (31%)
  waiting for transfers between devices  21.2 us (25%)
  local copies, waits for them, and re-layouts  5.83 us (7%)
  between operations  0.88 us (1%)
    ppermute x28, starting transfers between devices, over(): return lax.ppermute(value, 'band', pairs)  30.5 us
    ppermute x28, waiting for transfers between devices, over(): return lax.ppermute(value, 'band', pairs)  18.8 us
    pallas_call x1, Pallas kernels, on_device(): pl.pallas_call(functools.partial(embed_kernel, ring, per_step, slots), ou...  10.3 us
    pallas_call x1, Pallas kernels, on_device(): pl.pallas_call(functools.partial(back_kernel, places, slots, list_len, pe...  7.22 us
    pallas_call x5, Pallas kernels, pick(): pl.pallas_call(functools.partial(pick_kernel, owners, slots, chips), out_...  5.35 us
    unnamed x12, local copies, waits for them, and re-layouts  4.22 us
    ppermute x6, waiting for transfers between devices, over_core(): return lax.ppermute(value, 'band', [(i, i ^ 1) for i in range(self.n_band)])  2.35 us
  transfers between devices with their start and end apart: 34, of which 20 were waited for; matrix products, arithmetic and copies ran while one was open for 2% of the time, Pallas kernels for 8%

profile of v6, /device:TPU:0, one launch (start us, length us, event | category | flops | bytes accessed | tf_op | source)
XLA Modules:
  0.0 86.2 jit_solution(18128925418942638515)
XLA Ops:
  0.6 10.3 %embed.1 = (bf16[4096,512]{1,0:T(8,128)(2,1)S(1)}, bf16[33,32,512]{2,1,0:T(8,128)(2,1)S(1)}, bf16[33,32,512]{2,1,0:T(8,128)(2,1)S(1)}, s32[5,64]{1,0:T(8,128)S(1)}) custom-call(s32[1]{0:T(128)} %bitcast.me_ref, s32[4,256]{1,0:T(4,128)} %bitcast.12, s32[4,256]{1,0:T(4,128)} %bitcast.13, bf16[227,4096]{1,0:T(8,128)(2,1)} %bitcast.11, bf16[227,512]{1,0:T(8,128)(2,1)} %w1_ref.1, ...), custom_call_target="tpu_custom_call" | custom-call | flops 3636461568 | bytes 2908160 | tf_op jit(solution)/shard_map/embed/pallas_call | solution.py:280
  11.0 2.0 %copy-done = bf16[4096,512]{1,0:T(8,128)(2,1)} copy-done((bf16[4096,512]{1,0:T(8,128)(2,1)}, bf16[4096,512]{1,0:T(8,128)(2,1)S(1)}, u32[]{:S(2)}) %copy-start) | copy-done | bytes 4194328
  13.4 2.3 %collective-permute-done.other = bf16[33,32,512]{2,1,0:T(8,128)(2,1)S(1)} collective-permute-done((bf16[33,32,512]{2,1,0:T(8,128)(2,1)S(1)}, bf16[33,32,512]{2,1,0:T(8,128)(2,1)S(1)}, u32[]{:S(2)}, u32[]{:S(2)}) %collective-permute-start) | collective-permute-done | bytes 1081376 | tf_op jit(solution)/shard_map/ppermute | solution.py:50
  16.7 3.0 %collective-permute-start.1 = (bf16[4,32,512]{2,1,0:T(8,128)(2,1)S(1)}, bf16[4,32,512]{2,1,0:T(8,128)(2,1)S(1)}, u32[]{:S(2)}, u32[]{:S(2)}) collective-permute-start(bf16[4,32,512]{2,1,0:T(8,128)(2,1)S(1)} %get-tuple-element.39), channel_id=1, source_target_pairs={{0,4},{1,5},{2,0},{3,1},{4,8},{5,9},{6,2},{7,3},{8,12},{9,13},{10,... | collective-permute-start | bytes 393224 | tf_op jit(solution)/shard_map/ppermute | solution.py:59
  19.7 2.0 %collective-permute-start.4 = (bf16[4,32,512]{2,1,0:T(8,128)(2,1)S(1)}, bf16[4,32,512]{2,1,0:T(8,128)(2,1)S(1)}, u32[]{:S(2)}, u32[]{:S(2)}) collective-permute-start(bf16[4,32,512]{2,1,0:T(8,128)(2,1)S(1)} %get-tuple-element.41), channel_id=1, source_target_pairs={{0,4},{1,5},{2,0},{3,1},{4,8},{5,9},{6,2},{7,3},{8,12},{9,13},{10,... | collective-permute-start | bytes 393224 | tf_op jit(solution)/shard_map/ppermute | solution.py:59
  21.7 1.3 %own_chunks.1.own.token = f32[8,8,32,512]{3,2,1,0:T(8,128)S(1)} custom-call(s32[5,64]{1,0:T(8,128)S(1)} %get-tuple-element.35.table_ref, bf16[33,32,512]{2,1,0:T(8,128)(2,1)S(1)} %get-tuple-element.37.kept, bf16[33,32,512]{2,1,0:T(8,128)(2,1)S(1)} %collective-permute-done.other), custom_call_target="tpu_custom_call" | custom-call | bytes 4325376 | tf_op jit(solution)/shard_map/own_chunks/pallas_call | solution.py:327
  23.9 2.2 %collective-permute-start.2 = (bf16[4,32,512]{2,1,0:T(8,128)(2,1)S(1)}, bf16[4,32,512]{2,1,0:T(8,128)(2,1)S(1)}, u32[]{:S(2)}, u32[]{:S(2)}) collective-permute-start(bf16[4,32,512]{2,1,0:T(8,128)(2,1)S(1)} %add_r3a.1.token), channel_id=1, source_target_pairs={{0,4},{1,5},{2,0},{3,1},{4,8},{5,9},{6,2},{7,3},{8,12},{9,13},{10,... | collective-permute-start | bytes 393224 | tf_op jit(solution)/shard_map/ppermute | solution.py:59
  26.7 2.2 %collective-permute-start.8 = (bf16[4,32,512]{2,1,0:T(8,128)(2,1)S(1)}, bf16[4,32,512]{2,1,0:T(8,128)(2,1)S(1)}, u32[]{:S(2)}, u32[]{:S(2)}) collective-permute-start(bf16[4,32,512]{2,1,0:T(8,128)(2,1)S(1)} %add_r2b.1.token), channel_id=1, source_target_pairs={{0,4},{1,5},{2,0},{3,1},{4,8},{5,9},{6,2},{7,3},{8,12},{9,13},{10,... | collective-permute-start | bytes 393224 | tf_op jit(solution)/shard_map/ppermute | solution.py:59
  29.7 2.5 %collective-permute-start.6 = (bf16[4,32,512]{2,1,0:T(8,128)(2,1)S(1)}, bf16[4,32,512]{2,1,0:T(8,128)(2,1)S(1)}, u32[]{:S(2)}, u32[]{:S(2)}) collective-permute-start(bf16[4,32,512]{2,1,0:T(8,128)(2,1)S(1)} %add_r2a.1.token), channel_id=1, source_target_pairs={{0,4},{1,5},{2,0},{3,1},{4,8},{5,9},{6,2},{7,3},{8,12},{9,13},{10,... | collective-permute-start | bytes 393224 | tf_op jit(solution)/shard_map/ppermute | solution.py:59
  33.3 2.1 %collective-permute-start.13 = (bf16[4,32,512]{2,1,0:T(8,128)(2,1)S(1)}, bf16[4,32,512]{2,1,0:T(8,128)(2,1)S(1)}, u32[]{:S(2)}, u32[]{:S(2)}) collective-permute-start(bf16[4,32,512]{2,1,0:T(8,128)(2,1)S(1)} %add_r1b.1.token), channel_id=1, source_target_pairs={{0,4},{1,5},{2,0},{3,1},{4,8},{5,9},{6,2},{7,3},{8,12},{9,13},{10,... | collective-permute-start | bytes 393224 | tf_op jit(solution)/shard_map/ppermute | solution.py:59
  36.1 2.1 %collective-permute-done.11.came = bf16[4,32,512]{2,1,0:T(8,128)(2,1)S(1)} collective-permute-done((bf16[4,32,512]{2,1,0:T(8,128)(2,1)S(1)}, bf16[4,32,512]{2,1,0:T(8,128)(2,1)S(1)}, u32[]{:S(2)}, u32[]{:S(2)}) %collective-permute-start.11) | collective-permute-done | bytes 131104 | tf_op jit(solution)/shard_map/ppermute | solution.py:59
  38.5 1.8 %collective-permute-start.10 = (bf16[4,32,512]{2,1,0:T(8,128)(2,1)S(1)}, bf16[4,32,512]{2,1,0:T(8,128)(2,1)S(1)}, u32[]{:S(2)}, u32[]{:S(2)}) collective-permute-start(bf16[4,32,512]{2,1,0:T(8,128)(2,1)S(1)} %add_r1a.1.token), channel_id=1, source_target_pairs={{0,4},{1,5},{2,0},{3,1},{4,8},{5,9},{6,2},{7,3},{8,12},{9,13},{10,... | collective-permute-start | bytes 393224 | tf_op jit(solution)/shard_map/ppermute | solution.py:59
  41.0 2.3 %collective-permute-done.12.left_b = bf16[4,32,512]{2,1,0:T(8,128)(2,1)S(1)} collective-permute-done((bf16[4,32,512]{2,1,0:T(8,128)(2,1)S(1)}, bf16[4,32,512]{2,1,0:T(8,128)(2,1)S(1)}, u32[]{:S(2)}, u32[]{:S(2)}) %collective-permute-start.12) | collective-permute-done | bytes 131104 | tf_op jit(solution)/shard_map/ppermute | solution.py:59
  43.5 1.5 %mesh_step.1 = (bf16[256,512]{1,0:T(8,128)(2,1)}, bf16[128,512]{1,0:T(8,128)(2,1)S(1)}, bf16[128,512]{1,0:T(8,128)(2,1)S(1)}) custom-call(bf16[256,512]{1,0:T(8,128)(2,1)S(1)} %copy-done.4, bf16[512,512]{1,0:T(8,128)(2,1)S(1)} %copy-done.2, bf16[512,512]{1,0:T(8,128)(2,1)S(1)} %copy-done.3, f32[1,512]{1,0:T(1,128)S(1)} %bitcast.9, ...), custom_call_target="tpu_custom_call" | custom-call | flops 268435456 | bytes 1048576 | tf_op jit(solution)/shard_map/mesh_step/pallas_call | solution.py:373
  45.0 1.8 %collective-permute-start.16 = (bf16[128,512]{1,0:T(8,128)(2,1)S(1)}, bf16[128,512]{1,0:T(8,128)(2,1)S(1)}, u32[]{:S(2)}, u32[]{:S(2)}) collective-permute-start(bf16[128,512]{1,0:T(8,128)(2,1)S(1)} %get-tuple-element.43.refs_0_), channel_id=1, source_target_pairs={{0,4},{1,5},{2,0},{3,1},{4,8},{5,9},{6,2},{7,3},{8,12},{9,13},{10,... | collective-permute-start | bytes 393224 | tf_op jit(solution)/shard_map/ppermute | solution.py:59
  47.0 1.8 %collective-permute-start.18 = (bf16[128,512]{1,0:T(8,128)(2,1)S(1)}, bf16[128,512]{1,0:T(8,128)(2,1)S(1)}, u32[]{:S(2)}, u32[]{:S(2)}) collective-permute-start(bf16[128,512]{1,0:T(8,128)(2,1)S(1)} %get-tuple-element.44.refs_1_), channel_id=1, source_target_pairs={{0,4},{1,5},{2,0},{3,1},{4,8},{5,9},{6,2},{7,3},{8,12},{9,13},{10,... | collective-permute-start | bytes 393224 | tf_op jit(solution)/shard_map/ppermute | solution.py:59
  50.4 2.3 %collective-permute-done.17.refs_1_ = bf16[128,512]{1,0:T(8,128)(2,1)S(1)} collective-permute-done((bf16[128,512]{1,0:T(8,128)(2,1)S(1)}, bf16[128,512]{1,0:T(8,128)(2,1)S(1)}, u32[]{:S(2)}, u32[]{:S(2)}) %collective-permute-start.17) | collective-permute-done | bytes 131104 | tf_op jit(solution)/shard_map/ppermute | solution.py:59
  52.7 1.6 %collective-permute-start.21 = (bf16[128,512]{1,0:T(8,128)(2,1)S(1)}, bf16[128,512]{1,0:T(8,128)(2,1)S(1)}, u32[]{:S(2)}, u32[]{:S(2)}) collective-permute-start(bf16[128,512]{1,0:T(8,128)(2,1)S(1)} %get-tuple-element.47.refs_2_.refs_0_), channel_id=1, source_target_pairs={{0,4},{1,5},{2,0},{3,1},{4,8},{5,9},{6,2},{7,3},{8,12},{9,13},{10,... | collective-permute-start | bytes 393224 | tf_op jit(solution)/shard_map/ppermute | solution.py:59
  55.5 1.6 %collective-permute-start.23 = (bf16[128,512]{1,0:T(8,128)(2,1)S(1)}, bf16[128,512]{1,0:T(8,128)(2,1)S(1)}, u32[]{:S(2)}, u32[]{:S(2)}) collective-permute-start(bf16[128,512]{1,0:T(8,128)(2,1)S(1)} %get-tuple-element.48.refs_1_), channel_id=1, source_target_pairs={{0,4},{1,5},{2,0},{3,1},{4,8},{5,9},{6,2},{7,3},{8,12},{9,13},{10,... | collective-permute-start | bytes 393224 | tf_op jit(solution)/shard_map/ppermute | solution.py:59
  59.1 1.5 %collective-permute-done.22.refs_1_ = bf16[128,512]{1,0:T(8,128)(2,1)S(1)} collective-permute-done((bf16[128,512]{1,0:T(8,128)(2,1)S(1)}, bf16[128,512]{1,0:T(8,128)(2,1)S(1)}, u32[]{:S(2)}, u32[]{:S(2)}) %collective-permute-start.22) | collective-permute-done | bytes 131104 | tf_op jit(solution)/shard_map/ppermute | solution.py:59
  60.6 1.1 %collective-permute-start.26 = (bf16[128,512]{1,0:T(8,128)(2,1)S(1)}, bf16[128,512]{1,0:T(8,128)(2,1)S(1)}, u32[]{:S(2)}, u32[]{:S(2)}) collective-permute-start(bf16[128,512]{1,0:T(8,128)(2,1)S(1)} %get-tuple-element.53.refs_2_.refs_0_), channel_id=1, source_target_pairs={{0,4},{1,5},{2,0},{3,1},{4,8},{5,9},{6,2},{7,3},{8,12},{9,13},{10,... | collective-permute-start | bytes 393224 | tf_op jit(solution)/shard_map/ppermute | solution.py:59
  61.7 0.9 %collective-permute-start.27 = (bf16[128,512]{1,0:T(8,128)(2,1)S(1)}, bf16[128,512]{1,0:T(8,128)(2,1)S(1)}, u32[]{:S(2)}, u32[]{:S(2)}) collective-permute-start(bf16[128,512]{1,0:T(8,128)(2,1)S(1)} %get-tuple-element.56.refs_3_), channel_id=1, source_target_pairs={{0,2},{1,3},{2,6},{3,7},{4,0},{5,1},{6,10},{7,11},{8,4},{9,5},{10,... | collective-permute-start | bytes 393224 | tf_op jit(solution)/shard_map/ppermute | solution.py:59
  63.1 1.3 %collective-permute-start.28 = (bf16[128,512]{1,0:T(8,128)(2,1)S(1)}, bf16[128,512]{1,0:T(8,128)(2,1)S(1)}, u32[]{:S(2)}, u32[]{:S(2)}) collective-permute-start(bf16[128,512]{1,0:T(8,128)(2,1)S(1)} %get-tuple-element.54.refs_1_), channel_id=1, source_target_pairs={{0,4},{1,5},{2,0},{3,1},{4,8},{5,9},{6,2},{7,3},{8,12},{9,13},{10,... | collective-permute-start | bytes 393224 | tf_op jit(solution)/shard_map/ppermute | solution.py:59
  65.1 1.4 %pick_6.1 = (bf16[8,32,512]{2,1,0:T(8,128)(2,1)S(1)}, bf16[8,32,512]{2,1,0:T(8,128)(2,1)}) custom-call(s32[5,64]{1,0:T(8,128)S(1)} %get-tuple-element.35.table_ref, bf16[128,512]{1,0:T(8,128)(2,1)S(1)} %get-tuple-element.53.refs_2_.refs_0_, bf16[128,512]{1,0:T(8,128)(2,1)S(1)} %get-tuple-element.54.refs_1_, bf16[128,512]{1,0:T(8,128)(2,1)S(1)} %get-tuple-element.55.refs_2_, ...), custom_call_target="tpu_custom_call" | custom-call | bytes 524288 | tf_op jit(solution)/shard_map/pick_6/pallas_call | solution.py:400
  67.0 1.8 %collective-permute-start.31 = (bf16[128,512]{1,0:T(8,128)(2,1)S(1)}, bf16[128,512]{1,0:T(8,128)(2,1)S(1)}, u32[]{:S(2)}, u32[]{:S(2)}) collective-permute-start(bf16[128,512]{1,0:T(8,128)(2,1)S(1)} %get-tuple-element.59.refs_2_.refs_0_), channel_id=1, source_target_pairs={{0,4},{1,5},{2,0},{3,1},{4,8},{5,9},{6,2},{7,3},{8,12},{9,13},{10,... | collective-permute-start | bytes 393224 | tf_op jit(solution)/shard_map/ppermute | solution.py:59
  69.4 1.4 %pick_5.1 = (bf16[8,32,512]{2,1,0:T(8,128)(2,1)S(1)}, bf16[8,32,512]{2,1,0:T(8,128)(2,1)}) custom-call(s32[5,64]{1,0:T(8,128)S(1)} %get-tuple-element.35.table_ref, bf16[128,512]{1,0:T(8,128)(2,1)S(1)} %get-tuple-element.59.refs_2_.refs_0_, bf16[128,512]{1,0:T(8,128)(2,1)S(1)} %get-tuple-element.60.refs_1_, bf16[128,512]{1,0:T(8,128)(2,1)S(1)} %get-tuple-element.61.refs_2_, ...), custom_call_target="tpu_custom_call" | custom-call | bytes 524288 | tf_op jit(solution)/shard_map/pick_5/pallas_call | solution.py:400
  70.8 1.7 %collective-permute-done.31.refs_0_ = bf16[128,512]{1,0:T(8,128)(2,1)S(1)} collective-permute-done((bf16[128,512]{1,0:T(8,128)(2,1)S(1)}, bf16[128,512]{1,0:T(8,128)(2,1)S(1)}, u32[]{:S(2)}, u32[]{:S(2)}) %collective-permute-start.31) | collective-permute-done | bytes 131104 | tf_op jit(solution)/shard_map/ppermute | solution.py:59
  72.5 1.3 %collective-permute-done.32.refs_1_ = bf16[128,512]{1,0:T(8,128)(2,1)S(1)} collective-permute-done((bf16[128,512]{1,0:T(8,128)(2,1)S(1)}, bf16[128,512]{1,0:T(8,128)(2,1)S(1)}, u32[]{:S(2)}, u32[]{:S(2)}) %collective-permute-start.32) | collective-permute-done | bytes 131104 | tf_op jit(solution)/shard_map/ppermute | solution.py:59
  73.8 1.3 %pick_4.1 = (bf16[4,32,512]{2,1,0:T(8,128)(2,1)S(1)}, bf16[4,32,512]{2,1,0:T(8,128)(2,1)}) custom-call(s32[5,64]{1,0:T(8,128)S(1)} %get-tuple-element.35.table_ref, bf16[128,512]{1,0:T(8,128)(2,1)S(1)} %collective-permute-done.31.refs_0_, bf16[128,512]{1,0:T(8,128)(2,1)S(1)} %collective-permute-done.32.refs_1_), custom_call_target="tpu_custom_call" | custom-call | bytes 262144 | tf_op jit(solution)/shard_map/pick_4/pallas_call | solution.py:400
  75.1 1.6 %copy.26 = bf16[16,128,256]{1,2,0:T(8,128)(2,1)S(1)} copy(bf16[16,128,256]{2,1,0:T(8,128)(2,1)} %bitcast.10) | data formatting | bytes 2097152 | tf_op jit(solution)/shard_map/reshape | solution.py:430
  76.8 2.2 %copy-done.1 = bf16[4096,512]{1,0:T(8,128)(2,1)S(1)} copy-done((bf16[4096,512]{1,0:T(8,128)(2,1)S(1)}, bf16[4096,512]{1,0:T(8,128)(2,1)}, u32[]{:S(2)}) %copy-start.1) | copy-done | bytes 4194328
  79.0 7.2 %back.1 = bf16[4096,512]{1,0:T(8,128)(2,1)} custom-call(s32[5,64]{1,0:T(8,128)S(1)} %get-tuple-element.35.table_ref, bf16[4096,512]{1,0:T(8,128)(2,1)S(1)} %copy-done.1, bf16[16,256,128]{2,1,0:T(8,128)(2,1)S(1)} %bitcast.8, bf16[4,32,512]{2,1,0:T(8,128)(2,1)S(1)} %get-tuple-element.45.refs_2_.rest_0_, ...), custom_call_target="tpu_custom_call" | custom-call | flops 536870912 | bytes 9437184 | tf_op jit(solution)/shard_map/back/pallas_call | solution.py:433
  (75 shorter events, 13.9 us)
Async XLA Ops:
  16.7 7.2 %collective-permute-start.1 = (bf16[4,32,512]{2,1,0:T(8,128)(2,1)S(1)}, bf16[4,32,512]{2,1,0:T(8,128)(2,1)S(1)}, u32[]{:S(2)}, u32[]{:S(2)}) collective-permute-start(bf16[4,32,512]{2,1,0:T(8,128)(2,1)S(1)} %get-tuple-element.39), channel_id=1, source_target_pairs={{0,4},{1,5},{2,0},{3,1},{4,8},{5,9},{6,2},{7,3},{8,12},{9,13},{10,... | collective-permute-start | bytes 393224 | tf_op jit(solution)/shard_map/ppermute | solution.py:59
  19.7 6.4 %collective-permute-start.5 = (bf16[4,32,512]{2,1,0:T(8,128)(2,1)S(1)}, bf16[4,32,512]{2,1,0:T(8,128)(2,1)S(1)}, u32[]{:S(2)}, u32[]{:S(2)}) collective-permute-start(bf16[4,32,512]{2,1,0:T(8,128)(2,1)S(1)} %get-tuple-element.42), channel_id=1, source_target_pairs={{0,2},{1,3},{2,6},{3,7},{4,0},{5,1},{6,10},{7,11},{8,4},{9,5},{10,... | collective-permute-start | bytes 393224 | tf_op jit(solution)/shard_map/ppermute | solution.py:59
  19.7 7.0 %collective-permute-start.4 = (bf16[4,32,512]{2,1,0:T(8,128)(2,1)S(1)}, bf16[4,32,512]{2,1,0:T(8,128)(2,1)S(1)}, u32[]{:S(2)}, u32[]{:S(2)}) collective-permute-start(bf16[4,32,512]{2,1,0:T(8,128)(2,1)S(1)} %get-tuple-element.41), channel_id=1, source_target_pairs={{0,4},{1,5},{2,0},{3,1},{4,8},{5,9},{6,2},{7,3},{8,12},{9,13},{10,... | collective-permute-start | bytes 393224 | tf_op jit(solution)/shard_map/ppermute | solution.py:59
  21.7 7.2 %collective-permute-start.3 = (bf16[4,32,512]{2,1,0:T(8,128)(2,1)S(1)}, bf16[4,32,512]{2,1,0:T(8,128)(2,1)S(1)}, u32[]{:S(2)}, u32[]{:S(2)}) collective-permute-start(bf16[4,32,512]{2,1,0:T(8,128)(2,1)S(1)} %get-tuple-element.40), channel_id=1, source_target_pairs={{0,2},{1,3},{2,6},{3,7},{4,0},{5,1},{6,10},{7,11},{8,4},{9,5},{10,... | collective-permute-start | bytes 393224 | tf_op jit(solution)/shard_map/ppermute | solution.py:59
  23.9 5.8 %collective-permute-start.2 = (bf16[4,32,512]{2,1,0:T(8,128)(2,1)S(1)}, bf16[4,32,512]{2,1,0:T(8,128)(2,1)S(1)}, u32[]{:S(2)}, u32[]{:S(2)}) collective-permute-start(bf16[4,32,512]{2,1,0:T(8,128)(2,1)S(1)} %add_r3a.1.token), channel_id=1, source_target_pairs={{0,4},{1,5},{2,0},{3,1},{4,8},{5,9},{6,2},{7,3},{8,12},{9,13},{10,... | collective-permute-start | bytes 393224 | tf_op jit(solution)/shard_map/ppermute | solution.py:59
  26.1 6.4 %collective-permute-start.9 = (bf16[4,32,512]{2,1,0:T(8,128)(2,1)S(1)}, bf16[4,32,512]{2,1,0:T(8,128)(2,1)S(1)}, u32[]{:S(2)}, u32[]{:S(2)}) collective-permute-start(bf16[4,32,512]{2,1,0:T(8,128)(2,1)S(1)} %add_l3b.1.token), channel_id=1, source_target_pairs={{0,2},{1,3},{2,6},{3,7},{4,0},{5,1},{6,10},{7,11},{8,4},{9,5},{10,... | collective-permute-start | bytes 393224 | tf_op jit(solution)/shard_map/ppermute | solution.py:59
  26.7 6.5 %collective-permute-start.8 = (bf16[4,32,512]{2,1,0:T(8,128)(2,1)S(1)}, bf16[4,32,512]{2,1,0:T(8,128)(2,1)S(1)}, u32[]{:S(2)}, u32[]{:S(2)}) collective-permute-start(bf16[4,32,512]{2,1,0:T(8,128)(2,1)S(1)} %add_r2b.1.token), channel_id=1, source_target_pairs={{0,4},{1,5},{2,0},{3,1},{4,8},{5,9},{6,2},{7,3},{8,12},{9,13},{10,... | collective-permute-start | bytes 393224 | tf_op jit(solution)/shard_map/ppermute | solution.py:59
  28.9 6.4 %collective-permute-start.7 = (bf16[4,32,512]{2,1,0:T(8,128)(2,1)S(1)}, bf16[4,32,512]{2,1,0:T(8,128)(2,1)S(1)}, u32[]{:S(2)}, u32[]{:S(2)}) collective-permute-start(bf16[4,32,512]{2,1,0:T(8,128)(2,1)S(1)} %add_l2a.1.token), channel_id=1, source_target_pairs={{0,2},{1,3},{2,6},{3,7},{4,0},{5,1},{6,10},{7,11},{8,4},{9,5},{10,... | collective-permute-start | bytes 393224 | tf_op jit(solution)/shard_map/ppermute | solution.py:59
  29.7 6.3 %collective-permute-start.6 = (bf16[4,32,512]{2,1,0:T(8,128)(2,1)S(1)}, bf16[4,32,512]{2,1,0:T(8,128)(2,1)S(1)}, u32[]{:S(2)}, u32[]{:S(2)}) collective-permute-start(bf16[4,32,512]{2,1,0:T(8,128)(2,1)S(1)} %add_r2a.1.token), channel_id=1, source_target_pairs={{0,4},{1,5},{2,0},{3,1},{4,8},{5,9},{6,2},{7,3},{8,12},{9,13},{10,... | collective-permute-start | bytes 393224 | tf_op jit(solution)/shard_map/ppermute | solution.py:59
  32.5 5.7 %collective-permute-start.11 = (bf16[4,32,512]{2,1,0:T(8,128)(2,1)S(1)}, bf16[4,32,512]{2,1,0:T(8,128)(2,1)S(1)}, u32[]{:S(2)}, u32[]{:S(2)}) collective-permute-start(bf16[4,32,512]{2,1,0:T(8,128)(2,1)S(1)} %add_l2b.1.token), channel_id=1, source_target_pairs={{0,2},{1,3},{2,6},{3,7},{4,0},{5,1},{6,10},{7,11},{8,4},{9,5},{10,... | collective-permute-start | bytes 393224 | tf_op jit(solution)/shard_map/ppermute | solution.py:59
  33.3 7.7 %collective-permute-start.13 = (bf16[4,32,512]{2,1,0:T(8,128)(2,1)S(1)}, bf16[4,32,512]{2,1,0:T(8,128)(2,1)S(1)}, u32[]{:S(2)}, u32[]{:S(2)}) collective-permute-start(bf16[4,32,512]{2,1,0:T(8,128)(2,1)S(1)} %add_r1b.1.token), channel_id=1, source_target_pairs={{0,4},{1,5},{2,0},{3,1},{4,8},{5,9},{6,2},{7,3},{8,12},{9,13},{10,... | collective-permute-start | bytes 393224 | tf_op jit(solution)/shard_map/ppermute | solution.py:59
  35.4 5.6 %collective-permute-start.14 = (bf16[4,32,512]{2,1,0:T(8,128)(2,1)S(1)}, bf16[4,32,512]{2,1,0:T(8,128)(2,1)S(1)}, u32[]{:S(2)}, u32[]{:S(2)}) collective-permute-start(bf16[4,32,512]{2,1,0:T(8,128)(2,1)S(1)} %add_l1a.1.token), channel_id=1, source_target_pairs={{0,2},{1,3},{2,6},{3,7},{4,0},{5,1},{6,10},{7,11},{8,4},{9,5},{10,... | collective-permute-start | bytes 393224 | tf_op jit(solution)/shard_map/ppermute | solution.py:59
  38.2 5.0 %collective-permute-start.12 = (bf16[4,32,512]{2,1,0:T(8,128)(2,1)S(1)}, bf16[4,32,512]{2,1,0:T(8,128)(2,1)S(1)}, u32[]{:S(2)}, u32[]{:S(2)}) collective-permute-start(bf16[4,32,512]{2,1,0:T(8,128)(2,1)S(1)} %add_l1b.1), channel_id=1, source_target_pairs={{0,2},{1,3},{2,6},{3,7},{4,0},{5,1},{6,10},{7,11},{8,4},{9,5},{10,... | collective-permute-start | bytes 393224 | tf_op jit(solution)/shard_map/ppermute | solution.py:59
  38.5 5.0 %collective-permute-start.10 = (bf16[4,32,512]{2,1,0:T(8,128)(2,1)S(1)}, bf16[4,32,512]{2,1,0:T(8,128)(2,1)S(1)}, u32[]{:S(2)}, u32[]{:S(2)}) collective-permute-start(bf16[4,32,512]{2,1,0:T(8,128)(2,1)S(1)} %add_r1a.1.token), channel_id=1, source_target_pairs={{0,4},{1,5},{2,0},{3,1},{4,8},{5,9},{6,2},{7,3},{8,12},{9,13},{10,... | collective-permute-start | bytes 393224 | tf_op jit(solution)/shard_map/ppermute | solution.py:59
  45.0 5.4 %collective-permute-start.16 = (bf16[128,512]{1,0:T(8,128)(2,1)S(1)}, bf16[128,512]{1,0:T(8,128)(2,1)S(1)}, u32[]{:S(2)}, u32[]{:S(2)}) collective-permute-start(bf16[128,512]{1,0:T(8,128)(2,1)S(1)} %get-tuple-element.43.refs_0_), channel_id=1, source_target_pairs={{0,4},{1,5},{2,0},{3,1},{4,8},{5,9},{6,2},{7,3},{8,12},{9,13},{10,... | collective-permute-start | bytes 393224 | tf_op jit(solution)/shard_map/ppermute | solution.py:59
  46.7 6.0 %collective-permute-start.17 = (bf16[128,512]{1,0:T(8,128)(2,1)S(1)}, bf16[128,512]{1,0:T(8,128)(2,1)S(1)}, u32[]{:S(2)}, u32[]{:S(2)}) collective-permute-start(bf16[128,512]{1,0:T(8,128)(2,1)S(1)} %get-tuple-element.44.refs_1_), channel_id=1, source_target_pairs={{0,2},{1,3},{2,6},{3,7},{4,0},{5,1},{6,10},{7,11},{8,4},{9,5},{10,... | collective-permute-start | bytes 393224 | tf_op jit(solution)/shard_map/ppermute | solution.py:59
  47.0 7.8 %collective-permute-start.18 = (bf16[128,512]{1,0:T(8,128)(2,1)S(1)}, bf16[128,512]{1,0:T(8,128)(2,1)S(1)}, u32[]{:S(2)}, u32[]{:S(2)}) collective-permute-start(bf16[128,512]{1,0:T(8,128)(2,1)S(1)} %get-tuple-element.44.refs_1_), channel_id=1, source_target_pairs={{0,4},{1,5},{2,0},{3,1},{4,8},{5,9},{6,2},{7,3},{8,12},{9,13},{10,... | collective-permute-start | bytes 393224 | tf_op jit(solution)/shard_map/ppermute | solution.py:59
  48.8 6.8 %collective-permute-start.19 = (bf16[128,512]{1,0:T(8,128)(2,1)S(1)}, bf16[128,512]{1,0:T(8,128)(2,1)S(1)}, u32[]{:S(2)}, u32[]{:S(2)}) collective-permute-start(bf16[128,512]{1,0:T(8,128)(2,1)S(1)} %get-tuple-element.43.refs_0_), channel_id=1, source_target_pairs={{0,2},{1,3},{2,6},{3,7},{4,0},{5,1},{6,10},{7,11},{8,4},{9,5},{10,... | collective-permute-start | bytes 393224 | tf_op jit(solution)/shard_map/ppermute | solution.py:59
  52.7 6.4 %collective-permute-start.21 = (bf16[128,512]{1,0:T(8,128)(2,1)S(1)}, bf16[128,512]{1,0:T(8,128)(2,1)S(1)}, u32[]{:S(2)}, u32[]{:S(2)}) collective-permute-start(bf16[128,512]{1,0:T(8,128)(2,1)S(1)} %get-tuple-element.47.refs_2_.refs_0_), channel_id=1, source_target_pairs={{0,4},{1,5},{2,0},{3,1},{4,8},{5,9},{6,2},{7,3},{8,12},{9,13},{10,... | collective-permute-start | bytes 393224 | tf_op jit(solution)/shard_map/ppermute | solution.py:59
  54.3 6.3 %collective-permute-start.22 = (bf16[128,512]{1,0:T(8,128)(2,1)S(1)}, bf16[128,512]{1,0:T(8,128)(2,1)S(1)}, u32[]{:S(2)}, u32[]{:S(2)}) collective-permute-start(bf16[128,512]{1,0:T(8,128)(2,1)S(1)} %get-tuple-element.50.refs_3_), channel_id=1, source_target_pairs={{0,2},{1,3},{2,6},{3,7},{4,0},{5,1},{6,10},{7,11},{8,4},{9,5},{10,... | collective-permute-start | bytes 393224 | tf_op jit(solution)/shard_map/ppermute | solution.py:59
  55.5 7.1 %collective-permute-start.23 = (bf16[128,512]{1,0:T(8,128)(2,1)S(1)}, bf16[128,512]{1,0:T(8,128)(2,1)S(1)}, u32[]{:S(2)}, u32[]{:S(2)}) collective-permute-start(bf16[128,512]{1,0:T(8,128)(2,1)S(1)} %get-tuple-element.48.refs_1_), channel_id=1, source_target_pairs={{0,4},{1,5},{2,0},{3,1},{4,8},{5,9},{6,2},{7,3},{8,12},{9,13},{10,... | collective-permute-start | bytes 393224 | tf_op jit(solution)/shard_map/ppermute | solution.py:59
  57.1 6.0 %collective-permute-start.24 = (bf16[128,512]{1,0:T(8,128)(2,1)S(1)}, bf16[128,512]{1,0:T(8,128)(2,1)S(1)}, u32[]{:S(2)}, u32[]{:S(2)}) collective-permute-start(bf16[128,512]{1,0:T(8,128)(2,1)S(1)} %get-tuple-element.49.refs_2_), channel_id=1, source_target_pairs={{0,2},{1,3},{2,6},{3,7},{4,0},{5,1},{6,10},{7,11},{8,4},{9,5},{10,... | collective-permute-start | bytes 393224 | tf_op jit(solution)/shard_map/ppermute | solution.py:59
  60.6 5.9 %collective-permute-start.26 = (bf16[128,512]{1,0:T(8,128)(2,1)S(1)}, bf16[128,512]{1,0:T(8,128)(2,1)S(1)}, u32[]{:S(2)}, u32[]{:S(2)}) collective-permute-start(bf16[128,512]{1,0:T(8,128)(2,1)S(1)} %get-tuple-element.53.refs_2_.refs_0_), channel_id=1, source_target_pairs={{0,4},{1,5},{2,0},{3,1},{4,8},{5,9},{6,2},{7,3},{8,12},{9,13},{10,... | collective-permute-start | bytes 393224 | tf_op jit(solution)/shard_map/ppermute | solution.py:59
  61.7 5.3 %collective-permute-start.27 = (bf16[128,512]{1,0:T(8,128)(2,1)S(1)}, bf16[128,512]{1,0:T(8,128)(2,1)S(1)}, u32[]{:S(2)}, u32[]{:S(2)}) collective-permute-start(bf16[128,512]{1,0:T(8,128)(2,1)S(1)} %get-tuple-element.56.refs_3_), channel_id=1, source_target_pairs={{0,2},{1,3},{2,6},{3,7},{4,0},{5,1},{6,10},{7,11},{8,4},{9,5},{10,... | collective-permute-start | bytes 393224 | tf_op jit(solution)/shard_map/ppermute | solution.py:59
  63.1 5.8 %collective-permute-start.28 = (bf16[128,512]{1,0:T(8,128)(2,1)S(1)}, bf16[128,512]{1,0:T(8,128)(2,1)S(1)}, u32[]{:S(2)}, u32[]{:S(2)}) collective-permute-start(bf16[128,512]{1,0:T(8,128)(2,1)S(1)} %get-tuple-element.54.refs_1_), channel_id=1, source_target_pairs={{0,4},{1,5},{2,0},{3,1},{4,8},{5,9},{6,2},{7,3},{8,12},{9,13},{10,... | collective-permute-start | bytes 393224 | tf_op jit(solution)/shard_map/ppermute | solution.py:59
  64.4 5.0 %collective-permute-start.29 = (bf16[128,512]{1,0:T(8,128)(2,1)S(1)}, bf16[128,512]{1,0:T(8,128)(2,1)S(1)}, u32[]{:S(2)}, u32[]{:S(2)}) collective-permute-start(bf16[128,512]{1,0:T(8,128)(2,1)S(1)} %get-tuple-element.55.refs_2_), channel_id=1, source_target_pairs={{0,2},{1,3},{2,6},{3,7},{4,0},{5,1},{6,10},{7,11},{8,4},{9,5},{10,... | collective-permute-start | bytes 393224 | tf_op jit(solution)/shard_map/ppermute | solution.py:59
  65.1 11.6 %collective-permute-start.20 = (bf16[8,32,512]{2,1,0:T(8,128)(2,1)S(1)}, bf16[8,32,512]{2,1,0:T(8,128)(2,1)S(1)}, u32[]{:S(2)}, u32[]{:S(2)}) collective-permute-start(bf16[8,32,512]{2,1,0:T(8,128)(2,1)S(1)} %get-tuple-element.52), channel_id=1, source_target_pairs={{0,1},{1,0},{2,3},{3,2},{4,5},{5,4},{6,7},{7,6},{8,9},{9,8},{10,11... | collective-permute-start | bytes 786440 | tf_op jit(solution)/shard_map/ppermute | solution.py:50
  66.5 10.3 %collective-permute-start.25 = (bf16[8,32,512]{2,1,0:T(8,128)(2,1)}, bf16[8,32,512]{2,1,0:T(8,128)(2,1)S(1)}, u32[]{:S(2)}, u32[]{:S(2)}) collective-permute-start(bf16[8,32,512]{2,1,0:T(8,128)(2,1)} %get-tuple-element.58), channel_id=1, source_target_pairs={{0,1},{1,0},{2,3},{3,2},{4,5},{5,4},{6,7},{7,6},{8,9},{9,8},{10,11... | collective-permute-start | bytes 786440 | tf_op jit(solution)/shard_map/ppermute | solution.py:50
  67.0 5.5 %collective-permute-start.31 = (bf16[128,512]{1,0:T(8,128)(2,1)S(1)}, bf16[128,512]{1,0:T(8,128)(2,1)S(1)}, u32[]{:S(2)}, u32[]{:S(2)}) collective-permute-start(bf16[128,512]{1,0:T(8,128)(2,1)S(1)} %get-tuple-element.59.refs_2_.refs_0_), channel_id=1, source_target_pairs={{0,4},{1,5},{2,0},{3,1},{4,8},{5,9},{6,2},{7,3},{8,12},{9,13},{10,... | collective-permute-start | bytes 393224 | tf_op jit(solution)/shard_map/ppermute | solution.py:59
  68.9 5.0 %collective-permute-start.32 = (bf16[128,512]{1,0:T(8,128)(2,1)S(1)}, bf16[128,512]{1,0:T(8,128)(2,1)S(1)}, u32[]{:S(2)}, u32[]{:S(2)}) collective-permute-start(bf16[128,512]{1,0:T(8,128)(2,1)S(1)} %get-tuple-element.62.refs_3_), channel_id=1, source_target_pairs={{0,2},{1,3},{2,6},{3,7},{4,0},{5,1},{6,10},{7,11},{8,4},{9,5},{10,... | collective-permute-start | bytes 393224 | tf_op jit(solution)/shard_map/ppermute | solution.py:59
  70.7 6.0 %collective-permute-start.30 = (bf16[8,32,512]{2,1,0:T(8,128)(2,1)}, bf16[8,32,512]{2,1,0:T(8,128)(2,1)S(1)}, u32[]{:S(2)}, u32[]{:S(2)}) collective-permute-start(bf16[8,32,512]{2,1,0:T(8,128)(2,1)} %get-tuple-element.64), channel_id=1, source_target_pairs={{0,1},{1,0},{2,3},{3,2},{4,5},{5,4},{6,7},{7,6},{8,9},{9,8},{10,11... | collective-permute-start | bytes 786440 | tf_op jit(solution)/shard_map/ppermute | solution.py:50
  72.5 4.3 %collective-permute-start.15 = (bf16[4,32,512]{2,1,0:T(8,128)(2,1)S(1)}, bf16[4,32,512]{2,1,0:T(8,128)(2,1)S(1)}, u32[]{:S(2)}, u32[]{:S(2)}) collective-permute-start(bf16[4,32,512]{2,1,0:T(8,128)(2,1)S(1)} %get-tuple-element.46), channel_id=1, source_target_pairs={{0,1},{1,0},{2,3},{3,2},{4,5},{5,4},{6,7},{7,6},{8,9},{9,8},{10,11... | collective-permute-start | bytes 393224 | tf_op jit(solution)/shard_map/ppermute | solution.py:50
  (8 other events, 38.2 us)

commit v7 on v6

--- a/solution.py
+++ b/solution.py
@@ -55,7 +55,7 @@
             chip, core = divmod(i, N_CORE)
             z, y = divmod(chip, self.n_y)
             ring = z if y == 0 else self.chips - 1 - z
-            pairs.append((i, self.index(ring + by, core)))
+            pairs.append((i, self.index(ring + (-by if core else by), core)))
         return lax.ppermute(value, "band", pairs)
 
     def entry(self, lists_ref, me, block, k):
@@ -63,7 +63,12 @@
         ring, core = self.place(owner)
         my_ring, my_core = self.place(me)
         ahead = split(ring - my_ring + self.chips, self.chips)[1]
-        return ahead, core ^ my_core, tile
+        left = (ahead > self.far).astype(jnp.int32)
+        shared = (ahead == 0) | (ahead == self.far)
+        handler = jnp.where(shared, core, left)
+        distance = jnp.where(ahead > self.far, self.chips - ahead, ahead)
+        group = jnp.maximum(2 * distance - 1 + (core ^ handler), 0)
+        return handler ^ my_core, group, tile
 
 
 def embed_kernel(
@@ -78,9 +83,9 @@
 
     def spot(index, b, k):
         block = step * per_step + b
-        ahead, across, tile = ring.entry(lists_ref, index, index * blk_count + block, k)
+        across, group, tile = ring.entry(lists_ref, index, index * blk_count + block, k)
         slot = split(block * list_len + k, ring.n_band)[0]
-        return (across * ring.chips + ahead) * slots + slot, tile
+        return (across * ring.chips + group) * slots + slot, tile
 
     def embedded(rows):
         first = lax.dot_general(
@@ -118,81 +123,60 @@
                 sent_ref[jnp.where(place >= spare, place - spare, spare)] = masked
 
 
-def add_entries(total, table_ref, owner, slots, kept, other, chips):
+def add_entries(total, table_ref, group, slots, kept, other, groups):
     for slot in range(slots):
-        place = owner * slots + slot
+        place = group * slots + slot
         total[table_ref[0, place]] += kept[place].astype(F32)
-        total[table_ref[1, chips * slots + place]] += other[place].astype(F32)
-
-
-def far_kernel(
-    ring, slots, table_ref, kept, other, far_right, far_left, next_right, next_left, total
+        total[table_ref[1, groups * slots + place]] += other[place].astype(F32)
+
+
+def far_kernel(slots, groups, table_ref, kept, other, far, before, total):
+    for group, out in ((groups - 1, far), (groups - 2, before)):
+        total[...] = jnp.zeros_like(total)
+        add_entries(total, table_ref, group, slots, kept, other, groups)
+        out[...] = total[...].astype(BF16)
+
+
+def own_kernel(slots, groups, table_ref, kept, other, own):
+    group = pl.program_id(0)
+    total = own.at[group]
+    total[...] = jnp.zeros_like(total)
+    add_entries(total, table_ref, group, slots, kept, other, groups)
+
+
+def add_kernel(group, own, came, token, out):
+    del token
+    out[...] = (own[group] + came[...].astype(F32)).astype(BF16)
+
+
+def mesh_kernel(
+    latent_ref, up_ref, down_ref, gain_ref, own, came, neighbour, out_ref, piece_ref
 ):
-    half = total.shape[0] // 2
-    for number, owner in enumerate((ring.far, ring.far - 1, ring.chips - ring.far + 1)):
-        total[...] = jnp.zeros_like(total)
-        add_entries(total, table_ref, owner, slots, kept, other, ring.chips)
-        if number == 0:
-            far_right[...] = total[:half].astype(BF16)
-            far_left[...] = total[half:].astype(BF16)
-        elif number == 1:
-            next_right[...] = total[half:].astype(BF16)
-        else:
-            next_left[...] = total[:half].astype(BF16)
-
-
-def own_kernel(ring, slots, table_ref, kept, other, own):
-    number = pl.program_id(0)
-    owner = number + (number >= ring.far).astype(jnp.int32)
-    total = own.at[owner]
-    total[...] = jnp.zeros_like(total)
-    add_entries(total, table_ref, owner, slots, kept, other, ring.chips)
-
-
-def mesh_kernel(
-    latent_ref, up_ref, down_ref, gain_ref, own, right_a, left_b, right_b, left_a,
-    out_ref, out_a, out_b,
-):
-    tiles, tile_rows, width = own.shape[1:]
-    half = tiles // 2
-    lower = own[0, :half] + right_a[...].astype(F32) + left_a[...].astype(F32)
-    upper = own[0, half:] + right_b[...].astype(F32) + left_b[...].astype(F32)
-    came = jnp.concatenate([lower, upper], axis=0).reshape(tiles * tile_rows, width)
-    mesh_in = latent_ref[...].astype(F32) + came
+    total = own[0] + came[...].astype(F32) + neighbour[...].astype(F32)
+    mesh_in = latent_ref[...].astype(F32) + total.reshape(latent_ref.shape)
     normed = layer_norm(mesh_in, gain_ref[...]).astype(BF16)
     hidden = silu(jnp.dot(normed, up_ref[...], preferred_element_type=F32)).astype(BF16)
     out = (mesh_in + jnp.dot(hidden, down_ref[...], preferred_element_type=F32)).astype(BF16)
     out_ref[...] = out
-    out_a[...] = out[: half * tile_rows]
-    out_b[...] = out[half * tile_rows :]
-
-
-def add_kernel(owner, part, own, came, token, out):
-    del token
-    count = out.shape[0]
-    mine = own[owner, part * count : (part + 1) * count]
-    out[...] = (mine + came[...].astype(F32)).astype(BF16)
+    piece_ref[...] = out
 
 
 def order_kernel(*refs):
     del refs
 
 
-def pick_kernel(owners, slots, chips, table_ref, *refs):
-    halves, (mine, theirs) = refs[:-2], refs[-2:]
+def pick_kernel(chosen, slots, groups, table_ref, *refs):
+    pieces, (mine, theirs) = refs[:-2], refs[-2:]
     tile_rows = mine.shape[1]
-    count = halves[0].shape[0] // tile_rows
-    for number, owner in enumerate(owners):
-        lower, upper = halves[2 * number : 2 * number + 2]
+    for number, group in enumerate(chosen):
         for slot in range(slots):
             for way, out in enumerate((mine, theirs)):
-                place = (way * chips + owner) * slots + slot
-                tile, mask = table_ref[way, place], table_ref[2 + way, place]
-                above = tile >= count
-                within = jnp.where(above, tile - count, tile)
-                rows = pl.ds(pl.multiple_of(within * tile_rows, tile_rows), tile_rows)
-                value = jnp.where(above, upper[rows], lower[rows])
-                out[number * slots + slot] = jnp.where(mask == 1, value, jnp.zeros_like(value))
+                place = (way * groups + group) * slots + slot
+                tile = table_ref[way, place]
+                rows = pl.ds(pl.multiple_of(tile * tile_rows, tile_rows), tile_rows)
+                value = pieces[number][rows]
+                listed = table_ref[2 + way, place] == 1
+                out[number * slots + slot] = jnp.where(listed, value, jnp.zeros_like(value))
 
 
 def back_kernel(places, slots, list_len, per_step, table_ref, latent_ref, weights_ref, *rest):
@@ -263,7 +247,6 @@
     channels, width = embed_in.shape
     node_rows = mesh_latent.shape[0]
     tiles = node_rows // tile_rows
-    half_tiles, half_rows = tiles // 2, node_rows // 2
     entries = blk_count * list_len
     slots = entries // n_band
     ring = Ring(n_band, n_y, tiles)
@@ -279,7 +262,7 @@
     held_shape = (chips * slots + 1, tile_rows, width)
     latent, kept, sent, table = pl.pallas_call(
         functools.partial(embed_kernel, ring, per_step, slots),
-        out_shape=[shape((blk_count * block_rows, width))]
+        out_shape=[pltpu.HBM((blk_count * block_rows, width), BF16)]
         + [shape(held_shape)] * N_CORE
         + [shape((5, entries), jnp.int32)],
         grid_spec=pltpu.PrefetchScalarGridSpec(
@@ -307,26 +290,25 @@
     other = ring.over_core(sent)
 
     dense = (tiles, tile_rows, width)
-    half_dense = (half_tiles, tile_rows, width)
-
     in_vmem = pl.BlockSpec(memory_space=pltpu.VMEM)
-    far_right, far_left, next_right, next_left = pl.pallas_call(
-        functools.partial(far_kernel, ring, slots),
-        out_shape=[shape(half_dense)] * 4,
+    in_any = pl.BlockSpec(memory_space=pl.ANY)
+    first, second = pl.pallas_call(
+        functools.partial(far_kernel, slots, chips),
+        out_shape=[shape(dense)] * 2,
         grid_spec=pltpu.PrefetchScalarGridSpec(
             num_scalar_prefetch=1,
             grid=(1,),
             in_specs=[in_vmem] * 2,
-            out_specs=[in_vmem] * 4,
+            out_specs=[in_vmem] * 2,
             scratch_shapes=[pltpu.VMEM(dense, F32)],
         ),
         compiler_params=params(8),
         cost_estimate=cost(0, kept),
-        name="far_chunks",
+        name="far_sums",
     )(table, kept, other)
     own = pl.pallas_call(
-        functools.partial(own_kernel, ring, slots),
-        out_shape=shape((chips,) + dense, F32),
+        functools.partial(own_kernel, slots, chips),
+        out_shape=shape((chips - 1,) + dense, F32),
         grid_spec=pltpu.PrefetchScalarGridSpec(
             num_scalar_prefetch=1,
             grid=(chips - 1,),
@@ -335,97 +317,88 @@
         ),
         compiler_params=params(8 if n_band <= 16 else 24),
         cost_estimate=cost(0, kept, kept, kept, kept),
-        name="own_chunks",
+        name="own_sums",
     )(table, kept, other)
 
-    lower, upper = 0, 1
-
-    def add_own(distance, part, value, token):
+    def add_own(group, value, token):
         return pl.pallas_call(
-            functools.partial(add_kernel, distance % chips, part),
-            out_shape=shape(half_dense),
-            in_specs=[in_vmem] * 2 + [pl.BlockSpec(memory_space=pl.ANY)],
+            functools.partial(add_kernel, group),
+            out_shape=shape(dense),
+            in_specs=[in_vmem] * 2 + [in_any],
             out_specs=in_vmem,
             compiler_params=params(8),
             cost_estimate=cost(0, value, value),
-            name=f"add_{'lr'[distance > 0]}{abs(distance)}{'ab'[part]}",
+            name=f"add_{group}",
         )(own, value, token)
 
-    def both(values):
-        return [ring.over(values[0], 1), ring.over(values[1], -1)]
-
-    def both_with_own(distance, parts, values, token):
-        sent = []
-        for way, part, value in zip((1, -1), parts, values):
-            token = add_own(way * distance, part, value, token)
-            sent.append(ring.over(token, way))
-        return sent, token
-
-    first, second = both((far_right, far_left)), both((next_right, next_left))
+    first, second = ring.over(first, 1), ring.over(second, 1)
     token = own
-    for distance in range(far - 1, 0, -1):
-        first, token = both_with_own(distance, (lower, upper), first, token)
-        if distance > 1:
-            second, token = both_with_own(distance - 1, (upper, lower), second, token)
+    for group in range(chips - 3, 0, -1):
+        if group % 2:
+            token = add_own(group, first, token)
+            first = ring.over(token, 1)
+        else:
+            token = add_own(group, second, token)
+            second = ring.over(token, 1)
+    second = ring.over_core(second)
 
     mesh_gain = mesh_gain.reshape(1, width)
-    came = (*first, *second)
-    mesh_out, out_a, out_b = pl.pallas_call(
+    mesh_out, piece = pl.pallas_call(
         mesh_kernel,
-        out_shape=[shape((node_rows, width))] + [shape((half_rows, width))] * 2,
-        in_specs=[in_vmem] * 9,
-        out_specs=[in_vmem] * 3,
+        out_shape=[shape((node_rows, width))] * 2,
+        in_specs=[in_vmem] * 7,
+        out_specs=[in_vmem] * 2,
         compiler_params=params(16),
         cost_estimate=cost(4 * node_rows * width * width, mesh_up, mesh_down),
         name="mesh_step",
-    )(mesh_latent, mesh_up, mesh_down, mesh_gain, own, *came)
-
-    def in_order(values, token):
+    )(mesh_latent, mesh_up, mesh_down, mesh_gain, own, first, second)
+
+    def in_order(value, token):
         return pl.pallas_call(
             order_kernel,
-            out_shape=[shape(v.shape) for v in values],
-            in_specs=[pl.BlockSpec(memory_space=pl.ANY)] * (len(values) + 1),
-            out_specs=[pl.BlockSpec(memory_space=pl.ANY)] * len(values),
-            input_output_aliases={i: i for i in range(len(values))},
+            out_shape=shape(value.shape),
+            in_specs=[in_any] * 2,
+            out_specs=in_any,
+            input_output_aliases={0: 0},
             compiler_params=params(1),
             cost_estimate=cost(0),
             name="in_order",
-        )(*values, token)
+        )(value, token)
 
     pieces, places = [], []
 
-    def pick(owners, halves):
-        owners = [owner % chips for owner in owners]
-        out = shape((len(owners) * slots, tile_rows, width))
+    def pick(chosen, values):
+        out = shape((len(chosen) * slots, tile_rows, width))
         mine, theirs = pl.pallas_call(
-            functools.partial(pick_kernel, owners, slots, chips),
+            functools.partial(pick_kernel, chosen, slots, chips),
             out_shape=[out] * 2,
             grid_spec=pltpu.PrefetchScalarGridSpec(
                 num_scalar_prefetch=1,
                 grid=(1,),
-                in_specs=[in_vmem] * len(halves),
+                in_specs=[in_vmem] * len(values),
                 out_specs=[in_vmem] * 2,
             ),
             compiler_params=params(8),
-            cost_estimate=cost(0, *halves),
-            name=f"pick_{owners[0]}",
-        )(table, *halves)
+            cost_estimate=cost(0, *values),
+            name=f"pick_{chosen[0]}",
+        )(table, *values)
         for across, value in enumerate((mine, ring.over_core(theirs))):
             pieces.append(value)
-            places.append([across * chips + owner for owner in owners])
+            places.append([across * chips + group for group in chosen])
         return mine
 
-    first, second = both((out_a, out_b)), both((out_b, out_a))
-    token = pick([0], (out_a, out_b))
+    first = ring.over(piece, -1)
+    second = ring.over(ring.over_core(piece), -1)
+    token = pick([0], [piece])
     for distance in range(1, far):
         first = in_order(first, token)
-        onward = both(first)
-        second = in_order(second, first[0])
+        onward = ring.over(first, -1)
+        second = in_order(second, first)
         if distance < far - 1:
-            after = both(second)
-        token = pick([-distance, distance], (first[0], second[0], second[1], first[1]))
+            after = ring.over(second, -1)
+        token = pick([2 * distance - 1, 2 * distance], [first, second])
         first, second = onward, after
-    pick([far], first)
+    pick([chips - 1], [first])
 
     weights = jnp.swapaxes(interp.reshape(blk_count, list_len * tile_rows, block_rows), 1, 2)
     per_step = 4

time: 86.5 us -> 87.4 us (1.010)
  waiting for transfers between devices: 21.2 us -> 25.5 us
  local copies, waits for them, and re-layouts: 5.83 us -> 3.82 us
  starting transfers between devices: 31.5 us -> 29.6 us
    ppermute x28 -> x14, waiting for transfers between devices: 18.8 us -> 23.1 us  [over(): return lax.ppermute(value, 'band', pairs)]
    ppermute x28 -> x14, starting transfers between devices: 30.5 us -> 28.1 us  [over(): return lax.ppermute(value, 'band', pairs)]
    unnamed x12 -> x10, local copies, waits for them, and re-layouts: 4.22 us -> 2.21 us
    pallas_call x24 -> x19, Pallas kernels: 9.32 us -> 9.13 us  [the longest x5 5.28 us: pick(): pl.pallas_call(functools.partial(pick_kernel, chosen, slots, chips), out_...]
    ppermute x6 -> x8, waiting for transfers between devices: 2.35 us -> 2.35 us  [over_core(): return lax.ppermute(value, 'band', [(i, i ^ 1) for i in range(self.n_band)])]
  transfers between devices with their start and end apart: 34 -> 22, of which waited for: 20 -> 15; matrix products, arithmetic and copies ran while one was open for 2% -> 2% of each run, Pallas kernels for 8% -> 8%
where the time goes in v7:
time: 87.4 us; the launch traced here: 87.1 us
  starting transfers between devices  29.6 us (34%)
  Pallas kernels  27.5 us (31%)
  waiting for transfers between devices  25.5 us (29%)
  local copies, waits for them, and re-layouts  3.82 us (4%)
    ppermute x14, starting transfers between devices, over(): return lax.ppermute(value, 'band', pairs)  28.1 us
    ppermute x14, waiting for transfers between devices, over(): return lax.ppermute(value, 'band', pairs)  23.1 us
    pallas_call x1, Pallas kernels, on_device(): pl.pallas_call(functools.partial(embed_kernel, ring, per_step, slots), ou...  11.1 us
    pallas_call x1, Pallas kernels, on_device(): pl.pallas_call(functools.partial(back_kernel, places, slots, list_len, pe...  7.22 us
    pallas_call x5, Pallas kernels, pick(): pl.pallas_call(functools.partial(pick_kernel, chosen, slots, chips), out_...  5.28 us
    ppermute x8, waiting for transfers between devices, over_core(): return lax.ppermute(value, 'band', [(i, i ^ 1) for i in range(self.n_band)])  2.35 us
    unnamed x10, local copies, waits for them, and re-layouts  2.21 us
  transfers between devices with their start and end apart: 22, of which 15 were waited for; matrix products, arithmetic and copies ran while one was open for 2% of the time, Pallas kernels for 8%

profile of v7, /device:TPU:0, one launch (start us, length us, event | category | flops | bytes accessed | tf_op | source)
XLA Modules:
  0.0 87.1 jit_solution(11069971529574378028)
XLA Ops:
  0.6 11.1 %embed.1 = (bf16[4096,512]{1,0:T(8,128)(2,1)}, bf16[33,32,512]{2,1,0:T(8,128)(2,1)S(1)}, bf16[33,32,512]{2,1,0:T(8,128)(2,1)S(1)}, s32[5,64]{1,0:T(8,128)S(1)}) custom-call(s32[1]{0:T(128)} %bitcast.me_ref, s32[4,256]{1,0:T(4,128)} %bitcast.12, s32[4,256]{1,0:T(4,128)} %bitcast.13, bf16[227,4096]{1,0:T(8,128)(2,1)} %bitcast.11, bf16[227,512]{1,0:T(8,128)(2,1)} %w1_ref.1, ...), custom_call_target="tpu_custom_call" | custom-call | flops 3636461568 | bytes 2908160 | tf_op jit(solution)/shard_map/embed/pallas_call | solution.py:263
  12.2 2.3 %collective-permute-done.other = bf16[33,32,512]{2,1,0:T(8,128)(2,1)S(1)} collective-permute-done((bf16[33,32,512]{2,1,0:T(8,128)(2,1)S(1)}, bf16[33,32,512]{2,1,0:T(8,128)(2,1)S(1)}, u32[]{:S(2)}, u32[]{:S(2)}) %collective-permute-start) | collective-permute-done | bytes 1081376 | tf_op jit(solution)/shard_map/ppermute | solution.py:50
  15.4 3.0 %collective-permute-start.1 = (bf16[8,32,512]{2,1,0:T(8,128)(2,1)S(1)}, bf16[8,32,512]{2,1,0:T(8,128)(2,1)S(1)}, u32[]{:S(2)}, u32[]{:S(2)}) collective-permute-start(bf16[8,32,512]{2,1,0:T(8,128)(2,1)S(1)} %get-tuple-element.24), channel_id=1, source_target_pairs={{0,4},{1,3},{2,0},{3,7},{4,8},{5,1},{6,2},{7,11},{8,12},{9,5},{10,... | collective-permute-start | bytes 786440 | tf_op jit(solution)/shard_map/ppermute | solution.py:59
  18.4 1.6 %collective-permute-start.3 = (bf16[8,32,512]{2,1,0:T(8,128)(2,1)S(1)}, bf16[8,32,512]{2,1,0:T(8,128)(2,1)S(1)}, u32[]{:S(2)}, u32[]{:S(2)}) collective-permute-start(bf16[8,32,512]{2,1,0:T(8,128)(2,1)S(1)} %get-tuple-element.25), channel_id=1, source_target_pairs={{0,4},{1,3},{2,0},{3,7},{4,8},{5,1},{6,2},{7,11},{8,12},{9,5},{10,... | collective-permute-start | bytes 786440 | tf_op jit(solution)/shard_map/ppermute | solution.py:59
  19.9 1.3 %own_sums.1.own.token = f32[7,8,32,512]{3,2,1,0:T(8,128)S(1)} custom-call(s32[5,64]{1,0:T(8,128)S(1)} %get-tuple-element.20.table_ref, bf16[33,32,512]{2,1,0:T(8,128)(2,1)S(1)} %get-tuple-element.22.kept, bf16[33,32,512]{2,1,0:T(8,128)(2,1)S(1)} %collective-permute-done.other), custom_call_target="tpu_custom_call" | custom-call | bytes 4325376 | tf_op jit(solution)/shard_map/own_sums/pallas_call | solution.py:309
  21.3 1.4 %collective-permute-done.1.came = bf16[8,32,512]{2,1,0:T(8,128)(2,1)S(1)} collective-permute-done((bf16[8,32,512]{2,1,0:T(8,128)(2,1)S(1)}, bf16[8,32,512]{2,1,0:T(8,128)(2,1)S(1)}, u32[]{:S(2)}, u32[]{:S(2)}) %collective-permute-start.1) | collective-permute-done | bytes 262176 | tf_op jit(solution)/shard_map/ppermute | solution.py:59
  22.7 2.1 %collective-permute-start.2 = (bf16[8,32,512]{2,1,0:T(8,128)(2,1)S(1)}, bf16[8,32,512]{2,1,0:T(8,128)(2,1)S(1)}, u32[]{:S(2)}, u32[]{:S(2)}) collective-permute-start(bf16[8,32,512]{2,1,0:T(8,128)(2,1)S(1)} %add_5.1.token), channel_id=1, source_target_pairs={{0,4},{1,3},{2,0},{3,7},{4,8},{5,1},{6,2},{7,11},{8,12},{9,5},{10,... | collective-permute-start | bytes 786440 | tf_op jit(solution)/shard_map/ppermute | solution.py:59
  25.5 2.1 %collective-permute-start.5 = (bf16[8,32,512]{2,1,0:T(8,128)(2,1)S(1)}, bf16[8,32,512]{2,1,0:T(8,128)(2,1)S(1)}, u32[]{:S(2)}, u32[]{:S(2)}) collective-permute-start(bf16[8,32,512]{2,1,0:T(8,128)(2,1)S(1)} %add_4.1.token), channel_id=1, source_target_pairs={{0,4},{1,3},{2,0},{3,7},{4,8},{5,1},{6,2},{7,11},{8,12},{9,5},{10,... | collective-permute-start | bytes 786440 | tf_op jit(solution)/shard_map/ppermute | solution.py:59
  27.6 1.5 %collective-permute-done.2.came = bf16[8,32,512]{2,1,0:T(8,128)(2,1)S(1)} collective-permute-done((bf16[8,32,512]{2,1,0:T(8,128)(2,1)S(1)}, bf16[8,32,512]{2,1,0:T(8,128)(2,1)S(1)}, u32[]{:S(2)}, u32[]{:S(2)}) %collective-permute-start.2) | collective-permute-done | bytes 262176 | tf_op jit(solution)/shard_map/ppermute | solution.py:59
  29.2 2.8 %collective-permute-done.5.came = bf16[8,32,512]{2,1,0:T(8,128)(2,1)S(1)} collective-permute-done((bf16[8,32,512]{2,1,0:T(8,128)(2,1)S(1)}, bf16[8,32,512]{2,1,0:T(8,128)(2,1)S(1)}, u32[]{:S(2)}, u32[]{:S(2)}) %collective-permute-start.5) | collective-permute-done | bytes 262176 | tf_op jit(solution)/shard_map/ppermute | solution.py:59
  32.0 2.1 %collective-permute-start.7 = (bf16[8,32,512]{2,1,0:T(8,128)(2,1)S(1)}, bf16[8,32,512]{2,1,0:T(8,128)(2,1)S(1)}, u32[]{:S(2)}, u32[]{:S(2)}) collective-permute-start(bf16[8,32,512]{2,1,0:T(8,128)(2,1)S(1)} %add_2.1.token), channel_id=1, source_target_pairs={{0,4},{1,3},{2,0},{3,7},{4,8},{5,1},{6,2},{7,11},{8,12},{9,5},{10,... | collective-permute-start | bytes 786440 | tf_op jit(solution)/shard_map/ppermute | solution.py:59
  34.2 1.6 %collective-permute-start.4 = (bf16[8,32,512]{2,1,0:T(8,128)(2,1)S(1)}, bf16[8,32,512]{2,1,0:T(8,128)(2,1)S(1)}, u32[]{:S(2)}, u32[]{:S(2)}) collective-permute-start(bf16[8,32,512]{2,1,0:T(8,128)(2,1)S(1)} %add_3.1.token), channel_id=1, source_target_pairs={{0,4},{1,3},{2,0},{3,7},{4,8},{5,1},{6,2},{7,11},{8,12},{9,5},{10,... | collective-permute-start | bytes 786440 | tf_op jit(solution)/shard_map/ppermute | solution.py:59
  35.7 2.7 %collective-permute-done.7 = bf16[8,32,512]{2,1,0:T(8,128)(2,1)S(1)} collective-permute-done((bf16[8,32,512]{2,1,0:T(8,128)(2,1)S(1)}, bf16[8,32,512]{2,1,0:T(8,128)(2,1)S(1)}, u32[]{:S(2)}, u32[]{:S(2)}) %collective-permute-start.7) | collective-permute-done | bytes 262176 | tf_op jit(solution)/shard_map/ppermute | solution.py:59
  38.5 2.8 %collective-permute-done.4.came = bf16[8,32,512]{2,1,0:T(8,128)(2,1)S(1)} collective-permute-done((bf16[8,32,512]{2,1,0:T(8,128)(2,1)S(1)}, bf16[8,32,512]{2,1,0:T(8,128)(2,1)S(1)}, u32[]{:S(2)}, u32[]{:S(2)}) %collective-permute-start.4) | collective-permute-done | bytes 262176 | tf_op jit(solution)/shard_map/ppermute | solution.py:59
  41.3 2.1 %collective-permute-start.6 = (bf16[8,32,512]{2,1,0:T(8,128)(2,1)S(1)}, bf16[8,32,512]{2,1,0:T(8,128)(2,1)S(1)}, u32[]{:S(2)}, u32[]{:S(2)}) collective-permute-start(bf16[8,32,512]{2,1,0:T(8,128)(2,1)S(1)} %add_1.1), channel_id=1, source_target_pairs={{0,4},{1,3},{2,0},{3,7},{4,8},{5,1},{6,2},{7,11},{8,12},{9,5},{10,... | collective-permute-start | bytes 786440 | tf_op jit(solution)/shard_map/ppermute | solution.py:59
  43.4 4.3 %collective-permute-done.6.came = bf16[8,32,512]{2,1,0:T(8,128)(2,1)S(1)} collective-permute-done((bf16[8,32,512]{2,1,0:T(8,128)(2,1)S(1)}, bf16[8,32,512]{2,1,0:T(8,128)(2,1)S(1)}, u32[]{:S(2)}, u32[]{:S(2)}) %collective-permute-start.6) | collective-permute-done | bytes 262176 | tf_op jit(solution)/shard_map/ppermute | solution.py:59
  47.8 1.5 %mesh_step.1 = (bf16[256,512]{1,0:T(8,128)(2,1)}, bf16[256,512]{1,0:T(8,128)(2,1)S(1)}) custom-call(bf16[256,512]{1,0:T(8,128)(2,1)S(1)} %copy-done.3, bf16[512,512]{1,0:T(8,128)(2,1)S(1)} %copy-done.1, bf16[512,512]{1,0:T(8,128)(2,1)S(1)} %copy-done.2, f32[1,512]{1,0:T(1,128)S(1)} %bitcast.9, f32[7,8,32,512]{3,2,1,0:T(8,128)S(1)} %own_sums.1.own.token, ...), custom_call_target="tpu_custom_call" | custom-call | flops 268435456 | bytes 1048576 | tf_op jit(solution)/shard_map/mesh_step/pallas_call | solution.py:346
  49.2 2.0 %collective-permute-start.10 = (bf16[256,512]{1,0:T(8,128)(2,1)S(1)}, bf16[256,512]{1,0:T(8,128)(2,1)S(1)}, u32[]{:S(2)}, u32[]{:S(2)}) collective-permute-start(bf16[256,512]{1,0:T(8,128)(2,1)S(1)} %get-tuple-element.26.refs_0_), channel_id=1, source_target_pairs={{0,2},{1,5},{2,6},{3,1},{4,0},{5,9},{6,10},{7,3},{8,4},{9,13},{10,... | collective-permute-start | bytes 786440 | tf_op jit(solution)/shard_map/ppermute | solution.py:59
  51.3 1.6 %collective-permute-start.12 = (bf16[256,512]{1,0:T(8,128)(2,1)S(1)}, bf16[256,512]{1,0:T(8,128)(2,1)S(1)}, u32[]{:S(2)}, u32[]{:S(2)}) collective-permute-start(bf16[256,512]{1,0:T(8,128)(2,1)S(1)} %collective-permute-done.11), channel_id=1, source_target_pairs={{0,2},{1,5},{2,6},{3,1},{4,0},{5,9},{6,10},{7,3},{8,4},{9,13},{10,... | collective-permute-start | bytes 786440 | tf_op jit(solution)/shard_map/ppermute | solution.py:59
  53.5 2.2 %collective-permute-done.10.refs_0_ = bf16[256,512]{1,0:T(8,128)(2,1)S(1)} collective-permute-done((bf16[256,512]{1,0:T(8,128)(2,1)S(1)}, bf16[256,512]{1,0:T(8,128)(2,1)S(1)}, u32[]{:S(2)}, u32[]{:S(2)}) %collective-permute-start.10) | collective-permute-done | bytes 262176 | tf_op jit(solution)/shard_map/ppermute | solution.py:59
  55.7 2.0 %collective-permute-start.14 = (bf16[256,512]{1,0:T(8,128)(2,1)S(1)}, bf16[256,512]{1,0:T(8,128)(2,1)S(1)}, u32[]{:S(2)}, u32[]{:S(2)}) collective-permute-start(bf16[256,512]{1,0:T(8,128)(2,1)S(1)} %in_order.6.refs_1_.refs_0_), channel_id=1, source_target_pairs={{0,2},{1,5},{2,6},{3,1},{4,0},{5,9},{6,10},{7,3},{8,4},{9,13},{10,... | collective-permute-start | bytes 786440 | tf_op jit(solution)/shard_map/ppermute | solution.py:59
  58.5 2.0 %collective-permute-start.15 = (bf16[256,512]{1,0:T(8,128)(2,1)S(1)}, bf16[256,512]{1,0:T(8,128)(2,1)S(1)}, u32[]{:S(2)}, u32[]{:S(2)}) collective-permute-start(bf16[256,512]{1,0:T(8,128)(2,1)S(1)} %in_order.7.refs_1_), channel_id=1, source_target_pairs={{0,2},{1,5},{2,6},{3,1},{4,0},{5,9},{6,10},{7,3},{8,4},{9,13},{10,... | collective-permute-start | bytes 786440 | tf_op jit(solution)/shard_map/ppermute | solution.py:59
  62.0 2.0 %collective-permute-start.17 = (bf16[256,512]{1,0:T(8,128)(2,1)S(1)}, bf16[256,512]{1,0:T(8,128)(2,1)S(1)}, u32[]{:S(2)}, u32[]{:S(2)}) collective-permute-start(bf16[256,512]{1,0:T(8,128)(2,1)S(1)} %in_order.8.refs_1_.refs_0_), channel_id=1, source_target_pairs={{0,2},{1,5},{2,6},{3,1},{4,0},{5,9},{6,10},{7,3},{8,4},{9,13},{10,... | collective-permute-start | bytes 786440 | tf_op jit(solution)/shard_map/ppermute | solution.py:59
  64.8 2.0 %collective-permute-start.18 = (bf16[256,512]{1,0:T(8,128)(2,1)S(1)}, bf16[256,512]{1,0:T(8,128)(2,1)S(1)}, u32[]{:S(2)}, u32[]{:S(2)}) collective-permute-start(bf16[256,512]{1,0:T(8,128)(2,1)S(1)} %in_order.9.refs_1_), channel_id=1, source_target_pairs={{0,2},{1,5},{2,6},{3,1},{4,0},{5,9},{6,10},{7,3},{8,4},{9,13},{10,... | collective-permute-start | bytes 786440 | tf_op jit(solution)/shard_map/ppermute | solution.py:59
  66.8 1.4 %pick_3.1 = (bf16[8,32,512]{2,1,0:T(8,128)(2,1)S(1)}, bf16[8,32,512]{2,1,0:T(8,128)(2,1)}) custom-call(s32[5,64]{1,0:T(8,128)S(1)} %get-tuple-element.20.table_ref, bf16[256,512]{1,0:T(8,128)(2,1)S(1)} %in_order.8.refs_1_.refs_0_, bf16[256,512]{1,0:T(8,128)(2,1)S(1)} %in_order.9.refs_1_), custom_call_target="tpu_custom_call" | custom-call | bytes 524288 | tf_op jit(solution)/shard_map/pick_3/pallas_call | solution.py:372
  68.4 2.0 %collective-permute-start.20 = (bf16[256,512]{1,0:T(8,128)(2,1)S(1)}, bf16[256,512]{1,0:T(8,128)(2,1)S(1)}, u32[]{:S(2)}, u32[]{:S(2)}) collective-permute-start(bf16[256,512]{1,0:T(8,128)(2,1)S(1)} %in_order.10.refs_1_.refs_0_), channel_id=1, source_target_pairs={{0,2},{1,5},{2,6},{3,1},{4,0},{5,9},{6,10},{7,3},{8,4},{9,13},{10,... | collective-permute-start | bytes 786440 | tf_op jit(solution)/shard_map/ppermute | solution.py:59
  71.2 1.3 %pick_5.1 = (bf16[8,32,512]{2,1,0:T(8,128)(2,1)S(1)}, bf16[8,32,512]{2,1,0:T(8,128)(2,1)}) custom-call(s32[5,64]{1,0:T(8,128)S(1)} %get-tuple-element.20.table_ref, bf16[256,512]{1,0:T(8,128)(2,1)S(1)} %in_order.10.refs_1_.refs_0_, bf16[256,512]{1,0:T(8,128)(2,1)S(1)} %in_order.11.refs_1_), custom_call_target="tpu_custom_call" | custom-call | bytes 524288 | tf_op jit(solution)/shard_map/pick_5/pallas_call | solution.py:372
  73.1 1.7 %collective-permute-done.20.refs_0_ = bf16[256,512]{1,0:T(8,128)(2,1)S(1)} collective-permute-done((bf16[256,512]{1,0:T(8,128)(2,1)S(1)}, bf16[256,512]{1,0:T(8,128)(2,1)S(1)}, u32[]{:S(2)}, u32[]{:S(2)}) %collective-permute-start.20) | collective-permute-done | bytes 262176 | tf_op jit(solution)/shard_map/ppermute | solution.py:59
  74.8 1.3 %pick_7.1 = (bf16[4,32,512]{2,1,0:T(8,128)(2,1)S(1)}, bf16[4,32,512]{2,1,0:T(8,128)(2,1)}) custom-call(s32[5,64]{1,0:T(8,128)S(1)} %get-tuple-element.20.table_ref, bf16[256,512]{1,0:T(8,128)(2,1)S(1)} %collective-permute-done.20.refs_0_), custom_call_target="tpu_custom_call" | custom-call | bytes 262144 | tf_op jit(solution)/shard_map/pick_7/pallas_call | solution.py:372
  76.1 1.6 %copy.20 = bf16[16,128,256]{1,2,0:T(8,128)(2,1)S(1)} copy(bf16[16,128,256]{2,1,0:T(8,128)(2,1)} %bitcast.10) | data formatting | bytes 2097152 | tf_op jit(solution)/shard_map/reshape | solution.py:403
  77.7 2.2 %copy-done = bf16[4096,512]{1,0:T(8,128)(2,1)S(1)} copy-done((bf16[4096,512]{1,0:T(8,128)(2,1)S(1)}, bf16[4096,512]{1,0:T(8,128)(2,1)}, u32[]{:S(2)}) %copy-start) | copy-done | bytes 4194328
  79.9 7.2 %back.1 = bf16[4096,512]{1,0:T(8,128)(2,1)} custom-call(s32[5,64]{1,0:T(8,128)S(1)} %get-tuple-element.20.table_ref, bf16[4096,512]{1,0:T(8,128)(2,1)S(1)} %copy-done, bf16[16,256,128]{2,1,0:T(8,128)(2,1)S(1)} %bitcast.8, bf16[4,32,512]{2,1,0:T(8,128)(2,1)S(1)} %get-tuple-element.27.refs_1_.rest_0_, bf16[4,32,512]{2,1,0:T(8,128)(2,1)S(1)} %collective-permute-done.9.rest_1_, ...), custom_call_target="tpu_custom_call" | custom-call | flops 536870912 | bytes 9437184 | tf_op jit(solution)/shard_map/back/pallas_call | solution.py:406
  (44 shorter events, 7.7 us)
Async XLA Ops:
  11.7 2.8 %collective-permute-start = (bf16[33,32,512]{2,1,0:T(8,128)(2,1)S(1)}, bf16[33,32,512]{2,1,0:T(8,128)(2,1)S(1)}, u32[]{:S(2)}, u32[]{:S(2)}) collective-permute-start(bf16[33,32,512]{2,1,0:T(8,128)(2,1)S(1)} %get-tuple-element.23), channel_id=1, source_target_pairs={{0,1},{1,0},{2,3},{3,2},{4,5},{5,4},{6,7},{7,6},{8,9},{9,8},{10,11... | collective-permute-start | bytes 3244040 | tf_op jit(solution)/shard_map/ppermute | solution.py:50
  15.4 7.3 %collective-permute-start.1 = (bf16[8,32,512]{2,1,0:T(8,128)(2,1)S(1)}, bf16[8,32,512]{2,1,0:T(8,128)(2,1)S(1)}, u32[]{:S(2)}, u32[]{:S(2)}) collective-permute-start(bf16[8,32,512]{2,1,0:T(8,128)(2,1)S(1)} %get-tuple-element.24), channel_id=1, source_target_pairs={{0,4},{1,3},{2,0},{3,7},{4,8},{5,1},{6,2},{7,11},{8,12},{9,5},{10,... | collective-permute-start | bytes 786440 | tf_op jit(solution)/shard_map/ppermute | solution.py:59
  18.4 7.1 %collective-permute-start.3 = (bf16[8,32,512]{2,1,0:T(8,128)(2,1)S(1)}, bf16[8,32,512]{2,1,0:T(8,128)(2,1)S(1)}, u32[]{:S(2)}, u32[]{:S(2)}) collective-permute-start(bf16[8,32,512]{2,1,0:T(8,128)(2,1)S(1)} %get-tuple-element.25), channel_id=1, source_target_pairs={{0,4},{1,3},{2,0},{3,7},{4,8},{5,1},{6,2},{7,11},{8,12},{9,5},{10,... | collective-permute-start | bytes 786440 | tf_op jit(solution)/shard_map/ppermute | solution.py:59
  22.7 6.4 %collective-permute-start.2 = (bf16[8,32,512]{2,1,0:T(8,128)(2,1)S(1)}, bf16[8,32,512]{2,1,0:T(8,128)(2,1)S(1)}, u32[]{:S(2)}, u32[]{:S(2)}) collective-permute-start(bf16[8,32,512]{2,1,0:T(8,128)(2,1)S(1)} %add_5.1.token), channel_id=1, source_target_pairs={{0,4},{1,3},{2,0},{3,7},{4,8},{5,1},{6,2},{7,11},{8,12},{9,5},{10,... | collective-permute-start | bytes 786440 | tf_op jit(solution)/shard_map/ppermute | solution.py:59
  25.5 6.4 %collective-permute-start.5 = (bf16[8,32,512]{2,1,0:T(8,128)(2,1)S(1)}, bf16[8,32,512]{2,1,0:T(8,128)(2,1)S(1)}, u32[]{:S(2)}, u32[]{:S(2)}) collective-permute-start(bf16[8,32,512]{2,1,0:T(8,128)(2,1)S(1)} %add_4.1.token), channel_id=1, source_target_pairs={{0,4},{1,3},{2,0},{3,7},{4,8},{5,1},{6,2},{7,11},{8,12},{9,5},{10,... | collective-permute-start | bytes 786440 | tf_op jit(solution)/shard_map/ppermute | solution.py:59
  32.0 15.8 %copy-start.1 = (bf16[512,512]{1,0:T(8,128)(2,1)S(1)}, bf16[512,512]{1,0:T(8,128)(2,1)}, u32[]{:S(2)}) copy-start(bf16[512,512]{1,0:T(8,128)(2,1)} %up_ref.1) | copy-start | bytes 1572868
  32.0 15.7 %copy-start.2 = (bf16[512,512]{1,0:T(8,128)(2,1)S(1)}, bf16[512,512]{1,0:T(8,128)(2,1)}, u32[]{:S(2)}) copy-start(bf16[512,512]{1,0:T(8,128)(2,1)} %down_ref.1) | copy-start | bytes 1572868
  32.0 15.7 %copy-start.3 = (bf16[256,512]{1,0:T(8,128)(2,1)S(1)}, bf16[256,512]{1,0:T(8,128)(2,1)}, u32[]{:S(2)}) copy-start(bf16[256,512]{1,0:T(8,128)(2,1)} %latent_ref.1) | copy-start | bytes 786436
  32.0 15.7 %copy-start.4 = (f32[512]{0:T(512)S(1)}, f32[512]{0:T(512)}, u32[]{:S(2)}) copy-start(f32[512]{0:T(512)} %param.21) | copy-start | bytes 6148
  32.0 6.4 %collective-permute-start.7 = (bf16[8,32,512]{2,1,0:T(8,128)(2,1)S(1)}, bf16[8,32,512]{2,1,0:T(8,128)(2,1)S(1)}, u32[]{:S(2)}, u32[]{:S(2)}) collective-permute-start(bf16[8,32,512]{2,1,0:T(8,128)(2,1)S(1)} %add_2.1.token), channel_id=1, source_target_pairs={{0,4},{1,3},{2,0},{3,7},{4,8},{5,1},{6,2},{7,11},{8,12},{9,5},{10,... | collective-permute-start | bytes 786440 | tf_op jit(solution)/shard_map/ppermute | solution.py:59
  34.2 7.1 %collective-permute-start.4 = (bf16[8,32,512]{2,1,0:T(8,128)(2,1)S(1)}, bf16[8,32,512]{2,1,0:T(8,128)(2,1)S(1)}, u32[]{:S(2)}, u32[]{:S(2)}) collective-permute-start(bf16[8,32,512]{2,1,0:T(8,128)(2,1)S(1)} %add_3.1.token), channel_id=1, source_target_pairs={{0,4},{1,3},{2,0},{3,7},{4,8},{5,1},{6,2},{7,11},{8,12},{9,5},{10,... | collective-permute-start | bytes 786440 | tf_op jit(solution)/shard_map/ppermute | solution.py:59
  38.5 5.0 %collective-permute-start.8 = (bf16[8,32,512]{2,1,0:T(8,128)(2,1)S(1)}, bf16[8,32,512]{2,1,0:T(8,128)(2,1)S(1)}, u32[]{:S(2)}, u32[]{:S(2)}) collective-permute-start(bf16[8,32,512]{2,1,0:T(8,128)(2,1)S(1)} %collective-permute-done.7), channel_id=1, source_target_pairs={{0,1},{1,0},{2,3},{3,2},{4,5},{5,4},{6,7},{7,6},{8,9},{9,8},{10,11... | collective-permute-start | bytes 786440 | tf_op jit(solution)/shard_map/ppermute | solution.py:50
  41.3 6.4 %collective-permute-start.6 = (bf16[8,32,512]{2,1,0:T(8,128)(2,1)S(1)}, bf16[8,32,512]{2,1,0:T(8,128)(2,1)S(1)}, u32[]{:S(2)}, u32[]{:S(2)}) collective-permute-start(bf16[8,32,512]{2,1,0:T(8,128)(2,1)S(1)} %add_1.1), channel_id=1, source_target_pairs={{0,4},{1,3},{2,0},{3,7},{4,8},{5,1},{6,2},{7,11},{8,12},{9,5},{10,... | collective-permute-start | bytes 786440 | tf_op jit(solution)/shard_map/ppermute | solution.py:59
  49.2 2.0 %collective-permute-start.11 = (bf16[256,512]{1,0:T(8,128)(2,1)S(1)}, bf16[256,512]{1,0:T(8,128)(2,1)S(1)}, u32[]{:S(2)}, u32[]{:S(2)}) collective-permute-start(bf16[256,512]{1,0:T(8,128)(2,1)S(1)} %get-tuple-element.26.refs_0_), channel_id=1, source_target_pairs={{0,1},{1,0},{2,3},{3,2},{4,5},{5,4},{6,7},{7,6},{8,9},{9,8},{10,11... | collective-permute-start | bytes 786440 | tf_op jit(solution)/shard_map/ppermute | solution.py:50
  49.2 6.4 %collective-permute-start.10 = (bf16[256,512]{1,0:T(8,128)(2,1)S(1)}, bf16[256,512]{1,0:T(8,128)(2,1)S(1)}, u32[]{:S(2)}, u32[]{:S(2)}) collective-permute-start(bf16[256,512]{1,0:T(8,128)(2,1)S(1)} %get-tuple-element.26.refs_0_), channel_id=1, source_target_pairs={{0,2},{1,5},{2,6},{3,1},{4,0},{5,9},{6,10},{7,3},{8,4},{9,13},{10,... | collective-permute-start | bytes 786440 | tf_op jit(solution)/shard_map/ppermute | solution.py:59
  51.3 7.2 %collective-permute-start.12 = (bf16[256,512]{1,0:T(8,128)(2,1)S(1)}, bf16[256,512]{1,0:T(8,128)(2,1)S(1)}, u32[]{:S(2)}, u32[]{:S(2)}) collective-permute-start(bf16[256,512]{1,0:T(8,128)(2,1)S(1)} %collective-permute-done.11), channel_id=1, source_target_pairs={{0,2},{1,5},{2,6},{3,1},{4,0},{5,9},{6,10},{7,3},{8,4},{9,13},{10,... | collective-permute-start | bytes 786440 | tf_op jit(solution)/shard_map/ppermute | solution.py:59
  55.7 6.4 %collective-permute-start.14 = (bf16[256,512]{1,0:T(8,128)(2,1)S(1)}, bf16[256,512]{1,0:T(8,128)(2,1)S(1)}, u32[]{:S(2)}, u32[]{:S(2)}) collective-permute-start(bf16[256,512]{1,0:T(8,128)(2,1)S(1)} %in_order.6.refs_1_.refs_0_), channel_id=1, source_target_pairs={{0,2},{1,5},{2,6},{3,1},{4,0},{5,9},{6,10},{7,3},{8,4},{9,13},{10,... | collective-permute-start | bytes 786440 | tf_op jit(solution)/shard_map/ppermute | solution.py:59
  58.5 6.4 %collective-permute-start.15 = (bf16[256,512]{1,0:T(8,128)(2,1)S(1)}, bf16[256,512]{1,0:T(8,128)(2,1)S(1)}, u32[]{:S(2)}, u32[]{:S(2)}) collective-permute-start(bf16[256,512]{1,0:T(8,128)(2,1)S(1)} %in_order.7.refs_1_), channel_id=1, source_target_pairs={{0,2},{1,5},{2,6},{3,1},{4,0},{5,9},{6,10},{7,3},{8,4},{9,13},{10,... | collective-permute-start | bytes 786440 | tf_op jit(solution)/shard_map/ppermute | solution.py:59
  62.0 6.4 %collective-permute-start.17 = (bf16[256,512]{1,0:T(8,128)(2,1)S(1)}, bf16[256,512]{1,0:T(8,128)(2,1)S(1)}, u32[]{:S(2)}, u32[]{:S(2)}) collective-permute-start(bf16[256,512]{1,0:T(8,128)(2,1)S(1)} %in_order.8.refs_1_.refs_0_), channel_id=1, source_target_pairs={{0,2},{1,5},{2,6},{3,1},{4,0},{5,9},{6,10},{7,3},{8,4},{9,13},{10,... | collective-permute-start | bytes 786440 | tf_op jit(solution)/shard_map/ppermute | solution.py:59
  64.8 6.4 %collective-permute-start.18 = (bf16[256,512]{1,0:T(8,128)(2,1)S(1)}, bf16[256,512]{1,0:T(8,128)(2,1)S(1)}, u32[]{:S(2)}, u32[]{:S(2)}) collective-permute-start(bf16[256,512]{1,0:T(8,128)(2,1)S(1)} %in_order.9.refs_1_), channel_id=1, source_target_pairs={{0,2},{1,5},{2,6},{3,1},{4,0},{5,9},{6,10},{7,3},{8,4},{9,13},{10,... | collective-permute-start | bytes 786440 | tf_op jit(solution)/shard_map/ppermute | solution.py:59
  68.4 6.4 %collective-permute-start.20 = (bf16[256,512]{1,0:T(8,128)(2,1)S(1)}, bf16[256,512]{1,0:T(8,128)(2,1)S(1)}, u32[]{:S(2)}, u32[]{:S(2)}) collective-permute-start(bf16[256,512]{1,0:T(8,128)(2,1)S(1)} %in_order.10.refs_1_.refs_0_), channel_id=1, source_target_pairs={{0,2},{1,5},{2,6},{3,1},{4,0},{5,9},{6,10},{7,3},{8,4},{9,13},{10,... | collective-permute-start | bytes 786440 | tf_op jit(solution)/shard_map/ppermute | solution.py:59
  70.4 7.3 %collective-permute-start.13 = (bf16[8,32,512]{2,1,0:T(8,128)(2,1)S(1)}, bf16[8,32,512]{2,1,0:T(8,128)(2,1)S(1)}, u32[]{:S(2)}, u32[]{:S(2)}) collective-permute-start(bf16[8,32,512]{2,1,0:T(8,128)(2,1)S(1)} %get-tuple-element.30), channel_id=1, source_target_pairs={{0,1},{1,0},{2,3},{3,2},{4,5},{5,4},{6,7},{7,6},{8,9},{9,8},{10,11... | collective-permute-start | bytes 786440 | tf_op jit(solution)/shard_map/ppermute | solution.py:50
  70.4 7.3 %collective-permute-start.16 = (bf16[8,32,512]{2,1,0:T(8,128)(2,1)}, bf16[8,32,512]{2,1,0:T(8,128)(2,1)S(1)}, u32[]{:S(2)}, u32[]{:S(2)}) collective-permute-start(bf16[8,32,512]{2,1,0:T(8,128)(2,1)} %get-tuple-element.32), channel_id=1, source_target_pairs={{0,1},{1,0},{2,3},{3,2},{4,5},{5,4},{6,7},{7,6},{8,9},{9,8},{10,11... | collective-permute-start | bytes 786440 | tf_op jit(solution)/shard_map/ppermute | solution.py:50
  72.6 5.2 %collective-permute-start.19 = (bf16[8,32,512]{2,1,0:T(8,128)(2,1)}, bf16[8,32,512]{2,1,0:T(8,128)(2,1)S(1)}, u32[]{:S(2)}, u32[]{:S(2)}) collective-permute-start(bf16[8,32,512]{2,1,0:T(8,128)(2,1)} %get-tuple-element.34), channel_id=1, source_target_pairs={{0,1},{1,0},{2,3},{3,2},{4,5},{5,4},{6,7},{7,6},{8,9},{9,8},{10,11... | collective-permute-start | bytes 786440 | tf_op jit(solution)/shard_map/ppermute | solution.py:50
  72.6 5.1 %collective-permute-start.9 = (bf16[4,32,512]{2,1,0:T(8,128)(2,1)S(1)}, bf16[4,32,512]{2,1,0:T(8,128)(2,1)S(1)}, u32[]{:S(2)}, u32[]{:S(2)}) collective-permute-start(bf16[4,32,512]{2,1,0:T(8,128)(2,1)S(1)} %get-tuple-element.28), channel_id=1, source_target_pairs={{0,1},{1,0},{2,3},{3,2},{4,5},{5,4},{6,7},{7,6},{8,9},{9,8},{10,11... | collective-permute-start | bytes 393224 | tf_op jit(solution)/shard_map/ppermute | solution.py:50
  76.1 1.7 %collective-permute-start.21 = (bf16[4,32,512]{2,1,0:T(8,128)(2,1)}, bf16[4,32,512]{2,1,0:T(8,128)(2,1)S(1)}, u32[]{:S(2)}, u32[]{:S(2)}) collective-permute-start(bf16[4,32,512]{2,1,0:T(8,128)(2,1)} %get-tuple-element.36), channel_id=1, source_target_pairs={{0,1},{1,0},{2,3},{3,2},{4,5},{5,4},{6,7},{7,6},{8,9},{9,8},{10,11... | collective-permute-start | bytes 393224 | tf_op jit(solution)/shard_map/ppermute | solution.py:50
  77.7 2.2 %copy-start = (bf16[4096,512]{1,0:T(8,128)(2,1)S(1)}, bf16[4096,512]{1,0:T(8,128)(2,1)}, u32[]{:S(2)}) copy-start(bf16[4096,512]{1,0:T(8,128)(2,1)} %get-tuple-element.21.latent_ref) | copy-start | bytes 12582916

commit v8 on v7

--- a/solution.py
+++ b/solution.py
@@ -10,6 +10,8 @@
 F32 = jnp.float32
 BF16 = jnp.bfloat16
 N_CORE = 2
+STRIP = 32
+PART = 2
 
 
 def silu(values):
@@ -49,13 +51,13 @@
     def over_core(self, value):
         return lax.ppermute(value, "band", [(i, i ^ 1) for i in range(self.n_band)])
 
-    def over(self, value, by):
+    def over(self, value, by, cross=0):
         pairs = []
         for i in range(self.n_band):
             chip, core = divmod(i, N_CORE)
             z, y = divmod(chip, self.n_y)
             ring = z if y == 0 else self.chips - 1 - z
-            pairs.append((i, self.index(ring + (-by if core else by), core)))
+            pairs.append((i, self.index(ring + (-by if core else by), core ^ cross)))
         return lax.ppermute(value, "band", pairs)
 
     def entry(self, lists_ref, me, block, k):
@@ -71,52 +73,57 @@
         return handler ^ my_core, group, tile
 
 
+def strips(rows):
+    return [slice(r, r + STRIP) for r in range(rows.start, rows.stop, STRIP)]
+
+
 def embed_kernel(
     ring, per_step, slots, me_ref, lists_ref, mask_ref,
     x_ref, w1_ref, w2_ref, gain_ref, interp_ref,
-    latent_ref, kept_ref, sent_ref, table_ref,
+    latent_ref, kept_ref, sent_ref, table_ref, wide, hidden,
 ):
     step = pl.program_id(0)
     me = me_ref[0]
     list_len, tile_rows, block_rows = interp_ref.shape[1:]
     blk_count = pl.num_programs(0) * per_step
-
-    def spot(index, b, k):
-        block = step * per_step + b
+    groups = ring.chips
+
+    def spot(index, block, k):
         across, group, tile = ring.entry(lists_ref, index, index * blk_count + block, k)
         slot = split(block * list_len + k, ring.n_band)[0]
-        return (across * ring.chips + group) * slots + slot, tile
-
-    def embedded(rows):
-        first = lax.dot_general(
+        return across, group, tile, slot
+
+    part_rows = PART * block_rows
+    spans = [slice(i * part_rows, (i + 1) * part_rows) for i in range(per_step // PART)]
+    for rows in spans:
+        wide[rows] = lax.dot_general(
             x_ref[:, rows], w1_ref[...], (((0,), (0,)), ((), ())), preferred_element_type=F32
         )
-        return jnp.dot(silu(first).astype(BF16), w2_ref[...], preferred_element_type=F32)
-
+    for rows in spans:
+        for strip in strips(rows):
+            hidden[strip] = silu(wide[strip]).astype(BF16)
+        wide[rows] = jnp.dot(hidden[rows], w2_ref[...], preferred_element_type=F32)
     spare = kept_ref.shape[0] - 1
-    parts = 2
-    part_rows = latent_ref.shape[0] // parts
-    spans = [slice(i * part_rows, (i + 1) * part_rows) for i in range(parts)]
-    befores = [embedded(rows) for rows in spans]
     for number, rows in enumerate(spans):
-        latent = layer_norm(befores[number], gain_ref[...]).astype(BF16)
-        latent_ref[rows] = latent
-        for i in range(per_step // parts):
-            b = number * (per_step // parts) + i
+        for strip in strips(rows):
+            latent_ref[strip] = layer_norm(wide[strip], gain_ref[...]).astype(BF16)
+        for b in range(number * PART, (number + 1) * PART):
             block = step * per_step + b
             weights = interp_ref[b].reshape(list_len * tile_rows, block_rows)
-            part = jnp.dot(
-                weights, latent[i * block_rows : (i + 1) * block_rows], preferred_element_type=F32
-            )
+            latent = latent_ref[b * block_rows : (b + 1) * block_rows]
+            part = jnp.dot(weights, latent, preferred_element_type=F32)
             for k in range(list_len):
-                place, tile = spot(me, b, k)
-                there, its_tile = spot(me ^ 1, b, k)
+                across, group, tile, slot = spot(me, block, k)
+                place = (across * groups + group) * slots + slot
                 mask = mask_ref[k, me * blk_count + block]
                 table_ref[0, place] = tile
-                table_ref[1, there] = its_tile
-                table_ref[2, place] = mask
-                table_ref[3, there] = mask_ref[k, (me ^ 1) * blk_count + block]
-                table_ref[4, block * list_len + k] = place
+                found = group * slots + jnp.where(group == groups - 1, tile, slot)
+                table_ref[2, block * list_len + k] = found + across * (
+                    (groups - 1) * slots + ring.tiles
+                )
+                table_ref[3, block * list_len + k] = mask
+                across, group, tile, slot = spot(me ^ 1, block, k)
+                table_ref[1, (across * groups + group) * slots + slot] = tile
                 masked = part[k * tile_rows : (k + 1) * tile_rows] * mask.astype(F32)
                 masked = masked.astype(BF16)
                 kept_ref[jnp.minimum(place, spare)] = masked
@@ -165,49 +172,53 @@
     del refs
 
 
-def pick_kernel(chosen, slots, groups, table_ref, *refs):
-    pieces, (mine, theirs) = refs[:-2], refs[-2:]
-    tile_rows = mine.shape[1]
+def pick_kernel(chosen, slots, groups, tile_rows, table_ref, *refs):
+    pieces, outs = refs[:-2], refs[-2:]
     for number, group in enumerate(chosen):
         for slot in range(slots):
-            for way, out in enumerate((mine, theirs)):
-                place = (way * groups + group) * slots + slot
-                tile = table_ref[way, place]
+            for way, out in enumerate(outs):
+                tile = table_ref[way, (way * groups + group) * slots + slot]
                 rows = pl.ds(pl.multiple_of(tile * tile_rows, tile_rows), tile_rows)
-                value = pieces[number][rows]
-                listed = table_ref[2 + way, place] == 1
-                out[number * slots + slot] = jnp.where(listed, value, jnp.zeros_like(value))
-
-
-def back_kernel(places, slots, list_len, per_step, table_ref, latent_ref, weights_ref, *rest):
-    count = len(places)
-    pieces, (out_ref, held, sems) = rest[:count], rest[count:]
+                into = (number * slots + slot) * tile_rows
+                out[into : into + tile_rows] = pieces[number][rows]
+
+
+def turn_kernel(interp_ref, token, out_ref):
+    del token
+    for b in range(interp_ref.shape[0]):
+        out_ref[b] = interp_ref[b].reshape(out_ref.shape[2], out_ref.shape[1]).T
+
+
+def back_kernel(starts, list_len, per_step, table_ref, latent_ref, weights_ref, *rest):
+    count = len(starts)
+    pieces, (out_ref, held, total, sems) = rest[:count], rest[count:]
     step = pl.program_id(0)
     block_rows = weights_ref.shape[1]
+    tile_rows = weights_ref.shape[2] // list_len
 
     @pl.when(step == 0)
     def _():
         copies = []
-        for i, (piece, place) in enumerate(zip(pieces, places)):
-            for number, start in enumerate(place):
-                copies.append(
-                    pltpu.make_async_copy(
-                        piece.at[pl.ds(number * slots, slots)],
-                        held.at[pl.ds(start * slots, slots)],
-                        sems.at[len(copies)],
-                    )
-                )
+        for i, (piece, start) in enumerate(zip(pieces, starts)):
+            into = held.at[pl.ds(start, piece.shape[0])]
+            copies.append(pltpu.make_async_copy(piece, into, sems.at[i]))
         for copy in copies:
             copy.start()
         for copy in copies:
             copy.wait()
 
     for b in range(per_step):
-        first = (step * per_step + b) * list_len
-        value = jnp.concatenate([held[table_ref[4, first + k]] for k in range(list_len)], axis=0)
-        back = jnp.dot(weights_ref[b], value, preferred_element_type=F32)
+        values = []
+        for k in range(list_len):
+            entry = (step * per_step + b) * list_len + k
+            rows = pl.ds(pl.multiple_of(table_ref[2, entry] * tile_rows, tile_rows), tile_rows)
+            value = held[rows]
+            values.append(jnp.where(table_ref[3, entry] == 1, value, jnp.zeros_like(value)))
+        value = jnp.concatenate(values, axis=0)
         rows = slice(b * block_rows, (b + 1) * block_rows)
-        out_ref[rows] = (latent_ref[rows].astype(F32) + back).astype(BF16)
+        total[rows] = jnp.dot(weights_ref[b], value, preferred_element_type=F32)
+        for strip in strips(rows):
+            out_ref[strip] = (latent_ref[strip].astype(F32) + total[strip]).astype(BF16)
 
 
 def whole(array):
@@ -264,7 +275,7 @@
         functools.partial(embed_kernel, ring, per_step, slots),
         out_shape=[pltpu.HBM((blk_count * block_rows, width), BF16)]
         + [shape(held_shape)] * N_CORE
-        + [shape((5, entries), jnp.int32)],
+        + [shape((4, entries), jnp.int32)],
         grid_spec=pltpu.PrefetchScalarGridSpec(
             num_scalar_prefetch=3,
             grid=(blk_count // per_step,),
@@ -278,6 +289,7 @@
             out_specs=[pl.BlockSpec((rows, width), lambda i, *_: (i, 0))]
             + [pl.BlockSpec(memory_space=pltpu.VMEM)] * N_CORE
             + [pl.BlockSpec(memory_space=pltpu.SMEM)],
+            scratch_shapes=[pltpu.VMEM((rows, width), F32), pltpu.VMEM((rows, width), BF16)],
         ),
         compiler_params=params(24),
         cost_estimate=cost(
@@ -320,39 +332,6 @@
         name="own_sums",
     )(table, kept, other)
 
-    def add_own(group, value, token):
-        return pl.pallas_call(
-            functools.partial(add_kernel, group),
-            out_shape=shape(dense),
-            in_specs=[in_vmem] * 2 + [in_any],
-            out_specs=in_vmem,
-            compiler_params=params(8),
-            cost_estimate=cost(0, value, value),
-            name=f"add_{group}",
-        )(own, value, token)
-
-    first, second = ring.over(first, 1), ring.over(second, 1)
-    token = own
-    for group in range(chips - 3, 0, -1):
-        if group % 2:
-            token = add_own(group, first, token)
-            first = ring.over(token, 1)
-        else:
-            token = add_own(group, second, token)
-            second = ring.over(token, 1)
-    second = ring.over_core(second)
-
-    mesh_gain = mesh_gain.reshape(1, width)
-    mesh_out, piece = pl.pallas_call(
-        mesh_kernel,
-        out_shape=[shape((node_rows, width))] * 2,
-        in_specs=[in_vmem] * 7,
-        out_specs=[in_vmem] * 2,
-        compiler_params=params(16),
-        cost_estimate=cost(4 * node_rows * width * width, mesh_up, mesh_down),
-        name="mesh_step",
-    )(mesh_latent, mesh_up, mesh_down, mesh_gain, own, first, second)
-
     def in_order(value, token):
         return pl.pallas_call(
             order_kernel,
@@ -365,12 +344,60 @@
             name="in_order",
         )(value, token)
 
-    pieces, places = [], []
+    def add_own(group, value, token):
+        return pl.pallas_call(
+            functools.partial(add_kernel, group),
+            out_shape=shape(dense),
+            in_specs=[in_vmem] * 2 + [in_any],
+            out_specs=in_vmem,
+            compiler_params=params(8),
+            cost_estimate=cost(0),
+            name=f"add_{group}",
+        )(own, value, token)
+
+    first, second = ring.over(first, 1), ring.over(second, 1)
+    turned = (blk_count, block_rows, list_len * tile_rows)
+    per_step = 4
+    token = weights = pl.pallas_call(
+        turn_kernel,
+        out_shape=shape(turned),
+        grid=(blk_count // per_step,),
+        in_specs=[pl.BlockSpec((per_step,) + interp.shape[1:], lambda i: (i, 0, 0, 0)), in_any],
+        out_specs=pl.BlockSpec((per_step,) + turned[1:], lambda i: (i, 0, 0)),
+        compiler_params=params(8),
+        cost_estimate=cost(0, interp, interp),
+        name="turn",
+    )(interp, own)
+    for group in range(chips - 3, 0, -1):
+        if group % 2:
+            token = add_own(group, first, token)
+            first = ring.over(token, 1)
+        else:
+            token = add_own(group, second, token)
+            second = ring.over(token, 1, int(group == 2))
+
+    mesh_gain = mesh_gain.reshape(1, width)
+    mesh_out, piece = pl.pallas_call(
+        mesh_kernel,
+        out_shape=[shape((node_rows, width))] * 2,
+        in_specs=[in_vmem] * 7,
+        out_specs=[in_vmem] * 2,
+        compiler_params=params(16),
+        cost_estimate=cost(4 * node_rows * width * width, mesh_up, mesh_down),
+        name="mesh_step",
+    )(mesh_latent, mesh_up, mesh_down, mesh_gain, own, first, second)
+
+    pieces, starts = [], []
+
+    def share(index, mine, theirs):
+        for across, value in enumerate((mine, ring.over_core(theirs))):
+            pieces.append(value)
+            starts.append((across * ((chips - 1) * slots + tiles) + index) * tile_rows)
 
     def pick(chosen, values):
-        out = shape((len(chosen) * slots, tile_rows, width))
+        out = shape((len(chosen) * slots * tile_rows, width))
         mine, theirs = pl.pallas_call(
-            functools.partial(pick_kernel, chosen, slots, chips),
+            functools.partial(pick_kernel, chosen, slots, chips, tile_rows),
             out_shape=[out] * 2,
             grid_spec=pltpu.PrefetchScalarGridSpec(
                 num_scalar_prefetch=1,
@@ -382,13 +409,11 @@
             cost_estimate=cost(0, *values),
             name=f"pick_{chosen[0]}",
         )(table, *values)
-        for across, value in enumerate((mine, ring.over_core(theirs))):
-            pieces.append(value)
-            places.append([across * chips + group for group in chosen])
+        share(chosen[0] * slots, mine, theirs)
         return mine
 
     first = ring.over(piece, -1)
-    second = ring.over(ring.over_core(piece), -1)
+    second = ring.over(piece, 1, 1)
     token = pick([0], [piece])
     for distance in range(1, far):
         first = in_order(first, token)
@@ -398,13 +423,12 @@
             after = ring.over(second, -1)
         token = pick([2 * distance - 1, 2 * distance], [first, second])
         first, second = onward, after
-    pick([chips - 1], [first])
-
-    weights = jnp.swapaxes(interp.reshape(blk_count, list_len * tile_rows, block_rows), 1, 2)
+    share((chips - 1) * slots, first, first)
+
     per_step = 4
     rows = per_step * block_rows
     grid_out = pl.pallas_call(
-        functools.partial(back_kernel, places, slots, list_len, per_step),
+        functools.partial(back_kernel, starts, list_len, per_step),
         out_shape=shape((blk_count * block_rows, width)),
         grid_spec=pltpu.PrefetchScalarGridSpec(
             num_scalar_prefetch=1,
@@ -416,8 +440,9 @@
             + [pl.BlockSpec(memory_space=pl.ANY)] * len(pieces),
             out_specs=pl.BlockSpec((rows, width), lambda i, *_: (i, 0)),
             scratch_shapes=[
-                pltpu.VMEM((entries, tile_rows, width), BF16),
-                pltpu.SemaphoreType.DMA((n_band,)),
+                pltpu.VMEM((N_CORE * ((chips - 1) * slots + tiles) * tile_rows, width), BF16),
+                pltpu.VMEM((rows, width), F32),
+                pltpu.SemaphoreType.DMA((len(pieces),)),
             ],
         ),
         compiler_params=params(20),
@@ -425,7 +450,7 @@
             2 * blk_count * block_rows * width * list_len * tile_rows, latent, latent, interp
         ),
         name="back",
-    )(table, latent, weights, *pieces)
+    )(table, in_hbm(latent), weights, *pieces)
     return (grid_out, mesh_out)
 
 

time: 87.4 us -> 80.2 us (0.918)
  starting transfers between devices: 29.6 us -> 21.9 us
  waiting for transfers between devices: 25.5 us -> 32.9 us
  local copies, waits for them, and re-layouts: 3.82 us -> 0.03 us
  Pallas kernels: 27.5 us -> 24.3 us
    ppermute x14, starting transfers between devices: 28.1 us -> 20.4 us  [over(): return lax.ppermute(value, 'band', pairs)]
    ppermute x14, waiting for transfers between devices: 23.1 us -> 29.4 us  [over(): return lax.ppermute(value, 'band', pairs)]
    pallas_call x6, Pallas kernels: 12.5 us -> 9.73 us  [the longest x1 6.81 us: on_device(): pl.pallas_call(functools.partial(back_kernel, starts, list_len, per_step)...]
    unnamed x10, local copies, waits for them, and re-layouts: 2.21 us -> 0.03 us
    reshape x1 -> x0, local copies, waits for them, and re-layouts: 1.61 us -> none  [on_device(): interp.reshape(blk_count, list_len * tile_rows, block_rows)]
    ppermute x8 -> x6, waiting for transfers between devices: 2.35 us -> 3.56 us  [over_core(): return lax.ppermute(value, 'band', [(i, i ^ 1) for i in range(self.n_band)])]
  transfers between devices with their start and end apart: 22 -> 20, of which waited for: 15 -> 15; matrix products, arithmetic and copies ran while one was open for 2% -> 0% of each run, Pallas kernels for 8% -> 6%
where the time goes in v8:
time: 80.2 us; the launch traced here: 80 us
  waiting for transfers between devices  32.9 us (41%)
  Pallas kernels  24.3 us (30%)
  starting transfers between devices  21.9 us (27%)
  between operations  0.81 us (1%)
    ppermute x14, waiting for transfers between devices, over(): return lax.ppermute(value, 'band', pairs)  29.4 us
    ppermute x14, starting transfers between devices, over(): return lax.ppermute(value, 'band', pairs)  20.4 us
    pallas_call x1, Pallas kernels, on_device(): pl.pallas_call(functools.partial(embed_kernel, ring, per_step, slots), ou...  10.7 us
    pallas_call x1, Pallas kernels, on_device(): pl.pallas_call(functools.partial(back_kernel, starts, list_len, per_step)...  6.81 us
    ppermute x6, waiting for transfers between devices, over_core(): return lax.ppermute(value, 'band', [(i, i ^ 1) for i in range(self.n_band)])  3.56 us
    pallas_call x4, Pallas kernels, pick(): pl.pallas_call(functools.partial(pick_kernel, chosen, slots, chips, tile_...  2.4 us
  transfers between devices with their start and end apart: 20, of which 15 were waited for; matrix products, arithmetic and copies ran while one was open for 0% of the time, Pallas kernels for 6%

profile of v8, /device:TPU:0, one launch (start us, length us, event | category | flops | bytes accessed | tf_op | source)
XLA Modules:
  0.0 80.0 jit_solution(11300737564878573819)
XLA Ops:
  0.6 10.7 %embed.1 = (bf16[4096,512]{1,0:T(8,128)(2,1)}, bf16[33,32,512]{2,1,0:T(8,128)(2,1)S(1)}, bf16[33,32,512]{2,1,0:T(8,128)(2,1)S(1)}, s32[4,64]{1,0:T(4,128)S(1)}) custom-call(s32[1]{0:T(128)} %bitcast.me_ref, s32[4,256]{1,0:T(4,128)} %bitcast.8, s32[4,256]{1,0:T(4,128)} %bitcast.9, bf16[227,4096]{1,0:T(8,128)(2,1)} %bitcast.7, bf16[227,512]{1,0:T(8,128)(2,1)} %w1_ref.1, ...), custom_call_target="tpu_custom_call" | custom-call | flops 3636461568 | bytes 2908160 | tf_op jit(solution)/shard_map/embed/pallas_call | solution.py:274
  11.8 2.3 %collective-permute-done.other = bf16[33,32,512]{2,1,0:T(8,128)(2,1)S(1)} collective-permute-done((bf16[33,32,512]{2,1,0:T(8,128)(2,1)S(1)}, bf16[33,32,512]{2,1,0:T(8,128)(2,1)S(1)}, u32[]{:S(2)}, u32[]{:S(2)}) %collective-permute-start) | collective-permute-done | bytes 1081376 | tf_op jit(solution)/shard_map/ppermute | solution.py:52
  14.2 0.8 far_sums.1
  15.0 3.0 %collective-permute-start.1 = (bf16[8,32,512]{2,1,0:T(8,128)(2,1)S(1)}, bf16[8,32,512]{2,1,0:T(8,128)(2,1)S(1)}, u32[]{:S(2)}, u32[]{:S(2)}) collective-permute-start(bf16[8,32,512]{2,1,0:T(8,128)(2,1)S(1)} %get-tuple-element.22), channel_id=1, source_target_pairs={{0,4},{1,3},{2,0},{3,7},{4,8},{5,1},{6,2},{7,11},{8,12},{9,5},{10,... | collective-permute-start | bytes 786440 | tf_op jit(solution)/shard_map/ppermute | solution.py:61
  18.0 1.6 %collective-permute-start.3 = (bf16[8,32,512]{2,1,0:T(8,128)(2,1)S(1)}, bf16[8,32,512]{2,1,0:T(8,128)(2,1)S(1)}, u32[]{:S(2)}, u32[]{:S(2)}) collective-permute-start(bf16[8,32,512]{2,1,0:T(8,128)(2,1)S(1)} %get-tuple-element.23), channel_id=1, source_target_pairs={{0,4},{1,3},{2,0},{3,7},{4,8},{5,1},{6,2},{7,11},{8,12},{9,5},{10,... | collective-permute-start | bytes 786440 | tf_op jit(solution)/shard_map/ppermute | solution.py:61
  19.5 1.3 %own_sums.1.token.own = f32[7,8,32,512]{3,2,1,0:T(8,128)S(1)} custom-call(s32[4,64]{1,0:T(4,128)S(1)} %get-tuple-element.18.table_ref, bf16[33,32,512]{2,1,0:T(8,128)(2,1)S(1)} %get-tuple-element.20.kept, bf16[33,32,512]{2,1,0:T(8,128)(2,1)S(1)} %collective-permute-done.other), custom_call_target="tpu_custom_call" | custom-call | bytes 4325376 | tf_op jit(solution)/shard_map/own_sums/pallas_call | solution.py:321
  21.4 0.9 %collective-permute-done.1.came = bf16[8,32,512]{2,1,0:T(8,128)(2,1)S(1)} collective-permute-done((bf16[8,32,512]{2,1,0:T(8,128)(2,1)S(1)}, bf16[8,32,512]{2,1,0:T(8,128)(2,1)S(1)}, u32[]{:S(2)}, u32[]{:S(2)}) %collective-permute-start.1) | collective-permute-done | bytes 262176 | tf_op jit(solution)/shard_map/ppermute | solution.py:61
  22.3 2.1 %collective-permute-start.2 = (bf16[8,32,512]{2,1,0:T(8,128)(2,1)S(1)}, bf16[8,32,512]{2,1,0:T(8,128)(2,1)S(1)}, u32[]{:S(2)}, u32[]{:S(2)}) collective-permute-start(bf16[8,32,512]{2,1,0:T(8,128)(2,1)S(1)} %add_5.1.token), channel_id=1, source_target_pairs={{0,4},{1,3},{2,0},{3,7},{4,8},{5,1},{6,2},{7,11},{8,12},{9,5},{10,... | collective-permute-start | bytes 786440 | tf_op jit(solution)/shard_map/ppermute | solution.py:61
  24.4 0.6 collective-permute-done.3.came
  25.1 2.1 %collective-permute-start.5 = (bf16[8,32,512]{2,1,0:T(8,128)(2,1)S(1)}, bf16[8,32,512]{2,1,0:T(8,128)(2,1)S(1)}, u32[]{:S(2)}, u32[]{:S(2)}) collective-permute-start(bf16[8,32,512]{2,1,0:T(8,128)(2,1)S(1)} %add_4.1.token), channel_id=1, source_target_pairs={{0,4},{1,3},{2,0},{3,7},{4,8},{5,1},{6,2},{7,11},{8,12},{9,5},{10,... | collective-permute-start | bytes 786440 | tf_op jit(solution)/shard_map/ppermute | solution.py:61
  27.2 1.5 %collective-permute-done.2.came = bf16[8,32,512]{2,1,0:T(8,128)(2,1)S(1)} collective-permute-done((bf16[8,32,512]{2,1,0:T(8,128)(2,1)S(1)}, bf16[8,32,512]{2,1,0:T(8,128)(2,1)S(1)}, u32[]{:S(2)}, u32[]{:S(2)}) %collective-permute-start.2) | collective-permute-done | bytes 262176 | tf_op jit(solution)/shard_map/ppermute | solution.py:61
  28.8 2.1 %collective-permute-start.4 = (bf16[8,32,512]{2,1,0:T(8,128)(2,1)S(1)}, bf16[8,32,512]{2,1,0:T(8,128)(2,1)S(1)}, u32[]{:S(2)}, u32[]{:S(2)}) collective-permute-start(bf16[8,32,512]{2,1,0:T(8,128)(2,1)S(1)} %add_3.1.token), channel_id=1, source_target_pairs={{0,4},{1,3},{2,0},{3,7},{4,8},{5,1},{6,2},{7,11},{8,12},{9,5},{10,... | collective-permute-start | bytes 786440 | tf_op jit(solution)/shard_map/ppermute | solution.py:61
  30.9 0.6 collective-permute-done.5.came
  31.8 3.4 %collective-permute-done.4.came = bf16[8,32,512]{2,1,0:T(8,128)(2,1)S(1)} collective-permute-done((bf16[8,32,512]{2,1,0:T(8,128)(2,1)S(1)}, bf16[8,32,512]{2,1,0:T(8,128)(2,1)S(1)}, u32[]{:S(2)}, u32[]{:S(2)}) %collective-permute-start.4) | collective-permute-done | bytes 262176 | tf_op jit(solution)/shard_map/ppermute | solution.py:61
  35.3 2.1 %collective-permute-start.6 = (bf16[8,32,512]{2,1,0:T(8,128)(2,1)S(1)}, bf16[8,32,512]{2,1,0:T(8,128)(2,1)S(1)}, u32[]{:S(2)}, u32[]{:S(2)}) collective-permute-start(bf16[8,32,512]{2,1,0:T(8,128)(2,1)S(1)} %add_1.1), channel_id=1, source_target_pairs={{0,4},{1,3},{2,0},{3,7},{4,8},{5,1},{6,2},{7,11},{8,12},{9,5},{10,... | collective-permute-start | bytes 786440 | tf_op jit(solution)/shard_map/ppermute | solution.py:61
  37.6 4.1 %collective-permute-done.6.came = bf16[8,32,512]{2,1,0:T(8,128)(2,1)S(1)} collective-permute-done((bf16[8,32,512]{2,1,0:T(8,128)(2,1)S(1)}, bf16[8,32,512]{2,1,0:T(8,128)(2,1)S(1)}, u32[]{:S(2)}, u32[]{:S(2)}) %collective-permute-start.6) | collective-permute-done | bytes 262176 | tf_op jit(solution)/shard_map/ppermute | solution.py:61
  41.7 1.5 %mesh_step.1 = (bf16[256,512]{1,0:T(8,128)(2,1)}, bf16[256,512]{1,0:T(8,128)(2,1)S(1)}) custom-call(bf16[256,512]{1,0:T(8,128)(2,1)S(1)} %copy-done.3, bf16[512,512]{1,0:T(8,128)(2,1)S(1)} %copy-done.1, bf16[512,512]{1,0:T(8,128)(2,1)S(1)} %copy-done.2, f32[1,512]{1,0:T(1,128)S(1)} %bitcast.6, f32[7,8,32,512]{3,2,1,0:T(8,128)S(1)} %own_sums.1.token.own, ...), custom_call_target="tpu_custom_call" | custom-call | flops 268435456 | bytes 1048576 | tf_op jit(solution)/shard_map/mesh_step/pallas_call | solution.py:380
  43.2 2.0 %collective-permute-start.9 = (bf16[256,512]{1,0:T(8,128)(2,1)S(1)}, bf16[256,512]{1,0:T(8,128)(2,1)S(1)}, u32[]{:S(2)}, u32[]{:S(2)}) collective-permute-start(bf16[256,512]{1,0:T(8,128)(2,1)S(1)} %get-tuple-element.24.refs_0_), channel_id=1, source_target_pairs={{0,2},{1,5},{2,6},{3,1},{4,0},{5,9},{6,10},{7,3},{8,4},{9,13},{10,... | collective-permute-start | bytes 786440 | tf_op jit(solution)/shard_map/ppermute | solution.py:61
  45.2 0.6 pick_0.1
  45.9 4.4 %collective-permute-done.9.refs_0_ = bf16[256,512]{1,0:T(8,128)(2,1)S(1)} collective-permute-done((bf16[256,512]{1,0:T(8,128)(2,1)S(1)}, bf16[256,512]{1,0:T(8,128)(2,1)S(1)}, u32[]{:S(2)}, u32[]{:S(2)}) %collective-permute-start.9) | collective-permute-done | bytes 262176 | tf_op jit(solution)/shard_map/ppermute | solution.py:61
  50.3 2.4 %collective-permute-start.12 = (bf16[256,512]{1,0:T(8,128)(2,1)S(1)}, bf16[256,512]{1,0:T(8,128)(2,1)S(1)}, u32[]{:S(2)}, u32[]{:S(2)}) collective-permute-start(bf16[256,512]{1,0:T(8,128)(2,1)S(1)} %in_order.6.refs_1_.refs_0_), channel_id=1, source_target_pairs={{0,2},{1,5},{2,6},{3,1},{4,0},{5,9},{6,10},{7,3},{8,4},{9,13},{10,... | collective-permute-start | bytes 786440 | tf_op jit(solution)/shard_map/ppermute | solution.py:61
  52.6 1.7 %collective-permute-start.13 = (bf16[256,512]{1,0:T(8,128)(2,1)S(1)}, bf16[256,512]{1,0:T(8,128)(2,1)S(1)}, u32[]{:S(2)}, u32[]{:S(2)}) collective-permute-start(bf16[256,512]{1,0:T(8,128)(2,1)S(1)} %in_order.7.refs_1_), channel_id=1, source_target_pairs={{0,2},{1,5},{2,6},{3,1},{4,0},{5,9},{6,10},{7,3},{8,4},{9,13},{10,... | collective-permute-start | bytes 786440 | tf_op jit(solution)/shard_map/ppermute | solution.py:61
  54.4 0.6 pick_1.1
  55.0 3.7 %collective-permute-done.12.refs_0_ = bf16[256,512]{1,0:T(8,128)(2,1)S(1)} collective-permute-done((bf16[256,512]{1,0:T(8,128)(2,1)S(1)}, bf16[256,512]{1,0:T(8,128)(2,1)S(1)}, u32[]{:S(2)}, u32[]{:S(2)}) %collective-permute-start.12) | collective-permute-done | bytes 262176 | tf_op jit(solution)/shard_map/ppermute | solution.py:61
  59.0 2.5 %collective-permute-done.13.refs_0_ = bf16[256,512]{1,0:T(8,128)(2,1)S(1)} collective-permute-done((bf16[256,512]{1,0:T(8,128)(2,1)S(1)}, bf16[256,512]{1,0:T(8,128)(2,1)S(1)}, u32[]{:S(2)}, u32[]{:S(2)}) %collective-permute-start.13) | collective-permute-done | bytes 262176 | tf_op jit(solution)/shard_map/ppermute | solution.py:61
  61.8 0.6 pick_3.1
  62.4 2.6 %collective-permute-done.15.refs_0_ = bf16[256,512]{1,0:T(8,128)(2,1)S(1)} collective-permute-done((bf16[256,512]{1,0:T(8,128)(2,1)S(1)}, bf16[256,512]{1,0:T(8,128)(2,1)S(1)}, u32[]{:S(2)}, u32[]{:S(2)}) %collective-permute-start.15) | collective-permute-done | bytes 262176 | tf_op jit(solution)/shard_map/ppermute | solution.py:61
  65.9 2.0 %collective-permute-done.16.refs_0_ = bf16[256,512]{1,0:T(8,128)(2,1)S(1)} collective-permute-done((bf16[256,512]{1,0:T(8,128)(2,1)S(1)}, bf16[256,512]{1,0:T(8,128)(2,1)S(1)}, u32[]{:S(2)}, u32[]{:S(2)}) %collective-permute-start.16) | collective-permute-done | bytes 262176 | tf_op jit(solution)/shard_map/ppermute | solution.py:61
  67.9 0.6 pick_5.1
  68.6 2.9 %collective-permute-done.18.rest_8_ = bf16[256,512]{1,0:T(8,128)(2,1)S(1)} collective-permute-done((bf16[256,512]{1,0:T(8,128)(2,1)S(1)}, bf16[256,512]{1,0:T(8,128)(2,1)S(1)}, u32[]{:S(2)}, u32[]{:S(2)}) %collective-permute-start.18) | collective-permute-done | bytes 262176 | tf_op jit(solution)/shard_map/ppermute | solution.py:61
  72.0 1.2 %collective-permute-done.8.rest_1_ = bf16[128,512]{1,0:T(8,128)(2,1)S(1)} collective-permute-done((bf16[128,512]{1,0:T(8,128)(2,1)S(1)}, bf16[128,512]{1,0:T(8,128)(2,1)S(1)}, u32[]{:S(2)}, u32[]{:S(2)}) %collective-permute-start.8) | collective-permute-done | bytes 131104 | tf_op jit(solution)/shard_map/ppermute | solution.py:52
  73.2 6.8 %back.1 = bf16[4096,512]{1,0:T(8,128)(2,1)} custom-call(s32[4,64]{1,0:T(4,128)S(1)} %get-tuple-element.18.table_ref, bf16[4096,512]{1,0:T(8,128)(2,1)} %get-tuple-element.19.latent_ref, bf16[16,256,128]{2,1,0:T(8,128)(2,1)S(1)} %turn.1.token.weights_ref, bf16[128,512]{1,0:T(8,128)(2,1)S(1)} %get-tuple-element.25.refs_1_.rest_0_, ...), custom_call_target="tpu_custom_call" | custom-call | flops 536870912 | bytes 9437184 | tf_op jit(solution)/shard_map/back/pallas_call | solution.py:430
  (39 shorter events, 3.8 us)
Async XLA Ops:
  11.4 2.8 %collective-permute-start = (bf16[33,32,512]{2,1,0:T(8,128)(2,1)S(1)}, bf16[33,32,512]{2,1,0:T(8,128)(2,1)S(1)}, u32[]{:S(2)}, u32[]{:S(2)}) collective-permute-start(bf16[33,32,512]{2,1,0:T(8,128)(2,1)S(1)} %get-tuple-element.21), channel_id=1, source_target_pairs={{0,1},{1,0},{2,3},{3,2},{4,5},{5,4},{6,7},{7,6},{8,9},{9,8},{10,11... | collective-permute-start | bytes 3244040 | tf_op jit(solution)/shard_map/ppermute | solution.py:52
  15.0 7.3 %collective-permute-start.1 = (bf16[8,32,512]{2,1,0:T(8,128)(2,1)S(1)}, bf16[8,32,512]{2,1,0:T(8,128)(2,1)S(1)}, u32[]{:S(2)}, u32[]{:S(2)}) collective-permute-start(bf16[8,32,512]{2,1,0:T(8,128)(2,1)S(1)} %get-tuple-element.22), channel_id=1, source_target_pairs={{0,4},{1,3},{2,0},{3,7},{4,8},{5,1},{6,2},{7,11},{8,12},{9,5},{10,... | collective-permute-start | bytes 786440 | tf_op jit(solution)/shard_map/ppermute | solution.py:61
  17.9 2.9 %copy-start = (bf16[16,4,32,256]{3,2,1,0:T(8,128)(2,1)S(1)}, bf16[16,4,32,256]{3,2,1,0:T(8,128)(2,1)}, u32[]{:S(2)}) copy-start(bf16[16,4,32,256]{3,2,1,0:T(8,128)(2,1)} %interp_ref.3) | copy-start | bytes 3145732
  18.0 7.1 %collective-permute-start.3 = (bf16[8,32,512]{2,1,0:T(8,128)(2,1)S(1)}, bf16[8,32,512]{2,1,0:T(8,128)(2,1)S(1)}, u32[]{:S(2)}, u32[]{:S(2)}) collective-permute-start(bf16[8,32,512]{2,1,0:T(8,128)(2,1)S(1)} %get-tuple-element.23), channel_id=1, source_target_pairs={{0,4},{1,3},{2,0},{3,7},{4,8},{5,1},{6,2},{7,11},{8,12},{9,5},{10,... | collective-permute-start | bytes 786440 | tf_op jit(solution)/shard_map/ppermute | solution.py:61
  22.3 6.4 %collective-permute-start.2 = (bf16[8,32,512]{2,1,0:T(8,128)(2,1)S(1)}, bf16[8,32,512]{2,1,0:T(8,128)(2,1)S(1)}, u32[]{:S(2)}, u32[]{:S(2)}) collective-permute-start(bf16[8,32,512]{2,1,0:T(8,128)(2,1)S(1)} %add_5.1.token), channel_id=1, source_target_pairs={{0,4},{1,3},{2,0},{3,7},{4,8},{5,1},{6,2},{7,11},{8,12},{9,5},{10,... | collective-permute-start | bytes 786440 | tf_op jit(solution)/shard_map/ppermute | solution.py:61
  25.1 6.4 %collective-permute-start.5 = (bf16[8,32,512]{2,1,0:T(8,128)(2,1)S(1)}, bf16[8,32,512]{2,1,0:T(8,128)(2,1)S(1)}, u32[]{:S(2)}, u32[]{:S(2)}) collective-permute-start(bf16[8,32,512]{2,1,0:T(8,128)(2,1)S(1)} %add_4.1.token), channel_id=1, source_target_pairs={{0,4},{1,3},{2,0},{3,7},{4,8},{5,1},{6,2},{7,11},{8,12},{9,5},{10,... | collective-permute-start | bytes 786440 | tf_op jit(solution)/shard_map/ppermute | solution.py:61
  28.8 6.4 %collective-permute-start.4 = (bf16[8,32,512]{2,1,0:T(8,128)(2,1)S(1)}, bf16[8,32,512]{2,1,0:T(8,128)(2,1)S(1)}, u32[]{:S(2)}, u32[]{:S(2)}) collective-permute-start(bf16[8,32,512]{2,1,0:T(8,128)(2,1)S(1)} %add_3.1.token), channel_id=1, source_target_pairs={{0,4},{1,3},{2,0},{3,7},{4,8},{5,1},{6,2},{7,11},{8,12},{9,5},{10,... | collective-permute-start | bytes 786440 | tf_op jit(solution)/shard_map/ppermute | solution.py:61
  31.6 10.1 %copy-start.1 = (bf16[512,512]{1,0:T(8,128)(2,1)S(1)}, bf16[512,512]{1,0:T(8,128)(2,1)}, u32[]{:S(2)}) copy-start(bf16[512,512]{1,0:T(8,128)(2,1)} %up_ref.1) | copy-start | bytes 1572868
  31.6 10.1 %copy-start.2 = (bf16[512,512]{1,0:T(8,128)(2,1)S(1)}, bf16[512,512]{1,0:T(8,128)(2,1)}, u32[]{:S(2)}) copy-start(bf16[512,512]{1,0:T(8,128)(2,1)} %down_ref.1) | copy-start | bytes 1572868
  31.6 10.1 %copy-start.3 = (bf16[256,512]{1,0:T(8,128)(2,1)S(1)}, bf16[256,512]{1,0:T(8,128)(2,1)}, u32[]{:S(2)}) copy-start(bf16[256,512]{1,0:T(8,128)(2,1)} %latent_ref.1) | copy-start | bytes 786436
  31.6 10.1 %copy-start.4 = (f32[512]{0:T(512)S(1)}, f32[512]{0:T(512)}, u32[]{:S(2)}) copy-start(f32[512]{0:T(512)} %param.21) | copy-start | bytes 6148
  31.7 6.0 %collective-permute-start.7 = (bf16[8,32,512]{2,1,0:T(8,128)(2,1)S(1)}, bf16[8,32,512]{2,1,0:T(8,128)(2,1)S(1)}, u32[]{:S(2)}, u32[]{:S(2)}) collective-permute-start(bf16[8,32,512]{2,1,0:T(8,128)(2,1)S(1)} %add_2.1.token), channel_id=1, source_target_pairs={{0,5},{1,2},{2,1},{3,6},{4,9},{5,0},{6,3},{7,10},{8,13},{9,4},{10,... | collective-permute-start | bytes 786440 | tf_op jit(solution)/shard_map/ppermute | solution.py:61
  35.3 6.4 %collective-permute-start.6 = (bf16[8,32,512]{2,1,0:T(8,128)(2,1)S(1)}, bf16[8,32,512]{2,1,0:T(8,128)(2,1)S(1)}, u32[]{:S(2)}, u32[]{:S(2)}) collective-permute-start(bf16[8,32,512]{2,1,0:T(8,128)(2,1)S(1)} %add_1.1), channel_id=1, source_target_pairs={{0,4},{1,3},{2,0},{3,7},{4,8},{5,1},{6,2},{7,11},{8,12},{9,5},{10,... | collective-permute-start | bytes 786440 | tf_op jit(solution)/shard_map/ppermute | solution.py:61
  43.2 7.1 %collective-permute-start.9 = (bf16[256,512]{1,0:T(8,128)(2,1)S(1)}, bf16[256,512]{1,0:T(8,128)(2,1)S(1)}, u32[]{:S(2)}, u32[]{:S(2)}) collective-permute-start(bf16[256,512]{1,0:T(8,128)(2,1)S(1)} %get-tuple-element.24.refs_0_), channel_id=1, source_target_pairs={{0,2},{1,5},{2,6},{3,1},{4,0},{5,9},{6,10},{7,3},{8,4},{9,13},{10,... | collective-permute-start | bytes 786440 | tf_op jit(solution)/shard_map/ppermute | solution.py:61
  45.8 6.9 %collective-permute-start.10 = (bf16[256,512]{1,0:T(8,128)(2,1)S(1)}, bf16[256,512]{1,0:T(8,128)(2,1)S(1)}, u32[]{:S(2)}, u32[]{:S(2)}) collective-permute-start(bf16[256,512]{1,0:T(8,128)(2,1)S(1)} %get-tuple-element.24.refs_0_), channel_id=1, source_target_pairs={{0,5},{1,2},{2,1},{3,6},{4,9},{5,0},{6,3},{7,10},{8,13},{9,4},{10,... | collective-permute-start | bytes 786440 | tf_op jit(solution)/shard_map/ppermute | solution.py:61
  50.3 8.4 %collective-permute-start.12 = (bf16[256,512]{1,0:T(8,128)(2,1)S(1)}, bf16[256,512]{1,0:T(8,128)(2,1)S(1)}, u32[]{:S(2)}, u32[]{:S(2)}) collective-permute-start(bf16[256,512]{1,0:T(8,128)(2,1)S(1)} %in_order.6.refs_1_.refs_0_), channel_id=1, source_target_pairs={{0,2},{1,5},{2,6},{3,1},{4,0},{5,9},{6,10},{7,3},{8,4},{9,13},{10,... | collective-permute-start | bytes 786440 | tf_op jit(solution)/shard_map/ppermute | solution.py:61
  52.6 8.9 %collective-permute-start.13 = (bf16[256,512]{1,0:T(8,128)(2,1)S(1)}, bf16[256,512]{1,0:T(8,128)(2,1)S(1)}, u32[]{:S(2)}, u32[]{:S(2)}) collective-permute-start(bf16[256,512]{1,0:T(8,128)(2,1)S(1)} %in_order.7.refs_1_), channel_id=1, source_target_pairs={{0,2},{1,5},{2,6},{3,1},{4,0},{5,9},{6,10},{7,3},{8,4},{9,13},{10,... | collective-permute-start | bytes 786440 | tf_op jit(solution)/shard_map/ppermute | solution.py:61
  58.7 6.4 %collective-permute-start.15 = (bf16[256,512]{1,0:T(8,128)(2,1)S(1)}, bf16[256,512]{1,0:T(8,128)(2,1)S(1)}, u32[]{:S(2)}, u32[]{:S(2)}) collective-permute-start(bf16[256,512]{1,0:T(8,128)(2,1)S(1)} %in_order.8.refs_1_.refs_0_), channel_id=1, source_target_pairs={{0,2},{1,5},{2,6},{3,1},{4,0},{5,9},{6,10},{7,3},{8,4},{9,13},{10,... | collective-permute-start | bytes 786440 | tf_op jit(solution)/shard_map/ppermute | solution.py:61
  61.5 6.4 %collective-permute-start.16 = (bf16[256,512]{1,0:T(8,128)(2,1)S(1)}, bf16[256,512]{1,0:T(8,128)(2,1)S(1)}, u32[]{:S(2)}, u32[]{:S(2)}) collective-permute-start(bf16[256,512]{1,0:T(8,128)(2,1)S(1)} %in_order.9.refs_1_), channel_id=1, source_target_pairs={{0,2},{1,5},{2,6},{3,1},{4,0},{5,9},{6,10},{7,3},{8,4},{9,13},{10,... | collective-permute-start | bytes 786440 | tf_op jit(solution)/shard_map/ppermute | solution.py:61
  65.1 6.4 %collective-permute-start.18 = (bf16[256,512]{1,0:T(8,128)(2,1)S(1)}, bf16[256,512]{1,0:T(8,128)(2,1)S(1)}, u32[]{:S(2)}, u32[]{:S(2)}) collective-permute-start(bf16[256,512]{1,0:T(8,128)(2,1)S(1)} %in_order.10.refs_1_.refs_0_), channel_id=1, source_target_pairs={{0,2},{1,5},{2,6},{3,1},{4,0},{5,9},{6,10},{7,3},{8,4},{9,13},{10,... | collective-permute-start | bytes 786440 | tf_op jit(solution)/shard_map/ppermute | solution.py:61
  65.4 7.8 %collective-permute-start.11 = (bf16[256,512]{1,0:T(8,128)(2,1)S(1)}, bf16[256,512]{1,0:T(8,128)(2,1)S(1)}, u32[]{:S(2)}, u32[]{:S(2)}) collective-permute-start(bf16[256,512]{1,0:T(8,128)(2,1)S(1)} %get-tuple-element.28), channel_id=1, source_target_pairs={{0,1},{1,0},{2,3},{3,2},{4,5},{5,4},{6,7},{7,6},{8,9},{9,8},{10,11... | collective-permute-start | bytes 786440 | tf_op jit(solution)/shard_map/ppermute | solution.py:52
  65.4 7.8 %collective-permute-start.14 = (bf16[256,512]{1,0:T(8,128)(2,1)S(1)}, bf16[256,512]{1,0:T(8,128)(2,1)S(1)}, u32[]{:S(2)}, u32[]{:S(2)}) collective-permute-start(bf16[256,512]{1,0:T(8,128)(2,1)S(1)} %get-tuple-element.30), channel_id=1, source_target_pairs={{0,1},{1,0},{2,3},{3,2},{4,5},{5,4},{6,7},{7,6},{8,9},{9,8},{10,11... | collective-permute-start | bytes 786440 | tf_op jit(solution)/shard_map/ppermute | solution.py:52
  68.5 4.7 %collective-permute-start.17 = (bf16[256,512]{1,0:T(8,128)(2,1)S(1)}, bf16[256,512]{1,0:T(8,128)(2,1)S(1)}, u32[]{:S(2)}, u32[]{:S(2)}) collective-permute-start(bf16[256,512]{1,0:T(8,128)(2,1)S(1)} %get-tuple-element.32), channel_id=1, source_target_pairs={{0,1},{1,0},{2,3},{3,2},{4,5},{5,4},{6,7},{7,6},{8,9},{9,8},{10,11... | collective-permute-start | bytes 786440 | tf_op jit(solution)/shard_map/ppermute | solution.py:52
  71.4 1.7 %collective-permute-start.19 = (bf16[256,512]{1,0:T(8,128)(2,1)S(1)}, bf16[256,512]{1,0:T(8,128)(2,1)S(1)}, u32[]{:S(2)}, u32[]{:S(2)}) collective-permute-start(bf16[256,512]{1,0:T(8,128)(2,1)S(1)} %collective-permute-done.18.rest_8_), channel_id=1, source_target_pairs={{0,1},{1,0},{2,3},{3,2},{4,5},{5,4},{6,7},{7,6},{8,9},{9,8},{10,11... | collective-permute-start | bytes 786440 | tf_op jit(solution)/shard_map/ppermute | solution.py:52
  71.4 1.7 %collective-permute-start.8 = (bf16[128,512]{1,0:T(8,128)(2,1)S(1)}, bf16[128,512]{1,0:T(8,128)(2,1)S(1)}, u32[]{:S(2)}, u32[]{:S(2)}) collective-permute-start(bf16[128,512]{1,0:T(8,128)(2,1)S(1)} %get-tuple-element.26), channel_id=1, source_target_pairs={{0,1},{1,0},{2,3},{3,2},{4,5},{5,4},{6,7},{7,6},{8,9},{9,8},{10,11... | collective-permute-start | bytes 393224 | tf_op jit(solution)/shard_map/ppermute | solution.py:52

commit v9 on v8

--- a/solution.py
+++ b/solution.py
@@ -11,7 +11,7 @@
 BF16 = jnp.bfloat16
 N_CORE = 2
 STRIP = 32
-PART = 2
+PART = 4
 
 
 def silu(values):
@@ -80,7 +80,7 @@
 def embed_kernel(
     ring, per_step, slots, me_ref, lists_ref, mask_ref,
     x_ref, w1_ref, w2_ref, gain_ref, interp_ref,
-    latent_ref, kept_ref, sent_ref, table_ref, wide, hidden,
+    latent_ref, kept_ref, far_ref, rest_ref, table_ref, wide, hidden,
 ):
     step = pl.program_id(0)
     me = me_ref[0]
@@ -103,7 +103,7 @@
         for strip in strips(rows):
             hidden[strip] = silu(wide[strip]).astype(BF16)
         wide[rows] = jnp.dot(hidden[rows], w2_ref[...], preferred_element_type=F32)
-    spare = kept_ref.shape[0] - 1
+    kept_spare, far_spare, rest_spare = (ref.shape[0] - 1 for ref in (kept_ref, far_ref, rest_ref))
     for number, rows in enumerate(spans):
         for strip in strips(rows):
             latent_ref[strip] = layer_norm(wide[strip], gain_ref[...]).astype(BF16)
@@ -126,21 +126,24 @@
                 table_ref[1, (across * groups + group) * slots + slot] = tile
                 masked = part[k * tile_rows : (k + 1) * tile_rows] * mask.astype(F32)
                 masked = masked.astype(BF16)
-                kept_ref[jnp.minimum(place, spare)] = masked
-                sent_ref[jnp.where(place >= spare, place - spare, spare)] = masked
-
-
-def add_entries(total, table_ref, group, slots, kept, other, groups):
+                kept_ref[jnp.minimum(place, kept_spare)] = masked
+                there = place - kept_spare
+                rest_ref[jnp.where(there < 0, rest_spare, jnp.minimum(there, rest_spare))] = masked
+                beyond = there - rest_spare
+                far_ref[jnp.where(beyond < 0, far_spare, beyond)] = masked
+
+
+def add_entries(total, table_ref, group, slots, kept, other, groups, first=0):
     for slot in range(slots):
         place = group * slots + slot
         total[table_ref[0, place]] += kept[place].astype(F32)
-        total[table_ref[1, groups * slots + place]] += other[place].astype(F32)
+        total[table_ref[1, groups * slots + place]] += other[place - first * slots].astype(F32)
 
 
 def far_kernel(slots, groups, table_ref, kept, other, far, before, total):
     for group, out in ((groups - 1, far), (groups - 2, before)):
         total[...] = jnp.zeros_like(total)
-        add_entries(total, table_ref, group, slots, kept, other, groups)
+        add_entries(total, table_ref, group, slots, kept, other, groups, groups - 2)
         out[...] = total[...].astype(BF16)
 
 
@@ -268,13 +271,13 @@
         return pltpu.with_memory_space_constraint(array, pltpu.HBM)
 
     gain = embed_gain.reshape(1, width)
-    per_step = 4
+    per_step = 8
     rows = per_step * block_rows
-    held_shape = (chips * slots + 1, tile_rows, width)
-    latent, kept, sent, table = pl.pallas_call(
+    counts = (chips * slots, 2 * slots, (chips - 2) * slots)
+    latent, kept, sent_far, sent_rest, table = pl.pallas_call(
         functools.partial(embed_kernel, ring, per_step, slots),
         out_shape=[pltpu.HBM((blk_count * block_rows, width), BF16)]
-        + [shape(held_shape)] * N_CORE
+        + [shape((count + 1, tile_rows, width)) for count in counts]
         + [shape((4, entries), jnp.int32)],
         grid_spec=pltpu.PrefetchScalarGridSpec(
             num_scalar_prefetch=3,
@@ -287,11 +290,11 @@
                 pl.BlockSpec((per_step,) + interp.shape[1:], lambda i, *_: (i, 0, 0, 0)),
             ],
             out_specs=[pl.BlockSpec((rows, width), lambda i, *_: (i, 0))]
-            + [pl.BlockSpec(memory_space=pltpu.VMEM)] * N_CORE
+            + [pl.BlockSpec(memory_space=pltpu.VMEM)] * len(counts)
             + [pl.BlockSpec(memory_space=pltpu.SMEM)],
             scratch_shapes=[pltpu.VMEM((rows, width), F32), pltpu.VMEM((rows, width), BF16)],
         ),
-        compiler_params=params(24),
+        compiler_params=params(32),
         cost_estimate=cost(
             2 * blk_count * block_rows * width * (channels + width + list_len * tile_rows),
             grid_features,
@@ -299,39 +302,11 @@
         ),
         name="embed",
     )(lists[0], *map(in_hbm, lists[1:] + (grid_features.T, embed_in, embed_out, gain, interp)))
-    other = ring.over_core(sent)
+    other_far = ring.over_core(sent_far)
 
     dense = (tiles, tile_rows, width)
     in_vmem = pl.BlockSpec(memory_space=pltpu.VMEM)
     in_any = pl.BlockSpec(memory_space=pl.ANY)
-    first, second = pl.pallas_call(
-        functools.partial(far_kernel, slots, chips),
-        out_shape=[shape(dense)] * 2,
-        grid_spec=pltpu.PrefetchScalarGridSpec(
-            num_scalar_prefetch=1,
-            grid=(1,),
-            in_specs=[in_vmem] * 2,
-            out_specs=[in_vmem] * 2,
-            scratch_shapes=[pltpu.VMEM(dense, F32)],
-        ),
-        compiler_params=params(8),
-        cost_estimate=cost(0, kept),
-        name="far_sums",
-    )(table, kept, other)
-    own = pl.pallas_call(
-        functools.partial(own_kernel, slots, chips),
-        out_shape=shape((chips - 1,) + dense, F32),
-        grid_spec=pltpu.PrefetchScalarGridSpec(
-            num_scalar_prefetch=1,
-            grid=(chips - 1,),
-            in_specs=[in_vmem] * 2,
-            out_specs=in_vmem,
-        ),
-        compiler_params=params(8 if n_band <= 16 else 24),
-        cost_estimate=cost(0, kept, kept, kept, kept),
-        name="own_sums",
-    )(table, kept, other)
-
     def in_order(value, token):
         return pl.pallas_call(
             order_kernel,
@@ -343,6 +318,35 @@
             cost_estimate=cost(0),
             name="in_order",
         )(value, token)
+
+    first, second = pl.pallas_call(
+        functools.partial(far_kernel, slots, chips),
+        out_shape=[shape(dense)] * 2,
+        grid_spec=pltpu.PrefetchScalarGridSpec(
+            num_scalar_prefetch=1,
+            grid=(1,),
+            in_specs=[in_vmem] * 2,
+            out_specs=[in_vmem] * 2,
+            scratch_shapes=[pltpu.VMEM(dense, F32)],
+        ),
+        compiler_params=params(8),
+        cost_estimate=cost(0, kept),
+        name="far_sums",
+    )(table, kept, other_far)
+    other_rest = ring.over_core(in_order(sent_rest, first))
+    own = pl.pallas_call(
+        functools.partial(own_kernel, slots, chips),
+        out_shape=shape((chips - 2,) + dense, F32),
+        grid_spec=pltpu.PrefetchScalarGridSpec(
+            num_scalar_prefetch=1,
+            grid=(chips - 2,),
+            in_specs=[in_vmem] * 2,
+            out_specs=in_vmem,
+        ),
+        compiler_params=params(8 if n_band <= 16 else 24),
+        cost_estimate=cost(0, kept, kept, kept, kept),
+        name="own_sums",
+    )(table, kept, other_rest)
 
     def add_own(group, value, token):
         return pl.pallas_call(
@@ -414,14 +418,17 @@
 
     first = ring.over(piece, -1)
     second = ring.over(piece, 1, 1)
-    token = pick([0], [piece])
+    token = piece
     for distance in range(1, far):
         first = in_order(first, token)
         onward = ring.over(first, -1)
         second = in_order(second, first)
         if distance < far - 1:
             after = ring.over(second, -1)
-        token = pick([2 * distance - 1, 2 * distance], [first, second])
+        chosen, values = [2 * distance - 1, 2 * distance], [first, second]
+        if distance == 1:
+            chosen, values = [0] + chosen, [piece] + values
+        token = pick(chosen, values)
         first, second = onward, after
     share((chips - 1) * slots, first, first)
 

time: 80.2 us -> 78.6 us (0.980)
  waiting for transfers between devices: 32.9 us -> 28.7 us
  starting transfers between devices: 21.9 us -> 25.2 us
    ppermute x14, waiting for transfers between devices: 29.4 us -> 26 us  [over(): return lax.ppermute(value, 'band', pairs)]
    ppermute x14, starting transfers between devices: 20.4 us -> 23.8 us  [over(): return lax.ppermute(value, 'band', pairs)]
    ppermute x6, waiting for transfers between devices: 3.56 us -> 2.73 us  [over_core(): return lax.ppermute(value, 'band', [(i, i ^ 1) for i in range(self.n_band)])]
    pallas_call x4 -> x3, Pallas kernels: 2.4 us -> 1.83 us  [pick(): pl.pallas_call(functools.partial(pick_kernel, chosen, slots, chips, tile_...]
  transfers between devices with their start and end apart: 20 -> 20, of which waited for: 15 -> 15; matrix products, arithmetic and copies ran while one was open for 0% -> 0% of each run, Pallas kernels for 6% -> 5%
where the time goes in v9:
time: 78.6 us; the launch traced here: 78.4 us
  waiting for transfers between devices  28.7 us (37%)
  starting transfers between devices  25.2 us (32%)
  Pallas kernels  23.6 us (30%)
  between operations  0.81 us (1%)
    ppermute x14, waiting for transfers between devices, over(): return lax.ppermute(value, 'band', pairs)  26 us
    ppermute x14, starting transfers between devices, over(): return lax.ppermute(value, 'band', pairs)  23.8 us
    pallas_call x1, Pallas kernels, on_device(): pl.pallas_call(functools.partial(embed_kernel, ring, per_step, slots), ou...  10.7 us
    pallas_call x1, Pallas kernels, on_device(): pl.pallas_call(functools.partial(back_kernel, starts, list_len, per_step)...  6.82 us
    ppermute x6, waiting for transfers between devices, over_core(): return lax.ppermute(value, 'band', [(i, i ^ 1) for i in range(self.n_band)])  2.73 us
    pallas_call x3, Pallas kernels, pick(): pl.pallas_call(functools.partial(pick_kernel, chosen, slots, chips, tile_...  1.83 us
  transfers between devices with their start and end apart: 20, of which 15 were waited for; matrix products, arithmetic and copies ran while one was open for 0% of the time, Pallas kernels for 5%

profile of v9, /device:TPU:0, one launch (start us, length us, event | category | flops | bytes accessed | tf_op | source)
XLA Modules:
  0.0 78.4 jit_solution(9561461720514600512)
XLA Ops:
  0.6 10.7 %embed.1 = (bf16[4096,512]{1,0:T(8,128)(2,1)}, bf16[33,32,512]{2,1,0:T(8,128)(2,1)S(1)}, bf16[9,32,512]{2,1,0:T(8,128)(2,1)S(1)}, bf16[25,32,512]{2,1,0:T(8,128)(2,1)S(1)}, s32[4,64]{1,0:T(4,128)S(1)}) custom-call(s32[1]{0:T(128)} %bitcast.me_ref, s32[4,256]{1,0:T(4,128)} %bitcast.8, s32[4,256]{1,0:T(4,128)} %bitcast.9, bf16[227,4096]{1,0:T(8,128)(2,1)} %bitcast.7, ...), custom_call_target="tpu_custom_call" | custom-call | flops 3636461568 | bytes 2908160 | tf_op jit(solution)/shard_map/embed/pallas_call | solution.py:277
  11.8 1.2 %collective-permute-done.other = bf16[9,32,512]{2,1,0:T(8,128)(2,1)S(1)} collective-permute-done((bf16[9,32,512]{2,1,0:T(8,128)(2,1)S(1)}, bf16[9,32,512]{2,1,0:T(8,128)(2,1)S(1)}, u32[]{:S(2)}, u32[]{:S(2)}) %collective-permute-start) | collective-permute-done | bytes 294944 | tf_op jit(solution)/shard_map/ppermute | solution.py:52
  13.0 0.8 %far_sums.1 = (bf16[8,32,512]{2,1,0:T(8,128)(2,1)S(1)}, bf16[8,32,512]{2,1,0:T(8,128)(2,1)S(1)}) custom-call(s32[4,64]{1,0:T(4,128)S(1)} %get-tuple-element.17.table_ref, bf16[33,32,512]{2,1,0:T(8,128)(2,1)S(1)} %get-tuple-element.19.kept, bf16[9,32,512]{2,1,0:T(8,128)(2,1)S(1)} %collective-permute-done.other), custom_call_target="tpu_custom_call" | custom-call | bytes 1081344 | tf_op jit(solution)/shard_map/far_sums/pallas_call | solution.py:322
  14.2 2.7 %collective-permute-start.2 = (bf16[8,32,512]{2,1,0:T(8,128)(2,1)S(1)}, bf16[8,32,512]{2,1,0:T(8,128)(2,1)S(1)}, u32[]{:S(2)}, u32[]{:S(2)}) collective-permute-start(bf16[8,32,512]{2,1,0:T(8,128)(2,1)S(1)} %get-tuple-element.22.refs_1_), channel_id=1, source_target_pairs={{0,4},{1,3},{2,0},{3,7},{4,8},{5,1},{6,2},{7,11},{8,12},{9,5},{10,... | collective-permute-start | bytes 786440 | tf_op jit(solution)/shard_map/ppermute | solution.py:61
  16.9 1.6 %collective-permute-start.4 = (bf16[8,32,512]{2,1,0:T(8,128)(2,1)S(1)}, bf16[8,32,512]{2,1,0:T(8,128)(2,1)S(1)}, u32[]{:S(2)}, u32[]{:S(2)}) collective-permute-start(bf16[8,32,512]{2,1,0:T(8,128)(2,1)S(1)} %get-tuple-element.23), channel_id=1, source_target_pairs={{0,4},{1,3},{2,0},{3,7},{4,8},{5,1},{6,2},{7,11},{8,12},{9,5},{10,... | collective-permute-start | bytes 786440 | tf_op jit(solution)/shard_map/ppermute | solution.py:61
  18.5 1.2 %own_sums.1.token.own = f32[6,8,32,512]{3,2,1,0:T(8,128)S(1)} custom-call(s32[4,64]{1,0:T(4,128)S(1)} %get-tuple-element.17.table_ref, bf16[33,32,512]{2,1,0:T(8,128)(2,1)S(1)} %get-tuple-element.19.kept, bf16[25,32,512]{2,1,0:T(8,128)(2,1)S(1)} %collective-permute-done.1.other), custom_call_target="tpu_custom_call" | custom-call | bytes 4325376 | tf_op jit(solution)/shard_map/own_sums/pallas_call | solution.py:337
  20.3 1.0 %collective-permute-done.2.came = bf16[8,32,512]{2,1,0:T(8,128)(2,1)S(1)} collective-permute-done((bf16[8,32,512]{2,1,0:T(8,128)(2,1)S(1)}, bf16[8,32,512]{2,1,0:T(8,128)(2,1)S(1)}, u32[]{:S(2)}, u32[]{:S(2)}) %collective-permute-start.2) | collective-permute-done | bytes 262176 | tf_op jit(solution)/shard_map/ppermute | solution.py:61
  21.3 2.1 %collective-permute-start.3 = (bf16[8,32,512]{2,1,0:T(8,128)(2,1)S(1)}, bf16[8,32,512]{2,1,0:T(8,128)(2,1)S(1)}, u32[]{:S(2)}, u32[]{:S(2)}) collective-permute-start(bf16[8,32,512]{2,1,0:T(8,128)(2,1)S(1)} %add_5.1.token), channel_id=1, source_target_pairs={{0,4},{1,3},{2,0},{3,7},{4,8},{5,1},{6,2},{7,11},{8,12},{9,5},{10,... | collective-permute-start | bytes 786440 | tf_op jit(solution)/shard_map/ppermute | solution.py:61
  23.4 0.6 collective-permute-done.4.came
  24.1 2.1 %collective-permute-start.6 = (bf16[8,32,512]{2,1,0:T(8,128)(2,1)S(1)}, bf16[8,32,512]{2,1,0:T(8,128)(2,1)S(1)}, u32[]{:S(2)}, u32[]{:S(2)}) collective-permute-start(bf16[8,32,512]{2,1,0:T(8,128)(2,1)S(1)} %add_4.1.token), channel_id=1, source_target_pairs={{0,4},{1,3},{2,0},{3,7},{4,8},{5,1},{6,2},{7,11},{8,12},{9,5},{10,... | collective-permute-start | bytes 786440 | tf_op jit(solution)/shard_map/ppermute | solution.py:61
  26.2 1.5 %collective-permute-done.3.came = bf16[8,32,512]{2,1,0:T(8,128)(2,1)S(1)} collective-permute-done((bf16[8,32,512]{2,1,0:T(8,128)(2,1)S(1)}, bf16[8,32,512]{2,1,0:T(8,128)(2,1)S(1)}, u32[]{:S(2)}, u32[]{:S(2)}) %collective-permute-start.3) | collective-permute-done | bytes 262176 | tf_op jit(solution)/shard_map/ppermute | solution.py:61
  27.8 2.1 %collective-permute-start.5 = (bf16[8,32,512]{2,1,0:T(8,128)(2,1)S(1)}, bf16[8,32,512]{2,1,0:T(8,128)(2,1)S(1)}, u32[]{:S(2)}, u32[]{:S(2)}) collective-permute-start(bf16[8,32,512]{2,1,0:T(8,128)(2,1)S(1)} %add_3.1.token), channel_id=1, source_target_pairs={{0,4},{1,3},{2,0},{3,7},{4,8},{5,1},{6,2},{7,11},{8,12},{9,5},{10,... | collective-permute-start | bytes 786440 | tf_op jit(solution)/shard_map/ppermute | solution.py:61
  31.0 3.2 %collective-permute-done.5.came = bf16[8,32,512]{2,1,0:T(8,128)(2,1)S(1)} collective-permute-done((bf16[8,32,512]{2,1,0:T(8,128)(2,1)S(1)}, bf16[8,32,512]{2,1,0:T(8,128)(2,1)S(1)}, u32[]{:S(2)}, u32[]{:S(2)}) %collective-permute-start.5) | collective-permute-done | bytes 262176 | tf_op jit(solution)/shard_map/ppermute | solution.py:61
  34.3 2.1 %collective-permute-start.7 = (bf16[8,32,512]{2,1,0:T(8,128)(2,1)S(1)}, bf16[8,32,512]{2,1,0:T(8,128)(2,1)S(1)}, u32[]{:S(2)}, u32[]{:S(2)}) collective-permute-start(bf16[8,32,512]{2,1,0:T(8,128)(2,1)S(1)} %add_1.1), channel_id=1, source_target_pairs={{0,4},{1,3},{2,0},{3,7},{4,8},{5,1},{6,2},{7,11},{8,12},{9,5},{10,... | collective-permute-start | bytes 786440 | tf_op jit(solution)/shard_map/ppermute | solution.py:61
  36.7 4.1 %collective-permute-done.7.came = bf16[8,32,512]{2,1,0:T(8,128)(2,1)S(1)} collective-permute-done((bf16[8,32,512]{2,1,0:T(8,128)(2,1)S(1)}, bf16[8,32,512]{2,1,0:T(8,128)(2,1)S(1)}, u32[]{:S(2)}, u32[]{:S(2)}) %collective-permute-start.7) | collective-permute-done | bytes 262176 | tf_op jit(solution)/shard_map/ppermute | solution.py:61
  40.8 1.5 %mesh_step.1 = (bf16[256,512]{1,0:T(8,128)(2,1)}, bf16[256,512]{1,0:T(8,128)(2,1)S(1)}) custom-call(bf16[256,512]{1,0:T(8,128)(2,1)S(1)} %copy-done.3, bf16[512,512]{1,0:T(8,128)(2,1)S(1)} %copy-done.1, bf16[512,512]{1,0:T(8,128)(2,1)S(1)} %copy-done.2, f32[1,512]{1,0:T(1,128)S(1)} %bitcast.6, f32[6,8,32,512]{3,2,1,0:T(8,128)S(1)} %own_sums.1.token.own, ...), custom_call_target="tpu_custom_call" | custom-call | flops 268435456 | bytes 1048576 | tf_op jit(solution)/shard_map/mesh_step/pallas_call | solution.py:384
  42.2 2.0 %collective-permute-start.9 = (bf16[256,512]{1,0:T(8,128)(2,1)S(1)}, bf16[256,512]{1,0:T(8,128)(2,1)S(1)}, u32[]{:S(2)}, u32[]{:S(2)}) collective-permute-start(bf16[256,512]{1,0:T(8,128)(2,1)S(1)} %get-tuple-element.24.refs_1_.refs_0_), channel_id=1, source_target_pairs={{0,2},{1,5},{2,6},{3,1},{4,0},{5,9},{6,10},{7,3},{8,4},{9,13},{10,... | collective-permute-start | bytes 786440 | tf_op jit(solution)/shard_map/ppermute | solution.py:61
  44.2 5.8 %collective-permute-done.9.refs_0_ = bf16[256,512]{1,0:T(8,128)(2,1)S(1)} collective-permute-done((bf16[256,512]{1,0:T(8,128)(2,1)S(1)}, bf16[256,512]{1,0:T(8,128)(2,1)S(1)}, u32[]{:S(2)}, u32[]{:S(2)}) %collective-permute-start.9) | collective-permute-done | bytes 262176 | tf_op jit(solution)/shard_map/ppermute | solution.py:61
  50.0 2.4 %collective-permute-start.12 = (bf16[256,512]{1,0:T(8,128)(2,1)S(1)}, bf16[256,512]{1,0:T(8,128)(2,1)S(1)}, u32[]{:S(2)}, u32[]{:S(2)}) collective-permute-start(bf16[256,512]{1,0:T(8,128)(2,1)S(1)} %in_order.8.refs_1_), channel_id=1, source_target_pairs={{0,2},{1,5},{2,6},{3,1},{4,0},{5,9},{6,10},{7,3},{8,4},{9,13},{10,... | collective-permute-start | bytes 786440 | tf_op jit(solution)/shard_map/ppermute | solution.py:61
  52.4 1.6 %collective-permute-start.13 = (bf16[256,512]{1,0:T(8,128)(2,1)S(1)}, bf16[256,512]{1,0:T(8,128)(2,1)S(1)}, u32[]{:S(2)}, u32[]{:S(2)}) collective-permute-start(bf16[256,512]{1,0:T(8,128)(2,1)S(1)} %in_order.9.refs_2_), channel_id=1, source_target_pairs={{0,2},{1,5},{2,6},{3,1},{4,0},{5,9},{6,10},{7,3},{8,4},{9,13},{10,... | collective-permute-start | bytes 786440 | tf_op jit(solution)/shard_map/ppermute | solution.py:61
  54.0 0.6 pick_0.1
  54.6 2.6 %collective-permute-done.12.refs_0_ = bf16[256,512]{1,0:T(8,128)(2,1)S(1)} collective-permute-done((bf16[256,512]{1,0:T(8,128)(2,1)S(1)}, bf16[256,512]{1,0:T(8,128)(2,1)S(1)}, u32[]{:S(2)}, u32[]{:S(2)}) %collective-permute-start.12) | collective-permute-done | bytes 262176 | tf_op jit(solution)/shard_map/ppermute | solution.py:61
  57.3 1.5 %collective-permute-start.15 = (bf16[256,512]{1,0:T(8,128)(2,1)S(1)}, bf16[256,512]{1,0:T(8,128)(2,1)S(1)}, u32[]{:S(2)}, u32[]{:S(2)}) collective-permute-start(bf16[256,512]{1,0:T(8,128)(2,1)S(1)} %in_order.10.refs_1_.refs_0_), channel_id=1, source_target_pairs={{0,2},{1,5},{2,6},{3,1},{4,0},{5,9},{6,10},{7,3},{8,4},{9,13},{10,... | collective-permute-start | bytes 786440 | tf_op jit(solution)/shard_map/ppermute | solution.py:61
  58.8 1.3 %collective-permute-done.13.refs_0_ = bf16[256,512]{1,0:T(8,128)(2,1)S(1)} collective-permute-done((bf16[256,512]{1,0:T(8,128)(2,1)S(1)}, bf16[256,512]{1,0:T(8,128)(2,1)S(1)}, u32[]{:S(2)}, u32[]{:S(2)}) %collective-permute-start.13) | collective-permute-done | bytes 262176 | tf_op jit(solution)/shard_map/ppermute | solution.py:61
  60.1 1.5 %collective-permute-start.16 = (bf16[256,512]{1,0:T(8,128)(2,1)S(1)}, bf16[256,512]{1,0:T(8,128)(2,1)S(1)}, u32[]{:S(2)}, u32[]{:S(2)}) collective-permute-start(bf16[256,512]{1,0:T(8,128)(2,1)S(1)} %in_order.11.refs_1_), channel_id=1, source_target_pairs={{0,2},{1,5},{2,6},{3,1},{4,0},{5,9},{6,10},{7,3},{8,4},{9,13},{10,... | collective-permute-start | bytes 786440 | tf_op jit(solution)/shard_map/ppermute | solution.py:61
  62.2 1.4 %collective-permute-done.15.refs_0_ = bf16[256,512]{1,0:T(8,128)(2,1)S(1)} collective-permute-done((bf16[256,512]{1,0:T(8,128)(2,1)S(1)}, bf16[256,512]{1,0:T(8,128)(2,1)S(1)}, u32[]{:S(2)}, u32[]{:S(2)}) %collective-permute-start.15) | collective-permute-done | bytes 262176 | tf_op jit(solution)/shard_map/ppermute | solution.py:61
  63.7 1.5 %collective-permute-start.18 = (bf16[256,512]{1,0:T(8,128)(2,1)S(1)}, bf16[256,512]{1,0:T(8,128)(2,1)S(1)}, u32[]{:S(2)}, u32[]{:S(2)}) collective-permute-start(bf16[256,512]{1,0:T(8,128)(2,1)S(1)} %in_order.12.refs_1_.refs_0_), channel_id=1, source_target_pairs={{0,2},{1,5},{2,6},{3,1},{4,0},{5,9},{6,10},{7,3},{8,4},{9,13},{10,... | collective-permute-start | bytes 786440 | tf_op jit(solution)/shard_map/ppermute | solution.py:61
  65.7 0.8 %collective-permute-done.16.refs_0_ = bf16[256,512]{1,0:T(8,128)(2,1)S(1)} collective-permute-done((bf16[256,512]{1,0:T(8,128)(2,1)S(1)}, bf16[256,512]{1,0:T(8,128)(2,1)S(1)}, u32[]{:S(2)}, u32[]{:S(2)}) %collective-permute-start.16) | collective-permute-done | bytes 262176 | tf_op jit(solution)/shard_map/ppermute | solution.py:61
  66.5 0.6 pick_5.1
  67.2 2.9 %collective-permute-done.18.rest_6_ = bf16[256,512]{1,0:T(8,128)(2,1)S(1)} collective-permute-done((bf16[256,512]{1,0:T(8,128)(2,1)S(1)}, bf16[256,512]{1,0:T(8,128)(2,1)S(1)}, u32[]{:S(2)}, u32[]{:S(2)}) %collective-permute-start.18) | collective-permute-done | bytes 262176 | tf_op jit(solution)/shard_map/ppermute | solution.py:61
  70.1 1.5 %collective-permute-done.19.rest_7_ = bf16[256,512]{1,0:T(8,128)(2,1)S(1)} collective-permute-done((bf16[256,512]{1,0:T(8,128)(2,1)S(1)}, bf16[256,512]{1,0:T(8,128)(2,1)S(1)}, u32[]{:S(2)}, u32[]{:S(2)}) %collective-permute-start.19) | collective-permute-done | bytes 262176 | tf_op jit(solution)/shard_map/ppermute | solution.py:52
  71.6 6.8 %back.1 = bf16[4096,512]{1,0:T(8,128)(2,1)} custom-call(s32[4,64]{1,0:T(4,128)S(1)} %get-tuple-element.17.table_ref, bf16[4096,512]{1,0:T(8,128)(2,1)} %get-tuple-element.18.latent_ref, bf16[16,256,128]{2,1,0:T(8,128)(2,1)S(1)} %turn.1.token.weights_ref, bf16[384,512]{1,0:T(8,128)(2,1)S(1)} %get-tuple-element.25.refs_1_.rest_0_, ...), custom_call_target="tpu_custom_call" | custom-call | flops 536870912 | bytes 9437184 | tf_op jit(solution)/shard_map/back/pallas_call | solution.py:437
  (39 shorter events, 4.1 us)
Async XLA Ops:
  11.3 1.7 %collective-permute-start = (bf16[9,32,512]{2,1,0:T(8,128)(2,1)S(1)}, bf16[9,32,512]{2,1,0:T(8,128)(2,1)S(1)}, u32[]{:S(2)}, u32[]{:S(2)}) collective-permute-start(bf16[9,32,512]{2,1,0:T(8,128)(2,1)S(1)} %get-tuple-element.21), channel_id=1, source_target_pairs={{0,1},{1,0},{2,3},{3,2},{4,5},{5,4},{6,7},{7,6},{8,9},{9,8},{10,11... | collective-permute-start | bytes 884744 | tf_op jit(solution)/shard_map/ppermute | solution.py:52
  13.8 5.9 %copy-start = (bf16[16,4,32,256]{3,2,1,0:T(8,128)(2,1)S(1)}, bf16[16,4,32,256]{3,2,1,0:T(8,128)(2,1)}, u32[]{:S(2)}) copy-start(bf16[16,4,32,256]{3,2,1,0:T(8,128)(2,1)} %interp_ref.3) | copy-start | bytes 3145732
  13.8 4.7 %collective-permute-start.1 = (bf16[25,32,512]{2,1,0:T(8,128)(2,1)S(1)}, bf16[25,32,512]{2,1,0:T(8,128)(2,1)S(1)}, u32[]{:S(2)}, u32[]{:S(2)}) collective-permute-start(bf16[25,32,512]{2,1,0:T(8,128)(2,1)S(1)} %in_order.7), channel_id=1, source_target_pairs={{0,1},{1,0},{2,3},{3,2},{4,5},{5,4},{6,7},{7,6},{8,9},{9,8},{10,11... | collective-permute-start | bytes 2457608 | tf_op jit(solution)/shard_map/ppermute | solution.py:52
  14.2 7.0 %collective-permute-start.2 = (bf16[8,32,512]{2,1,0:T(8,128)(2,1)S(1)}, bf16[8,32,512]{2,1,0:T(8,128)(2,1)S(1)}, u32[]{:S(2)}, u32[]{:S(2)}) collective-permute-start(bf16[8,32,512]{2,1,0:T(8,128)(2,1)S(1)} %get-tuple-element.22.refs_1_), channel_id=1, source_target_pairs={{0,4},{1,3},{2,0},{3,7},{4,8},{5,1},{6,2},{7,11},{8,12},{9,5},{10,... | collective-permute-start | bytes 786440 | tf_op jit(solution)/shard_map/ppermute | solution.py:61
  16.9 7.1 %collective-permute-start.4 = (bf16[8,32,512]{2,1,0:T(8,128)(2,1)S(1)}, bf16[8,32,512]{2,1,0:T(8,128)(2,1)S(1)}, u32[]{:S(2)}, u32[]{:S(2)}) collective-permute-start(bf16[8,32,512]{2,1,0:T(8,128)(2,1)S(1)} %get-tuple-element.23), channel_id=1, source_target_pairs={{0,4},{1,3},{2,0},{3,7},{4,8},{5,1},{6,2},{7,11},{8,12},{9,5},{10,... | collective-permute-start | bytes 786440 | tf_op jit(solution)/shard_map/ppermute | solution.py:61
  21.3 6.4 %collective-permute-start.3 = (bf16[8,32,512]{2,1,0:T(8,128)(2,1)S(1)}, bf16[8,32,512]{2,1,0:T(8,128)(2,1)S(1)}, u32[]{:S(2)}, u32[]{:S(2)}) collective-permute-start(bf16[8,32,512]{2,1,0:T(8,128)(2,1)S(1)} %add_5.1.token), channel_id=1, source_target_pairs={{0,4},{1,3},{2,0},{3,7},{4,8},{5,1},{6,2},{7,11},{8,12},{9,5},{10,... | collective-permute-start | bytes 786440 | tf_op jit(solution)/shard_map/ppermute | solution.py:61
  24.1 6.4 %collective-permute-start.6 = (bf16[8,32,512]{2,1,0:T(8,128)(2,1)S(1)}, bf16[8,32,512]{2,1,0:T(8,128)(2,1)S(1)}, u32[]{:S(2)}, u32[]{:S(2)}) collective-permute-start(bf16[8,32,512]{2,1,0:T(8,128)(2,1)S(1)} %add_4.1.token), channel_id=1, source_target_pairs={{0,4},{1,3},{2,0},{3,7},{4,8},{5,1},{6,2},{7,11},{8,12},{9,5},{10,... | collective-permute-start | bytes 786440 | tf_op jit(solution)/shard_map/ppermute | solution.py:61
  27.8 13.0 %copy-start.1 = (bf16[512,512]{1,0:T(8,128)(2,1)S(1)}, bf16[512,512]{1,0:T(8,128)(2,1)}, u32[]{:S(2)}) copy-start(bf16[512,512]{1,0:T(8,128)(2,1)} %up_ref.1) | copy-start | bytes 1572868
  27.8 13.0 %copy-start.2 = (bf16[512,512]{1,0:T(8,128)(2,1)S(1)}, bf16[512,512]{1,0:T(8,128)(2,1)}, u32[]{:S(2)}) copy-start(bf16[512,512]{1,0:T(8,128)(2,1)} %down_ref.1) | copy-start | bytes 1572868
  27.8 12.9 %copy-start.3 = (bf16[256,512]{1,0:T(8,128)(2,1)S(1)}, bf16[256,512]{1,0:T(8,128)(2,1)}, u32[]{:S(2)}) copy-start(bf16[256,512]{1,0:T(8,128)(2,1)} %latent_ref.1) | copy-start | bytes 786436
  27.8 12.9 %copy-start.4 = (f32[512]{0:T(512)S(1)}, f32[512]{0:T(512)}, u32[]{:S(2)}) copy-start(f32[512]{0:T(512)} %param.21) | copy-start | bytes 6148
  27.8 6.4 %collective-permute-start.5 = (bf16[8,32,512]{2,1,0:T(8,128)(2,1)S(1)}, bf16[8,32,512]{2,1,0:T(8,128)(2,1)S(1)}, u32[]{:S(2)}, u32[]{:S(2)}) collective-permute-start(bf16[8,32,512]{2,1,0:T(8,128)(2,1)S(1)} %add_3.1.token), channel_id=1, source_target_pairs={{0,4},{1,3},{2,0},{3,7},{4,8},{5,1},{6,2},{7,11},{8,12},{9,5},{10,... | collective-permute-start | bytes 786440 | tf_op jit(solution)/shard_map/ppermute | solution.py:61
  30.6 6.1 %collective-permute-start.8 = (bf16[8,32,512]{2,1,0:T(8,128)(2,1)S(1)}, bf16[8,32,512]{2,1,0:T(8,128)(2,1)S(1)}, u32[]{:S(2)}, u32[]{:S(2)}) collective-permute-start(bf16[8,32,512]{2,1,0:T(8,128)(2,1)S(1)} %add_2.1.token), channel_id=1, source_target_pairs={{0,5},{1,2},{2,1},{3,6},{4,9},{5,0},{6,3},{7,10},{8,13},{9,4},{10,... | collective-permute-start | bytes 786440 | tf_op jit(solution)/shard_map/ppermute | solution.py:61
  34.3 6.4 %collective-permute-start.7 = (bf16[8,32,512]{2,1,0:T(8,128)(2,1)S(1)}, bf16[8,32,512]{2,1,0:T(8,128)(2,1)S(1)}, u32[]{:S(2)}, u32[]{:S(2)}) collective-permute-start(bf16[8,32,512]{2,1,0:T(8,128)(2,1)S(1)} %add_1.1), channel_id=1, source_target_pairs={{0,4},{1,3},{2,0},{3,7},{4,8},{5,1},{6,2},{7,11},{8,12},{9,5},{10,... | collective-permute-start | bytes 786440 | tf_op jit(solution)/shard_map/ppermute | solution.py:61
  42.2 7.8 %collective-permute-start.9 = (bf16[256,512]{1,0:T(8,128)(2,1)S(1)}, bf16[256,512]{1,0:T(8,128)(2,1)S(1)}, u32[]{:S(2)}, u32[]{:S(2)}) collective-permute-start(bf16[256,512]{1,0:T(8,128)(2,1)S(1)} %get-tuple-element.24.refs_1_.refs_0_), channel_id=1, source_target_pairs={{0,2},{1,5},{2,6},{3,1},{4,0},{5,9},{6,10},{7,3},{8,4},{9,13},{10,... | collective-permute-start | bytes 786440 | tf_op jit(solution)/shard_map/ppermute | solution.py:61
  44.2 8.2 %collective-permute-start.10 = (bf16[256,512]{1,0:T(8,128)(2,1)S(1)}, bf16[256,512]{1,0:T(8,128)(2,1)S(1)}, u32[]{:S(2)}, u32[]{:S(2)}) collective-permute-start(bf16[256,512]{1,0:T(8,128)(2,1)S(1)} %get-tuple-element.24.refs_1_.refs_0_), channel_id=1, source_target_pairs={{0,5},{1,2},{2,1},{3,6},{4,9},{5,0},{6,3},{7,10},{8,13},{9,4},{10,... | collective-permute-start | bytes 786440 | tf_op jit(solution)/shard_map/ppermute | solution.py:61
  50.0 7.3 %collective-permute-start.12 = (bf16[256,512]{1,0:T(8,128)(2,1)S(1)}, bf16[256,512]{1,0:T(8,128)(2,1)S(1)}, u32[]{:S(2)}, u32[]{:S(2)}) collective-permute-start(bf16[256,512]{1,0:T(8,128)(2,1)S(1)} %in_order.8.refs_1_), channel_id=1, source_target_pairs={{0,2},{1,5},{2,6},{3,1},{4,0},{5,9},{6,10},{7,3},{8,4},{9,13},{10,... | collective-permute-start | bytes 786440 | tf_op jit(solution)/shard_map/ppermute | solution.py:61
  52.4 7.7 %collective-permute-start.13 = (bf16[256,512]{1,0:T(8,128)(2,1)S(1)}, bf16[256,512]{1,0:T(8,128)(2,1)S(1)}, u32[]{:S(2)}, u32[]{:S(2)}) collective-permute-start(bf16[256,512]{1,0:T(8,128)(2,1)S(1)} %in_order.9.refs_2_), channel_id=1, source_target_pairs={{0,2},{1,5},{2,6},{3,1},{4,0},{5,9},{6,10},{7,3},{8,4},{9,13},{10,... | collective-permute-start | bytes 786440 | tf_op jit(solution)/shard_map/ppermute | solution.py:61
  57.3 6.4 %collective-permute-start.15 = (bf16[256,512]{1,0:T(8,128)(2,1)S(1)}, bf16[256,512]{1,0:T(8,128)(2,1)S(1)}, u32[]{:S(2)}, u32[]{:S(2)}) collective-permute-start(bf16[256,512]{1,0:T(8,128)(2,1)S(1)} %in_order.10.refs_1_.refs_0_), channel_id=1, source_target_pairs={{0,2},{1,5},{2,6},{3,1},{4,0},{5,9},{6,10},{7,3},{8,4},{9,13},{10,... | collective-permute-start | bytes 786440 | tf_op jit(solution)/shard_map/ppermute | solution.py:61
  60.1 6.4 %collective-permute-start.16 = (bf16[256,512]{1,0:T(8,128)(2,1)S(1)}, bf16[256,512]{1,0:T(8,128)(2,1)S(1)}, u32[]{:S(2)}, u32[]{:S(2)}) collective-permute-start(bf16[256,512]{1,0:T(8,128)(2,1)S(1)} %in_order.11.refs_1_), channel_id=1, source_target_pairs={{0,2},{1,5},{2,6},{3,1},{4,0},{5,9},{6,10},{7,3},{8,4},{9,13},{10,... | collective-permute-start | bytes 786440 | tf_op jit(solution)/shard_map/ppermute | solution.py:61
  63.7 6.4 %collective-permute-start.18 = (bf16[256,512]{1,0:T(8,128)(2,1)S(1)}, bf16[256,512]{1,0:T(8,128)(2,1)S(1)}, u32[]{:S(2)}, u32[]{:S(2)}) collective-permute-start(bf16[256,512]{1,0:T(8,128)(2,1)S(1)} %in_order.12.refs_1_.refs_0_), channel_id=1, source_target_pairs={{0,2},{1,5},{2,6},{3,1},{4,0},{5,9},{6,10},{7,3},{8,4},{9,13},{10,... | collective-permute-start | bytes 786440 | tf_op jit(solution)/shard_map/ppermute | solution.py:61
  65.2 4.9 %collective-permute-start.11 = (bf16[384,512]{1,0:T(8,128)(2,1)S(1)}, bf16[384,512]{1,0:T(8,128)(2,1)S(1)}, u32[]{:S(2)}, u32[]{:S(2)}) collective-permute-start(bf16[384,512]{1,0:T(8,128)(2,1)S(1)} %get-tuple-element.26), channel_id=1, source_target_pairs={{0,1},{1,0},{2,3},{3,2},{4,5},{5,4},{6,7},{7,6},{8,9},{9,8},{10,11... | collective-permute-start | bytes 1179656 | tf_op jit(solution)/shard_map/ppermute | solution.py:52
  65.2 4.9 %collective-permute-start.14 = (bf16[256,512]{1,0:T(8,128)(2,1)S(1)}, bf16[256,512]{1,0:T(8,128)(2,1)S(1)}, u32[]{:S(2)}, u32[]{:S(2)}) collective-permute-start(bf16[256,512]{1,0:T(8,128)(2,1)S(1)} %get-tuple-element.28), channel_id=1, source_target_pairs={{0,1},{1,0},{2,3},{3,2},{4,5},{5,4},{6,7},{7,6},{8,9},{9,8},{10,11... | collective-permute-start | bytes 786440 | tf_op jit(solution)/shard_map/ppermute | solution.py:52
  67.1 3.0 %collective-permute-start.17 = (bf16[256,512]{1,0:T(8,128)(2,1)S(1)}, bf16[256,512]{1,0:T(8,128)(2,1)S(1)}, u32[]{:S(2)}, u32[]{:S(2)}) collective-permute-start(bf16[256,512]{1,0:T(8,128)(2,1)S(1)} %get-tuple-element.30), channel_id=1, source_target_pairs={{0,1},{1,0},{2,3},{3,2},{4,5},{5,4},{6,7},{7,6},{8,9},{9,8},{10,11... | collective-permute-start | bytes 786440 | tf_op jit(solution)/shard_map/ppermute | solution.py:52
  70.0 1.5 %collective-permute-start.19 = (bf16[256,512]{1,0:T(8,128)(2,1)S(1)}, bf16[256,512]{1,0:T(8,128)(2,1)S(1)}, u32[]{:S(2)}, u32[]{:S(2)}) collective-permute-start(bf16[256,512]{1,0:T(8,128)(2,1)S(1)} %collective-permute-done.18.rest_6_), channel_id=1, source_target_pairs={{0,1},{1,0},{2,3},{3,2},{4,5},{5,4},{6,7},{7,6},{8,9},{9,8},{10,11... | collective-permute-start | bytes 786440 | tf_op jit(solution)/shard_map/ppermute | solution.py:52

commit v10 on v9

--- a/solution.py
+++ b/solution.py
@@ -78,50 +78,75 @@
 
 
 def embed_kernel(
-    ring, per_step, slots, me_ref, lists_ref, mask_ref,
-    x_ref, w1_ref, w2_ref, gain_ref, interp_ref,
-    latent_ref, kept_ref, far_ref, rest_ref, table_ref, wide, hidden,
+    ring, slots, me_ref, lists_ref, mask_ref, x_any, w1_any, w2_any, gain_ref, interp_any,
+    latent_any, kept_ref, far_ref, rest_ref, table_ref,
+    x_ref, w1_ref, w2_ref, interp_ref, wide, hidden, latent_ref, sems,
 ):
-    step = pl.program_id(0)
     me = me_ref[0]
-    list_len, tile_rows, block_rows = interp_ref.shape[1:]
-    blk_count = pl.num_programs(0) * per_step
+    blk_count, list_len, tile_rows, block_rows = interp_ref.shape
     groups = ring.chips
+    parts = x_ref.shape[0]
+    part_rows = x_ref.shape[2]
+    part_blocks = part_rows // block_rows
+    spans = [slice(i * part_rows, (i + 1) * part_rows) for i in range(parts)]
+
+    copies = []
+
+    def copy(source, target):
+        copies.append(pltpu.make_async_copy(source, target, sems.at[len(copies)]))
+        return copies[-1]
+
+    w1_in, w2_in = copy(w1_any, w1_ref), copy(w2_any, w2_ref)
+    x_in = [copy(x_any.at[:, pl.ds(s.start, part_rows)], x_ref.at[i]) for i, s in enumerate(spans)]
+    interp_in = []
+    for i in range(parts):
+        blocks = pl.ds(i * part_blocks, part_blocks)
+        interp_in.append(copy(interp_any.at[blocks], interp_ref.at[blocks]))
+    latent_out = []
+    for s in spans:
+        rows = pl.ds(s.start, part_rows)
+        latent_out.append(copy(latent_ref.at[rows], latent_any.at[rows]))
+    for started in (w1_in, x_in[0], w2_in, interp_in[0]):
+        started.start()
+    for i in range(1, parts):
+        x_in[i].start()
+        interp_in[i].start()
 
     def spot(index, block, k):
         across, group, tile = ring.entry(lists_ref, index, index * blk_count + block, k)
-        slot = split(block * list_len + k, ring.n_band)[0]
-        return across, group, tile, slot
-
-    part_rows = PART * block_rows
-    spans = [slice(i * part_rows, (i + 1) * part_rows) for i in range(per_step // PART)]
-    for rows in spans:
-        wide[rows] = lax.dot_general(
-            x_ref[:, rows], w1_ref[...], (((0,), (0,)), ((), ())), preferred_element_type=F32
+        return across, group, tile, (block * list_len + k) // ring.n_band
+
+    kept_spare, far_spare, rest_spare = (ref.shape[0] - 1 for ref in (kept_ref, far_ref, rest_ref))
+
+    def first_layer(i):
+        x_in[i].wait()
+        wide[spans[i]] = lax.dot_general(
+            x_ref[i], w1_ref[...], (((0,), (0,)), ((), ())), preferred_element_type=F32
         )
-    for rows in spans:
-        for strip in strips(rows):
+
+    def second_layer(i):
+        for strip in strips(spans[i]):
             hidden[strip] = silu(wide[strip]).astype(BF16)
-        wide[rows] = jnp.dot(hidden[rows], w2_ref[...], preferred_element_type=F32)
-    kept_spare, far_spare, rest_spare = (ref.shape[0] - 1 for ref in (kept_ref, far_ref, rest_ref))
-    for number, rows in enumerate(spans):
-        for strip in strips(rows):
+        wide[spans[i]] = jnp.dot(hidden[spans[i]], w2_ref[...], preferred_element_type=F32)
+
+    def listed_sums(i):
+        for strip in strips(spans[i]):
             latent_ref[strip] = layer_norm(wide[strip], gain_ref[...]).astype(BF16)
-        for b in range(number * PART, (number + 1) * PART):
-            block = step * per_step + b
-            weights = interp_ref[b].reshape(list_len * tile_rows, block_rows)
-            latent = latent_ref[b * block_rows : (b + 1) * block_rows]
+        latent_out[i].start()
+        interp_in[i].wait()
+        for block in range(i * part_blocks, (i + 1) * part_blocks):
+            weights = interp_ref[block].reshape(list_len * tile_rows, block_rows)
+            latent = latent_ref[block * block_rows : (block + 1) * block_rows]
             part = jnp.dot(weights, latent, preferred_element_type=F32)
             for k in range(list_len):
+                entry = block * list_len + k
                 across, group, tile, slot = spot(me, block, k)
                 place = (across * groups + group) * slots + slot
                 mask = mask_ref[k, me * blk_count + block]
                 table_ref[0, place] = tile
                 found = group * slots + jnp.where(group == groups - 1, tile, slot)
-                table_ref[2, block * list_len + k] = found + across * (
-                    (groups - 1) * slots + ring.tiles
-                )
-                table_ref[3, block * list_len + k] = mask
+                table_ref[2, entry] = found + across * ((groups - 1) * slots + ring.tiles)
+                table_ref[3, entry] = mask
                 across, group, tile, slot = spot(me ^ 1, block, k)
                 table_ref[1, (across * groups + group) * slots + slot] = tile
                 masked = part[k * tile_rows : (k + 1) * tile_rows] * mask.astype(F32)
@@ -131,6 +156,19 @@
                 rest_ref[jnp.where(there < 0, rest_spare, jnp.minimum(there, rest_spare))] = masked
                 beyond = there - rest_spare
                 far_ref[jnp.where(beyond < 0, far_spare, beyond)] = masked
+
+    w1_in.wait()
+    first_layer(0)
+    w2_in.wait()
+    for i in range(parts):
+        if i + 1 < parts:
+            first_layer(i + 1)
+        second_layer(i)
+        if i:
+            listed_sums(i - 1)
+    listed_sums(parts - 1)
+    for started in latent_out:
+        started.wait()
 
 
 def add_entries(total, table_ref, group, slots, kept, other, groups, first=0):
@@ -192,36 +230,47 @@
         out_ref[b] = interp_ref[b].reshape(out_ref.shape[2], out_ref.shape[1]).T
 
 
-def back_kernel(starts, list_len, per_step, table_ref, latent_ref, weights_ref, *rest):
+def back_kernel(starts, list_len, table_ref, weights_ref, latent_any, *rest):
     count = len(starts)
-    pieces, (out_ref, held, total, sems) = rest[:count], rest[count:]
-    step = pl.program_id(0)
-    block_rows = weights_ref.shape[1]
-    tile_rows = weights_ref.shape[2] // list_len
-
-    @pl.when(step == 0)
-    def _():
-        copies = []
-        for i, (piece, start) in enumerate(zip(pieces, starts)):
-            into = held.at[pl.ds(start, piece.shape[0])]
-            copies.append(pltpu.make_async_copy(piece, into, sems.at[i]))
-        for copy in copies:
-            copy.start()
-        for copy in copies:
-            copy.wait()
-
-    for b in range(per_step):
+    pieces, (out_any, held, latent_ref, total, out_ref, sems) = rest[:count], rest[count:]
+    blk_count, block_rows, listed = weights_ref.shape
+    tile_rows = listed // list_len
+    copies = []
+
+    def copy(source, target):
+        copies.append(pltpu.make_async_copy(source, target, sems.at[len(copies)]))
+        return copies[-1]
+
+    pieces_in = []
+    for piece, start in zip(pieces, starts):
+        pieces_in.append(copy(piece, held.at[pl.ds(start, piece.shape[0])]))
+    part_rows = PART * block_rows
+    parts = [pl.ds(i * part_rows, part_rows) for i in range(blk_count // PART)]
+    latent_in = [copy(latent_any.at[rows], latent_ref.at[rows]) for rows in parts]
+    outs = [copy(out_ref.at[rows], out_any.at[rows]) for rows in parts]
+    for started in pieces_in + latent_in:
+        started.start()
+    for started in pieces_in:
+        started.wait()
+
+    for block in range(blk_count):
         values = []
         for k in range(list_len):
-            entry = (step * per_step + b) * list_len + k
+            entry = block * list_len + k
             rows = pl.ds(pl.multiple_of(table_ref[2, entry] * tile_rows, tile_rows), tile_rows)
             value = held[rows]
             values.append(jnp.where(table_ref[3, entry] == 1, value, jnp.zeros_like(value)))
         value = jnp.concatenate(values, axis=0)
-        rows = slice(b * block_rows, (b + 1) * block_rows)
-        total[rows] = jnp.dot(weights_ref[b], value, preferred_element_type=F32)
+        rows = slice(block * block_rows, (block + 1) * block_rows)
+        total[rows] = jnp.dot(weights_ref[block], value, preferred_element_type=F32)
+        if block % PART == 0:
+            latent_in[block // PART].wait()
         for strip in strips(rows):
             out_ref[strip] = (latent_ref[strip].astype(F32) + total[strip]).astype(BF16)
+        if block % PART == PART - 1:
+            outs[block // PART].start()
+    for started in outs:
+        started.wait()
 
 
 def whole(array):
@@ -271,32 +320,37 @@
         return pltpu.with_memory_space_constraint(array, pltpu.HBM)
 
     gain = embed_gain.reshape(1, width)
-    per_step = 8
-    rows = per_step * block_rows
+    in_vmem = pl.BlockSpec(memory_space=pltpu.VMEM)
+    in_any = pl.BlockSpec(memory_space=pl.ANY)
+    grid_rows = blk_count * block_rows
+    parts, part_rows = blk_count // PART, PART * block_rows
     counts = (chips * slots, 2 * slots, (chips - 2) * slots)
     latent, kept, sent_far, sent_rest, table = pl.pallas_call(
-        functools.partial(embed_kernel, ring, per_step, slots),
-        out_shape=[pltpu.HBM((blk_count * block_rows, width), BF16)]
+        functools.partial(embed_kernel, ring, slots),
+        out_shape=[pltpu.HBM((grid_rows, width), BF16)]
         + [shape((count + 1, tile_rows, width)) for count in counts]
         + [shape((4, entries), jnp.int32)],
         grid_spec=pltpu.PrefetchScalarGridSpec(
             num_scalar_prefetch=3,
-            grid=(blk_count // per_step,),
-            in_specs=[
-                pl.BlockSpec((channels, rows), lambda i, *_: (0, i)),
-                whole(embed_in),
-                whole(embed_out),
-                whole(gain),
-                pl.BlockSpec((per_step,) + interp.shape[1:], lambda i, *_: (i, 0, 0, 0)),
+            grid=(1,),
+            in_specs=[in_any] * 3 + [whole(gain), in_any],
+            out_specs=[in_any]
+            + [in_vmem] * len(counts)
+            + [pl.BlockSpec(memory_space=pltpu.SMEM)],
+            scratch_shapes=[
+                pltpu.VMEM((parts, channels, part_rows), BF16),
+                pltpu.VMEM(embed_in.shape, BF16),
+                pltpu.VMEM(embed_out.shape, BF16),
+                pltpu.VMEM(interp.shape, BF16),
+                pltpu.VMEM((grid_rows, width), F32),
+                pltpu.VMEM((grid_rows, width), BF16),
+                pltpu.VMEM((grid_rows, width), BF16),
+                pltpu.SemaphoreType.DMA((2 + 3 * parts,)),
             ],
-            out_specs=[pl.BlockSpec((rows, width), lambda i, *_: (i, 0))]
-            + [pl.BlockSpec(memory_space=pltpu.VMEM)] * len(counts)
-            + [pl.BlockSpec(memory_space=pltpu.SMEM)],
-            scratch_shapes=[pltpu.VMEM((rows, width), F32), pltpu.VMEM((rows, width), BF16)],
         ),
-        compiler_params=params(32),
+        compiler_params=params(40),
         cost_estimate=cost(
-            2 * blk_count * block_rows * width * (channels + width + list_len * tile_rows),
+            2 * grid_rows * width * (channels + width + list_len * tile_rows),
             grid_features,
             interp,
         ),
@@ -305,8 +359,7 @@
     other_far = ring.over_core(sent_far)
 
     dense = (tiles, tile_rows, width)
-    in_vmem = pl.BlockSpec(memory_space=pltpu.VMEM)
-    in_any = pl.BlockSpec(memory_space=pl.ANY)
+
     def in_order(value, token):
         return pl.pallas_call(
             order_kernel,
@@ -432,32 +485,26 @@
         first, second = onward, after
     share((chips - 1) * slots, first, first)
 
-    per_step = 4
-    rows = per_step * block_rows
     grid_out = pl.pallas_call(
-        functools.partial(back_kernel, starts, list_len, per_step),
-        out_shape=shape((blk_count * block_rows, width)),
+        functools.partial(back_kernel, starts, list_len),
+        out_shape=shape((grid_rows, width)),
         grid_spec=pltpu.PrefetchScalarGridSpec(
             num_scalar_prefetch=1,
-            grid=(blk_count // per_step,),
-            in_specs=[
-                pl.BlockSpec((rows, width), lambda i, *_: (i, 0)),
-                pl.BlockSpec((per_step,) + weights.shape[1:], lambda i, *_: (i, 0, 0)),
-            ]
-            + [pl.BlockSpec(memory_space=pl.ANY)] * len(pieces),
-            out_specs=pl.BlockSpec((rows, width), lambda i, *_: (i, 0)),
+            grid=(1,),
+            in_specs=[in_vmem] + [in_any] * (1 + len(pieces)),
+            out_specs=in_any,
             scratch_shapes=[
                 pltpu.VMEM((N_CORE * ((chips - 1) * slots + tiles) * tile_rows, width), BF16),
-                pltpu.VMEM((rows, width), F32),
-                pltpu.SemaphoreType.DMA((len(pieces),)),
+                pltpu.VMEM((grid_rows, width), BF16),
+                pltpu.VMEM((grid_rows, width), F32),
+                pltpu.VMEM((grid_rows, width), BF16),
+                pltpu.SemaphoreType.DMA((len(pieces) + 2 * parts,)),
             ],
         ),
-        compiler_params=params(20),
-        cost_estimate=cost(
-            2 * blk_count * block_rows * width * list_len * tile_rows, latent, latent, interp
-        ),
+        compiler_params=params(32),
+        cost_estimate=cost(2 * grid_rows * width * list_len * tile_rows, latent, latent, interp),
         name="back",
-    )(table, in_hbm(latent), weights, *pieces)
+    )(table, weights, in_hbm(latent), *pieces)
     return (grid_out, mesh_out)
 
 

time: 78.6 us -> 80.5 us (1.024)
  Pallas kernels: 23.6 us -> 25.4 us
    pallas_call x2, Pallas kernels: 17.5 us -> 19.4 us  [the longest x1 14.3 us: on_device(): pl.pallas_call(functools.partial(embed_kernel, ring, slots), out_shape=[p...]
where the time goes in v10:
time: 80.5 us; the launch traced here: 80.3 us
  waiting for transfers between devices  28.8 us (36%)
  Pallas kernels  25.4 us (32%)
  starting transfers between devices  25.3 us (31%)
  between operations  0.82 us (1%)
    ppermute x14, waiting for transfers between devices, over(): return lax.ppermute(value, 'band', pairs)  26.1 us
    ppermute x14, starting transfers between devices, over(): return lax.ppermute(value, 'band', pairs)  23.7 us
    pallas_call x1, Pallas kernels, on_device(): pl.pallas_call(functools.partial(embed_kernel, ring, slots), out_shape=[p...  14.3 us
    pallas_call x1, Pallas kernels, on_device(): pl.pallas_call(functools.partial(back_kernel, starts, list_len), out_shap...  5.02 us
    ppermute x6, waiting for transfers between devices, over_core(): return lax.ppermute(value, 'band', [(i, i ^ 1) for i in range(self.n_band)])  2.73 us
    pallas_call x3, Pallas kernels, pick(): pl.pallas_call(functools.partial(pick_kernel, chosen, slots, chips, tile_...  1.83 us
  transfers between devices with their start and end apart: 20, of which 15 were waited for; matrix products, arithmetic and copies ran while one was open for 0% of the time, Pallas kernels for 5%

profile of v10, /device:TPU:0, one launch (start us, length us, event | category | flops | bytes accessed | tf_op | source)
XLA Modules:
  0.0 80.3 jit_solution(11514281798619515806)
XLA Ops:
  0.6 14.3 %embed.1 = (bf16[4096,512]{1,0:T(8,128)(2,1)}, bf16[33,32,512]{2,1,0:T(8,128)(2,1)S(1)}, bf16[9,32,512]{2,1,0:T(8,128)(2,1)S(1)}, bf16[25,32,512]{2,1,0:T(8,128)(2,1)S(1)}, s32[4,64]{1,0:T(4,128)S(1)}) custom-call(s32[1]{0:T(128)} %bitcast.me_ref, s32[4,256]{1,0:T(4,128)} %bitcast.8, s32[4,256]{1,0:T(4,128)} %bitcast.9, bf16[227,4096]{1,0:T(8,128)(2,1)} %bitcast.7, ...), custom_call_target="tpu_custom_call" | custom-call | flops 3636461568 | bytes 2908160 | tf_op jit(solution)/shard_map/embed/pallas_call | solution.py:328
  15.5 1.2 %collective-permute-done.other = bf16[9,32,512]{2,1,0:T(8,128)(2,1)S(1)} collective-permute-done((bf16[9,32,512]{2,1,0:T(8,128)(2,1)S(1)}, bf16[9,32,512]{2,1,0:T(8,128)(2,1)S(1)}, u32[]{:S(2)}, u32[]{:S(2)}) %collective-permute-start) | collective-permute-done | bytes 294944 | tf_op jit(solution)/shard_map/ppermute | solution.py:52
  16.7 0.8 far_sums.1
  18.0 2.7 %collective-permute-start.2 = (bf16[8,32,512]{2,1,0:T(8,128)(2,1)S(1)}, bf16[8,32,512]{2,1,0:T(8,128)(2,1)S(1)}, u32[]{:S(2)}, u32[]{:S(2)}) collective-permute-start(bf16[8,32,512]{2,1,0:T(8,128)(2,1)S(1)} %get-tuple-element.21.refs_1_), channel_id=1, source_target_pairs={{0,4},{1,3},{2,0},{3,7},{4,8},{5,1},{6,2},{7,11},{8,12},{9,5},{10,... | collective-permute-start | bytes 786440 | tf_op jit(solution)/shard_map/ppermute | solution.py:61
  20.7 1.6 %collective-permute-start.4 = (bf16[8,32,512]{2,1,0:T(8,128)(2,1)S(1)}, bf16[8,32,512]{2,1,0:T(8,128)(2,1)S(1)}, u32[]{:S(2)}, u32[]{:S(2)}) collective-permute-start(bf16[8,32,512]{2,1,0:T(8,128)(2,1)S(1)} %get-tuple-element.23), channel_id=1, source_target_pairs={{0,4},{1,3},{2,0},{3,7},{4,8},{5,1},{6,2},{7,11},{8,12},{9,5},{10,... | collective-permute-start | bytes 786440 | tf_op jit(solution)/shard_map/ppermute | solution.py:61
  22.3 1.2 %own_sums.1.token.own = f32[6,8,32,512]{3,2,1,0:T(8,128)S(1)} custom-call(s32[4,64]{1,0:T(4,128)S(1)} %get-tuple-element.17.table_ref, bf16[33,32,512]{2,1,0:T(8,128)(2,1)S(1)} %get-tuple-element.18.kept, bf16[25,32,512]{2,1,0:T(8,128)(2,1)S(1)} %collective-permute-done.1.other), custom_call_target="tpu_custom_call" | custom-call | bytes 4325376 | tf_op jit(solution)/shard_map/own_sums/pallas_call | solution.py:390
  24.0 1.0 %collective-permute-done.2.came = bf16[8,32,512]{2,1,0:T(8,128)(2,1)S(1)} collective-permute-done((bf16[8,32,512]{2,1,0:T(8,128)(2,1)S(1)}, bf16[8,32,512]{2,1,0:T(8,128)(2,1)S(1)}, u32[]{:S(2)}, u32[]{:S(2)}) %collective-permute-start.2) | collective-permute-done | bytes 262176 | tf_op jit(solution)/shard_map/ppermute | solution.py:61
  25.0 2.1 %collective-permute-start.3 = (bf16[8,32,512]{2,1,0:T(8,128)(2,1)S(1)}, bf16[8,32,512]{2,1,0:T(8,128)(2,1)S(1)}, u32[]{:S(2)}, u32[]{:S(2)}) collective-permute-start(bf16[8,32,512]{2,1,0:T(8,128)(2,1)S(1)} %add_5.1.token), channel_id=1, source_target_pairs={{0,4},{1,3},{2,0},{3,7},{4,8},{5,1},{6,2},{7,11},{8,12},{9,5},{10,... | collective-permute-start | bytes 786440 | tf_op jit(solution)/shard_map/ppermute | solution.py:61
  27.2 0.6 collective-permute-done.4.came
  27.8 2.1 %collective-permute-start.6 = (bf16[8,32,512]{2,1,0:T(8,128)(2,1)S(1)}, bf16[8,32,512]{2,1,0:T(8,128)(2,1)S(1)}, u32[]{:S(2)}, u32[]{:S(2)}) collective-permute-start(bf16[8,32,512]{2,1,0:T(8,128)(2,1)S(1)} %add_4.1.token), channel_id=1, source_target_pairs={{0,4},{1,3},{2,0},{3,7},{4,8},{5,1},{6,2},{7,11},{8,12},{9,5},{10,... | collective-permute-start | bytes 786440 | tf_op jit(solution)/shard_map/ppermute | solution.py:61
  30.0 1.5 %collective-permute-done.3.came = bf16[8,32,512]{2,1,0:T(8,128)(2,1)S(1)} collective-permute-done((bf16[8,32,512]{2,1,0:T(8,128)(2,1)S(1)}, bf16[8,32,512]{2,1,0:T(8,128)(2,1)S(1)}, u32[]{:S(2)}, u32[]{:S(2)}) %collective-permute-start.3) | collective-permute-done | bytes 262176 | tf_op jit(solution)/shard_map/ppermute | solution.py:61
  31.5 2.1 %collective-permute-start.5 = (bf16[8,32,512]{2,1,0:T(8,128)(2,1)S(1)}, bf16[8,32,512]{2,1,0:T(8,128)(2,1)S(1)}, u32[]{:S(2)}, u32[]{:S(2)}) collective-permute-start(bf16[8,32,512]{2,1,0:T(8,128)(2,1)S(1)} %add_3.1.token), channel_id=1, source_target_pairs={{0,4},{1,3},{2,0},{3,7},{4,8},{5,1},{6,2},{7,11},{8,12},{9,5},{10,... | collective-permute-start | bytes 786440 | tf_op jit(solution)/shard_map/ppermute | solution.py:61
  34.7 3.2 %collective-permute-done.5.came = bf16[8,32,512]{2,1,0:T(8,128)(2,1)S(1)} collective-permute-done((bf16[8,32,512]{2,1,0:T(8,128)(2,1)S(1)}, bf16[8,32,512]{2,1,0:T(8,128)(2,1)S(1)}, u32[]{:S(2)}, u32[]{:S(2)}) %collective-permute-start.5) | collective-permute-done | bytes 262176 | tf_op jit(solution)/shard_map/ppermute | solution.py:61
  38.0 2.1 %collective-permute-start.7 = (bf16[8,32,512]{2,1,0:T(8,128)(2,1)S(1)}, bf16[8,32,512]{2,1,0:T(8,128)(2,1)S(1)}, u32[]{:S(2)}, u32[]{:S(2)}) collective-permute-start(bf16[8,32,512]{2,1,0:T(8,128)(2,1)S(1)} %add_1.1), channel_id=1, source_target_pairs={{0,4},{1,3},{2,0},{3,7},{4,8},{5,1},{6,2},{7,11},{8,12},{9,5},{10,... | collective-permute-start | bytes 786440 | tf_op jit(solution)/shard_map/ppermute | solution.py:61
  40.4 4.1 %collective-permute-done.7.came = bf16[8,32,512]{2,1,0:T(8,128)(2,1)S(1)} collective-permute-done((bf16[8,32,512]{2,1,0:T(8,128)(2,1)S(1)}, bf16[8,32,512]{2,1,0:T(8,128)(2,1)S(1)}, u32[]{:S(2)}, u32[]{:S(2)}) %collective-permute-start.7) | collective-permute-done | bytes 262176 | tf_op jit(solution)/shard_map/ppermute | solution.py:61
  44.5 1.5 %mesh_step.1 = (bf16[256,512]{1,0:T(8,128)(2,1)}, bf16[256,512]{1,0:T(8,128)(2,1)S(1)}) custom-call(bf16[256,512]{1,0:T(8,128)(2,1)S(1)} %copy-done.3, bf16[512,512]{1,0:T(8,128)(2,1)S(1)} %copy-done.1, bf16[512,512]{1,0:T(8,128)(2,1)S(1)} %copy-done.2, f32[1,512]{1,0:T(1,128)S(1)} %bitcast.6, f32[6,8,32,512]{3,2,1,0:T(8,128)S(1)} %own_sums.1.token.own, ...), custom_call_target="tpu_custom_call" | custom-call | flops 268435456 | bytes 1048576 | tf_op jit(solution)/shard_map/mesh_step/pallas_call | solution.py:437
  45.9 2.0 %collective-permute-start.9 = (bf16[256,512]{1,0:T(8,128)(2,1)S(1)}, bf16[256,512]{1,0:T(8,128)(2,1)S(1)}, u32[]{:S(2)}, u32[]{:S(2)}) collective-permute-start(bf16[256,512]{1,0:T(8,128)(2,1)S(1)} %get-tuple-element.24.refs_1_.refs_0_), channel_id=1, source_target_pairs={{0,2},{1,5},{2,6},{3,1},{4,0},{5,9},{6,10},{7,3},{8,4},{9,13},{10,... | collective-permute-start | bytes 786440 | tf_op jit(solution)/shard_map/ppermute | solution.py:61
  48.0 5.8 %collective-permute-done.9.refs_0_ = bf16[256,512]{1,0:T(8,128)(2,1)S(1)} collective-permute-done((bf16[256,512]{1,0:T(8,128)(2,1)S(1)}, bf16[256,512]{1,0:T(8,128)(2,1)S(1)}, u32[]{:S(2)}, u32[]{:S(2)}) %collective-permute-start.9) | collective-permute-done | bytes 262176 | tf_op jit(solution)/shard_map/ppermute | solution.py:61
  53.8 2.4 %collective-permute-start.12 = (bf16[256,512]{1,0:T(8,128)(2,1)S(1)}, bf16[256,512]{1,0:T(8,128)(2,1)S(1)}, u32[]{:S(2)}, u32[]{:S(2)}) collective-permute-start(bf16[256,512]{1,0:T(8,128)(2,1)S(1)} %in_order.8.refs_1_), channel_id=1, source_target_pairs={{0,2},{1,5},{2,6},{3,1},{4,0},{5,9},{6,10},{7,3},{8,4},{9,13},{10,... | collective-permute-start | bytes 786440 | tf_op jit(solution)/shard_map/ppermute | solution.py:61
  56.1 1.6 %collective-permute-start.13 = (bf16[256,512]{1,0:T(8,128)(2,1)S(1)}, bf16[256,512]{1,0:T(8,128)(2,1)S(1)}, u32[]{:S(2)}, u32[]{:S(2)}) collective-permute-start(bf16[256,512]{1,0:T(8,128)(2,1)S(1)} %in_order.9.refs_2_), channel_id=1, source_target_pairs={{0,2},{1,5},{2,6},{3,1},{4,0},{5,9},{6,10},{7,3},{8,4},{9,13},{10,... | collective-permute-start | bytes 786440 | tf_op jit(solution)/shard_map/ppermute | solution.py:61
  57.7 0.6 pick_0.1
  58.3 2.7 %collective-permute-done.12.refs_0_ = bf16[256,512]{1,0:T(8,128)(2,1)S(1)} collective-permute-done((bf16[256,512]{1,0:T(8,128)(2,1)S(1)}, bf16[256,512]{1,0:T(8,128)(2,1)S(1)}, u32[]{:S(2)}, u32[]{:S(2)}) %collective-permute-start.12) | collective-permute-done | bytes 262176 | tf_op jit(solution)/shard_map/ppermute | solution.py:61
  61.0 1.5 %collective-permute-start.15 = (bf16[256,512]{1,0:T(8,128)(2,1)S(1)}, bf16[256,512]{1,0:T(8,128)(2,1)S(1)}, u32[]{:S(2)}, u32[]{:S(2)}) collective-permute-start(bf16[256,512]{1,0:T(8,128)(2,1)S(1)} %in_order.10.refs_1_.refs_0_), channel_id=1, source_target_pairs={{0,2},{1,5},{2,6},{3,1},{4,0},{5,9},{6,10},{7,3},{8,4},{9,13},{10,... | collective-permute-start | bytes 786440 | tf_op jit(solution)/shard_map/ppermute | solution.py:61
  62.5 1.3 %collective-permute-done.13.refs_0_ = bf16[256,512]{1,0:T(8,128)(2,1)S(1)} collective-permute-done((bf16[256,512]{1,0:T(8,128)(2,1)S(1)}, bf16[256,512]{1,0:T(8,128)(2,1)S(1)}, u32[]{:S(2)}, u32[]{:S(2)}) %collective-permute-start.13) | collective-permute-done | bytes 262176 | tf_op jit(solution)/shard_map/ppermute | solution.py:61
  63.8 1.5 %collective-permute-start.16 = (bf16[256,512]{1,0:T(8,128)(2,1)S(1)}, bf16[256,512]{1,0:T(8,128)(2,1)S(1)}, u32[]{:S(2)}, u32[]{:S(2)}) collective-permute-start(bf16[256,512]{1,0:T(8,128)(2,1)S(1)} %in_order.11.refs_1_), channel_id=1, source_target_pairs={{0,2},{1,5},{2,6},{3,1},{4,0},{5,9},{6,10},{7,3},{8,4},{9,13},{10,... | collective-permute-start | bytes 786440 | tf_op jit(solution)/shard_map/ppermute | solution.py:61
  65.9 1.5 %collective-permute-done.15.refs_0_ = bf16[256,512]{1,0:T(8,128)(2,1)S(1)} collective-permute-done((bf16[256,512]{1,0:T(8,128)(2,1)S(1)}, bf16[256,512]{1,0:T(8,128)(2,1)S(1)}, u32[]{:S(2)}, u32[]{:S(2)}) %collective-permute-start.15) | collective-permute-done | bytes 262176 | tf_op jit(solution)/shard_map/ppermute | solution.py:61
  67.4 1.5 %collective-permute-start.18 = (bf16[256,512]{1,0:T(8,128)(2,1)S(1)}, bf16[256,512]{1,0:T(8,128)(2,1)S(1)}, u32[]{:S(2)}, u32[]{:S(2)}) collective-permute-start(bf16[256,512]{1,0:T(8,128)(2,1)S(1)} %in_order.12.refs_1_.refs_0_), channel_id=1, source_target_pairs={{0,2},{1,5},{2,6},{3,1},{4,0},{5,9},{6,10},{7,3},{8,4},{9,13},{10,... | collective-permute-start | bytes 786440 | tf_op jit(solution)/shard_map/ppermute | solution.py:61
  69.4 0.8 %collective-permute-done.16.refs_0_ = bf16[256,512]{1,0:T(8,128)(2,1)S(1)} collective-permute-done((bf16[256,512]{1,0:T(8,128)(2,1)S(1)}, bf16[256,512]{1,0:T(8,128)(2,1)S(1)}, u32[]{:S(2)}, u32[]{:S(2)}) %collective-permute-start.16) | collective-permute-done | bytes 262176 | tf_op jit(solution)/shard_map/ppermute | solution.py:61
  70.2 0.6 pick_5.1
  70.9 2.9 %collective-permute-done.18.rest_6_ = bf16[256,512]{1,0:T(8,128)(2,1)S(1)} collective-permute-done((bf16[256,512]{1,0:T(8,128)(2,1)S(1)}, bf16[256,512]{1,0:T(8,128)(2,1)S(1)}, u32[]{:S(2)}, u32[]{:S(2)}) %collective-permute-start.18) | collective-permute-done | bytes 262176 | tf_op jit(solution)/shard_map/ppermute | solution.py:61
  73.8 1.5 %collective-permute-done.19.rest_7_ = bf16[256,512]{1,0:T(8,128)(2,1)S(1)} collective-permute-done((bf16[256,512]{1,0:T(8,128)(2,1)S(1)}, bf16[256,512]{1,0:T(8,128)(2,1)S(1)}, u32[]{:S(2)}, u32[]{:S(2)}) %collective-permute-start.19) | collective-permute-done | bytes 262176 | tf_op jit(solution)/shard_map/ppermute | solution.py:52
  75.3 5.0 %back.1 = bf16[4096,512]{1,0:T(8,128)(2,1)} custom-call(s32[4,64]{1,0:T(4,128)S(1)} %get-tuple-element.17.table_ref, bf16[16,256,128]{2,1,0:T(8,128)(2,1)S(1)} %turn.1.token.weights_ref, bf16[4096,512]{1,0:T(8,128)(2,1)} %get-tuple-element.22.latent_any, bf16[384,512]{1,0:T(8,128)(2,1)S(1)} %get-tuple-element.25.refs_1_.rest_0_, ...), custom_call_target="tpu_custom_call" | custom-call | flops 536870912 | bytes 9437184 | tf_op jit(solution)/shard_map/back/pallas_call | solution.py:488
  (39 shorter events, 4.2 us)
Async XLA Ops:
  15.0 1.7 %collective-permute-start = (bf16[9,32,512]{2,1,0:T(8,128)(2,1)S(1)}, bf16[9,32,512]{2,1,0:T(8,128)(2,1)S(1)}, u32[]{:S(2)}, u32[]{:S(2)}) collective-permute-start(bf16[9,32,512]{2,1,0:T(8,128)(2,1)S(1)} %get-tuple-element.20), channel_id=1, source_target_pairs={{0,1},{1,0},{2,3},{3,2},{4,5},{5,4},{6,7},{7,6},{8,9},{9,8},{10,11... | collective-permute-start | bytes 884744 | tf_op jit(solution)/shard_map/ppermute | solution.py:52
  17.5 5.9 %copy-start = (bf16[16,4,32,256]{3,2,1,0:T(8,128)(2,1)S(1)}, bf16[16,4,32,256]{3,2,1,0:T(8,128)(2,1)}, u32[]{:S(2)}) copy-start(bf16[16,4,32,256]{3,2,1,0:T(8,128)(2,1)} %interp_ref.1) | copy-start | bytes 3145732
  17.5 4.7 %collective-permute-start.1 = (bf16[25,32,512]{2,1,0:T(8,128)(2,1)S(1)}, bf16[25,32,512]{2,1,0:T(8,128)(2,1)S(1)}, u32[]{:S(2)}, u32[]{:S(2)}) collective-permute-start(bf16[25,32,512]{2,1,0:T(8,128)(2,1)S(1)} %in_order.7), channel_id=1, source_target_pairs={{0,1},{1,0},{2,3},{3,2},{4,5},{5,4},{6,7},{7,6},{8,9},{9,8},{10,11... | collective-permute-start | bytes 2457608 | tf_op jit(solution)/shard_map/ppermute | solution.py:52
  18.0 7.0 %collective-permute-start.2 = (bf16[8,32,512]{2,1,0:T(8,128)(2,1)S(1)}, bf16[8,32,512]{2,1,0:T(8,128)(2,1)S(1)}, u32[]{:S(2)}, u32[]{:S(2)}) collective-permute-start(bf16[8,32,512]{2,1,0:T(8,128)(2,1)S(1)} %get-tuple-element.21.refs_1_), channel_id=1, source_target_pairs={{0,4},{1,3},{2,0},{3,7},{4,8},{5,1},{6,2},{7,11},{8,12},{9,5},{10,... | collective-permute-start | bytes 786440 | tf_op jit(solution)/shard_map/ppermute | solution.py:61
  20.7 7.1 %collective-permute-start.4 = (bf16[8,32,512]{2,1,0:T(8,128)(2,1)S(1)}, bf16[8,32,512]{2,1,0:T(8,128)(2,1)S(1)}, u32[]{:S(2)}, u32[]{:S(2)}) collective-permute-start(bf16[8,32,512]{2,1,0:T(8,128)(2,1)S(1)} %get-tuple-element.23), channel_id=1, source_target_pairs={{0,4},{1,3},{2,0},{3,7},{4,8},{5,1},{6,2},{7,11},{8,12},{9,5},{10,... | collective-permute-start | bytes 786440 | tf_op jit(solution)/shard_map/ppermute | solution.py:61
  25.0 6.4 %collective-permute-start.3 = (bf16[8,32,512]{2,1,0:T(8,128)(2,1)S(1)}, bf16[8,32,512]{2,1,0:T(8,128)(2,1)S(1)}, u32[]{:S(2)}, u32[]{:S(2)}) collective-permute-start(bf16[8,32,512]{2,1,0:T(8,128)(2,1)S(1)} %add_5.1.token), channel_id=1, source_target_pairs={{0,4},{1,3},{2,0},{3,7},{4,8},{5,1},{6,2},{7,11},{8,12},{9,5},{10,... | collective-permute-start | bytes 786440 | tf_op jit(solution)/shard_map/ppermute | solution.py:61
  27.8 6.4 %collective-permute-start.6 = (bf16[8,32,512]{2,1,0:T(8,128)(2,1)S(1)}, bf16[8,32,512]{2,1,0:T(8,128)(2,1)S(1)}, u32[]{:S(2)}, u32[]{:S(2)}) collective-permute-start(bf16[8,32,512]{2,1,0:T(8,128)(2,1)S(1)} %add_4.1.token), channel_id=1, source_target_pairs={{0,4},{1,3},{2,0},{3,7},{4,8},{5,1},{6,2},{7,11},{8,12},{9,5},{10,... | collective-permute-start | bytes 786440 | tf_op jit(solution)/shard_map/ppermute | solution.py:61
  31.5 13.0 %copy-start.1 = (bf16[512,512]{1,0:T(8,128)(2,1)S(1)}, bf16[512,512]{1,0:T(8,128)(2,1)}, u32[]{:S(2)}) copy-start(bf16[512,512]{1,0:T(8,128)(2,1)} %up_ref.1) | copy-start | bytes 1572868
  31.5 13.0 %copy-start.2 = (bf16[512,512]{1,0:T(8,128)(2,1)S(1)}, bf16[512,512]{1,0:T(8,128)(2,1)}, u32[]{:S(2)}) copy-start(bf16[512,512]{1,0:T(8,128)(2,1)} %down_ref.1) | copy-start | bytes 1572868
  31.5 12.9 %copy-start.3 = (bf16[256,512]{1,0:T(8,128)(2,1)S(1)}, bf16[256,512]{1,0:T(8,128)(2,1)}, u32[]{:S(2)}) copy-start(bf16[256,512]{1,0:T(8,128)(2,1)} %latent_ref.1) | copy-start | bytes 786436
  31.5 12.9 %copy-start.4 = (f32[512]{0:T(512)S(1)}, f32[512]{0:T(512)}, u32[]{:S(2)}) copy-start(f32[512]{0:T(512)} %param.21) | copy-start | bytes 6148
  31.5 6.4 %collective-permute-start.5 = (bf16[8,32,512]{2,1,0:T(8,128)(2,1)S(1)}, bf16[8,32,512]{2,1,0:T(8,128)(2,1)S(1)}, u32[]{:S(2)}, u32[]{:S(2)}) collective-permute-start(bf16[8,32,512]{2,1,0:T(8,128)(2,1)S(1)} %add_3.1.token), channel_id=1, source_target_pairs={{0,4},{1,3},{2,0},{3,7},{4,8},{5,1},{6,2},{7,11},{8,12},{9,5},{10,... | collective-permute-start | bytes 786440 | tf_op jit(solution)/shard_map/ppermute | solution.py:61
  34.3 6.1 %collective-permute-start.8 = (bf16[8,32,512]{2,1,0:T(8,128)(2,1)S(1)}, bf16[8,32,512]{2,1,0:T(8,128)(2,1)S(1)}, u32[]{:S(2)}, u32[]{:S(2)}) collective-permute-start(bf16[8,32,512]{2,1,0:T(8,128)(2,1)S(1)} %add_2.1.token), channel_id=1, source_target_pairs={{0,5},{1,2},{2,1},{3,6},{4,9},{5,0},{6,3},{7,10},{8,13},{9,4},{10,... | collective-permute-start | bytes 786440 | tf_op jit(solution)/shard_map/ppermute | solution.py:61
  38.0 6.4 %collective-permute-start.7 = (bf16[8,32,512]{2,1,0:T(8,128)(2,1)S(1)}, bf16[8,32,512]{2,1,0:T(8,128)(2,1)S(1)}, u32[]{:S(2)}, u32[]{:S(2)}) collective-permute-start(bf16[8,32,512]{2,1,0:T(8,128)(2,1)S(1)} %add_1.1), channel_id=1, source_target_pairs={{0,4},{1,3},{2,0},{3,7},{4,8},{5,1},{6,2},{7,11},{8,12},{9,5},{10,... | collective-permute-start | bytes 786440 | tf_op jit(solution)/shard_map/ppermute | solution.py:61
  45.9 7.8 %collective-permute-start.9 = (bf16[256,512]{1,0:T(8,128)(2,1)S(1)}, bf16[256,512]{1,0:T(8,128)(2,1)S(1)}, u32[]{:S(2)}, u32[]{:S(2)}) collective-permute-start(bf16[256,512]{1,0:T(8,128)(2,1)S(1)} %get-tuple-element.24.refs_1_.refs_0_), channel_id=1, source_target_pairs={{0,2},{1,5},{2,6},{3,1},{4,0},{5,9},{6,10},{7,3},{8,4},{9,13},{10,... | collective-permute-start | bytes 786440 | tf_op jit(solution)/shard_map/ppermute | solution.py:61
  48.0 8.2 %collective-permute-start.10 = (bf16[256,512]{1,0:T(8,128)(2,1)S(1)}, bf16[256,512]{1,0:T(8,128)(2,1)S(1)}, u32[]{:S(2)}, u32[]{:S(2)}) collective-permute-start(bf16[256,512]{1,0:T(8,128)(2,1)S(1)} %get-tuple-element.24.refs_1_.refs_0_), channel_id=1, source_target_pairs={{0,5},{1,2},{2,1},{3,6},{4,9},{5,0},{6,3},{7,10},{8,13},{9,4},{10,... | collective-permute-start | bytes 786440 | tf_op jit(solution)/shard_map/ppermute | solution.py:61
  53.8 7.3 %collective-permute-start.12 = (bf16[256,512]{1,0:T(8,128)(2,1)S(1)}, bf16[256,512]{1,0:T(8,128)(2,1)S(1)}, u32[]{:S(2)}, u32[]{:S(2)}) collective-permute-start(bf16[256,512]{1,0:T(8,128)(2,1)S(1)} %in_order.8.refs_1_), channel_id=1, source_target_pairs={{0,2},{1,5},{2,6},{3,1},{4,0},{5,9},{6,10},{7,3},{8,4},{9,13},{10,... | collective-permute-start | bytes 786440 | tf_op jit(solution)/shard_map/ppermute | solution.py:61
  56.1 7.7 %collective-permute-start.13 = (bf16[256,512]{1,0:T(8,128)(2,1)S(1)}, bf16[256,512]{1,0:T(8,128)(2,1)S(1)}, u32[]{:S(2)}, u32[]{:S(2)}) collective-permute-start(bf16[256,512]{1,0:T(8,128)(2,1)S(1)} %in_order.9.refs_2_), channel_id=1, source_target_pairs={{0,2},{1,5},{2,6},{3,1},{4,0},{5,9},{6,10},{7,3},{8,4},{9,13},{10,... | collective-permute-start | bytes 786440 | tf_op jit(solution)/shard_map/ppermute | solution.py:61
  61.0 6.4 %collective-permute-start.15 = (bf16[256,512]{1,0:T(8,128)(2,1)S(1)}, bf16[256,512]{1,0:T(8,128)(2,1)S(1)}, u32[]{:S(2)}, u32[]{:S(2)}) collective-permute-start(bf16[256,512]{1,0:T(8,128)(2,1)S(1)} %in_order.10.refs_1_.refs_0_), channel_id=1, source_target_pairs={{0,2},{1,5},{2,6},{3,1},{4,0},{5,9},{6,10},{7,3},{8,4},{9,13},{10,... | collective-permute-start | bytes 786440 | tf_op jit(solution)/shard_map/ppermute | solution.py:61
  63.8 6.4 %collective-permute-start.16 = (bf16[256,512]{1,0:T(8,128)(2,1)S(1)}, bf16[256,512]{1,0:T(8,128)(2,1)S(1)}, u32[]{:S(2)}, u32[]{:S(2)}) collective-permute-start(bf16[256,512]{1,0:T(8,128)(2,1)S(1)} %in_order.11.refs_1_), channel_id=1, source_target_pairs={{0,2},{1,5},{2,6},{3,1},{4,0},{5,9},{6,10},{7,3},{8,4},{9,13},{10,... | collective-permute-start | bytes 786440 | tf_op jit(solution)/shard_map/ppermute | solution.py:61
  67.4 6.4 %collective-permute-start.18 = (bf16[256,512]{1,0:T(8,128)(2,1)S(1)}, bf16[256,512]{1,0:T(8,128)(2,1)S(1)}, u32[]{:S(2)}, u32[]{:S(2)}) collective-permute-start(bf16[256,512]{1,0:T(8,128)(2,1)S(1)} %in_order.12.refs_1_.refs_0_), channel_id=1, source_target_pairs={{0,2},{1,5},{2,6},{3,1},{4,0},{5,9},{6,10},{7,3},{8,4},{9,13},{10,... | collective-permute-start | bytes 786440 | tf_op jit(solution)/shard_map/ppermute | solution.py:61
  68.9 4.9 %collective-permute-start.11 = (bf16[384,512]{1,0:T(8,128)(2,1)S(1)}, bf16[384,512]{1,0:T(8,128)(2,1)S(1)}, u32[]{:S(2)}, u32[]{:S(2)}) collective-permute-start(bf16[384,512]{1,0:T(8,128)(2,1)S(1)} %get-tuple-element.26), channel_id=1, source_target_pairs={{0,1},{1,0},{2,3},{3,2},{4,5},{5,4},{6,7},{7,6},{8,9},{9,8},{10,11... | collective-permute-start | bytes 1179656 | tf_op jit(solution)/shard_map/ppermute | solution.py:52
  68.9 4.9 %collective-permute-start.14 = (bf16[256,512]{1,0:T(8,128)(2,1)S(1)}, bf16[256,512]{1,0:T(8,128)(2,1)S(1)}, u32[]{:S(2)}, u32[]{:S(2)}) collective-permute-start(bf16[256,512]{1,0:T(8,128)(2,1)S(1)} %get-tuple-element.28), channel_id=1, source_target_pairs={{0,1},{1,0},{2,3},{3,2},{4,5},{5,4},{6,7},{7,6},{8,9},{9,8},{10,11... | collective-permute-start | bytes 786440 | tf_op jit(solution)/shard_map/ppermute | solution.py:52
  70.8 3.0 %collective-permute-start.17 = (bf16[256,512]{1,0:T(8,128)(2,1)S(1)}, bf16[256,512]{1,0:T(8,128)(2,1)S(1)}, u32[]{:S(2)}, u32[]{:S(2)}) collective-permute-start(bf16[256,512]{1,0:T(8,128)(2,1)S(1)} %get-tuple-element.30), channel_id=1, source_target_pairs={{0,1},{1,0},{2,3},{3,2},{4,5},{5,4},{6,7},{7,6},{8,9},{9,8},{10,11... | collective-permute-start | bytes 786440 | tf_op jit(solution)/shard_map/ppermute | solution.py:52
  73.8 1.5 %collective-permute-start.19 = (bf16[256,512]{1,0:T(8,128)(2,1)S(1)}, bf16[256,512]{1,0:T(8,128)(2,1)S(1)}, u32[]{:S(2)}, u32[]{:S(2)}) collective-permute-start(bf16[256,512]{1,0:T(8,128)(2,1)S(1)} %collective-permute-done.18.rest_6_), channel_id=1, source_target_pairs={{0,1},{1,0},{2,3},{3,2},{4,5},{5,4},{6,7},{7,6},{8,9},{9,8},{10,11... | collective-permute-start | bytes 786440 | tf_op jit(solution)/shard_map/ppermute | solution.py:52

commit v11 on v10

--- a/solution.py
+++ b/solution.py
@@ -11,7 +11,8 @@
 BF16 = jnp.bfloat16
 N_CORE = 2
 STRIP = 32
-PART = 4
+PART = 2
+BACK_PART = 4
 
 
 def silu(values):
@@ -80,64 +81,73 @@
 def embed_kernel(
     ring, slots, me_ref, lists_ref, mask_ref, x_any, w1_any, w2_any, gain_ref, interp_any,
     latent_any, kept_ref, far_ref, rest_ref, table_ref,
-    x_ref, w1_ref, w2_ref, interp_ref, wide, hidden, latent_ref, sems,
+    x_ref, w1_ref, w2_ref, interp_ref, wide, hidden, before, latent_ref, sems,
 ):
     me = me_ref[0]
     blk_count, list_len, tile_rows, block_rows = interp_ref.shape
     groups = ring.chips
-    parts = x_ref.shape[0]
-    part_rows = x_ref.shape[2]
+    parts, _, part_rows = x_ref.shape
     part_blocks = part_rows // block_rows
-    spans = [slice(i * part_rows, (i + 1) * part_rows) for i in range(parts)]
-
-    copies = []
-
-    def copy(source, target):
-        copies.append(pltpu.make_async_copy(source, target, sems.at[len(copies)]))
-        return copies[-1]
-
-    w1_in, w2_in = copy(w1_any, w1_ref), copy(w2_any, w2_ref)
-    x_in = [copy(x_any.at[:, pl.ds(s.start, part_rows)], x_ref.at[i]) for i, s in enumerate(spans)]
-    interp_in = []
-    for i in range(parts):
-        blocks = pl.ds(i * part_blocks, part_blocks)
-        interp_in.append(copy(interp_any.at[blocks], interp_ref.at[blocks]))
-    latent_out = []
-    for s in spans:
-        rows = pl.ds(s.start, part_rows)
-        latent_out.append(copy(latent_ref.at[rows], latent_any.at[rows]))
-    for started in (w1_in, x_in[0], w2_in, interp_in[0]):
-        started.start()
+    chunk = slice(0, part_rows)
+
+    def rows_of(i):
+        return pl.ds(pl.multiple_of(i * part_rows, part_rows), part_rows)
+
+    def blocks_of(i):
+        return pl.ds(i * part_blocks, part_blocks)
+
+    w1_in = pltpu.make_async_copy(w1_any, w1_ref, sems.at[0])
+    w2_in = pltpu.make_async_copy(w2_any, w2_ref, sems.at[1])
+
+    def x_in(i):
+        return pltpu.make_async_copy(x_any.at[:, rows_of(i)], x_ref.at[i], sems.at[2 + i])
+
+    def interp_in(i):
+        blocks = blocks_of(i)
+        return pltpu.make_async_copy(
+            interp_any.at[blocks], interp_ref.at[blocks], sems.at[2 + parts + i]
+        )
+
+    def latent_out(i):
+        rows = rows_of(i)
+        return pltpu.make_async_copy(
+            latent_ref.at[rows], latent_any.at[rows], sems.at[2 + 2 * parts + i]
+        )
+
+    w1_in.start()
+    x_in(0).start()
+    w2_in.start()
+    interp_in(0).start()
     for i in range(1, parts):
-        x_in[i].start()
-        interp_in[i].start()
+        x_in(i).start()
+        interp_in(i).start()
+    w1_in.wait()
+    w2_in.wait()
 
     def spot(index, block, k):
         across, group, tile = ring.entry(lists_ref, index, index * blk_count + block, k)
-        return across, group, tile, (block * list_len + k) // ring.n_band
+        return across, group, tile, split(block * list_len + k, ring.n_band)[0]
 
     kept_spare, far_spare, rest_spare = (ref.shape[0] - 1 for ref in (kept_ref, far_ref, rest_ref))
 
-    def first_layer(i):
-        x_in[i].wait()
-        wide[spans[i]] = lax.dot_general(
+    def one_chunk(i, carry):
+        x_in(i).wait()
+        wide[...] = lax.dot_general(
             x_ref[i], w1_ref[...], (((0,), (0,)), ((), ())), preferred_element_type=F32
         )
-
-    def second_layer(i):
-        for strip in strips(spans[i]):
+        for strip in strips(chunk):
             hidden[strip] = silu(wide[strip]).astype(BF16)
-        wide[spans[i]] = jnp.dot(hidden[spans[i]], w2_ref[...], preferred_element_type=F32)
-
-    def listed_sums(i):
-        for strip in strips(spans[i]):
-            latent_ref[strip] = layer_norm(wide[strip], gain_ref[...]).astype(BF16)
-        latent_out[i].start()
-        interp_in[i].wait()
-        for block in range(i * part_blocks, (i + 1) * part_blocks):
+        before[...] = jnp.dot(hidden[...], w2_ref[...], preferred_element_type=F32)
+        for strip in strips(chunk):
+            rows = pl.ds(pl.multiple_of(i * part_rows + strip.start, STRIP), STRIP)
+            latent_ref[rows] = layer_norm(before[strip], gain_ref[...]).astype(BF16)
+        latent_out(i).start()
+        interp_in(i).wait()
+        for b in range(part_blocks):
+            block = i * part_blocks + b
             weights = interp_ref[block].reshape(list_len * tile_rows, block_rows)
-            latent = latent_ref[block * block_rows : (block + 1) * block_rows]
-            part = jnp.dot(weights, latent, preferred_element_type=F32)
+            rows = pl.ds(pl.multiple_of(block * block_rows, block_rows), block_rows)
+            part = jnp.dot(weights, latent_ref[rows], preferred_element_type=F32)
             for k in range(list_len):
                 entry = block * list_len + k
                 across, group, tile, slot = spot(me, block, k)
@@ -156,19 +166,11 @@
                 rest_ref[jnp.where(there < 0, rest_spare, jnp.minimum(there, rest_spare))] = masked
                 beyond = there - rest_spare
                 far_ref[jnp.where(beyond < 0, far_spare, beyond)] = masked
-
-    w1_in.wait()
-    first_layer(0)
-    w2_in.wait()
+        return carry
+
+    lax.fori_loop(0, parts, one_chunk, 0)
     for i in range(parts):
-        if i + 1 < parts:
-            first_layer(i + 1)
-        second_layer(i)
-        if i:
-            listed_sums(i - 1)
-    listed_sums(parts - 1)
-    for started in latent_out:
-        started.wait()
+        latent_out(i).wait()
 
 
 def add_entries(total, table_ref, group, slots, kept, other, groups, first=0):
@@ -235,42 +237,54 @@
     pieces, (out_any, held, latent_ref, total, out_ref, sems) = rest[:count], rest[count:]
     blk_count, block_rows, listed = weights_ref.shape
     tile_rows = listed // list_len
-    copies = []
-
-    def copy(source, target):
-        copies.append(pltpu.make_async_copy(source, target, sems.at[len(copies)]))
-        return copies[-1]
+    part_rows = total.shape[0]
+    part_blocks = part_rows // block_rows
+    parts = blk_count // part_blocks
+
+    def rows_of(i):
+        return pl.ds(pl.multiple_of(i * part_rows, part_rows), part_rows)
+
+    def latent_in(i):
+        rows = rows_of(i)
+        return pltpu.make_async_copy(latent_any.at[rows], latent_ref.at[rows], sems.at[i])
+
+    def out(i):
+        rows = rows_of(i)
+        return pltpu.make_async_copy(out_ref.at[rows], out_any.at[rows], sems.at[parts + i])
 
     pieces_in = []
-    for piece, start in zip(pieces, starts):
-        pieces_in.append(copy(piece, held.at[pl.ds(start, piece.shape[0])]))
-    part_rows = PART * block_rows
-    parts = [pl.ds(i * part_rows, part_rows) for i in range(blk_count // PART)]
-    latent_in = [copy(latent_any.at[rows], latent_ref.at[rows]) for rows in parts]
-    outs = [copy(out_ref.at[rows], out_any.at[rows]) for rows in parts]
-    for started in pieces_in + latent_in:
-        started.start()
-    for started in pieces_in:
-        started.wait()
-
-    for block in range(blk_count):
-        values = []
-        for k in range(list_len):
-            entry = block * list_len + k
-            rows = pl.ds(pl.multiple_of(table_ref[2, entry] * tile_rows, tile_rows), tile_rows)
-            value = held[rows]
-            values.append(jnp.where(table_ref[3, entry] == 1, value, jnp.zeros_like(value)))
-        value = jnp.concatenate(values, axis=0)
-        rows = slice(block * block_rows, (block + 1) * block_rows)
-        total[rows] = jnp.dot(weights_ref[block], value, preferred_element_type=F32)
-        if block % PART == 0:
-            latent_in[block // PART].wait()
-        for strip in strips(rows):
-            out_ref[strip] = (latent_ref[strip].astype(F32) + total[strip]).astype(BF16)
-        if block % PART == PART - 1:
-            outs[block // PART].start()
-    for started in outs:
-        started.wait()
+    for i, (piece, start) in enumerate(zip(pieces, starts)):
+        into = held.at[pl.ds(start, piece.shape[0])]
+        pieces_in.append(pltpu.make_async_copy(piece, into, sems.at[2 * parts + i]))
+    for copy in pieces_in:
+        copy.start()
+    for i in range(parts):
+        latent_in(i).start()
+    for copy in pieces_in:
+        copy.wait()
+
+    def one_chunk(i, carry):
+        latent_in(i).wait()
+        for b in range(part_blocks):
+            block = i * part_blocks + b
+            values = []
+            for k in range(list_len):
+                entry = block * list_len + k
+                rows = pl.ds(pl.multiple_of(table_ref[2, entry] * tile_rows, tile_rows), tile_rows)
+                value = held[rows]
+                values.append(jnp.where(table_ref[3, entry] == 1, value, jnp.zeros_like(value)))
+            value = jnp.concatenate(values, axis=0)
+            span = slice(b * block_rows, (b + 1) * block_rows)
+            total[span] = jnp.dot(weights_ref[block], value, preferred_element_type=F32)
+            for strip in strips(span):
+                rows = pl.ds(pl.multiple_of(i * part_rows + strip.start, STRIP), STRIP)
+                out_ref[rows] = (latent_ref[rows].astype(F32) + total[strip]).astype(BF16)
+        out(i).start()
+        return carry
+
+    lax.fori_loop(0, parts, one_chunk, 0)
+    for i in range(parts):
+        out(i).wait()
 
 
 def whole(array):
@@ -342,8 +356,9 @@
                 pltpu.VMEM(embed_in.shape, BF16),
                 pltpu.VMEM(embed_out.shape, BF16),
                 pltpu.VMEM(interp.shape, BF16),
-                pltpu.VMEM((grid_rows, width), F32),
-                pltpu.VMEM((grid_rows, width), BF16),
+                pltpu.VMEM((part_rows, width), F32),
+                pltpu.VMEM((part_rows, width), BF16),
+                pltpu.VMEM((part_rows, width), F32),
                 pltpu.VMEM((grid_rows, width), BF16),
                 pltpu.SemaphoreType.DMA((2 + 3 * parts,)),
             ],
@@ -496,9 +511,9 @@
             scratch_shapes=[
                 pltpu.VMEM((N_CORE * ((chips - 1) * slots + tiles) * tile_rows, width), BF16),
                 pltpu.VMEM((grid_rows, width), BF16),
-                pltpu.VMEM((grid_rows, width), F32),
+                pltpu.VMEM((BACK_PART * block_rows, width), F32),
                 pltpu.VMEM((grid_rows, width), BF16),
-                pltpu.SemaphoreType.DMA((len(pieces) + 2 * parts,)),
+                pltpu.SemaphoreType.DMA((len(pieces) + 2 * (blk_count // BACK_PART),)),
             ],
         ),
         compiler_params=params(32),

time: 80.5 us -> 80.6 us (level)
  no operation moved by 1% of the time
where the time goes in v11:
time: 80.6 us; the launch traced here: 80.3 us
  waiting for transfers between devices  28.7 us (36%)
  Pallas kernels  25.5 us (32%)
  starting transfers between devices  25.3 us (31%)
  between operations  0.82 us (1%)
    ppermute x14, waiting for transfers between devices, over(): return lax.ppermute(value, 'band', pairs)  26 us
    ppermute x14, starting transfers between devices, over(): return lax.ppermute(value, 'band', pairs)  23.8 us
    pallas_call x1, Pallas kernels, on_device(): pl.pallas_call(functools.partial(embed_kernel, ring, slots), out_shape=[p...  14 us
    pallas_call x1, Pallas kernels, on_device(): pl.pallas_call(functools.partial(back_kernel, starts, list_len), out_shap...  5.38 us
    ppermute x6, waiting for transfers between devices, over_core(): return lax.ppermute(value, 'band', [(i, i ^ 1) for i in range(self.n_band)])  2.73 us
    pallas_call x3, Pallas kernels, pick(): pl.pallas_call(functools.partial(pick_kernel, chosen, slots, chips, tile_...  1.83 us
  transfers between devices with their start and end apart: 20, of which 15 were waited for; matrix products, arithmetic and copies ran while one was open for 0% of the time, Pallas kernels for 5%

profile of v11, /device:TPU:0, one launch (start us, length us, event | category | flops | bytes accessed | tf_op | source)
XLA Modules:
  0.0 80.3 jit_solution(16212522967652536489)
XLA Ops:
  0.6 14.0 %embed.1 = (bf16[4096,512]{1,0:T(8,128)(2,1)}, bf16[33,32,512]{2,1,0:T(8,128)(2,1)S(1)}, bf16[9,32,512]{2,1,0:T(8,128)(2,1)S(1)}, bf16[25,32,512]{2,1,0:T(8,128)(2,1)S(1)}, s32[4,64]{1,0:T(4,128)S(1)}) custom-call(s32[1]{0:T(128)} %bitcast.me_ref, s32[4,256]{1,0:T(4,128)} %bitcast.8, s32[4,256]{1,0:T(4,128)} %bitcast.9, bf16[227,4096]{1,0:T(8,128)(2,1)} %bitcast.7, ...), custom_call_target="tpu_custom_call" | custom-call | flops 3636461568 | bytes 2908160 | tf_op jit(solution)/shard_map/embed/pallas_call | solution.py:342
  15.1 1.2 %collective-permute-done.other = bf16[9,32,512]{2,1,0:T(8,128)(2,1)S(1)} collective-permute-done((bf16[9,32,512]{2,1,0:T(8,128)(2,1)S(1)}, bf16[9,32,512]{2,1,0:T(8,128)(2,1)S(1)}, u32[]{:S(2)}, u32[]{:S(2)}) %collective-permute-start) | collective-permute-done | bytes 294944 | tf_op jit(solution)/shard_map/ppermute | solution.py:53
  16.3 0.8 far_sums.1
  17.6 2.7 %collective-permute-start.2 = (bf16[8,32,512]{2,1,0:T(8,128)(2,1)S(1)}, bf16[8,32,512]{2,1,0:T(8,128)(2,1)S(1)}, u32[]{:S(2)}, u32[]{:S(2)}) collective-permute-start(bf16[8,32,512]{2,1,0:T(8,128)(2,1)S(1)} %get-tuple-element.21.refs_1_), channel_id=1, source_target_pairs={{0,4},{1,3},{2,0},{3,7},{4,8},{5,1},{6,2},{7,11},{8,12},{9,5},{10,... | collective-permute-start | bytes 786440 | tf_op jit(solution)/shard_map/ppermute | solution.py:62
  20.3 1.6 %collective-permute-start.4 = (bf16[8,32,512]{2,1,0:T(8,128)(2,1)S(1)}, bf16[8,32,512]{2,1,0:T(8,128)(2,1)S(1)}, u32[]{:S(2)}, u32[]{:S(2)}) collective-permute-start(bf16[8,32,512]{2,1,0:T(8,128)(2,1)S(1)} %get-tuple-element.23), channel_id=1, source_target_pairs={{0,4},{1,3},{2,0},{3,7},{4,8},{5,1},{6,2},{7,11},{8,12},{9,5},{10,... | collective-permute-start | bytes 786440 | tf_op jit(solution)/shard_map/ppermute | solution.py:62
  21.9 1.2 %own_sums.1.token.own = f32[6,8,32,512]{3,2,1,0:T(8,128)S(1)} custom-call(s32[4,64]{1,0:T(4,128)S(1)} %get-tuple-element.17.table_ref, bf16[33,32,512]{2,1,0:T(8,128)(2,1)S(1)} %get-tuple-element.18.kept, bf16[25,32,512]{2,1,0:T(8,128)(2,1)S(1)} %collective-permute-done.1.other), custom_call_target="tpu_custom_call" | custom-call | bytes 4325376 | tf_op jit(solution)/shard_map/own_sums/pallas_call | solution.py:405
  23.6 1.0 %collective-permute-done.2.came = bf16[8,32,512]{2,1,0:T(8,128)(2,1)S(1)} collective-permute-done((bf16[8,32,512]{2,1,0:T(8,128)(2,1)S(1)}, bf16[8,32,512]{2,1,0:T(8,128)(2,1)S(1)}, u32[]{:S(2)}, u32[]{:S(2)}) %collective-permute-start.2) | collective-permute-done | bytes 262176 | tf_op jit(solution)/shard_map/ppermute | solution.py:62
  24.7 2.1 %collective-permute-start.3 = (bf16[8,32,512]{2,1,0:T(8,128)(2,1)S(1)}, bf16[8,32,512]{2,1,0:T(8,128)(2,1)S(1)}, u32[]{:S(2)}, u32[]{:S(2)}) collective-permute-start(bf16[8,32,512]{2,1,0:T(8,128)(2,1)S(1)} %add_5.1.token), channel_id=1, source_target_pairs={{0,4},{1,3},{2,0},{3,7},{4,8},{5,1},{6,2},{7,11},{8,12},{9,5},{10,... | collective-permute-start | bytes 786440 | tf_op jit(solution)/shard_map/ppermute | solution.py:62
  26.8 0.6 collective-permute-done.4.came
  27.5 2.1 %collective-permute-start.6 = (bf16[8,32,512]{2,1,0:T(8,128)(2,1)S(1)}, bf16[8,32,512]{2,1,0:T(8,128)(2,1)S(1)}, u32[]{:S(2)}, u32[]{:S(2)}) collective-permute-start(bf16[8,32,512]{2,1,0:T(8,128)(2,1)S(1)} %add_4.1.token), channel_id=1, source_target_pairs={{0,4},{1,3},{2,0},{3,7},{4,8},{5,1},{6,2},{7,11},{8,12},{9,5},{10,... | collective-permute-start | bytes 786440 | tf_op jit(solution)/shard_map/ppermute | solution.py:62
  29.6 1.5 %collective-permute-done.3.came = bf16[8,32,512]{2,1,0:T(8,128)(2,1)S(1)} collective-permute-done((bf16[8,32,512]{2,1,0:T(8,128)(2,1)S(1)}, bf16[8,32,512]{2,1,0:T(8,128)(2,1)S(1)}, u32[]{:S(2)}, u32[]{:S(2)}) %collective-permute-start.3) | collective-permute-done | bytes 262176 | tf_op jit(solution)/shard_map/ppermute | solution.py:62
  31.2 2.1 %collective-permute-start.5 = (bf16[8,32,512]{2,1,0:T(8,128)(2,1)S(1)}, bf16[8,32,512]{2,1,0:T(8,128)(2,1)S(1)}, u32[]{:S(2)}, u32[]{:S(2)}) collective-permute-start(bf16[8,32,512]{2,1,0:T(8,128)(2,1)S(1)} %add_3.1.token), channel_id=1, source_target_pairs={{0,4},{1,3},{2,0},{3,7},{4,8},{5,1},{6,2},{7,11},{8,12},{9,5},{10,... | collective-permute-start | bytes 786440 | tf_op jit(solution)/shard_map/ppermute | solution.py:62
  34.4 3.2 %collective-permute-done.5.came = bf16[8,32,512]{2,1,0:T(8,128)(2,1)S(1)} collective-permute-done((bf16[8,32,512]{2,1,0:T(8,128)(2,1)S(1)}, bf16[8,32,512]{2,1,0:T(8,128)(2,1)S(1)}, u32[]{:S(2)}, u32[]{:S(2)}) %collective-permute-start.5) | collective-permute-done | bytes 262176 | tf_op jit(solution)/shard_map/ppermute | solution.py:62
  37.7 2.1 %collective-permute-start.7 = (bf16[8,32,512]{2,1,0:T(8,128)(2,1)S(1)}, bf16[8,32,512]{2,1,0:T(8,128)(2,1)S(1)}, u32[]{:S(2)}, u32[]{:S(2)}) collective-permute-start(bf16[8,32,512]{2,1,0:T(8,128)(2,1)S(1)} %add_1.1), channel_id=1, source_target_pairs={{0,4},{1,3},{2,0},{3,7},{4,8},{5,1},{6,2},{7,11},{8,12},{9,5},{10,... | collective-permute-start | bytes 786440 | tf_op jit(solution)/shard_map/ppermute | solution.py:62
  40.0 4.1 %collective-permute-done.7.came = bf16[8,32,512]{2,1,0:T(8,128)(2,1)S(1)} collective-permute-done((bf16[8,32,512]{2,1,0:T(8,128)(2,1)S(1)}, bf16[8,32,512]{2,1,0:T(8,128)(2,1)S(1)}, u32[]{:S(2)}, u32[]{:S(2)}) %collective-permute-start.7) | collective-permute-done | bytes 262176 | tf_op jit(solution)/shard_map/ppermute | solution.py:62
  44.1 1.5 %mesh_step.1 = (bf16[256,512]{1,0:T(8,128)(2,1)}, bf16[256,512]{1,0:T(8,128)(2,1)S(1)}) custom-call(bf16[256,512]{1,0:T(8,128)(2,1)S(1)} %copy-done.3, bf16[512,512]{1,0:T(8,128)(2,1)S(1)} %copy-done.1, bf16[512,512]{1,0:T(8,128)(2,1)S(1)} %copy-done.2, f32[1,512]{1,0:T(1,128)S(1)} %bitcast.6, f32[6,8,32,512]{3,2,1,0:T(8,128)S(1)} %own_sums.1.token.own, ...), custom_call_target="tpu_custom_call" | custom-call | flops 268435456 | bytes 1048576 | tf_op jit(solution)/shard_map/mesh_step/pallas_call | solution.py:452
  45.6 2.0 %collective-permute-start.9 = (bf16[256,512]{1,0:T(8,128)(2,1)S(1)}, bf16[256,512]{1,0:T(8,128)(2,1)S(1)}, u32[]{:S(2)}, u32[]{:S(2)}) collective-permute-start(bf16[256,512]{1,0:T(8,128)(2,1)S(1)} %get-tuple-element.24.refs_1_.refs_0_), channel_id=1, source_target_pairs={{0,2},{1,5},{2,6},{3,1},{4,0},{5,9},{6,10},{7,3},{8,4},{9,13},{10,... | collective-permute-start | bytes 786440 | tf_op jit(solution)/shard_map/ppermute | solution.py:62
  47.6 5.8 %collective-permute-done.9.refs_0_ = bf16[256,512]{1,0:T(8,128)(2,1)S(1)} collective-permute-done((bf16[256,512]{1,0:T(8,128)(2,1)S(1)}, bf16[256,512]{1,0:T(8,128)(2,1)S(1)}, u32[]{:S(2)}, u32[]{:S(2)}) %collective-permute-start.9) | collective-permute-done | bytes 262176 | tf_op jit(solution)/shard_map/ppermute | solution.py:62
  53.4 2.5 %collective-permute-start.12 = (bf16[256,512]{1,0:T(8,128)(2,1)S(1)}, bf16[256,512]{1,0:T(8,128)(2,1)S(1)}, u32[]{:S(2)}, u32[]{:S(2)}) collective-permute-start(bf16[256,512]{1,0:T(8,128)(2,1)S(1)} %in_order.8.refs_1_), channel_id=1, source_target_pairs={{0,2},{1,5},{2,6},{3,1},{4,0},{5,9},{6,10},{7,3},{8,4},{9,13},{10,... | collective-permute-start | bytes 786440 | tf_op jit(solution)/shard_map/ppermute | solution.py:62
  55.9 1.5 %collective-permute-start.13 = (bf16[256,512]{1,0:T(8,128)(2,1)S(1)}, bf16[256,512]{1,0:T(8,128)(2,1)S(1)}, u32[]{:S(2)}, u32[]{:S(2)}) collective-permute-start(bf16[256,512]{1,0:T(8,128)(2,1)S(1)} %in_order.9.refs_2_), channel_id=1, source_target_pairs={{0,2},{1,5},{2,6},{3,1},{4,0},{5,9},{6,10},{7,3},{8,4},{9,13},{10,... | collective-permute-start | bytes 786440 | tf_op jit(solution)/shard_map/ppermute | solution.py:62
  57.3 0.6 pick_0.1
  58.0 2.7 %collective-permute-done.12.refs_0_ = bf16[256,512]{1,0:T(8,128)(2,1)S(1)} collective-permute-done((bf16[256,512]{1,0:T(8,128)(2,1)S(1)}, bf16[256,512]{1,0:T(8,128)(2,1)S(1)}, u32[]{:S(2)}, u32[]{:S(2)}) %collective-permute-start.12) | collective-permute-done | bytes 262176 | tf_op jit(solution)/shard_map/ppermute | solution.py:62
  60.7 1.5 %collective-permute-start.15 = (bf16[256,512]{1,0:T(8,128)(2,1)S(1)}, bf16[256,512]{1,0:T(8,128)(2,1)S(1)}, u32[]{:S(2)}, u32[]{:S(2)}) collective-permute-start(bf16[256,512]{1,0:T(8,128)(2,1)S(1)} %in_order.10.refs_1_.refs_0_), channel_id=1, source_target_pairs={{0,2},{1,5},{2,6},{3,1},{4,0},{5,9},{6,10},{7,3},{8,4},{9,13},{10,... | collective-permute-start | bytes 786440 | tf_op jit(solution)/shard_map/ppermute | solution.py:62
  62.2 1.3 %collective-permute-done.13.refs_0_ = bf16[256,512]{1,0:T(8,128)(2,1)S(1)} collective-permute-done((bf16[256,512]{1,0:T(8,128)(2,1)S(1)}, bf16[256,512]{1,0:T(8,128)(2,1)S(1)}, u32[]{:S(2)}, u32[]{:S(2)}) %collective-permute-start.13) | collective-permute-done | bytes 262176 | tf_op jit(solution)/shard_map/ppermute | solution.py:62
  63.5 1.5 %collective-permute-start.16 = (bf16[256,512]{1,0:T(8,128)(2,1)S(1)}, bf16[256,512]{1,0:T(8,128)(2,1)S(1)}, u32[]{:S(2)}, u32[]{:S(2)}) collective-permute-start(bf16[256,512]{1,0:T(8,128)(2,1)S(1)} %in_order.11.refs_1_), channel_id=1, source_target_pairs={{0,2},{1,5},{2,6},{3,1},{4,0},{5,9},{6,10},{7,3},{8,4},{9,13},{10,... | collective-permute-start | bytes 786440 | tf_op jit(solution)/shard_map/ppermute | solution.py:62
  65.6 1.4 %collective-permute-done.15.refs_0_ = bf16[256,512]{1,0:T(8,128)(2,1)S(1)} collective-permute-done((bf16[256,512]{1,0:T(8,128)(2,1)S(1)}, bf16[256,512]{1,0:T(8,128)(2,1)S(1)}, u32[]{:S(2)}, u32[]{:S(2)}) %collective-permute-start.15) | collective-permute-done | bytes 262176 | tf_op jit(solution)/shard_map/ppermute | solution.py:62
  67.0 1.5 %collective-permute-start.18 = (bf16[256,512]{1,0:T(8,128)(2,1)S(1)}, bf16[256,512]{1,0:T(8,128)(2,1)S(1)}, u32[]{:S(2)}, u32[]{:S(2)}) collective-permute-start(bf16[256,512]{1,0:T(8,128)(2,1)S(1)} %in_order.12.refs_1_.refs_0_), channel_id=1, source_target_pairs={{0,2},{1,5},{2,6},{3,1},{4,0},{5,9},{6,10},{7,3},{8,4},{9,13},{10,... | collective-permute-start | bytes 786440 | tf_op jit(solution)/shard_map/ppermute | solution.py:62
  69.1 0.7 collective-permute-done.16.refs_0_
  69.9 0.6 pick_5.1
  70.5 2.9 %collective-permute-done.18.rest_6_ = bf16[256,512]{1,0:T(8,128)(2,1)S(1)} collective-permute-done((bf16[256,512]{1,0:T(8,128)(2,1)S(1)}, bf16[256,512]{1,0:T(8,128)(2,1)S(1)}, u32[]{:S(2)}, u32[]{:S(2)}) %collective-permute-start.18) | collective-permute-done | bytes 262176 | tf_op jit(solution)/shard_map/ppermute | solution.py:62
  73.4 1.5 %collective-permute-done.19.rest_7_ = bf16[256,512]{1,0:T(8,128)(2,1)S(1)} collective-permute-done((bf16[256,512]{1,0:T(8,128)(2,1)S(1)}, bf16[256,512]{1,0:T(8,128)(2,1)S(1)}, u32[]{:S(2)}, u32[]{:S(2)}) %collective-permute-start.19) | collective-permute-done | bytes 262176 | tf_op jit(solution)/shard_map/ppermute | solution.py:53
  75.0 5.4 %back.1 = bf16[4096,512]{1,0:T(8,128)(2,1)} custom-call(s32[4,64]{1,0:T(4,128)S(1)} %get-tuple-element.17.table_ref, bf16[16,256,128]{2,1,0:T(8,128)(2,1)S(1)} %turn.1.token.weights_ref, bf16[4096,512]{1,0:T(8,128)(2,1)} %get-tuple-element.22.latent_any, bf16[384,512]{1,0:T(8,128)(2,1)S(1)} %get-tuple-element.25.refs_1_.rest_0_, ...), custom_call_target="tpu_custom_call" | custom-call | flops 536870912 | bytes 9437184 | tf_op jit(solution)/shard_map/back/pallas_call | solution.py:503
  (39 shorter events, 4.2 us)
Async XLA Ops:
  14.6 1.7 %collective-permute-start = (bf16[9,32,512]{2,1,0:T(8,128)(2,1)S(1)}, bf16[9,32,512]{2,1,0:T(8,128)(2,1)S(1)}, u32[]{:S(2)}, u32[]{:S(2)}) collective-permute-start(bf16[9,32,512]{2,1,0:T(8,128)(2,1)S(1)} %get-tuple-element.20), channel_id=1, source_target_pairs={{0,1},{1,0},{2,3},{3,2},{4,5},{5,4},{6,7},{7,6},{8,9},{9,8},{10,11... | collective-permute-start | bytes 884744 | tf_op jit(solution)/shard_map/ppermute | solution.py:53
  17.1 5.9 %copy-start = (bf16[16,4,32,256]{3,2,1,0:T(8,128)(2,1)S(1)}, bf16[16,4,32,256]{3,2,1,0:T(8,128)(2,1)}, u32[]{:S(2)}) copy-start(bf16[16,4,32,256]{3,2,1,0:T(8,128)(2,1)} %interp_ref.1) | copy-start | bytes 3145732
  17.2 4.7 %collective-permute-start.1 = (bf16[25,32,512]{2,1,0:T(8,128)(2,1)S(1)}, bf16[25,32,512]{2,1,0:T(8,128)(2,1)S(1)}, u32[]{:S(2)}, u32[]{:S(2)}) collective-permute-start(bf16[25,32,512]{2,1,0:T(8,128)(2,1)S(1)} %in_order.7), channel_id=1, source_target_pairs={{0,1},{1,0},{2,3},{3,2},{4,5},{5,4},{6,7},{7,6},{8,9},{9,8},{10,11... | collective-permute-start | bytes 2457608 | tf_op jit(solution)/shard_map/ppermute | solution.py:53
  17.6 7.0 %collective-permute-start.2 = (bf16[8,32,512]{2,1,0:T(8,128)(2,1)S(1)}, bf16[8,32,512]{2,1,0:T(8,128)(2,1)S(1)}, u32[]{:S(2)}, u32[]{:S(2)}) collective-permute-start(bf16[8,32,512]{2,1,0:T(8,128)(2,1)S(1)} %get-tuple-element.21.refs_1_), channel_id=1, source_target_pairs={{0,4},{1,3},{2,0},{3,7},{4,8},{5,1},{6,2},{7,11},{8,12},{9,5},{10,... | collective-permute-start | bytes 786440 | tf_op jit(solution)/shard_map/ppermute | solution.py:62
  20.3 7.1 %collective-permute-start.4 = (bf16[8,32,512]{2,1,0:T(8,128)(2,1)S(1)}, bf16[8,32,512]{2,1,0:T(8,128)(2,1)S(1)}, u32[]{:S(2)}, u32[]{:S(2)}) collective-permute-start(bf16[8,32,512]{2,1,0:T(8,128)(2,1)S(1)} %get-tuple-element.23), channel_id=1, source_target_pairs={{0,4},{1,3},{2,0},{3,7},{4,8},{5,1},{6,2},{7,11},{8,12},{9,5},{10,... | collective-permute-start | bytes 786440 | tf_op jit(solution)/shard_map/ppermute | solution.py:62
  24.7 6.4 %collective-permute-start.3 = (bf16[8,32,512]{2,1,0:T(8,128)(2,1)S(1)}, bf16[8,32,512]{2,1,0:T(8,128)(2,1)S(1)}, u32[]{:S(2)}, u32[]{:S(2)}) collective-permute-start(bf16[8,32,512]{2,1,0:T(8,128)(2,1)S(1)} %add_5.1.token), channel_id=1, source_target_pairs={{0,4},{1,3},{2,0},{3,7},{4,8},{5,1},{6,2},{7,11},{8,12},{9,5},{10,... | collective-permute-start | bytes 786440 | tf_op jit(solution)/shard_map/ppermute | solution.py:62
  27.5 6.4 %collective-permute-start.6 = (bf16[8,32,512]{2,1,0:T(8,128)(2,1)S(1)}, bf16[8,32,512]{2,1,0:T(8,128)(2,1)S(1)}, u32[]{:S(2)}, u32[]{:S(2)}) collective-permute-start(bf16[8,32,512]{2,1,0:T(8,128)(2,1)S(1)} %add_4.1.token), channel_id=1, source_target_pairs={{0,4},{1,3},{2,0},{3,7},{4,8},{5,1},{6,2},{7,11},{8,12},{9,5},{10,... | collective-permute-start | bytes 786440 | tf_op jit(solution)/shard_map/ppermute | solution.py:62
  31.2 13.0 %copy-start.1 = (bf16[512,512]{1,0:T(8,128)(2,1)S(1)}, bf16[512,512]{1,0:T(8,128)(2,1)}, u32[]{:S(2)}) copy-start(bf16[512,512]{1,0:T(8,128)(2,1)} %up_ref.1) | copy-start | bytes 1572868
  31.2 13.0 %copy-start.2 = (bf16[512,512]{1,0:T(8,128)(2,1)S(1)}, bf16[512,512]{1,0:T(8,128)(2,1)}, u32[]{:S(2)}) copy-start(bf16[512,512]{1,0:T(8,128)(2,1)} %down_ref.1) | copy-start | bytes 1572868
  31.2 12.9 %copy-start.3 = (bf16[256,512]{1,0:T(8,128)(2,1)S(1)}, bf16[256,512]{1,0:T(8,128)(2,1)}, u32[]{:S(2)}) copy-start(bf16[256,512]{1,0:T(8,128)(2,1)} %latent_ref.1) | copy-start | bytes 786436
  31.2 12.9 %copy-start.4 = (f32[512]{0:T(512)S(1)}, f32[512]{0:T(512)}, u32[]{:S(2)}) copy-start(f32[512]{0:T(512)} %param.21) | copy-start | bytes 6148
  31.2 6.4 %collective-permute-start.5 = (bf16[8,32,512]{2,1,0:T(8,128)(2,1)S(1)}, bf16[8,32,512]{2,1,0:T(8,128)(2,1)S(1)}, u32[]{:S(2)}, u32[]{:S(2)}) collective-permute-start(bf16[8,32,512]{2,1,0:T(8,128)(2,1)S(1)} %add_3.1.token), channel_id=1, source_target_pairs={{0,4},{1,3},{2,0},{3,7},{4,8},{5,1},{6,2},{7,11},{8,12},{9,5},{10,... | collective-permute-start | bytes 786440 | tf_op jit(solution)/shard_map/ppermute | solution.py:62
  34.0 6.1 %collective-permute-start.8 = (bf16[8,32,512]{2,1,0:T(8,128)(2,1)S(1)}, bf16[8,32,512]{2,1,0:T(8,128)(2,1)S(1)}, u32[]{:S(2)}, u32[]{:S(2)}) collective-permute-start(bf16[8,32,512]{2,1,0:T(8,128)(2,1)S(1)} %add_2.1.token), channel_id=1, source_target_pairs={{0,5},{1,2},{2,1},{3,6},{4,9},{5,0},{6,3},{7,10},{8,13},{9,4},{10,... | collective-permute-start | bytes 786440 | tf_op jit(solution)/shard_map/ppermute | solution.py:62
  37.7 6.4 %collective-permute-start.7 = (bf16[8,32,512]{2,1,0:T(8,128)(2,1)S(1)}, bf16[8,32,512]{2,1,0:T(8,128)(2,1)S(1)}, u32[]{:S(2)}, u32[]{:S(2)}) collective-permute-start(bf16[8,32,512]{2,1,0:T(8,128)(2,1)S(1)} %add_1.1), channel_id=1, source_target_pairs={{0,4},{1,3},{2,0},{3,7},{4,8},{5,1},{6,2},{7,11},{8,12},{9,5},{10,... | collective-permute-start | bytes 786440 | tf_op jit(solution)/shard_map/ppermute | solution.py:62
  45.6 7.8 %collective-permute-start.9 = (bf16[256,512]{1,0:T(8,128)(2,1)S(1)}, bf16[256,512]{1,0:T(8,128)(2,1)S(1)}, u32[]{:S(2)}, u32[]{:S(2)}) collective-permute-start(bf16[256,512]{1,0:T(8,128)(2,1)S(1)} %get-tuple-element.24.refs_1_.refs_0_), channel_id=1, source_target_pairs={{0,2},{1,5},{2,6},{3,1},{4,0},{5,9},{6,10},{7,3},{8,4},{9,13},{10,... | collective-permute-start | bytes 786440 | tf_op jit(solution)/shard_map/ppermute | solution.py:62
  47.6 8.2 %collective-permute-start.10 = (bf16[256,512]{1,0:T(8,128)(2,1)S(1)}, bf16[256,512]{1,0:T(8,128)(2,1)S(1)}, u32[]{:S(2)}, u32[]{:S(2)}) collective-permute-start(bf16[256,512]{1,0:T(8,128)(2,1)S(1)} %get-tuple-element.24.refs_1_.refs_0_), channel_id=1, source_target_pairs={{0,5},{1,2},{2,1},{3,6},{4,9},{5,0},{6,3},{7,10},{8,13},{9,4},{10,... | collective-permute-start | bytes 786440 | tf_op jit(solution)/shard_map/ppermute | solution.py:62
  53.4 7.3 %collective-permute-start.12 = (bf16[256,512]{1,0:T(8,128)(2,1)S(1)}, bf16[256,512]{1,0:T(8,128)(2,1)S(1)}, u32[]{:S(2)}, u32[]{:S(2)}) collective-permute-start(bf16[256,512]{1,0:T(8,128)(2,1)S(1)} %in_order.8.refs_1_), channel_id=1, source_target_pairs={{0,2},{1,5},{2,6},{3,1},{4,0},{5,9},{6,10},{7,3},{8,4},{9,13},{10,... | collective-permute-start | bytes 786440 | tf_op jit(solution)/shard_map/ppermute | solution.py:62
  55.9 7.6 %collective-permute-start.13 = (bf16[256,512]{1,0:T(8,128)(2,1)S(1)}, bf16[256,512]{1,0:T(8,128)(2,1)S(1)}, u32[]{:S(2)}, u32[]{:S(2)}) collective-permute-start(bf16[256,512]{1,0:T(8,128)(2,1)S(1)} %in_order.9.refs_2_), channel_id=1, source_target_pairs={{0,2},{1,5},{2,6},{3,1},{4,0},{5,9},{6,10},{7,3},{8,4},{9,13},{10,... | collective-permute-start | bytes 786440 | tf_op jit(solution)/shard_map/ppermute | solution.py:62
  60.7 6.4 %collective-permute-start.15 = (bf16[256,512]{1,0:T(8,128)(2,1)S(1)}, bf16[256,512]{1,0:T(8,128)(2,1)S(1)}, u32[]{:S(2)}, u32[]{:S(2)}) collective-permute-start(bf16[256,512]{1,0:T(8,128)(2,1)S(1)} %in_order.10.refs_1_.refs_0_), channel_id=1, source_target_pairs={{0,2},{1,5},{2,6},{3,1},{4,0},{5,9},{6,10},{7,3},{8,4},{9,13},{10,... | collective-permute-start | bytes 786440 | tf_op jit(solution)/shard_map/ppermute | solution.py:62
  63.5 6.4 %collective-permute-start.16 = (bf16[256,512]{1,0:T(8,128)(2,1)S(1)}, bf16[256,512]{1,0:T(8,128)(2,1)S(1)}, u32[]{:S(2)}, u32[]{:S(2)}) collective-permute-start(bf16[256,512]{1,0:T(8,128)(2,1)S(1)} %in_order.11.refs_1_), channel_id=1, source_target_pairs={{0,2},{1,5},{2,6},{3,1},{4,0},{5,9},{6,10},{7,3},{8,4},{9,13},{10,... | collective-permute-start | bytes 786440 | tf_op jit(solution)/shard_map/ppermute | solution.py:62
  67.0 6.4 %collective-permute-start.18 = (bf16[256,512]{1,0:T(8,128)(2,1)S(1)}, bf16[256,512]{1,0:T(8,128)(2,1)S(1)}, u32[]{:S(2)}, u32[]{:S(2)}) collective-permute-start(bf16[256,512]{1,0:T(8,128)(2,1)S(1)} %in_order.12.refs_1_.refs_0_), channel_id=1, source_target_pairs={{0,2},{1,5},{2,6},{3,1},{4,0},{5,9},{6,10},{7,3},{8,4},{9,13},{10,... | collective-permute-start | bytes 786440 | tf_op jit(solution)/shard_map/ppermute | solution.py:62
  68.6 4.8 %collective-permute-start.11 = (bf16[384,512]{1,0:T(8,128)(2,1)S(1)}, bf16[384,512]{1,0:T(8,128)(2,1)S(1)}, u32[]{:S(2)}, u32[]{:S(2)}) collective-permute-start(bf16[384,512]{1,0:T(8,128)(2,1)S(1)} %get-tuple-element.26), channel_id=1, source_target_pairs={{0,1},{1,0},{2,3},{3,2},{4,5},{5,4},{6,7},{7,6},{8,9},{9,8},{10,11... | collective-permute-start | bytes 1179656 | tf_op jit(solution)/shard_map/ppermute | solution.py:53
  68.6 4.8 %collective-permute-start.14 = (bf16[256,512]{1,0:T(8,128)(2,1)S(1)}, bf16[256,512]{1,0:T(8,128)(2,1)S(1)}, u32[]{:S(2)}, u32[]{:S(2)}) collective-permute-start(bf16[256,512]{1,0:T(8,128)(2,1)S(1)} %get-tuple-element.28), channel_id=1, source_target_pairs={{0,1},{1,0},{2,3},{3,2},{4,5},{5,4},{6,7},{7,6},{8,9},{9,8},{10,11... | collective-permute-start | bytes 786440 | tf_op jit(solution)/shard_map/ppermute | solution.py:53
  70.5 3.0 %collective-permute-start.17 = (bf16[256,512]{1,0:T(8,128)(2,1)S(1)}, bf16[256,512]{1,0:T(8,128)(2,1)S(1)}, u32[]{:S(2)}, u32[]{:S(2)}) collective-permute-start(bf16[256,512]{1,0:T(8,128)(2,1)S(1)} %get-tuple-element.30), channel_id=1, source_target_pairs={{0,1},{1,0},{2,3},{3,2},{4,5},{5,4},{6,7},{7,6},{8,9},{9,8},{10,11... | collective-permute-start | bytes 786440 | tf_op jit(solution)/shard_map/ppermute | solution.py:53
  73.4 1.5 %collective-permute-start.19 = (bf16[256,512]{1,0:T(8,128)(2,1)S(1)}, bf16[256,512]{1,0:T(8,128)(2,1)S(1)}, u32[]{:S(2)}, u32[]{:S(2)}) collective-permute-start(bf16[256,512]{1,0:T(8,128)(2,1)S(1)} %collective-permute-done.18.rest_6_), channel_id=1, source_target_pairs={{0,1},{1,0},{2,3},{3,2},{4,5},{5,4},{6,7},{7,6},{8,9},{9,8},{10,11... | collective-permute-start | bytes 786440 | tf_op jit(solution)/shard_map/ppermute | solution.py:53

commit v12 on v10

--- a/solution.py
+++ b/solution.py
@@ -78,97 +78,65 @@
 
 
 def embed_kernel(
-    ring, slots, me_ref, lists_ref, mask_ref, x_any, w1_any, w2_any, gain_ref, interp_any,
-    latent_any, kept_ref, far_ref, rest_ref, table_ref,
-    x_ref, w1_ref, w2_ref, interp_ref, wide, hidden, latent_ref, sems,
+    ring, slots, me_ref, lists_ref, mask_ref, x_ref, w1_ref, w2_ref, gain_ref, interp_ref,
+    latent_any, kept_ref, far_ref, rest_ref, table_ref, wide, hidden, latent_ref, sems,
 ):
+    step, steps = pl.program_id(0), pl.num_programs(0)
     me = me_ref[0]
-    blk_count, list_len, tile_rows, block_rows = interp_ref.shape
+    part_blocks, list_len, tile_rows, block_rows = interp_ref.shape
+    blk_count = steps * part_blocks
     groups = ring.chips
-    parts = x_ref.shape[0]
-    part_rows = x_ref.shape[2]
-    part_blocks = part_rows // block_rows
-    spans = [slice(i * part_rows, (i + 1) * part_rows) for i in range(parts)]
-
-    copies = []
-
-    def copy(source, target):
-        copies.append(pltpu.make_async_copy(source, target, sems.at[len(copies)]))
-        return copies[-1]
-
-    w1_in, w2_in = copy(w1_any, w1_ref), copy(w2_any, w2_ref)
-    x_in = [copy(x_any.at[:, pl.ds(s.start, part_rows)], x_ref.at[i]) for i, s in enumerate(spans)]
-    interp_in = []
-    for i in range(parts):
-        blocks = pl.ds(i * part_blocks, part_blocks)
-        interp_in.append(copy(interp_any.at[blocks], interp_ref.at[blocks]))
-    latent_out = []
-    for s in spans:
-        rows = pl.ds(s.start, part_rows)
-        latent_out.append(copy(latent_ref.at[rows], latent_any.at[rows]))
-    for started in (w1_in, x_in[0], w2_in, interp_in[0]):
-        started.start()
-    for i in range(1, parts):
-        x_in[i].start()
-        interp_in[i].start()
+    part_rows = wide.shape[0]
+    chunk = slice(0, part_rows)
+
+    def latent_out(i):
+        rows = pl.ds(pl.multiple_of(i * part_rows, part_rows), part_rows)
+        return pltpu.make_async_copy(latent_ref.at[rows], latent_any.at[rows], sems.at[i])
 
     def spot(index, block, k):
         across, group, tile = ring.entry(lists_ref, index, index * blk_count + block, k)
-        return across, group, tile, (block * list_len + k) // ring.n_band
+        return across, group, tile, split(block * list_len + k, ring.n_band)[0]
+
+    wide[...] = lax.dot_general(
+        x_ref[...], w1_ref[...], (((0,), (0,)), ((), ())), preferred_element_type=F32
+    )
+    for strip in strips(chunk):
+        hidden[strip] = silu(wide[strip]).astype(BF16)
+    wide[...] = jnp.dot(hidden[...], w2_ref[...], preferred_element_type=F32)
+    for strip in strips(chunk):
+        rows = pl.ds(pl.multiple_of(step * part_rows + strip.start, STRIP), STRIP)
+        latent_ref[rows] = layer_norm(wide[strip], gain_ref[...]).astype(BF16)
+    latent_out(step).start()
 
     kept_spare, far_spare, rest_spare = (ref.shape[0] - 1 for ref in (kept_ref, far_ref, rest_ref))
-
-    def first_layer(i):
-        x_in[i].wait()
-        wide[spans[i]] = lax.dot_general(
-            x_ref[i], w1_ref[...], (((0,), (0,)), ((), ())), preferred_element_type=F32
-        )
-
-    def second_layer(i):
-        for strip in strips(spans[i]):
-            hidden[strip] = silu(wide[strip]).astype(BF16)
-        wide[spans[i]] = jnp.dot(hidden[spans[i]], w2_ref[...], preferred_element_type=F32)
-
-    def listed_sums(i):
-        for strip in strips(spans[i]):
-            latent_ref[strip] = layer_norm(wide[strip], gain_ref[...]).astype(BF16)
-        latent_out[i].start()
-        interp_in[i].wait()
-        for block in range(i * part_blocks, (i + 1) * part_blocks):
-            weights = interp_ref[block].reshape(list_len * tile_rows, block_rows)
-            latent = latent_ref[block * block_rows : (block + 1) * block_rows]
-            part = jnp.dot(weights, latent, preferred_element_type=F32)
-            for k in range(list_len):
-                entry = block * list_len + k
-                across, group, tile, slot = spot(me, block, k)
-                place = (across * groups + group) * slots + slot
-                mask = mask_ref[k, me * blk_count + block]
-                table_ref[0, place] = tile
-                found = group * slots + jnp.where(group == groups - 1, tile, slot)
-                table_ref[2, entry] = found + across * ((groups - 1) * slots + ring.tiles)
-                table_ref[3, entry] = mask
-                across, group, tile, slot = spot(me ^ 1, block, k)
-                table_ref[1, (across * groups + group) * slots + slot] = tile
-                masked = part[k * tile_rows : (k + 1) * tile_rows] * mask.astype(F32)
-                masked = masked.astype(BF16)
-                kept_ref[jnp.minimum(place, kept_spare)] = masked
-                there = place - kept_spare
-                rest_ref[jnp.where(there < 0, rest_spare, jnp.minimum(there, rest_spare))] = masked
-                beyond = there - rest_spare
-                far_ref[jnp.where(beyond < 0, far_spare, beyond)] = masked
-
-    w1_in.wait()
-    first_layer(0)
-    w2_in.wait()
-    for i in range(parts):
-        if i + 1 < parts:
-            first_layer(i + 1)
-        second_layer(i)
-        if i:
-            listed_sums(i - 1)
-    listed_sums(parts - 1)
-    for started in latent_out:
-        started.wait()
+    for b in range(part_blocks):
+        block = step * part_blocks + b
+        weights = interp_ref[b].reshape(list_len * tile_rows, block_rows)
+        rows = pl.ds(pl.multiple_of(block * block_rows, block_rows), block_rows)
+        part = jnp.dot(weights, latent_ref[rows], preferred_element_type=F32)
+        for k in range(list_len):
+            entry = block * list_len + k
+            across, group, tile, slot = spot(me, block, k)
+            place = (across * groups + group) * slots + slot
+            mask = mask_ref[k, me * blk_count + block]
+            table_ref[0, place] = tile
+            found = group * slots + jnp.where(group == groups - 1, tile, slot)
+            table_ref[2, entry] = found + across * ((groups - 1) * slots + ring.tiles)
+            table_ref[3, entry] = mask
+            across, group, tile, slot = spot(me ^ 1, block, k)
+            table_ref[1, (across * groups + group) * slots + slot] = tile
+            masked = part[k * tile_rows : (k + 1) * tile_rows] * mask.astype(F32)
+            masked = masked.astype(BF16)
+            kept_ref[jnp.minimum(place, kept_spare)] = masked
+            there = place - kept_spare
+            rest_ref[jnp.where(there < 0, rest_spare, jnp.minimum(there, rest_spare))] = masked
+            beyond = there - rest_spare
+            far_ref[jnp.where(beyond < 0, far_spare, beyond)] = masked
+
+    @pl.when(step == steps - 1)
+    def _():
+        for i in range(sems.shape[0]):
+            latent_out(i).wait()
 
 
 def add_entries(total, table_ref, group, slots, kept, other, groups, first=0):
@@ -332,20 +300,22 @@
         + [shape((4, entries), jnp.int32)],
         grid_spec=pltpu.PrefetchScalarGridSpec(
             num_scalar_prefetch=3,
-            grid=(1,),
-            in_specs=[in_any] * 3 + [whole(gain), in_any],
+            grid=(parts,),
+            in_specs=[
+                pl.BlockSpec((channels, part_rows), lambda i, *_: (0, i)),
+                whole(embed_in),
+                whole(embed_out),
+                whole(gain),
+                pl.BlockSpec((PART,) + interp.shape[1:], lambda i, *_: (i, 0, 0, 0)),
+            ],
             out_specs=[in_any]
             + [in_vmem] * len(counts)
             + [pl.BlockSpec(memory_space=pltpu.SMEM)],
             scratch_shapes=[
-                pltpu.VMEM((parts, channels, part_rows), BF16),
-                pltpu.VMEM(embed_in.shape, BF16),
-                pltpu.VMEM(embed_out.shape, BF16),
-                pltpu.VMEM(interp.shape, BF16),
-                pltpu.VMEM((grid_rows, width), F32),
+                pltpu.VMEM((part_rows, width), F32),
+                pltpu.VMEM((part_rows, width), BF16),
                 pltpu.VMEM((grid_rows, width), BF16),
-                pltpu.VMEM((grid_rows, width), BF16),
-                pltpu.SemaphoreType.DMA((2 + 3 * parts,)),
+                pltpu.SemaphoreType.DMA((parts,)),
             ],
         ),
         compiler_params=params(40),

time: 80.5 us -> 78.8 us (0.979)
  Pallas kernels: 25.4 us -> 23.7 us
    pallas_call x1, Pallas kernels: 14.3 us -> 12.6 us  [on_device(): pl.pallas_call(functools.partial(embed_kernel, ring, slots), out_shape=[p...]
where the time goes in v12:
time: 78.8 us; the launch traced here: 78.6 us
  waiting for transfers between devices  28.8 us (37%)
  starting transfers between devices  25.3 us (32%)
  Pallas kernels  23.7 us (30%)
  between operations  0.82 us (1%)
    ppermute x14, waiting for transfers between devices, over(): return lax.ppermute(value, 'band', pairs)  26.1 us
    ppermute x14, starting transfers between devices, over(): return lax.ppermute(value, 'band', pairs)  23.7 us
    pallas_call x1, Pallas kernels, on_device(): pl.pallas_call(functools.partial(embed_kernel, ring, slots), out_shape=[p...  12.6 us
    pallas_call x1, Pallas kernels, on_device(): pl.pallas_call(functools.partial(back_kernel, starts, list_len), out_shap...  5.03 us
    ppermute x6, waiting for transfers between devices, over_core(): return lax.ppermute(value, 'band', [(i, i ^ 1) for i in range(self.n_band)])  2.73 us
    pallas_call x3, Pallas kernels, pick(): pl.pallas_call(functools.partial(pick_kernel, chosen, slots, chips, tile_...  1.83 us
  transfers between devices with their start and end apart: 20, of which 15 were waited for; matrix products, arithmetic and copies ran while one was open for 0% of the time, Pallas kernels for 5%

profile of v12, /device:TPU:0, one launch (start us, length us, event | category | flops | bytes accessed | tf_op | source)
XLA Modules:
  0.0 78.6 jit_solution(558451112774883966)
XLA Ops:
  0.6 12.6 %embed.1 = (bf16[4096,512]{1,0:T(8,128)(2,1)}, bf16[33,32,512]{2,1,0:T(8,128)(2,1)S(1)}, bf16[9,32,512]{2,1,0:T(8,128)(2,1)S(1)}, bf16[25,32,512]{2,1,0:T(8,128)(2,1)S(1)}, s32[4,64]{1,0:T(4,128)S(1)}) custom-call(s32[1]{0:T(128)} %bitcast.me_ref, s32[4,256]{1,0:T(4,128)} %bitcast.8, s32[4,256]{1,0:T(4,128)} %bitcast.9, bf16[227,4096]{1,0:T(8,128)(2,1)} %bitcast.7, ...), custom_call_target="tpu_custom_call" | custom-call | flops 3636461568 | bytes 2908160 | tf_op jit(solution)/shard_map/embed/pallas_call | solution.py:296
  13.7 1.2 %collective-permute-done.other = bf16[9,32,512]{2,1,0:T(8,128)(2,1)S(1)} collective-permute-done((bf16[9,32,512]{2,1,0:T(8,128)(2,1)S(1)}, bf16[9,32,512]{2,1,0:T(8,128)(2,1)S(1)}, u32[]{:S(2)}, u32[]{:S(2)}) %collective-permute-start) | collective-permute-done | bytes 294944 | tf_op jit(solution)/shard_map/ppermute | solution.py:52
  14.9 0.8 %far_sums.1 = (bf16[8,32,512]{2,1,0:T(8,128)(2,1)S(1)}, bf16[8,32,512]{2,1,0:T(8,128)(2,1)S(1)}) custom-call(s32[4,64]{1,0:T(4,128)S(1)} %get-tuple-element.17.table_ref, bf16[33,32,512]{2,1,0:T(8,128)(2,1)S(1)} %get-tuple-element.18.kept, bf16[9,32,512]{2,1,0:T(8,128)(2,1)S(1)} %collective-permute-done.other), custom_call_target="tpu_custom_call" | custom-call | bytes 1081344 | tf_op jit(solution)/shard_map/far_sums/pallas_call | solution.py:345
  16.2 2.7 %collective-permute-start.2 = (bf16[8,32,512]{2,1,0:T(8,128)(2,1)S(1)}, bf16[8,32,512]{2,1,0:T(8,128)(2,1)S(1)}, u32[]{:S(2)}, u32[]{:S(2)}) collective-permute-start(bf16[8,32,512]{2,1,0:T(8,128)(2,1)S(1)} %get-tuple-element.21.refs_1_), channel_id=1, source_target_pairs={{0,4},{1,3},{2,0},{3,7},{4,8},{5,1},{6,2},{7,11},{8,12},{9,5},{10,... | collective-permute-start | bytes 786440 | tf_op jit(solution)/shard_map/ppermute | solution.py:61
  18.9 1.6 %collective-permute-start.4 = (bf16[8,32,512]{2,1,0:T(8,128)(2,1)S(1)}, bf16[8,32,512]{2,1,0:T(8,128)(2,1)S(1)}, u32[]{:S(2)}, u32[]{:S(2)}) collective-permute-start(bf16[8,32,512]{2,1,0:T(8,128)(2,1)S(1)} %get-tuple-element.23), channel_id=1, source_target_pairs={{0,4},{1,3},{2,0},{3,7},{4,8},{5,1},{6,2},{7,11},{8,12},{9,5},{10,... | collective-permute-start | bytes 786440 | tf_op jit(solution)/shard_map/ppermute | solution.py:61
  20.5 1.2 %own_sums.1.token.own = f32[6,8,32,512]{3,2,1,0:T(8,128)S(1)} custom-call(s32[4,64]{1,0:T(4,128)S(1)} %get-tuple-element.17.table_ref, bf16[33,32,512]{2,1,0:T(8,128)(2,1)S(1)} %get-tuple-element.18.kept, bf16[25,32,512]{2,1,0:T(8,128)(2,1)S(1)} %collective-permute-done.1.other), custom_call_target="tpu_custom_call" | custom-call | bytes 4325376 | tf_op jit(solution)/shard_map/own_sums/pallas_call | solution.py:360
  22.2 1.0 %collective-permute-done.2.came = bf16[8,32,512]{2,1,0:T(8,128)(2,1)S(1)} collective-permute-done((bf16[8,32,512]{2,1,0:T(8,128)(2,1)S(1)}, bf16[8,32,512]{2,1,0:T(8,128)(2,1)S(1)}, u32[]{:S(2)}, u32[]{:S(2)}) %collective-permute-start.2) | collective-permute-done | bytes 262176 | tf_op jit(solution)/shard_map/ppermute | solution.py:61
  23.2 2.1 %collective-permute-start.3 = (bf16[8,32,512]{2,1,0:T(8,128)(2,1)S(1)}, bf16[8,32,512]{2,1,0:T(8,128)(2,1)S(1)}, u32[]{:S(2)}, u32[]{:S(2)}) collective-permute-start(bf16[8,32,512]{2,1,0:T(8,128)(2,1)S(1)} %add_5.1.token), channel_id=1, source_target_pairs={{0,4},{1,3},{2,0},{3,7},{4,8},{5,1},{6,2},{7,11},{8,12},{9,5},{10,... | collective-permute-start | bytes 786440 | tf_op jit(solution)/shard_map/ppermute | solution.py:61
  25.4 0.6 collective-permute-done.4.came
  26.1 2.1 %collective-permute-start.6 = (bf16[8,32,512]{2,1,0:T(8,128)(2,1)S(1)}, bf16[8,32,512]{2,1,0:T(8,128)(2,1)S(1)}, u32[]{:S(2)}, u32[]{:S(2)}) collective-permute-start(bf16[8,32,512]{2,1,0:T(8,128)(2,1)S(1)} %add_4.1.token), channel_id=1, source_target_pairs={{0,4},{1,3},{2,0},{3,7},{4,8},{5,1},{6,2},{7,11},{8,12},{9,5},{10,... | collective-permute-start | bytes 786440 | tf_op jit(solution)/shard_map/ppermute | solution.py:61
  28.2 1.5 %collective-permute-done.3.came = bf16[8,32,512]{2,1,0:T(8,128)(2,1)S(1)} collective-permute-done((bf16[8,32,512]{2,1,0:T(8,128)(2,1)S(1)}, bf16[8,32,512]{2,1,0:T(8,128)(2,1)S(1)}, u32[]{:S(2)}, u32[]{:S(2)}) %collective-permute-start.3) | collective-permute-done | bytes 262176 | tf_op jit(solution)/shard_map/ppermute | solution.py:61
  29.8 2.1 %collective-permute-start.5 = (bf16[8,32,512]{2,1,0:T(8,128)(2,1)S(1)}, bf16[8,32,512]{2,1,0:T(8,128)(2,1)S(1)}, u32[]{:S(2)}, u32[]{:S(2)}) collective-permute-start(bf16[8,32,512]{2,1,0:T(8,128)(2,1)S(1)} %add_3.1.token), channel_id=1, source_target_pairs={{0,4},{1,3},{2,0},{3,7},{4,8},{5,1},{6,2},{7,11},{8,12},{9,5},{10,... | collective-permute-start | bytes 786440 | tf_op jit(solution)/shard_map/ppermute | solution.py:61
  33.0 3.2 %collective-permute-done.5.came = bf16[8,32,512]{2,1,0:T(8,128)(2,1)S(1)} collective-permute-done((bf16[8,32,512]{2,1,0:T(8,128)(2,1)S(1)}, bf16[8,32,512]{2,1,0:T(8,128)(2,1)S(1)}, u32[]{:S(2)}, u32[]{:S(2)}) %collective-permute-start.5) | collective-permute-done | bytes 262176 | tf_op jit(solution)/shard_map/ppermute | solution.py:61
  36.3 2.1 %collective-permute-start.7 = (bf16[8,32,512]{2,1,0:T(8,128)(2,1)S(1)}, bf16[8,32,512]{2,1,0:T(8,128)(2,1)S(1)}, u32[]{:S(2)}, u32[]{:S(2)}) collective-permute-start(bf16[8,32,512]{2,1,0:T(8,128)(2,1)S(1)} %add_1.1), channel_id=1, source_target_pairs={{0,4},{1,3},{2,0},{3,7},{4,8},{5,1},{6,2},{7,11},{8,12},{9,5},{10,... | collective-permute-start | bytes 786440 | tf_op jit(solution)/shard_map/ppermute | solution.py:61
  38.6 4.1 %collective-permute-done.7.came = bf16[8,32,512]{2,1,0:T(8,128)(2,1)S(1)} collective-permute-done((bf16[8,32,512]{2,1,0:T(8,128)(2,1)S(1)}, bf16[8,32,512]{2,1,0:T(8,128)(2,1)S(1)}, u32[]{:S(2)}, u32[]{:S(2)}) %collective-permute-start.7) | collective-permute-done | bytes 262176 | tf_op jit(solution)/shard_map/ppermute | solution.py:61
  42.7 1.5 %mesh_step.1 = (bf16[256,512]{1,0:T(8,128)(2,1)}, bf16[256,512]{1,0:T(8,128)(2,1)S(1)}) custom-call(bf16[256,512]{1,0:T(8,128)(2,1)S(1)} %copy-done.3, bf16[512,512]{1,0:T(8,128)(2,1)S(1)} %copy-done.1, bf16[512,512]{1,0:T(8,128)(2,1)S(1)} %copy-done.2, f32[1,512]{1,0:T(1,128)S(1)} %bitcast.6, f32[6,8,32,512]{3,2,1,0:T(8,128)S(1)} %own_sums.1.token.own, ...), custom_call_target="tpu_custom_call" | custom-call | flops 268435456 | bytes 1048576 | tf_op jit(solution)/shard_map/mesh_step/pallas_call | solution.py:407
  44.2 2.0 %collective-permute-start.9 = (bf16[256,512]{1,0:T(8,128)(2,1)S(1)}, bf16[256,512]{1,0:T(8,128)(2,1)S(1)}, u32[]{:S(2)}, u32[]{:S(2)}) collective-permute-start(bf16[256,512]{1,0:T(8,128)(2,1)S(1)} %get-tuple-element.24.refs_1_.refs_0_), channel_id=1, source_target_pairs={{0,2},{1,5},{2,6},{3,1},{4,0},{5,9},{6,10},{7,3},{8,4},{9,13},{10,... | collective-permute-start | bytes 786440 | tf_op jit(solution)/shard_map/ppermute | solution.py:61
  46.2 5.8 %collective-permute-done.9.refs_0_ = bf16[256,512]{1,0:T(8,128)(2,1)S(1)} collective-permute-done((bf16[256,512]{1,0:T(8,128)(2,1)S(1)}, bf16[256,512]{1,0:T(8,128)(2,1)S(1)}, u32[]{:S(2)}, u32[]{:S(2)}) %collective-permute-start.9) | collective-permute-done | bytes 262176 | tf_op jit(solution)/shard_map/ppermute | solution.py:61
  52.0 2.4 %collective-permute-start.12 = (bf16[256,512]{1,0:T(8,128)(2,1)S(1)}, bf16[256,512]{1,0:T(8,128)(2,1)S(1)}, u32[]{:S(2)}, u32[]{:S(2)}) collective-permute-start(bf16[256,512]{1,0:T(8,128)(2,1)S(1)} %in_order.8.refs_1_), channel_id=1, source_target_pairs={{0,2},{1,5},{2,6},{3,1},{4,0},{5,9},{6,10},{7,3},{8,4},{9,13},{10,... | collective-permute-start | bytes 786440 | tf_op jit(solution)/shard_map/ppermute | solution.py:61
  54.4 1.6 %collective-permute-start.13 = (bf16[256,512]{1,0:T(8,128)(2,1)S(1)}, bf16[256,512]{1,0:T(8,128)(2,1)S(1)}, u32[]{:S(2)}, u32[]{:S(2)}) collective-permute-start(bf16[256,512]{1,0:T(8,128)(2,1)S(1)} %in_order.9.refs_2_), channel_id=1, source_target_pairs={{0,2},{1,5},{2,6},{3,1},{4,0},{5,9},{6,10},{7,3},{8,4},{9,13},{10,... | collective-permute-start | bytes 786440 | tf_op jit(solution)/shard_map/ppermute | solution.py:61
  56.0 0.6 pick_0.1
  56.6 2.7 %collective-permute-done.12.refs_0_ = bf16[256,512]{1,0:T(8,128)(2,1)S(1)} collective-permute-done((bf16[256,512]{1,0:T(8,128)(2,1)S(1)}, bf16[256,512]{1,0:T(8,128)(2,1)S(1)}, u32[]{:S(2)}, u32[]{:S(2)}) %collective-permute-start.12) | collective-permute-done | bytes 262176 | tf_op jit(solution)/shard_map/ppermute | solution.py:61
  59.3 1.5 %collective-permute-start.15 = (bf16[256,512]{1,0:T(8,128)(2,1)S(1)}, bf16[256,512]{1,0:T(8,128)(2,1)S(1)}, u32[]{:S(2)}, u32[]{:S(2)}) collective-permute-start(bf16[256,512]{1,0:T(8,128)(2,1)S(1)} %in_order.10.refs_1_.refs_0_), channel_id=1, source_target_pairs={{0,2},{1,5},{2,6},{3,1},{4,0},{5,9},{6,10},{7,3},{8,4},{9,13},{10,... | collective-permute-start | bytes 786440 | tf_op jit(solution)/shard_map/ppermute | solution.py:61
  60.7 1.3 %collective-permute-done.13.refs_0_ = bf16[256,512]{1,0:T(8,128)(2,1)S(1)} collective-permute-done((bf16[256,512]{1,0:T(8,128)(2,1)S(1)}, bf16[256,512]{1,0:T(8,128)(2,1)S(1)}, u32[]{:S(2)}, u32[]{:S(2)}) %collective-permute-start.13) | collective-permute-done | bytes 262176 | tf_op jit(solution)/shard_map/ppermute | solution.py:61
  62.1 1.5 %collective-permute-start.16 = (bf16[256,512]{1,0:T(8,128)(2,1)S(1)}, bf16[256,512]{1,0:T(8,128)(2,1)S(1)}, u32[]{:S(2)}, u32[]{:S(2)}) collective-permute-start(bf16[256,512]{1,0:T(8,128)(2,1)S(1)} %in_order.11.refs_1_), channel_id=1, source_target_pairs={{0,2},{1,5},{2,6},{3,1},{4,0},{5,9},{6,10},{7,3},{8,4},{9,13},{10,... | collective-permute-start | bytes 786440 | tf_op jit(solution)/shard_map/ppermute | solution.py:61
  64.2 1.5 %collective-permute-done.15.refs_0_ = bf16[256,512]{1,0:T(8,128)(2,1)S(1)} collective-permute-done((bf16[256,512]{1,0:T(8,128)(2,1)S(1)}, bf16[256,512]{1,0:T(8,128)(2,1)S(1)}, u32[]{:S(2)}, u32[]{:S(2)}) %collective-permute-start.15) | collective-permute-done | bytes 262176 | tf_op jit(solution)/shard_map/ppermute | solution.py:61
  65.6 1.5 %collective-permute-start.18 = (bf16[256,512]{1,0:T(8,128)(2,1)S(1)}, bf16[256,512]{1,0:T(8,128)(2,1)S(1)}, u32[]{:S(2)}, u32[]{:S(2)}) collective-permute-start(bf16[256,512]{1,0:T(8,128)(2,1)S(1)} %in_order.12.refs_1_.refs_0_), channel_id=1, source_target_pairs={{0,2},{1,5},{2,6},{3,1},{4,0},{5,9},{6,10},{7,3},{8,4},{9,13},{10,... | collective-permute-start | bytes 786440 | tf_op jit(solution)/shard_map/ppermute | solution.py:61
  67.6 0.8 %collective-permute-done.16.refs_0_ = bf16[256,512]{1,0:T(8,128)(2,1)S(1)} collective-permute-done((bf16[256,512]{1,0:T(8,128)(2,1)S(1)}, bf16[256,512]{1,0:T(8,128)(2,1)S(1)}, u32[]{:S(2)}, u32[]{:S(2)}) %collective-permute-start.16) | collective-permute-done | bytes 262176 | tf_op jit(solution)/shard_map/ppermute | solution.py:61
  68.4 0.6 pick_5.1
  69.1 2.9 %collective-permute-done.18.rest_6_ = bf16[256,512]{1,0:T(8,128)(2,1)S(1)} collective-permute-done((bf16[256,512]{1,0:T(8,128)(2,1)S(1)}, bf16[256,512]{1,0:T(8,128)(2,1)S(1)}, u32[]{:S(2)}, u32[]{:S(2)}) %collective-permute-start.18) | collective-permute-done | bytes 262176 | tf_op jit(solution)/shard_map/ppermute | solution.py:61
  72.0 1.5 %collective-permute-done.19.rest_7_ = bf16[256,512]{1,0:T(8,128)(2,1)S(1)} collective-permute-done((bf16[256,512]{1,0:T(8,128)(2,1)S(1)}, bf16[256,512]{1,0:T(8,128)(2,1)S(1)}, u32[]{:S(2)}, u32[]{:S(2)}) %collective-permute-start.19) | collective-permute-done | bytes 262176 | tf_op jit(solution)/shard_map/ppermute | solution.py:52
  73.5 5.0 %back.1 = bf16[4096,512]{1,0:T(8,128)(2,1)} custom-call(s32[4,64]{1,0:T(4,128)S(1)} %get-tuple-element.17.table_ref, bf16[16,256,128]{2,1,0:T(8,128)(2,1)S(1)} %turn.1.token.weights_ref, bf16[4096,512]{1,0:T(8,128)(2,1)} %get-tuple-element.22.latent_any, bf16[384,512]{1,0:T(8,128)(2,1)S(1)} %get-tuple-element.25.refs_1_.rest_0_, ...), custom_call_target="tpu_custom_call" | custom-call | flops 536870912 | bytes 9437184 | tf_op jit(solution)/shard_map/back/pallas_call | solution.py:458
  (39 shorter events, 4.2 us)
Async XLA Ops:
  13.2 1.7 %collective-permute-start = (bf16[9,32,512]{2,1,0:T(8,128)(2,1)S(1)}, bf16[9,32,512]{2,1,0:T(8,128)(2,1)S(1)}, u32[]{:S(2)}, u32[]{:S(2)}) collective-permute-start(bf16[9,32,512]{2,1,0:T(8,128)(2,1)S(1)} %get-tuple-element.20), channel_id=1, source_target_pairs={{0,1},{1,0},{2,3},{3,2},{4,5},{5,4},{6,7},{7,6},{8,9},{9,8},{10,11... | collective-permute-start | bytes 884744 | tf_op jit(solution)/shard_map/ppermute | solution.py:52
  15.7 6.0 %copy-start = (bf16[16,4,32,256]{3,2,1,0:T(8,128)(2,1)S(1)}, bf16[16,4,32,256]{3,2,1,0:T(8,128)(2,1)}, u32[]{:S(2)}) copy-start(bf16[16,4,32,256]{3,2,1,0:T(8,128)(2,1)} %interp_ref.3) | copy-start | bytes 3145732
  15.8 4.7 %collective-permute-start.1 = (bf16[25,32,512]{2,1,0:T(8,128)(2,1)S(1)}, bf16[25,32,512]{2,1,0:T(8,128)(2,1)S(1)}, u32[]{:S(2)}, u32[]{:S(2)}) collective-permute-start(bf16[25,32,512]{2,1,0:T(8,128)(2,1)S(1)} %in_order.7), channel_id=1, source_target_pairs={{0,1},{1,0},{2,3},{3,2},{4,5},{5,4},{6,7},{7,6},{8,9},{9,8},{10,11... | collective-permute-start | bytes 2457608 | tf_op jit(solution)/shard_map/ppermute | solution.py:52
  16.2 7.0 %collective-permute-start.2 = (bf16[8,32,512]{2,1,0:T(8,128)(2,1)S(1)}, bf16[8,32,512]{2,1,0:T(8,128)(2,1)S(1)}, u32[]{:S(2)}, u32[]{:S(2)}) collective-permute-start(bf16[8,32,512]{2,1,0:T(8,128)(2,1)S(1)} %get-tuple-element.21.refs_1_), channel_id=1, source_target_pairs={{0,4},{1,3},{2,0},{3,7},{4,8},{5,1},{6,2},{7,11},{8,12},{9,5},{10,... | collective-permute-start | bytes 786440 | tf_op jit(solution)/shard_map/ppermute | solution.py:61
  18.9 7.1 %collective-permute-start.4 = (bf16[8,32,512]{2,1,0:T(8,128)(2,1)S(1)}, bf16[8,32,512]{2,1,0:T(8,128)(2,1)S(1)}, u32[]{:S(2)}, u32[]{:S(2)}) collective-permute-start(bf16[8,32,512]{2,1,0:T(8,128)(2,1)S(1)} %get-tuple-element.23), channel_id=1, source_target_pairs={{0,4},{1,3},{2,0},{3,7},{4,8},{5,1},{6,2},{7,11},{8,12},{9,5},{10,... | collective-permute-start | bytes 786440 | tf_op jit(solution)/shard_map/ppermute | solution.py:61
  23.2 6.4 %collective-permute-start.3 = (bf16[8,32,512]{2,1,0:T(8,128)(2,1)S(1)}, bf16[8,32,512]{2,1,0:T(8,128)(2,1)S(1)}, u32[]{:S(2)}, u32[]{:S(2)}) collective-permute-start(bf16[8,32,512]{2,1,0:T(8,128)(2,1)S(1)} %add_5.1.token), channel_id=1, source_target_pairs={{0,4},{1,3},{2,0},{3,7},{4,8},{5,1},{6,2},{7,11},{8,12},{9,5},{10,... | collective-permute-start | bytes 786440 | tf_op jit(solution)/shard_map/ppermute | solution.py:61
  26.1 6.4 %collective-permute-start.6 = (bf16[8,32,512]{2,1,0:T(8,128)(2,1)S(1)}, bf16[8,32,512]{2,1,0:T(8,128)(2,1)S(1)}, u32[]{:S(2)}, u32[]{:S(2)}) collective-permute-start(bf16[8,32,512]{2,1,0:T(8,128)(2,1)S(1)} %add_4.1.token), channel_id=1, source_target_pairs={{0,4},{1,3},{2,0},{3,7},{4,8},{5,1},{6,2},{7,11},{8,12},{9,5},{10,... | collective-permute-start | bytes 786440 | tf_op jit(solution)/shard_map/ppermute | solution.py:61
  29.7 13.0 %copy-start.1 = (bf16[512,512]{1,0:T(8,128)(2,1)S(1)}, bf16[512,512]{1,0:T(8,128)(2,1)}, u32[]{:S(2)}) copy-start(bf16[512,512]{1,0:T(8,128)(2,1)} %up_ref.1) | copy-start | bytes 1572868
  29.7 13.0 %copy-start.2 = (bf16[512,512]{1,0:T(8,128)(2,1)S(1)}, bf16[512,512]{1,0:T(8,128)(2,1)}, u32[]{:S(2)}) copy-start(bf16[512,512]{1,0:T(8,128)(2,1)} %down_ref.1) | copy-start | bytes 1572868
  29.8 12.9 %copy-start.3 = (bf16[256,512]{1,0:T(8,128)(2,1)S(1)}, bf16[256,512]{1,0:T(8,128)(2,1)}, u32[]{:S(2)}) copy-start(bf16[256,512]{1,0:T(8,128)(2,1)} %latent_ref.1) | copy-start | bytes 786436
  29.8 12.9 %copy-start.4 = (f32[512]{0:T(512)S(1)}, f32[512]{0:T(512)}, u32[]{:S(2)}) copy-start(f32[512]{0:T(512)} %param.21) | copy-start | bytes 6148
  29.8 6.4 %collective-permute-start.5 = (bf16[8,32,512]{2,1,0:T(8,128)(2,1)S(1)}, bf16[8,32,512]{2,1,0:T(8,128)(2,1)S(1)}, u32[]{:S(2)}, u32[]{:S(2)}) collective-permute-start(bf16[8,32,512]{2,1,0:T(8,128)(2,1)S(1)} %add_3.1.token), channel_id=1, source_target_pairs={{0,4},{1,3},{2,0},{3,7},{4,8},{5,1},{6,2},{7,11},{8,12},{9,5},{10,... | collective-permute-start | bytes 786440 | tf_op jit(solution)/shard_map/ppermute | solution.py:61
  32.6 6.1 %collective-permute-start.8 = (bf16[8,32,512]{2,1,0:T(8,128)(2,1)S(1)}, bf16[8,32,512]{2,1,0:T(8,128)(2,1)S(1)}, u32[]{:S(2)}, u32[]{:S(2)}) collective-permute-start(bf16[8,32,512]{2,1,0:T(8,128)(2,1)S(1)} %add_2.1.token), channel_id=1, source_target_pairs={{0,5},{1,2},{2,1},{3,6},{4,9},{5,0},{6,3},{7,10},{8,13},{9,4},{10,... | collective-permute-start | bytes 786440 | tf_op jit(solution)/shard_map/ppermute | solution.py:61
  36.3 6.4 %collective-permute-start.7 = (bf16[8,32,512]{2,1,0:T(8,128)(2,1)S(1)}, bf16[8,32,512]{2,1,0:T(8,128)(2,1)S(1)}, u32[]{:S(2)}, u32[]{:S(2)}) collective-permute-start(bf16[8,32,512]{2,1,0:T(8,128)(2,1)S(1)} %add_1.1), channel_id=1, source_target_pairs={{0,4},{1,3},{2,0},{3,7},{4,8},{5,1},{6,2},{7,11},{8,12},{9,5},{10,... | collective-permute-start | bytes 786440 | tf_op jit(solution)/shard_map/ppermute | solution.py:61
  44.2 7.8 %collective-permute-start.9 = (bf16[256,512]{1,0:T(8,128)(2,1)S(1)}, bf16[256,512]{1,0:T(8,128)(2,1)S(1)}, u32[]{:S(2)}, u32[]{:S(2)}) collective-permute-start(bf16[256,512]{1,0:T(8,128)(2,1)S(1)} %get-tuple-element.24.refs_1_.refs_0_), channel_id=1, source_target_pairs={{0,2},{1,5},{2,6},{3,1},{4,0},{5,9},{6,10},{7,3},{8,4},{9,13},{10,... | collective-permute-start | bytes 786440 | tf_op jit(solution)/shard_map/ppermute | solution.py:61
  46.2 8.2 %collective-permute-start.10 = (bf16[256,512]{1,0:T(8,128)(2,1)S(1)}, bf16[256,512]{1,0:T(8,128)(2,1)S(1)}, u32[]{:S(2)}, u32[]{:S(2)}) collective-permute-start(bf16[256,512]{1,0:T(8,128)(2,1)S(1)} %get-tuple-element.24.refs_1_.refs_0_), channel_id=1, source_target_pairs={{0,5},{1,2},{2,1},{3,6},{4,9},{5,0},{6,3},{7,10},{8,13},{9,4},{10,... | collective-permute-start | bytes 786440 | tf_op jit(solution)/shard_map/ppermute | solution.py:61
  52.0 7.3 %collective-permute-start.12 = (bf16[256,512]{1,0:T(8,128)(2,1)S(1)}, bf16[256,512]{1,0:T(8,128)(2,1)S(1)}, u32[]{:S(2)}, u32[]{:S(2)}) collective-permute-start(bf16[256,512]{1,0:T(8,128)(2,1)S(1)} %in_order.8.refs_1_), channel_id=1, source_target_pairs={{0,2},{1,5},{2,6},{3,1},{4,0},{5,9},{6,10},{7,3},{8,4},{9,13},{10,... | collective-permute-start | bytes 786440 | tf_op jit(solution)/shard_map/ppermute | solution.py:61
  54.4 7.7 %collective-permute-start.13 = (bf16[256,512]{1,0:T(8,128)(2,1)S(1)}, bf16[256,512]{1,0:T(8,128)(2,1)S(1)}, u32[]{:S(2)}, u32[]{:S(2)}) collective-permute-start(bf16[256,512]{1,0:T(8,128)(2,1)S(1)} %in_order.9.refs_2_), channel_id=1, source_target_pairs={{0,2},{1,5},{2,6},{3,1},{4,0},{5,9},{6,10},{7,3},{8,4},{9,13},{10,... | collective-permute-start | bytes 786440 | tf_op jit(solution)/shard_map/ppermute | solution.py:61
  59.3 6.4 %collective-permute-start.15 = (bf16[256,512]{1,0:T(8,128)(2,1)S(1)}, bf16[256,512]{1,0:T(8,128)(2,1)S(1)}, u32[]{:S(2)}, u32[]{:S(2)}) collective-permute-start(bf16[256,512]{1,0:T(8,128)(2,1)S(1)} %in_order.10.refs_1_.refs_0_), channel_id=1, source_target_pairs={{0,2},{1,5},{2,6},{3,1},{4,0},{5,9},{6,10},{7,3},{8,4},{9,13},{10,... | collective-permute-start | bytes 786440 | tf_op jit(solution)/shard_map/ppermute | solution.py:61
  62.1 6.4 %collective-permute-start.16 = (bf16[256,512]{1,0:T(8,128)(2,1)S(1)}, bf16[256,512]{1,0:T(8,128)(2,1)S(1)}, u32[]{:S(2)}, u32[]{:S(2)}) collective-permute-start(bf16[256,512]{1,0:T(8,128)(2,1)S(1)} %in_order.11.refs_1_), channel_id=1, source_target_pairs={{0,2},{1,5},{2,6},{3,1},{4,0},{5,9},{6,10},{7,3},{8,4},{9,13},{10,... | collective-permute-start | bytes 786440 | tf_op jit(solution)/shard_map/ppermute | solution.py:61
  65.6 6.4 %collective-permute-start.18 = (bf16[256,512]{1,0:T(8,128)(2,1)S(1)}, bf16[256,512]{1,0:T(8,128)(2,1)S(1)}, u32[]{:S(2)}, u32[]{:S(2)}) collective-permute-start(bf16[256,512]{1,0:T(8,128)(2,1)S(1)} %in_order.12.refs_1_.refs_0_), channel_id=1, source_target_pairs={{0,2},{1,5},{2,6},{3,1},{4,0},{5,9},{6,10},{7,3},{8,4},{9,13},{10,... | collective-permute-start | bytes 786440 | tf_op jit(solution)/shard_map/ppermute | solution.py:61
  67.1 4.9 %collective-permute-start.11 = (bf16[384,512]{1,0:T(8,128)(2,1)S(1)}, bf16[384,512]{1,0:T(8,128)(2,1)S(1)}, u32[]{:S(2)}, u32[]{:S(2)}) collective-permute-start(bf16[384,512]{1,0:T(8,128)(2,1)S(1)} %get-tuple-element.26), channel_id=1, source_target_pairs={{0,1},{1,0},{2,3},{3,2},{4,5},{5,4},{6,7},{7,6},{8,9},{9,8},{10,11... | collective-permute-start | bytes 1179656 | tf_op jit(solution)/shard_map/ppermute | solution.py:52
  67.1 4.9 %collective-permute-start.14 = (bf16[256,512]{1,0:T(8,128)(2,1)S(1)}, bf16[256,512]{1,0:T(8,128)(2,1)S(1)}, u32[]{:S(2)}, u32[]{:S(2)}) collective-permute-start(bf16[256,512]{1,0:T(8,128)(2,1)S(1)} %get-tuple-element.28), channel_id=1, source_target_pairs={{0,1},{1,0},{2,3},{3,2},{4,5},{5,4},{6,7},{7,6},{8,9},{9,8},{10,11... | collective-permute-start | bytes 786440 | tf_op jit(solution)/shard_map/ppermute | solution.py:52
  69.1 3.0 %collective-permute-start.17 = (bf16[256,512]{1,0:T(8,128)(2,1)S(1)}, bf16[256,512]{1,0:T(8,128)(2,1)S(1)}, u32[]{:S(2)}, u32[]{:S(2)}) collective-permute-start(bf16[256,512]{1,0:T(8,128)(2,1)S(1)} %get-tuple-element.30), channel_id=1, source_target_pairs={{0,1},{1,0},{2,3},{3,2},{4,5},{5,4},{6,7},{7,6},{8,9},{9,8},{10,11... | collective-permute-start | bytes 786440 | tf_op jit(solution)/shard_map/ppermute | solution.py:52
  72.0 1.5 %collective-permute-start.19 = (bf16[256,512]{1,0:T(8,128)(2,1)S(1)}, bf16[256,512]{1,0:T(8,128)(2,1)S(1)}, u32[]{:S(2)}, u32[]{:S(2)}) collective-permute-start(bf16[256,512]{1,0:T(8,128)(2,1)S(1)} %collective-permute-done.18.rest_6_), channel_id=1, source_target_pairs={{0,1},{1,0},{2,3},{3,2},{4,5},{5,4},{6,7},{7,6},{8,9},{9,8},{10,11... | collective-permute-start | bytes 786440 | tf_op jit(solution)/shard_map/ppermute | solution.py:52

commit v13 on v9

--- a/solution.py
+++ b/solution.py
@@ -11,7 +11,8 @@
 BF16 = jnp.bfloat16
 N_CORE = 2
 STRIP = 32
-PART = 4
+PART = 2
+BACK_PART = 4
 
 
 def silu(values):
@@ -51,14 +52,20 @@
     def over_core(self, value):
         return lax.ppermute(value, "band", [(i, i ^ 1) for i in range(self.n_band)])
 
-    def over(self, value, by, cross=0):
+    def over(self, value, right):
         pairs = []
         for i in range(self.n_band):
             chip, core = divmod(i, N_CORE)
             z, y = divmod(chip, self.n_y)
             ring = z if y == 0 else self.chips - 1 - z
-            pairs.append((i, self.index(ring + (-by if core else by), core ^ cross)))
+            pairs.append((i, self.index(ring + (1 if core == right else -1), 1 - core)))
         return lax.ppermute(value, "band", pairs)
+
+    def over_first(self, value, distance):
+        return self.over(value, distance % 2)
+
+    def over_second(self, value, distance):
+        return self.over(value, (distance + 1) % 2)
 
     def entry(self, lists_ref, me, block, k):
         owner, tile = split(lists_ref[k, block], self.tiles)
@@ -66,11 +73,11 @@
         my_ring, my_core = self.place(me)
         ahead = split(ring - my_ring + self.chips, self.chips)[1]
         left = (ahead > self.far).astype(jnp.int32)
+        distance = jnp.where(ahead > self.far, self.chips - ahead, ahead)
         shared = (ahead == 0) | (ahead == self.far)
-        handler = jnp.where(shared, core, left)
-        distance = jnp.where(ahead > self.far, self.chips - ahead, ahead)
-        group = jnp.maximum(2 * distance - 1 + (core ^ handler), 0)
-        return handler ^ my_core, group, tile
+        stream = jnp.where(shared, 0, core ^ left)
+        group = jnp.maximum(2 * distance - 1 + stream, 0)
+        return ((distance + core) & 1) ^ my_core, group, tile
 
 
 def strips(rows):
@@ -192,36 +199,47 @@
         out_ref[b] = interp_ref[b].reshape(out_ref.shape[2], out_ref.shape[1]).T
 
 
-def back_kernel(starts, list_len, per_step, table_ref, latent_ref, weights_ref, *rest):
+def back_kernel(starts, list_len, table_ref, weights_ref, latent_any, *rest):
     count = len(starts)
-    pieces, (out_ref, held, total, sems) = rest[:count], rest[count:]
-    step = pl.program_id(0)
-    block_rows = weights_ref.shape[1]
-    tile_rows = weights_ref.shape[2] // list_len
-
-    @pl.when(step == 0)
-    def _():
-        copies = []
-        for i, (piece, start) in enumerate(zip(pieces, starts)):
-            into = held.at[pl.ds(start, piece.shape[0])]
-            copies.append(pltpu.make_async_copy(piece, into, sems.at[i]))
-        for copy in copies:
-            copy.start()
-        for copy in copies:
-            copy.wait()
-
-    for b in range(per_step):
+    pieces, (out_any, held, latent_ref, total, out_ref, sems) = rest[:count], rest[count:]
+    blk_count, block_rows, listed = weights_ref.shape
+    tile_rows = listed // list_len
+    copies = []
+
+    def copy(source, target):
+        copies.append(pltpu.make_async_copy(source, target, sems.at[len(copies)]))
+        return copies[-1]
+
+    pieces_in = []
+    for piece, start in zip(pieces, starts):
+        pieces_in.append(copy(piece, held.at[pl.ds(start, piece.shape[0])]))
+    part_rows = BACK_PART * block_rows
+    parts = [pl.ds(i * part_rows, part_rows) for i in range(blk_count // BACK_PART)]
+    latent_in = [copy(latent_any.at[rows], latent_ref.at[rows]) for rows in parts]
+    outs = [copy(out_ref.at[rows], out_any.at[rows]) for rows in parts]
+    for started in pieces_in + latent_in:
+        started.start()
+    for started in pieces_in:
+        started.wait()
+
+    for block in range(blk_count):
         values = []
         for k in range(list_len):
-            entry = (step * per_step + b) * list_len + k
+            entry = block * list_len + k
             rows = pl.ds(pl.multiple_of(table_ref[2, entry] * tile_rows, tile_rows), tile_rows)
             value = held[rows]
             values.append(jnp.where(table_ref[3, entry] == 1, value, jnp.zeros_like(value)))
         value = jnp.concatenate(values, axis=0)
-        rows = slice(b * block_rows, (b + 1) * block_rows)
-        total[rows] = jnp.dot(weights_ref[b], value, preferred_element_type=F32)
+        rows = slice(block * block_rows, (block + 1) * block_rows)
+        total[rows] = jnp.dot(weights_ref[block], value, preferred_element_type=F32)
+        if block % BACK_PART == 0:
+            latent_in[block // BACK_PART].wait()
         for strip in strips(rows):
             out_ref[strip] = (latent_ref[strip].astype(F32) + total[strip]).astype(BF16)
+        if block % BACK_PART == BACK_PART - 1:
+            outs[block // BACK_PART].start()
+    for started in outs:
+        started.wait()
 
 
 def whole(array):
@@ -271,7 +289,10 @@
         return pltpu.with_memory_space_constraint(array, pltpu.HBM)
 
     gain = embed_gain.reshape(1, width)
-    per_step = 8
+    in_vmem = pl.BlockSpec(memory_space=pltpu.VMEM)
+    in_any = pl.BlockSpec(memory_space=pl.ANY)
+    grid_rows = blk_count * block_rows
+    per_step = 4
     rows = per_step * block_rows
     counts = (chips * slots, 2 * slots, (chips - 2) * slots)
     latent, kept, sent_far, sent_rest, table = pl.pallas_call(
@@ -294,7 +315,7 @@
             + [pl.BlockSpec(memory_space=pltpu.SMEM)],
             scratch_shapes=[pltpu.VMEM((rows, width), F32), pltpu.VMEM((rows, width), BF16)],
         ),
-        compiler_params=params(32),
+        compiler_params=params(24),
         cost_estimate=cost(
             2 * blk_count * block_rows * width * (channels + width + list_len * tile_rows),
             grid_features,
@@ -305,8 +326,7 @@
     other_far = ring.over_core(sent_far)
 
     dense = (tiles, tile_rows, width)
-    in_vmem = pl.BlockSpec(memory_space=pltpu.VMEM)
-    in_any = pl.BlockSpec(memory_space=pl.ANY)
+
     def in_order(value, token):
         return pl.pallas_call(
             order_kernel,
@@ -359,7 +379,7 @@
             name=f"add_{group}",
         )(own, value, token)
 
-    first, second = ring.over(first, 1), ring.over(second, 1)
+    first, second = ring.over_first(first, far), ring.over_second(second, far - 1)
     turned = (blk_count, block_rows, list_len * tile_rows)
     per_step = 4
     token = weights = pl.pallas_call(
@@ -373,12 +393,13 @@
         name="turn",
     )(interp, own)
     for group in range(chips - 3, 0, -1):
+        distance = (group + 1) // 2
         if group % 2:
             token = add_own(group, first, token)
-            first = ring.over(token, 1)
+            first = ring.over_first(token, distance)
         else:
             token = add_own(group, second, token)
-            second = ring.over(token, 1, int(group == 2))
+            second = ring.over_second(token, distance)
 
     mesh_gain = mesh_gain.reshape(1, width)
     mesh_out, piece = pl.pallas_call(
@@ -416,15 +437,14 @@
         share(chosen[0] * slots, mine, theirs)
         return mine
 
-    first = ring.over(piece, -1)
-    second = ring.over(piece, 1, 1)
+    first, second = ring.over_first(piece, 1), ring.over_second(piece, 1)
     token = piece
     for distance in range(1, far):
         first = in_order(first, token)
-        onward = ring.over(first, -1)
+        onward = ring.over_first(first, distance + 1)
         second = in_order(second, first)
         if distance < far - 1:
-            after = ring.over(second, -1)
+            after = ring.over_second(second, distance + 1)
         chosen, values = [2 * distance - 1, 2 * distance], [first, second]
         if distance == 1:
             chosen, values = [0] + chosen, [piece] + values
@@ -432,32 +452,26 @@
         first, second = onward, after
     share((chips - 1) * slots, first, first)
 
-    per_step = 4
-    rows = per_step * block_rows
     grid_out = pl.pallas_call(
-        functools.partial(back_kernel, starts, list_len, per_step),
-        out_shape=shape((blk_count * block_rows, width)),
+        functools.partial(back_kernel, starts, list_len),
+        out_shape=shape((grid_rows, width)),
         grid_spec=pltpu.PrefetchScalarGridSpec(
             num_scalar_prefetch=1,
-            grid=(blk_count // per_step,),
-            in_specs=[
-                pl.BlockSpec((rows, width), lambda i, *_: (i, 0)),
-                pl.BlockSpec((per_step,) + weights.shape[1:], lambda i, *_: (i, 0, 0)),
-            ]
-            + [pl.BlockSpec(memory_space=pl.ANY)] * len(pieces),
-            out_specs=pl.BlockSpec((rows, width), lambda i, *_: (i, 0)),
+            grid=(1,),
+            in_specs=[in_vmem] + [in_any] * (1 + len(pieces)),
+            out_specs=in_any,
             scratch_shapes=[
                 pltpu.VMEM((N_CORE * ((chips - 1) * slots + tiles) * tile_rows, width), BF16),
-                pltpu.VMEM((rows, width), F32),
-                pltpu.SemaphoreType.DMA((len(pieces),)),
+                pltpu.VMEM((grid_rows, width), BF16),
+                pltpu.VMEM((grid_rows, width), F32),
+                pltpu.VMEM((grid_rows, width), BF16),
+                pltpu.SemaphoreType.DMA((len(pieces) + 2 * (blk_count // BACK_PART),)),
             ],
         ),
-        compiler_params=params(20),
-        cost_estimate=cost(
-            2 * blk_count * block_rows * width * list_len * tile_rows, latent, latent, interp
-        ),
+        compiler_params=params(32),
+        cost_estimate=cost(2 * grid_rows * width * list_len * tile_rows, latent, latent, interp),
         name="back",
-    )(table, in_hbm(latent), weights, *pieces)
+    )(table, weights, in_hbm(latent), *pieces)
     return (grid_out, mesh_out)
 
 

time: 78.6 us -> 78.7 us (level); the launches traced: 78.4 us -> 77.3 us
  Pallas kernels: 23.6 us -> 22 us
  starting transfers between devices: 25.2 us -> 26.3 us
    pallas_call x1, Pallas kernels: 6.82 us -> 5.03 us  [on_device(): pl.pallas_call(functools.partial(back_kernel, starts, list_len), out_shap...]
    ppermute x14, starting transfers between devices: 23.8 us -> 24.8 us  [over(): return lax.ppermute(value, 'band', pairs)]
  transfers between devices with their start and end apart: 20 -> 20, of which waited for: 15 -> 13; matrix products, arithmetic and copies ran while one was open for 0% -> 0% of each run, Pallas kernels for 5% -> 5%
where the time goes in v13:
time: 78.7 us; the launch traced here: 77.3 us
  waiting for transfers between devices  28.2 us (36%)
  starting transfers between devices  26.3 us (33%)
  Pallas kernels  22 us (28%)
  between operations  0.81 us (1%)
    ppermute x14, waiting for transfers between devices, over(): return lax.ppermute(value, 'band', pairs)  25.4 us
    ppermute x14, starting transfers between devices, over(): return lax.ppermute(value, 'band', pairs)  24.8 us
    pallas_call x1, Pallas kernels, on_device(): pl.pallas_call(functools.partial(embed_kernel, ring, per_step, slots), ou...  10.9 us
    pallas_call x1, Pallas kernels, on_device(): pl.pallas_call(functools.partial(back_kernel, starts, list_len), out_shap...  5.03 us
    ppermute x6, waiting for transfers between devices, over_core(): return lax.ppermute(value, 'band', [(i, i ^ 1) for i in range(self.n_band)])  2.73 us
    pallas_call x3, Pallas kernels, pick(): pl.pallas_call(functools.partial(pick_kernel, chosen, slots, chips, tile_...  1.83 us
  transfers between devices with their start and end apart: 20, of which 13 were waited for; matrix products, arithmetic and copies ran while one was open for 0% of the time, Pallas kernels for 5%

profile of v13, /device:TPU:0, one launch (start us, length us, event | category | flops | bytes accessed | tf_op | source)
XLA Modules:
  0.0 77.3 jit_solution(2675445593621623791)
XLA Ops:
  0.6 10.9 %embed.1 = (bf16[4096,512]{1,0:T(8,128)(2,1)}, bf16[33,32,512]{2,1,0:T(8,128)(2,1)S(1)}, bf16[9,32,512]{2,1,0:T(8,128)(2,1)S(1)}, bf16[25,32,512]{2,1,0:T(8,128)(2,1)S(1)}, s32[4,64]{1,0:T(4,128)S(1)}) custom-call(s32[1]{0:T(128)} %bitcast.me_ref, s32[4,256]{1,0:T(4,128)} %bitcast.8, s32[4,256]{1,0:T(4,128)} %bitcast.9, bf16[227,4096]{1,0:T(8,128)(2,1)} %bitcast.7, ...), custom_call_target="tpu_custom_call" | custom-call | flops 3636461568 | bytes 2908160 | tf_op jit(solution)/shard_map/embed/pallas_call | solution.py:298
  12.0 1.2 %collective-permute-done.other = bf16[9,32,512]{2,1,0:T(8,128)(2,1)S(1)} collective-permute-done((bf16[9,32,512]{2,1,0:T(8,128)(2,1)S(1)}, bf16[9,32,512]{2,1,0:T(8,128)(2,1)S(1)}, u32[]{:S(2)}, u32[]{:S(2)}) %collective-permute-start) | collective-permute-done | bytes 294944 | tf_op jit(solution)/shard_map/ppermute | solution.py:53
  13.2 0.8 %far_sums.1 = (bf16[8,32,512]{2,1,0:T(8,128)(2,1)S(1)}, bf16[8,32,512]{2,1,0:T(8,128)(2,1)S(1)}) custom-call(s32[4,64]{1,0:T(4,128)S(1)} %get-tuple-element.17.table_ref, bf16[33,32,512]{2,1,0:T(8,128)(2,1)S(1)} %get-tuple-element.18.kept, bf16[9,32,512]{2,1,0:T(8,128)(2,1)S(1)} %collective-permute-done.other), custom_call_target="tpu_custom_call" | custom-call | bytes 1081344 | tf_op jit(solution)/shard_map/far_sums/pallas_call | solution.py:342
  14.5 2.7 %collective-permute-start.2 = (bf16[8,32,512]{2,1,0:T(8,128)(2,1)S(1)}, bf16[8,32,512]{2,1,0:T(8,128)(2,1)S(1)}, u32[]{:S(2)}, u32[]{:S(2)}) collective-permute-start(bf16[8,32,512]{2,1,0:T(8,128)(2,1)S(1)} %get-tuple-element.21.refs_1_), channel_id=1, source_target_pairs={{0,5},{1,2},{2,1},{3,6},{4,9},{5,0},{6,3},{7,10},{8,13},{9,4},{10,... | collective-permute-start | bytes 786440 | tf_op jit(solution)/shard_map/ppermute | solution.py:62
  17.2 1.2 %own_sums.1.token.own = f32[6,8,32,512]{3,2,1,0:T(8,128)S(1)} custom-call(s32[4,64]{1,0:T(4,128)S(1)} %get-tuple-element.17.table_ref, bf16[33,32,512]{2,1,0:T(8,128)(2,1)S(1)} %get-tuple-element.18.kept, bf16[25,32,512]{2,1,0:T(8,128)(2,1)S(1)} %collective-permute-done.1.other), custom_call_target="tpu_custom_call" | custom-call | bytes 4325376 | tf_op jit(solution)/shard_map/own_sums/pallas_call | solution.py:357
  18.9 2.3 %collective-permute-done.2.came = bf16[8,32,512]{2,1,0:T(8,128)(2,1)S(1)} collective-permute-done((bf16[8,32,512]{2,1,0:T(8,128)(2,1)S(1)}, bf16[8,32,512]{2,1,0:T(8,128)(2,1)S(1)}, u32[]{:S(2)}, u32[]{:S(2)}) %collective-permute-start.2) | collective-permute-done | bytes 262176 | tf_op jit(solution)/shard_map/ppermute | solution.py:62
  21.3 2.0 %collective-permute-start.3 = (bf16[8,32,512]{2,1,0:T(8,128)(2,1)S(1)}, bf16[8,32,512]{2,1,0:T(8,128)(2,1)S(1)}, u32[]{:S(2)}, u32[]{:S(2)}) collective-permute-start(bf16[8,32,512]{2,1,0:T(8,128)(2,1)S(1)} %add_5.1.token), channel_id=1, source_target_pairs={{0,3},{1,4},{2,7},{3,0},{4,1},{5,8},{6,11},{7,2},{8,5},{9,12},{10,... | collective-permute-start | bytes 786440 | tf_op jit(solution)/shard_map/ppermute | solution.py:62
  23.3 0.7 collective-permute-done.4.came
  24.1 2.1 %collective-permute-start.6 = (bf16[8,32,512]{2,1,0:T(8,128)(2,1)S(1)}, bf16[8,32,512]{2,1,0:T(8,128)(2,1)S(1)}, u32[]{:S(2)}, u32[]{:S(2)}) collective-permute-start(bf16[8,32,512]{2,1,0:T(8,128)(2,1)S(1)} %add_4.1.token), channel_id=1, source_target_pairs={{0,3},{1,4},{2,7},{3,0},{4,1},{5,8},{6,11},{7,2},{8,5},{9,12},{10,... | collective-permute-start | bytes 786440 | tf_op jit(solution)/shard_map/ppermute | solution.py:62
  26.2 1.2 %collective-permute-done.3.came = bf16[8,32,512]{2,1,0:T(8,128)(2,1)S(1)} collective-permute-done((bf16[8,32,512]{2,1,0:T(8,128)(2,1)S(1)}, bf16[8,32,512]{2,1,0:T(8,128)(2,1)S(1)}, u32[]{:S(2)}, u32[]{:S(2)}) %collective-permute-start.3) | collective-permute-done | bytes 262176 | tf_op jit(solution)/shard_map/ppermute | solution.py:62
  27.5 2.2 %collective-permute-start.5 = (bf16[8,32,512]{2,1,0:T(8,128)(2,1)S(1)}, bf16[8,32,512]{2,1,0:T(8,128)(2,1)S(1)}, u32[]{:S(2)}, u32[]{:S(2)}) collective-permute-start(bf16[8,32,512]{2,1,0:T(8,128)(2,1)S(1)} %add_3.1.token), channel_id=1, source_target_pairs={{0,5},{1,2},{2,1},{3,6},{4,9},{5,0},{6,3},{7,10},{8,13},{9,4},{10,... | collective-permute-start | bytes 786440 | tf_op jit(solution)/shard_map/ppermute | solution.py:62
  29.6 0.7 collective-permute-done.6.came
  30.4 2.4 %collective-permute-start.8 = (bf16[8,32,512]{2,1,0:T(8,128)(2,1)S(1)}, bf16[8,32,512]{2,1,0:T(8,128)(2,1)S(1)}, u32[]{:S(2)}, u32[]{:S(2)}) collective-permute-start(bf16[8,32,512]{2,1,0:T(8,128)(2,1)S(1)} %add_2.1.token), channel_id=1, source_target_pairs={{0,5},{1,2},{2,1},{3,6},{4,9},{5,0},{6,3},{7,10},{8,13},{9,4},{10,... | collective-permute-start | bytes 786440 | tf_op jit(solution)/shard_map/ppermute | solution.py:62
  32.8 0.9 %collective-permute-done.5.came = bf16[8,32,512]{2,1,0:T(8,128)(2,1)S(1)} collective-permute-done((bf16[8,32,512]{2,1,0:T(8,128)(2,1)S(1)}, bf16[8,32,512]{2,1,0:T(8,128)(2,1)S(1)}, u32[]{:S(2)}, u32[]{:S(2)}) %collective-permute-start.5) | collective-permute-done | bytes 262176 | tf_op jit(solution)/shard_map/ppermute | solution.py:62
  33.8 2.0 %collective-permute-start.7 = (bf16[8,32,512]{2,1,0:T(8,128)(2,1)S(1)}, bf16[8,32,512]{2,1,0:T(8,128)(2,1)S(1)}, u32[]{:S(2)}, u32[]{:S(2)}) collective-permute-start(bf16[8,32,512]{2,1,0:T(8,128)(2,1)S(1)} %add_1.1), channel_id=1, source_target_pairs={{0,3},{1,4},{2,7},{3,0},{4,1},{5,8},{6,11},{7,2},{8,5},{9,12},{10,... | collective-permute-start | bytes 786440 | tf_op jit(solution)/shard_map/ppermute | solution.py:62
  35.8 1.4 %collective-permute-done.8.neighbour = bf16[8,32,512]{2,1,0:T(8,128)(2,1)S(1)} collective-permute-done((bf16[8,32,512]{2,1,0:T(8,128)(2,1)S(1)}, bf16[8,32,512]{2,1,0:T(8,128)(2,1)S(1)}, u32[]{:S(2)}, u32[]{:S(2)}) %collective-permute-start.8) | collective-permute-done | bytes 262176 | tf_op jit(solution)/shard_map/ppermute | solution.py:62
  37.2 2.7 %collective-permute-done.7.came = bf16[8,32,512]{2,1,0:T(8,128)(2,1)S(1)} collective-permute-done((bf16[8,32,512]{2,1,0:T(8,128)(2,1)S(1)}, bf16[8,32,512]{2,1,0:T(8,128)(2,1)S(1)}, u32[]{:S(2)}, u32[]{:S(2)}) %collective-permute-start.7) | collective-permute-done | bytes 262176 | tf_op jit(solution)/shard_map/ppermute | solution.py:62
  39.9 1.5 %mesh_step.1 = (bf16[256,512]{1,0:T(8,128)(2,1)}, bf16[256,512]{1,0:T(8,128)(2,1)S(1)}) custom-call(bf16[256,512]{1,0:T(8,128)(2,1)S(1)} %copy-done.3, bf16[512,512]{1,0:T(8,128)(2,1)S(1)} %copy-done.1, bf16[512,512]{1,0:T(8,128)(2,1)S(1)} %copy-done.2, f32[1,512]{1,0:T(1,128)S(1)} %bitcast.6, f32[6,8,32,512]{3,2,1,0:T(8,128)S(1)} %own_sums.1.token.own, ...), custom_call_target="tpu_custom_call" | custom-call | flops 268435456 | bytes 1048576 | tf_op jit(solution)/shard_map/mesh_step/pallas_call | solution.py:405
  41.3 1.7 %collective-permute-start.9 = (bf16[256,512]{1,0:T(8,128)(2,1)S(1)}, bf16[256,512]{1,0:T(8,128)(2,1)S(1)}, u32[]{:S(2)}, u32[]{:S(2)}) collective-permute-start(bf16[256,512]{1,0:T(8,128)(2,1)S(1)} %get-tuple-element.24.refs_1_.refs_0_), channel_id=1, source_target_pairs={{0,3},{1,4},{2,7},{3,0},{4,1},{5,8},{6,11},{7,2},{8,5},{9,12},{10,... | collective-permute-start | bytes 786440 | tf_op jit(solution)/shard_map/ppermute | solution.py:62
  43.1 1.7 %collective-permute-start.10 = (bf16[256,512]{1,0:T(8,128)(2,1)S(1)}, bf16[256,512]{1,0:T(8,128)(2,1)S(1)}, u32[]{:S(2)}, u32[]{:S(2)}) collective-permute-start(bf16[256,512]{1,0:T(8,128)(2,1)S(1)} %get-tuple-element.24.refs_1_.refs_0_), channel_id=1, source_target_pairs={{0,5},{1,2},{2,1},{3,6},{4,9},{5,0},{6,3},{7,10},{8,13},{9,4},{10,... | collective-permute-start | bytes 786440 | tf_op jit(solution)/shard_map/ppermute | solution.py:62
  44.8 4.0 %collective-permute-done.9.refs_0_ = bf16[256,512]{1,0:T(8,128)(2,1)S(1)} collective-permute-done((bf16[256,512]{1,0:T(8,128)(2,1)S(1)}, bf16[256,512]{1,0:T(8,128)(2,1)S(1)}, u32[]{:S(2)}, u32[]{:S(2)}) %collective-permute-start.9) | collective-permute-done | bytes 262176 | tf_op jit(solution)/shard_map/ppermute | solution.py:62
  48.8 2.4 %collective-permute-start.12 = (bf16[256,512]{1,0:T(8,128)(2,1)S(1)}, bf16[256,512]{1,0:T(8,128)(2,1)S(1)}, u32[]{:S(2)}, u32[]{:S(2)}) collective-permute-start(bf16[256,512]{1,0:T(8,128)(2,1)S(1)} %in_order.8.refs_1_), channel_id=1, source_target_pairs={{0,5},{1,2},{2,1},{3,6},{4,9},{5,0},{6,3},{7,10},{8,13},{9,4},{10,... | collective-permute-start | bytes 786440 | tf_op jit(solution)/shard_map/ppermute | solution.py:62
  51.7 0.6 pick_0.1
  52.3 4.6 %collective-permute-done.12.refs_0_ = bf16[256,512]{1,0:T(8,128)(2,1)S(1)} collective-permute-done((bf16[256,512]{1,0:T(8,128)(2,1)S(1)}, bf16[256,512]{1,0:T(8,128)(2,1)S(1)}, u32[]{:S(2)}, u32[]{:S(2)}) %collective-permute-start.12) | collective-permute-done | bytes 262176 | tf_op jit(solution)/shard_map/ppermute | solution.py:62
  57.0 1.9 %collective-permute-start.15 = (bf16[256,512]{1,0:T(8,128)(2,1)S(1)}, bf16[256,512]{1,0:T(8,128)(2,1)S(1)}, u32[]{:S(2)}, u32[]{:S(2)}) collective-permute-start(bf16[256,512]{1,0:T(8,128)(2,1)S(1)} %in_order.10.refs_1_.refs_0_), channel_id=1, source_target_pairs={{0,3},{1,4},{2,7},{3,0},{4,1},{5,8},{6,11},{7,2},{8,5},{9,12},{10,... | collective-permute-start | bytes 786440 | tf_op jit(solution)/shard_map/ppermute | solution.py:62
  58.9 1.3 %collective-permute-start.16 = (bf16[256,512]{1,0:T(8,128)(2,1)S(1)}, bf16[256,512]{1,0:T(8,128)(2,1)S(1)}, u32[]{:S(2)}, u32[]{:S(2)}) collective-permute-start(bf16[256,512]{1,0:T(8,128)(2,1)S(1)} %in_order.11.refs_1_), channel_id=1, source_target_pairs={{0,5},{1,2},{2,1},{3,6},{4,9},{5,0},{6,3},{7,10},{8,13},{9,4},{10,... | collective-permute-start | bytes 786440 | tf_op jit(solution)/shard_map/ppermute | solution.py:62
  60.8 4.1 %collective-permute-done.15.refs_0_ = bf16[256,512]{1,0:T(8,128)(2,1)S(1)} collective-permute-done((bf16[256,512]{1,0:T(8,128)(2,1)S(1)}, bf16[256,512]{1,0:T(8,128)(2,1)S(1)}, u32[]{:S(2)}, u32[]{:S(2)}) %collective-permute-start.15) | collective-permute-done | bytes 262176 | tf_op jit(solution)/shard_map/ppermute | solution.py:62
  64.9 1.8 %collective-permute-start.18 = (bf16[256,512]{1,0:T(8,128)(2,1)S(1)}, bf16[256,512]{1,0:T(8,128)(2,1)S(1)}, u32[]{:S(2)}, u32[]{:S(2)}) collective-permute-start(bf16[256,512]{1,0:T(8,128)(2,1)S(1)} %in_order.12.refs_1_.refs_0_), channel_id=1, source_target_pairs={{0,5},{1,2},{2,1},{3,6},{4,9},{5,0},{6,3},{7,10},{8,13},{9,4},{10,... | collective-permute-start | bytes 786440 | tf_op jit(solution)/shard_map/ppermute | solution.py:62
  67.2 0.6 pick_5.1
  67.9 2.8 %collective-permute-done.18.rest_6_ = bf16[256,512]{1,0:T(8,128)(2,1)S(1)} collective-permute-done((bf16[256,512]{1,0:T(8,128)(2,1)S(1)}, bf16[256,512]{1,0:T(8,128)(2,1)S(1)}, u32[]{:S(2)}, u32[]{:S(2)}) %collective-permute-start.18) | collective-permute-done | bytes 262176 | tf_op jit(solution)/shard_map/ppermute | solution.py:62
  70.8 1.5 %collective-permute-done.19.rest_7_ = bf16[256,512]{1,0:T(8,128)(2,1)S(1)} collective-permute-done((bf16[256,512]{1,0:T(8,128)(2,1)S(1)}, bf16[256,512]{1,0:T(8,128)(2,1)S(1)}, u32[]{:S(2)}, u32[]{:S(2)}) %collective-permute-start.19) | collective-permute-done | bytes 262176 | tf_op jit(solution)/shard_map/ppermute | solution.py:53
  72.3 5.0 %back.1 = bf16[4096,512]{1,0:T(8,128)(2,1)} custom-call(s32[4,64]{1,0:T(4,128)S(1)} %get-tuple-element.17.table_ref, bf16[16,256,128]{2,1,0:T(8,128)(2,1)S(1)} %turn.1.token.weights_ref, bf16[4096,512]{1,0:T(8,128)(2,1)} %get-tuple-element.22.latent_any, bf16[384,512]{1,0:T(8,128)(2,1)S(1)} %get-tuple-element.25.refs_1_.rest_0_, ...), custom_call_target="tpu_custom_call" | custom-call | flops 536870912 | bytes 9437184 | tf_op jit(solution)/shard_map/back/pallas_call | solution.py:455
  (39 shorter events, 3.4 us)
Async XLA Ops:
  11.6 1.7 %collective-permute-start = (bf16[9,32,512]{2,1,0:T(8,128)(2,1)S(1)}, bf16[9,32,512]{2,1,0:T(8,128)(2,1)S(1)}, u32[]{:S(2)}, u32[]{:S(2)}) collective-permute-start(bf16[9,32,512]{2,1,0:T(8,128)(2,1)S(1)} %get-tuple-element.20), channel_id=1, source_target_pairs={{0,1},{1,0},{2,3},{3,2},{4,5},{5,4},{6,7},{7,6},{8,9},{9,8},{10,11... | collective-permute-start | bytes 884744 | tf_op jit(solution)/shard_map/ppermute | solution.py:53
  14.0 4.4 %copy-start = (bf16[16,4,32,256]{3,2,1,0:T(8,128)(2,1)S(1)}, bf16[16,4,32,256]{3,2,1,0:T(8,128)(2,1)}, u32[]{:S(2)}) copy-start(bf16[16,4,32,256]{3,2,1,0:T(8,128)(2,1)} %interp_ref.3) | copy-start | bytes 3145732
  14.0 3.2 %collective-permute-start.1 = (bf16[25,32,512]{2,1,0:T(8,128)(2,1)S(1)}, bf16[25,32,512]{2,1,0:T(8,128)(2,1)S(1)}, u32[]{:S(2)}, u32[]{:S(2)}) collective-permute-start(bf16[25,32,512]{2,1,0:T(8,128)(2,1)S(1)} %in_order.7), channel_id=1, source_target_pairs={{0,1},{1,0},{2,3},{3,2},{4,5},{5,4},{6,7},{7,6},{8,9},{9,8},{10,11... | collective-permute-start | bytes 2457608 | tf_op jit(solution)/shard_map/ppermute | solution.py:53
  14.5 6.7 %collective-permute-start.2 = (bf16[8,32,512]{2,1,0:T(8,128)(2,1)S(1)}, bf16[8,32,512]{2,1,0:T(8,128)(2,1)S(1)}, u32[]{:S(2)}, u32[]{:S(2)}) collective-permute-start(bf16[8,32,512]{2,1,0:T(8,128)(2,1)S(1)} %get-tuple-element.21.refs_1_), channel_id=1, source_target_pairs={{0,5},{1,2},{2,1},{3,6},{4,9},{5,0},{6,3},{7,10},{8,13},{9,4},{10,... | collective-permute-start | bytes 786440 | tf_op jit(solution)/shard_map/ppermute | solution.py:62
  17.2 6.9 %collective-permute-start.4 = (bf16[8,32,512]{2,1,0:T(8,128)(2,1)S(1)}, bf16[8,32,512]{2,1,0:T(8,128)(2,1)S(1)}, u32[]{:S(2)}, u32[]{:S(2)}) collective-permute-start(bf16[8,32,512]{2,1,0:T(8,128)(2,1)S(1)} %get-tuple-element.23), channel_id=1, source_target_pairs={{0,5},{1,2},{2,1},{3,6},{4,9},{5,0},{6,3},{7,10},{8,13},{9,4},{10,... | collective-permute-start | bytes 786440 | tf_op jit(solution)/shard_map/ppermute | solution.py:62
  21.3 6.1 %collective-permute-start.3 = (bf16[8,32,512]{2,1,0:T(8,128)(2,1)S(1)}, bf16[8,32,512]{2,1,0:T(8,128)(2,1)S(1)}, u32[]{:S(2)}, u32[]{:S(2)}) collective-permute-start(bf16[8,32,512]{2,1,0:T(8,128)(2,1)S(1)} %add_5.1.token), channel_id=1, source_target_pairs={{0,3},{1,4},{2,7},{3,0},{4,1},{5,8},{6,11},{7,2},{8,5},{9,12},{10,... | collective-permute-start | bytes 786440 | tf_op jit(solution)/shard_map/ppermute | solution.py:62
  24.1 6.2 %collective-permute-start.6 = (bf16[8,32,512]{2,1,0:T(8,128)(2,1)S(1)}, bf16[8,32,512]{2,1,0:T(8,128)(2,1)S(1)}, u32[]{:S(2)}, u32[]{:S(2)}) collective-permute-start(bf16[8,32,512]{2,1,0:T(8,128)(2,1)S(1)} %add_4.1.token), channel_id=1, source_target_pairs={{0,3},{1,4},{2,7},{3,0},{4,1},{5,8},{6,11},{7,2},{8,5},{9,12},{10,... | collective-permute-start | bytes 786440 | tf_op jit(solution)/shard_map/ppermute | solution.py:62
  27.4 12.4 %copy-start.1 = (bf16[512,512]{1,0:T(8,128)(2,1)S(1)}, bf16[512,512]{1,0:T(8,128)(2,1)}, u32[]{:S(2)}) copy-start(bf16[512,512]{1,0:T(8,128)(2,1)} %up_ref.1) | copy-start | bytes 1572868
  27.4 12.4 %copy-start.2 = (bf16[512,512]{1,0:T(8,128)(2,1)S(1)}, bf16[512,512]{1,0:T(8,128)(2,1)}, u32[]{:S(2)}) copy-start(bf16[512,512]{1,0:T(8,128)(2,1)} %down_ref.1) | copy-start | bytes 1572868
  27.5 12.4 %copy-start.3 = (bf16[256,512]{1,0:T(8,128)(2,1)S(1)}, bf16[256,512]{1,0:T(8,128)(2,1)}, u32[]{:S(2)}) copy-start(bf16[256,512]{1,0:T(8,128)(2,1)} %latent_ref.1) | copy-start | bytes 786436
  27.5 12.4 %copy-start.4 = (f32[512]{0:T(512)S(1)}, f32[512]{0:T(512)}, u32[]{:S(2)}) copy-start(f32[512]{0:T(512)} %param.21) | copy-start | bytes 6148
  27.5 6.2 %collective-permute-start.5 = (bf16[8,32,512]{2,1,0:T(8,128)(2,1)S(1)}, bf16[8,32,512]{2,1,0:T(8,128)(2,1)S(1)}, u32[]{:S(2)}, u32[]{:S(2)}) collective-permute-start(bf16[8,32,512]{2,1,0:T(8,128)(2,1)S(1)} %add_3.1.token), channel_id=1, source_target_pairs={{0,5},{1,2},{2,1},{3,6},{4,9},{5,0},{6,3},{7,10},{8,13},{9,4},{10,... | collective-permute-start | bytes 786440 | tf_op jit(solution)/shard_map/ppermute | solution.py:62
  30.4 6.7 %collective-permute-start.8 = (bf16[8,32,512]{2,1,0:T(8,128)(2,1)S(1)}, bf16[8,32,512]{2,1,0:T(8,128)(2,1)S(1)}, u32[]{:S(2)}, u32[]{:S(2)}) collective-permute-start(bf16[8,32,512]{2,1,0:T(8,128)(2,1)S(1)} %add_2.1.token), channel_id=1, source_target_pairs={{0,5},{1,2},{2,1},{3,6},{4,9},{5,0},{6,3},{7,10},{8,13},{9,4},{10,... | collective-permute-start | bytes 786440 | tf_op jit(solution)/shard_map/ppermute | solution.py:62
  33.8 6.1 %collective-permute-start.7 = (bf16[8,32,512]{2,1,0:T(8,128)(2,1)S(1)}, bf16[8,32,512]{2,1,0:T(8,128)(2,1)S(1)}, u32[]{:S(2)}, u32[]{:S(2)}) collective-permute-start(bf16[8,32,512]{2,1,0:T(8,128)(2,1)S(1)} %add_1.1), channel_id=1, source_target_pairs={{0,3},{1,4},{2,7},{3,0},{4,1},{5,8},{6,11},{7,2},{8,5},{9,12},{10,... | collective-permute-start | bytes 786440 | tf_op jit(solution)/shard_map/ppermute | solution.py:62
  41.3 7.4 %collective-permute-start.9 = (bf16[256,512]{1,0:T(8,128)(2,1)S(1)}, bf16[256,512]{1,0:T(8,128)(2,1)S(1)}, u32[]{:S(2)}, u32[]{:S(2)}) collective-permute-start(bf16[256,512]{1,0:T(8,128)(2,1)S(1)} %get-tuple-element.24.refs_1_.refs_0_), channel_id=1, source_target_pairs={{0,3},{1,4},{2,7},{3,0},{4,1},{5,8},{6,11},{7,2},{8,5},{9,12},{10,... | collective-permute-start | bytes 786440 | tf_op jit(solution)/shard_map/ppermute | solution.py:62
  43.1 8.1 %collective-permute-start.10 = (bf16[256,512]{1,0:T(8,128)(2,1)S(1)}, bf16[256,512]{1,0:T(8,128)(2,1)S(1)}, u32[]{:S(2)}, u32[]{:S(2)}) collective-permute-start(bf16[256,512]{1,0:T(8,128)(2,1)S(1)} %get-tuple-element.24.refs_1_.refs_0_), channel_id=1, source_target_pairs={{0,5},{1,2},{2,1},{3,6},{4,9},{5,0},{6,3},{7,10},{8,13},{9,4},{10,... | collective-permute-start | bytes 786440 | tf_op jit(solution)/shard_map/ppermute | solution.py:62
  48.8 8.2 %collective-permute-start.12 = (bf16[256,512]{1,0:T(8,128)(2,1)S(1)}, bf16[256,512]{1,0:T(8,128)(2,1)S(1)}, u32[]{:S(2)}, u32[]{:S(2)}) collective-permute-start(bf16[256,512]{1,0:T(8,128)(2,1)S(1)} %in_order.8.refs_1_), channel_id=1, source_target_pairs={{0,5},{1,2},{2,1},{3,6},{4,9},{5,0},{6,3},{7,10},{8,13},{9,4},{10,... | collective-permute-start | bytes 786440 | tf_op jit(solution)/shard_map/ppermute | solution.py:62
  51.2 7.7 %collective-permute-start.13 = (bf16[256,512]{1,0:T(8,128)(2,1)S(1)}, bf16[256,512]{1,0:T(8,128)(2,1)S(1)}, u32[]{:S(2)}, u32[]{:S(2)}) collective-permute-start(bf16[256,512]{1,0:T(8,128)(2,1)S(1)} %in_order.9.refs_2_), channel_id=1, source_target_pairs={{0,3},{1,4},{2,7},{3,0},{4,1},{5,8},{6,11},{7,2},{8,5},{9,12},{10,... | collective-permute-start | bytes 786440 | tf_op jit(solution)/shard_map/ppermute | solution.py:62
  57.0 8.0 %collective-permute-start.15 = (bf16[256,512]{1,0:T(8,128)(2,1)S(1)}, bf16[256,512]{1,0:T(8,128)(2,1)S(1)}, u32[]{:S(2)}, u32[]{:S(2)}) collective-permute-start(bf16[256,512]{1,0:T(8,128)(2,1)S(1)} %in_order.10.refs_1_.refs_0_), channel_id=1, source_target_pairs={{0,3},{1,4},{2,7},{3,0},{4,1},{5,8},{6,11},{7,2},{8,5},{9,12},{10,... | collective-permute-start | bytes 786440 | tf_op jit(solution)/shard_map/ppermute | solution.py:62
  58.9 8.3 %collective-permute-start.16 = (bf16[256,512]{1,0:T(8,128)(2,1)S(1)}, bf16[256,512]{1,0:T(8,128)(2,1)S(1)}, u32[]{:S(2)}, u32[]{:S(2)}) collective-permute-start(bf16[256,512]{1,0:T(8,128)(2,1)S(1)} %in_order.11.refs_1_), channel_id=1, source_target_pairs={{0,5},{1,2},{2,1},{3,6},{4,9},{5,0},{6,3},{7,10},{8,13},{9,4},{10,... | collective-permute-start | bytes 786440 | tf_op jit(solution)/shard_map/ppermute | solution.py:62
  64.9 5.9 %collective-permute-start.18 = (bf16[256,512]{1,0:T(8,128)(2,1)S(1)}, bf16[256,512]{1,0:T(8,128)(2,1)S(1)}, u32[]{:S(2)}, u32[]{:S(2)}) collective-permute-start(bf16[256,512]{1,0:T(8,128)(2,1)S(1)} %in_order.12.refs_1_.refs_0_), channel_id=1, source_target_pairs={{0,5},{1,2},{2,1},{3,6},{4,9},{5,0},{6,3},{7,10},{8,13},{9,4},{10,... | collective-permute-start | bytes 786440 | tf_op jit(solution)/shard_map/ppermute | solution.py:62
  66.7 4.1 %collective-permute-start.11 = (bf16[384,512]{1,0:T(8,128)(2,1)S(1)}, bf16[384,512]{1,0:T(8,128)(2,1)S(1)}, u32[]{:S(2)}, u32[]{:S(2)}) collective-permute-start(bf16[384,512]{1,0:T(8,128)(2,1)S(1)} %get-tuple-element.26), channel_id=1, source_target_pairs={{0,1},{1,0},{2,3},{3,2},{4,5},{5,4},{6,7},{7,6},{8,9},{9,8},{10,11... | collective-permute-start | bytes 1179656 | tf_op jit(solution)/shard_map/ppermute | solution.py:53
  66.7 4.1 %collective-permute-start.14 = (bf16[256,512]{1,0:T(8,128)(2,1)S(1)}, bf16[256,512]{1,0:T(8,128)(2,1)S(1)}, u32[]{:S(2)}, u32[]{:S(2)}) collective-permute-start(bf16[256,512]{1,0:T(8,128)(2,1)S(1)} %get-tuple-element.28), channel_id=1, source_target_pairs={{0,1},{1,0},{2,3},{3,2},{4,5},{5,4},{6,7},{7,6},{8,9},{9,8},{10,11... | collective-permute-start | bytes 786440 | tf_op jit(solution)/shard_map/ppermute | solution.py:53
  67.8 2.9 %collective-permute-start.17 = (bf16[256,512]{1,0:T(8,128)(2,1)S(1)}, bf16[256,512]{1,0:T(8,128)(2,1)S(1)}, u32[]{:S(2)}, u32[]{:S(2)}) collective-permute-start(bf16[256,512]{1,0:T(8,128)(2,1)S(1)} %get-tuple-element.30), channel_id=1, source_target_pairs={{0,1},{1,0},{2,3},{3,2},{4,5},{5,4},{6,7},{7,6},{8,9},{9,8},{10,11... | collective-permute-start | bytes 786440 | tf_op jit(solution)/shard_map/ppermute | solution.py:53
  70.8 1.5 %collective-permute-start.19 = (bf16[256,512]{1,0:T(8,128)(2,1)S(1)}, bf16[256,512]{1,0:T(8,128)(2,1)S(1)}, u32[]{:S(2)}, u32[]{:S(2)}) collective-permute-start(bf16[256,512]{1,0:T(8,128)(2,1)S(1)} %collective-permute-done.18.rest_6_), channel_id=1, source_target_pairs={{0,1},{1,0},{2,3},{3,2},{4,5},{5,4},{6,7},{7,6},{8,9},{9,8},{10,11... | collective-permute-start | bytes 786440 | tf_op jit(solution)/shard_map/ppermute | solution.py:53

commit v14 on v13

--- a/solution.py
+++ b/solution.py
@@ -124,11 +124,10 @@
                 place = (across * groups + group) * slots + slot
                 mask = mask_ref[k, me * blk_count + block]
                 table_ref[0, place] = tile
-                found = group * slots + jnp.where(group == groups - 1, tile, slot)
-                table_ref[2, block * list_len + k] = found + across * (
-                    (groups - 1) * slots + ring.tiles
-                )
-                table_ref[3, block * list_len + k] = mask
+                beyond = group == groups - 1
+                near = (across * (groups - 1) + group) * slots + slot
+                table_ref[2, block * list_len + k] = jnp.where(beyond, tile, near)
+                table_ref[3, block * list_len + k] = mask * jnp.where(beyond, 2 + across, 1)
                 across, group, tile, slot = spot(me ^ 1, block, k)
                 table_ref[1, (across * groups + group) * slots + slot] = tile
                 masked = part[k * tile_rows : (k + 1) * tile_rows] * mask.astype(F32)
@@ -167,7 +166,7 @@
 
 
 def mesh_kernel(
-    latent_ref, up_ref, down_ref, gain_ref, own, came, neighbour, out_ref, piece_ref
+    latent_ref, up_ref, down_ref, gain_ref, own, came, neighbour, out_ref, first_ref, second_ref
 ):
     total = own[0] + came[...].astype(F32) + neighbour[...].astype(F32)
     mesh_in = latent_ref[...].astype(F32) + total.reshape(latent_ref.shape)
@@ -175,7 +174,8 @@
     hidden = silu(jnp.dot(normed, up_ref[...], preferred_element_type=F32)).astype(BF16)
     out = (mesh_in + jnp.dot(hidden, down_ref[...], preferred_element_type=F32)).astype(BF16)
     out_ref[...] = out
-    piece_ref[...] = out
+    first_ref[...] = out
+    second_ref[...] = out
 
 
 def order_kernel(*refs):
@@ -199,36 +199,47 @@
         out_ref[b] = interp_ref[b].reshape(out_ref.shape[2], out_ref.shape[1]).T
 
 
-def back_kernel(starts, list_len, table_ref, weights_ref, latent_any, *rest):
-    count = len(starts)
-    pieces, (out_any, held, latent_ref, total, out_ref, sems) = rest[:count], rest[count:]
+def join_kernel(*refs):
+    pieces, out = refs[:-1], refs[-1]
+    start = 0
+    for piece in pieces:
+        out[start : start + piece.shape[0]] = piece[...]
+        start += piece.shape[0]
+
+
+def back_kernel(
+    list_len, table_ref, weights_ref, near_ref, mine_ref, theirs_ref, latent_any,
+    out_any, latent_ref, total, out_ref, sems,
+):
     blk_count, block_rows, listed = weights_ref.shape
     tile_rows = listed // list_len
-    copies = []
-
-    def copy(source, target):
-        copies.append(pltpu.make_async_copy(source, target, sems.at[len(copies)]))
-        return copies[-1]
-
-    pieces_in = []
-    for piece, start in zip(pieces, starts):
-        pieces_in.append(copy(piece, held.at[pl.ds(start, piece.shape[0])]))
     part_rows = BACK_PART * block_rows
     parts = [pl.ds(i * part_rows, part_rows) for i in range(blk_count // BACK_PART)]
-    latent_in = [copy(latent_any.at[rows], latent_ref.at[rows]) for rows in parts]
-    outs = [copy(out_ref.at[rows], out_any.at[rows]) for rows in parts]
-    for started in pieces_in + latent_in:
-        started.start()
-    for started in pieces_in:
-        started.wait()
+    latent_in, outs = [], []
+    for i, rows in enumerate(parts):
+        latent_in.append(
+            pltpu.make_async_copy(latent_any.at[rows], latent_ref.at[rows], sems.at[i])
+        )
+        outs.append(
+            pltpu.make_async_copy(out_ref.at[rows], out_any.at[rows], sems.at[len(parts) + i])
+        )
+    for copy in latent_in:
+        copy.start()
+
+    def rows_at(tile):
+        return pl.ds(pl.multiple_of(tile * tile_rows, tile_rows), tile_rows)
 
     for block in range(blk_count):
         values = []
         for k in range(list_len):
             entry = block * list_len + k
-            rows = pl.ds(pl.multiple_of(table_ref[2, entry] * tile_rows, tile_rows), tile_rows)
-            value = held[rows]
-            values.append(jnp.where(table_ref[3, entry] == 1, value, jnp.zeros_like(value)))
+            place, kind = table_ref[2, entry], table_ref[3, entry]
+            here = jnp.where(kind > 1, 0, place)
+            beyond = jnp.where(kind > 1, place, 0)
+            value = near_ref[rows_at(here)]
+            value = jnp.where(kind == 2, mine_ref[rows_at(beyond)], value)
+            value = jnp.where(kind == 3, theirs_ref[rows_at(beyond)], value)
+            values.append(jnp.where(kind > 0, value, jnp.zeros_like(value)))
         value = jnp.concatenate(values, axis=0)
         rows = slice(block * block_rows, (block + 1) * block_rows)
         total[rows] = jnp.dot(weights_ref[block], value, preferred_element_type=F32)
@@ -238,8 +249,8 @@
             out_ref[strip] = (latent_ref[strip].astype(F32) + total[strip]).astype(BF16)
         if block % BACK_PART == BACK_PART - 1:
             outs[block // BACK_PART].start()
-    for started in outs:
-        started.wait()
+    for copy in outs:
+        copy.wait()
 
 
 def whole(array):
@@ -402,26 +413,21 @@
             second = ring.over_second(token, distance)
 
     mesh_gain = mesh_gain.reshape(1, width)
-    mesh_out, piece = pl.pallas_call(
+    mesh_out, piece, again = pl.pallas_call(
         mesh_kernel,
-        out_shape=[shape((node_rows, width))] * 2,
+        out_shape=[shape((node_rows, width))] * 3,
         in_specs=[in_vmem] * 7,
-        out_specs=[in_vmem] * 2,
+        out_specs=[in_vmem] * 3,
         compiler_params=params(16),
         cost_estimate=cost(4 * node_rows * width * width, mesh_up, mesh_down),
         name="mesh_step",
     )(mesh_latent, mesh_up, mesh_down, mesh_gain, own, first, second)
 
-    pieces, starts = [], []
-
-    def share(index, mine, theirs):
-        for across, value in enumerate((mine, ring.over_core(theirs))):
-            pieces.append(value)
-            starts.append((across * ((chips - 1) * slots + tiles) + index) * tile_rows)
+    mine, theirs = [], []
 
     def pick(chosen, values):
         out = shape((len(chosen) * slots * tile_rows, width))
-        mine, theirs = pl.pallas_call(
+        picked = pl.pallas_call(
             functools.partial(pick_kernel, chosen, slots, chips, tile_rows),
             out_shape=[out] * 2,
             grid_spec=pltpu.PrefetchScalarGridSpec(
@@ -434,44 +440,53 @@
             cost_estimate=cost(0, *values),
             name=f"pick_{chosen[0]}",
         )(table, *values)
-        share(chosen[0] * slots, mine, theirs)
-        return mine
-
-    first, second = ring.over_first(piece, 1), ring.over_second(piece, 1)
-    token = piece
+        mine.append(picked[0])
+        theirs.append(ring.over_core(picked[1]))
+
+    first = ring.over_first(piece, 1)
+    pick([0], [piece])
+    second = ring.over_second(in_order(again, theirs[0]), 1)
+    token = mine[0]
     for distance in range(1, far):
         first = in_order(first, token)
         onward = ring.over_first(first, distance + 1)
         second = in_order(second, first)
         if distance < far - 1:
             after = ring.over_second(second, distance + 1)
-        chosen, values = [2 * distance - 1, 2 * distance], [first, second]
-        if distance == 1:
-            chosen, values = [0] + chosen, [piece] + values
-        token = pick(chosen, values)
+        pick([2 * distance - 1, 2 * distance], [first, second])
+        token = mine[-1]
         first, second = onward, after
-    share((chips - 1) * slots, first, first)
+    tiles_far = [first, ring.over_core(first)]
+    near = mine + theirs
+    joined = pl.pallas_call(
+        join_kernel,
+        out_shape=shape((sum(piece.shape[0] for piece in near), width)),
+        in_specs=[in_vmem] * len(near),
+        out_specs=in_vmem,
+        compiler_params=params(8),
+        cost_estimate=cost(0, *near),
+        name="join",
+    )(*near)
 
     grid_out = pl.pallas_call(
-        functools.partial(back_kernel, starts, list_len),
+        functools.partial(back_kernel, list_len),
         out_shape=shape((grid_rows, width)),
         grid_spec=pltpu.PrefetchScalarGridSpec(
             num_scalar_prefetch=1,
             grid=(1,),
-            in_specs=[in_vmem] + [in_any] * (1 + len(pieces)),
+            in_specs=[in_vmem] * 4 + [in_any],
             out_specs=in_any,
             scratch_shapes=[
-                pltpu.VMEM((N_CORE * ((chips - 1) * slots + tiles) * tile_rows, width), BF16),
                 pltpu.VMEM((grid_rows, width), BF16),
                 pltpu.VMEM((grid_rows, width), F32),
                 pltpu.VMEM((grid_rows, width), BF16),
-                pltpu.SemaphoreType.DMA((len(pieces) + 2 * (blk_count // BACK_PART),)),
+                pltpu.SemaphoreType.DMA((2 * (blk_count // BACK_PART),)),
             ],
         ),
         compiler_params=params(32),
         cost_estimate=cost(2 * grid_rows * width * list_len * tile_rows, latent, latent, interp),
         name="back",
-    )(table, weights, in_hbm(latent), *pieces)
+    )(table, weights, joined, *tiles_far, in_hbm(latent))
     return (grid_out, mesh_out)
 
 

time: 78.7 us -> 74.7 us (0.949)
  the two profiles are of different devices: /device:TPU:0 before, /device:TPU:29 now
where the time goes in v14:
time: 74.7 us; the launch traced here: 74.5 us
  waiting for transfers between devices  42 us (56%)
  Pallas kernels  22.3 us (30%)
  starting transfers between devices  9.28 us (12%)
  between operations  0.86 us (1%)
    ppermute x14, waiting for transfers between devices, over(): return lax.ppermute(value, 'band', pairs)  38.1 us
    pallas_call x1, Pallas kernels, on_device(): pl.pallas_call(functools.partial(embed_kernel, ring, per_step, slots), ou...  11 us
    ppermute x14, starting transfers between devices, over(): return lax.ppermute(value, 'band', pairs)  5.88 us
    pallas_call x1, Pallas kernels, on_device(): pl.pallas_call(functools.partial(back_kernel, list_len), out_shape=shape(...  4.56 us
    ppermute x7, waiting for transfers between devices, over_core(): return lax.ppermute(value, 'band', [(i, i ^ 1) for i in range(self.n_band)])  3.86 us
    ppermute x7, starting transfers between devices, over_core(): return lax.ppermute(value, 'band', [(i, i ^ 1) for i in range(self.n_band)])  3.4 us
    pallas_call x4, Pallas kernels, pick(): pl.pallas_call(functools.partial(pick_kernel, chosen, slots, chips, tile_...  2.4 us
  transfers between devices with their start and end apart: 21, of which 17 were waited for; matrix products, arithmetic and copies ran while one was open for 0% of the time, Pallas kernels for 6%

profile of v14, /device:TPU:29, one launch (start us, length us, event | category | flops | bytes accessed | tf_op | source)
XLA Modules:
  0.0 74.5 jit_solution(12668332600506740498)
XLA Ops:
  0.6 11.0 %embed.1 = (bf16[4096,512]{1,0:T(8,128)(2,1)}, bf16[33,32,512]{2,1,0:T(8,128)(2,1)S(1)}, bf16[9,32,512]{2,1,0:T(8,128)(2,1)S(1)}, bf16[25,32,512]{2,1,0:T(8,128)(2,1)S(1)}, s32[4,64]{1,0:T(4,128)S(1)}) custom-call(s32[1]{0:T(128)} %bitcast.me_ref, s32[4,256]{1,0:T(4,128)} %bitcast.8, s32[4,256]{1,0:T(4,128)} %bitcast.9, bf16[227,4096]{1,0:T(8,128)(2,1)} %bitcast.7, ...), custom_call_target="tpu_custom_call" | custom-call | flops 3636461568 | bytes 2908160 | tf_op jit(solution)/shard_map/embed/pallas_call | solution.py:309
  11.6 0.7 collective-permute-start
  12.3 1.2 %collective-permute-done.other = bf16[9,32,512]{2,1,0:T(8,128)(2,1)S(1)} collective-permute-done((bf16[9,32,512]{2,1,0:T(8,128)(2,1)S(1)}, bf16[9,32,512]{2,1,0:T(8,128)(2,1)S(1)}, u32[]{:S(2)}, u32[]{:S(2)}) %collective-permute-start) | collective-permute-done | bytes 294944 | tf_op jit(solution)/shard_map/ppermute | solution.py:53
  13.5 0.8 %far_sums.1 = (bf16[8,32,512]{2,1,0:T(8,128)(2,1)S(1)}, bf16[8,32,512]{2,1,0:T(8,128)(2,1)S(1)}) custom-call(s32[4,64]{1,0:T(4,128)S(1)} %get-tuple-element.20.table_ref, bf16[33,32,512]{2,1,0:T(8,128)(2,1)S(1)} %get-tuple-element.21.kept, bf16[9,32,512]{2,1,0:T(8,128)(2,1)S(1)} %collective-permute-done.other), custom_call_target="tpu_custom_call" | custom-call | bytes 1081344 | tf_op jit(solution)/shard_map/far_sums/pallas_call | solution.py:353
  15.0 1.5 %collective-permute-start.4 = (bf16[8,32,512]{2,1,0:T(8,128)(2,1)S(1)}, bf16[8,32,512]{2,1,0:T(8,128)(2,1)S(1)}, u32[]{:S(2)}, u32[]{:S(2)}) collective-permute-start(bf16[8,32,512]{2,1,0:T(8,128)(2,1)S(1)} %get-tuple-element.25), channel_id=1, source_target_pairs={{0,5},{1,2},{2,1},{3,6},{4,9},{5,0},{6,3},{7,10},{8,13},{9,4},{10,... | collective-permute-start | bytes 786440 | tf_op jit(solution)/shard_map/ppermute | solution.py:62
  16.7 1.2 %own_sums.1.token.own = f32[6,8,32,512]{3,2,1,0:T(8,128)S(1)} custom-call(s32[4,64]{1,0:T(4,128)S(1)} %get-tuple-element.20.table_ref, bf16[33,32,512]{2,1,0:T(8,128)(2,1)S(1)} %get-tuple-element.21.kept, bf16[25,32,512]{2,1,0:T(8,128)(2,1)S(1)} %collective-permute-done.1.other), custom_call_target="tpu_custom_call" | custom-call | bytes 4325376 | tf_op jit(solution)/shard_map/own_sums/pallas_call | solution.py:368
  17.9 0.5 turn.1.token.weights_ref
  18.5 2.4 %collective-permute-done.2.came = bf16[8,32,512]{2,1,0:T(8,128)(2,1)S(1)} collective-permute-done((bf16[8,32,512]{2,1,0:T(8,128)(2,1)S(1)}, bf16[8,32,512]{2,1,0:T(8,128)(2,1)S(1)}, u32[]{:S(2)}, u32[]{:S(2)}) %collective-permute-start.2) | collective-permute-done | bytes 262176 | tf_op jit(solution)/shard_map/ppermute | solution.py:62
  21.0 2.9 %collective-permute-done.4.came = bf16[8,32,512]{2,1,0:T(8,128)(2,1)S(1)} collective-permute-done((bf16[8,32,512]{2,1,0:T(8,128)(2,1)S(1)}, bf16[8,32,512]{2,1,0:T(8,128)(2,1)S(1)}, u32[]{:S(2)}, u32[]{:S(2)}) %collective-permute-start.4) | collective-permute-done | bytes 262176 | tf_op jit(solution)/shard_map/ppermute | solution.py:62
  24.0 3.1 %collective-permute-done.3.came = bf16[8,32,512]{2,1,0:T(8,128)(2,1)S(1)} collective-permute-done((bf16[8,32,512]{2,1,0:T(8,128)(2,1)S(1)}, bf16[8,32,512]{2,1,0:T(8,128)(2,1)S(1)}, u32[]{:S(2)}, u32[]{:S(2)}) %collective-permute-start.3) | collective-permute-done | bytes 262176 | tf_op jit(solution)/shard_map/ppermute | solution.py:62
  27.3 3.2 %collective-permute-done.6.came = bf16[8,32,512]{2,1,0:T(8,128)(2,1)S(1)} collective-permute-done((bf16[8,32,512]{2,1,0:T(8,128)(2,1)S(1)}, bf16[8,32,512]{2,1,0:T(8,128)(2,1)S(1)}, u32[]{:S(2)}, u32[]{:S(2)}) %collective-permute-start.6) | collective-permute-done | bytes 262176 | tf_op jit(solution)/shard_map/ppermute | solution.py:62
  30.6 2.8 %collective-permute-done.5.came = bf16[8,32,512]{2,1,0:T(8,128)(2,1)S(1)} collective-permute-done((bf16[8,32,512]{2,1,0:T(8,128)(2,1)S(1)}, bf16[8,32,512]{2,1,0:T(8,128)(2,1)S(1)}, u32[]{:S(2)}, u32[]{:S(2)}) %collective-permute-start.5) | collective-permute-done | bytes 262176 | tf_op jit(solution)/shard_map/ppermute | solution.py:62
  33.5 3.8 %collective-permute-done.8.neighbour = bf16[8,32,512]{2,1,0:T(8,128)(2,1)S(1)} collective-permute-done((bf16[8,32,512]{2,1,0:T(8,128)(2,1)S(1)}, bf16[8,32,512]{2,1,0:T(8,128)(2,1)S(1)}, u32[]{:S(2)}, u32[]{:S(2)}) %collective-permute-start.8) | collective-permute-done | bytes 262176 | tf_op jit(solution)/shard_map/ppermute | solution.py:62
  37.3 2.2 %collective-permute-done.7.came = bf16[8,32,512]{2,1,0:T(8,128)(2,1)S(1)} collective-permute-done((bf16[8,32,512]{2,1,0:T(8,128)(2,1)S(1)}, bf16[8,32,512]{2,1,0:T(8,128)(2,1)S(1)}, u32[]{:S(2)}, u32[]{:S(2)}) %collective-permute-start.7) | collective-permute-done | bytes 262176 | tf_op jit(solution)/shard_map/ppermute | solution.py:62
  39.5 1.5 %mesh_step.1 = (bf16[256,512]{1,0:T(8,128)(2,1)}, bf16[256,512]{1,0:T(8,128)(2,1)S(1)}, bf16[256,512]{1,0:T(8,128)(2,1)S(1)}) custom-call(bf16[256,512]{1,0:T(8,128)(2,1)S(1)} %copy-done.3, bf16[512,512]{1,0:T(8,128)(2,1)S(1)} %copy-done.1, bf16[512,512]{1,0:T(8,128)(2,1)S(1)} %copy-done.2, f32[1,512]{1,0:T(1,128)S(1)} %bitcast.6, ...), custom_call_target="tpu_custom_call" | custom-call | flops 268435456 | bytes 1048576 | tf_op jit(solution)/shard_map/mesh_step/pallas_call | solution.py:416
  41.2 0.6 pick_0.1
  42.2 1.0 %collective-permute-done.10.refs_1_.refs_4_ = bf16[128,512]{1,0:T(8,128)(2,1)S(1)} collective-permute-done((bf16[128,512]{1,0:T(8,128)(2,1)S(1)}, bf16[128,512]{1,0:T(8,128)(2,1)S(1)}, u32[]{:S(2)}, u32[]{:S(2)}) %collective-permute-start.10) | collective-permute-done | bytes 131104 | tf_op jit(solution)/shard_map/ppermute | solution.py:53
  43.2 1.6 %collective-permute-start.11 = (bf16[256,512]{1,0:T(8,128)(2,1)S(1)}, bf16[256,512]{1,0:T(8,128)(2,1)S(1)}, u32[]{:S(2)}, u32[]{:S(2)}) collective-permute-start(bf16[256,512]{1,0:T(8,128)(2,1)S(1)} %in_order.10), channel_id=1, source_target_pairs={{0,5},{1,2},{2,1},{3,6},{4,9},{5,0},{6,3},{7,10},{8,13},{9,4},{10,... | collective-permute-start | bytes 786440 | tf_op jit(solution)/shard_map/ppermute | solution.py:62
  44.7 3.2 %collective-permute-done.9.refs_0_ = bf16[256,512]{1,0:T(8,128)(2,1)S(1)} collective-permute-done((bf16[256,512]{1,0:T(8,128)(2,1)S(1)}, bf16[256,512]{1,0:T(8,128)(2,1)S(1)}, u32[]{:S(2)}, u32[]{:S(2)}) %collective-permute-start.9) | collective-permute-done | bytes 262176 | tf_op jit(solution)/shard_map/ppermute | solution.py:62
  47.9 1.6 %collective-permute-done.11.refs_0_ = bf16[256,512]{1,0:T(8,128)(2,1)S(1)} collective-permute-done((bf16[256,512]{1,0:T(8,128)(2,1)S(1)}, bf16[256,512]{1,0:T(8,128)(2,1)S(1)}, u32[]{:S(2)}, u32[]{:S(2)}) %collective-permute-start.11) | collective-permute-done | bytes 262176 | tf_op jit(solution)/shard_map/ppermute | solution.py:62
  49.6 0.9 %collective-permute-start.13 = (bf16[256,512]{1,0:T(8,128)(2,1)S(1)}, bf16[256,512]{1,0:T(8,128)(2,1)S(1)}, u32[]{:S(2)}, u32[]{:S(2)}) collective-permute-start(bf16[256,512]{1,0:T(8,128)(2,1)S(1)} %in_order.11.refs_1_), channel_id=1, source_target_pairs={{0,3},{1,4},{2,7},{3,0},{4,1},{5,8},{6,11},{7,2},{8,5},{9,12},{10,... | collective-permute-start | bytes 786440 | tf_op jit(solution)/shard_map/ppermute | solution.py:62
  50.5 0.6 pick_1.1
  51.1 4.0 %collective-permute-done.12.refs_0_ = bf16[256,512]{1,0:T(8,128)(2,1)S(1)} collective-permute-done((bf16[256,512]{1,0:T(8,128)(2,1)S(1)}, bf16[256,512]{1,0:T(8,128)(2,1)S(1)}, u32[]{:S(2)}, u32[]{:S(2)}) %collective-permute-start.12) | collective-permute-done | bytes 262176 | tf_op jit(solution)/shard_map/ppermute | solution.py:62
  55.7 1.0 %collective-permute-start.15 = (bf16[256,512]{1,0:T(8,128)(2,1)S(1)}, bf16[256,512]{1,0:T(8,128)(2,1)S(1)}, u32[]{:S(2)}, u32[]{:S(2)}) collective-permute-start(bf16[256,512]{1,0:T(8,128)(2,1)S(1)} %in_order.13.refs_1_), channel_id=1, source_target_pairs={{0,5},{1,2},{2,1},{3,6},{4,9},{5,0},{6,3},{7,10},{8,13},{9,4},{10,... | collective-permute-start | bytes 786440 | tf_op jit(solution)/shard_map/ppermute | solution.py:62
  56.7 0.6 pick_3.1
  57.3 5.3 %collective-permute-done.14.refs_0_ = bf16[256,512]{1,0:T(8,128)(2,1)S(1)} collective-permute-done((bf16[256,512]{1,0:T(8,128)(2,1)S(1)}, bf16[256,512]{1,0:T(8,128)(2,1)S(1)}, u32[]{:S(2)}, u32[]{:S(2)}) %collective-permute-start.14) | collective-permute-done | bytes 262176 | tf_op jit(solution)/shard_map/ppermute | solution.py:62
  62.6 0.5 collective-permute-start.17
  63.1 0.6 pick_5.1
  63.7 1.4 %collective-permute-start.18 = (bf16[256,512]{1,0:T(8,128)(2,1)S(1)}, bf16[256,512]{1,0:T(8,128)(2,1)S(1)}, u32[]{:S(2)}, u32[]{:S(2)}) collective-permute-start(bf16[256,512]{1,0:T(8,128)(2,1)S(1)} %get-tuple-element.35), channel_id=1, source_target_pairs={{0,1},{1,0},{2,3},{3,2},{4,5},{5,4},{6,7},{7,6},{8,9},{9,8},{10,11... | collective-permute-start | bytes 786440 | tf_op jit(solution)/shard_map/ppermute | solution.py:53
  65.1 3.3 %collective-permute-done.19.mine_ref = bf16[256,512]{1,0:T(8,128)(2,1)S(1)} collective-permute-done((bf16[256,512]{1,0:T(8,128)(2,1)S(1)}, bf16[256,512]{1,0:T(8,128)(2,1)S(1)}, u32[]{:S(2)}, u32[]{:S(2)}) %collective-permute-start.19) | collective-permute-done | bytes 262176 | tf_op jit(solution)/shard_map/ppermute | solution.py:62
  68.5 1.4 %collective-permute-done.20.theirs_ref = bf16[256,512]{1,0:T(8,128)(2,1)S(1)} collective-permute-done((bf16[256,512]{1,0:T(8,128)(2,1)S(1)}, bf16[256,512]{1,0:T(8,128)(2,1)S(1)}, u32[]{:S(2)}, u32[]{:S(2)}) %collective-permute-start.20) | collective-permute-done | bytes 262176 | tf_op jit(solution)/shard_map/ppermute | solution.py:53
  69.9 4.6 %back.1 = bf16[4096,512]{1,0:T(8,128)(2,1)} custom-call(s32[4,64]{1,0:T(4,128)S(1)} %get-tuple-element.20.table_ref, bf16[16,256,128]{2,1,0:T(8,128)(2,1)S(1)} %turn.1.token.weights_ref, bf16[1792,512]{1,0:T(8,128)(2,1)S(1)} %join.1.near_ref, bf16[256,512]{1,0:T(8,128)(2,1)S(1)} %collective-permute-done.19.mine_ref, ...), custom_call_target="tpu_custom_call" | custom-call | flops 536870912 | bytes 9437184 | tf_op jit(solution)/shard_map/back/pallas_call | solution.py:471
  (44 shorter events, 2.8 us)
Async XLA Ops:
  11.6 1.9 %collective-permute-start = (bf16[9,32,512]{2,1,0:T(8,128)(2,1)S(1)}, bf16[9,32,512]{2,1,0:T(8,128)(2,1)S(1)}, u32[]{:S(2)}, u32[]{:S(2)}) collective-permute-start(bf16[9,32,512]{2,1,0:T(8,128)(2,1)S(1)} %get-tuple-element.23), channel_id=1, source_target_pairs={{0,1},{1,0},{2,3},{3,2},{4,5},{5,4},{6,7},{7,6},{8,9},{9,8},{10,11... | collective-permute-start | bytes 884744 | tf_op jit(solution)/shard_map/ppermute | solution.py:53
  14.3 3.6 %copy-start = (bf16[16,4,32,256]{3,2,1,0:T(8,128)(2,1)S(1)}, bf16[16,4,32,256]{3,2,1,0:T(8,128)(2,1)}, u32[]{:S(2)}) copy-start(bf16[16,4,32,256]{3,2,1,0:T(8,128)(2,1)} %interp_ref.3) | copy-start | bytes 3145732
  14.3 2.4 %collective-permute-start.1 = (bf16[25,32,512]{2,1,0:T(8,128)(2,1)S(1)}, bf16[25,32,512]{2,1,0:T(8,128)(2,1)S(1)}, u32[]{:S(2)}, u32[]{:S(2)}) collective-permute-start(bf16[25,32,512]{2,1,0:T(8,128)(2,1)S(1)} %in_order.8), channel_id=1, source_target_pairs={{0,1},{1,0},{2,3},{3,2},{4,5},{5,4},{6,7},{7,6},{8,9},{9,8},{10,11... | collective-permute-start | bytes 2457608 | tf_op jit(solution)/shard_map/ppermute | solution.py:53
  14.8 6.1 %collective-permute-start.2 = (bf16[8,32,512]{2,1,0:T(8,128)(2,1)S(1)}, bf16[8,32,512]{2,1,0:T(8,128)(2,1)S(1)}, u32[]{:S(2)}, u32[]{:S(2)}) collective-permute-start(bf16[8,32,512]{2,1,0:T(8,128)(2,1)S(1)} %get-tuple-element.24.refs_1_), channel_id=1, source_target_pairs={{0,5},{1,2},{2,1},{3,6},{4,9},{5,0},{6,3},{7,10},{8,13},{9,4},{10,... | collective-permute-start | bytes 786440 | tf_op jit(solution)/shard_map/ppermute | solution.py:62
  15.0 8.8 %collective-permute-start.4 = (bf16[8,32,512]{2,1,0:T(8,128)(2,1)S(1)}, bf16[8,32,512]{2,1,0:T(8,128)(2,1)S(1)}, u32[]{:S(2)}, u32[]{:S(2)}) collective-permute-start(bf16[8,32,512]{2,1,0:T(8,128)(2,1)S(1)} %get-tuple-element.25), channel_id=1, source_target_pairs={{0,5},{1,2},{2,1},{3,6},{4,9},{5,0},{6,3},{7,10},{8,13},{9,4},{10,... | collective-permute-start | bytes 786440 | tf_op jit(solution)/shard_map/ppermute | solution.py:62
  20.9 6.2 %collective-permute-start.3 = (bf16[8,32,512]{2,1,0:T(8,128)(2,1)S(1)}, bf16[8,32,512]{2,1,0:T(8,128)(2,1)S(1)}, u32[]{:S(2)}, u32[]{:S(2)}) collective-permute-start(bf16[8,32,512]{2,1,0:T(8,128)(2,1)S(1)} %add_5.1.token), channel_id=1, source_target_pairs={{0,3},{1,4},{2,7},{3,0},{4,1},{5,8},{6,11},{7,2},{8,5},{9,12},{10,... | collective-permute-start | bytes 786440 | tf_op jit(solution)/shard_map/ppermute | solution.py:62
  23.9 6.5 %collective-permute-start.6 = (bf16[8,32,512]{2,1,0:T(8,128)(2,1)S(1)}, bf16[8,32,512]{2,1,0:T(8,128)(2,1)S(1)}, u32[]{:S(2)}, u32[]{:S(2)}) collective-permute-start(bf16[8,32,512]{2,1,0:T(8,128)(2,1)S(1)} %add_4.1.token), channel_id=1, source_target_pairs={{0,3},{1,4},{2,7},{3,0},{4,1},{5,8},{6,11},{7,2},{8,5},{9,12},{10,... | collective-permute-start | bytes 786440 | tf_op jit(solution)/shard_map/ppermute | solution.py:62
  27.1 12.3 %copy-start.1 = (bf16[512,512]{1,0:T(8,128)(2,1)S(1)}, bf16[512,512]{1,0:T(8,128)(2,1)}, u32[]{:S(2)}) copy-start(bf16[512,512]{1,0:T(8,128)(2,1)} %up_ref.1) | copy-start | bytes 1572868
  27.2 12.3 %copy-start.2 = (bf16[512,512]{1,0:T(8,128)(2,1)S(1)}, bf16[512,512]{1,0:T(8,128)(2,1)}, u32[]{:S(2)}) copy-start(bf16[512,512]{1,0:T(8,128)(2,1)} %down_ref.1) | copy-start | bytes 1572868
  27.2 12.3 %copy-start.3 = (bf16[256,512]{1,0:T(8,128)(2,1)S(1)}, bf16[256,512]{1,0:T(8,128)(2,1)}, u32[]{:S(2)}) copy-start(bf16[256,512]{1,0:T(8,128)(2,1)} %latent_ref.1) | copy-start | bytes 786436
  27.2 12.3 %copy-start.4 = (f32[512]{0:T(512)S(1)}, f32[512]{0:T(512)}, u32[]{:S(2)}) copy-start(f32[512]{0:T(512)} %param.21) | copy-start | bytes 6148
  27.2 6.2 %collective-permute-start.5 = (bf16[8,32,512]{2,1,0:T(8,128)(2,1)S(1)}, bf16[8,32,512]{2,1,0:T(8,128)(2,1)S(1)}, u32[]{:S(2)}, u32[]{:S(2)}) collective-permute-start(bf16[8,32,512]{2,1,0:T(8,128)(2,1)S(1)} %add_3.1.token), channel_id=1, source_target_pairs={{0,5},{1,2},{2,1},{3,6},{4,9},{5,0},{6,3},{7,10},{8,13},{9,4},{10,... | collective-permute-start | bytes 786440 | tf_op jit(solution)/shard_map/ppermute | solution.py:62
  30.5 6.7 %collective-permute-start.8 = (bf16[8,32,512]{2,1,0:T(8,128)(2,1)S(1)}, bf16[8,32,512]{2,1,0:T(8,128)(2,1)S(1)}, u32[]{:S(2)}, u32[]{:S(2)}) collective-permute-start(bf16[8,32,512]{2,1,0:T(8,128)(2,1)S(1)} %add_2.1.token), channel_id=1, source_target_pairs={{0,5},{1,2},{2,1},{3,6},{4,9},{5,0},{6,3},{7,10},{8,13},{9,4},{10,... | collective-permute-start | bytes 786440 | tf_op jit(solution)/shard_map/ppermute | solution.py:62
  33.4 6.1 %collective-permute-start.7 = (bf16[8,32,512]{2,1,0:T(8,128)(2,1)S(1)}, bf16[8,32,512]{2,1,0:T(8,128)(2,1)S(1)}, u32[]{:S(2)}, u32[]{:S(2)}) collective-permute-start(bf16[8,32,512]{2,1,0:T(8,128)(2,1)S(1)} %add_1.1), channel_id=1, source_target_pairs={{0,3},{1,4},{2,7},{3,0},{4,1},{5,8},{6,11},{7,2},{8,5},{9,12},{10,... | collective-permute-start | bytes 786440 | tf_op jit(solution)/shard_map/ppermute | solution.py:62
  41.0 7.0 %collective-permute-start.9 = (bf16[256,512]{1,0:T(8,128)(2,1)S(1)}, bf16[256,512]{1,0:T(8,128)(2,1)S(1)}, u32[]{:S(2)}, u32[]{:S(2)}) collective-permute-start(bf16[256,512]{1,0:T(8,128)(2,1)S(1)} %get-tuple-element.26.refs_0_), channel_id=1, source_target_pairs={{0,3},{1,4},{2,7},{3,0},{4,1},{5,8},{6,11},{7,2},{8,5},{9,12},{10,... | collective-permute-start | bytes 786440 | tf_op jit(solution)/shard_map/ppermute | solution.py:62
  41.8 1.4 %collective-permute-start.10 = (bf16[128,512]{1,0:T(8,128)(2,1)S(1)}, bf16[128,512]{1,0:T(8,128)(2,1)S(1)}, u32[]{:S(2)}, u32[]{:S(2)}) collective-permute-start(bf16[128,512]{1,0:T(8,128)(2,1)S(1)} %get-tuple-element.29), channel_id=1, source_target_pairs={{0,1},{1,0},{2,3},{3,2},{4,5},{5,4},{6,7},{7,6},{8,9},{9,8},{10,11... | collective-permute-start | bytes 393224 | tf_op jit(solution)/shard_map/ppermute | solution.py:53
  43.2 6.4 %collective-permute-start.11 = (bf16[256,512]{1,0:T(8,128)(2,1)S(1)}, bf16[256,512]{1,0:T(8,128)(2,1)S(1)}, u32[]{:S(2)}, u32[]{:S(2)}) collective-permute-start(bf16[256,512]{1,0:T(8,128)(2,1)S(1)} %in_order.10), channel_id=1, source_target_pairs={{0,5},{1,2},{2,1},{3,6},{4,9},{5,0},{6,3},{7,10},{8,13},{9,4},{10,... | collective-permute-start | bytes 786440 | tf_op jit(solution)/shard_map/ppermute | solution.py:62
  47.9 7.2 %collective-permute-start.12 = (bf16[256,512]{1,0:T(8,128)(2,1)S(1)}, bf16[256,512]{1,0:T(8,128)(2,1)S(1)}, u32[]{:S(2)}, u32[]{:S(2)}) collective-permute-start(bf16[256,512]{1,0:T(8,128)(2,1)S(1)} %in_order.9.refs_1_.refs_0_), channel_id=1, source_target_pairs={{0,5},{1,2},{2,1},{3,6},{4,9},{5,0},{6,3},{7,10},{8,13},{9,4},{10,... | collective-permute-start | bytes 786440 | tf_op jit(solution)/shard_map/ppermute | solution.py:62
  49.6 6.1 %collective-permute-start.13 = (bf16[256,512]{1,0:T(8,128)(2,1)S(1)}, bf16[256,512]{1,0:T(8,128)(2,1)S(1)}, u32[]{:S(2)}, u32[]{:S(2)}) collective-permute-start(bf16[256,512]{1,0:T(8,128)(2,1)S(1)} %in_order.11.refs_1_), channel_id=1, source_target_pairs={{0,3},{1,4},{2,7},{3,0},{4,1},{5,8},{6,11},{7,2},{8,5},{9,12},{10,... | collective-permute-start | bytes 786440 | tf_op jit(solution)/shard_map/ppermute | solution.py:62
  55.2 7.4 %collective-permute-start.14 = (bf16[256,512]{1,0:T(8,128)(2,1)S(1)}, bf16[256,512]{1,0:T(8,128)(2,1)S(1)}, u32[]{:S(2)}, u32[]{:S(2)}) collective-permute-start(bf16[256,512]{1,0:T(8,128)(2,1)S(1)} %in_order.12.refs_1_.refs_0_), channel_id=1, source_target_pairs={{0,3},{1,4},{2,7},{3,0},{4,1},{5,8},{6,11},{7,2},{8,5},{9,12},{10,... | collective-permute-start | bytes 786440 | tf_op jit(solution)/shard_map/ppermute | solution.py:62
  55.7 7.5 %collective-permute-start.15 = (bf16[256,512]{1,0:T(8,128)(2,1)S(1)}, bf16[256,512]{1,0:T(8,128)(2,1)S(1)}, u32[]{:S(2)}, u32[]{:S(2)}) collective-permute-start(bf16[256,512]{1,0:T(8,128)(2,1)S(1)} %in_order.13.refs_1_), channel_id=1, source_target_pairs={{0,5},{1,2},{2,1},{3,6},{4,9},{5,0},{6,3},{7,10},{8,13},{9,4},{10,... | collective-permute-start | bytes 786440 | tf_op jit(solution)/shard_map/ppermute | solution.py:62
  62.6 5.8 %collective-permute-start.19 = (bf16[256,512]{1,0:T(8,128)(2,1)S(1)}, bf16[256,512]{1,0:T(8,128)(2,1)S(1)}, u32[]{:S(2)}, u32[]{:S(2)}) collective-permute-start(bf16[256,512]{1,0:T(8,128)(2,1)S(1)} %in_order.14.refs_1_.refs_0_), channel_id=1, source_target_pairs={{0,5},{1,2},{2,1},{3,6},{4,9},{5,0},{6,3},{7,10},{8,13},{9,4},{10,... | collective-permute-start | bytes 786440 | tf_op jit(solution)/shard_map/ppermute | solution.py:62
  62.6 5.8 %collective-permute-start.16 = (bf16[256,512]{1,0:T(8,128)(2,1)S(1)}, bf16[256,512]{1,0:T(8,128)(2,1)S(1)}, u32[]{:S(2)}, u32[]{:S(2)}) collective-permute-start(bf16[256,512]{1,0:T(8,128)(2,1)S(1)} %get-tuple-element.33), channel_id=1, source_target_pairs={{0,1},{1,0},{2,3},{3,2},{4,5},{5,4},{6,7},{7,6},{8,9},{9,8},{10,11... | collective-permute-start | bytes 786440 | tf_op jit(solution)/shard_map/ppermute | solution.py:53
  62.6 5.8 %collective-permute-start.17 = (bf16[256,512]{1,0:T(8,128)(2,1)S(1)}, bf16[256,512]{1,0:T(8,128)(2,1)S(1)}, u32[]{:S(2)}, u32[]{:S(2)}) collective-permute-start(bf16[256,512]{1,0:T(8,128)(2,1)S(1)} %get-tuple-element.34), channel_id=1, source_target_pairs={{0,1},{1,0},{2,3},{3,2},{4,5},{5,4},{6,7},{7,6},{8,9},{9,8},{10,11... | collective-permute-start | bytes 786440 | tf_op jit(solution)/shard_map/ppermute | solution.py:53
  63.7 4.7 %collective-permute-start.18 = (bf16[256,512]{1,0:T(8,128)(2,1)S(1)}, bf16[256,512]{1,0:T(8,128)(2,1)S(1)}, u32[]{:S(2)}, u32[]{:S(2)}) collective-permute-start(bf16[256,512]{1,0:T(8,128)(2,1)S(1)} %get-tuple-element.35), channel_id=1, source_target_pairs={{0,1},{1,0},{2,3},{3,2},{4,5},{5,4},{6,7},{7,6},{8,9},{9,8},{10,11... | collective-permute-start | bytes 786440 | tf_op jit(solution)/shard_map/ppermute | solution.py:53
  68.4 1.5 %collective-permute-start.20 = (bf16[256,512]{1,0:T(8,128)(2,1)S(1)}, bf16[256,512]{1,0:T(8,128)(2,1)S(1)}, u32[]{:S(2)}, u32[]{:S(2)}) collective-permute-start(bf16[256,512]{1,0:T(8,128)(2,1)S(1)} %collective-permute-done.19.mine_ref), channel_id=1, source_target_pairs={{0,1},{1,0},{2,3},{3,2},{4,5},{5,4},{6,7},{7,6},{8,9},{9,8},{10,11... | collective-permute-start | bytes 786440 | tf_op jit(solution)/shard_map/ppermute | solution.py:53

commit v15 on v14

--- a/solution.py
+++ b/solution.py
@@ -12,7 +12,7 @@
 N_CORE = 2
 STRIP = 32
 PART = 2
-BACK_PART = 4
+BACK_PART = 2
 
 
 def silu(values):
@@ -87,7 +87,7 @@
 def embed_kernel(
     ring, per_step, slots, me_ref, lists_ref, mask_ref,
     x_ref, w1_ref, w2_ref, gain_ref, interp_ref,
-    latent_ref, kept_ref, far_ref, rest_ref, table_ref, wide, hidden,
+    latent_ref, near_ref, far_ref, table_ref, wide, hidden,
 ):
     step = pl.program_id(0)
     me = me_ref[0]
@@ -110,7 +110,7 @@
         for strip in strips(rows):
             hidden[strip] = silu(wide[strip]).astype(BF16)
         wide[rows] = jnp.dot(hidden[rows], w2_ref[...], preferred_element_type=F32)
-    kept_spare, far_spare, rest_spare = (ref.shape[0] - 1 for ref in (kept_ref, far_ref, rest_ref))
+    near_spare, far_spare = near_ref.shape[0] - 1, far_ref.shape[0] - 1
     for number, rows in enumerate(spans):
         for strip in strips(rows):
             latent_ref[strip] = layer_norm(wide[strip], gain_ref[...]).astype(BF16)
@@ -132,24 +132,22 @@
                 table_ref[1, (across * groups + group) * slots + slot] = tile
                 masked = part[k * tile_rows : (k + 1) * tile_rows] * mask.astype(F32)
                 masked = masked.astype(BF16)
-                kept_ref[jnp.minimum(place, kept_spare)] = masked
-                there = place - kept_spare
-                rest_ref[jnp.where(there < 0, rest_spare, jnp.minimum(there, rest_spare))] = masked
-                beyond = there - rest_spare
-                far_ref[jnp.where(beyond < 0, far_spare, beyond)] = masked
-
-
-def add_entries(total, table_ref, group, slots, kept, other, groups, first=0):
+                near_ref[jnp.minimum(place, near_spare)] = masked
+                far_ref[jnp.where(place < near_spare, far_spare, place - near_spare)] = masked
+
+
+def add_entries(total, table_ref, group, slots, kept, other, groups, first):
     for slot in range(slots):
         place = group * slots + slot
         total[table_ref[0, place]] += kept[place].astype(F32)
-        total[table_ref[1, groups * slots + place]] += other[place - first * slots].astype(F32)
-
-
-def far_kernel(slots, groups, table_ref, kept, other, far, before, total):
+        total[table_ref[1, groups * slots + place]] += other[place + first * slots].astype(F32)
+
+
+def far_kernel(slots, groups, table_ref, kept, other, far, before, same, total):
+    del same
     for group, out in ((groups - 1, far), (groups - 2, before)):
         total[...] = jnp.zeros_like(total)
-        add_entries(total, table_ref, group, slots, kept, other, groups, groups - 2)
+        add_entries(total, table_ref, group, slots, kept, other, groups, 2 - groups)
         out[...] = total[...].astype(BF16)
 
 
@@ -157,7 +155,7 @@
     group = pl.program_id(0)
     total = own.at[group]
     total[...] = jnp.zeros_like(total)
-    add_entries(total, table_ref, group, slots, kept, other, groups)
+    add_entries(total, table_ref, group, slots, kept, other, groups, groups)
 
 
 def add_kernel(group, own, came, token, out):
@@ -305,8 +303,8 @@
     grid_rows = blk_count * block_rows
     per_step = 4
     rows = per_step * block_rows
-    counts = (chips * slots, 2 * slots, (chips - 2) * slots)
-    latent, kept, sent_far, sent_rest, table = pl.pallas_call(
+    counts = ((2 * chips - 2) * slots, 2 * slots)
+    latent, near, sent_far, table = pl.pallas_call(
         functools.partial(embed_kernel, ring, per_step, slots),
         out_shape=[pltpu.HBM((blk_count * block_rows, width), BF16)]
         + [shape((count + 1, tile_rows, width)) for count in counts]
@@ -350,21 +348,22 @@
             name="in_order",
         )(value, token)
 
-    first, second = pl.pallas_call(
+    first, second, near = pl.pallas_call(
         functools.partial(far_kernel, slots, chips),
-        out_shape=[shape(dense)] * 2,
+        out_shape=[shape(dense)] * 2 + [shape(near.shape)],
         grid_spec=pltpu.PrefetchScalarGridSpec(
             num_scalar_prefetch=1,
             grid=(1,),
             in_specs=[in_vmem] * 2,
-            out_specs=[in_vmem] * 2,
+            out_specs=[in_vmem] * 3,
             scratch_shapes=[pltpu.VMEM(dense, F32)],
         ),
+        input_output_aliases={1: 2},
         compiler_params=params(8),
-        cost_estimate=cost(0, kept),
+        cost_estimate=cost(0, near),
         name="far_sums",
-    )(table, kept, other_far)
-    other_rest = ring.over_core(in_order(sent_rest, first))
+    )(table, near, other_far)
+    other = ring.over_core(near)
     own = pl.pallas_call(
         functools.partial(own_kernel, slots, chips),
         out_shape=shape((chips - 2,) + dense, F32),
@@ -375,9 +374,9 @@
             out_specs=in_vmem,
         ),
         compiler_params=params(8 if n_band <= 16 else 24),
-        cost_estimate=cost(0, kept, kept, kept, kept),
+        cost_estimate=cost(0, near, near),
         name="own_sums",
-    )(table, kept, other_rest)
+    )(table, near, other)
 
     def add_own(group, value, token):
         return pl.pallas_call(
@@ -457,16 +456,16 @@
         token = mine[-1]
         first, second = onward, after
     tiles_far = [first, ring.over_core(first)]
-    near = mine + theirs
+    parts = mine + theirs
     joined = pl.pallas_call(
         join_kernel,
-        out_shape=shape((sum(piece.shape[0] for piece in near), width)),
-        in_specs=[in_vmem] * len(near),
+        out_shape=shape((sum(part.shape[0] for part in parts), width)),
+        in_specs=[in_vmem] * len(parts),
         out_specs=in_vmem,
         compiler_params=params(8),
-        cost_estimate=cost(0, *near),
+        cost_estimate=cost(0, *parts),
         name="join",
-    )(*near)
+    )(*parts)
 
     grid_out = pl.pallas_call(
         functools.partial(back_kernel, list_len),

time: 74.7 us -> 74.7 us (level)
  the two profiles are of different devices: /device:TPU:29 before, /device:TPU:0 now
where the time goes in v15:
time: 74.7 us; the launch traced here: 73.2 us
  starting transfers between devices  29 us (39%)
  Pallas kernels  22.5 us (30%)
  waiting for transfers between devices  20.9 us (28%)
  between operations  0.79 us (1%)
    ppermute x14, starting transfers between devices, over(): return lax.ppermute(value, 'band', pairs)  26 us
    ppermute x14, waiting for transfers between devices, over(): return lax.ppermute(value, 'band', pairs)  17 us
    pallas_call x1, Pallas kernels, on_device(): pl.pallas_call(functools.partial(embed_kernel, ring, per_step, slots), ou...  10.8 us
    pallas_call x1, Pallas kernels, on_device(): pl.pallas_call(functools.partial(back_kernel, list_len), out_shape=shape(...  4.86 us
    ppermute x7, waiting for transfers between devices, over_core(): return lax.ppermute(value, 'band', [(i, i ^ 1) for i in range(self.n_band)])  3.96 us
    ppermute x7, starting transfers between devices, over_core(): return lax.ppermute(value, 'band', [(i, i ^ 1) for i in range(self.n_band)])  2.98 us
    pallas_call x4, Pallas kernels, pick(): pl.pallas_call(functools.partial(pick_kernel, chosen, slots, chips, tile_...  2.4 us
  transfers between devices with their start and end apart: 21, of which 18 were waited for; matrix products, arithmetic and copies ran while one was open for 0% of the time, Pallas kernels for 6%

profile of v15, /device:TPU:0, one launch (start us, length us, event | category | flops | bytes accessed | tf_op | source)
XLA Modules:
  0.0 73.2 jit_solution(1668230424391021586)
XLA Ops:
  0.6 10.8 %embed.1 = (bf16[4096,512]{1,0:T(8,128)(2,1)}, bf16[57,32,512]{2,1,0:T(8,128)(2,1)S(1)}, bf16[9,32,512]{2,1,0:T(8,128)(2,1)S(1)}, s32[4,64]{1,0:T(4,128)S(1)}) custom-call(s32[1]{0:T(128)} %bitcast.me_ref, s32[4,256]{1,0:T(4,128)} %bitcast.8, s32[4,256]{1,0:T(4,128)} %bitcast.9, bf16[227,4096]{1,0:T(8,128)(2,1)} %bitcast.7, bf16[227,512]{1,0:T(8,128)(2,1)} %w1_ref.1, ...), custom_call_target="tpu_custom_call" | custom-call | flops 3636461568 | bytes 2908160 | tf_op jit(solution)/shard_map/embed/pallas_call | solution.py:307
  11.9 1.2 %collective-permute-done.other = bf16[9,32,512]{2,1,0:T(8,128)(2,1)S(1)} collective-permute-done((bf16[9,32,512]{2,1,0:T(8,128)(2,1)S(1)}, bf16[9,32,512]{2,1,0:T(8,128)(2,1)S(1)}, u32[]{:S(2)}, u32[]{:S(2)}) %collective-permute-start) | collective-permute-done | bytes 294944 | tf_op jit(solution)/shard_map/ppermute | solution.py:53
  13.1 0.8 %far_sums.1 = (bf16[8,32,512]{2,1,0:T(8,128)(2,1)S(1)}, bf16[8,32,512]{2,1,0:T(8,128)(2,1)S(1)}, bf16[57,32,512]{2,1,0:T(8,128)(2,1)S(1)}) custom-call(s32[4,64]{1,0:T(4,128)S(1)} %get-tuple-element.20.table_ref, bf16[57,32,512]{2,1,0:T(8,128)(2,1)S(1)} %get-tuple-element.21.kept, ...), custom_call_target="tpu_custom_call", output_to_operand_aliasing={{2}: (1, {})} | custom-call | bytes 1867776 | tf_op jit(solution)/shard_map/far_sums/pallas_call | solution.py:351
  14.4 2.7 %collective-permute-start.2 = (bf16[8,32,512]{2,1,0:T(8,128)(2,1)S(1)}, bf16[8,32,512]{2,1,0:T(8,128)(2,1)S(1)}, u32[]{:S(2)}, u32[]{:S(2)}) collective-permute-start(bf16[8,32,512]{2,1,0:T(8,128)(2,1)S(1)} %get-tuple-element.24), channel_id=1, source_target_pairs={{0,5},{1,2},{2,1},{3,6},{4,9},{5,0},{6,3},{7,10},{8,13},{9,4},{10,... | collective-permute-start | bytes 786440 | tf_op jit(solution)/shard_map/ppermute | solution.py:62
  17.8 1.2 %own_sums.1.token.own = f32[6,8,32,512]{3,2,1,0:T(8,128)S(1)} custom-call(s32[4,64]{1,0:T(4,128)S(1)} %get-tuple-element.20.table_ref, bf16[57,32,512]{2,1,0:T(8,128)(2,1)S(1)} %get-tuple-element.23.kept, bf16[57,32,512]{2,1,0:T(8,128)(2,1)S(1)} %collective-permute-done.1.other), custom_call_target="tpu_custom_call" | custom-call | bytes 3735552 | tf_op jit(solution)/shard_map/own_sums/pallas_call | solution.py:367
  19.6 1.6 %collective-permute-done.2.came = bf16[8,32,512]{2,1,0:T(8,128)(2,1)S(1)} collective-permute-done((bf16[8,32,512]{2,1,0:T(8,128)(2,1)S(1)}, bf16[8,32,512]{2,1,0:T(8,128)(2,1)S(1)}, u32[]{:S(2)}, u32[]{:S(2)}) %collective-permute-start.2) | collective-permute-done | bytes 262176 | tf_op jit(solution)/shard_map/ppermute | solution.py:62
  21.2 2.0 %collective-permute-start.3 = (bf16[8,32,512]{2,1,0:T(8,128)(2,1)S(1)}, bf16[8,32,512]{2,1,0:T(8,128)(2,1)S(1)}, u32[]{:S(2)}, u32[]{:S(2)}) collective-permute-start(bf16[8,32,512]{2,1,0:T(8,128)(2,1)S(1)} %add_5.1.token), channel_id=1, source_target_pairs={{0,3},{1,4},{2,7},{3,0},{4,1},{5,8},{6,11},{7,2},{8,5},{9,12},{10,... | collective-permute-start | bytes 786440 | tf_op jit(solution)/shard_map/ppermute | solution.py:62
  23.2 0.7 %collective-permute-done.4.came = bf16[8,32,512]{2,1,0:T(8,128)(2,1)S(1)} collective-permute-done((bf16[8,32,512]{2,1,0:T(8,128)(2,1)S(1)}, bf16[8,32,512]{2,1,0:T(8,128)(2,1)S(1)}, u32[]{:S(2)}, u32[]{:S(2)}) %collective-permute-start.4) | collective-permute-done | bytes 262176 | tf_op jit(solution)/shard_map/ppermute | solution.py:62
  24.0 2.1 %collective-permute-start.6 = (bf16[8,32,512]{2,1,0:T(8,128)(2,1)S(1)}, bf16[8,32,512]{2,1,0:T(8,128)(2,1)S(1)}, u32[]{:S(2)}, u32[]{:S(2)}) collective-permute-start(bf16[8,32,512]{2,1,0:T(8,128)(2,1)S(1)} %add_4.1.token), channel_id=1, source_target_pairs={{0,3},{1,4},{2,7},{3,0},{4,1},{5,8},{6,11},{7,2},{8,5},{9,12},{10,... | collective-permute-start | bytes 786440 | tf_op jit(solution)/shard_map/ppermute | solution.py:62
  26.1 1.2 %collective-permute-done.3.came = bf16[8,32,512]{2,1,0:T(8,128)(2,1)S(1)} collective-permute-done((bf16[8,32,512]{2,1,0:T(8,128)(2,1)S(1)}, bf16[8,32,512]{2,1,0:T(8,128)(2,1)S(1)}, u32[]{:S(2)}, u32[]{:S(2)}) %collective-permute-start.3) | collective-permute-done | bytes 262176 | tf_op jit(solution)/shard_map/ppermute | solution.py:62
  27.3 2.2 %collective-permute-start.5 = (bf16[8,32,512]{2,1,0:T(8,128)(2,1)S(1)}, bf16[8,32,512]{2,1,0:T(8,128)(2,1)S(1)}, u32[]{:S(2)}, u32[]{:S(2)}) collective-permute-start(bf16[8,32,512]{2,1,0:T(8,128)(2,1)S(1)} %add_3.1.token), channel_id=1, source_target_pairs={{0,5},{1,2},{2,1},{3,6},{4,9},{5,0},{6,3},{7,10},{8,13},{9,4},{10,... | collective-permute-start | bytes 786440 | tf_op jit(solution)/shard_map/ppermute | solution.py:62
  29.5 0.8 %collective-permute-done.6.came = bf16[8,32,512]{2,1,0:T(8,128)(2,1)S(1)} collective-permute-done((bf16[8,32,512]{2,1,0:T(8,128)(2,1)S(1)}, bf16[8,32,512]{2,1,0:T(8,128)(2,1)S(1)}, u32[]{:S(2)}, u32[]{:S(2)}) %collective-permute-start.6) | collective-permute-done | bytes 262176 | tf_op jit(solution)/shard_map/ppermute | solution.py:62
  30.4 2.4 %collective-permute-start.8 = (bf16[8,32,512]{2,1,0:T(8,128)(2,1)S(1)}, bf16[8,32,512]{2,1,0:T(8,128)(2,1)S(1)}, u32[]{:S(2)}, u32[]{:S(2)}) collective-permute-start(bf16[8,32,512]{2,1,0:T(8,128)(2,1)S(1)} %add_2.1.token), channel_id=1, source_target_pairs={{0,5},{1,2},{2,1},{3,6},{4,9},{5,0},{6,3},{7,10},{8,13},{9,4},{10,... | collective-permute-start | bytes 786440 | tf_op jit(solution)/shard_map/ppermute | solution.py:62
  32.8 0.7 %collective-permute-done.5.came = bf16[8,32,512]{2,1,0:T(8,128)(2,1)S(1)} collective-permute-done((bf16[8,32,512]{2,1,0:T(8,128)(2,1)S(1)}, bf16[8,32,512]{2,1,0:T(8,128)(2,1)S(1)}, u32[]{:S(2)}, u32[]{:S(2)}) %collective-permute-start.5) | collective-permute-done | bytes 262176 | tf_op jit(solution)/shard_map/ppermute | solution.py:62
  33.6 2.0 %collective-permute-start.7 = (bf16[8,32,512]{2,1,0:T(8,128)(2,1)S(1)}, bf16[8,32,512]{2,1,0:T(8,128)(2,1)S(1)}, u32[]{:S(2)}, u32[]{:S(2)}) collective-permute-start(bf16[8,32,512]{2,1,0:T(8,128)(2,1)S(1)} %add_1.1), channel_id=1, source_target_pairs={{0,3},{1,4},{2,7},{3,0},{4,1},{5,8},{6,11},{7,2},{8,5},{9,12},{10,... | collective-permute-start | bytes 786440 | tf_op jit(solution)/shard_map/ppermute | solution.py:62
  35.6 1.6 %collective-permute-done.8.neighbour = bf16[8,32,512]{2,1,0:T(8,128)(2,1)S(1)} collective-permute-done((bf16[8,32,512]{2,1,0:T(8,128)(2,1)S(1)}, bf16[8,32,512]{2,1,0:T(8,128)(2,1)S(1)}, u32[]{:S(2)}, u32[]{:S(2)}) %collective-permute-start.8) | collective-permute-done | bytes 262176 | tf_op jit(solution)/shard_map/ppermute | solution.py:62
  37.2 2.5 %collective-permute-done.7.came = bf16[8,32,512]{2,1,0:T(8,128)(2,1)S(1)} collective-permute-done((bf16[8,32,512]{2,1,0:T(8,128)(2,1)S(1)}, bf16[8,32,512]{2,1,0:T(8,128)(2,1)S(1)}, u32[]{:S(2)}, u32[]{:S(2)}) %collective-permute-start.7) | collective-permute-done | bytes 262176 | tf_op jit(solution)/shard_map/ppermute | solution.py:62
  39.7 1.5 %mesh_step.1 = (bf16[256,512]{1,0:T(8,128)(2,1)}, bf16[256,512]{1,0:T(8,128)(2,1)S(1)}, bf16[256,512]{1,0:T(8,128)(2,1)S(1)}) custom-call(bf16[256,512]{1,0:T(8,128)(2,1)S(1)} %copy-done.3, bf16[512,512]{1,0:T(8,128)(2,1)S(1)} %copy-done.1, bf16[512,512]{1,0:T(8,128)(2,1)S(1)} %copy-done.2, f32[1,512]{1,0:T(1,128)S(1)} %bitcast.6, ...), custom_call_target="tpu_custom_call" | custom-call | flops 268435456 | bytes 1048576 | tf_op jit(solution)/shard_map/mesh_step/pallas_call | solution.py:415
  41.2 1.9 %collective-permute-start.9 = (bf16[256,512]{1,0:T(8,128)(2,1)S(1)}, bf16[256,512]{1,0:T(8,128)(2,1)S(1)}, u32[]{:S(2)}, u32[]{:S(2)}) collective-permute-start(bf16[256,512]{1,0:T(8,128)(2,1)S(1)} %get-tuple-element.26.refs_0_), channel_id=1, source_target_pairs={{0,3},{1,4},{2,7},{3,0},{4,1},{5,8},{6,11},{7,2},{8,5},{9,12},{10,... | collective-permute-start | bytes 786440 | tf_op jit(solution)/shard_map/ppermute | solution.py:62
  44.2 1.0 %collective-permute-done.10.refs_1_.refs_4_ = bf16[128,512]{1,0:T(8,128)(2,1)S(1)} collective-permute-done((bf16[128,512]{1,0:T(8,128)(2,1)S(1)}, bf16[128,512]{1,0:T(8,128)(2,1)S(1)}, u32[]{:S(2)}, u32[]{:S(2)}) %collective-permute-start.10) | collective-permute-done | bytes 131104 | tf_op jit(solution)/shard_map/ppermute | solution.py:53
  45.2 1.5 %collective-permute-start.11 = (bf16[256,512]{1,0:T(8,128)(2,1)S(1)}, bf16[256,512]{1,0:T(8,128)(2,1)S(1)}, u32[]{:S(2)}, u32[]{:S(2)}) collective-permute-start(bf16[256,512]{1,0:T(8,128)(2,1)S(1)} %in_order.8), channel_id=1, source_target_pairs={{0,5},{1,2},{2,1},{3,6},{4,9},{5,0},{6,3},{7,10},{8,13},{9,4},{10,... | collective-permute-start | bytes 786440 | tf_op jit(solution)/shard_map/ppermute | solution.py:62
  47.1 1.9 %collective-permute-start.12 = (bf16[256,512]{1,0:T(8,128)(2,1)S(1)}, bf16[256,512]{1,0:T(8,128)(2,1)S(1)}, u32[]{:S(2)}, u32[]{:S(2)}) collective-permute-start(bf16[256,512]{1,0:T(8,128)(2,1)S(1)} %in_order.7.refs_1_.refs_0_), channel_id=1, source_target_pairs={{0,5},{1,2},{2,1},{3,6},{4,9},{5,0},{6,3},{7,10},{8,13},{9,4},{10,... | collective-permute-start | bytes 786440 | tf_op jit(solution)/shard_map/ppermute | solution.py:62
  49.0 2.0 %collective-permute-done.11.refs_0_ = bf16[256,512]{1,0:T(8,128)(2,1)S(1)} collective-permute-done((bf16[256,512]{1,0:T(8,128)(2,1)S(1)}, bf16[256,512]{1,0:T(8,128)(2,1)S(1)}, u32[]{:S(2)}, u32[]{:S(2)}) %collective-permute-start.11) | collective-permute-done | bytes 262176 | tf_op jit(solution)/shard_map/ppermute | solution.py:62
  51.0 1.5 %collective-permute-start.13 = (bf16[256,512]{1,0:T(8,128)(2,1)S(1)}, bf16[256,512]{1,0:T(8,128)(2,1)S(1)}, u32[]{:S(2)}, u32[]{:S(2)}) collective-permute-start(bf16[256,512]{1,0:T(8,128)(2,1)S(1)} %in_order.9.refs_1_), channel_id=1, source_target_pairs={{0,3},{1,4},{2,7},{3,0},{4,1},{5,8},{6,11},{7,2},{8,5},{9,12},{10,... | collective-permute-start | bytes 786440 | tf_op jit(solution)/shard_map/ppermute | solution.py:62
  53.1 0.7 %collective-permute-done.12.refs_0_ = bf16[256,512]{1,0:T(8,128)(2,1)S(1)} collective-permute-done((bf16[256,512]{1,0:T(8,128)(2,1)S(1)}, bf16[256,512]{1,0:T(8,128)(2,1)S(1)}, u32[]{:S(2)}, u32[]{:S(2)}) %collective-permute-start.12) | collective-permute-done | bytes 262176 | tf_op jit(solution)/shard_map/ppermute | solution.py:62
  53.8 1.5 %collective-permute-start.14 = (bf16[256,512]{1,0:T(8,128)(2,1)S(1)}, bf16[256,512]{1,0:T(8,128)(2,1)S(1)}, u32[]{:S(2)}, u32[]{:S(2)}) collective-permute-start(bf16[256,512]{1,0:T(8,128)(2,1)S(1)} %in_order.10.refs_1_.refs_0_), channel_id=1, source_target_pairs={{0,3},{1,4},{2,7},{3,0},{4,1},{5,8},{6,11},{7,2},{8,5},{9,12},{10,... | collective-permute-start | bytes 786440 | tf_op jit(solution)/shard_map/ppermute | solution.py:62
  55.4 1.8 %collective-permute-done.13.refs_0_ = bf16[256,512]{1,0:T(8,128)(2,1)S(1)} collective-permute-done((bf16[256,512]{1,0:T(8,128)(2,1)S(1)}, bf16[256,512]{1,0:T(8,128)(2,1)S(1)}, u32[]{:S(2)}, u32[]{:S(2)}) %collective-permute-start.13) | collective-permute-done | bytes 262176 | tf_op jit(solution)/shard_map/ppermute | solution.py:62
  57.2 1.8 %collective-permute-start.15 = (bf16[256,512]{1,0:T(8,128)(2,1)S(1)}, bf16[256,512]{1,0:T(8,128)(2,1)S(1)}, u32[]{:S(2)}, u32[]{:S(2)}) collective-permute-start(bf16[256,512]{1,0:T(8,128)(2,1)S(1)} %in_order.11.refs_1_), channel_id=1, source_target_pairs={{0,5},{1,2},{2,1},{3,6},{4,9},{5,0},{6,3},{7,10},{8,13},{9,4},{10,... | collective-permute-start | bytes 786440 | tf_op jit(solution)/shard_map/ppermute | solution.py:62
  60.0 2.5 %collective-permute-start.19 = (bf16[256,512]{1,0:T(8,128)(2,1)S(1)}, bf16[256,512]{1,0:T(8,128)(2,1)S(1)}, u32[]{:S(2)}, u32[]{:S(2)}) collective-permute-start(bf16[256,512]{1,0:T(8,128)(2,1)S(1)} %in_order.12.refs_1_.refs_0_), channel_id=1, source_target_pairs={{0,5},{1,2},{2,1},{3,6},{4,9},{5,0},{6,3},{7,10},{8,13},{9,4},{10,... | collective-permute-start | bytes 786440 | tf_op jit(solution)/shard_map/ppermute | solution.py:62
  64.5 2.0 %collective-permute-done.19.mine_ref = bf16[256,512]{1,0:T(8,128)(2,1)S(1)} collective-permute-done((bf16[256,512]{1,0:T(8,128)(2,1)S(1)}, bf16[256,512]{1,0:T(8,128)(2,1)S(1)}, u32[]{:S(2)}, u32[]{:S(2)}) %collective-permute-start.19) | collective-permute-done | bytes 262176 | tf_op jit(solution)/shard_map/ppermute | solution.py:62
  67.3 1.0 %collective-permute-done.20.theirs_ref = bf16[256,512]{1,0:T(8,128)(2,1)S(1)} collective-permute-done((bf16[256,512]{1,0:T(8,128)(2,1)S(1)}, bf16[256,512]{1,0:T(8,128)(2,1)S(1)}, u32[]{:S(2)}, u32[]{:S(2)}) %collective-permute-start.20) | collective-permute-done | bytes 262176 | tf_op jit(solution)/shard_map/ppermute | solution.py:53
  68.3 4.9 %back.1 = bf16[4096,512]{1,0:T(8,128)(2,1)} custom-call(s32[4,64]{1,0:T(4,128)S(1)} %get-tuple-element.20.table_ref, bf16[16,256,128]{2,1,0:T(8,128)(2,1)S(1)} %turn.1.token.weights_ref, bf16[1792,512]{1,0:T(8,128)(2,1)S(1)} %join.1.near_ref, bf16[256,512]{1,0:T(8,128)(2,1)S(1)} %collective-permute-done.19.mine_ref, ...), custom_call_target="tpu_custom_call" | custom-call | flops 536870912 | bytes 9437184 | tf_op jit(solution)/shard_map/back/pallas_call | solution.py:470
  (43 shorter events, 8.4 us)
Async XLA Ops:
  11.5 1.7 %collective-permute-start = (bf16[9,32,512]{2,1,0:T(8,128)(2,1)S(1)}, bf16[9,32,512]{2,1,0:T(8,128)(2,1)S(1)}, u32[]{:S(2)}, u32[]{:S(2)}) collective-permute-start(bf16[9,32,512]{2,1,0:T(8,128)(2,1)S(1)} %get-tuple-element.22), channel_id=1, source_target_pairs={{0,1},{1,0},{2,3},{3,2},{4,5},{5,4},{6,7},{7,6},{8,9},{9,8},{10,11... | collective-permute-start | bytes 884744 | tf_op jit(solution)/shard_map/ppermute | solution.py:53
  13.9 3.9 %collective-permute-start.1 = (bf16[57,32,512]{2,1,0:T(8,128)(2,1)S(1)}, bf16[57,32,512]{2,1,0:T(8,128)(2,1)S(1)}, u32[]{:S(2)}, u32[]{:S(2)}) collective-permute-start(bf16[57,32,512]{2,1,0:T(8,128)(2,1)S(1)} %get-tuple-element.23.kept), channel_id=1, source_target_pairs={{0,1},{1,0},{2,3},{3,2},{4,5},{5,4},{6,7},{7,6},{8,9},{9,8},{10,11... | collective-permute-start | bytes 5603336 | tf_op jit(solution)/shard_map/ppermute | solution.py:53
  14.4 6.7 %collective-permute-start.2 = (bf16[8,32,512]{2,1,0:T(8,128)(2,1)S(1)}, bf16[8,32,512]{2,1,0:T(8,128)(2,1)S(1)}, u32[]{:S(2)}, u32[]{:S(2)}) collective-permute-start(bf16[8,32,512]{2,1,0:T(8,128)(2,1)S(1)} %get-tuple-element.24), channel_id=1, source_target_pairs={{0,5},{1,2},{2,1},{3,6},{4,9},{5,0},{6,3},{7,10},{8,13},{9,4},{10,... | collective-permute-start | bytes 786440 | tf_op jit(solution)/shard_map/ppermute | solution.py:62
  17.1 2.0 %copy-start = (bf16[16,4,32,256]{3,2,1,0:T(8,128)(2,1)S(1)}, bf16[16,4,32,256]{3,2,1,0:T(8,128)(2,1)}, u32[]{:S(2)}) copy-start(bf16[16,4,32,256]{3,2,1,0:T(8,128)(2,1)} %interp_ref.3) | copy-start | bytes 3145732
  17.1 6.9 %collective-permute-start.4 = (bf16[8,32,512]{2,1,0:T(8,128)(2,1)S(1)}, bf16[8,32,512]{2,1,0:T(8,128)(2,1)S(1)}, u32[]{:S(2)}, u32[]{:S(2)}) collective-permute-start(bf16[8,32,512]{2,1,0:T(8,128)(2,1)S(1)} %get-tuple-element.25), channel_id=1, source_target_pairs={{0,5},{1,2},{2,1},{3,6},{4,9},{5,0},{6,3},{7,10},{8,13},{9,4},{10,... | collective-permute-start | bytes 786440 | tf_op jit(solution)/shard_map/ppermute | solution.py:62
  21.2 6.1 %collective-permute-start.3 = (bf16[8,32,512]{2,1,0:T(8,128)(2,1)S(1)}, bf16[8,32,512]{2,1,0:T(8,128)(2,1)S(1)}, u32[]{:S(2)}, u32[]{:S(2)}) collective-permute-start(bf16[8,32,512]{2,1,0:T(8,128)(2,1)S(1)} %add_5.1.token), channel_id=1, source_target_pairs={{0,3},{1,4},{2,7},{3,0},{4,1},{5,8},{6,11},{7,2},{8,5},{9,12},{10,... | collective-permute-start | bytes 786440 | tf_op jit(solution)/shard_map/ppermute | solution.py:62
  24.0 6.3 %collective-permute-start.6 = (bf16[8,32,512]{2,1,0:T(8,128)(2,1)S(1)}, bf16[8,32,512]{2,1,0:T(8,128)(2,1)S(1)}, u32[]{:S(2)}, u32[]{:S(2)}) collective-permute-start(bf16[8,32,512]{2,1,0:T(8,128)(2,1)S(1)} %add_4.1.token), channel_id=1, source_target_pairs={{0,3},{1,4},{2,7},{3,0},{4,1},{5,8},{6,11},{7,2},{8,5},{9,12},{10,... | collective-permute-start | bytes 786440 | tf_op jit(solution)/shard_map/ppermute | solution.py:62
  27.3 6.2 %collective-permute-start.5 = (bf16[8,32,512]{2,1,0:T(8,128)(2,1)S(1)}, bf16[8,32,512]{2,1,0:T(8,128)(2,1)S(1)}, u32[]{:S(2)}, u32[]{:S(2)}) collective-permute-start(bf16[8,32,512]{2,1,0:T(8,128)(2,1)S(1)} %add_3.1.token), channel_id=1, source_target_pairs={{0,5},{1,2},{2,1},{3,6},{4,9},{5,0},{6,3},{7,10},{8,13},{9,4},{10,... | collective-permute-start | bytes 786440 | tf_op jit(solution)/shard_map/ppermute | solution.py:62
  30.4 9.3 %copy-start.1 = (bf16[512,512]{1,0:T(8,128)(2,1)S(1)}, bf16[512,512]{1,0:T(8,128)(2,1)}, u32[]{:S(2)}) copy-start(bf16[512,512]{1,0:T(8,128)(2,1)} %up_ref.1) | copy-start | bytes 1572868
  30.4 9.3 %copy-start.2 = (bf16[512,512]{1,0:T(8,128)(2,1)S(1)}, bf16[512,512]{1,0:T(8,128)(2,1)}, u32[]{:S(2)}) copy-start(bf16[512,512]{1,0:T(8,128)(2,1)} %down_ref.1) | copy-start | bytes 1572868
  30.4 9.3 %copy-start.3 = (bf16[256,512]{1,0:T(8,128)(2,1)S(1)}, bf16[256,512]{1,0:T(8,128)(2,1)}, u32[]{:S(2)}) copy-start(bf16[256,512]{1,0:T(8,128)(2,1)} %latent_ref.1) | copy-start | bytes 786436
  30.4 9.3 %copy-start.4 = (f32[512]{0:T(512)S(1)}, f32[512]{0:T(512)}, u32[]{:S(2)}) copy-start(f32[512]{0:T(512)} %param.21) | copy-start | bytes 6148
  30.4 6.8 %collective-permute-start.8 = (bf16[8,32,512]{2,1,0:T(8,128)(2,1)S(1)}, bf16[8,32,512]{2,1,0:T(8,128)(2,1)S(1)}, u32[]{:S(2)}, u32[]{:S(2)}) collective-permute-start(bf16[8,32,512]{2,1,0:T(8,128)(2,1)S(1)} %add_2.1.token), channel_id=1, source_target_pairs={{0,5},{1,2},{2,1},{3,6},{4,9},{5,0},{6,3},{7,10},{8,13},{9,4},{10,... | collective-permute-start | bytes 786440 | tf_op jit(solution)/shard_map/ppermute | solution.py:62
  33.6 6.1 %collective-permute-start.7 = (bf16[8,32,512]{2,1,0:T(8,128)(2,1)S(1)}, bf16[8,32,512]{2,1,0:T(8,128)(2,1)S(1)}, u32[]{:S(2)}, u32[]{:S(2)}) collective-permute-start(bf16[8,32,512]{2,1,0:T(8,128)(2,1)S(1)} %add_1.1), channel_id=1, source_target_pairs={{0,3},{1,4},{2,7},{3,0},{4,1},{5,8},{6,11},{7,2},{8,5},{9,12},{10,... | collective-permute-start | bytes 786440 | tf_op jit(solution)/shard_map/ppermute | solution.py:62
  41.2 5.9 %collective-permute-start.9 = (bf16[256,512]{1,0:T(8,128)(2,1)S(1)}, bf16[256,512]{1,0:T(8,128)(2,1)S(1)}, u32[]{:S(2)}, u32[]{:S(2)}) collective-permute-start(bf16[256,512]{1,0:T(8,128)(2,1)S(1)} %get-tuple-element.26.refs_0_), channel_id=1, source_target_pairs={{0,3},{1,4},{2,7},{3,0},{4,1},{5,8},{6,11},{7,2},{8,5},{9,12},{10,... | collective-permute-start | bytes 786440 | tf_op jit(solution)/shard_map/ppermute | solution.py:62
  43.6 1.6 %collective-permute-start.10 = (bf16[128,512]{1,0:T(8,128)(2,1)S(1)}, bf16[128,512]{1,0:T(8,128)(2,1)S(1)}, u32[]{:S(2)}, u32[]{:S(2)}) collective-permute-start(bf16[128,512]{1,0:T(8,128)(2,1)S(1)} %get-tuple-element.29), channel_id=1, source_target_pairs={{0,1},{1,0},{2,3},{3,2},{4,5},{5,4},{6,7},{7,6},{8,9},{9,8},{10,11... | collective-permute-start | bytes 393224 | tf_op jit(solution)/shard_map/ppermute | solution.py:53
  45.2 5.8 %collective-permute-start.11 = (bf16[256,512]{1,0:T(8,128)(2,1)S(1)}, bf16[256,512]{1,0:T(8,128)(2,1)S(1)}, u32[]{:S(2)}, u32[]{:S(2)}) collective-permute-start(bf16[256,512]{1,0:T(8,128)(2,1)S(1)} %in_order.8), channel_id=1, source_target_pairs={{0,5},{1,2},{2,1},{3,6},{4,9},{5,0},{6,3},{7,10},{8,13},{9,4},{10,... | collective-permute-start | bytes 786440 | tf_op jit(solution)/shard_map/ppermute | solution.py:62
  47.1 6.7 %collective-permute-start.12 = (bf16[256,512]{1,0:T(8,128)(2,1)S(1)}, bf16[256,512]{1,0:T(8,128)(2,1)S(1)}, u32[]{:S(2)}, u32[]{:S(2)}) collective-permute-start(bf16[256,512]{1,0:T(8,128)(2,1)S(1)} %in_order.7.refs_1_.refs_0_), channel_id=1, source_target_pairs={{0,5},{1,2},{2,1},{3,6},{4,9},{5,0},{6,3},{7,10},{8,13},{9,4},{10,... | collective-permute-start | bytes 786440 | tf_op jit(solution)/shard_map/ppermute | solution.py:62
  51.0 6.2 %collective-permute-start.13 = (bf16[256,512]{1,0:T(8,128)(2,1)S(1)}, bf16[256,512]{1,0:T(8,128)(2,1)S(1)}, u32[]{:S(2)}, u32[]{:S(2)}) collective-permute-start(bf16[256,512]{1,0:T(8,128)(2,1)S(1)} %in_order.9.refs_1_), channel_id=1, source_target_pairs={{0,3},{1,4},{2,7},{3,0},{4,1},{5,8},{6,11},{7,2},{8,5},{9,12},{10,... | collective-permute-start | bytes 786440 | tf_op jit(solution)/shard_map/ppermute | solution.py:62
  53.8 6.2 %collective-permute-start.14 = (bf16[256,512]{1,0:T(8,128)(2,1)S(1)}, bf16[256,512]{1,0:T(8,128)(2,1)S(1)}, u32[]{:S(2)}, u32[]{:S(2)}) collective-permute-start(bf16[256,512]{1,0:T(8,128)(2,1)S(1)} %in_order.10.refs_1_.refs_0_), channel_id=1, source_target_pairs={{0,3},{1,4},{2,7},{3,0},{4,1},{5,8},{6,11},{7,2},{8,5},{9,12},{10,... | collective-permute-start | bytes 786440 | tf_op jit(solution)/shard_map/ppermute | solution.py:62
  57.2 6.4 %collective-permute-start.15 = (bf16[256,512]{1,0:T(8,128)(2,1)S(1)}, bf16[256,512]{1,0:T(8,128)(2,1)S(1)}, u32[]{:S(2)}, u32[]{:S(2)}) collective-permute-start(bf16[256,512]{1,0:T(8,128)(2,1)S(1)} %in_order.11.refs_1_), channel_id=1, source_target_pairs={{0,5},{1,2},{2,1},{3,6},{4,9},{5,0},{6,3},{7,10},{8,13},{9,4},{10,... | collective-permute-start | bytes 786440 | tf_op jit(solution)/shard_map/ppermute | solution.py:62
  60.0 6.5 %collective-permute-start.19 = (bf16[256,512]{1,0:T(8,128)(2,1)S(1)}, bf16[256,512]{1,0:T(8,128)(2,1)S(1)}, u32[]{:S(2)}, u32[]{:S(2)}) collective-permute-start(bf16[256,512]{1,0:T(8,128)(2,1)S(1)} %in_order.12.refs_1_.refs_0_), channel_id=1, source_target_pairs={{0,5},{1,2},{2,1},{3,6},{4,9},{5,0},{6,3},{7,10},{8,13},{9,4},{10,... | collective-permute-start | bytes 786440 | tf_op jit(solution)/shard_map/ppermute | solution.py:62
  62.5 4.7 %collective-permute-start.16 = (bf16[256,512]{1,0:T(8,128)(2,1)S(1)}, bf16[256,512]{1,0:T(8,128)(2,1)S(1)}, u32[]{:S(2)}, u32[]{:S(2)}) collective-permute-start(bf16[256,512]{1,0:T(8,128)(2,1)S(1)} %get-tuple-element.33), channel_id=1, source_target_pairs={{0,1},{1,0},{2,3},{3,2},{4,5},{5,4},{6,7},{7,6},{8,9},{9,8},{10,11... | collective-permute-start | bytes 786440 | tf_op jit(solution)/shard_map/ppermute | solution.py:53
  62.5 4.7 %collective-permute-start.17 = (bf16[256,512]{1,0:T(8,128)(2,1)S(1)}, bf16[256,512]{1,0:T(8,128)(2,1)S(1)}, u32[]{:S(2)}, u32[]{:S(2)}) collective-permute-start(bf16[256,512]{1,0:T(8,128)(2,1)S(1)} %get-tuple-element.34), channel_id=1, source_target_pairs={{0,1},{1,0},{2,3},{3,2},{4,5},{5,4},{6,7},{7,6},{8,9},{9,8},{10,11... | collective-permute-start | bytes 786440 | tf_op jit(solution)/shard_map/ppermute | solution.py:53
  64.2 3.0 %collective-permute-start.18 = (bf16[256,512]{1,0:T(8,128)(2,1)S(1)}, bf16[256,512]{1,0:T(8,128)(2,1)S(1)}, u32[]{:S(2)}, u32[]{:S(2)}) collective-permute-start(bf16[256,512]{1,0:T(8,128)(2,1)S(1)} %get-tuple-element.35), channel_id=1, source_target_pairs={{0,1},{1,0},{2,3},{3,2},{4,5},{5,4},{6,7},{7,6},{8,9},{9,8},{10,11... | collective-permute-start | bytes 786440 | tf_op jit(solution)/shard_map/ppermute | solution.py:53
  66.5 1.8 %collective-permute-start.20 = (bf16[256,512]{1,0:T(8,128)(2,1)S(1)}, bf16[256,512]{1,0:T(8,128)(2,1)S(1)}, u32[]{:S(2)}, u32[]{:S(2)}) collective-permute-start(bf16[256,512]{1,0:T(8,128)(2,1)S(1)} %collective-permute-done.19.mine_ref), channel_id=1, source_target_pairs={{0,1},{1,0},{2,3},{3,2},{4,5},{5,4},{6,7},{7,6},{8,9},{9,8},{10,11... | collective-permute-start | bytes 786440 | tf_op jit(solution)/shard_map/ppermute | solution.py:53

commit v16 on v15

--- a/solution.py
+++ b/solution.py
@@ -12,7 +12,7 @@
 N_CORE = 2
 STRIP = 32
 PART = 2
-BACK_PART = 2
+BACK_PART = 4
 
 
 def silu(values):
@@ -67,8 +67,7 @@
     def over_second(self, value, distance):
         return self.over(value, (distance + 1) % 2)
 
-    def entry(self, lists_ref, me, block, k):
-        owner, tile = split(lists_ref[k, block], self.tiles)
+    def seen(self, owner, me):
         ring, core = self.place(owner)
         my_ring, my_core = self.place(me)
         ahead = split(ring - my_ring + self.chips, self.chips)[1]
@@ -77,7 +76,7 @@
         shared = (ahead == 0) | (ahead == self.far)
         stream = jnp.where(shared, 0, core ^ left)
         group = jnp.maximum(2 * distance - 1 + stream, 0)
-        return ((distance + core) & 1) ^ my_core, group, tile
+        return ((distance + core) & 1) ^ my_core, group
 
 
 def strips(rows):
@@ -87,7 +86,7 @@
 def embed_kernel(
     ring, per_step, slots, me_ref, lists_ref, mask_ref,
     x_ref, w1_ref, w2_ref, gain_ref, interp_ref,
-    latent_ref, near_ref, far_ref, table_ref, wide, hidden,
+    latent_ref, near_ref, far_ref, table_ref, wide, hidden, owners_ref,
 ):
     step = pl.program_id(0)
     me = me_ref[0]
@@ -95,10 +94,20 @@
     blk_count = pl.num_programs(0) * per_step
     groups = ring.chips
 
-    def spot(index, block, k):
-        across, group, tile = ring.entry(lists_ref, index, index * blk_count + block, k)
+    @pl.when(step == 0)
+    def _():
+        def note(owner, carry):
+            across, group = ring.seen(owner, me)
+            owners_ref[0, owner] = (across * groups + group) * slots
+            owners_ref[1, owner] = ((across ^ 1) * groups + group) * slots
+            return carry
+
+        lax.fori_loop(0, ring.n_band, note, 0)
+
+    def spot(who, block, k):
+        owner, tile = split(lists_ref[k, (me ^ who) * blk_count + block], ring.tiles)
         slot = split(block * list_len + k, ring.n_band)[0]
-        return across, group, tile, slot
+        return owners_ref[who, owner] + slot, tile
 
     part_rows = PART * block_rows
     spans = [slice(i * part_rows, (i + 1) * part_rows) for i in range(per_step // PART)]
@@ -120,16 +129,16 @@
             latent = latent_ref[b * block_rows : (b + 1) * block_rows]
             part = jnp.dot(weights, latent, preferred_element_type=F32)
             for k in range(list_len):
-                across, group, tile, slot = spot(me, block, k)
-                place = (across * groups + group) * slots + slot
+                place, tile = spot(0, block, k)
                 mask = mask_ref[k, me * blk_count + block]
                 table_ref[0, place] = tile
-                beyond = group == groups - 1
-                near = (across * (groups - 1) + group) * slots + slot
+                across = (place >= groups * slots).astype(jnp.int32)
+                near = place - across * slots
+                beyond = place - across * groups * slots >= (groups - 1) * slots
                 table_ref[2, block * list_len + k] = jnp.where(beyond, tile, near)
                 table_ref[3, block * list_len + k] = mask * jnp.where(beyond, 2 + across, 1)
-                across, group, tile, slot = spot(me ^ 1, block, k)
-                table_ref[1, (across * groups + group) * slots + slot] = tile
+                there, its_tile = spot(1, block, k)
+                table_ref[1, there] = its_tile
                 masked = part[k * tile_rows : (k + 1) * tile_rows] * mask.astype(F32)
                 masked = masked.astype(BF16)
                 near_ref[jnp.minimum(place, near_spare)] = masked
@@ -322,7 +331,11 @@
             out_specs=[pl.BlockSpec((rows, width), lambda i, *_: (i, 0))]
             + [pl.BlockSpec(memory_space=pltpu.VMEM)] * len(counts)
             + [pl.BlockSpec(memory_space=pltpu.SMEM)],
-            scratch_shapes=[pltpu.VMEM((rows, width), F32), pltpu.VMEM((rows, width), BF16)],
+            scratch_shapes=[
+                pltpu.VMEM((rows, width), F32),
+                pltpu.VMEM((rows, width), BF16),
+                pltpu.SMEM((2, n_band), jnp.int32),
+            ],
         ),
         compiler_params=params(24),
         cost_estimate=cost(

time: 74.7 us -> 73.4 us (0.983)
  Pallas kernels: 22.5 us -> 21.2 us
    pallas_call x1, Pallas kernels: 10.8 us -> 9.82 us  [on_device(): pl.pallas_call(functools.partial(embed_kernel, ring, per_step, slots), ou...]
where the time goes in v16:
time: 73.4 us; the launch traced here: 71.9 us
  starting transfers between devices  29 us (40%)
  Pallas kernels  21.2 us (29%)
  waiting for transfers between devices  21 us (29%)
  between operations  0.79 us (1%)
    ppermute x14, starting transfers between devices, over(): return lax.ppermute(value, 'band', pairs)  25.9 us
    ppermute x14, waiting for transfers between devices, over(): return lax.ppermute(value, 'band', pairs)  17 us
    pallas_call x1, Pallas kernels, on_device(): pl.pallas_call(functools.partial(embed_kernel, ring, per_step, slots), ou...  9.82 us
    pallas_call x1, Pallas kernels, on_device(): pl.pallas_call(functools.partial(back_kernel, list_len), out_shape=shape(...  4.57 us
    ppermute x7, waiting for transfers between devices, over_core(): return lax.ppermute(value, 'band', [(i, i ^ 1) for i in range(self.n_band)])  3.96 us
    ppermute x7, starting transfers between devices, over_core(): return lax.ppermute(value, 'band', [(i, i ^ 1) for i in range(self.n_band)])  3.02 us
    pallas_call x4, Pallas kernels, pick(): pl.pallas_call(functools.partial(pick_kernel, chosen, slots, chips, tile_...  2.4 us
  transfers between devices with their start and end apart: 21, of which 18 were waited for; matrix products, arithmetic and copies ran while one was open for 0% of the time, Pallas kernels for 6%

profile of v16, /device:TPU:0, one launch (start us, length us, event | category | flops | bytes accessed | tf_op | source)
XLA Modules:
  0.0 71.9 jit_solution(12090569275913188488)
XLA Ops:
  0.6 9.8 %embed.1 = (bf16[4096,512]{1,0:T(8,128)(2,1)}, bf16[57,32,512]{2,1,0:T(8,128)(2,1)S(1)}, bf16[9,32,512]{2,1,0:T(8,128)(2,1)S(1)}, s32[4,64]{1,0:T(4,128)S(1)}) custom-call(s32[1]{0:T(128)} %bitcast.me_ref, s32[4,256]{1,0:T(4,128)} %bitcast.8, s32[4,256]{1,0:T(4,128)} %bitcast.9, bf16[227,4096]{1,0:T(8,128)(2,1)} %bitcast.7, bf16[227,512]{1,0:T(8,128)(2,1)} %w1_ref.1, ...), custom_call_target="tpu_custom_call" | custom-call | flops 3636461568 | bytes 2908160 | tf_op jit(solution)/shard_map/embed/pallas_call | solution.py:316
  10.9 1.2 %collective-permute-done.other = bf16[9,32,512]{2,1,0:T(8,128)(2,1)S(1)} collective-permute-done((bf16[9,32,512]{2,1,0:T(8,128)(2,1)S(1)}, bf16[9,32,512]{2,1,0:T(8,128)(2,1)S(1)}, u32[]{:S(2)}, u32[]{:S(2)}) %collective-permute-start) | collective-permute-done | bytes 294944 | tf_op jit(solution)/shard_map/ppermute | solution.py:53
  12.1 0.8 %far_sums.1 = (bf16[8,32,512]{2,1,0:T(8,128)(2,1)S(1)}, bf16[8,32,512]{2,1,0:T(8,128)(2,1)S(1)}, bf16[57,32,512]{2,1,0:T(8,128)(2,1)S(1)}) custom-call(s32[4,64]{1,0:T(4,128)S(1)} %get-tuple-element.20.table_ref, bf16[57,32,512]{2,1,0:T(8,128)(2,1)S(1)} %get-tuple-element.21.kept, ...), custom_call_target="tpu_custom_call", output_to_operand_aliasing={{2}: (1, {})} | custom-call | bytes 1867776 | tf_op jit(solution)/shard_map/far_sums/pallas_call | solution.py:364
  13.4 2.7 %collective-permute-start.2 = (bf16[8,32,512]{2,1,0:T(8,128)(2,1)S(1)}, bf16[8,32,512]{2,1,0:T(8,128)(2,1)S(1)}, u32[]{:S(2)}, u32[]{:S(2)}) collective-permute-start(bf16[8,32,512]{2,1,0:T(8,128)(2,1)S(1)} %get-tuple-element.24), channel_id=1, source_target_pairs={{0,5},{1,2},{2,1},{3,6},{4,9},{5,0},{6,3},{7,10},{8,13},{9,4},{10,... | collective-permute-start | bytes 786440 | tf_op jit(solution)/shard_map/ppermute | solution.py:62
  16.1 0.7 %collective-permute-done.1.other = bf16[57,32,512]{2,1,0:T(8,128)(2,1)S(1)} collective-permute-done((bf16[57,32,512]{2,1,0:T(8,128)(2,1)S(1)}, bf16[57,32,512]{2,1,0:T(8,128)(2,1)S(1)}, u32[]{:S(2)}, u32[]{:S(2)}) %collective-permute-start.1) | collective-permute-done | bytes 1867808 | tf_op jit(solution)/shard_map/ppermute | solution.py:53
  16.8 1.2 %own_sums.1.token.own = f32[6,8,32,512]{3,2,1,0:T(8,128)S(1)} custom-call(s32[4,64]{1,0:T(4,128)S(1)} %get-tuple-element.20.table_ref, bf16[57,32,512]{2,1,0:T(8,128)(2,1)S(1)} %get-tuple-element.23.kept, bf16[57,32,512]{2,1,0:T(8,128)(2,1)S(1)} %collective-permute-done.1.other), custom_call_target="tpu_custom_call" | custom-call | bytes 3735552 | tf_op jit(solution)/shard_map/own_sums/pallas_call | solution.py:380
  18.6 1.5 %collective-permute-done.2.came = bf16[8,32,512]{2,1,0:T(8,128)(2,1)S(1)} collective-permute-done((bf16[8,32,512]{2,1,0:T(8,128)(2,1)S(1)}, bf16[8,32,512]{2,1,0:T(8,128)(2,1)S(1)}, u32[]{:S(2)}, u32[]{:S(2)}) %collective-permute-start.2) | collective-permute-done | bytes 262176 | tf_op jit(solution)/shard_map/ppermute | solution.py:62
  20.1 2.0 %collective-permute-start.3 = (bf16[8,32,512]{2,1,0:T(8,128)(2,1)S(1)}, bf16[8,32,512]{2,1,0:T(8,128)(2,1)S(1)}, u32[]{:S(2)}, u32[]{:S(2)}) collective-permute-start(bf16[8,32,512]{2,1,0:T(8,128)(2,1)S(1)} %add_5.1.token), channel_id=1, source_target_pairs={{0,3},{1,4},{2,7},{3,0},{4,1},{5,8},{6,11},{7,2},{8,5},{9,12},{10,... | collective-permute-start | bytes 786440 | tf_op jit(solution)/shard_map/ppermute | solution.py:62
  22.2 0.7 %collective-permute-done.4.came = bf16[8,32,512]{2,1,0:T(8,128)(2,1)S(1)} collective-permute-done((bf16[8,32,512]{2,1,0:T(8,128)(2,1)S(1)}, bf16[8,32,512]{2,1,0:T(8,128)(2,1)S(1)}, u32[]{:S(2)}, u32[]{:S(2)}) %collective-permute-start.4) | collective-permute-done | bytes 262176 | tf_op jit(solution)/shard_map/ppermute | solution.py:62
  23.0 2.1 %collective-permute-start.6 = (bf16[8,32,512]{2,1,0:T(8,128)(2,1)S(1)}, bf16[8,32,512]{2,1,0:T(8,128)(2,1)S(1)}, u32[]{:S(2)}, u32[]{:S(2)}) collective-permute-start(bf16[8,32,512]{2,1,0:T(8,128)(2,1)S(1)} %add_4.1.token), channel_id=1, source_target_pairs={{0,3},{1,4},{2,7},{3,0},{4,1},{5,8},{6,11},{7,2},{8,5},{9,12},{10,... | collective-permute-start | bytes 786440 | tf_op jit(solution)/shard_map/ppermute | solution.py:62
  25.1 1.2 %collective-permute-done.3.came = bf16[8,32,512]{2,1,0:T(8,128)(2,1)S(1)} collective-permute-done((bf16[8,32,512]{2,1,0:T(8,128)(2,1)S(1)}, bf16[8,32,512]{2,1,0:T(8,128)(2,1)S(1)}, u32[]{:S(2)}, u32[]{:S(2)}) %collective-permute-start.3) | collective-permute-done | bytes 262176 | tf_op jit(solution)/shard_map/ppermute | solution.py:62
  26.3 2.2 %collective-permute-start.5 = (bf16[8,32,512]{2,1,0:T(8,128)(2,1)S(1)}, bf16[8,32,512]{2,1,0:T(8,128)(2,1)S(1)}, u32[]{:S(2)}, u32[]{:S(2)}) collective-permute-start(bf16[8,32,512]{2,1,0:T(8,128)(2,1)S(1)} %add_3.1.token), channel_id=1, source_target_pairs={{0,5},{1,2},{2,1},{3,6},{4,9},{5,0},{6,3},{7,10},{8,13},{9,4},{10,... | collective-permute-start | bytes 786440 | tf_op jit(solution)/shard_map/ppermute | solution.py:62
  28.5 0.8 %collective-permute-done.6.came = bf16[8,32,512]{2,1,0:T(8,128)(2,1)S(1)} collective-permute-done((bf16[8,32,512]{2,1,0:T(8,128)(2,1)S(1)}, bf16[8,32,512]{2,1,0:T(8,128)(2,1)S(1)}, u32[]{:S(2)}, u32[]{:S(2)}) %collective-permute-start.6) | collective-permute-done | bytes 262176 | tf_op jit(solution)/shard_map/ppermute | solution.py:62
  29.4 2.4 %collective-permute-start.8 = (bf16[8,32,512]{2,1,0:T(8,128)(2,1)S(1)}, bf16[8,32,512]{2,1,0:T(8,128)(2,1)S(1)}, u32[]{:S(2)}, u32[]{:S(2)}) collective-permute-start(bf16[8,32,512]{2,1,0:T(8,128)(2,1)S(1)} %add_2.1.token), channel_id=1, source_target_pairs={{0,5},{1,2},{2,1},{3,6},{4,9},{5,0},{6,3},{7,10},{8,13},{9,4},{10,... | collective-permute-start | bytes 786440 | tf_op jit(solution)/shard_map/ppermute | solution.py:62
  32.6 2.0 %collective-permute-start.7 = (bf16[8,32,512]{2,1,0:T(8,128)(2,1)S(1)}, bf16[8,32,512]{2,1,0:T(8,128)(2,1)S(1)}, u32[]{:S(2)}, u32[]{:S(2)}) collective-permute-start(bf16[8,32,512]{2,1,0:T(8,128)(2,1)S(1)} %add_1.1), channel_id=1, source_target_pairs={{0,3},{1,4},{2,7},{3,0},{4,1},{5,8},{6,11},{7,2},{8,5},{9,12},{10,... | collective-permute-start | bytes 786440 | tf_op jit(solution)/shard_map/ppermute | solution.py:62
  34.6 1.6 %collective-permute-done.8.neighbour = bf16[8,32,512]{2,1,0:T(8,128)(2,1)S(1)} collective-permute-done((bf16[8,32,512]{2,1,0:T(8,128)(2,1)S(1)}, bf16[8,32,512]{2,1,0:T(8,128)(2,1)S(1)}, u32[]{:S(2)}, u32[]{:S(2)}) %collective-permute-start.8) | collective-permute-done | bytes 262176 | tf_op jit(solution)/shard_map/ppermute | solution.py:62
  36.2 2.4 %collective-permute-done.7.came = bf16[8,32,512]{2,1,0:T(8,128)(2,1)S(1)} collective-permute-done((bf16[8,32,512]{2,1,0:T(8,128)(2,1)S(1)}, bf16[8,32,512]{2,1,0:T(8,128)(2,1)S(1)}, u32[]{:S(2)}, u32[]{:S(2)}) %collective-permute-start.7) | collective-permute-done | bytes 262176 | tf_op jit(solution)/shard_map/ppermute | solution.py:62
  38.7 1.5 %mesh_step.1 = (bf16[256,512]{1,0:T(8,128)(2,1)}, bf16[256,512]{1,0:T(8,128)(2,1)S(1)}, bf16[256,512]{1,0:T(8,128)(2,1)S(1)}) custom-call(bf16[256,512]{1,0:T(8,128)(2,1)S(1)} %copy-done.3, bf16[512,512]{1,0:T(8,128)(2,1)S(1)} %copy-done.1, bf16[512,512]{1,0:T(8,128)(2,1)S(1)} %copy-done.2, f32[1,512]{1,0:T(1,128)S(1)} %bitcast.6, ...), custom_call_target="tpu_custom_call" | custom-call | flops 268435456 | bytes 1048576 | tf_op jit(solution)/shard_map/mesh_step/pallas_call | solution.py:428
  40.2 1.9 %collective-permute-start.9 = (bf16[256,512]{1,0:T(8,128)(2,1)S(1)}, bf16[256,512]{1,0:T(8,128)(2,1)S(1)}, u32[]{:S(2)}, u32[]{:S(2)}) collective-permute-start(bf16[256,512]{1,0:T(8,128)(2,1)S(1)} %get-tuple-element.26.refs_0_), channel_id=1, source_target_pairs={{0,3},{1,4},{2,7},{3,0},{4,1},{5,8},{6,11},{7,2},{8,5},{9,12},{10,... | collective-permute-start | bytes 786440 | tf_op jit(solution)/shard_map/ppermute | solution.py:62
  43.2 1.0 %collective-permute-done.10.refs_1_.refs_4_ = bf16[128,512]{1,0:T(8,128)(2,1)S(1)} collective-permute-done((bf16[128,512]{1,0:T(8,128)(2,1)S(1)}, bf16[128,512]{1,0:T(8,128)(2,1)S(1)}, u32[]{:S(2)}, u32[]{:S(2)}) %collective-permute-start.10) | collective-permute-done | bytes 131104 | tf_op jit(solution)/shard_map/ppermute | solution.py:53
  44.2 1.5 %collective-permute-start.11 = (bf16[256,512]{1,0:T(8,128)(2,1)S(1)}, bf16[256,512]{1,0:T(8,128)(2,1)S(1)}, u32[]{:S(2)}, u32[]{:S(2)}) collective-permute-start(bf16[256,512]{1,0:T(8,128)(2,1)S(1)} %in_order.8), channel_id=1, source_target_pairs={{0,5},{1,2},{2,1},{3,6},{4,9},{5,0},{6,3},{7,10},{8,13},{9,4},{10,... | collective-permute-start | bytes 786440 | tf_op jit(solution)/shard_map/ppermute | solution.py:62
  46.1 1.9 %collective-permute-start.12 = (bf16[256,512]{1,0:T(8,128)(2,1)S(1)}, bf16[256,512]{1,0:T(8,128)(2,1)S(1)}, u32[]{:S(2)}, u32[]{:S(2)}) collective-permute-start(bf16[256,512]{1,0:T(8,128)(2,1)S(1)} %in_order.7.refs_1_.refs_0_), channel_id=1, source_target_pairs={{0,5},{1,2},{2,1},{3,6},{4,9},{5,0},{6,3},{7,10},{8,13},{9,4},{10,... | collective-permute-start | bytes 786440 | tf_op jit(solution)/shard_map/ppermute | solution.py:62
  48.0 2.0 %collective-permute-done.11.refs_0_ = bf16[256,512]{1,0:T(8,128)(2,1)S(1)} collective-permute-done((bf16[256,512]{1,0:T(8,128)(2,1)S(1)}, bf16[256,512]{1,0:T(8,128)(2,1)S(1)}, u32[]{:S(2)}, u32[]{:S(2)}) %collective-permute-start.11) | collective-permute-done | bytes 262176 | tf_op jit(solution)/shard_map/ppermute | solution.py:62
  50.0 1.4 %collective-permute-start.13 = (bf16[256,512]{1,0:T(8,128)(2,1)S(1)}, bf16[256,512]{1,0:T(8,128)(2,1)S(1)}, u32[]{:S(2)}, u32[]{:S(2)}) collective-permute-start(bf16[256,512]{1,0:T(8,128)(2,1)S(1)} %in_order.9.refs_1_), channel_id=1, source_target_pairs={{0,3},{1,4},{2,7},{3,0},{4,1},{5,8},{6,11},{7,2},{8,5},{9,12},{10,... | collective-permute-start | bytes 786440 | tf_op jit(solution)/shard_map/ppermute | solution.py:62
  52.1 0.7 %collective-permute-done.12.refs_0_ = bf16[256,512]{1,0:T(8,128)(2,1)S(1)} collective-permute-done((bf16[256,512]{1,0:T(8,128)(2,1)S(1)}, bf16[256,512]{1,0:T(8,128)(2,1)S(1)}, u32[]{:S(2)}, u32[]{:S(2)}) %collective-permute-start.12) | collective-permute-done | bytes 262176 | tf_op jit(solution)/shard_map/ppermute | solution.py:62
  52.8 1.5 %collective-permute-start.14 = (bf16[256,512]{1,0:T(8,128)(2,1)S(1)}, bf16[256,512]{1,0:T(8,128)(2,1)S(1)}, u32[]{:S(2)}, u32[]{:S(2)}) collective-permute-start(bf16[256,512]{1,0:T(8,128)(2,1)S(1)} %in_order.10.refs_1_.refs_0_), channel_id=1, source_target_pairs={{0,3},{1,4},{2,7},{3,0},{4,1},{5,8},{6,11},{7,2},{8,5},{9,12},{10,... | collective-permute-start | bytes 786440 | tf_op jit(solution)/shard_map/ppermute | solution.py:62
  54.4 1.8 %collective-permute-done.13.refs_0_ = bf16[256,512]{1,0:T(8,128)(2,1)S(1)} collective-permute-done((bf16[256,512]{1,0:T(8,128)(2,1)S(1)}, bf16[256,512]{1,0:T(8,128)(2,1)S(1)}, u32[]{:S(2)}, u32[]{:S(2)}) %collective-permute-start.13) | collective-permute-done | bytes 262176 | tf_op jit(solution)/shard_map/ppermute | solution.py:62
  56.2 1.8 %collective-permute-start.15 = (bf16[256,512]{1,0:T(8,128)(2,1)S(1)}, bf16[256,512]{1,0:T(8,128)(2,1)S(1)}, u32[]{:S(2)}, u32[]{:S(2)}) collective-permute-start(bf16[256,512]{1,0:T(8,128)(2,1)S(1)} %in_order.11.refs_1_), channel_id=1, source_target_pairs={{0,5},{1,2},{2,1},{3,6},{4,9},{5,0},{6,3},{7,10},{8,13},{9,4},{10,... | collective-permute-start | bytes 786440 | tf_op jit(solution)/shard_map/ppermute | solution.py:62
  59.0 2.5 %collective-permute-start.19 = (bf16[256,512]{1,0:T(8,128)(2,1)S(1)}, bf16[256,512]{1,0:T(8,128)(2,1)S(1)}, u32[]{:S(2)}, u32[]{:S(2)}) collective-permute-start(bf16[256,512]{1,0:T(8,128)(2,1)S(1)} %in_order.12.refs_1_.refs_0_), channel_id=1, source_target_pairs={{0,5},{1,2},{2,1},{3,6},{4,9},{5,0},{6,3},{7,10},{8,13},{9,4},{10,... | collective-permute-start | bytes 786440 | tf_op jit(solution)/shard_map/ppermute | solution.py:62
  63.6 2.0 %collective-permute-done.19.mine_ref = bf16[256,512]{1,0:T(8,128)(2,1)S(1)} collective-permute-done((bf16[256,512]{1,0:T(8,128)(2,1)S(1)}, bf16[256,512]{1,0:T(8,128)(2,1)S(1)}, u32[]{:S(2)}, u32[]{:S(2)}) %collective-permute-start.19) | collective-permute-done | bytes 262176 | tf_op jit(solution)/shard_map/ppermute | solution.py:62
  66.3 1.0 %collective-permute-done.20.theirs_ref = bf16[256,512]{1,0:T(8,128)(2,1)S(1)} collective-permute-done((bf16[256,512]{1,0:T(8,128)(2,1)S(1)}, bf16[256,512]{1,0:T(8,128)(2,1)S(1)}, u32[]{:S(2)}, u32[]{:S(2)}) %collective-permute-start.20) | collective-permute-done | bytes 262176 | tf_op jit(solution)/shard_map/ppermute | solution.py:53
  67.3 4.6 %back.1 = bf16[4096,512]{1,0:T(8,128)(2,1)} custom-call(s32[4,64]{1,0:T(4,128)S(1)} %get-tuple-element.20.table_ref, bf16[16,256,128]{2,1,0:T(8,128)(2,1)S(1)} %turn.1.token.weights_ref, bf16[1792,512]{1,0:T(8,128)(2,1)S(1)} %join.1.near_ref, bf16[256,512]{1,0:T(8,128)(2,1)S(1)} %collective-permute-done.19.mine_ref, ...), custom_call_target="tpu_custom_call" | custom-call | flops 536870912 | bytes 9437184 | tf_op jit(solution)/shard_map/back/pallas_call | solution.py:483
  (43 shorter events, 8.5 us)
Async XLA Ops:
  10.5 1.7 %collective-permute-start = (bf16[9,32,512]{2,1,0:T(8,128)(2,1)S(1)}, bf16[9,32,512]{2,1,0:T(8,128)(2,1)S(1)}, u32[]{:S(2)}, u32[]{:S(2)}) collective-permute-start(bf16[9,32,512]{2,1,0:T(8,128)(2,1)S(1)} %get-tuple-element.22), channel_id=1, source_target_pairs={{0,1},{1,0},{2,3},{3,2},{4,5},{5,4},{6,7},{7,6},{8,9},{9,8},{10,11... | collective-permute-start | bytes 884744 | tf_op jit(solution)/shard_map/ppermute | solution.py:53
  12.9 3.9 %collective-permute-start.1 = (bf16[57,32,512]{2,1,0:T(8,128)(2,1)S(1)}, bf16[57,32,512]{2,1,0:T(8,128)(2,1)S(1)}, u32[]{:S(2)}, u32[]{:S(2)}) collective-permute-start(bf16[57,32,512]{2,1,0:T(8,128)(2,1)S(1)} %get-tuple-element.23.kept), channel_id=1, source_target_pairs={{0,1},{1,0},{2,3},{3,2},{4,5},{5,4},{6,7},{7,6},{8,9},{9,8},{10,11... | collective-permute-start | bytes 5603336 | tf_op jit(solution)/shard_map/ppermute | solution.py:53
  13.4 6.7 %collective-permute-start.2 = (bf16[8,32,512]{2,1,0:T(8,128)(2,1)S(1)}, bf16[8,32,512]{2,1,0:T(8,128)(2,1)S(1)}, u32[]{:S(2)}, u32[]{:S(2)}) collective-permute-start(bf16[8,32,512]{2,1,0:T(8,128)(2,1)S(1)} %get-tuple-element.24), channel_id=1, source_target_pairs={{0,5},{1,2},{2,1},{3,6},{4,9},{5,0},{6,3},{7,10},{8,13},{9,4},{10,... | collective-permute-start | bytes 786440 | tf_op jit(solution)/shard_map/ppermute | solution.py:62
  16.0 2.0 %copy-start = (bf16[16,4,32,256]{3,2,1,0:T(8,128)(2,1)S(1)}, bf16[16,4,32,256]{3,2,1,0:T(8,128)(2,1)}, u32[]{:S(2)}) copy-start(bf16[16,4,32,256]{3,2,1,0:T(8,128)(2,1)} %interp_ref.3) | copy-start | bytes 3145732
  16.0 6.9 %collective-permute-start.4 = (bf16[8,32,512]{2,1,0:T(8,128)(2,1)S(1)}, bf16[8,32,512]{2,1,0:T(8,128)(2,1)S(1)}, u32[]{:S(2)}, u32[]{:S(2)}) collective-permute-start(bf16[8,32,512]{2,1,0:T(8,128)(2,1)S(1)} %get-tuple-element.25), channel_id=1, source_target_pairs={{0,5},{1,2},{2,1},{3,6},{4,9},{5,0},{6,3},{7,10},{8,13},{9,4},{10,... | collective-permute-start | bytes 786440 | tf_op jit(solution)/shard_map/ppermute | solution.py:62
  20.1 6.1 %collective-permute-start.3 = (bf16[8,32,512]{2,1,0:T(8,128)(2,1)S(1)}, bf16[8,32,512]{2,1,0:T(8,128)(2,1)S(1)}, u32[]{:S(2)}, u32[]{:S(2)}) collective-permute-start(bf16[8,32,512]{2,1,0:T(8,128)(2,1)S(1)} %add_5.1.token), channel_id=1, source_target_pairs={{0,3},{1,4},{2,7},{3,0},{4,1},{5,8},{6,11},{7,2},{8,5},{9,12},{10,... | collective-permute-start | bytes 786440 | tf_op jit(solution)/shard_map/ppermute | solution.py:62
  23.0 6.3 %collective-permute-start.6 = (bf16[8,32,512]{2,1,0:T(8,128)(2,1)S(1)}, bf16[8,32,512]{2,1,0:T(8,128)(2,1)S(1)}, u32[]{:S(2)}, u32[]{:S(2)}) collective-permute-start(bf16[8,32,512]{2,1,0:T(8,128)(2,1)S(1)} %add_4.1.token), channel_id=1, source_target_pairs={{0,3},{1,4},{2,7},{3,0},{4,1},{5,8},{6,11},{7,2},{8,5},{9,12},{10,... | collective-permute-start | bytes 786440 | tf_op jit(solution)/shard_map/ppermute | solution.py:62
  26.3 6.2 %collective-permute-start.5 = (bf16[8,32,512]{2,1,0:T(8,128)(2,1)S(1)}, bf16[8,32,512]{2,1,0:T(8,128)(2,1)S(1)}, u32[]{:S(2)}, u32[]{:S(2)}) collective-permute-start(bf16[8,32,512]{2,1,0:T(8,128)(2,1)S(1)} %add_3.1.token), channel_id=1, source_target_pairs={{0,5},{1,2},{2,1},{3,6},{4,9},{5,0},{6,3},{7,10},{8,13},{9,4},{10,... | collective-permute-start | bytes 786440 | tf_op jit(solution)/shard_map/ppermute | solution.py:62
  29.4 9.3 %copy-start.1 = (bf16[512,512]{1,0:T(8,128)(2,1)S(1)}, bf16[512,512]{1,0:T(8,128)(2,1)}, u32[]{:S(2)}) copy-start(bf16[512,512]{1,0:T(8,128)(2,1)} %up_ref.1) | copy-start | bytes 1572868
  29.4 9.3 %copy-start.2 = (bf16[512,512]{1,0:T(8,128)(2,1)S(1)}, bf16[512,512]{1,0:T(8,128)(2,1)}, u32[]{:S(2)}) copy-start(bf16[512,512]{1,0:T(8,128)(2,1)} %down_ref.1) | copy-start | bytes 1572868
  29.4 9.3 %copy-start.3 = (bf16[256,512]{1,0:T(8,128)(2,1)S(1)}, bf16[256,512]{1,0:T(8,128)(2,1)}, u32[]{:S(2)}) copy-start(bf16[256,512]{1,0:T(8,128)(2,1)} %latent_ref.1) | copy-start | bytes 786436
  29.4 9.3 %copy-start.4 = (f32[512]{0:T(512)S(1)}, f32[512]{0:T(512)}, u32[]{:S(2)}) copy-start(f32[512]{0:T(512)} %param.21) | copy-start | bytes 6148
  29.4 6.8 %collective-permute-start.8 = (bf16[8,32,512]{2,1,0:T(8,128)(2,1)S(1)}, bf16[8,32,512]{2,1,0:T(8,128)(2,1)S(1)}, u32[]{:S(2)}, u32[]{:S(2)}) collective-permute-start(bf16[8,32,512]{2,1,0:T(8,128)(2,1)S(1)} %add_2.1.token), channel_id=1, source_target_pairs={{0,5},{1,2},{2,1},{3,6},{4,9},{5,0},{6,3},{7,10},{8,13},{9,4},{10,... | collective-permute-start | bytes 786440 | tf_op jit(solution)/shard_map/ppermute | solution.py:62
  32.6 6.1 %collective-permute-start.7 = (bf16[8,32,512]{2,1,0:T(8,128)(2,1)S(1)}, bf16[8,32,512]{2,1,0:T(8,128)(2,1)S(1)}, u32[]{:S(2)}, u32[]{:S(2)}) collective-permute-start(bf16[8,32,512]{2,1,0:T(8,128)(2,1)S(1)} %add_1.1), channel_id=1, source_target_pairs={{0,3},{1,4},{2,7},{3,0},{4,1},{5,8},{6,11},{7,2},{8,5},{9,12},{10,... | collective-permute-start | bytes 786440 | tf_op jit(solution)/shard_map/ppermute | solution.py:62
  40.2 5.9 %collective-permute-start.9 = (bf16[256,512]{1,0:T(8,128)(2,1)S(1)}, bf16[256,512]{1,0:T(8,128)(2,1)S(1)}, u32[]{:S(2)}, u32[]{:S(2)}) collective-permute-start(bf16[256,512]{1,0:T(8,128)(2,1)S(1)} %get-tuple-element.26.refs_0_), channel_id=1, source_target_pairs={{0,3},{1,4},{2,7},{3,0},{4,1},{5,8},{6,11},{7,2},{8,5},{9,12},{10,... | collective-permute-start | bytes 786440 | tf_op jit(solution)/shard_map/ppermute | solution.py:62
  42.6 1.6 %collective-permute-start.10 = (bf16[128,512]{1,0:T(8,128)(2,1)S(1)}, bf16[128,512]{1,0:T(8,128)(2,1)S(1)}, u32[]{:S(2)}, u32[]{:S(2)}) collective-permute-start(bf16[128,512]{1,0:T(8,128)(2,1)S(1)} %get-tuple-element.29), channel_id=1, source_target_pairs={{0,1},{1,0},{2,3},{3,2},{4,5},{5,4},{6,7},{7,6},{8,9},{9,8},{10,11... | collective-permute-start | bytes 393224 | tf_op jit(solution)/shard_map/ppermute | solution.py:53
  44.2 5.8 %collective-permute-start.11 = (bf16[256,512]{1,0:T(8,128)(2,1)S(1)}, bf16[256,512]{1,0:T(8,128)(2,1)S(1)}, u32[]{:S(2)}, u32[]{:S(2)}) collective-permute-start(bf16[256,512]{1,0:T(8,128)(2,1)S(1)} %in_order.8), channel_id=1, source_target_pairs={{0,5},{1,2},{2,1},{3,6},{4,9},{5,0},{6,3},{7,10},{8,13},{9,4},{10,... | collective-permute-start | bytes 786440 | tf_op jit(solution)/shard_map/ppermute | solution.py:62
  46.1 6.7 %collective-permute-start.12 = (bf16[256,512]{1,0:T(8,128)(2,1)S(1)}, bf16[256,512]{1,0:T(8,128)(2,1)S(1)}, u32[]{:S(2)}, u32[]{:S(2)}) collective-permute-start(bf16[256,512]{1,0:T(8,128)(2,1)S(1)} %in_order.7.refs_1_.refs_0_), channel_id=1, source_target_pairs={{0,5},{1,2},{2,1},{3,6},{4,9},{5,0},{6,3},{7,10},{8,13},{9,4},{10,... | collective-permute-start | bytes 786440 | tf_op jit(solution)/shard_map/ppermute | solution.py:62
  50.0 6.2 %collective-permute-start.13 = (bf16[256,512]{1,0:T(8,128)(2,1)S(1)}, bf16[256,512]{1,0:T(8,128)(2,1)S(1)}, u32[]{:S(2)}, u32[]{:S(2)}) collective-permute-start(bf16[256,512]{1,0:T(8,128)(2,1)S(1)} %in_order.9.refs_1_), channel_id=1, source_target_pairs={{0,3},{1,4},{2,7},{3,0},{4,1},{5,8},{6,11},{7,2},{8,5},{9,12},{10,... | collective-permute-start | bytes 786440 | tf_op jit(solution)/shard_map/ppermute | solution.py:62
  52.8 6.2 %collective-permute-start.14 = (bf16[256,512]{1,0:T(8,128)(2,1)S(1)}, bf16[256,512]{1,0:T(8,128)(2,1)S(1)}, u32[]{:S(2)}, u32[]{:S(2)}) collective-permute-start(bf16[256,512]{1,0:T(8,128)(2,1)S(1)} %in_order.10.refs_1_.refs_0_), channel_id=1, source_target_pairs={{0,3},{1,4},{2,7},{3,0},{4,1},{5,8},{6,11},{7,2},{8,5},{9,12},{10,... | collective-permute-start | bytes 786440 | tf_op jit(solution)/shard_map/ppermute | solution.py:62
  56.2 6.4 %collective-permute-start.15 = (bf16[256,512]{1,0:T(8,128)(2,1)S(1)}, bf16[256,512]{1,0:T(8,128)(2,1)S(1)}, u32[]{:S(2)}, u32[]{:S(2)}) collective-permute-start(bf16[256,512]{1,0:T(8,128)(2,1)S(1)} %in_order.11.refs_1_), channel_id=1, source_target_pairs={{0,5},{1,2},{2,1},{3,6},{4,9},{5,0},{6,3},{7,10},{8,13},{9,4},{10,... | collective-permute-start | bytes 786440 | tf_op jit(solution)/shard_map/ppermute | solution.py:62
  59.0 6.5 %collective-permute-start.19 = (bf16[256,512]{1,0:T(8,128)(2,1)S(1)}, bf16[256,512]{1,0:T(8,128)(2,1)S(1)}, u32[]{:S(2)}, u32[]{:S(2)}) collective-permute-start(bf16[256,512]{1,0:T(8,128)(2,1)S(1)} %in_order.12.refs_1_.refs_0_), channel_id=1, source_target_pairs={{0,5},{1,2},{2,1},{3,6},{4,9},{5,0},{6,3},{7,10},{8,13},{9,4},{10,... | collective-permute-start | bytes 786440 | tf_op jit(solution)/shard_map/ppermute | solution.py:62
  61.5 4.7 %collective-permute-start.16 = (bf16[256,512]{1,0:T(8,128)(2,1)S(1)}, bf16[256,512]{1,0:T(8,128)(2,1)S(1)}, u32[]{:S(2)}, u32[]{:S(2)}) collective-permute-start(bf16[256,512]{1,0:T(8,128)(2,1)S(1)} %get-tuple-element.33), channel_id=1, source_target_pairs={{0,1},{1,0},{2,3},{3,2},{4,5},{5,4},{6,7},{7,6},{8,9},{9,8},{10,11... | collective-permute-start | bytes 786440 | tf_op jit(solution)/shard_map/ppermute | solution.py:53
  61.5 4.7 %collective-permute-start.17 = (bf16[256,512]{1,0:T(8,128)(2,1)S(1)}, bf16[256,512]{1,0:T(8,128)(2,1)S(1)}, u32[]{:S(2)}, u32[]{:S(2)}) collective-permute-start(bf16[256,512]{1,0:T(8,128)(2,1)S(1)} %get-tuple-element.34), channel_id=1, source_target_pairs={{0,1},{1,0},{2,3},{3,2},{4,5},{5,4},{6,7},{7,6},{8,9},{9,8},{10,11... | collective-permute-start | bytes 786440 | tf_op jit(solution)/shard_map/ppermute | solution.py:53
  63.2 3.0 %collective-permute-start.18 = (bf16[256,512]{1,0:T(8,128)(2,1)S(1)}, bf16[256,512]{1,0:T(8,128)(2,1)S(1)}, u32[]{:S(2)}, u32[]{:S(2)}) collective-permute-start(bf16[256,512]{1,0:T(8,128)(2,1)S(1)} %get-tuple-element.35), channel_id=1, source_target_pairs={{0,1},{1,0},{2,3},{3,2},{4,5},{5,4},{6,7},{7,6},{8,9},{9,8},{10,11... | collective-permute-start | bytes 786440 | tf_op jit(solution)/shard_map/ppermute | solution.py:53
  65.5 1.8 %collective-permute-start.20 = (bf16[256,512]{1,0:T(8,128)(2,1)S(1)}, bf16[256,512]{1,0:T(8,128)(2,1)S(1)}, u32[]{:S(2)}, u32[]{:S(2)}) collective-permute-start(bf16[256,512]{1,0:T(8,128)(2,1)S(1)} %collective-permute-done.19.mine_ref), channel_id=1, source_target_pairs={{0,1},{1,0},{2,3},{3,2},{4,5},{5,4},{6,7},{7,6},{8,9},{9,8},{10,11... | collective-permute-start | bytes 786440 | tf_op jit(solution)/shard_map/ppermute | solution.py:53

commit v17 on v16

--- a/solution.py
+++ b/solution.py
@@ -132,11 +132,8 @@
                 place, tile = spot(0, block, k)
                 mask = mask_ref[k, me * blk_count + block]
                 table_ref[0, place] = tile
-                across = (place >= groups * slots).astype(jnp.int32)
-                near = place - across * slots
-                beyond = place - across * groups * slots >= (groups - 1) * slots
-                table_ref[2, block * list_len + k] = jnp.where(beyond, tile, near)
-                table_ref[3, block * list_len + k] = mask * jnp.where(beyond, 2 + across, 1)
+                table_ref[2, place] = block * list_len + k
+                table_ref[3, block * list_len + k] = mask
                 there, its_tile = spot(1, block, k)
                 table_ref[1, there] = its_tile
                 masked = part[k * tile_rows : (k + 1) * tile_rows] * mask.astype(F32)
@@ -152,12 +149,11 @@
         total[table_ref[1, groups * slots + place]] += other[place + first * slots].astype(F32)
 
 
-def far_kernel(slots, groups, table_ref, kept, other, far, before, same, total):
-    del same
-    for group, out in ((groups - 1, far), (groups - 2, before)):
-        total[...] = jnp.zeros_like(total)
-        add_entries(total, table_ref, group, slots, kept, other, groups, 2 - groups)
-        out[...] = total[...].astype(BF16)
+def far_kernel(group, slots, groups, table_ref, kept, other, *rest):
+    out, _, total = rest[-3:]
+    total[...] = jnp.zeros_like(total)
+    add_entries(total, table_ref, group, slots, kept, other, groups, 2 - groups)
+    out[...] = total[...].astype(BF16)
 
 
 def own_kernel(slots, groups, table_ref, kept, other, own):
@@ -206,18 +202,25 @@
         out_ref[b] = interp_ref[b].reshape(out_ref.shape[2], out_ref.shape[1]).T
 
 
-def join_kernel(*refs):
-    pieces, out = refs[:-1], refs[-1]
-    start = 0
-    for piece in pieces:
-        out[start : start + piece.shape[0]] = piece[...]
-        start += piece.shape[0]
+def join_kernel(slots, groups, tile_rows, table_ref, *refs):
+    parts, out = refs[:-1], refs[-1]
+    for across in range(N_CORE):
+        place = across * groups * slots
+        for part in parts[across * len(parts) // N_CORE : (across + 1) * len(parts) // N_CORE]:
+            for start in range(0, part.shape[0], tile_rows):
+                entry = table_ref[2, place]
+                value = part[start : start + tile_rows]
+                listed = table_ref[3, entry] == 1
+                rows = pl.ds(pl.multiple_of(entry * tile_rows, tile_rows), tile_rows)
+                out[rows] = jnp.where(listed, value, jnp.zeros_like(value))
+                place += 1
 
 
 def back_kernel(
-    list_len, table_ref, weights_ref, near_ref, mine_ref, theirs_ref, latent_any,
-    out_any, latent_ref, total, out_ref, sems,
+    slots, groups, list_len, table_ref, weights_ref, tiles_ref, mine_ref, theirs_ref, latent_any,
+    out_any, same, latent_ref, total, out_ref, sems,
 ):
+    del same
     blk_count, block_rows, listed = weights_ref.shape
     tile_rows = listed // list_len
     part_rows = BACK_PART * block_rows
@@ -236,18 +239,16 @@
     def rows_at(tile):
         return pl.ds(pl.multiple_of(tile * tile_rows, tile_rows), tile_rows)
 
+    for across, block_ref in enumerate((mine_ref, theirs_ref)):
+        for slot in range(slots):
+            place = ((across + 1) * groups - 1) * slots + slot
+            entry = table_ref[2, place]
+            value = block_ref[rows_at(table_ref[0, place])]
+            value = jnp.where(table_ref[3, entry] == 1, value, jnp.zeros_like(value))
+            tiles_ref[rows_at(entry)] = value
+
     for block in range(blk_count):
-        values = []
-        for k in range(list_len):
-            entry = block * list_len + k
-            place, kind = table_ref[2, entry], table_ref[3, entry]
-            here = jnp.where(kind > 1, 0, place)
-            beyond = jnp.where(kind > 1, place, 0)
-            value = near_ref[rows_at(here)]
-            value = jnp.where(kind == 2, mine_ref[rows_at(beyond)], value)
-            value = jnp.where(kind == 3, theirs_ref[rows_at(beyond)], value)
-            values.append(jnp.where(kind > 0, value, jnp.zeros_like(value)))
-        value = jnp.concatenate(values, axis=0)
+        value = tiles_ref[block * listed : (block + 1) * listed]
         rows = slice(block * block_rows, (block + 1) * block_rows)
         total[rows] = jnp.dot(weights_ref[block], value, preferred_element_type=F32)
         if block % BACK_PART == 0:
@@ -361,22 +362,29 @@
             name="in_order",
         )(value, token)
 
-    first, second, near = pl.pallas_call(
-        functools.partial(far_kernel, slots, chips),
-        out_shape=[shape(dense)] * 2 + [shape(near.shape)],
-        grid_spec=pltpu.PrefetchScalarGridSpec(
-            num_scalar_prefetch=1,
-            grid=(1,),
-            in_specs=[in_vmem] * 2,
-            out_specs=[in_vmem] * 3,
-            scratch_shapes=[pltpu.VMEM(dense, F32)],
-        ),
-        input_output_aliases={1: 2},
-        compiler_params=params(8),
-        cost_estimate=cost(0, near),
-        name="far_sums",
-    )(table, near, other_far)
-    other = ring.over_core(near)
+
+    def far_sums(group, near, *token):
+        handed, spec = (token[0], in_any) if token else (near, in_vmem)
+        return pl.pallas_call(
+            functools.partial(far_kernel, group, slots, chips),
+            out_shape=[shape(dense), shape(handed.shape)],
+            grid_spec=pltpu.PrefetchScalarGridSpec(
+                num_scalar_prefetch=1,
+                grid=(1,),
+                in_specs=[in_vmem] * 2 + [in_any] * len(token),
+                out_specs=[in_vmem, spec],
+                scratch_shapes=[pltpu.VMEM(dense, F32)],
+            ),
+            input_output_aliases={3 if token else 1: 1},
+            compiler_params=params(8),
+            cost_estimate=cost(0),
+            name=f"far_{group}",
+        )(table, near, other_far, *token)
+
+    first, near = far_sums(chips - 1, near)
+    first = ring.over_first(first, far)
+    second, other = far_sums(chips - 2, near, ring.over_core(near))
+    second = ring.over_second(second, far - 1)
     own = pl.pallas_call(
         functools.partial(own_kernel, slots, chips),
         out_shape=shape((chips - 2,) + dense, F32),
@@ -402,7 +410,6 @@
             name=f"add_{group}",
         )(own, value, token)
 
-    first, second = ring.over_first(first, far), ring.over_second(second, far - 1)
     turned = (blk_count, block_rows, list_len * tile_rows)
     per_step = 4
     token = weights = pl.pallas_call(
@@ -470,24 +477,29 @@
         first, second = onward, after
     tiles_far = [first, ring.over_core(first)]
     parts = mine + theirs
+    by_entry = shape((entries * tile_rows, width))
     joined = pl.pallas_call(
-        join_kernel,
-        out_shape=shape((sum(part.shape[0] for part in parts), width)),
-        in_specs=[in_vmem] * len(parts),
-        out_specs=in_vmem,
+        functools.partial(join_kernel, slots, chips, tile_rows),
+        out_shape=by_entry,
+        grid_spec=pltpu.PrefetchScalarGridSpec(
+            num_scalar_prefetch=1,
+            grid=(1,),
+            in_specs=[in_vmem] * len(parts),
+            out_specs=in_vmem,
+        ),
         compiler_params=params(8),
         cost_estimate=cost(0, *parts),
         name="join",
-    )(*parts)
-
-    grid_out = pl.pallas_call(
-        functools.partial(back_kernel, list_len),
-        out_shape=shape((grid_rows, width)),
+    )(table, *parts)
+
+    grid_out, _ = pl.pallas_call(
+        functools.partial(back_kernel, slots, chips, list_len),
+        out_shape=[shape((grid_rows, width)), by_entry],
         grid_spec=pltpu.PrefetchScalarGridSpec(
             num_scalar_prefetch=1,
             grid=(1,),
             in_specs=[in_vmem] * 4 + [in_any],
-            out_specs=in_any,
+            out_specs=[in_any, in_vmem],
             scratch_shapes=[
                 pltpu.VMEM((grid_rows, width), BF16),
                 pltpu.VMEM((grid_rows, width), F32),
@@ -495,6 +507,7 @@
                 pltpu.SemaphoreType.DMA((2 * (blk_count // BACK_PART),)),
             ],
         ),
+        input_output_aliases={2: 1},
         compiler_params=params(32),
         cost_estimate=cost(2 * grid_rows * width * list_len * tile_rows, latent, latent, interp),
         name="back",

time: 73.4 us -> 80.4 us (1.095)
  the two profiles are of different devices: /device:TPU:0 before, /device:TPU:29 now
where the time goes in v17:
time: 80.4 us; the launch traced here: 80.2 us
  waiting for transfers between devices  47.7 us (59%)
  Pallas kernels  22.2 us (28%)
  starting transfers between devices  9.44 us (12%)
  between operations  0.86 us (1%)
    ppermute x14, waiting for transfers between devices, over(): return lax.ppermute(value, 'band', pairs)  41.6 us
    pallas_call x1, Pallas kernels, on_device(): pl.pallas_call(functools.partial(embed_kernel, ring, per_step, slots), ou...  9.73 us
    ppermute x14, starting transfers between devices, over(): return lax.ppermute(value, 'band', pairs)  6.14 us
    ppermute x7, waiting for transfers between devices, over_core(): return lax.ppermute(value, 'band', [(i, i ^ 1) for i in range(self.n_band)])  6.1 us
    pallas_call x1, Pallas kernels, on_device(): pl.pallas_call(functools.partial(back_kernel, slots, chips, list_len), ou...  4.49 us
    ppermute x7, starting transfers between devices, over_core(): return lax.ppermute(value, 'band', [(i, i ^ 1) for i in range(self.n_band)])  3.3 us
    pallas_call x4, Pallas kernels, pick(): pl.pallas_call(functools.partial(pick_kernel, chosen, slots, chips, tile_...  2.4 us
  transfers between devices with their start and end apart: 21, of which 13 were waited for; matrix products, arithmetic and copies ran while one was open for 0% of the time, Pallas kernels for 7%

profile of v17, /device:TPU:29, one launch (start us, length us, event | category | flops | bytes accessed | tf_op | source)
XLA Modules:
  0.0 80.2 jit_solution(13203755336528137564)
XLA Ops:
  0.6 9.7 %embed.1 = (bf16[4096,512]{1,0:T(8,128)(2,1)}, bf16[57,32,512]{2,1,0:T(8,128)(2,1)S(1)}, bf16[9,32,512]{2,1,0:T(8,128)(2,1)S(1)}, s32[4,64]{1,0:T(4,128)S(1)}) custom-call(s32[1]{0:T(128)} %bitcast.me_ref, s32[4,256]{1,0:T(4,128)} %bitcast.8, s32[4,256]{1,0:T(4,128)} %bitcast.9, bf16[227,4096]{1,0:T(8,128)(2,1)} %bitcast.7, bf16[227,512]{1,0:T(8,128)(2,1)} %w1_ref.1, ...), custom_call_target="tpu_custom_call" | custom-call | flops 3636461568 | bytes 2908160 | tf_op jit(solution)/shard_map/embed/pallas_call | solution.py:317
  10.4 0.7 collective-permute-start
  11.0 1.2 %collective-permute-done.other = bf16[9,32,512]{2,1,0:T(8,128)(2,1)S(1)} collective-permute-done((bf16[9,32,512]{2,1,0:T(8,128)(2,1)S(1)}, bf16[9,32,512]{2,1,0:T(8,128)(2,1)S(1)}, u32[]{:S(2)}, u32[]{:S(2)}) %collective-permute-start) | collective-permute-done | bytes 294944 | tf_op jit(solution)/shard_map/ppermute | solution.py:53
  12.2 0.7 far_7.1
  13.6 3.2 %collective-permute-done.1.rest_0_ = bf16[57,32,512]{2,1,0:T(8,128)(2,1)S(1)} collective-permute-done((bf16[57,32,512]{2,1,0:T(8,128)(2,1)S(1)}, bf16[57,32,512]{2,1,0:T(8,128)(2,1)S(1)}, u32[]{:S(2)}, u32[]{:S(2)}) %collective-permute-start.1) | collective-permute-done | bytes 1867808 | tf_op jit(solution)/shard_map/ppermute | solution.py:53
  16.8 0.7 far_6.1
  17.5 1.2 %own_sums.1.token.own = f32[6,8,32,512]{3,2,1,0:T(8,128)S(1)} custom-call(s32[4,64]{1,0:T(4,128)S(1)} %get-tuple-element.22.table_ref, bf16[57,32,512]{2,1,0:T(8,128)(2,1)S(1)} %get-tuple-element.25.kept, bf16[57,32,512]{2,1,0:T(8,128)(2,1)S(1)} %get-tuple-element.26.other), custom_call_target="tpu_custom_call" | custom-call | bytes 3735552 | tf_op jit(solution)/shard_map/own_sums/pallas_call | solution.py:388
  18.7 0.6 collective-permute-start.4
  19.3 0.5 turn.1.token.weights_ref
  20.1 7.2 %collective-permute-done.4.came = bf16[8,32,512]{2,1,0:T(8,128)(2,1)S(1)} collective-permute-done((bf16[8,32,512]{2,1,0:T(8,128)(2,1)S(1)}, bf16[8,32,512]{2,1,0:T(8,128)(2,1)S(1)}, u32[]{:S(2)}, u32[]{:S(2)}) %collective-permute-start.4) | collective-permute-done | bytes 262176 | tf_op jit(solution)/shard_map/ppermute | solution.py:62
  27.4 0.9 %collective-permute-start.5 = (bf16[8,32,512]{2,1,0:T(8,128)(2,1)S(1)}, bf16[8,32,512]{2,1,0:T(8,128)(2,1)S(1)}, u32[]{:S(2)}, u32[]{:S(2)}) collective-permute-start(bf16[8,32,512]{2,1,0:T(8,128)(2,1)S(1)} %add_3.1.token), channel_id=1, source_target_pairs={{0,5},{1,2},{2,1},{3,6},{4,9},{5,0},{6,3},{7,10},{8,13},{9,4},{10,... | collective-permute-start | bytes 786440 | tf_op jit(solution)/shard_map/ppermute | solution.py:62
  28.3 7.8 %collective-permute-done.6.came = bf16[8,32,512]{2,1,0:T(8,128)(2,1)S(1)} collective-permute-done((bf16[8,32,512]{2,1,0:T(8,128)(2,1)S(1)}, bf16[8,32,512]{2,1,0:T(8,128)(2,1)S(1)}, u32[]{:S(2)}, u32[]{:S(2)}) %collective-permute-start.6) | collective-permute-done | bytes 262176 | tf_op jit(solution)/shard_map/ppermute | solution.py:62
  36.8 8.0 %collective-permute-done.8.neighbour = bf16[8,32,512]{2,1,0:T(8,128)(2,1)S(1)} collective-permute-done((bf16[8,32,512]{2,1,0:T(8,128)(2,1)S(1)}, bf16[8,32,512]{2,1,0:T(8,128)(2,1)S(1)}, u32[]{:S(2)}, u32[]{:S(2)}) %collective-permute-start.8) | collective-permute-done | bytes 262176 | tf_op jit(solution)/shard_map/ppermute | solution.py:62
  44.8 1.5 %mesh_step.1 = (bf16[256,512]{1,0:T(8,128)(2,1)}, bf16[256,512]{1,0:T(8,128)(2,1)S(1)}, bf16[256,512]{1,0:T(8,128)(2,1)S(1)}) custom-call(bf16[256,512]{1,0:T(8,128)(2,1)S(1)} %copy-done.3, bf16[512,512]{1,0:T(8,128)(2,1)S(1)} %copy-done.1, bf16[512,512]{1,0:T(8,128)(2,1)S(1)} %copy-done.2, f32[1,512]{1,0:T(1,128)S(1)} %bitcast.6, ...), custom_call_target="tpu_custom_call" | custom-call | flops 268435456 | bytes 1048576 | tf_op jit(solution)/shard_map/mesh_step/pallas_call | solution.py:435
  46.3 0.6 pick_0.1
  47.4 1.0 %collective-permute-done.10.refs_1_.refs_4_ = bf16[128,512]{1,0:T(8,128)(2,1)S(1)} collective-permute-done((bf16[128,512]{1,0:T(8,128)(2,1)S(1)}, bf16[128,512]{1,0:T(8,128)(2,1)S(1)}, u32[]{:S(2)}, u32[]{:S(2)}) %collective-permute-start.10) | collective-permute-done | bytes 131104 | tf_op jit(solution)/shard_map/ppermute | solution.py:53
  48.3 1.7 %collective-permute-start.11 = (bf16[256,512]{1,0:T(8,128)(2,1)S(1)}, bf16[256,512]{1,0:T(8,128)(2,1)S(1)}, u32[]{:S(2)}, u32[]{:S(2)}) collective-permute-start(bf16[256,512]{1,0:T(8,128)(2,1)S(1)} %in_order.8), channel_id=1, source_target_pairs={{0,5},{1,2},{2,1},{3,6},{4,9},{5,0},{6,3},{7,10},{8,13},{9,4},{10,... | collective-permute-start | bytes 786440 | tf_op jit(solution)/shard_map/ppermute | solution.py:62
  50.1 3.4 %collective-permute-done.9.refs_0_ = bf16[256,512]{1,0:T(8,128)(2,1)S(1)} collective-permute-done((bf16[256,512]{1,0:T(8,128)(2,1)S(1)}, bf16[256,512]{1,0:T(8,128)(2,1)S(1)}, u32[]{:S(2)}, u32[]{:S(2)}) %collective-permute-start.9) | collective-permute-done | bytes 262176 | tf_op jit(solution)/shard_map/ppermute | solution.py:62
  53.4 1.5 %collective-permute-done.11.refs_0_ = bf16[256,512]{1,0:T(8,128)(2,1)S(1)} collective-permute-done((bf16[256,512]{1,0:T(8,128)(2,1)S(1)}, bf16[256,512]{1,0:T(8,128)(2,1)S(1)}, u32[]{:S(2)}, u32[]{:S(2)}) %collective-permute-start.11) | collective-permute-done | bytes 262176 | tf_op jit(solution)/shard_map/ppermute | solution.py:62
  54.9 1.0 %collective-permute-start.13 = (bf16[256,512]{1,0:T(8,128)(2,1)S(1)}, bf16[256,512]{1,0:T(8,128)(2,1)S(1)}, u32[]{:S(2)}, u32[]{:S(2)}) collective-permute-start(bf16[256,512]{1,0:T(8,128)(2,1)S(1)} %in_order.9.refs_1_), channel_id=1, source_target_pairs={{0,3},{1,4},{2,7},{3,0},{4,1},{5,8},{6,11},{7,2},{8,5},{9,12},{10,... | collective-permute-start | bytes 786440 | tf_op jit(solution)/shard_map/ppermute | solution.py:62
  55.9 0.6 pick_1.1
  56.5 4.3 %collective-permute-done.12.refs_0_ = bf16[256,512]{1,0:T(8,128)(2,1)S(1)} collective-permute-done((bf16[256,512]{1,0:T(8,128)(2,1)S(1)}, bf16[256,512]{1,0:T(8,128)(2,1)S(1)}, u32[]{:S(2)}, u32[]{:S(2)}) %collective-permute-start.12) | collective-permute-done | bytes 262176 | tf_op jit(solution)/shard_map/ppermute | solution.py:62
  61.1 0.9 %collective-permute-start.15 = (bf16[256,512]{1,0:T(8,128)(2,1)S(1)}, bf16[256,512]{1,0:T(8,128)(2,1)S(1)}, u32[]{:S(2)}, u32[]{:S(2)}) collective-permute-start(bf16[256,512]{1,0:T(8,128)(2,1)S(1)} %in_order.11.refs_1_), channel_id=1, source_target_pairs={{0,5},{1,2},{2,1},{3,6},{4,9},{5,0},{6,3},{7,10},{8,13},{9,4},{10,... | collective-permute-start | bytes 786440 | tf_op jit(solution)/shard_map/ppermute | solution.py:62
  62.0 0.6 pick_3.1
  62.7 5.8 %collective-permute-done.14.refs_0_ = bf16[256,512]{1,0:T(8,128)(2,1)S(1)} collective-permute-done((bf16[256,512]{1,0:T(8,128)(2,1)S(1)}, bf16[256,512]{1,0:T(8,128)(2,1)S(1)}, u32[]{:S(2)}, u32[]{:S(2)}) %collective-permute-start.14) | collective-permute-done | bytes 262176 | tf_op jit(solution)/shard_map/ppermute | solution.py:62
  68.4 0.5 collective-permute-start.17
  68.9 0.6 pick_5.1
  69.5 1.2 %collective-permute-start.18 = (bf16[256,512]{1,0:T(8,128)(2,1)S(1)}, bf16[256,512]{1,0:T(8,128)(2,1)S(1)}, u32[]{:S(2)}, u32[]{:S(2)}) collective-permute-start(bf16[256,512]{1,0:T(8,128)(2,1)S(1)} %get-tuple-element.38), channel_id=1, source_target_pairs={{0,1},{1,0},{2,3},{3,2},{4,5},{5,4},{6,7},{7,6},{8,9},{9,8},{10,11... | collective-permute-start | bytes 786440 | tf_op jit(solution)/shard_map/ppermute | solution.py:53
  70.8 3.4 %collective-permute-done.19.mine_ref = bf16[256,512]{1,0:T(8,128)(2,1)S(1)} collective-permute-done((bf16[256,512]{1,0:T(8,128)(2,1)S(1)}, bf16[256,512]{1,0:T(8,128)(2,1)S(1)}, u32[]{:S(2)}, u32[]{:S(2)}) %collective-permute-start.19) | collective-permute-done | bytes 262176 | tf_op jit(solution)/shard_map/ppermute | solution.py:62
  74.2 0.8 %join.1.tiles_ref = bf16[2048,512]{1,0:T(8,128)(2,1)S(1)} custom-call(s32[4,64]{1,0:T(4,128)S(1)} %get-tuple-element.22.table_ref, bf16[128,512]{1,0:T(8,128)(2,1)S(1)} %get-tuple-element.30.refs_1_.refs_0_, bf16[256,512]{1,0:T(8,128)(2,1)S(1)} %get-tuple-element.33.refs_1_, bf16[256,512]{1,0:T(8,128)(2,1)S(1)} %get-tuple-element.34.refs_1_.refs_2_, ...), custom_call_target="tpu_custom_call" | custom-call | bytes 1835008 | tf_op jit(solution)/shard_map/join/pallas_call | solution.py:481
  75.1 0.7 collective-permute-done.20.theirs_ref
  75.7 4.5 %back.1 = (bf16[4096,512]{1,0:T(8,128)(2,1)}, bf16[2048,512]{1,0:T(8,128)(2,1)S(1)}) custom-call(s32[4,64]{1,0:T(4,128)S(1)} %get-tuple-element.22.table_ref, bf16[16,256,128]{2,1,0:T(8,128)(2,1)S(1)} %turn.1.token.weights_ref, bf16[2048,512]{1,0:T(8,128)(2,1)S(1)} %join.1.tiles_ref, ...), custom_call_target="tpu_custom_call", output_to_operand_aliasing={{1}: (2, {})} | custom-call | flops 536870912 | bytes 9437184 | tf_op jit(solution)/shard_map/back/pallas_call | solution.py:495
  (44 shorter events, 2.6 us)
Async XLA Ops:
  10.4 1.9 %collective-permute-start = (bf16[9,32,512]{2,1,0:T(8,128)(2,1)S(1)}, bf16[9,32,512]{2,1,0:T(8,128)(2,1)S(1)}, u32[]{:S(2)}, u32[]{:S(2)}) collective-permute-start(bf16[9,32,512]{2,1,0:T(8,128)(2,1)S(1)} %get-tuple-element.24), channel_id=1, source_target_pairs={{0,1},{1,0},{2,3},{3,2},{4,5},{5,4},{6,7},{7,6},{8,9},{9,8},{10,11... | collective-permute-start | bytes 884744 | tf_op jit(solution)/shard_map/ppermute | solution.py:53
  12.9 3.9 %collective-permute-start.1 = (bf16[57,32,512]{2,1,0:T(8,128)(2,1)S(1)}, bf16[57,32,512]{2,1,0:T(8,128)(2,1)S(1)}, u32[]{:S(2)}, u32[]{:S(2)}) collective-permute-start(bf16[57,32,512]{2,1,0:T(8,128)(2,1)S(1)} %get-tuple-element.25.kept), channel_id=1, source_target_pairs={{0,1},{1,0},{2,3},{3,2},{4,5},{5,4},{6,7},{7,6},{8,9},{9,8},{10,11... | collective-permute-start | bytes 5603336 | tf_op jit(solution)/shard_map/ppermute | solution.py:53
  13.4 6.4 %collective-permute-start.2 = (bf16[8,32,512]{2,1,0:T(8,128)(2,1)S(1)}, bf16[8,32,512]{2,1,0:T(8,128)(2,1)S(1)}, u32[]{:S(2)}, u32[]{:S(2)}) collective-permute-start(bf16[8,32,512]{2,1,0:T(8,128)(2,1)S(1)} %get-tuple-element.27), channel_id=1, source_target_pairs={{0,5},{1,2},{2,1},{3,6},{4,9},{5,0},{6,3},{7,10},{8,13},{9,4},{10,... | collective-permute-start | bytes 786440 | tf_op jit(solution)/shard_map/ppermute | solution.py:62
  17.5 1.8 %copy-start = (bf16[16,4,32,256]{3,2,1,0:T(8,128)(2,1)S(1)}, bf16[16,4,32,256]{3,2,1,0:T(8,128)(2,1)}, u32[]{:S(2)}) copy-start(bf16[16,4,32,256]{3,2,1,0:T(8,128)(2,1)} %interp_ref.3) | copy-start | bytes 3145732
  18.7 8.5 %collective-permute-start.4 = (bf16[8,32,512]{2,1,0:T(8,128)(2,1)S(1)}, bf16[8,32,512]{2,1,0:T(8,128)(2,1)S(1)}, u32[]{:S(2)}, u32[]{:S(2)}) collective-permute-start(bf16[8,32,512]{2,1,0:T(8,128)(2,1)S(1)} %get-tuple-element.28), channel_id=1, source_target_pairs={{0,5},{1,2},{2,1},{3,6},{4,9},{5,0},{6,3},{7,10},{8,13},{9,4},{10,... | collective-permute-start | bytes 786440 | tf_op jit(solution)/shard_map/ppermute | solution.py:62
  19.9 7.5 %collective-permute-start.3 = (bf16[8,32,512]{2,1,0:T(8,128)(2,1)S(1)}, bf16[8,32,512]{2,1,0:T(8,128)(2,1)S(1)}, u32[]{:S(2)}, u32[]{:S(2)}) collective-permute-start(bf16[8,32,512]{2,1,0:T(8,128)(2,1)S(1)} %add_5.1.token), channel_id=1, source_target_pairs={{0,3},{1,4},{2,7},{3,0},{4,1},{5,8},{6,11},{7,2},{8,5},{9,12},{10,... | collective-permute-start | bytes 786440 | tf_op jit(solution)/shard_map/ppermute | solution.py:62
  27.3 8.8 %collective-permute-start.6 = (bf16[8,32,512]{2,1,0:T(8,128)(2,1)S(1)}, bf16[8,32,512]{2,1,0:T(8,128)(2,1)S(1)}, u32[]{:S(2)}, u32[]{:S(2)}) collective-permute-start(bf16[8,32,512]{2,1,0:T(8,128)(2,1)S(1)} %add_4.1.token), channel_id=1, source_target_pairs={{0,3},{1,4},{2,7},{3,0},{4,1},{5,8},{6,11},{7,2},{8,5},{9,12},{10,... | collective-permute-start | bytes 786440 | tf_op jit(solution)/shard_map/ppermute | solution.py:62
  27.4 8.8 %collective-permute-start.5 = (bf16[8,32,512]{2,1,0:T(8,128)(2,1)S(1)}, bf16[8,32,512]{2,1,0:T(8,128)(2,1)S(1)}, u32[]{:S(2)}, u32[]{:S(2)}) collective-permute-start(bf16[8,32,512]{2,1,0:T(8,128)(2,1)S(1)} %add_3.1.token), channel_id=1, source_target_pairs={{0,5},{1,2},{2,1},{3,6},{4,9},{5,0},{6,3},{7,10},{8,13},{9,4},{10,... | collective-permute-start | bytes 786440 | tf_op jit(solution)/shard_map/ppermute | solution.py:62
  36.2 8.7 %copy-start.1 = (bf16[512,512]{1,0:T(8,128)(2,1)S(1)}, bf16[512,512]{1,0:T(8,128)(2,1)}, u32[]{:S(2)}) copy-start(bf16[512,512]{1,0:T(8,128)(2,1)} %up_ref.1) | copy-start | bytes 1572868
  36.2 8.7 %copy-start.2 = (bf16[512,512]{1,0:T(8,128)(2,1)S(1)}, bf16[512,512]{1,0:T(8,128)(2,1)}, u32[]{:S(2)}) copy-start(bf16[512,512]{1,0:T(8,128)(2,1)} %down_ref.1) | copy-start | bytes 1572868
  36.2 8.6 %copy-start.3 = (bf16[256,512]{1,0:T(8,128)(2,1)S(1)}, bf16[256,512]{1,0:T(8,128)(2,1)}, u32[]{:S(2)}) copy-start(bf16[256,512]{1,0:T(8,128)(2,1)} %latent_ref.1) | copy-start | bytes 786436
  36.2 8.6 %copy-start.4 = (f32[512]{0:T(512)S(1)}, f32[512]{0:T(512)}, u32[]{:S(2)}) copy-start(f32[512]{0:T(512)} %param.21) | copy-start | bytes 6148
  36.2 8.6 %collective-permute-start.8 = (bf16[8,32,512]{2,1,0:T(8,128)(2,1)S(1)}, bf16[8,32,512]{2,1,0:T(8,128)(2,1)S(1)}, u32[]{:S(2)}, u32[]{:S(2)}) collective-permute-start(bf16[8,32,512]{2,1,0:T(8,128)(2,1)S(1)} %add_2.1.token), channel_id=1, source_target_pairs={{0,5},{1,2},{2,1},{3,6},{4,9},{5,0},{6,3},{7,10},{8,13},{9,4},{10,... | collective-permute-start | bytes 786440 | tf_op jit(solution)/shard_map/ppermute | solution.py:62
  36.4 8.5 %collective-permute-start.7 = (bf16[8,32,512]{2,1,0:T(8,128)(2,1)S(1)}, bf16[8,32,512]{2,1,0:T(8,128)(2,1)S(1)}, u32[]{:S(2)}, u32[]{:S(2)}) collective-permute-start(bf16[8,32,512]{2,1,0:T(8,128)(2,1)S(1)} %add_1.1), channel_id=1, source_target_pairs={{0,3},{1,4},{2,7},{3,0},{4,1},{5,8},{6,11},{7,2},{8,5},{9,12},{10,... | collective-permute-start | bytes 786440 | tf_op jit(solution)/shard_map/ppermute | solution.py:62
  46.3 7.1 %collective-permute-start.9 = (bf16[256,512]{1,0:T(8,128)(2,1)S(1)}, bf16[256,512]{1,0:T(8,128)(2,1)S(1)}, u32[]{:S(2)}, u32[]{:S(2)}) collective-permute-start(bf16[256,512]{1,0:T(8,128)(2,1)S(1)} %get-tuple-element.29.refs_0_), channel_id=1, source_target_pairs={{0,3},{1,4},{2,7},{3,0},{4,1},{5,8},{6,11},{7,2},{8,5},{9,12},{10,... | collective-permute-start | bytes 786440 | tf_op jit(solution)/shard_map/ppermute | solution.py:62
  46.9 1.4 %collective-permute-start.10 = (bf16[128,512]{1,0:T(8,128)(2,1)S(1)}, bf16[128,512]{1,0:T(8,128)(2,1)S(1)}, u32[]{:S(2)}, u32[]{:S(2)}) collective-permute-start(bf16[128,512]{1,0:T(8,128)(2,1)S(1)} %get-tuple-element.32), channel_id=1, source_target_pairs={{0,1},{1,0},{2,3},{3,2},{4,5},{5,4},{6,7},{7,6},{8,9},{9,8},{10,11... | collective-permute-start | bytes 393224 | tf_op jit(solution)/shard_map/ppermute | solution.py:53
  48.3 6.6 %collective-permute-start.11 = (bf16[256,512]{1,0:T(8,128)(2,1)S(1)}, bf16[256,512]{1,0:T(8,128)(2,1)S(1)}, u32[]{:S(2)}, u32[]{:S(2)}) collective-permute-start(bf16[256,512]{1,0:T(8,128)(2,1)S(1)} %in_order.8), channel_id=1, source_target_pairs={{0,5},{1,2},{2,1},{3,6},{4,9},{5,0},{6,3},{7,10},{8,13},{9,4},{10,... | collective-permute-start | bytes 786440 | tf_op jit(solution)/shard_map/ppermute | solution.py:62
  53.4 7.4 %collective-permute-start.12 = (bf16[256,512]{1,0:T(8,128)(2,1)S(1)}, bf16[256,512]{1,0:T(8,128)(2,1)S(1)}, u32[]{:S(2)}, u32[]{:S(2)}) collective-permute-start(bf16[256,512]{1,0:T(8,128)(2,1)S(1)} %in_order.7.refs_1_.refs_0_), channel_id=1, source_target_pairs={{0,5},{1,2},{2,1},{3,6},{4,9},{5,0},{6,3},{7,10},{8,13},{9,4},{10,... | collective-permute-start | bytes 786440 | tf_op jit(solution)/shard_map/ppermute | solution.py:62
  54.9 6.2 %collective-permute-start.13 = (bf16[256,512]{1,0:T(8,128)(2,1)S(1)}, bf16[256,512]{1,0:T(8,128)(2,1)S(1)}, u32[]{:S(2)}, u32[]{:S(2)}) collective-permute-start(bf16[256,512]{1,0:T(8,128)(2,1)S(1)} %in_order.9.refs_1_), channel_id=1, source_target_pairs={{0,3},{1,4},{2,7},{3,0},{4,1},{5,8},{6,11},{7,2},{8,5},{9,12},{10,... | collective-permute-start | bytes 786440 | tf_op jit(solution)/shard_map/ppermute | solution.py:62
  60.8 7.6 %collective-permute-start.14 = (bf16[256,512]{1,0:T(8,128)(2,1)S(1)}, bf16[256,512]{1,0:T(8,128)(2,1)S(1)}, u32[]{:S(2)}, u32[]{:S(2)}) collective-permute-start(bf16[256,512]{1,0:T(8,128)(2,1)S(1)} %in_order.10.refs_1_.refs_0_), channel_id=1, source_target_pairs={{0,3},{1,4},{2,7},{3,0},{4,1},{5,8},{6,11},{7,2},{8,5},{9,12},{10,... | collective-permute-start | bytes 786440 | tf_op jit(solution)/shard_map/ppermute | solution.py:62
  61.1 7.8 %collective-permute-start.15 = (bf16[256,512]{1,0:T(8,128)(2,1)S(1)}, bf16[256,512]{1,0:T(8,128)(2,1)S(1)}, u32[]{:S(2)}, u32[]{:S(2)}) collective-permute-start(bf16[256,512]{1,0:T(8,128)(2,1)S(1)} %in_order.11.refs_1_), channel_id=1, source_target_pairs={{0,5},{1,2},{2,1},{3,6},{4,9},{5,0},{6,3},{7,10},{8,13},{9,4},{10,... | collective-permute-start | bytes 786440 | tf_op jit(solution)/shard_map/ppermute | solution.py:62
  68.4 5.8 %collective-permute-start.19 = (bf16[256,512]{1,0:T(8,128)(2,1)S(1)}, bf16[256,512]{1,0:T(8,128)(2,1)S(1)}, u32[]{:S(2)}, u32[]{:S(2)}) collective-permute-start(bf16[256,512]{1,0:T(8,128)(2,1)S(1)} %in_order.12.refs_1_.refs_0_), channel_id=1, source_target_pairs={{0,5},{1,2},{2,1},{3,6},{4,9},{5,0},{6,3},{7,10},{8,13},{9,4},{10,... | collective-permute-start | bytes 786440 | tf_op jit(solution)/shard_map/ppermute | solution.py:62
  68.4 5.8 %collective-permute-start.16 = (bf16[256,512]{1,0:T(8,128)(2,1)S(1)}, bf16[256,512]{1,0:T(8,128)(2,1)S(1)}, u32[]{:S(2)}, u32[]{:S(2)}) collective-permute-start(bf16[256,512]{1,0:T(8,128)(2,1)S(1)} %get-tuple-element.36), channel_id=1, source_target_pairs={{0,1},{1,0},{2,3},{3,2},{4,5},{5,4},{6,7},{7,6},{8,9},{9,8},{10,11... | collective-permute-start | bytes 786440 | tf_op jit(solution)/shard_map/ppermute | solution.py:53
  68.4 5.8 %collective-permute-start.17 = (bf16[256,512]{1,0:T(8,128)(2,1)S(1)}, bf16[256,512]{1,0:T(8,128)(2,1)S(1)}, u32[]{:S(2)}, u32[]{:S(2)}) collective-permute-start(bf16[256,512]{1,0:T(8,128)(2,1)S(1)} %get-tuple-element.37), channel_id=1, source_target_pairs={{0,1},{1,0},{2,3},{3,2},{4,5},{5,4},{6,7},{7,6},{8,9},{9,8},{10,11... | collective-permute-start | bytes 786440 | tf_op jit(solution)/shard_map/ppermute | solution.py:53
  69.5 4.7 %collective-permute-start.18 = (bf16[256,512]{1,0:T(8,128)(2,1)S(1)}, bf16[256,512]{1,0:T(8,128)(2,1)S(1)}, u32[]{:S(2)}, u32[]{:S(2)}) collective-permute-start(bf16[256,512]{1,0:T(8,128)(2,1)S(1)} %get-tuple-element.38), channel_id=1, source_target_pairs={{0,1},{1,0},{2,3},{3,2},{4,5},{5,4},{6,7},{7,6},{8,9},{9,8},{10,11... | collective-permute-start | bytes 786440 | tf_op jit(solution)/shard_map/ppermute | solution.py:53
  74.2 1.5 %collective-permute-start.20 = (bf16[256,512]{1,0:T(8,128)(2,1)S(1)}, bf16[256,512]{1,0:T(8,128)(2,1)S(1)}, u32[]{:S(2)}, u32[]{:S(2)}) collective-permute-start(bf16[256,512]{1,0:T(8,128)(2,1)S(1)} %collective-permute-done.19.mine_ref), channel_id=1, source_target_pairs={{0,1},{1,0},{2,3},{3,2},{4,5},{5,4},{6,7},{7,6},{8,9},{9,8},{10,11... | collective-permute-start | bytes 786440 | tf_op jit(solution)/shard_map/ppermute | solution.py:53

commit v18 on v16

--- a/solution.py
+++ b/solution.py
@@ -86,7 +86,7 @@
 def embed_kernel(
     ring, per_step, slots, me_ref, lists_ref, mask_ref,
     x_ref, w1_ref, w2_ref, gain_ref, interp_ref,
-    latent_ref, near_ref, far_ref, table_ref, wide, hidden, owners_ref,
+    latent_ref, near_ref, far_ref, table_ref, wide, hidden, owners_ref, places_ref,
 ):
     step = pl.program_id(0)
     me = me_ref[0]
@@ -108,6 +108,27 @@
         owner, tile = split(lists_ref[k, (me ^ who) * blk_count + block], ring.tiles)
         slot = split(block * list_len + k, ring.n_band)[0]
         return owners_ref[who, owner] + slot, tile
+
+    near_spare, far_spare = near_ref.shape[0] - 1, far_ref.shape[0] - 1
+    for b in range(per_step):
+        block = step * per_step + b
+        for k in range(list_len):
+            entry = block * list_len + k
+            place, tile = spot(0, block, k)
+            mask = mask_ref[k, me * blk_count + block]
+            table_ref[0, place] = tile
+            across = (place >= groups * slots).astype(jnp.int32)
+            near = place - across * slots
+            beyond = place - across * groups * slots >= (groups - 1) * slots
+            table_ref[2, entry] = jnp.where(beyond, tile, near)
+            table_ref[3, entry] = mask * jnp.where(beyond, 2 + across, 1)
+            there, its_tile = spot(1, block, k)
+            table_ref[1, there] = its_tile
+            places_ref[0, b * list_len + k] = jnp.minimum(place, near_spare)
+            places_ref[1, b * list_len + k] = jnp.where(
+                place < near_spare, far_spare, place - near_spare
+            )
+            places_ref[2, b * list_len + k] = mask
 
     part_rows = PART * block_rows
     spans = [slice(i * part_rows, (i + 1) * part_rows) for i in range(per_step // PART)]
@@ -119,30 +140,19 @@
         for strip in strips(rows):
             hidden[strip] = silu(wide[strip]).astype(BF16)
         wide[rows] = jnp.dot(hidden[rows], w2_ref[...], preferred_element_type=F32)
-    near_spare, far_spare = near_ref.shape[0] - 1, far_ref.shape[0] - 1
     for number, rows in enumerate(spans):
         for strip in strips(rows):
             latent_ref[strip] = layer_norm(wide[strip], gain_ref[...]).astype(BF16)
         for b in range(number * PART, (number + 1) * PART):
-            block = step * per_step + b
             weights = interp_ref[b].reshape(list_len * tile_rows, block_rows)
             latent = latent_ref[b * block_rows : (b + 1) * block_rows]
             part = jnp.dot(weights, latent, preferred_element_type=F32)
             for k in range(list_len):
-                place, tile = spot(0, block, k)
-                mask = mask_ref[k, me * blk_count + block]
-                table_ref[0, place] = tile
-                across = (place >= groups * slots).astype(jnp.int32)
-                near = place - across * slots
-                beyond = place - across * groups * slots >= (groups - 1) * slots
-                table_ref[2, block * list_len + k] = jnp.where(beyond, tile, near)
-                table_ref[3, block * list_len + k] = mask * jnp.where(beyond, 2 + across, 1)
-                there, its_tile = spot(1, block, k)
-                table_ref[1, there] = its_tile
-                masked = part[k * tile_rows : (k + 1) * tile_rows] * mask.astype(F32)
-                masked = masked.astype(BF16)
-                near_ref[jnp.minimum(place, near_spare)] = masked
-                far_ref[jnp.where(place < near_spare, far_spare, place - near_spare)] = masked
+                number_here = b * list_len + k
+                mask = places_ref[2, number_here].astype(F32)
+                masked = (part[k * tile_rows : (k + 1) * tile_rows] * mask).astype(BF16)
+                near_ref[places_ref[0, number_here]] = masked
+                far_ref[places_ref[1, number_here]] = masked
 
 
 def add_entries(total, table_ref, group, slots, kept, other, groups, first):
@@ -173,14 +183,13 @@
 
 
 def mesh_kernel(
-    latent_ref, up_ref, down_ref, gain_ref, own, came, neighbour, out_ref, first_ref, second_ref
+    latent_ref, up_ref, down_ref, gain_ref, own, came, neighbour, first_ref, second_ref
 ):
     total = own[0] + came[...].astype(F32) + neighbour[...].astype(F32)
     mesh_in = latent_ref[...].astype(F32) + total.reshape(latent_ref.shape)
     normed = layer_norm(mesh_in, gain_ref[...]).astype(BF16)
     hidden = silu(jnp.dot(normed, up_ref[...], preferred_element_type=F32)).astype(BF16)
     out = (mesh_in + jnp.dot(hidden, down_ref[...], preferred_element_type=F32)).astype(BF16)
-    out_ref[...] = out
     first_ref[...] = out
     second_ref[...] = out
 
@@ -190,10 +199,12 @@
 
 
 def pick_kernel(chosen, slots, groups, tile_rows, table_ref, *refs):
-    pieces, outs = refs[:-2], refs[-2:]
+    pieces, outs = refs[: len(chosen)], refs[len(chosen) :]
+    for out in outs[2:]:
+        out[...] = pieces[0][...]
     for number, group in enumerate(chosen):
         for slot in range(slots):
-            for way, out in enumerate(outs):
+            for way, out in enumerate(outs[:2]):
                 tile = table_ref[way, (way * groups + group) * slots + slot]
                 rows = pl.ds(pl.multiple_of(tile * tile_rows, tile_rows), tile_rows)
                 into = (number * slots + slot) * tile_rows
@@ -335,6 +346,7 @@
                 pltpu.VMEM((rows, width), F32),
                 pltpu.VMEM((rows, width), BF16),
                 pltpu.SMEM((2, n_band), jnp.int32),
+                pltpu.SMEM((3, per_step * list_len), jnp.int32),
             ],
         ),
         compiler_params=params(24),
@@ -425,11 +437,11 @@
             second = ring.over_second(token, distance)
 
     mesh_gain = mesh_gain.reshape(1, width)
-    mesh_out, piece, again = pl.pallas_call(
+    piece, again = pl.pallas_call(
         mesh_kernel,
-        out_shape=[shape((node_rows, width))] * 3,
+        out_shape=[shape((node_rows, width))] * 2,
         in_specs=[in_vmem] * 7,
-        out_specs=[in_vmem] * 3,
+        out_specs=[in_vmem] * 2,
         compiler_params=params(16),
         cost_estimate=cost(4 * node_rows * width * width, mesh_up, mesh_down),
         name="mesh_step",
@@ -438,15 +450,17 @@
     mine, theirs = [], []
 
     def pick(chosen, values):
-        out = shape((len(chosen) * slots * tile_rows, width))
+        outs = [shape((len(chosen) * slots * tile_rows, width))] * 2
+        if chosen == [0]:
+            outs.append(shape((node_rows, width)))
         picked = pl.pallas_call(
             functools.partial(pick_kernel, chosen, slots, chips, tile_rows),
-            out_shape=[out] * 2,
+            out_shape=outs,
             grid_spec=pltpu.PrefetchScalarGridSpec(
                 num_scalar_prefetch=1,
                 grid=(1,),
                 in_specs=[in_vmem] * len(values),
-                out_specs=[in_vmem] * 2,
+                out_specs=[in_vmem] * len(outs),
             ),
             compiler_params=params(8),
             cost_estimate=cost(0, *values),
@@ -454,9 +468,10 @@
         )(table, *values)
         mine.append(picked[0])
         theirs.append(ring.over_core(picked[1]))
+        return picked[-1]
 
     first = ring.over_first(piece, 1)
-    pick([0], [piece])
+    mesh_out = pick([0], [piece])
     second = ring.over_second(in_order(again, theirs[0]), 1)
     token = mine[0]
     for distance in range(1, far):

time: 73.4 us -> 72.1 us (0.982); the launches traced: 71.9 us -> 71.9 us
  transfers between devices with their start and end apart: 21 -> 21, of which waited for: 18 -> 17; matrix products, arithmetic and copies ran while one was open for 0% -> 0% of each run, Pallas kernels for 6% -> 7%
where the time goes in v18:
time: 72.1 us; the launch traced here: 71.9 us
  starting transfers between devices  28.5 us (40%)
  waiting for transfers between devices  21.4 us (30%)
  Pallas kernels  21.1 us (29%)
  between operations  0.79 us (1%)
    ppermute x14, starting transfers between devices, over(): return lax.ppermute(value, 'band', pairs)  25.8 us
    ppermute x14, waiting for transfers between devices, over(): return lax.ppermute(value, 'band', pairs)  17.4 us
    pallas_call x1, Pallas kernels, on_device(): pl.pallas_call(functools.partial(embed_kernel, ring, per_step, slots), ou...  9.83 us
    pallas_call x1, Pallas kernels, on_device(): pl.pallas_call(functools.partial(back_kernel, list_len), out_shape=shape(...  4.55 us
    ppermute x7, waiting for transfers between devices, over_core(): return lax.ppermute(value, 'band', [(i, i ^ 1) for i in range(self.n_band)])  3.97 us
    pallas_call x4, Pallas kernels, pick(): pl.pallas_call(functools.partial(pick_kernel, chosen, slots, chips, tile_...  3.11 us
    ppermute x7, starting transfers between devices, over_core(): return lax.ppermute(value, 'band', [(i, i ^ 1) for i in range(self.n_band)])  2.69 us
  transfers between devices with their start and end apart: 21, of which 17 were waited for; matrix products, arithmetic and copies ran while one was open for 0% of the time, Pallas kernels for 7%

profile of v18, /device:TPU:0, one launch (start us, length us, event | category | flops | bytes accessed | tf_op | source)
XLA Modules:
  0.0 71.9 jit_solution(14036712177419908988)
XLA Ops:
  0.6 9.8 %embed.1 = (bf16[4096,512]{1,0:T(8,128)(2,1)}, bf16[57,32,512]{2,1,0:T(8,128)(2,1)S(1)}, bf16[9,32,512]{2,1,0:T(8,128)(2,1)S(1)}, s32[4,64]{1,0:T(4,128)S(1)}) custom-call(s32[1]{0:T(128)} %bitcast.me_ref, s32[4,256]{1,0:T(4,128)} %bitcast.8, s32[4,256]{1,0:T(4,128)} %bitcast.9, bf16[227,4096]{1,0:T(8,128)(2,1)} %bitcast.7, bf16[227,512]{1,0:T(8,128)(2,1)} %w1_ref.1, ...), custom_call_target="tpu_custom_call" | custom-call | flops 3636461568 | bytes 2908160 | tf_op jit(solution)/shard_map/embed/pallas_call | solution.py:327
  10.9 1.2 %collective-permute-done.other = bf16[9,32,512]{2,1,0:T(8,128)(2,1)S(1)} collective-permute-done((bf16[9,32,512]{2,1,0:T(8,128)(2,1)S(1)}, bf16[9,32,512]{2,1,0:T(8,128)(2,1)S(1)}, u32[]{:S(2)}, u32[]{:S(2)}) %collective-permute-start) | collective-permute-done | bytes 294944 | tf_op jit(solution)/shard_map/ppermute | solution.py:53
  12.1 0.8 %far_sums.1 = (bf16[8,32,512]{2,1,0:T(8,128)(2,1)S(1)}, bf16[8,32,512]{2,1,0:T(8,128)(2,1)S(1)}, bf16[57,32,512]{2,1,0:T(8,128)(2,1)S(1)}) custom-call(s32[4,64]{1,0:T(4,128)S(1)} %get-tuple-element.20.table_ref, bf16[57,32,512]{2,1,0:T(8,128)(2,1)S(1)} %get-tuple-element.21.kept, ...), custom_call_target="tpu_custom_call", output_to_operand_aliasing={{2}: (1, {})} | custom-call | bytes 1867776 | tf_op jit(solution)/shard_map/far_sums/pallas_call | solution.py:376
  13.4 2.7 %collective-permute-start.2 = (bf16[8,32,512]{2,1,0:T(8,128)(2,1)S(1)}, bf16[8,32,512]{2,1,0:T(8,128)(2,1)S(1)}, u32[]{:S(2)}, u32[]{:S(2)}) collective-permute-start(bf16[8,32,512]{2,1,0:T(8,128)(2,1)S(1)} %get-tuple-element.24), channel_id=1, source_target_pairs={{0,5},{1,2},{2,1},{3,6},{4,9},{5,0},{6,3},{7,10},{8,13},{9,4},{10,... | collective-permute-start | bytes 786440 | tf_op jit(solution)/shard_map/ppermute | solution.py:62
  16.1 0.7 %collective-permute-done.1.other = bf16[57,32,512]{2,1,0:T(8,128)(2,1)S(1)} collective-permute-done((bf16[57,32,512]{2,1,0:T(8,128)(2,1)S(1)}, bf16[57,32,512]{2,1,0:T(8,128)(2,1)S(1)}, u32[]{:S(2)}, u32[]{:S(2)}) %collective-permute-start.1) | collective-permute-done | bytes 1867808 | tf_op jit(solution)/shard_map/ppermute | solution.py:53
  16.8 1.2 %own_sums.1.token.own = f32[6,8,32,512]{3,2,1,0:T(8,128)S(1)} custom-call(s32[4,64]{1,0:T(4,128)S(1)} %get-tuple-element.20.table_ref, bf16[57,32,512]{2,1,0:T(8,128)(2,1)S(1)} %get-tuple-element.23.kept, bf16[57,32,512]{2,1,0:T(8,128)(2,1)S(1)} %collective-permute-done.1.other), custom_call_target="tpu_custom_call" | custom-call | bytes 3735552 | tf_op jit(solution)/shard_map/own_sums/pallas_call | solution.py:392
  18.6 1.5 %collective-permute-done.2.came = bf16[8,32,512]{2,1,0:T(8,128)(2,1)S(1)} collective-permute-done((bf16[8,32,512]{2,1,0:T(8,128)(2,1)S(1)}, bf16[8,32,512]{2,1,0:T(8,128)(2,1)S(1)}, u32[]{:S(2)}, u32[]{:S(2)}) %collective-permute-start.2) | collective-permute-done | bytes 262176 | tf_op jit(solution)/shard_map/ppermute | solution.py:62
  20.2 2.0 %collective-permute-start.3 = (bf16[8,32,512]{2,1,0:T(8,128)(2,1)S(1)}, bf16[8,32,512]{2,1,0:T(8,128)(2,1)S(1)}, u32[]{:S(2)}, u32[]{:S(2)}) collective-permute-start(bf16[8,32,512]{2,1,0:T(8,128)(2,1)S(1)} %add_5.1.token), channel_id=1, source_target_pairs={{0,3},{1,4},{2,7},{3,0},{4,1},{5,8},{6,11},{7,2},{8,5},{9,12},{10,... | collective-permute-start | bytes 786440 | tf_op jit(solution)/shard_map/ppermute | solution.py:62
  23.0 2.1 %collective-permute-start.6 = (bf16[8,32,512]{2,1,0:T(8,128)(2,1)S(1)}, bf16[8,32,512]{2,1,0:T(8,128)(2,1)S(1)}, u32[]{:S(2)}, u32[]{:S(2)}) collective-permute-start(bf16[8,32,512]{2,1,0:T(8,128)(2,1)S(1)} %add_4.1.token), channel_id=1, source_target_pairs={{0,3},{1,4},{2,7},{3,0},{4,1},{5,8},{6,11},{7,2},{8,5},{9,12},{10,... | collective-permute-start | bytes 786440 | tf_op jit(solution)/shard_map/ppermute | solution.py:62
  25.1 1.2 %collective-permute-done.3.came = bf16[8,32,512]{2,1,0:T(8,128)(2,1)S(1)} collective-permute-done((bf16[8,32,512]{2,1,0:T(8,128)(2,1)S(1)}, bf16[8,32,512]{2,1,0:T(8,128)(2,1)S(1)}, u32[]{:S(2)}, u32[]{:S(2)}) %collective-permute-start.3) | collective-permute-done | bytes 262176 | tf_op jit(solution)/shard_map/ppermute | solution.py:62
  26.3 2.2 %collective-permute-start.5 = (bf16[8,32,512]{2,1,0:T(8,128)(2,1)S(1)}, bf16[8,32,512]{2,1,0:T(8,128)(2,1)S(1)}, u32[]{:S(2)}, u32[]{:S(2)}) collective-permute-start(bf16[8,32,512]{2,1,0:T(8,128)(2,1)S(1)} %add_3.1.token), channel_id=1, source_target_pairs={{0,5},{1,2},{2,1},{3,6},{4,9},{5,0},{6,3},{7,10},{8,13},{9,4},{10,... | collective-permute-start | bytes 786440 | tf_op jit(solution)/shard_map/ppermute | solution.py:62
  28.5 0.8 %collective-permute-done.6.came = bf16[8,32,512]{2,1,0:T(8,128)(2,1)S(1)} collective-permute-done((bf16[8,32,512]{2,1,0:T(8,128)(2,1)S(1)}, bf16[8,32,512]{2,1,0:T(8,128)(2,1)S(1)}, u32[]{:S(2)}, u32[]{:S(2)}) %collective-permute-start.6) | collective-permute-done | bytes 262176 | tf_op jit(solution)/shard_map/ppermute | solution.py:62
  29.4 2.4 %collective-permute-start.8 = (bf16[8,32,512]{2,1,0:T(8,128)(2,1)S(1)}, bf16[8,32,512]{2,1,0:T(8,128)(2,1)S(1)}, u32[]{:S(2)}, u32[]{:S(2)}) collective-permute-start(bf16[8,32,512]{2,1,0:T(8,128)(2,1)S(1)} %add_2.1.token), channel_id=1, source_target_pairs={{0,5},{1,2},{2,1},{3,6},{4,9},{5,0},{6,3},{7,10},{8,13},{9,4},{10,... | collective-permute-start | bytes 786440 | tf_op jit(solution)/shard_map/ppermute | solution.py:62
  32.6 2.0 %collective-permute-start.7 = (bf16[8,32,512]{2,1,0:T(8,128)(2,1)S(1)}, bf16[8,32,512]{2,1,0:T(8,128)(2,1)S(1)}, u32[]{:S(2)}, u32[]{:S(2)}) collective-permute-start(bf16[8,32,512]{2,1,0:T(8,128)(2,1)S(1)} %add_1.1), channel_id=1, source_target_pairs={{0,3},{1,4},{2,7},{3,0},{4,1},{5,8},{6,11},{7,2},{8,5},{9,12},{10,... | collective-permute-start | bytes 786440 | tf_op jit(solution)/shard_map/ppermute | solution.py:62
  34.6 1.6 %collective-permute-done.8.neighbour = bf16[8,32,512]{2,1,0:T(8,128)(2,1)S(1)} collective-permute-done((bf16[8,32,512]{2,1,0:T(8,128)(2,1)S(1)}, bf16[8,32,512]{2,1,0:T(8,128)(2,1)S(1)}, u32[]{:S(2)}, u32[]{:S(2)}) %collective-permute-start.8) | collective-permute-done | bytes 262176 | tf_op jit(solution)/shard_map/ppermute | solution.py:62
  36.2 2.5 %collective-permute-done.7.came = bf16[8,32,512]{2,1,0:T(8,128)(2,1)S(1)} collective-permute-done((bf16[8,32,512]{2,1,0:T(8,128)(2,1)S(1)}, bf16[8,32,512]{2,1,0:T(8,128)(2,1)S(1)}, u32[]{:S(2)}, u32[]{:S(2)}) %collective-permute-start.7) | collective-permute-done | bytes 262176 | tf_op jit(solution)/shard_map/ppermute | solution.py:62
  38.7 0.7 %mesh_step.1 = (bf16[256,512]{1,0:T(8,128)(2,1)S(1)}, bf16[256,512]{1,0:T(8,128)(2,1)S(1)}) custom-call(bf16[256,512]{1,0:T(8,128)(2,1)S(1)} %copy-done.3, bf16[512,512]{1,0:T(8,128)(2,1)S(1)} %copy-done.1, bf16[512,512]{1,0:T(8,128)(2,1)S(1)} %copy-done.2, f32[1,512]{1,0:T(1,128)S(1)} %bitcast.6, f32[6,8,32,512]{3,2,1,0:T(8,128)S(1)} %own_sums.1.token.own, ...), custom_call_target="tpu_custom_call" | custom-call | flops 268435456 | bytes 1048576 | tf_op jit(solution)/shard_map/mesh_step/pallas_call | solution.py:440
  39.5 1.9 %collective-permute-start.9 = (bf16[256,512]{1,0:T(8,128)(2,1)S(1)}, bf16[256,512]{1,0:T(8,128)(2,1)S(1)}, u32[]{:S(2)}, u32[]{:S(2)}) collective-permute-start(bf16[256,512]{1,0:T(8,128)(2,1)S(1)} %get-tuple-element.26.refs_0_), channel_id=1, source_target_pairs={{0,3},{1,4},{2,7},{3,0},{4,1},{5,8},{6,11},{7,2},{8,5},{9,12},{10,... | collective-permute-start | bytes 786440 | tf_op jit(solution)/shard_map/ppermute | solution.py:62
  41.4 1.3 %pick_0.1 = (bf16[128,512]{1,0:T(8,128)(2,1)S(1)}, bf16[128,512]{1,0:T(8,128)(2,1)S(1)}, bf16[256,512]{1,0:T(8,128)(2,1)}) custom-call(s32[4,64]{1,0:T(4,128)S(1)} %get-tuple-element.20.table_ref, bf16[256,512]{1,0:T(8,128)(2,1)S(1)} %get-tuple-element.26.refs_0_), custom_call_target="tpu_custom_call" | custom-call | bytes 262144 | tf_op jit(solution)/shard_map/pick_0/pallas_call | solution.py:456
  43.2 1.0 %collective-permute-done.10.refs_1_.refs_4_ = bf16[128,512]{1,0:T(8,128)(2,1)S(1)} collective-permute-done((bf16[128,512]{1,0:T(8,128)(2,1)S(1)}, bf16[128,512]{1,0:T(8,128)(2,1)S(1)}, u32[]{:S(2)}, u32[]{:S(2)}) %collective-permute-start.10) | collective-permute-done | bytes 131104 | tf_op jit(solution)/shard_map/ppermute | solution.py:53
  44.2 1.6 %collective-permute-start.11 = (bf16[256,512]{1,0:T(8,128)(2,1)S(1)}, bf16[256,512]{1,0:T(8,128)(2,1)S(1)}, u32[]{:S(2)}, u32[]{:S(2)}) collective-permute-start(bf16[256,512]{1,0:T(8,128)(2,1)S(1)} %in_order.8), channel_id=1, source_target_pairs={{0,5},{1,2},{2,1},{3,6},{4,9},{5,0},{6,3},{7,10},{8,13},{9,4},{10,... | collective-permute-start | bytes 786440 | tf_op jit(solution)/shard_map/ppermute | solution.py:62
  45.8 1.6 %collective-permute-start.12 = (bf16[256,512]{1,0:T(8,128)(2,1)S(1)}, bf16[256,512]{1,0:T(8,128)(2,1)S(1)}, u32[]{:S(2)}, u32[]{:S(2)}) collective-permute-start(bf16[256,512]{1,0:T(8,128)(2,1)S(1)} %in_order.7.refs_1_.refs_0_), channel_id=1, source_target_pairs={{0,5},{1,2},{2,1},{3,6},{4,9},{5,0},{6,3},{7,10},{8,13},{9,4},{10,... | collective-permute-start | bytes 786440 | tf_op jit(solution)/shard_map/ppermute | solution.py:62
  47.3 2.7 %collective-permute-done.11.refs_0_ = bf16[256,512]{1,0:T(8,128)(2,1)S(1)} collective-permute-done((bf16[256,512]{1,0:T(8,128)(2,1)S(1)}, bf16[256,512]{1,0:T(8,128)(2,1)S(1)}, u32[]{:S(2)}, u32[]{:S(2)}) %collective-permute-start.11) | collective-permute-done | bytes 262176 | tf_op jit(solution)/shard_map/ppermute | solution.py:62
  50.0 1.5 %collective-permute-start.13 = (bf16[256,512]{1,0:T(8,128)(2,1)S(1)}, bf16[256,512]{1,0:T(8,128)(2,1)S(1)}, u32[]{:S(2)}, u32[]{:S(2)}) collective-permute-start(bf16[256,512]{1,0:T(8,128)(2,1)S(1)} %in_order.9.refs_1_), channel_id=1, source_target_pairs={{0,3},{1,4},{2,7},{3,0},{4,1},{5,8},{6,11},{7,2},{8,5},{9,12},{10,... | collective-permute-start | bytes 786440 | tf_op jit(solution)/shard_map/ppermute | solution.py:62
  52.1 0.7 %collective-permute-done.12.refs_0_ = bf16[256,512]{1,0:T(8,128)(2,1)S(1)} collective-permute-done((bf16[256,512]{1,0:T(8,128)(2,1)S(1)}, bf16[256,512]{1,0:T(8,128)(2,1)S(1)}, u32[]{:S(2)}, u32[]{:S(2)}) %collective-permute-start.12) | collective-permute-done | bytes 262176 | tf_op jit(solution)/shard_map/ppermute | solution.py:62
  52.8 1.5 %collective-permute-start.14 = (bf16[256,512]{1,0:T(8,128)(2,1)S(1)}, bf16[256,512]{1,0:T(8,128)(2,1)S(1)}, u32[]{:S(2)}, u32[]{:S(2)}) collective-permute-start(bf16[256,512]{1,0:T(8,128)(2,1)S(1)} %in_order.10.refs_1_.refs_0_), channel_id=1, source_target_pairs={{0,3},{1,4},{2,7},{3,0},{4,1},{5,8},{6,11},{7,2},{8,5},{9,12},{10,... | collective-permute-start | bytes 786440 | tf_op jit(solution)/shard_map/ppermute | solution.py:62
  54.4 1.8 %collective-permute-done.13.refs_0_ = bf16[256,512]{1,0:T(8,128)(2,1)S(1)} collective-permute-done((bf16[256,512]{1,0:T(8,128)(2,1)S(1)}, bf16[256,512]{1,0:T(8,128)(2,1)S(1)}, u32[]{:S(2)}, u32[]{:S(2)}) %collective-permute-start.13) | collective-permute-done | bytes 262176 | tf_op jit(solution)/shard_map/ppermute | solution.py:62
  56.2 1.8 %collective-permute-start.15 = (bf16[256,512]{1,0:T(8,128)(2,1)S(1)}, bf16[256,512]{1,0:T(8,128)(2,1)S(1)}, u32[]{:S(2)}, u32[]{:S(2)}) collective-permute-start(bf16[256,512]{1,0:T(8,128)(2,1)S(1)} %in_order.11.refs_1_), channel_id=1, source_target_pairs={{0,5},{1,2},{2,1},{3,6},{4,9},{5,0},{6,3},{7,10},{8,13},{9,4},{10,... | collective-permute-start | bytes 786440 | tf_op jit(solution)/shard_map/ppermute | solution.py:62
  59.0 2.5 %collective-permute-start.19 = (bf16[256,512]{1,0:T(8,128)(2,1)S(1)}, bf16[256,512]{1,0:T(8,128)(2,1)S(1)}, u32[]{:S(2)}, u32[]{:S(2)}) collective-permute-start(bf16[256,512]{1,0:T(8,128)(2,1)S(1)} %in_order.12.refs_1_.refs_0_), channel_id=1, source_target_pairs={{0,5},{1,2},{2,1},{3,6},{4,9},{5,0},{6,3},{7,10},{8,13},{9,4},{10,... | collective-permute-start | bytes 786440 | tf_op jit(solution)/shard_map/ppermute | solution.py:62
  63.4 2.2 %collective-permute-done.19.mine_ref = bf16[256,512]{1,0:T(8,128)(2,1)S(1)} collective-permute-done((bf16[256,512]{1,0:T(8,128)(2,1)S(1)}, bf16[256,512]{1,0:T(8,128)(2,1)S(1)}, u32[]{:S(2)}, u32[]{:S(2)}) %collective-permute-start.19) | collective-permute-done | bytes 262176 | tf_op jit(solution)/shard_map/ppermute | solution.py:62
  66.3 1.0 %collective-permute-done.20.theirs_ref = bf16[256,512]{1,0:T(8,128)(2,1)S(1)} collective-permute-done((bf16[256,512]{1,0:T(8,128)(2,1)S(1)}, bf16[256,512]{1,0:T(8,128)(2,1)S(1)}, u32[]{:S(2)}, u32[]{:S(2)}) %collective-permute-start.20) | collective-permute-done | bytes 262176 | tf_op jit(solution)/shard_map/ppermute | solution.py:53
  67.3 4.6 %back.1 = bf16[4096,512]{1,0:T(8,128)(2,1)} custom-call(s32[4,64]{1,0:T(4,128)S(1)} %get-tuple-element.20.table_ref, bf16[16,256,128]{2,1,0:T(8,128)(2,1)S(1)} %turn.1.token.weights_ref, bf16[1792,512]{1,0:T(8,128)(2,1)S(1)} %join.1.near_ref, bf16[256,512]{1,0:T(8,128)(2,1)S(1)} %collective-permute-done.19.mine_ref, ...), custom_call_target="tpu_custom_call" | custom-call | flops 536870912 | bytes 9437184 | tf_op jit(solution)/shard_map/back/pallas_call | solution.py:498
  (43 shorter events, 7.9 us)
Async XLA Ops:
  10.5 1.7 %collective-permute-start = (bf16[9,32,512]{2,1,0:T(8,128)(2,1)S(1)}, bf16[9,32,512]{2,1,0:T(8,128)(2,1)S(1)}, u32[]{:S(2)}, u32[]{:S(2)}) collective-permute-start(bf16[9,32,512]{2,1,0:T(8,128)(2,1)S(1)} %get-tuple-element.22), channel_id=1, source_target_pairs={{0,1},{1,0},{2,3},{3,2},{4,5},{5,4},{6,7},{7,6},{8,9},{9,8},{10,11... | collective-permute-start | bytes 884744 | tf_op jit(solution)/shard_map/ppermute | solution.py:53
  12.9 3.9 %collective-permute-start.1 = (bf16[57,32,512]{2,1,0:T(8,128)(2,1)S(1)}, bf16[57,32,512]{2,1,0:T(8,128)(2,1)S(1)}, u32[]{:S(2)}, u32[]{:S(2)}) collective-permute-start(bf16[57,32,512]{2,1,0:T(8,128)(2,1)S(1)} %get-tuple-element.23.kept), channel_id=1, source_target_pairs={{0,1},{1,0},{2,3},{3,2},{4,5},{5,4},{6,7},{7,6},{8,9},{9,8},{10,11... | collective-permute-start | bytes 5603336 | tf_op jit(solution)/shard_map/ppermute | solution.py:53
  13.4 6.7 %collective-permute-start.2 = (bf16[8,32,512]{2,1,0:T(8,128)(2,1)S(1)}, bf16[8,32,512]{2,1,0:T(8,128)(2,1)S(1)}, u32[]{:S(2)}, u32[]{:S(2)}) collective-permute-start(bf16[8,32,512]{2,1,0:T(8,128)(2,1)S(1)} %get-tuple-element.24), channel_id=1, source_target_pairs={{0,5},{1,2},{2,1},{3,6},{4,9},{5,0},{6,3},{7,10},{8,13},{9,4},{10,... | collective-permute-start | bytes 786440 | tf_op jit(solution)/shard_map/ppermute | solution.py:62
  16.0 2.0 %copy-start = (bf16[16,4,32,256]{3,2,1,0:T(8,128)(2,1)S(1)}, bf16[16,4,32,256]{3,2,1,0:T(8,128)(2,1)}, u32[]{:S(2)}) copy-start(bf16[16,4,32,256]{3,2,1,0:T(8,128)(2,1)} %interp_ref.3) | copy-start | bytes 3145732
  16.1 6.9 %collective-permute-start.4 = (bf16[8,32,512]{2,1,0:T(8,128)(2,1)S(1)}, bf16[8,32,512]{2,1,0:T(8,128)(2,1)S(1)}, u32[]{:S(2)}, u32[]{:S(2)}) collective-permute-start(bf16[8,32,512]{2,1,0:T(8,128)(2,1)S(1)} %get-tuple-element.25), channel_id=1, source_target_pairs={{0,5},{1,2},{2,1},{3,6},{4,9},{5,0},{6,3},{7,10},{8,13},{9,4},{10,... | collective-permute-start | bytes 786440 | tf_op jit(solution)/shard_map/ppermute | solution.py:62
  20.2 6.1 %collective-permute-start.3 = (bf16[8,32,512]{2,1,0:T(8,128)(2,1)S(1)}, bf16[8,32,512]{2,1,0:T(8,128)(2,1)S(1)}, u32[]{:S(2)}, u32[]{:S(2)}) collective-permute-start(bf16[8,32,512]{2,1,0:T(8,128)(2,1)S(1)} %add_5.1.token), channel_id=1, source_target_pairs={{0,3},{1,4},{2,7},{3,0},{4,1},{5,8},{6,11},{7,2},{8,5},{9,12},{10,... | collective-permute-start | bytes 786440 | tf_op jit(solution)/shard_map/ppermute | solution.py:62
  23.0 6.3 %collective-permute-start.6 = (bf16[8,32,512]{2,1,0:T(8,128)(2,1)S(1)}, bf16[8,32,512]{2,1,0:T(8,128)(2,1)S(1)}, u32[]{:S(2)}, u32[]{:S(2)}) collective-permute-start(bf16[8,32,512]{2,1,0:T(8,128)(2,1)S(1)} %add_4.1.token), channel_id=1, source_target_pairs={{0,3},{1,4},{2,7},{3,0},{4,1},{5,8},{6,11},{7,2},{8,5},{9,12},{10,... | collective-permute-start | bytes 786440 | tf_op jit(solution)/shard_map/ppermute | solution.py:62
  26.3 6.2 %collective-permute-start.5 = (bf16[8,32,512]{2,1,0:T(8,128)(2,1)S(1)}, bf16[8,32,512]{2,1,0:T(8,128)(2,1)S(1)}, u32[]{:S(2)}, u32[]{:S(2)}) collective-permute-start(bf16[8,32,512]{2,1,0:T(8,128)(2,1)S(1)} %add_3.1.token), channel_id=1, source_target_pairs={{0,5},{1,2},{2,1},{3,6},{4,9},{5,0},{6,3},{7,10},{8,13},{9,4},{10,... | collective-permute-start | bytes 786440 | tf_op jit(solution)/shard_map/ppermute | solution.py:62
  29.4 9.3 %copy-start.1 = (bf16[512,512]{1,0:T(8,128)(2,1)S(1)}, bf16[512,512]{1,0:T(8,128)(2,1)}, u32[]{:S(2)}) copy-start(bf16[512,512]{1,0:T(8,128)(2,1)} %up_ref.1) | copy-start | bytes 1572868
  29.4 9.3 %copy-start.2 = (bf16[512,512]{1,0:T(8,128)(2,1)S(1)}, bf16[512,512]{1,0:T(8,128)(2,1)}, u32[]{:S(2)}) copy-start(bf16[512,512]{1,0:T(8,128)(2,1)} %down_ref.1) | copy-start | bytes 1572868
  29.4 9.3 %copy-start.3 = (bf16[256,512]{1,0:T(8,128)(2,1)S(1)}, bf16[256,512]{1,0:T(8,128)(2,1)}, u32[]{:S(2)}) copy-start(bf16[256,512]{1,0:T(8,128)(2,1)} %latent_ref.1) | copy-start | bytes 786436
  29.4 9.3 %copy-start.4 = (f32[512]{0:T(512)S(1)}, f32[512]{0:T(512)}, u32[]{:S(2)}) copy-start(f32[512]{0:T(512)} %param.21) | copy-start | bytes 6148
  29.4 6.8 %collective-permute-start.8 = (bf16[8,32,512]{2,1,0:T(8,128)(2,1)S(1)}, bf16[8,32,512]{2,1,0:T(8,128)(2,1)S(1)}, u32[]{:S(2)}, u32[]{:S(2)}) collective-permute-start(bf16[8,32,512]{2,1,0:T(8,128)(2,1)S(1)} %add_2.1.token), channel_id=1, source_target_pairs={{0,5},{1,2},{2,1},{3,6},{4,9},{5,0},{6,3},{7,10},{8,13},{9,4},{10,... | collective-permute-start | bytes 786440 | tf_op jit(solution)/shard_map/ppermute | solution.py:62
  32.6 6.1 %collective-permute-start.7 = (bf16[8,32,512]{2,1,0:T(8,128)(2,1)S(1)}, bf16[8,32,512]{2,1,0:T(8,128)(2,1)S(1)}, u32[]{:S(2)}, u32[]{:S(2)}) collective-permute-start(bf16[8,32,512]{2,1,0:T(8,128)(2,1)S(1)} %add_1.1), channel_id=1, source_target_pairs={{0,3},{1,4},{2,7},{3,0},{4,1},{5,8},{6,11},{7,2},{8,5},{9,12},{10,... | collective-permute-start | bytes 786440 | tf_op jit(solution)/shard_map/ppermute | solution.py:62
  39.5 6.3 %collective-permute-start.9 = (bf16[256,512]{1,0:T(8,128)(2,1)S(1)}, bf16[256,512]{1,0:T(8,128)(2,1)S(1)}, u32[]{:S(2)}, u32[]{:S(2)}) collective-permute-start(bf16[256,512]{1,0:T(8,128)(2,1)S(1)} %get-tuple-element.26.refs_0_), channel_id=1, source_target_pairs={{0,3},{1,4},{2,7},{3,0},{4,1},{5,8},{6,11},{7,2},{8,5},{9,12},{10,... | collective-permute-start | bytes 786440 | tf_op jit(solution)/shard_map/ppermute | solution.py:62
  42.7 1.5 %collective-permute-start.10 = (bf16[128,512]{1,0:T(8,128)(2,1)S(1)}, bf16[128,512]{1,0:T(8,128)(2,1)S(1)}, u32[]{:S(2)}, u32[]{:S(2)}) collective-permute-start(bf16[128,512]{1,0:T(8,128)(2,1)S(1)} %get-tuple-element.29), channel_id=1, source_target_pairs={{0,1},{1,0},{2,3},{3,2},{4,5},{5,4},{6,7},{7,6},{8,9},{9,8},{10,11... | collective-permute-start | bytes 393224 | tf_op jit(solution)/shard_map/ppermute | solution.py:53
  44.2 5.8 %collective-permute-start.11 = (bf16[256,512]{1,0:T(8,128)(2,1)S(1)}, bf16[256,512]{1,0:T(8,128)(2,1)S(1)}, u32[]{:S(2)}, u32[]{:S(2)}) collective-permute-start(bf16[256,512]{1,0:T(8,128)(2,1)S(1)} %in_order.8), channel_id=1, source_target_pairs={{0,5},{1,2},{2,1},{3,6},{4,9},{5,0},{6,3},{7,10},{8,13},{9,4},{10,... | collective-permute-start | bytes 786440 | tf_op jit(solution)/shard_map/ppermute | solution.py:62
  45.8 7.0 %collective-permute-start.12 = (bf16[256,512]{1,0:T(8,128)(2,1)S(1)}, bf16[256,512]{1,0:T(8,128)(2,1)S(1)}, u32[]{:S(2)}, u32[]{:S(2)}) collective-permute-start(bf16[256,512]{1,0:T(8,128)(2,1)S(1)} %in_order.7.refs_1_.refs_0_), channel_id=1, source_target_pairs={{0,5},{1,2},{2,1},{3,6},{4,9},{5,0},{6,3},{7,10},{8,13},{9,4},{10,... | collective-permute-start | bytes 786440 | tf_op jit(solution)/shard_map/ppermute | solution.py:62
  50.0 6.2 %collective-permute-start.13 = (bf16[256,512]{1,0:T(8,128)(2,1)S(1)}, bf16[256,512]{1,0:T(8,128)(2,1)S(1)}, u32[]{:S(2)}, u32[]{:S(2)}) collective-permute-start(bf16[256,512]{1,0:T(8,128)(2,1)S(1)} %in_order.9.refs_1_), channel_id=1, source_target_pairs={{0,3},{1,4},{2,7},{3,0},{4,1},{5,8},{6,11},{7,2},{8,5},{9,12},{10,... | collective-permute-start | bytes 786440 | tf_op jit(solution)/shard_map/ppermute | solution.py:62
  52.8 6.2 %collective-permute-start.14 = (bf16[256,512]{1,0:T(8,128)(2,1)S(1)}, bf16[256,512]{1,0:T(8,128)(2,1)S(1)}, u32[]{:S(2)}, u32[]{:S(2)}) collective-permute-start(bf16[256,512]{1,0:T(8,128)(2,1)S(1)} %in_order.10.refs_1_.refs_0_), channel_id=1, source_target_pairs={{0,3},{1,4},{2,7},{3,0},{4,1},{5,8},{6,11},{7,2},{8,5},{9,12},{10,... | collective-permute-start | bytes 786440 | tf_op jit(solution)/shard_map/ppermute | solution.py:62
  56.2 6.4 %collective-permute-start.15 = (bf16[256,512]{1,0:T(8,128)(2,1)S(1)}, bf16[256,512]{1,0:T(8,128)(2,1)S(1)}, u32[]{:S(2)}, u32[]{:S(2)}) collective-permute-start(bf16[256,512]{1,0:T(8,128)(2,1)S(1)} %in_order.11.refs_1_), channel_id=1, source_target_pairs={{0,5},{1,2},{2,1},{3,6},{4,9},{5,0},{6,3},{7,10},{8,13},{9,4},{10,... | collective-permute-start | bytes 786440 | tf_op jit(solution)/shard_map/ppermute | solution.py:62
  59.0 6.6 %collective-permute-start.19 = (bf16[256,512]{1,0:T(8,128)(2,1)S(1)}, bf16[256,512]{1,0:T(8,128)(2,1)S(1)}, u32[]{:S(2)}, u32[]{:S(2)}) collective-permute-start(bf16[256,512]{1,0:T(8,128)(2,1)S(1)} %in_order.12.refs_1_.refs_0_), channel_id=1, source_target_pairs={{0,5},{1,2},{2,1},{3,6},{4,9},{5,0},{6,3},{7,10},{8,13},{9,4},{10,... | collective-permute-start | bytes 786440 | tf_op jit(solution)/shard_map/ppermute | solution.py:62
  61.5 4.6 %collective-permute-start.16 = (bf16[256,512]{1,0:T(8,128)(2,1)S(1)}, bf16[256,512]{1,0:T(8,128)(2,1)S(1)}, u32[]{:S(2)}, u32[]{:S(2)}) collective-permute-start(bf16[256,512]{1,0:T(8,128)(2,1)S(1)} %get-tuple-element.33), channel_id=1, source_target_pairs={{0,1},{1,0},{2,3},{3,2},{4,5},{5,4},{6,7},{7,6},{8,9},{9,8},{10,11... | collective-permute-start | bytes 786440 | tf_op jit(solution)/shard_map/ppermute | solution.py:53
  61.5 4.6 %collective-permute-start.17 = (bf16[256,512]{1,0:T(8,128)(2,1)S(1)}, bf16[256,512]{1,0:T(8,128)(2,1)S(1)}, u32[]{:S(2)}, u32[]{:S(2)}) collective-permute-start(bf16[256,512]{1,0:T(8,128)(2,1)S(1)} %get-tuple-element.34), channel_id=1, source_target_pairs={{0,1},{1,0},{2,3},{3,2},{4,5},{5,4},{6,7},{7,6},{8,9},{9,8},{10,11... | collective-permute-start | bytes 786440 | tf_op jit(solution)/shard_map/ppermute | solution.py:53
  63.2 3.0 %collective-permute-start.18 = (bf16[256,512]{1,0:T(8,128)(2,1)S(1)}, bf16[256,512]{1,0:T(8,128)(2,1)S(1)}, u32[]{:S(2)}, u32[]{:S(2)}) collective-permute-start(bf16[256,512]{1,0:T(8,128)(2,1)S(1)} %get-tuple-element.35), channel_id=1, source_target_pairs={{0,1},{1,0},{2,3},{3,2},{4,5},{5,4},{6,7},{7,6},{8,9},{9,8},{10,11... | collective-permute-start | bytes 786440 | tf_op jit(solution)/shard_map/ppermute | solution.py:53
  65.6 1.7 %collective-permute-start.20 = (bf16[256,512]{1,0:T(8,128)(2,1)S(1)}, bf16[256,512]{1,0:T(8,128)(2,1)S(1)}, u32[]{:S(2)}, u32[]{:S(2)}) collective-permute-start(bf16[256,512]{1,0:T(8,128)(2,1)S(1)} %collective-permute-done.19.mine_ref), channel_id=1, source_target_pairs={{0,1},{1,0},{2,3},{3,2},{4,5},{5,4},{6,7},{7,6},{8,9},{9,8},{10,11... | collective-permute-start | bytes 786440 | tf_op jit(solution)/shard_map/ppermute | solution.py:53

commit v19 on v18

--- a/solution.py
+++ b/solution.py
@@ -11,7 +11,7 @@
 BF16 = jnp.bfloat16
 N_CORE = 2
 STRIP = 32
-PART = 2
+PART = 4
 BACK_PART = 4
 
 

time: 72.1 us -> 72.5 us (level)
  no operation moved by 1% of the time
where the time goes in v19:
time: 72.5 us; the launch traced here: 72.3 us
  starting transfers between devices  28.7 us (40%)
  Pallas kernels  21.6 us (30%)
  waiting for transfers between devices  21.3 us (29%)
  between operations  0.79 us (1%)
    ppermute x14, starting transfers between devices, over(): return lax.ppermute(value, 'band', pairs)  25.7 us
    ppermute x14, waiting for transfers between devices, over(): return lax.ppermute(value, 'band', pairs)  17.3 us
    pallas_call x1, Pallas kernels, on_device(): pl.pallas_call(functools.partial(embed_kernel, ring, per_step, slots), ou...  10.3 us
    pallas_call x1, Pallas kernels, on_device(): pl.pallas_call(functools.partial(back_kernel, list_len), out_shape=shape(...  4.57 us
    ppermute x7, waiting for transfers between devices, over_core(): return lax.ppermute(value, 'band', [(i, i ^ 1) for i in range(self.n_band)])  3.98 us
    pallas_call x4, Pallas kernels, pick(): pl.pallas_call(functools.partial(pick_kernel, chosen, slots, chips, tile_...  3.11 us
    ppermute x7, starting transfers between devices, over_core(): return lax.ppermute(value, 'band', [(i, i ^ 1) for i in range(self.n_band)])  2.93 us
  transfers between devices with their start and end apart: 21, of which 17 were waited for; matrix products, arithmetic and copies ran while one was open for 0% of the time, Pallas kernels for 7%

profile of v19, /device:TPU:0, one launch (start us, length us, event | category | flops | bytes accessed | tf_op | source)
XLA Modules:
  0.0 72.3 jit_solution(15247191985940292275)
XLA Ops:
  0.6 10.3 %embed.1 = (bf16[4096,512]{1,0:T(8,128)(2,1)}, bf16[57,32,512]{2,1,0:T(8,128)(2,1)S(1)}, bf16[9,32,512]{2,1,0:T(8,128)(2,1)S(1)}, s32[4,64]{1,0:T(4,128)S(1)}) custom-call(s32[1]{0:T(128)} %bitcast.me_ref, s32[4,256]{1,0:T(4,128)} %bitcast.8, s32[4,256]{1,0:T(4,128)} %bitcast.9, bf16[227,4096]{1,0:T(8,128)(2,1)} %bitcast.7, bf16[227,512]{1,0:T(8,128)(2,1)} %w1_ref.1, ...), custom_call_target="tpu_custom_call" | custom-call | flops 3636461568 | bytes 2908160 | tf_op jit(solution)/shard_map/embed/pallas_call | solution.py:327
  11.3 1.2 %collective-permute-done.other = bf16[9,32,512]{2,1,0:T(8,128)(2,1)S(1)} collective-permute-done((bf16[9,32,512]{2,1,0:T(8,128)(2,1)S(1)}, bf16[9,32,512]{2,1,0:T(8,128)(2,1)S(1)}, u32[]{:S(2)}, u32[]{:S(2)}) %collective-permute-start) | collective-permute-done | bytes 294944 | tf_op jit(solution)/shard_map/ppermute | solution.py:53
  12.6 0.8 %far_sums.1 = (bf16[8,32,512]{2,1,0:T(8,128)(2,1)S(1)}, bf16[8,32,512]{2,1,0:T(8,128)(2,1)S(1)}, bf16[57,32,512]{2,1,0:T(8,128)(2,1)S(1)}) custom-call(s32[4,64]{1,0:T(4,128)S(1)} %get-tuple-element.20.table_ref, bf16[57,32,512]{2,1,0:T(8,128)(2,1)S(1)} %get-tuple-element.21.kept, ...), custom_call_target="tpu_custom_call", output_to_operand_aliasing={{2}: (1, {})} | custom-call | bytes 1867776 | tf_op jit(solution)/shard_map/far_sums/pallas_call | solution.py:376
  13.8 2.7 %collective-permute-start.2 = (bf16[8,32,512]{2,1,0:T(8,128)(2,1)S(1)}, bf16[8,32,512]{2,1,0:T(8,128)(2,1)S(1)}, u32[]{:S(2)}, u32[]{:S(2)}) collective-permute-start(bf16[8,32,512]{2,1,0:T(8,128)(2,1)S(1)} %get-tuple-element.24), channel_id=1, source_target_pairs={{0,5},{1,2},{2,1},{3,6},{4,9},{5,0},{6,3},{7,10},{8,13},{9,4},{10,... | collective-permute-start | bytes 786440 | tf_op jit(solution)/shard_map/ppermute | solution.py:62
  16.5 0.8 %collective-permute-done.1.other = bf16[57,32,512]{2,1,0:T(8,128)(2,1)S(1)} collective-permute-done((bf16[57,32,512]{2,1,0:T(8,128)(2,1)S(1)}, bf16[57,32,512]{2,1,0:T(8,128)(2,1)S(1)}, u32[]{:S(2)}, u32[]{:S(2)}) %collective-permute-start.1) | collective-permute-done | bytes 1867808 | tf_op jit(solution)/shard_map/ppermute | solution.py:53
  17.3 1.2 %own_sums.1.token.own = f32[6,8,32,512]{3,2,1,0:T(8,128)S(1)} custom-call(s32[4,64]{1,0:T(4,128)S(1)} %get-tuple-element.20.table_ref, bf16[57,32,512]{2,1,0:T(8,128)(2,1)S(1)} %get-tuple-element.23.kept, bf16[57,32,512]{2,1,0:T(8,128)(2,1)S(1)} %collective-permute-done.1.other), custom_call_target="tpu_custom_call" | custom-call | bytes 3735552 | tf_op jit(solution)/shard_map/own_sums/pallas_call | solution.py:392
  19.0 1.5 %collective-permute-done.2.came = bf16[8,32,512]{2,1,0:T(8,128)(2,1)S(1)} collective-permute-done((bf16[8,32,512]{2,1,0:T(8,128)(2,1)S(1)}, bf16[8,32,512]{2,1,0:T(8,128)(2,1)S(1)}, u32[]{:S(2)}, u32[]{:S(2)}) %collective-permute-start.2) | collective-permute-done | bytes 262176 | tf_op jit(solution)/shard_map/ppermute | solution.py:62
  20.6 2.1 %collective-permute-start.3 = (bf16[8,32,512]{2,1,0:T(8,128)(2,1)S(1)}, bf16[8,32,512]{2,1,0:T(8,128)(2,1)S(1)}, u32[]{:S(2)}, u32[]{:S(2)}) collective-permute-start(bf16[8,32,512]{2,1,0:T(8,128)(2,1)S(1)} %add_5.1.token), channel_id=1, source_target_pairs={{0,3},{1,4},{2,7},{3,0},{4,1},{5,8},{6,11},{7,2},{8,5},{9,12},{10,... | collective-permute-start | bytes 786440 | tf_op jit(solution)/shard_map/ppermute | solution.py:62
  23.4 2.1 %collective-permute-start.6 = (bf16[8,32,512]{2,1,0:T(8,128)(2,1)S(1)}, bf16[8,32,512]{2,1,0:T(8,128)(2,1)S(1)}, u32[]{:S(2)}, u32[]{:S(2)}) collective-permute-start(bf16[8,32,512]{2,1,0:T(8,128)(2,1)S(1)} %add_4.1.token), channel_id=1, source_target_pairs={{0,3},{1,4},{2,7},{3,0},{4,1},{5,8},{6,11},{7,2},{8,5},{9,12},{10,... | collective-permute-start | bytes 786440 | tf_op jit(solution)/shard_map/ppermute | solution.py:62
  25.5 1.1 %collective-permute-done.3.came = bf16[8,32,512]{2,1,0:T(8,128)(2,1)S(1)} collective-permute-done((bf16[8,32,512]{2,1,0:T(8,128)(2,1)S(1)}, bf16[8,32,512]{2,1,0:T(8,128)(2,1)S(1)}, u32[]{:S(2)}, u32[]{:S(2)}) %collective-permute-start.3) | collective-permute-done | bytes 262176 | tf_op jit(solution)/shard_map/ppermute | solution.py:62
  26.7 2.1 %collective-permute-start.5 = (bf16[8,32,512]{2,1,0:T(8,128)(2,1)S(1)}, bf16[8,32,512]{2,1,0:T(8,128)(2,1)S(1)}, u32[]{:S(2)}, u32[]{:S(2)}) collective-permute-start(bf16[8,32,512]{2,1,0:T(8,128)(2,1)S(1)} %add_3.1.token), channel_id=1, source_target_pairs={{0,5},{1,2},{2,1},{3,6},{4,9},{5,0},{6,3},{7,10},{8,13},{9,4},{10,... | collective-permute-start | bytes 786440 | tf_op jit(solution)/shard_map/ppermute | solution.py:62
  28.9 0.9 %collective-permute-done.6.came = bf16[8,32,512]{2,1,0:T(8,128)(2,1)S(1)} collective-permute-done((bf16[8,32,512]{2,1,0:T(8,128)(2,1)S(1)}, bf16[8,32,512]{2,1,0:T(8,128)(2,1)S(1)}, u32[]{:S(2)}, u32[]{:S(2)}) %collective-permute-start.6) | collective-permute-done | bytes 262176 | tf_op jit(solution)/shard_map/ppermute | solution.py:62
  29.9 2.4 %collective-permute-start.8 = (bf16[8,32,512]{2,1,0:T(8,128)(2,1)S(1)}, bf16[8,32,512]{2,1,0:T(8,128)(2,1)S(1)}, u32[]{:S(2)}, u32[]{:S(2)}) collective-permute-start(bf16[8,32,512]{2,1,0:T(8,128)(2,1)S(1)} %add_2.1.token), channel_id=1, source_target_pairs={{0,5},{1,2},{2,1},{3,6},{4,9},{5,0},{6,3},{7,10},{8,13},{9,4},{10,... | collective-permute-start | bytes 786440 | tf_op jit(solution)/shard_map/ppermute | solution.py:62
  33.0 2.1 %collective-permute-start.7 = (bf16[8,32,512]{2,1,0:T(8,128)(2,1)S(1)}, bf16[8,32,512]{2,1,0:T(8,128)(2,1)S(1)}, u32[]{:S(2)}, u32[]{:S(2)}) collective-permute-start(bf16[8,32,512]{2,1,0:T(8,128)(2,1)S(1)} %add_1.1), channel_id=1, source_target_pairs={{0,3},{1,4},{2,7},{3,0},{4,1},{5,8},{6,11},{7,2},{8,5},{9,12},{10,... | collective-permute-start | bytes 786440 | tf_op jit(solution)/shard_map/ppermute | solution.py:62
  35.1 1.6 %collective-permute-done.8.neighbour = bf16[8,32,512]{2,1,0:T(8,128)(2,1)S(1)} collective-permute-done((bf16[8,32,512]{2,1,0:T(8,128)(2,1)S(1)}, bf16[8,32,512]{2,1,0:T(8,128)(2,1)S(1)}, u32[]{:S(2)}, u32[]{:S(2)}) %collective-permute-start.8) | collective-permute-done | bytes 262176 | tf_op jit(solution)/shard_map/ppermute | solution.py:62
  36.7 2.4 %collective-permute-done.7.came = bf16[8,32,512]{2,1,0:T(8,128)(2,1)S(1)} collective-permute-done((bf16[8,32,512]{2,1,0:T(8,128)(2,1)S(1)}, bf16[8,32,512]{2,1,0:T(8,128)(2,1)S(1)}, u32[]{:S(2)}, u32[]{:S(2)}) %collective-permute-start.7) | collective-permute-done | bytes 262176 | tf_op jit(solution)/shard_map/ppermute | solution.py:62
  39.1 0.7 %mesh_step.1 = (bf16[256,512]{1,0:T(8,128)(2,1)S(1)}, bf16[256,512]{1,0:T(8,128)(2,1)S(1)}) custom-call(bf16[256,512]{1,0:T(8,128)(2,1)S(1)} %copy-done.3, bf16[512,512]{1,0:T(8,128)(2,1)S(1)} %copy-done.1, bf16[512,512]{1,0:T(8,128)(2,1)S(1)} %copy-done.2, f32[1,512]{1,0:T(1,128)S(1)} %bitcast.6, f32[6,8,32,512]{3,2,1,0:T(8,128)S(1)} %own_sums.1.token.own, ...), custom_call_target="tpu_custom_call" | custom-call | flops 268435456 | bytes 1048576 | tf_op jit(solution)/shard_map/mesh_step/pallas_call | solution.py:440
  39.9 2.0 %collective-permute-start.9 = (bf16[256,512]{1,0:T(8,128)(2,1)S(1)}, bf16[256,512]{1,0:T(8,128)(2,1)S(1)}, u32[]{:S(2)}, u32[]{:S(2)}) collective-permute-start(bf16[256,512]{1,0:T(8,128)(2,1)S(1)} %get-tuple-element.26.refs_0_), channel_id=1, source_target_pairs={{0,3},{1,4},{2,7},{3,0},{4,1},{5,8},{6,11},{7,2},{8,5},{9,12},{10,... | collective-permute-start | bytes 786440 | tf_op jit(solution)/shard_map/ppermute | solution.py:62
  41.9 1.3 %pick_0.1 = (bf16[128,512]{1,0:T(8,128)(2,1)S(1)}, bf16[128,512]{1,0:T(8,128)(2,1)S(1)}, bf16[256,512]{1,0:T(8,128)(2,1)}) custom-call(s32[4,64]{1,0:T(4,128)S(1)} %get-tuple-element.20.table_ref, bf16[256,512]{1,0:T(8,128)(2,1)S(1)} %get-tuple-element.26.refs_0_), custom_call_target="tpu_custom_call" | custom-call | bytes 262144 | tf_op jit(solution)/shard_map/pick_0/pallas_call | solution.py:456
  43.7 1.0 %collective-permute-done.10.refs_1_.refs_4_ = bf16[128,512]{1,0:T(8,128)(2,1)S(1)} collective-permute-done((bf16[128,512]{1,0:T(8,128)(2,1)S(1)}, bf16[128,512]{1,0:T(8,128)(2,1)S(1)}, u32[]{:S(2)}, u32[]{:S(2)}) %collective-permute-start.10) | collective-permute-done | bytes 131104 | tf_op jit(solution)/shard_map/ppermute | solution.py:53
  44.6 1.5 %collective-permute-start.11 = (bf16[256,512]{1,0:T(8,128)(2,1)S(1)}, bf16[256,512]{1,0:T(8,128)(2,1)S(1)}, u32[]{:S(2)}, u32[]{:S(2)}) collective-permute-start(bf16[256,512]{1,0:T(8,128)(2,1)S(1)} %in_order.8), channel_id=1, source_target_pairs={{0,5},{1,2},{2,1},{3,6},{4,9},{5,0},{6,3},{7,10},{8,13},{9,4},{10,... | collective-permute-start | bytes 786440 | tf_op jit(solution)/shard_map/ppermute | solution.py:62
  46.2 1.6 %collective-permute-start.12 = (bf16[256,512]{1,0:T(8,128)(2,1)S(1)}, bf16[256,512]{1,0:T(8,128)(2,1)S(1)}, u32[]{:S(2)}, u32[]{:S(2)}) collective-permute-start(bf16[256,512]{1,0:T(8,128)(2,1)S(1)} %in_order.7.refs_1_.refs_0_), channel_id=1, source_target_pairs={{0,5},{1,2},{2,1},{3,6},{4,9},{5,0},{6,3},{7,10},{8,13},{9,4},{10,... | collective-permute-start | bytes 786440 | tf_op jit(solution)/shard_map/ppermute | solution.py:62
  47.8 2.7 %collective-permute-done.11.refs_0_ = bf16[256,512]{1,0:T(8,128)(2,1)S(1)} collective-permute-done((bf16[256,512]{1,0:T(8,128)(2,1)S(1)}, bf16[256,512]{1,0:T(8,128)(2,1)S(1)}, u32[]{:S(2)}, u32[]{:S(2)}) %collective-permute-start.11) | collective-permute-done | bytes 262176 | tf_op jit(solution)/shard_map/ppermute | solution.py:62
  50.4 1.5 %collective-permute-start.13 = (bf16[256,512]{1,0:T(8,128)(2,1)S(1)}, bf16[256,512]{1,0:T(8,128)(2,1)S(1)}, u32[]{:S(2)}, u32[]{:S(2)}) collective-permute-start(bf16[256,512]{1,0:T(8,128)(2,1)S(1)} %in_order.9.refs_1_), channel_id=1, source_target_pairs={{0,3},{1,4},{2,7},{3,0},{4,1},{5,8},{6,11},{7,2},{8,5},{9,12},{10,... | collective-permute-start | bytes 786440 | tf_op jit(solution)/shard_map/ppermute | solution.py:62
  52.5 0.7 %collective-permute-done.12.refs_0_ = bf16[256,512]{1,0:T(8,128)(2,1)S(1)} collective-permute-done((bf16[256,512]{1,0:T(8,128)(2,1)S(1)}, bf16[256,512]{1,0:T(8,128)(2,1)S(1)}, u32[]{:S(2)}, u32[]{:S(2)}) %collective-permute-start.12) | collective-permute-done | bytes 262176 | tf_op jit(solution)/shard_map/ppermute | solution.py:62
  53.3 1.5 %collective-permute-start.14 = (bf16[256,512]{1,0:T(8,128)(2,1)S(1)}, bf16[256,512]{1,0:T(8,128)(2,1)S(1)}, u32[]{:S(2)}, u32[]{:S(2)}) collective-permute-start(bf16[256,512]{1,0:T(8,128)(2,1)S(1)} %in_order.10.refs_1_.refs_0_), channel_id=1, source_target_pairs={{0,3},{1,4},{2,7},{3,0},{4,1},{5,8},{6,11},{7,2},{8,5},{9,12},{10,... | collective-permute-start | bytes 786440 | tf_op jit(solution)/shard_map/ppermute | solution.py:62
  54.8 1.8 %collective-permute-done.13.refs_0_ = bf16[256,512]{1,0:T(8,128)(2,1)S(1)} collective-permute-done((bf16[256,512]{1,0:T(8,128)(2,1)S(1)}, bf16[256,512]{1,0:T(8,128)(2,1)S(1)}, u32[]{:S(2)}, u32[]{:S(2)}) %collective-permute-start.13) | collective-permute-done | bytes 262176 | tf_op jit(solution)/shard_map/ppermute | solution.py:62
  56.6 1.7 %collective-permute-start.15 = (bf16[256,512]{1,0:T(8,128)(2,1)S(1)}, bf16[256,512]{1,0:T(8,128)(2,1)S(1)}, u32[]{:S(2)}, u32[]{:S(2)}) collective-permute-start(bf16[256,512]{1,0:T(8,128)(2,1)S(1)} %in_order.11.refs_1_), channel_id=1, source_target_pairs={{0,5},{1,2},{2,1},{3,6},{4,9},{5,0},{6,3},{7,10},{8,13},{9,4},{10,... | collective-permute-start | bytes 786440 | tf_op jit(solution)/shard_map/ppermute | solution.py:62
  59.4 2.5 %collective-permute-start.19 = (bf16[256,512]{1,0:T(8,128)(2,1)S(1)}, bf16[256,512]{1,0:T(8,128)(2,1)S(1)}, u32[]{:S(2)}, u32[]{:S(2)}) collective-permute-start(bf16[256,512]{1,0:T(8,128)(2,1)S(1)} %in_order.12.refs_1_.refs_0_), channel_id=1, source_target_pairs={{0,5},{1,2},{2,1},{3,6},{4,9},{5,0},{6,3},{7,10},{8,13},{9,4},{10,... | collective-permute-start | bytes 786440 | tf_op jit(solution)/shard_map/ppermute | solution.py:62
  64.0 2.0 %collective-permute-done.19.mine_ref = bf16[256,512]{1,0:T(8,128)(2,1)S(1)} collective-permute-done((bf16[256,512]{1,0:T(8,128)(2,1)S(1)}, bf16[256,512]{1,0:T(8,128)(2,1)S(1)}, u32[]{:S(2)}, u32[]{:S(2)}) %collective-permute-start.19) | collective-permute-done | bytes 262176 | tf_op jit(solution)/shard_map/ppermute | solution.py:62
  66.8 1.0 %collective-permute-done.20.theirs_ref = bf16[256,512]{1,0:T(8,128)(2,1)S(1)} collective-permute-done((bf16[256,512]{1,0:T(8,128)(2,1)S(1)}, bf16[256,512]{1,0:T(8,128)(2,1)S(1)}, u32[]{:S(2)}, u32[]{:S(2)}) %collective-permute-start.20) | collective-permute-done | bytes 262176 | tf_op jit(solution)/shard_map/ppermute | solution.py:53
  67.8 4.6 %back.1 = bf16[4096,512]{1,0:T(8,128)(2,1)} custom-call(s32[4,64]{1,0:T(4,128)S(1)} %get-tuple-element.20.table_ref, bf16[16,256,128]{2,1,0:T(8,128)(2,1)S(1)} %turn.1.token.weights_ref, bf16[1792,512]{1,0:T(8,128)(2,1)S(1)} %join.1.near_ref, bf16[256,512]{1,0:T(8,128)(2,1)S(1)} %collective-permute-done.19.mine_ref, ...), custom_call_target="tpu_custom_call" | custom-call | flops 536870912 | bytes 9437184 | tf_op jit(solution)/shard_map/back/pallas_call | solution.py:498
  (43 shorter events, 8.2 us)
Async XLA Ops:
  10.9 1.7 %collective-permute-start = (bf16[9,32,512]{2,1,0:T(8,128)(2,1)S(1)}, bf16[9,32,512]{2,1,0:T(8,128)(2,1)S(1)}, u32[]{:S(2)}, u32[]{:S(2)}) collective-permute-start(bf16[9,32,512]{2,1,0:T(8,128)(2,1)S(1)} %get-tuple-element.22), channel_id=1, source_target_pairs={{0,1},{1,0},{2,3},{3,2},{4,5},{5,4},{6,7},{7,6},{8,9},{9,8},{10,11... | collective-permute-start | bytes 884744 | tf_op jit(solution)/shard_map/ppermute | solution.py:53
  13.4 3.9 %collective-permute-start.1 = (bf16[57,32,512]{2,1,0:T(8,128)(2,1)S(1)}, bf16[57,32,512]{2,1,0:T(8,128)(2,1)S(1)}, u32[]{:S(2)}, u32[]{:S(2)}) collective-permute-start(bf16[57,32,512]{2,1,0:T(8,128)(2,1)S(1)} %get-tuple-element.23.kept), channel_id=1, source_target_pairs={{0,1},{1,0},{2,3},{3,2},{4,5},{5,4},{6,7},{7,6},{8,9},{9,8},{10,11... | collective-permute-start | bytes 5603336 | tf_op jit(solution)/shard_map/ppermute | solution.py:53
  13.8 6.7 %collective-permute-start.2 = (bf16[8,32,512]{2,1,0:T(8,128)(2,1)S(1)}, bf16[8,32,512]{2,1,0:T(8,128)(2,1)S(1)}, u32[]{:S(2)}, u32[]{:S(2)}) collective-permute-start(bf16[8,32,512]{2,1,0:T(8,128)(2,1)S(1)} %get-tuple-element.24), channel_id=1, source_target_pairs={{0,5},{1,2},{2,1},{3,6},{4,9},{5,0},{6,3},{7,10},{8,13},{9,4},{10,... | collective-permute-start | bytes 786440 | tf_op jit(solution)/shard_map/ppermute | solution.py:62
  16.5 2.0 %copy-start = (bf16[16,4,32,256]{3,2,1,0:T(8,128)(2,1)S(1)}, bf16[16,4,32,256]{3,2,1,0:T(8,128)(2,1)}, u32[]{:S(2)}) copy-start(bf16[16,4,32,256]{3,2,1,0:T(8,128)(2,1)} %interp_ref.3) | copy-start | bytes 3145732
  16.5 6.9 %collective-permute-start.4 = (bf16[8,32,512]{2,1,0:T(8,128)(2,1)S(1)}, bf16[8,32,512]{2,1,0:T(8,128)(2,1)S(1)}, u32[]{:S(2)}, u32[]{:S(2)}) collective-permute-start(bf16[8,32,512]{2,1,0:T(8,128)(2,1)S(1)} %get-tuple-element.25), channel_id=1, source_target_pairs={{0,5},{1,2},{2,1},{3,6},{4,9},{5,0},{6,3},{7,10},{8,13},{9,4},{10,... | collective-permute-start | bytes 786440 | tf_op jit(solution)/shard_map/ppermute | solution.py:62
  20.6 6.1 %collective-permute-start.3 = (bf16[8,32,512]{2,1,0:T(8,128)(2,1)S(1)}, bf16[8,32,512]{2,1,0:T(8,128)(2,1)S(1)}, u32[]{:S(2)}, u32[]{:S(2)}) collective-permute-start(bf16[8,32,512]{2,1,0:T(8,128)(2,1)S(1)} %add_5.1.token), channel_id=1, source_target_pairs={{0,3},{1,4},{2,7},{3,0},{4,1},{5,8},{6,11},{7,2},{8,5},{9,12},{10,... | collective-permute-start | bytes 786440 | tf_op jit(solution)/shard_map/ppermute | solution.py:62
  23.4 6.3 %collective-permute-start.6 = (bf16[8,32,512]{2,1,0:T(8,128)(2,1)S(1)}, bf16[8,32,512]{2,1,0:T(8,128)(2,1)S(1)}, u32[]{:S(2)}, u32[]{:S(2)}) collective-permute-start(bf16[8,32,512]{2,1,0:T(8,128)(2,1)S(1)} %add_4.1.token), channel_id=1, source_target_pairs={{0,3},{1,4},{2,7},{3,0},{4,1},{5,8},{6,11},{7,2},{8,5},{9,12},{10,... | collective-permute-start | bytes 786440 | tf_op jit(solution)/shard_map/ppermute | solution.py:62
  26.7 6.2 %collective-permute-start.5 = (bf16[8,32,512]{2,1,0:T(8,128)(2,1)S(1)}, bf16[8,32,512]{2,1,0:T(8,128)(2,1)S(1)}, u32[]{:S(2)}, u32[]{:S(2)}) collective-permute-start(bf16[8,32,512]{2,1,0:T(8,128)(2,1)S(1)} %add_3.1.token), channel_id=1, source_target_pairs={{0,5},{1,2},{2,1},{3,6},{4,9},{5,0},{6,3},{7,10},{8,13},{9,4},{10,... | collective-permute-start | bytes 786440 | tf_op jit(solution)/shard_map/ppermute | solution.py:62
  29.8 9.3 %copy-start.1 = (bf16[512,512]{1,0:T(8,128)(2,1)S(1)}, bf16[512,512]{1,0:T(8,128)(2,1)}, u32[]{:S(2)}) copy-start(bf16[512,512]{1,0:T(8,128)(2,1)} %up_ref.1) | copy-start | bytes 1572868
  29.8 9.3 %copy-start.2 = (bf16[512,512]{1,0:T(8,128)(2,1)S(1)}, bf16[512,512]{1,0:T(8,128)(2,1)}, u32[]{:S(2)}) copy-start(bf16[512,512]{1,0:T(8,128)(2,1)} %down_ref.1) | copy-start | bytes 1572868
  29.8 9.3 %copy-start.3 = (bf16[256,512]{1,0:T(8,128)(2,1)S(1)}, bf16[256,512]{1,0:T(8,128)(2,1)}, u32[]{:S(2)}) copy-start(bf16[256,512]{1,0:T(8,128)(2,1)} %latent_ref.1) | copy-start | bytes 786436
  29.8 9.3 %copy-start.4 = (f32[512]{0:T(512)S(1)}, f32[512]{0:T(512)}, u32[]{:S(2)}) copy-start(f32[512]{0:T(512)} %param.21) | copy-start | bytes 6148
  29.9 6.8 %collective-permute-start.8 = (bf16[8,32,512]{2,1,0:T(8,128)(2,1)S(1)}, bf16[8,32,512]{2,1,0:T(8,128)(2,1)S(1)}, u32[]{:S(2)}, u32[]{:S(2)}) collective-permute-start(bf16[8,32,512]{2,1,0:T(8,128)(2,1)S(1)} %add_2.1.token), channel_id=1, source_target_pairs={{0,5},{1,2},{2,1},{3,6},{4,9},{5,0},{6,3},{7,10},{8,13},{9,4},{10,... | collective-permute-start | bytes 786440 | tf_op jit(solution)/shard_map/ppermute | solution.py:62
  33.0 6.1 %collective-permute-start.7 = (bf16[8,32,512]{2,1,0:T(8,128)(2,1)S(1)}, bf16[8,32,512]{2,1,0:T(8,128)(2,1)S(1)}, u32[]{:S(2)}, u32[]{:S(2)}) collective-permute-start(bf16[8,32,512]{2,1,0:T(8,128)(2,1)S(1)} %add_1.1), channel_id=1, source_target_pairs={{0,3},{1,4},{2,7},{3,0},{4,1},{5,8},{6,11},{7,2},{8,5},{9,12},{10,... | collective-permute-start | bytes 786440 | tf_op jit(solution)/shard_map/ppermute | solution.py:62
  39.9 6.3 %collective-permute-start.9 = (bf16[256,512]{1,0:T(8,128)(2,1)S(1)}, bf16[256,512]{1,0:T(8,128)(2,1)S(1)}, u32[]{:S(2)}, u32[]{:S(2)}) collective-permute-start(bf16[256,512]{1,0:T(8,128)(2,1)S(1)} %get-tuple-element.26.refs_0_), channel_id=1, source_target_pairs={{0,3},{1,4},{2,7},{3,0},{4,1},{5,8},{6,11},{7,2},{8,5},{9,12},{10,... | collective-permute-start | bytes 786440 | tf_op jit(solution)/shard_map/ppermute | solution.py:62
  43.2 1.5 %collective-permute-start.10 = (bf16[128,512]{1,0:T(8,128)(2,1)S(1)}, bf16[128,512]{1,0:T(8,128)(2,1)S(1)}, u32[]{:S(2)}, u32[]{:S(2)}) collective-permute-start(bf16[128,512]{1,0:T(8,128)(2,1)S(1)} %get-tuple-element.29), channel_id=1, source_target_pairs={{0,1},{1,0},{2,3},{3,2},{4,5},{5,4},{6,7},{7,6},{8,9},{9,8},{10,11... | collective-permute-start | bytes 393224 | tf_op jit(solution)/shard_map/ppermute | solution.py:53
  44.6 5.8 %collective-permute-start.11 = (bf16[256,512]{1,0:T(8,128)(2,1)S(1)}, bf16[256,512]{1,0:T(8,128)(2,1)S(1)}, u32[]{:S(2)}, u32[]{:S(2)}) collective-permute-start(bf16[256,512]{1,0:T(8,128)(2,1)S(1)} %in_order.8), channel_id=1, source_target_pairs={{0,5},{1,2},{2,1},{3,6},{4,9},{5,0},{6,3},{7,10},{8,13},{9,4},{10,... | collective-permute-start | bytes 786440 | tf_op jit(solution)/shard_map/ppermute | solution.py:62
  46.2 7.1 %collective-permute-start.12 = (bf16[256,512]{1,0:T(8,128)(2,1)S(1)}, bf16[256,512]{1,0:T(8,128)(2,1)S(1)}, u32[]{:S(2)}, u32[]{:S(2)}) collective-permute-start(bf16[256,512]{1,0:T(8,128)(2,1)S(1)} %in_order.7.refs_1_.refs_0_), channel_id=1, source_target_pairs={{0,5},{1,2},{2,1},{3,6},{4,9},{5,0},{6,3},{7,10},{8,13},{9,4},{10,... | collective-permute-start | bytes 786440 | tf_op jit(solution)/shard_map/ppermute | solution.py:62
  50.4 6.2 %collective-permute-start.13 = (bf16[256,512]{1,0:T(8,128)(2,1)S(1)}, bf16[256,512]{1,0:T(8,128)(2,1)S(1)}, u32[]{:S(2)}, u32[]{:S(2)}) collective-permute-start(bf16[256,512]{1,0:T(8,128)(2,1)S(1)} %in_order.9.refs_1_), channel_id=1, source_target_pairs={{0,3},{1,4},{2,7},{3,0},{4,1},{5,8},{6,11},{7,2},{8,5},{9,12},{10,... | collective-permute-start | bytes 786440 | tf_op jit(solution)/shard_map/ppermute | solution.py:62
  53.3 6.2 %collective-permute-start.14 = (bf16[256,512]{1,0:T(8,128)(2,1)S(1)}, bf16[256,512]{1,0:T(8,128)(2,1)S(1)}, u32[]{:S(2)}, u32[]{:S(2)}) collective-permute-start(bf16[256,512]{1,0:T(8,128)(2,1)S(1)} %in_order.10.refs_1_.refs_0_), channel_id=1, source_target_pairs={{0,3},{1,4},{2,7},{3,0},{4,1},{5,8},{6,11},{7,2},{8,5},{9,12},{10,... | collective-permute-start | bytes 786440 | tf_op jit(solution)/shard_map/ppermute | solution.py:62
  56.6 6.4 %collective-permute-start.15 = (bf16[256,512]{1,0:T(8,128)(2,1)S(1)}, bf16[256,512]{1,0:T(8,128)(2,1)S(1)}, u32[]{:S(2)}, u32[]{:S(2)}) collective-permute-start(bf16[256,512]{1,0:T(8,128)(2,1)S(1)} %in_order.11.refs_1_), channel_id=1, source_target_pairs={{0,5},{1,2},{2,1},{3,6},{4,9},{5,0},{6,3},{7,10},{8,13},{9,4},{10,... | collective-permute-start | bytes 786440 | tf_op jit(solution)/shard_map/ppermute | solution.py:62
  59.4 6.5 %collective-permute-start.19 = (bf16[256,512]{1,0:T(8,128)(2,1)S(1)}, bf16[256,512]{1,0:T(8,128)(2,1)S(1)}, u32[]{:S(2)}, u32[]{:S(2)}) collective-permute-start(bf16[256,512]{1,0:T(8,128)(2,1)S(1)} %in_order.12.refs_1_.refs_0_), channel_id=1, source_target_pairs={{0,5},{1,2},{2,1},{3,6},{4,9},{5,0},{6,3},{7,10},{8,13},{9,4},{10,... | collective-permute-start | bytes 786440 | tf_op jit(solution)/shard_map/ppermute | solution.py:62
  61.9 4.7 %collective-permute-start.16 = (bf16[256,512]{1,0:T(8,128)(2,1)S(1)}, bf16[256,512]{1,0:T(8,128)(2,1)S(1)}, u32[]{:S(2)}, u32[]{:S(2)}) collective-permute-start(bf16[256,512]{1,0:T(8,128)(2,1)S(1)} %get-tuple-element.33), channel_id=1, source_target_pairs={{0,1},{1,0},{2,3},{3,2},{4,5},{5,4},{6,7},{7,6},{8,9},{9,8},{10,11... | collective-permute-start | bytes 786440 | tf_op jit(solution)/shard_map/ppermute | solution.py:53
  61.9 4.7 %collective-permute-start.17 = (bf16[256,512]{1,0:T(8,128)(2,1)S(1)}, bf16[256,512]{1,0:T(8,128)(2,1)S(1)}, u32[]{:S(2)}, u32[]{:S(2)}) collective-permute-start(bf16[256,512]{1,0:T(8,128)(2,1)S(1)} %get-tuple-element.34), channel_id=1, source_target_pairs={{0,1},{1,0},{2,3},{3,2},{4,5},{5,4},{6,7},{7,6},{8,9},{9,8},{10,11... | collective-permute-start | bytes 786440 | tf_op jit(solution)/shard_map/ppermute | solution.py:53
  63.6 3.0 %collective-permute-start.18 = (bf16[256,512]{1,0:T(8,128)(2,1)S(1)}, bf16[256,512]{1,0:T(8,128)(2,1)S(1)}, u32[]{:S(2)}, u32[]{:S(2)}) collective-permute-start(bf16[256,512]{1,0:T(8,128)(2,1)S(1)} %get-tuple-element.35), channel_id=1, source_target_pairs={{0,1},{1,0},{2,3},{3,2},{4,5},{5,4},{6,7},{7,6},{8,9},{9,8},{10,11... | collective-permute-start | bytes 786440 | tf_op jit(solution)/shard_map/ppermute | solution.py:53
  65.9 1.8 %collective-permute-start.20 = (bf16[256,512]{1,0:T(8,128)(2,1)S(1)}, bf16[256,512]{1,0:T(8,128)(2,1)S(1)}, u32[]{:S(2)}, u32[]{:S(2)}) collective-permute-start(bf16[256,512]{1,0:T(8,128)(2,1)S(1)} %collective-permute-done.19.mine_ref), channel_id=1, source_target_pairs={{0,1},{1,0},{2,3},{3,2},{4,5},{5,4},{6,7},{7,6},{8,9},{9,8},{10,11... | collective-permute-start | bytes 786440 | tf_op jit(solution)/shard_map/ppermute | solution.py:53

commit v20 on v18

--- a/solution.py
+++ b/solution.py
@@ -199,12 +199,12 @@
 
 
 def pick_kernel(chosen, slots, groups, tile_rows, table_ref, *refs):
-    pieces, outs = refs[: len(chosen)], refs[len(chosen) :]
-    for out in outs[2:]:
-        out[...] = pieces[0][...]
+    pieces, outs, copied = refs[: len(chosen)], refs[-2:], refs[len(chosen) : -2]
+    for source, target in zip(copied[::2], copied[1::2]):
+        target[...] = source[...]
     for number, group in enumerate(chosen):
         for slot in range(slots):
-            for way, out in enumerate(outs[:2]):
+            for way, out in enumerate(outs):
                 tile = table_ref[way, (way * groups + group) * slots + slot]
                 rows = pl.ds(pl.multiple_of(tile * tile_rows, tile_rows), tile_rows)
                 into = (number * slots + slot) * tile_rows
@@ -449,29 +449,28 @@
 
     mine, theirs = [], []
 
-    def pick(chosen, values):
-        outs = [shape((len(chosen) * slots * tile_rows, width))] * 2
-        if chosen == [0]:
-            outs.append(shape((node_rows, width)))
+    def pick(chosen, values, *copied):
+        outs = [shape(v.shape) for v in copied]
+        outs += [shape((len(chosen) * slots * tile_rows, width))] * 2
         picked = pl.pallas_call(
             functools.partial(pick_kernel, chosen, slots, chips, tile_rows),
             out_shape=outs,
             grid_spec=pltpu.PrefetchScalarGridSpec(
                 num_scalar_prefetch=1,
                 grid=(1,),
-                in_specs=[in_vmem] * len(values),
+                in_specs=[in_vmem] * (len(values) + len(copied)),
                 out_specs=[in_vmem] * len(outs),
             ),
             compiler_params=params(8),
             cost_estimate=cost(0, *values),
             name=f"pick_{chosen[0]}",
-        )(table, *values)
-        mine.append(picked[0])
-        theirs.append(ring.over_core(picked[1]))
-        return picked[-1]
+        )(table, *values, *copied)
+        mine.append(picked[-2])
+        theirs.append(ring.over_core(picked[-1]))
+        return picked[:-2]
 
     first = ring.over_first(piece, 1)
-    mesh_out = pick([0], [piece])
+    pick([0], [piece])
     second = ring.over_second(in_order(again, theirs[0]), 1)
     token = mine[0]
     for distance in range(1, far):
@@ -480,7 +479,11 @@
         second = in_order(second, first)
         if distance < far - 1:
             after = ring.over_second(second, distance + 1)
-        pick([2 * distance - 1, 2 * distance], [first, second])
+        copied = pick(
+            [2 * distance - 1, 2 * distance], [first, second], *[piece] * (distance == 1)
+        )
+        if copied:
+            mesh_out = copied[0]
         token = mine[-1]
         first, second = onward, after
     tiles_far = [first, ring.over_core(first)]

time: 72.1 us -> 72.7 us (level)
  the two profiles are of different devices: /device:TPU:0 before, /device:TPU:29 now
where the time goes in v20:
time: 72.7 us; the launch traced here: 72.5 us
  waiting for transfers between devices  41.1 us (57%)
  Pallas kernels  21.2 us (29%)
  starting transfers between devices  9.4 us (13%)
  between operations  0.84 us (1%)
    ppermute x14, waiting for transfers between devices, over(): return lax.ppermute(value, 'band', pairs)  35.8 us
    pallas_call x1, Pallas kernels, on_device(): pl.pallas_call(functools.partial(embed_kernel, ring, per_step, slots), ou...  9.83 us
    ppermute x14, starting transfers between devices, over(): return lax.ppermute(value, 'band', pairs)  5.95 us
    ppermute x7, waiting for transfers between devices, over_core(): return lax.ppermute(value, 'band', [(i, i ^ 1) for i in range(self.n_band)])  5.36 us
    pallas_call x1, Pallas kernels, on_device(): pl.pallas_call(functools.partial(back_kernel, list_len), out_shape=shape(...  4.57 us
    ppermute x7, starting transfers between devices, over_core(): return lax.ppermute(value, 'band', [(i, i ^ 1) for i in range(self.n_band)])  3.45 us
    pallas_call x4, Pallas kernels, pick(): pl.pallas_call(functools.partial(pick_kernel, chosen, slots, chips, tile_...  3.11 us
  transfers between devices with their start and end apart: 21, of which 17 were waited for; matrix products, arithmetic and copies ran while one was open for 0% of the time, Pallas kernels for 7%

profile of v20, /device:TPU:29, one launch (start us, length us, event | category | flops | bytes accessed | tf_op | source)
XLA Modules:
  0.0 72.5 jit_solution(8895365846858372216)
XLA Ops:
  0.6 9.8 %embed.1 = (bf16[4096,512]{1,0:T(8,128)(2,1)}, bf16[57,32,512]{2,1,0:T(8,128)(2,1)S(1)}, bf16[9,32,512]{2,1,0:T(8,128)(2,1)S(1)}, s32[4,64]{1,0:T(4,128)S(1)}) custom-call(s32[1]{0:T(128)} %bitcast.me_ref, s32[4,256]{1,0:T(4,128)} %bitcast.8, s32[4,256]{1,0:T(4,128)} %bitcast.9, bf16[227,4096]{1,0:T(8,128)(2,1)} %bitcast.7, bf16[227,512]{1,0:T(8,128)(2,1)} %w1_ref.1, ...), custom_call_target="tpu_custom_call" | custom-call | flops 3636461568 | bytes 2908160 | tf_op jit(solution)/shard_map/embed/pallas_call | solution.py:327
  10.5 0.7 collective-permute-start
  11.1 1.2 %collective-permute-done.other = bf16[9,32,512]{2,1,0:T(8,128)(2,1)S(1)} collective-permute-done((bf16[9,32,512]{2,1,0:T(8,128)(2,1)S(1)}, bf16[9,32,512]{2,1,0:T(8,128)(2,1)S(1)}, u32[]{:S(2)}, u32[]{:S(2)}) %collective-permute-start) | collective-permute-done | bytes 294944 | tf_op jit(solution)/shard_map/ppermute | solution.py:53
  12.3 0.8 %far_sums.1 = (bf16[8,32,512]{2,1,0:T(8,128)(2,1)S(1)}, bf16[8,32,512]{2,1,0:T(8,128)(2,1)S(1)}, bf16[57,32,512]{2,1,0:T(8,128)(2,1)S(1)}) custom-call(s32[4,64]{1,0:T(4,128)S(1)} %get-tuple-element.20.table_ref, bf16[57,32,512]{2,1,0:T(8,128)(2,1)S(1)} %get-tuple-element.21.kept, ...), custom_call_target="tpu_custom_call", output_to_operand_aliasing={{2}: (1, {})} | custom-call | bytes 1867776 | tf_op jit(solution)/shard_map/far_sums/pallas_call | solution.py:376
  13.8 1.5 %collective-permute-start.4 = (bf16[8,32,512]{2,1,0:T(8,128)(2,1)S(1)}, bf16[8,32,512]{2,1,0:T(8,128)(2,1)S(1)}, u32[]{:S(2)}, u32[]{:S(2)}) collective-permute-start(bf16[8,32,512]{2,1,0:T(8,128)(2,1)S(1)} %get-tuple-element.25), channel_id=1, source_target_pairs={{0,5},{1,2},{2,1},{3,6},{4,9},{5,0},{6,3},{7,10},{8,13},{9,4},{10,... | collective-permute-start | bytes 786440 | tf_op jit(solution)/shard_map/ppermute | solution.py:62
  15.3 1.7 %collective-permute-done.1.other = bf16[57,32,512]{2,1,0:T(8,128)(2,1)S(1)} collective-permute-done((bf16[57,32,512]{2,1,0:T(8,128)(2,1)S(1)}, bf16[57,32,512]{2,1,0:T(8,128)(2,1)S(1)}, u32[]{:S(2)}, u32[]{:S(2)}) %collective-permute-start.1) | collective-permute-done | bytes 1867808 | tf_op jit(solution)/shard_map/ppermute | solution.py:53
  17.0 1.2 %own_sums.1.token.own = f32[6,8,32,512]{3,2,1,0:T(8,128)S(1)} custom-call(s32[4,64]{1,0:T(4,128)S(1)} %get-tuple-element.20.table_ref, bf16[57,32,512]{2,1,0:T(8,128)(2,1)S(1)} %get-tuple-element.23.kept, bf16[57,32,512]{2,1,0:T(8,128)(2,1)S(1)} %collective-permute-done.1.other), custom_call_target="tpu_custom_call" | custom-call | bytes 3735552 | tf_op jit(solution)/shard_map/own_sums/pallas_call | solution.py:392
  18.8 0.9 %collective-permute-done.2.came = bf16[8,32,512]{2,1,0:T(8,128)(2,1)S(1)} collective-permute-done((bf16[8,32,512]{2,1,0:T(8,128)(2,1)S(1)}, bf16[8,32,512]{2,1,0:T(8,128)(2,1)S(1)}, u32[]{:S(2)}, u32[]{:S(2)}) %collective-permute-start.2) | collective-permute-done | bytes 262176 | tf_op jit(solution)/shard_map/ppermute | solution.py:62
  19.8 2.9 %collective-permute-done.4.came = bf16[8,32,512]{2,1,0:T(8,128)(2,1)S(1)} collective-permute-done((bf16[8,32,512]{2,1,0:T(8,128)(2,1)S(1)}, bf16[8,32,512]{2,1,0:T(8,128)(2,1)S(1)}, u32[]{:S(2)}, u32[]{:S(2)}) %collective-permute-start.4) | collective-permute-done | bytes 262176 | tf_op jit(solution)/shard_map/ppermute | solution.py:62
  22.8 3.1 %collective-permute-done.3.came = bf16[8,32,512]{2,1,0:T(8,128)(2,1)S(1)} collective-permute-done((bf16[8,32,512]{2,1,0:T(8,128)(2,1)S(1)}, bf16[8,32,512]{2,1,0:T(8,128)(2,1)S(1)}, u32[]{:S(2)}, u32[]{:S(2)}) %collective-permute-start.3) | collective-permute-done | bytes 262176 | tf_op jit(solution)/shard_map/ppermute | solution.py:62
  26.0 3.3 %collective-permute-done.6.came = bf16[8,32,512]{2,1,0:T(8,128)(2,1)S(1)} collective-permute-done((bf16[8,32,512]{2,1,0:T(8,128)(2,1)S(1)}, bf16[8,32,512]{2,1,0:T(8,128)(2,1)S(1)}, u32[]{:S(2)}, u32[]{:S(2)}) %collective-permute-start.6) | collective-permute-done | bytes 262176 | tf_op jit(solution)/shard_map/ppermute | solution.py:62
  29.5 2.6 %collective-permute-done.5.came = bf16[8,32,512]{2,1,0:T(8,128)(2,1)S(1)} collective-permute-done((bf16[8,32,512]{2,1,0:T(8,128)(2,1)S(1)}, bf16[8,32,512]{2,1,0:T(8,128)(2,1)S(1)}, u32[]{:S(2)}, u32[]{:S(2)}) %collective-permute-start.5) | collective-permute-done | bytes 262176 | tf_op jit(solution)/shard_map/ppermute | solution.py:62
  32.2 4.0 %collective-permute-done.8.neighbour = bf16[8,32,512]{2,1,0:T(8,128)(2,1)S(1)} collective-permute-done((bf16[8,32,512]{2,1,0:T(8,128)(2,1)S(1)}, bf16[8,32,512]{2,1,0:T(8,128)(2,1)S(1)}, u32[]{:S(2)}, u32[]{:S(2)}) %collective-permute-start.8) | collective-permute-done | bytes 262176 | tf_op jit(solution)/shard_map/ppermute | solution.py:62
  36.3 2.0 %collective-permute-done.7.came = bf16[8,32,512]{2,1,0:T(8,128)(2,1)S(1)} collective-permute-done((bf16[8,32,512]{2,1,0:T(8,128)(2,1)S(1)}, bf16[8,32,512]{2,1,0:T(8,128)(2,1)S(1)}, u32[]{:S(2)}, u32[]{:S(2)}) %collective-permute-start.7) | collective-permute-done | bytes 262176 | tf_op jit(solution)/shard_map/ppermute | solution.py:62
  38.3 0.7 %mesh_step.1 = (bf16[256,512]{1,0:T(8,128)(2,1)S(1)}, bf16[256,512]{1,0:T(8,128)(2,1)S(1)}) custom-call(bf16[256,512]{1,0:T(8,128)(2,1)S(1)} %copy-done.3, bf16[512,512]{1,0:T(8,128)(2,1)S(1)} %copy-done.1, bf16[512,512]{1,0:T(8,128)(2,1)S(1)} %copy-done.2, f32[1,512]{1,0:T(1,128)S(1)} %bitcast.6, f32[6,8,32,512]{3,2,1,0:T(8,128)S(1)} %own_sums.1.token.own, ...), custom_call_target="tpu_custom_call" | custom-call | flops 268435456 | bytes 1048576 | tf_op jit(solution)/shard_map/mesh_step/pallas_call | solution.py:440
  39.5 0.6 pick_0.1
  40.4 1.0 %collective-permute-done.10.refs_1_.refs_4_ = bf16[128,512]{1,0:T(8,128)(2,1)S(1)} collective-permute-done((bf16[128,512]{1,0:T(8,128)(2,1)S(1)}, bf16[128,512]{1,0:T(8,128)(2,1)S(1)}, u32[]{:S(2)}, u32[]{:S(2)}) %collective-permute-start.10) | collective-permute-done | bytes 131104 | tf_op jit(solution)/shard_map/ppermute | solution.py:53
  41.5 1.6 %collective-permute-start.11 = (bf16[256,512]{1,0:T(8,128)(2,1)S(1)}, bf16[256,512]{1,0:T(8,128)(2,1)S(1)}, u32[]{:S(2)}, u32[]{:S(2)}) collective-permute-start(bf16[256,512]{1,0:T(8,128)(2,1)S(1)} %in_order.8), channel_id=1, source_target_pairs={{0,5},{1,2},{2,1},{3,6},{4,9},{5,0},{6,3},{7,10},{8,13},{9,4},{10,... | collective-permute-start | bytes 786440 | tf_op jit(solution)/shard_map/ppermute | solution.py:62
  43.0 3.1 %collective-permute-done.9.refs_0_ = bf16[256,512]{1,0:T(8,128)(2,1)S(1)} collective-permute-done((bf16[256,512]{1,0:T(8,128)(2,1)S(1)}, bf16[256,512]{1,0:T(8,128)(2,1)S(1)}, u32[]{:S(2)}, u32[]{:S(2)}) %collective-permute-start.9) | collective-permute-done | bytes 262176 | tf_op jit(solution)/shard_map/ppermute | solution.py:62
  46.1 1.7 %collective-permute-done.11.refs_0_ = bf16[256,512]{1,0:T(8,128)(2,1)S(1)} collective-permute-done((bf16[256,512]{1,0:T(8,128)(2,1)S(1)}, bf16[256,512]{1,0:T(8,128)(2,1)S(1)}, u32[]{:S(2)}, u32[]{:S(2)}) %collective-permute-start.11) | collective-permute-done | bytes 262176 | tf_op jit(solution)/shard_map/ppermute | solution.py:62
  47.8 0.9 %collective-permute-start.13 = (bf16[256,512]{1,0:T(8,128)(2,1)S(1)}, bf16[256,512]{1,0:T(8,128)(2,1)S(1)}, u32[]{:S(2)}, u32[]{:S(2)}) collective-permute-start(bf16[256,512]{1,0:T(8,128)(2,1)S(1)} %in_order.9.refs_1_), channel_id=1, source_target_pairs={{0,3},{1,4},{2,7},{3,0},{4,1},{5,8},{6,11},{7,2},{8,5},{9,12},{10,... | collective-permute-start | bytes 786440 | tf_op jit(solution)/shard_map/ppermute | solution.py:62
  48.7 1.3 %pick_1.1 = (bf16[256,512]{1,0:T(8,128)(2,1)}, bf16[256,512]{1,0:T(8,128)(2,1)S(1)}, bf16[256,512]{1,0:T(8,128)(2,1)S(1)}) custom-call(s32[4,64]{1,0:T(4,128)S(1)} %get-tuple-element.20.table_ref, bf16[256,512]{1,0:T(8,128)(2,1)S(1)} %in_order.7.refs_1_.refs_0_, bf16[256,512]{1,0:T(8,128)(2,1)S(1)} %in_order.9.refs_1_, ...), custom_call_target="tpu_custom_call" | custom-call | bytes 524288 | tf_op jit(solution)/shard_map/pick_1/pallas_call | solution.py:455
  50.0 3.2 %collective-permute-done.12.refs_0_ = bf16[256,512]{1,0:T(8,128)(2,1)S(1)} collective-permute-done((bf16[256,512]{1,0:T(8,128)(2,1)S(1)}, bf16[256,512]{1,0:T(8,128)(2,1)S(1)}, u32[]{:S(2)}, u32[]{:S(2)}) %collective-permute-start.12) | collective-permute-done | bytes 262176 | tf_op jit(solution)/shard_map/ppermute | solution.py:62
  53.2 0.7 collective-permute-done.13.refs_0_
  53.9 1.0 %collective-permute-start.15 = (bf16[256,512]{1,0:T(8,128)(2,1)S(1)}, bf16[256,512]{1,0:T(8,128)(2,1)S(1)}, u32[]{:S(2)}, u32[]{:S(2)}) collective-permute-start(bf16[256,512]{1,0:T(8,128)(2,1)S(1)} %in_order.11.refs_1_), channel_id=1, source_target_pairs={{0,5},{1,2},{2,1},{3,6},{4,9},{5,0},{6,3},{7,10},{8,13},{9,4},{10,... | collective-permute-start | bytes 786440 | tf_op jit(solution)/shard_map/ppermute | solution.py:62
  55.0 0.6 pick_3.1
  55.6 5.0 %collective-permute-done.14.refs_0_ = bf16[256,512]{1,0:T(8,128)(2,1)S(1)} collective-permute-done((bf16[256,512]{1,0:T(8,128)(2,1)S(1)}, bf16[256,512]{1,0:T(8,128)(2,1)S(1)}, u32[]{:S(2)}, u32[]{:S(2)}) %collective-permute-start.14) | collective-permute-done | bytes 262176 | tf_op jit(solution)/shard_map/ppermute | solution.py:62
  61.1 0.6 pick_5.1
  61.8 1.5 %collective-permute-start.18 = (bf16[256,512]{1,0:T(8,128)(2,1)S(1)}, bf16[256,512]{1,0:T(8,128)(2,1)S(1)}, u32[]{:S(2)}, u32[]{:S(2)}) collective-permute-start(bf16[256,512]{1,0:T(8,128)(2,1)S(1)} %get-tuple-element.35), channel_id=1, source_target_pairs={{0,1},{1,0},{2,3},{3,2},{4,5},{5,4},{6,7},{7,6},{8,9},{9,8},{10,11... | collective-permute-start | bytes 786440 | tf_op jit(solution)/shard_map/ppermute | solution.py:53
  63.2 3.2 %collective-permute-done.19.mine_ref = bf16[256,512]{1,0:T(8,128)(2,1)S(1)} collective-permute-done((bf16[256,512]{1,0:T(8,128)(2,1)S(1)}, bf16[256,512]{1,0:T(8,128)(2,1)S(1)}, u32[]{:S(2)}, u32[]{:S(2)}) %collective-permute-start.19) | collective-permute-done | bytes 262176 | tf_op jit(solution)/shard_map/ppermute | solution.py:62
  66.6 1.4 %collective-permute-done.20.theirs_ref = bf16[256,512]{1,0:T(8,128)(2,1)S(1)} collective-permute-done((bf16[256,512]{1,0:T(8,128)(2,1)S(1)}, bf16[256,512]{1,0:T(8,128)(2,1)S(1)}, u32[]{:S(2)}, u32[]{:S(2)}) %collective-permute-start.20) | collective-permute-done | bytes 262176 | tf_op jit(solution)/shard_map/ppermute | solution.py:53
  68.0 4.6 %back.1 = bf16[4096,512]{1,0:T(8,128)(2,1)} custom-call(s32[4,64]{1,0:T(4,128)S(1)} %get-tuple-element.20.table_ref, bf16[16,256,128]{2,1,0:T(8,128)(2,1)S(1)} %turn.1.token.weights_ref, bf16[1792,512]{1,0:T(8,128)(2,1)S(1)} %join.1.near_ref, bf16[256,512]{1,0:T(8,128)(2,1)S(1)} %collective-permute-done.19.mine_ref, ...), custom_call_target="tpu_custom_call" | custom-call | flops 536870912 | bytes 9437184 | tf_op jit(solution)/shard_map/back/pallas_call | solution.py:501
  (43 shorter events, 3.2 us)
Async XLA Ops:
  10.5 1.9 %collective-permute-start = (bf16[9,32,512]{2,1,0:T(8,128)(2,1)S(1)}, bf16[9,32,512]{2,1,0:T(8,128)(2,1)S(1)}, u32[]{:S(2)}, u32[]{:S(2)}) collective-permute-start(bf16[9,32,512]{2,1,0:T(8,128)(2,1)S(1)} %get-tuple-element.22), channel_id=1, source_target_pairs={{0,1},{1,0},{2,3},{3,2},{4,5},{5,4},{6,7},{7,6},{8,9},{9,8},{10,11... | collective-permute-start | bytes 884744 | tf_op jit(solution)/shard_map/ppermute | solution.py:53
  13.1 3.9 %collective-permute-start.1 = (bf16[57,32,512]{2,1,0:T(8,128)(2,1)S(1)}, bf16[57,32,512]{2,1,0:T(8,128)(2,1)S(1)}, u32[]{:S(2)}, u32[]{:S(2)}) collective-permute-start(bf16[57,32,512]{2,1,0:T(8,128)(2,1)S(1)} %get-tuple-element.23.kept), channel_id=1, source_target_pairs={{0,1},{1,0},{2,3},{3,2},{4,5},{5,4},{6,7},{7,6},{8,9},{9,8},{10,11... | collective-permute-start | bytes 5603336 | tf_op jit(solution)/shard_map/ppermute | solution.py:53
  13.6 6.1 %collective-permute-start.2 = (bf16[8,32,512]{2,1,0:T(8,128)(2,1)S(1)}, bf16[8,32,512]{2,1,0:T(8,128)(2,1)S(1)}, u32[]{:S(2)}, u32[]{:S(2)}) collective-permute-start(bf16[8,32,512]{2,1,0:T(8,128)(2,1)S(1)} %get-tuple-element.24), channel_id=1, source_target_pairs={{0,5},{1,2},{2,1},{3,6},{4,9},{5,0},{6,3},{7,10},{8,13},{9,4},{10,... | collective-permute-start | bytes 786440 | tf_op jit(solution)/shard_map/ppermute | solution.py:62
  13.8 4.4 %copy-start = (bf16[16,4,32,256]{3,2,1,0:T(8,128)(2,1)S(1)}, bf16[16,4,32,256]{3,2,1,0:T(8,128)(2,1)}, u32[]{:S(2)}) copy-start(bf16[16,4,32,256]{3,2,1,0:T(8,128)(2,1)} %interp_ref.3) | copy-start | bytes 3145732
  13.8 8.8 %collective-permute-start.4 = (bf16[8,32,512]{2,1,0:T(8,128)(2,1)S(1)}, bf16[8,32,512]{2,1,0:T(8,128)(2,1)S(1)}, u32[]{:S(2)}, u32[]{:S(2)}) collective-permute-start(bf16[8,32,512]{2,1,0:T(8,128)(2,1)S(1)} %get-tuple-element.25), channel_id=1, source_target_pairs={{0,5},{1,2},{2,1},{3,6},{4,9},{5,0},{6,3},{7,10},{8,13},{9,4},{10,... | collective-permute-start | bytes 786440 | tf_op jit(solution)/shard_map/ppermute | solution.py:62
  19.7 6.2 %collective-permute-start.3 = (bf16[8,32,512]{2,1,0:T(8,128)(2,1)S(1)}, bf16[8,32,512]{2,1,0:T(8,128)(2,1)S(1)}, u32[]{:S(2)}, u32[]{:S(2)}) collective-permute-start(bf16[8,32,512]{2,1,0:T(8,128)(2,1)S(1)} %add_5.1.token), channel_id=1, source_target_pairs={{0,3},{1,4},{2,7},{3,0},{4,1},{5,8},{6,11},{7,2},{8,5},{9,12},{10,... | collective-permute-start | bytes 786440 | tf_op jit(solution)/shard_map/ppermute | solution.py:62
  22.7 6.6 %collective-permute-start.6 = (bf16[8,32,512]{2,1,0:T(8,128)(2,1)S(1)}, bf16[8,32,512]{2,1,0:T(8,128)(2,1)S(1)}, u32[]{:S(2)}, u32[]{:S(2)}) collective-permute-start(bf16[8,32,512]{2,1,0:T(8,128)(2,1)S(1)} %add_4.1.token), channel_id=1, source_target_pairs={{0,3},{1,4},{2,7},{3,0},{4,1},{5,8},{6,11},{7,2},{8,5},{9,12},{10,... | collective-permute-start | bytes 786440 | tf_op jit(solution)/shard_map/ppermute | solution.py:62
  25.9 6.2 %collective-permute-start.5 = (bf16[8,32,512]{2,1,0:T(8,128)(2,1)S(1)}, bf16[8,32,512]{2,1,0:T(8,128)(2,1)S(1)}, u32[]{:S(2)}, u32[]{:S(2)}) collective-permute-start(bf16[8,32,512]{2,1,0:T(8,128)(2,1)S(1)} %add_3.1.token), channel_id=1, source_target_pairs={{0,5},{1,2},{2,1},{3,6},{4,9},{5,0},{6,3},{7,10},{8,13},{9,4},{10,... | collective-permute-start | bytes 786440 | tf_op jit(solution)/shard_map/ppermute | solution.py:62
  29.4 8.9 %copy-start.1 = (bf16[512,512]{1,0:T(8,128)(2,1)S(1)}, bf16[512,512]{1,0:T(8,128)(2,1)}, u32[]{:S(2)}) copy-start(bf16[512,512]{1,0:T(8,128)(2,1)} %up_ref.1) | copy-start | bytes 1572868
  29.4 8.9 %copy-start.2 = (bf16[512,512]{1,0:T(8,128)(2,1)S(1)}, bf16[512,512]{1,0:T(8,128)(2,1)}, u32[]{:S(2)}) copy-start(bf16[512,512]{1,0:T(8,128)(2,1)} %down_ref.1) | copy-start | bytes 1572868
  29.4 8.9 %copy-start.3 = (bf16[256,512]{1,0:T(8,128)(2,1)S(1)}, bf16[256,512]{1,0:T(8,128)(2,1)}, u32[]{:S(2)}) copy-start(bf16[256,512]{1,0:T(8,128)(2,1)} %latent_ref.1) | copy-start | bytes 786436
  29.4 8.9 %copy-start.4 = (f32[512]{0:T(512)S(1)}, f32[512]{0:T(512)}, u32[]{:S(2)}) copy-start(f32[512]{0:T(512)} %param.21) | copy-start | bytes 6148
  29.4 6.8 %collective-permute-start.8 = (bf16[8,32,512]{2,1,0:T(8,128)(2,1)S(1)}, bf16[8,32,512]{2,1,0:T(8,128)(2,1)S(1)}, u32[]{:S(2)}, u32[]{:S(2)}) collective-permute-start(bf16[8,32,512]{2,1,0:T(8,128)(2,1)S(1)} %add_2.1.token), channel_id=1, source_target_pairs={{0,5},{1,2},{2,1},{3,6},{4,9},{5,0},{6,3},{7,10},{8,13},{9,4},{10,... | collective-permute-start | bytes 786440 | tf_op jit(solution)/shard_map/ppermute | solution.py:62
  32.2 6.2 %collective-permute-start.7 = (bf16[8,32,512]{2,1,0:T(8,128)(2,1)S(1)}, bf16[8,32,512]{2,1,0:T(8,128)(2,1)S(1)}, u32[]{:S(2)}, u32[]{:S(2)}) collective-permute-start(bf16[8,32,512]{2,1,0:T(8,128)(2,1)S(1)} %add_1.1), channel_id=1, source_target_pairs={{0,3},{1,4},{2,7},{3,0},{4,1},{5,8},{6,11},{7,2},{8,5},{9,12},{10,... | collective-permute-start | bytes 786440 | tf_op jit(solution)/shard_map/ppermute | solution.py:62
  39.1 7.0 %collective-permute-start.9 = (bf16[256,512]{1,0:T(8,128)(2,1)S(1)}, bf16[256,512]{1,0:T(8,128)(2,1)S(1)}, u32[]{:S(2)}, u32[]{:S(2)}) collective-permute-start(bf16[256,512]{1,0:T(8,128)(2,1)S(1)} %get-tuple-element.26.refs_0_.refs_2_), channel_id=1, source_target_pairs={{0,3},{1,4},{2,7},{3,0},{4,1},{5,8},{6,11},{7,2},{8,5},{9,12},{10,... | collective-permute-start | bytes 786440 | tf_op jit(solution)/shard_map/ppermute | solution.py:62
  40.0 1.4 %collective-permute-start.10 = (bf16[128,512]{1,0:T(8,128)(2,1)S(1)}, bf16[128,512]{1,0:T(8,128)(2,1)S(1)}, u32[]{:S(2)}, u32[]{:S(2)}) collective-permute-start(bf16[128,512]{1,0:T(8,128)(2,1)S(1)} %get-tuple-element.29), channel_id=1, source_target_pairs={{0,1},{1,0},{2,3},{3,2},{4,5},{5,4},{6,7},{7,6},{8,9},{9,8},{10,11... | collective-permute-start | bytes 393224 | tf_op jit(solution)/shard_map/ppermute | solution.py:53
  41.5 6.4 %collective-permute-start.11 = (bf16[256,512]{1,0:T(8,128)(2,1)S(1)}, bf16[256,512]{1,0:T(8,128)(2,1)S(1)}, u32[]{:S(2)}, u32[]{:S(2)}) collective-permute-start(bf16[256,512]{1,0:T(8,128)(2,1)S(1)} %in_order.8), channel_id=1, source_target_pairs={{0,5},{1,2},{2,1},{3,6},{4,9},{5,0},{6,3},{7,10},{8,13},{9,4},{10,... | collective-permute-start | bytes 786440 | tf_op jit(solution)/shard_map/ppermute | solution.py:62
  46.1 7.2 %collective-permute-start.12 = (bf16[256,512]{1,0:T(8,128)(2,1)S(1)}, bf16[256,512]{1,0:T(8,128)(2,1)S(1)}, u32[]{:S(2)}, u32[]{:S(2)}) collective-permute-start(bf16[256,512]{1,0:T(8,128)(2,1)S(1)} %in_order.7.refs_1_.refs_0_), channel_id=1, source_target_pairs={{0,5},{1,2},{2,1},{3,6},{4,9},{5,0},{6,3},{7,10},{8,13},{9,4},{10,... | collective-permute-start | bytes 786440 | tf_op jit(solution)/shard_map/ppermute | solution.py:62
  47.8 6.1 %collective-permute-start.13 = (bf16[256,512]{1,0:T(8,128)(2,1)S(1)}, bf16[256,512]{1,0:T(8,128)(2,1)S(1)}, u32[]{:S(2)}, u32[]{:S(2)}) collective-permute-start(bf16[256,512]{1,0:T(8,128)(2,1)S(1)} %in_order.9.refs_1_), channel_id=1, source_target_pairs={{0,3},{1,4},{2,7},{3,0},{4,1},{5,8},{6,11},{7,2},{8,5},{9,12},{10,... | collective-permute-start | bytes 786440 | tf_op jit(solution)/shard_map/ppermute | solution.py:62
  53.2 7.4 %collective-permute-start.14 = (bf16[256,512]{1,0:T(8,128)(2,1)S(1)}, bf16[256,512]{1,0:T(8,128)(2,1)S(1)}, u32[]{:S(2)}, u32[]{:S(2)}) collective-permute-start(bf16[256,512]{1,0:T(8,128)(2,1)S(1)} %in_order.10.refs_1_.refs_0_), channel_id=1, source_target_pairs={{0,3},{1,4},{2,7},{3,0},{4,1},{5,8},{6,11},{7,2},{8,5},{9,12},{10,... | collective-permute-start | bytes 786440 | tf_op jit(solution)/shard_map/ppermute | solution.py:62
  53.9 7.2 %collective-permute-start.15 = (bf16[256,512]{1,0:T(8,128)(2,1)S(1)}, bf16[256,512]{1,0:T(8,128)(2,1)S(1)}, u32[]{:S(2)}, u32[]{:S(2)}) collective-permute-start(bf16[256,512]{1,0:T(8,128)(2,1)S(1)} %in_order.11.refs_1_), channel_id=1, source_target_pairs={{0,5},{1,2},{2,1},{3,6},{4,9},{5,0},{6,3},{7,10},{8,13},{9,4},{10,... | collective-permute-start | bytes 786440 | tf_op jit(solution)/shard_map/ppermute | solution.py:62
  60.6 5.8 %collective-permute-start.19 = (bf16[256,512]{1,0:T(8,128)(2,1)S(1)}, bf16[256,512]{1,0:T(8,128)(2,1)S(1)}, u32[]{:S(2)}, u32[]{:S(2)}) collective-permute-start(bf16[256,512]{1,0:T(8,128)(2,1)S(1)} %in_order.12.refs_1_.refs_0_), channel_id=1, source_target_pairs={{0,5},{1,2},{2,1},{3,6},{4,9},{5,0},{6,3},{7,10},{8,13},{9,4},{10,... | collective-permute-start | bytes 786440 | tf_op jit(solution)/shard_map/ppermute | solution.py:62
  60.6 5.8 %collective-permute-start.16 = (bf16[256,512]{1,0:T(8,128)(2,1)S(1)}, bf16[256,512]{1,0:T(8,128)(2,1)S(1)}, u32[]{:S(2)}, u32[]{:S(2)}) collective-permute-start(bf16[256,512]{1,0:T(8,128)(2,1)S(1)} %get-tuple-element.33), channel_id=1, source_target_pairs={{0,1},{1,0},{2,3},{3,2},{4,5},{5,4},{6,7},{7,6},{8,9},{9,8},{10,11... | collective-permute-start | bytes 786440 | tf_op jit(solution)/shard_map/ppermute | solution.py:53
  60.6 5.8 %collective-permute-start.17 = (bf16[256,512]{1,0:T(8,128)(2,1)S(1)}, bf16[256,512]{1,0:T(8,128)(2,1)S(1)}, u32[]{:S(2)}, u32[]{:S(2)}) collective-permute-start(bf16[256,512]{1,0:T(8,128)(2,1)S(1)} %get-tuple-element.34), channel_id=1, source_target_pairs={{0,1},{1,0},{2,3},{3,2},{4,5},{5,4},{6,7},{7,6},{8,9},{9,8},{10,11... | collective-permute-start | bytes 786440 | tf_op jit(solution)/shard_map/ppermute | solution.py:53
  61.8 4.7 %collective-permute-start.18 = (bf16[256,512]{1,0:T(8,128)(2,1)S(1)}, bf16[256,512]{1,0:T(8,128)(2,1)S(1)}, u32[]{:S(2)}, u32[]{:S(2)}) collective-permute-start(bf16[256,512]{1,0:T(8,128)(2,1)S(1)} %get-tuple-element.35), channel_id=1, source_target_pairs={{0,1},{1,0},{2,3},{3,2},{4,5},{5,4},{6,7},{7,6},{8,9},{9,8},{10,11... | collective-permute-start | bytes 786440 | tf_op jit(solution)/shard_map/ppermute | solution.py:53
  66.4 1.5 %collective-permute-start.20 = (bf16[256,512]{1,0:T(8,128)(2,1)S(1)}, bf16[256,512]{1,0:T(8,128)(2,1)S(1)}, u32[]{:S(2)}, u32[]{:S(2)}) collective-permute-start(bf16[256,512]{1,0:T(8,128)(2,1)S(1)} %collective-permute-done.19.mine_ref), channel_id=1, source_target_pairs={{0,1},{1,0},{2,3},{3,2},{4,5},{5,4},{6,7},{7,6},{8,9},{9,8},{10,11... | collective-permute-start | bytes 786440 | tf_op jit(solution)/shard_map/ppermute | solution.py:53

commit v21 on v18

--- a/solution.py
+++ b/solution.py
@@ -321,7 +321,7 @@
     in_vmem = pl.BlockSpec(memory_space=pltpu.VMEM)
     in_any = pl.BlockSpec(memory_space=pl.ANY)
     grid_rows = blk_count * block_rows
-    per_step = 4
+    per_step = 8
     rows = per_step * block_rows
     counts = ((2 * chips - 2) * slots, 2 * slots)
     latent, near, sent_far, table = pl.pallas_call(
@@ -349,7 +349,7 @@
                 pltpu.SMEM((3, per_step * list_len), jnp.int32),
             ],
         ),
-        compiler_params=params(24),
+        compiler_params=params(32),
         cost_estimate=cost(
             2 * blk_count * block_rows * width * (channels + width + list_len * tile_rows),
             grid_features,

time: 72.1 us -> 71.8 us (level)
  no operation moved by 1% of the time
where the time goes in v21:
time: 71.8 us; the launch traced here: 71.6 us
  starting transfers between devices  28.7 us (40%)
  waiting for transfers between devices  21.3 us (30%)
  Pallas kernels  20.9 us (29%)
  between operations  0.79 us (1%)
    ppermute x14, starting transfers between devices, over(): return lax.ppermute(value, 'band', pairs)  25.7 us
    ppermute x14, waiting for transfers between devices, over(): return lax.ppermute(value, 'band', pairs)  17.3 us
    pallas_call x1, Pallas kernels, on_device(): pl.pallas_call(functools.partial(embed_kernel, ring, per_step, slots), ou...  9.55 us
    pallas_call x1, Pallas kernels, on_device(): pl.pallas_call(functools.partial(back_kernel, list_len), out_shape=shape(...  4.57 us
    ppermute x7, waiting for transfers between devices, over_core(): return lax.ppermute(value, 'band', [(i, i ^ 1) for i in range(self.n_band)])  3.96 us
    pallas_call x4, Pallas kernels, pick(): pl.pallas_call(functools.partial(pick_kernel, chosen, slots, chips, tile_...  3.11 us
    ppermute x7, starting transfers between devices, over_core(): return lax.ppermute(value, 'band', [(i, i ^ 1) for i in range(self.n_band)])  2.98 us
  transfers between devices with their start and end apart: 21, of which 17 were waited for; matrix products, arithmetic and copies ran while one was open for 0% of the time, Pallas kernels for 7%

profile of v21, /device:TPU:0, one launch (start us, length us, event | category | flops | bytes accessed | tf_op | source)
XLA Modules:
  0.0 71.6 jit_solution(10529454169811697673)
XLA Ops:
  0.6 9.5 %embed.1 = (bf16[4096,512]{1,0:T(8,128)(2,1)}, bf16[57,32,512]{2,1,0:T(8,128)(2,1)S(1)}, bf16[9,32,512]{2,1,0:T(8,128)(2,1)S(1)}, s32[4,64]{1,0:T(4,128)S(1)}) custom-call(s32[1]{0:T(128)} %bitcast.me_ref, s32[4,256]{1,0:T(4,128)} %bitcast.8, s32[4,256]{1,0:T(4,128)} %bitcast.9, bf16[227,4096]{1,0:T(8,128)(2,1)} %bitcast.7, bf16[227,512]{1,0:T(8,128)(2,1)} %w1_ref.1, ...), custom_call_target="tpu_custom_call" | custom-call | flops 3636461568 | bytes 2908160 | tf_op jit(solution)/shard_map/embed/pallas_call | solution.py:327
  10.6 1.2 %collective-permute-done.other = bf16[9,32,512]{2,1,0:T(8,128)(2,1)S(1)} collective-permute-done((bf16[9,32,512]{2,1,0:T(8,128)(2,1)S(1)}, bf16[9,32,512]{2,1,0:T(8,128)(2,1)S(1)}, u32[]{:S(2)}, u32[]{:S(2)}) %collective-permute-start) | collective-permute-done | bytes 294944 | tf_op jit(solution)/shard_map/ppermute | solution.py:53
  11.8 0.8 %far_sums.1 = (bf16[8,32,512]{2,1,0:T(8,128)(2,1)S(1)}, bf16[8,32,512]{2,1,0:T(8,128)(2,1)S(1)}, bf16[57,32,512]{2,1,0:T(8,128)(2,1)S(1)}) custom-call(s32[4,64]{1,0:T(4,128)S(1)} %get-tuple-element.20.table_ref, bf16[57,32,512]{2,1,0:T(8,128)(2,1)S(1)} %get-tuple-element.21.kept, ...), custom_call_target="tpu_custom_call", output_to_operand_aliasing={{2}: (1, {})} | custom-call | bytes 1867776 | tf_op jit(solution)/shard_map/far_sums/pallas_call | solution.py:376
  13.1 2.7 %collective-permute-start.2 = (bf16[8,32,512]{2,1,0:T(8,128)(2,1)S(1)}, bf16[8,32,512]{2,1,0:T(8,128)(2,1)S(1)}, u32[]{:S(2)}, u32[]{:S(2)}) collective-permute-start(bf16[8,32,512]{2,1,0:T(8,128)(2,1)S(1)} %get-tuple-element.24), channel_id=1, source_target_pairs={{0,5},{1,2},{2,1},{3,6},{4,9},{5,0},{6,3},{7,10},{8,13},{9,4},{10,... | collective-permute-start | bytes 786440 | tf_op jit(solution)/shard_map/ppermute | solution.py:62
  15.8 0.7 %collective-permute-done.1.other = bf16[57,32,512]{2,1,0:T(8,128)(2,1)S(1)} collective-permute-done((bf16[57,32,512]{2,1,0:T(8,128)(2,1)S(1)}, bf16[57,32,512]{2,1,0:T(8,128)(2,1)S(1)}, u32[]{:S(2)}, u32[]{:S(2)}) %collective-permute-start.1) | collective-permute-done | bytes 1867808 | tf_op jit(solution)/shard_map/ppermute | solution.py:53
  16.5 1.2 %own_sums.1.token.own = f32[6,8,32,512]{3,2,1,0:T(8,128)S(1)} custom-call(s32[4,64]{1,0:T(4,128)S(1)} %get-tuple-element.20.table_ref, bf16[57,32,512]{2,1,0:T(8,128)(2,1)S(1)} %get-tuple-element.23.kept, bf16[57,32,512]{2,1,0:T(8,128)(2,1)S(1)} %collective-permute-done.1.other), custom_call_target="tpu_custom_call" | custom-call | bytes 3735552 | tf_op jit(solution)/shard_map/own_sums/pallas_call | solution.py:392
  18.3 1.5 %collective-permute-done.2.came = bf16[8,32,512]{2,1,0:T(8,128)(2,1)S(1)} collective-permute-done((bf16[8,32,512]{2,1,0:T(8,128)(2,1)S(1)}, bf16[8,32,512]{2,1,0:T(8,128)(2,1)S(1)}, u32[]{:S(2)}, u32[]{:S(2)}) %collective-permute-start.2) | collective-permute-done | bytes 262176 | tf_op jit(solution)/shard_map/ppermute | solution.py:62
  19.9 2.0 %collective-permute-start.3 = (bf16[8,32,512]{2,1,0:T(8,128)(2,1)S(1)}, bf16[8,32,512]{2,1,0:T(8,128)(2,1)S(1)}, u32[]{:S(2)}, u32[]{:S(2)}) collective-permute-start(bf16[8,32,512]{2,1,0:T(8,128)(2,1)S(1)} %add_5.1.token), channel_id=1, source_target_pairs={{0,3},{1,4},{2,7},{3,0},{4,1},{5,8},{6,11},{7,2},{8,5},{9,12},{10,... | collective-permute-start | bytes 786440 | tf_op jit(solution)/shard_map/ppermute | solution.py:62
  22.7 2.1 %collective-permute-start.6 = (bf16[8,32,512]{2,1,0:T(8,128)(2,1)S(1)}, bf16[8,32,512]{2,1,0:T(8,128)(2,1)S(1)}, u32[]{:S(2)}, u32[]{:S(2)}) collective-permute-start(bf16[8,32,512]{2,1,0:T(8,128)(2,1)S(1)} %add_4.1.token), channel_id=1, source_target_pairs={{0,3},{1,4},{2,7},{3,0},{4,1},{5,8},{6,11},{7,2},{8,5},{9,12},{10,... | collective-permute-start | bytes 786440 | tf_op jit(solution)/shard_map/ppermute | solution.py:62
  24.8 1.2 %collective-permute-done.3.came = bf16[8,32,512]{2,1,0:T(8,128)(2,1)S(1)} collective-permute-done((bf16[8,32,512]{2,1,0:T(8,128)(2,1)S(1)}, bf16[8,32,512]{2,1,0:T(8,128)(2,1)S(1)}, u32[]{:S(2)}, u32[]{:S(2)}) %collective-permute-start.3) | collective-permute-done | bytes 262176 | tf_op jit(solution)/shard_map/ppermute | solution.py:62
  26.0 2.2 %collective-permute-start.5 = (bf16[8,32,512]{2,1,0:T(8,128)(2,1)S(1)}, bf16[8,32,512]{2,1,0:T(8,128)(2,1)S(1)}, u32[]{:S(2)}, u32[]{:S(2)}) collective-permute-start(bf16[8,32,512]{2,1,0:T(8,128)(2,1)S(1)} %add_3.1.token), channel_id=1, source_target_pairs={{0,5},{1,2},{2,1},{3,6},{4,9},{5,0},{6,3},{7,10},{8,13},{9,4},{10,... | collective-permute-start | bytes 786440 | tf_op jit(solution)/shard_map/ppermute | solution.py:62
  28.2 0.8 %collective-permute-done.6.came = bf16[8,32,512]{2,1,0:T(8,128)(2,1)S(1)} collective-permute-done((bf16[8,32,512]{2,1,0:T(8,128)(2,1)S(1)}, bf16[8,32,512]{2,1,0:T(8,128)(2,1)S(1)}, u32[]{:S(2)}, u32[]{:S(2)}) %collective-permute-start.6) | collective-permute-done | bytes 262176 | tf_op jit(solution)/shard_map/ppermute | solution.py:62
  29.1 2.4 %collective-permute-start.8 = (bf16[8,32,512]{2,1,0:T(8,128)(2,1)S(1)}, bf16[8,32,512]{2,1,0:T(8,128)(2,1)S(1)}, u32[]{:S(2)}, u32[]{:S(2)}) collective-permute-start(bf16[8,32,512]{2,1,0:T(8,128)(2,1)S(1)} %add_2.1.token), channel_id=1, source_target_pairs={{0,5},{1,2},{2,1},{3,6},{4,9},{5,0},{6,3},{7,10},{8,13},{9,4},{10,... | collective-permute-start | bytes 786440 | tf_op jit(solution)/shard_map/ppermute | solution.py:62
  32.3 2.0 %collective-permute-start.7 = (bf16[8,32,512]{2,1,0:T(8,128)(2,1)S(1)}, bf16[8,32,512]{2,1,0:T(8,128)(2,1)S(1)}, u32[]{:S(2)}, u32[]{:S(2)}) collective-permute-start(bf16[8,32,512]{2,1,0:T(8,128)(2,1)S(1)} %add_1.1), channel_id=1, source_target_pairs={{0,3},{1,4},{2,7},{3,0},{4,1},{5,8},{6,11},{7,2},{8,5},{9,12},{10,... | collective-permute-start | bytes 786440 | tf_op jit(solution)/shard_map/ppermute | solution.py:62
  34.4 1.6 %collective-permute-done.8.neighbour = bf16[8,32,512]{2,1,0:T(8,128)(2,1)S(1)} collective-permute-done((bf16[8,32,512]{2,1,0:T(8,128)(2,1)S(1)}, bf16[8,32,512]{2,1,0:T(8,128)(2,1)S(1)}, u32[]{:S(2)}, u32[]{:S(2)}) %collective-permute-start.8) | collective-permute-done | bytes 262176 | tf_op jit(solution)/shard_map/ppermute | solution.py:62
  36.0 2.4 %collective-permute-done.7.came = bf16[8,32,512]{2,1,0:T(8,128)(2,1)S(1)} collective-permute-done((bf16[8,32,512]{2,1,0:T(8,128)(2,1)S(1)}, bf16[8,32,512]{2,1,0:T(8,128)(2,1)S(1)}, u32[]{:S(2)}, u32[]{:S(2)}) %collective-permute-start.7) | collective-permute-done | bytes 262176 | tf_op jit(solution)/shard_map/ppermute | solution.py:62
  38.4 0.7 %mesh_step.1 = (bf16[256,512]{1,0:T(8,128)(2,1)S(1)}, bf16[256,512]{1,0:T(8,128)(2,1)S(1)}) custom-call(bf16[256,512]{1,0:T(8,128)(2,1)S(1)} %copy-done.3, bf16[512,512]{1,0:T(8,128)(2,1)S(1)} %copy-done.1, bf16[512,512]{1,0:T(8,128)(2,1)S(1)} %copy-done.2, f32[1,512]{1,0:T(1,128)S(1)} %bitcast.6, f32[6,8,32,512]{3,2,1,0:T(8,128)S(1)} %own_sums.1.token.own, ...), custom_call_target="tpu_custom_call" | custom-call | flops 268435456 | bytes 1048576 | tf_op jit(solution)/shard_map/mesh_step/pallas_call | solution.py:440
  39.2 1.9 %collective-permute-start.9 = (bf16[256,512]{1,0:T(8,128)(2,1)S(1)}, bf16[256,512]{1,0:T(8,128)(2,1)S(1)}, u32[]{:S(2)}, u32[]{:S(2)}) collective-permute-start(bf16[256,512]{1,0:T(8,128)(2,1)S(1)} %get-tuple-element.26.refs_0_), channel_id=1, source_target_pairs={{0,3},{1,4},{2,7},{3,0},{4,1},{5,8},{6,11},{7,2},{8,5},{9,12},{10,... | collective-permute-start | bytes 786440 | tf_op jit(solution)/shard_map/ppermute | solution.py:62
  41.1 1.3 %pick_0.1 = (bf16[128,512]{1,0:T(8,128)(2,1)S(1)}, bf16[128,512]{1,0:T(8,128)(2,1)S(1)}, bf16[256,512]{1,0:T(8,128)(2,1)}) custom-call(s32[4,64]{1,0:T(4,128)S(1)} %get-tuple-element.20.table_ref, bf16[256,512]{1,0:T(8,128)(2,1)S(1)} %get-tuple-element.26.refs_0_), custom_call_target="tpu_custom_call" | custom-call | bytes 262144 | tf_op jit(solution)/shard_map/pick_0/pallas_call | solution.py:456
  43.0 1.0 %collective-permute-done.10.refs_1_.refs_4_ = bf16[128,512]{1,0:T(8,128)(2,1)S(1)} collective-permute-done((bf16[128,512]{1,0:T(8,128)(2,1)S(1)}, bf16[128,512]{1,0:T(8,128)(2,1)S(1)}, u32[]{:S(2)}, u32[]{:S(2)}) %collective-permute-start.10) | collective-permute-done | bytes 131104 | tf_op jit(solution)/shard_map/ppermute | solution.py:53
  44.0 1.5 %collective-permute-start.11 = (bf16[256,512]{1,0:T(8,128)(2,1)S(1)}, bf16[256,512]{1,0:T(8,128)(2,1)S(1)}, u32[]{:S(2)}, u32[]{:S(2)}) collective-permute-start(bf16[256,512]{1,0:T(8,128)(2,1)S(1)} %in_order.8), channel_id=1, source_target_pairs={{0,5},{1,2},{2,1},{3,6},{4,9},{5,0},{6,3},{7,10},{8,13},{9,4},{10,... | collective-permute-start | bytes 786440 | tf_op jit(solution)/shard_map/ppermute | solution.py:62
  45.5 1.6 %collective-permute-start.12 = (bf16[256,512]{1,0:T(8,128)(2,1)S(1)}, bf16[256,512]{1,0:T(8,128)(2,1)S(1)}, u32[]{:S(2)}, u32[]{:S(2)}) collective-permute-start(bf16[256,512]{1,0:T(8,128)(2,1)S(1)} %in_order.7.refs_1_.refs_0_), channel_id=1, source_target_pairs={{0,5},{1,2},{2,1},{3,6},{4,9},{5,0},{6,3},{7,10},{8,13},{9,4},{10,... | collective-permute-start | bytes 786440 | tf_op jit(solution)/shard_map/ppermute | solution.py:62
  47.1 2.7 %collective-permute-done.11.refs_0_ = bf16[256,512]{1,0:T(8,128)(2,1)S(1)} collective-permute-done((bf16[256,512]{1,0:T(8,128)(2,1)S(1)}, bf16[256,512]{1,0:T(8,128)(2,1)S(1)}, u32[]{:S(2)}, u32[]{:S(2)}) %collective-permute-start.11) | collective-permute-done | bytes 262176 | tf_op jit(solution)/shard_map/ppermute | solution.py:62
  49.8 1.5 %collective-permute-start.13 = (bf16[256,512]{1,0:T(8,128)(2,1)S(1)}, bf16[256,512]{1,0:T(8,128)(2,1)S(1)}, u32[]{:S(2)}, u32[]{:S(2)}) collective-permute-start(bf16[256,512]{1,0:T(8,128)(2,1)S(1)} %in_order.9.refs_1_), channel_id=1, source_target_pairs={{0,3},{1,4},{2,7},{3,0},{4,1},{5,8},{6,11},{7,2},{8,5},{9,12},{10,... | collective-permute-start | bytes 786440 | tf_op jit(solution)/shard_map/ppermute | solution.py:62
  51.8 0.7 %collective-permute-done.12.refs_0_ = bf16[256,512]{1,0:T(8,128)(2,1)S(1)} collective-permute-done((bf16[256,512]{1,0:T(8,128)(2,1)S(1)}, bf16[256,512]{1,0:T(8,128)(2,1)S(1)}, u32[]{:S(2)}, u32[]{:S(2)}) %collective-permute-start.12) | collective-permute-done | bytes 262176 | tf_op jit(solution)/shard_map/ppermute | solution.py:62
  52.6 1.5 %collective-permute-start.14 = (bf16[256,512]{1,0:T(8,128)(2,1)S(1)}, bf16[256,512]{1,0:T(8,128)(2,1)S(1)}, u32[]{:S(2)}, u32[]{:S(2)}) collective-permute-start(bf16[256,512]{1,0:T(8,128)(2,1)S(1)} %in_order.10.refs_1_.refs_0_), channel_id=1, source_target_pairs={{0,3},{1,4},{2,7},{3,0},{4,1},{5,8},{6,11},{7,2},{8,5},{9,12},{10,... | collective-permute-start | bytes 786440 | tf_op jit(solution)/shard_map/ppermute | solution.py:62
  54.1 1.8 %collective-permute-done.13.refs_0_ = bf16[256,512]{1,0:T(8,128)(2,1)S(1)} collective-permute-done((bf16[256,512]{1,0:T(8,128)(2,1)S(1)}, bf16[256,512]{1,0:T(8,128)(2,1)S(1)}, u32[]{:S(2)}, u32[]{:S(2)}) %collective-permute-start.13) | collective-permute-done | bytes 262176 | tf_op jit(solution)/shard_map/ppermute | solution.py:62
  55.9 1.8 %collective-permute-start.15 = (bf16[256,512]{1,0:T(8,128)(2,1)S(1)}, bf16[256,512]{1,0:T(8,128)(2,1)S(1)}, u32[]{:S(2)}, u32[]{:S(2)}) collective-permute-start(bf16[256,512]{1,0:T(8,128)(2,1)S(1)} %in_order.11.refs_1_), channel_id=1, source_target_pairs={{0,5},{1,2},{2,1},{3,6},{4,9},{5,0},{6,3},{7,10},{8,13},{9,4},{10,... | collective-permute-start | bytes 786440 | tf_op jit(solution)/shard_map/ppermute | solution.py:62
  58.7 2.5 %collective-permute-start.19 = (bf16[256,512]{1,0:T(8,128)(2,1)S(1)}, bf16[256,512]{1,0:T(8,128)(2,1)S(1)}, u32[]{:S(2)}, u32[]{:S(2)}) collective-permute-start(bf16[256,512]{1,0:T(8,128)(2,1)S(1)} %in_order.12.refs_1_.refs_0_), channel_id=1, source_target_pairs={{0,5},{1,2},{2,1},{3,6},{4,9},{5,0},{6,3},{7,10},{8,13},{9,4},{10,... | collective-permute-start | bytes 786440 | tf_op jit(solution)/shard_map/ppermute | solution.py:62
  63.3 2.0 %collective-permute-done.19.mine_ref = bf16[256,512]{1,0:T(8,128)(2,1)S(1)} collective-permute-done((bf16[256,512]{1,0:T(8,128)(2,1)S(1)}, bf16[256,512]{1,0:T(8,128)(2,1)S(1)}, u32[]{:S(2)}, u32[]{:S(2)}) %collective-permute-start.19) | collective-permute-done | bytes 262176 | tf_op jit(solution)/shard_map/ppermute | solution.py:62
  66.0 1.0 %collective-permute-done.20.theirs_ref = bf16[256,512]{1,0:T(8,128)(2,1)S(1)} collective-permute-done((bf16[256,512]{1,0:T(8,128)(2,1)S(1)}, bf16[256,512]{1,0:T(8,128)(2,1)S(1)}, u32[]{:S(2)}, u32[]{:S(2)}) %collective-permute-start.20) | collective-permute-done | bytes 262176 | tf_op jit(solution)/shard_map/ppermute | solution.py:53
  67.1 4.6 %back.1 = bf16[4096,512]{1,0:T(8,128)(2,1)} custom-call(s32[4,64]{1,0:T(4,128)S(1)} %get-tuple-element.20.table_ref, bf16[16,256,128]{2,1,0:T(8,128)(2,1)S(1)} %turn.1.token.weights_ref, bf16[1792,512]{1,0:T(8,128)(2,1)S(1)} %join.1.near_ref, bf16[256,512]{1,0:T(8,128)(2,1)S(1)} %collective-permute-done.19.mine_ref, ...), custom_call_target="tpu_custom_call" | custom-call | flops 536870912 | bytes 9437184 | tf_op jit(solution)/shard_map/back/pallas_call | solution.py:498
  (43 shorter events, 8.3 us)
Async XLA Ops:
  10.2 1.7 %collective-permute-start = (bf16[9,32,512]{2,1,0:T(8,128)(2,1)S(1)}, bf16[9,32,512]{2,1,0:T(8,128)(2,1)S(1)}, u32[]{:S(2)}, u32[]{:S(2)}) collective-permute-start(bf16[9,32,512]{2,1,0:T(8,128)(2,1)S(1)} %get-tuple-element.22), channel_id=1, source_target_pairs={{0,1},{1,0},{2,3},{3,2},{4,5},{5,4},{6,7},{7,6},{8,9},{9,8},{10,11... | collective-permute-start | bytes 884744 | tf_op jit(solution)/shard_map/ppermute | solution.py:53
  12.6 3.9 %collective-permute-start.1 = (bf16[57,32,512]{2,1,0:T(8,128)(2,1)S(1)}, bf16[57,32,512]{2,1,0:T(8,128)(2,1)S(1)}, u32[]{:S(2)}, u32[]{:S(2)}) collective-permute-start(bf16[57,32,512]{2,1,0:T(8,128)(2,1)S(1)} %get-tuple-element.23.kept), channel_id=1, source_target_pairs={{0,1},{1,0},{2,3},{3,2},{4,5},{5,4},{6,7},{7,6},{8,9},{9,8},{10,11... | collective-permute-start | bytes 5603336 | tf_op jit(solution)/shard_map/ppermute | solution.py:53
  13.1 6.7 %collective-permute-start.2 = (bf16[8,32,512]{2,1,0:T(8,128)(2,1)S(1)}, bf16[8,32,512]{2,1,0:T(8,128)(2,1)S(1)}, u32[]{:S(2)}, u32[]{:S(2)}) collective-permute-start(bf16[8,32,512]{2,1,0:T(8,128)(2,1)S(1)} %get-tuple-element.24), channel_id=1, source_target_pairs={{0,5},{1,2},{2,1},{3,6},{4,9},{5,0},{6,3},{7,10},{8,13},{9,4},{10,... | collective-permute-start | bytes 786440 | tf_op jit(solution)/shard_map/ppermute | solution.py:62
  15.8 2.0 %copy-start = (bf16[16,4,32,256]{3,2,1,0:T(8,128)(2,1)S(1)}, bf16[16,4,32,256]{3,2,1,0:T(8,128)(2,1)}, u32[]{:S(2)}) copy-start(bf16[16,4,32,256]{3,2,1,0:T(8,128)(2,1)} %interp_ref.3) | copy-start | bytes 3145732
  15.8 6.9 %collective-permute-start.4 = (bf16[8,32,512]{2,1,0:T(8,128)(2,1)S(1)}, bf16[8,32,512]{2,1,0:T(8,128)(2,1)S(1)}, u32[]{:S(2)}, u32[]{:S(2)}) collective-permute-start(bf16[8,32,512]{2,1,0:T(8,128)(2,1)S(1)} %get-tuple-element.25), channel_id=1, source_target_pairs={{0,5},{1,2},{2,1},{3,6},{4,9},{5,0},{6,3},{7,10},{8,13},{9,4},{10,... | collective-permute-start | bytes 786440 | tf_op jit(solution)/shard_map/ppermute | solution.py:62
  19.9 6.1 %collective-permute-start.3 = (bf16[8,32,512]{2,1,0:T(8,128)(2,1)S(1)}, bf16[8,32,512]{2,1,0:T(8,128)(2,1)S(1)}, u32[]{:S(2)}, u32[]{:S(2)}) collective-permute-start(bf16[8,32,512]{2,1,0:T(8,128)(2,1)S(1)} %add_5.1.token), channel_id=1, source_target_pairs={{0,3},{1,4},{2,7},{3,0},{4,1},{5,8},{6,11},{7,2},{8,5},{9,12},{10,... | collective-permute-start | bytes 786440 | tf_op jit(solution)/shard_map/ppermute | solution.py:62
  22.7 6.3 %collective-permute-start.6 = (bf16[8,32,512]{2,1,0:T(8,128)(2,1)S(1)}, bf16[8,32,512]{2,1,0:T(8,128)(2,1)S(1)}, u32[]{:S(2)}, u32[]{:S(2)}) collective-permute-start(bf16[8,32,512]{2,1,0:T(8,128)(2,1)S(1)} %add_4.1.token), channel_id=1, source_target_pairs={{0,3},{1,4},{2,7},{3,0},{4,1},{5,8},{6,11},{7,2},{8,5},{9,12},{10,... | collective-permute-start | bytes 786440 | tf_op jit(solution)/shard_map/ppermute | solution.py:62
  26.0 6.2 %collective-permute-start.5 = (bf16[8,32,512]{2,1,0:T(8,128)(2,1)S(1)}, bf16[8,32,512]{2,1,0:T(8,128)(2,1)S(1)}, u32[]{:S(2)}, u32[]{:S(2)}) collective-permute-start(bf16[8,32,512]{2,1,0:T(8,128)(2,1)S(1)} %add_3.1.token), channel_id=1, source_target_pairs={{0,5},{1,2},{2,1},{3,6},{4,9},{5,0},{6,3},{7,10},{8,13},{9,4},{10,... | collective-permute-start | bytes 786440 | tf_op jit(solution)/shard_map/ppermute | solution.py:62
  29.1 9.3 %copy-start.1 = (bf16[512,512]{1,0:T(8,128)(2,1)S(1)}, bf16[512,512]{1,0:T(8,128)(2,1)}, u32[]{:S(2)}) copy-start(bf16[512,512]{1,0:T(8,128)(2,1)} %up_ref.1) | copy-start | bytes 1572868
  29.1 9.3 %copy-start.2 = (bf16[512,512]{1,0:T(8,128)(2,1)S(1)}, bf16[512,512]{1,0:T(8,128)(2,1)}, u32[]{:S(2)}) copy-start(bf16[512,512]{1,0:T(8,128)(2,1)} %down_ref.1) | copy-start | bytes 1572868
  29.1 9.3 %copy-start.3 = (bf16[256,512]{1,0:T(8,128)(2,1)S(1)}, bf16[256,512]{1,0:T(8,128)(2,1)}, u32[]{:S(2)}) copy-start(bf16[256,512]{1,0:T(8,128)(2,1)} %latent_ref.1) | copy-start | bytes 786436
  29.1 9.3 %copy-start.4 = (f32[512]{0:T(512)S(1)}, f32[512]{0:T(512)}, u32[]{:S(2)}) copy-start(f32[512]{0:T(512)} %param.21) | copy-start | bytes 6148
  29.1 6.8 %collective-permute-start.8 = (bf16[8,32,512]{2,1,0:T(8,128)(2,1)S(1)}, bf16[8,32,512]{2,1,0:T(8,128)(2,1)S(1)}, u32[]{:S(2)}, u32[]{:S(2)}) collective-permute-start(bf16[8,32,512]{2,1,0:T(8,128)(2,1)S(1)} %add_2.1.token), channel_id=1, source_target_pairs={{0,5},{1,2},{2,1},{3,6},{4,9},{5,0},{6,3},{7,10},{8,13},{9,4},{10,... | collective-permute-start | bytes 786440 | tf_op jit(solution)/shard_map/ppermute | solution.py:62
  32.3 6.1 %collective-permute-start.7 = (bf16[8,32,512]{2,1,0:T(8,128)(2,1)S(1)}, bf16[8,32,512]{2,1,0:T(8,128)(2,1)S(1)}, u32[]{:S(2)}, u32[]{:S(2)}) collective-permute-start(bf16[8,32,512]{2,1,0:T(8,128)(2,1)S(1)} %add_1.1), channel_id=1, source_target_pairs={{0,3},{1,4},{2,7},{3,0},{4,1},{5,8},{6,11},{7,2},{8,5},{9,12},{10,... | collective-permute-start | bytes 786440 | tf_op jit(solution)/shard_map/ppermute | solution.py:62
  39.2 6.3 %collective-permute-start.9 = (bf16[256,512]{1,0:T(8,128)(2,1)S(1)}, bf16[256,512]{1,0:T(8,128)(2,1)S(1)}, u32[]{:S(2)}, u32[]{:S(2)}) collective-permute-start(bf16[256,512]{1,0:T(8,128)(2,1)S(1)} %get-tuple-element.26.refs_0_), channel_id=1, source_target_pairs={{0,3},{1,4},{2,7},{3,0},{4,1},{5,8},{6,11},{7,2},{8,5},{9,12},{10,... | collective-permute-start | bytes 786440 | tf_op jit(solution)/shard_map/ppermute | solution.py:62
  42.4 1.5 %collective-permute-start.10 = (bf16[128,512]{1,0:T(8,128)(2,1)S(1)}, bf16[128,512]{1,0:T(8,128)(2,1)S(1)}, u32[]{:S(2)}, u32[]{:S(2)}) collective-permute-start(bf16[128,512]{1,0:T(8,128)(2,1)S(1)} %get-tuple-element.29), channel_id=1, source_target_pairs={{0,1},{1,0},{2,3},{3,2},{4,5},{5,4},{6,7},{7,6},{8,9},{9,8},{10,11... | collective-permute-start | bytes 393224 | tf_op jit(solution)/shard_map/ppermute | solution.py:53
  44.0 5.8 %collective-permute-start.11 = (bf16[256,512]{1,0:T(8,128)(2,1)S(1)}, bf16[256,512]{1,0:T(8,128)(2,1)S(1)}, u32[]{:S(2)}, u32[]{:S(2)}) collective-permute-start(bf16[256,512]{1,0:T(8,128)(2,1)S(1)} %in_order.8), channel_id=1, source_target_pairs={{0,5},{1,2},{2,1},{3,6},{4,9},{5,0},{6,3},{7,10},{8,13},{9,4},{10,... | collective-permute-start | bytes 786440 | tf_op jit(solution)/shard_map/ppermute | solution.py:62
  45.5 7.1 %collective-permute-start.12 = (bf16[256,512]{1,0:T(8,128)(2,1)S(1)}, bf16[256,512]{1,0:T(8,128)(2,1)S(1)}, u32[]{:S(2)}, u32[]{:S(2)}) collective-permute-start(bf16[256,512]{1,0:T(8,128)(2,1)S(1)} %in_order.7.refs_1_.refs_0_), channel_id=1, source_target_pairs={{0,5},{1,2},{2,1},{3,6},{4,9},{5,0},{6,3},{7,10},{8,13},{9,4},{10,... | collective-permute-start | bytes 786440 | tf_op jit(solution)/shard_map/ppermute | solution.py:62
  49.8 6.2 %collective-permute-start.13 = (bf16[256,512]{1,0:T(8,128)(2,1)S(1)}, bf16[256,512]{1,0:T(8,128)(2,1)S(1)}, u32[]{:S(2)}, u32[]{:S(2)}) collective-permute-start(bf16[256,512]{1,0:T(8,128)(2,1)S(1)} %in_order.9.refs_1_), channel_id=1, source_target_pairs={{0,3},{1,4},{2,7},{3,0},{4,1},{5,8},{6,11},{7,2},{8,5},{9,12},{10,... | collective-permute-start | bytes 786440 | tf_op jit(solution)/shard_map/ppermute | solution.py:62
  52.6 6.2 %collective-permute-start.14 = (bf16[256,512]{1,0:T(8,128)(2,1)S(1)}, bf16[256,512]{1,0:T(8,128)(2,1)S(1)}, u32[]{:S(2)}, u32[]{:S(2)}) collective-permute-start(bf16[256,512]{1,0:T(8,128)(2,1)S(1)} %in_order.10.refs_1_.refs_0_), channel_id=1, source_target_pairs={{0,3},{1,4},{2,7},{3,0},{4,1},{5,8},{6,11},{7,2},{8,5},{9,12},{10,... | collective-permute-start | bytes 786440 | tf_op jit(solution)/shard_map/ppermute | solution.py:62
  55.9 6.4 %collective-permute-start.15 = (bf16[256,512]{1,0:T(8,128)(2,1)S(1)}, bf16[256,512]{1,0:T(8,128)(2,1)S(1)}, u32[]{:S(2)}, u32[]{:S(2)}) collective-permute-start(bf16[256,512]{1,0:T(8,128)(2,1)S(1)} %in_order.11.refs_1_), channel_id=1, source_target_pairs={{0,5},{1,2},{2,1},{3,6},{4,9},{5,0},{6,3},{7,10},{8,13},{9,4},{10,... | collective-permute-start | bytes 786440 | tf_op jit(solution)/shard_map/ppermute | solution.py:62
  58.7 6.5 %collective-permute-start.19 = (bf16[256,512]{1,0:T(8,128)(2,1)S(1)}, bf16[256,512]{1,0:T(8,128)(2,1)S(1)}, u32[]{:S(2)}, u32[]{:S(2)}) collective-permute-start(bf16[256,512]{1,0:T(8,128)(2,1)S(1)} %in_order.12.refs_1_.refs_0_), channel_id=1, source_target_pairs={{0,5},{1,2},{2,1},{3,6},{4,9},{5,0},{6,3},{7,10},{8,13},{9,4},{10,... | collective-permute-start | bytes 786440 | tf_op jit(solution)/shard_map/ppermute | solution.py:62
  61.2 4.7 %collective-permute-start.16 = (bf16[256,512]{1,0:T(8,128)(2,1)S(1)}, bf16[256,512]{1,0:T(8,128)(2,1)S(1)}, u32[]{:S(2)}, u32[]{:S(2)}) collective-permute-start(bf16[256,512]{1,0:T(8,128)(2,1)S(1)} %get-tuple-element.33), channel_id=1, source_target_pairs={{0,1},{1,0},{2,3},{3,2},{4,5},{5,4},{6,7},{7,6},{8,9},{9,8},{10,11... | collective-permute-start | bytes 786440 | tf_op jit(solution)/shard_map/ppermute | solution.py:53
  61.2 4.7 %collective-permute-start.17 = (bf16[256,512]{1,0:T(8,128)(2,1)S(1)}, bf16[256,512]{1,0:T(8,128)(2,1)S(1)}, u32[]{:S(2)}, u32[]{:S(2)}) collective-permute-start(bf16[256,512]{1,0:T(8,128)(2,1)S(1)} %get-tuple-element.34), channel_id=1, source_target_pairs={{0,1},{1,0},{2,3},{3,2},{4,5},{5,4},{6,7},{7,6},{8,9},{9,8},{10,11... | collective-permute-start | bytes 786440 | tf_op jit(solution)/shard_map/ppermute | solution.py:53
  62.9 3.0 %collective-permute-start.18 = (bf16[256,512]{1,0:T(8,128)(2,1)S(1)}, bf16[256,512]{1,0:T(8,128)(2,1)S(1)}, u32[]{:S(2)}, u32[]{:S(2)}) collective-permute-start(bf16[256,512]{1,0:T(8,128)(2,1)S(1)} %get-tuple-element.35), channel_id=1, source_target_pairs={{0,1},{1,0},{2,3},{3,2},{4,5},{5,4},{6,7},{7,6},{8,9},{9,8},{10,11... | collective-permute-start | bytes 786440 | tf_op jit(solution)/shard_map/ppermute | solution.py:53
  65.2 1.8 %collective-permute-start.20 = (bf16[256,512]{1,0:T(8,128)(2,1)S(1)}, bf16[256,512]{1,0:T(8,128)(2,1)S(1)}, u32[]{:S(2)}, u32[]{:S(2)}) collective-permute-start(bf16[256,512]{1,0:T(8,128)(2,1)S(1)} %collective-permute-done.19.mine_ref), channel_id=1, source_target_pairs={{0,1},{1,0},{2,3},{3,2},{4,5},{5,4},{6,7},{7,6},{8,9},{9,8},{10,11... | collective-permute-start | bytes 786440 | tf_op jit(solution)/shard_map/ppermute | solution.py:53
